TPU v7x, 32 devices: a whole 2x2x4 slice. The times are simulated.
32 devices in a mesh: row: 8 (over z, y), col: 4 (over x, core).
Axes of the slice: x: 2, y: 2, z: 4, core: 2. Of those that a mesh axis runs over, the one named last changes fastest.
Arguments:
- tile_values: float32 [4096, 128, 128], P(('row', 'col')), may hold values from -0.15625 to 0.15625
- tile_owner: int32 [4096, 1], P(('row', 'col')), may hold values from 0 to 31; in each aligned block of 128 rows (0 to 127, 128 to 255, ...) at most 8 rows name the same one
- tile_row: int32 [4096], P(('row', 'col')), may hold values from 0 to 23
- tile_col: int32 [4096], P(('row', 'col')), may hold values from 0 to 47
- tile_count: int32 [32], P(('row', 'col')), may hold values from 96 to 128, as said below
- relaxation: float32 [24576], P(('row', 'col')), may hold values from 0.3 to 1
- driving: float32 [24576, 64], P(('row', 'col')), may hold values from 0.2 to 2
- heat_weight: float32 [24576], P(('row', 'col')), may hold values from 0.1 to 3
Outputs:
- mode_flux: float32 [24576, 64], P(('row', 'col'))
- conductivity: float32 [64], replicated
Inputs may be any that keep to these rules, and one draw needn't show every extreme that they name: `tile_owner`: owner d stands for row index d // 4 and column index d % 4. Among the 128 slots of one device no owner appears more than 8 times; in some device some owner appears exactly 8 times; every owner appears somewhere. Device d's slots below tile_count[d] are used, the rest are ignored; some device uses all 128.
All inputs are finite; a program needn't handle non-finite values.
Results may differ from a plain program's by a relative error of at most 0.0001.
Values sent between devices are 32-bit elements; how exact they have to be, the bound alone decides.
No kernel may reach another device: no remote copies, remote signals or barrier semaphores. Data moves between devices by JAX's collectives and lax.ppermute only.
A program may use at most 128 MiB of HBM per device.

v0:
```python
import jax
import jax.numpy as jnp
from jax import lax
from jax.sharding import PartitionSpec as P

ITERS = 3
ROWT_DEV = 24


def shards(
    tile_values, tile_owner, tile_row, tile_col, tile_count, relaxation, driving, heat_weight
):
    n_rows = lax.axis_size("row")
    n_cols = lax.axis_size("col")
    devices = n_rows * n_cols
    per_device = tile_values.shape[0]
    tile_size = tile_values.shape[1]
    capacity = max(2, (2 * per_device + devices - 1) // devices)
    col_tiles = n_rows * ROWT_DEV // n_cols
    columns = driving.shape[1]
    owners = tile_owner[:, 0]
    positions = jnp.arange(per_device, dtype=jnp.int32)
    is_used = positions < tile_count[0]
    same_owner = (owners[:, None] == owners[None, :]) & (positions[None, :] < positions[:, None])
    arrival = jnp.sum(same_owner.astype(jnp.int32), axis=1)
    target = owners * capacity + arrival
    tile_code = jnp.where(is_used, tile_row * col_tiles + tile_col, -1)
    payload = jnp.zeros((devices * capacity, tile_size, tile_size), jnp.float32)
    payload = payload.at[target].set(jnp.where(is_used[:, None, None], tile_values, 0.0))
    labels = jnp.full((devices * capacity,), -1, jnp.int32).at[target].set(tile_code)
    got_values, got_labels = (
        lax.all_to_all(payload, ("row", "col"), split_axis=0, concat_axis=0, tiled=True),
        lax.all_to_all(labels, ("row", "col"), split_axis=0, concat_axis=0, tiled=True),
    )
    row_index = jnp.where(got_labels < 0, ROWT_DEV, got_labels // col_tiles)
    col_index = jnp.where(got_labels < 0, 0, got_labels % col_tiles)
    row_onehot = (jnp.arange(ROWT_DEV, dtype=jnp.int32)[:, None] == row_index[None, :]).astype(
        jnp.float32
    )
    mode_flux = relaxation[:, None] * driving
    for sweep in range(ITERS):
        panel = lax.all_gather(mode_flux, "row", axis=0, tiled=True)
        picked = panel.reshape(col_tiles, tile_size, columns)[col_index]
        products = jnp.einsum("sij,sjk->sik", got_values, picked, precision=lax.Precision.HIGHEST)
        partial_sum = jnp.einsum(
            "rs,sik->rik", row_onehot, products, precision=lax.Precision.HIGHEST
        )
        partial_sum = partial_sum.reshape(ROWT_DEV * tile_size, columns)
        summed = lax.psum_scatter(partial_sum, "col", scatter_dimension=0, tiled=True)
        mode_flux = relaxation[:, None] * (driving + summed)
    weighted_local = jnp.sum(heat_weight[:, None] * mode_flux, axis=0)
    weighted, weight_sum = lax.psum((weighted_local, jnp.sum(heat_weight)), ("row", "col"))
    conductivity = weighted / weight_sum
    return (mode_flux, conductivity)


def solution(mesh):
    placed = (
        P(("row", "col"), None, None),
        P(("row", "col"), None),
        P(("row", "col")),
        P(("row", "col")),
        P(("row", "col")),
        P(("row", "col")),
        P(("row", "col"), None),
        P(("row", "col")),
    )
    return jax.shard_map(
        shards,
        mesh=mesh,
        in_specs=placed,
        out_specs=(P(("row", "col"), None), P()),
        check_vma=False,
    )
```

profile of v0, /device:TPU:0, one launch (start us, length us, event | category | flops | bytes accessed | tf_op | source)
XLA Modules:
  0.0 805.4 jit_solution(3998050017770340490)
XLA Ops:
  11.7 7.3 all-to-all-start
  19.1 7.2 broadcast_select_fusion
  26.3 7.8 broadcast_in_dim.28
  34.1 23.5 %scatter_fusion = f32[256,128,128]{2,1,0:T(8,128)} fusion(f32[256,128,128]{2,1,0:T(8,128)} %broadcast_in_dim.28, s32[128]{0:T(128)S(1)} %fusion.16, f32[128,128,128]{2,1,0:T(8,128)} %broadcast_select_fusion), kind=kCustom, calls=%fused_computation.4 | custom fusion | bytes 25166336 | tf_op jit(solution)/shard_map/scatter | solution.py:29
  57.7 5.8 all-to-all-start.1
  65.2 130.6 %all-gather.4.cloned.1.call-done = f32[6144,64]{0,1:T(8,128)} async-done(((f32[768,64]{0,1:T(8,128)}), f32[6144,64]{0,1:T(8,128)}) %all-gather.4.cloned.1.call-update) | async-done | bytes 1572880 | tf_op jit(solution)/shard_map/all_gather | solution.py:42
  195.8 1.6 copy_bitcast_fusion.2
  197.4 4.3 gather_fusion
  201.7 250.9 %all-to-all-done.1 = f32[256,128,128]{2,1,0:T(8,128)} async-done(((f32[256,128,128]{2,1,0:T(8,128)}), f32[256,128,128]{2,1,0:T(8,128)}, u32[]{:S(2)}, u32[]{:S(2)}) %all-to-all-start.1) | async-done | bytes 16777248 | tf_op jit(solution)/shard_map/all_to_all | solution.py:32
  452.6 36.0 %fusion.19 = f32[256,128,64]{1,2,0:T(8,128)S(1)} fusion(f32[256,128,128]{2,1,0:T(8,128)} %all-to-all-done.1, f32[256,128,64]{1,2,0:T(8,128)} %gather_fusion), kind=kOutput, calls=%fused_computation.49 | convolution fusion | flops 3221225472 | bytes 33554432 | tf_op jit(solution)/shard_map/sij,sjk->sik/dot_general | solution.py:44
  488.6 7.5 fusion.4
  496.1 1.0 copy.50
  497.2 19.2 %reduce-scatter.4.cloned.1.call-done = f32[768,64]{0,1:T(8,128)} async-done(((f32[3072,64]{0,1:T(8,128)}), f32[768,64]{0,1:T(8,128)}) %reduce-scatter.4.cloned.1.call-update) | async-done | bytes 196624 | tf_op jit(solution)/shard_map/reduce_scatter | solution.py:49
  516.5 1.6 add_multiply_fusion.2
  518.2 45.6 %all-gather.6.cloned.1.call-done = f32[6144,64]{0,1:T(8,128)} async-done(((f32[768,64]{0,1:T(8,128)}), f32[6144,64]{0,1:T(8,128)}) %all-gather.6.cloned.1.call-update) | async-done | bytes 1572880 | tf_op jit(solution)/shard_map/all_gather | solution.py:42
  563.7 1.6 copy_bitcast_fusion.1
  565.3 4.4 gather_fusion.1
  569.7 35.7 %fusion.20 = f32[256,128,64]{1,2,0:T(8,128)S(1)} fusion(f32[256,128,128]{2,1,0:T(8,128)} %all-to-all-done.1, f32[256,128,64]{1,2,0:T(8,128)} %gather_fusion.1), kind=kOutput, calls=%fused_computation.50 | convolution fusion | flops 3221225472 | bytes 33554432 | tf_op jit(solution)/shard_map/sij,sjk->sik/dot_general | solution.py:44
  605.4 7.5 fusion.2
  612.9 1.0 copy.49
  614.0 22.2 %reduce-scatter.6.cloned.1.call-done = f32[768,64]{0,1:T(8,128)} async-done(((f32[3072,64]{0,1:T(8,128)}), f32[768,64]{0,1:T(8,128)}) %reduce-scatter.6.cloned.1.call-update) | async-done | bytes 196624 | tf_op jit(solution)/shard_map/reduce_scatter | solution.py:49
  636.2 1.6 add_multiply_fusion.1
  637.9 45.1 %all-gather.8.cloned.1.call-done = f32[6144,64]{0,1:T(8,128)} async-done(((f32[768,64]{0,1:T(8,128)}), f32[6144,64]{0,1:T(8,128)}) %all-gather.8.cloned.1.call-update) | async-done | bytes 1572880 | tf_op jit(solution)/shard_map/all_gather | solution.py:42
  683.0 1.6 copy_bitcast_fusion
  684.6 4.4 gather_fusion.2
  689.0 36.0 %fusion.21 = f32[256,128,64]{1,2,0:T(8,128)S(1)} fusion(f32[256,128,128]{2,1,0:T(8,128)} %all-to-all-done.1, f32[256,128,64]{1,2,0:T(8,128)} %gather_fusion.2), kind=kOutput, calls=%fused_computation.51 | convolution fusion | flops 3221225472 | bytes 33554432 | tf_op jit(solution)/shard_map/sij,sjk->sik/dot_general | solution.py:44
  725.0 7.5 fusion
  732.5 1.0 copy.48
  734.1 21.6 %reduce-scatter.8.cloned.1.call-done = f32[768,64]{0,1:T(8,128)} async-done(((f32[3072,64]{0,1:T(8,128)}), f32[768,64]{0,1:T(8,128)}) %reduce-scatter.8.cloned.1.call-update) | async-done | bytes 196624 | tf_op jit(solution)/shard_map/reduce_scatter | solution.py:49
  755.7 1.7 multiply_reduce_fusion
  757.5 39.6 %all-reduce = (f32[64]{0:T(128)S(1)}, f32[]{:T(128)}) all-reduce(f32[64]{0:T(128)S(1)} %get-tuple-element.8, f32[]{:T(128)} %reduce_sum.32), channel_id=1, replica_groups=mesh['row'=8,'col'=4] {'row','col'}, use_global_device_ids=true, to_apply=%region_7.8 | all-reduce | flops 65 | bytes 520 | tf_op jit(solution)/shard_map/psum | solution.py:52
  797.1 1.2 broadcast_divide_fusion
  (37 shorter events, 6.4 us)
Async XLA Ops:
  11.7 45.9 %all-to-all-start = ((s32[32,8,1]{1,2,0:T(1,128)}), s32[32,8,1]{1,2,0:T(1,128)S(1)}, u32[]{:S(2)}, u32[]{:S(2)}) async-start(s32[32,8,1]{1,2,0:T(1,128)} %bitcast.4), calls=%async_computation | async-start | bytes 32768 | tf_op jit(solution)/shard_map/all_to_all | solution.py:33
  57.7 5.9 copy-start
  57.7 5.9 copy-start.1
  57.7 394.9 %all-to-all-start.1 = ((f32[256,128,128]{2,1,0:T(8,128)}), f32[256,128,128]{2,1,0:T(8,128)}, u32[]{:S(2)}, u32[]{:S(2)}) async-start(f32[256,128,128]{2,1,0:T(8,128)} %scatter_fusion), calls=%async_computation.1 | async-start | bytes 33554432 | tf_op jit(solution)/shard_map/all_to_all | solution.py:32
  63.5 132.3 %all-gather.4.cloned.1.call-start = ((), (), s32[]{:S(2)}) async-start(), calls=%async_computation.5 | async-start | bytes 1769472 | tf_op jit(solution)/shard_map/all_gather | solution.py:42
  64.3 452.2 %reduce-scatter.4.cloned.1.call-start = ((), (), s32[]{:S(2)}) async-start(), calls=%async_computation.6 | async-start | bytes 983040 | tf_op jit(solution)/shard_map/reduce_scatter | solution.py:49
  497.2 66.6 %all-gather.6.cloned.1.call-start = ((), (), s32[]{:S(2)}) async-start(), calls=%async_computation.7 | async-start | bytes 1769472 | tf_op jit(solution)/shard_map/all_gather | solution.py:42
  518.1 118.1 %reduce-scatter.6.cloned.1.call-start = ((), (), s32[]{:S(2)}) async-start(), calls=%async_computation.8 | async-start | bytes 983040 | tf_op jit(solution)/shard_map/reduce_scatter | solution.py:49
  613.9 69.1 %all-gather.8.cloned.1.call-start = ((), (), s32[]{:S(2)}) async-start(), calls=%async_computation.9 | async-start | bytes 1769472 | tf_op jit(solution)/shard_map/all_gather | solution.py:42
  637.8 117.9 %reduce-scatter.8.cloned.1.call-start = ((), (), s32[]{:S(2)}) async-start(), calls=%async_computation.10 | async-start | bytes 983040 | tf_op jit(solution)/shard_map/reduce_scatter | solution.py:49
  724.9 8.6 %copy-start.2 = (f32[768]{0:T(1024)S(1)}, f32[768]{0:T(1024)}, u32[]{:S(2)}) copy-start(f32[768]{0:T(1024)} %param.15) | copy-start | bytes 9220
Sparse Core Ops, SparseCore 0:
  67.1 128.6 all-gather.3
  497.3 19.1 reduce-scatter.3
  519.5 44.2 all-gather.5
  614.1 22.0 reduce-scatter.5
  638.8 44.1 all-gather.7
  733.6 22.0 reduce-scatter.7
where the time goes:
time: 814 us; the launch traced here: 805 us
  waiting for transfers between devices  535 us (66%)
  matrix products  130 us (16%)
  local copies, waits for them, and re-layouts  54.4 us (7%)
  blocking collectives  39.6 us (5%)
  other arithmetic  17.3 us (2%)
  between operations  15.2 us (2%)
  starting transfers between devices  13.4 us (2%)
    all_to_all x1, waiting for transfers between devices, shards(): lax.all_to_all(payload, ('row', 'col'), split_axis=0, concat_axis=0, tile...  251 us
    all_gather x3, waiting for transfers between devices, shards(): panel = lax.all_gather(mode_flux, 'row', axis=0, tiled=True)  221 us
    dot_general x3, matrix products, shards(): jnp.einsum('sij,sjk->sik', got_values, picked, precision=lax.Precision.HI...  108 us
    reduce_scatter x3, waiting for transfers between devices, shards(): lax.psum_scatter(partial_sum, 'col', scatter_dimension=0, tiled=True)  63 us
    psum x1, blocking collectives, shards(): lax.psum((weighted_local, jnp.sum(heat_weight)), ('row', 'col'))  39.6 us
    scatter x1, local copies, waits for them, and re-layouts, shards(): payload.at[target].set(jnp.where(is_used[:, None, None], tile_values, 0.0))  23.5 us
    dot_general x3, matrix products, shards(): jnp.einsum('rs,sik->rik', row_onehot, products, precision=lax.Precision.H...  22.5 us
  transfers between devices with their start and end apart: 8, of which 7 were waited for; matrix products, arithmetic and copies ran while one was open for 6% of the time, Pallas kernels for 0%

commit v1 on v0

v1 whole, which is shorter than its diff:
```python
import functools

import jax
import jax.numpy as jnp
from jax import lax
from jax.experimental import pallas as pl
from jax.experimental.pallas import tpu as pltpu
from jax.sharding import Mesh
from jax.sharding import PartitionSpec as P

ITERS = 3
CORES = 2
STEP = 16
UNROLL = 8
CHIPS = ("row", "x")
ALL = ("row", "x", "core")
DIMS = (((1,), (1,)), ((), ()))


def apply_kernel(length, row_ref, col_ref, used_ref, flux_ref, own_ref, other_ref, out_ref):
    step = pl.program_id(0)

    @pl.when(step == 0)
    def _():
        out_ref[...] = jnp.zeros_like(out_ref)

    def add_tile(tile, slot):
        flux = flux_ref[col_ref[slot]] * used_ref[slot]
        tile_high = tile.astype(jnp.bfloat16)
        tile_low = (tile - tile_high.astype(jnp.float32)).astype(jnp.bfloat16)
        flux_high = flux.astype(jnp.bfloat16)
        flux_low = (flux - flux_high.astype(jnp.float32)).astype(jnp.bfloat16)
        both = lax.dot_general(
            jnp.concatenate([flux_high, flux_low], axis=0),
            tile_high,
            DIMS,
            preferred_element_type=jnp.float32,
        )
        low = lax.dot_general(flux_high, tile_low, DIMS, preferred_element_type=jnp.float32)
        temps = flux.shape[0]
        out_ref[row_ref[slot]] += both[:temps] + (both[temps:] + low)

    for part, ref in enumerate((own_ref, other_ref)):
        base = part * length + step * STEP

        @pl.loop(0, STEP // UNROLL)
        def _(group):
            for k in range(UNROLL):
                add_tile(ref[group * UNROLL + k], base + group * UNROLL + k)


def apply_tiles(row, col, used, flux, own, other):
    length, size, _ = own.shape
    num, temps, _ = flux.shape
    whole = pl.BlockSpec((num, temps, size), lambda i, *_: (0, 0, 0))
    some = pl.BlockSpec((STEP, size, size), lambda i, *_: (i, 0, 0))
    return pl.pallas_call(
        functools.partial(apply_kernel, length),
        out_shape=jax.ShapeDtypeStruct(flux.shape, jnp.float32),
        grid_spec=pltpu.PrefetchScalarGridSpec(
            num_scalar_prefetch=3,
            grid=(length // STEP,),
            in_specs=[whole, some, some],
            out_specs=whole,
        ),
        compiler_params=pltpu.CompilerParams(vmem_limit_bytes=40 * 1024 * 1024),
        cost_estimate=pl.CostEstimate(
            flops=2 * 2 * length * size * size * temps * 3,
            bytes_accessed=4 * (2 * length * size * size + 2 * num * temps * size),
            transcendentals=0,
        ),
    )(row, col, used, flux, own, other)


def shards(
    tile_values, tile_owner, tile_row, tile_col, tile_count, relaxation, driving, heat_weight
):
    n_cols = lax.axis_size("x") * CORES
    n_rows = lax.axis_size("row")
    length, size, _ = tile_values.shape
    modes, columns = driving.shape
    per = modes // size
    num = n_rows * n_cols * per
    half = columns // CORES
    core = lax.axis_index("core")
    swap = [(0, 1), (1, 0)]

    other_values = lax.ppermute(tile_values, "core", swap)
    owners = tile_owner[:, 0]
    row = (owners // n_cols) * (n_cols * per) + tile_row
    col = ((tile_col // per) * n_cols + owners % n_cols) * per + tile_col % per
    used = jnp.arange(length, dtype=jnp.int32) < tile_count[0]
    places = jnp.where(used, row * num + col, -1)
    places = jnp.concatenate([places, lax.ppermute(places, "core", swap)])
    is_used = places >= 0
    places = jnp.where(is_used, places, 0)
    row, col, used = places // num, places % num, is_used.astype(jnp.float32)

    def by_core(own, other):
        return jnp.concatenate(
            [jnp.where(core == 0, own, other), jnp.where(core == 0, other, own)], axis=0
        )

    drive = jnp.transpose(driving.reshape(per, size, columns), (0, 2, 1))
    relax = relaxation.reshape(per, 1, size)
    low, high = drive[:, :half], drive[:, half:]
    mine = jnp.where(core == 0, low, high)
    theirs = jnp.where(core == 0, high, low)
    packed = jnp.concatenate([theirs, jnp.broadcast_to(relax, (per, 8, size))], axis=1)
    got = lax.ppermute(packed, "core", swap)
    drive_half = by_core(mine, got[:, :half])
    relax_both = by_core(relax, got[:, half : half + 1])

    flux = relax_both * drive_half
    for sweep in range(ITERS):
        panel = lax.all_gather(flux, CHIPS, axis=0, tiled=True)
        partial_sum = apply_tiles(row, col, used, panel, tile_values, other_values)
        summed = lax.psum_scatter(partial_sum, CHIPS, scatter_dimension=0, tiled=True)
        flux = relax_both * (drive_half + summed)
    first, second = flux[:per], flux[per:]
    mine = jnp.where(core == 0, first, second)
    got = lax.ppermute(jnp.where(core == 0, second, first), "core", swap)
    both = jnp.concatenate(
        [jnp.where(core == 0, mine, got), jnp.where(core == 0, got, mine)], axis=1
    )
    mode_flux = jnp.transpose(both, (0, 2, 1)).reshape(modes, columns)
    weighted_local = jnp.sum(heat_weight[:, None] * mode_flux, axis=0)
    weighted, weight_sum = lax.psum((weighted_local, jnp.sum(heat_weight)), ALL)
    return (mode_flux, weighted / weight_sum)


def solution(mesh):
    n_rows, n_cols = mesh.shape["row"], mesh.shape["col"]
    chips = Mesh(mesh.devices.reshape(n_rows, n_cols // CORES, CORES), ALL)
    placed = (
        P(ALL, None, None),
        P(ALL, None),
        P(ALL),
        P(ALL),
        P(ALL),
        P(ALL),
        P(ALL, None),
        P(ALL),
    )
    return jax.shard_map(
        shards,
        mesh=chips,
        in_specs=placed,
        out_specs=(P(ALL, None), P()),
        check_vma=False,
    )
```

time: 814 us -> 732 us (0.90); the launches traced: 805 us -> 732 us
  matrix products: 130 us -> 0 us
  waiting for transfers between devices: 535 us -> 606 us
  Pallas kernels: 0 us -> 53.1 us
  local copies, waits for them, and re-layouts: 54.4 us -> 7.44 us
  starting transfers between devices: 13.4 us -> 1.79 us
  other arithmetic: 17.3 us -> 8.35 us
    reduce_scatter x3, waiting for transfers between devices: 63 us -> 387 us  [shards(): lax.psum_scatter(partial_sum, CHIPS, scatter_dimension=0, tiled=True)]
    all_to_all x2 -> x0, waiting for transfers between devices: 251 us -> none  [the longest x1 251 us: shards(): lax.all_to_all(payload, ('row', 'col'), split_axis=0, concat_axis=0, tile...]
    dot_general x6 -> x0, matrix products: 130 us -> none  [the longest x3 108 us: shards(): jnp.einsum('sij,sjk->sik', got_values, picked, precision=lax.Precision.HI...]
    pallas_call x0 -> x3, Pallas kernels: none -> 53.1 us  [apply_tiles(): pl.pallas_call(functools.partial(apply_kernel, length), out_shape=jax.Sha...]
    scatter x2 -> x0, local copies, waits for them, and re-layouts: 24.5 us -> none  [the longest x1 23.5 us: shards(): payload.at[target].set(jnp.where(is_used[:, None, None], tile_values, 0.0))]
    all_gather x3, waiting for transfers between devices: 221 us -> 206 us  [shards(): panel = lax.all_gather(flux, CHIPS, axis=0, tiled=True)]
    all_to_all x2 -> x0, starting transfers between devices: 13.1 us -> none  [the longest x1 7.3 us: shards(): lax.all_to_all(labels, ('row', 'col'), split_axis=0, concat_axis=0, tiled...]
    gather x3 -> x0, local copies, waits for them, and re-layouts: 13.1 us -> none  [shards(): picked = panel.reshape(col_tiles, tile_size, columns)[col_index]]
  transfers between devices with their start and end apart: 8 -> 10, of which waited for: 7 -> 9; matrix products, arithmetic and copies ran while one was open for 6% -> 0% of each run, Pallas kernels for 0% -> 0%
where the time goes in v1:
time: 732 us
  waiting for transfers between devices  606 us (83%)
  Pallas kernels  53.1 us (7%)
  blocking collectives  40.5 us (6%)
  between operations  14.8 us (2%)
  other arithmetic  8.35 us (1%)
  local copies, waits for them, and re-layouts  7.44 us (1%)
    reduce_scatter x3, waiting for transfers between devices, shards(): lax.psum_scatter(partial_sum, CHIPS, scatter_dimension=0, tiled=True)  387 us
    all_gather x3, waiting for transfers between devices, shards(): panel = lax.all_gather(flux, CHIPS, axis=0, tiled=True)  206 us
    pallas_call x3, Pallas kernels, apply_tiles(): pl.pallas_call(functools.partial(apply_kernel, length), out_shape=jax.Sha...  53.1 us
    psum x1, blocking collectives, shards(): weighted, weight_sum = lax.psum((weighted_local, jnp.sum(heat_weight)), ALL)  40.5 us
  transfers between devices with their start and end apart: 10, of which 9 were waited for; matrix products, arithmetic and copies ran while one was open for 0% of the time, Pallas kernels for 0%

profile of v1, /device:TPU:0, one launch (start us, length us, event | category | flops | bytes accessed | tf_op | source)
XLA Modules:
  0.0 731.6 jit_solution(8147218175837710640)
XLA Ops:
  7.2 0.5 collective-permute-start.2
  7.7 0.4 copy-done
  8.1 0.7 broadcast_in_dim.13
  8.8 0.5 collective-permute-start
  9.4 0.7 reshape.20
  10.1 10.6 %collective-permute-done = f32[6,40,128]{2,1,0:T(8,128)S(1)} collective-permute-done((f32[6,40,128]{2,1,0:T(8,128)S(1)}, f32[6,40,128]{2,1,0:T(8,128)S(1)}, u32[]{:S(2)}, u32[]{:S(2)}) %collective-permute-start) | collective-permute-done | bytes 122912 | tf_op jit(solution)/shard_map/ppermute | solution.py:110
  20.8 0.7 broadcast_multiply_fusion
  22.2 0.7 compare_select_fusion.1
  22.9 0.4 collective-permute-start.1
  23.3 0.8 collective-permute-done.1
  24.2 68.2 %all-gather.4.cloned.1.call-done.flux_ref = f32[192,32,128]{2,1,0:T(8,128)} async-done(((f32[12,32,128]{2,1,0:T(8,128)}), f32[192,32,128]{2,1,0:T(8,128)}) %all-gather.4.cloned.1.call-update) | async-done | bytes 3145744 | tf_op jit(solution)/shard_map/all_gather | solution.py:116
  92.4 1.9 copy-done.1
  94.3 17.7 %shard_map.95 = f32[192,32,128]{2,1,0:T(8,128)} custom-call(s32[256]{0:T(256)S(1)} %get-tuple-element.11.row_ref, s32[256]{0:T(256)S(1)} %get-tuple-element.10.col_ref, f32[256]{0:T(256)S(1)} %compare_convert_fusion.used_ref, f32[192,32,128]{2,1,0:T(8,128)S(1)} %copy-done.1, f32[128,128,128]{2,1,0:T(8,128)} %own_ref.5, ...), custom_call_target="tpu_custom_call" | custom-call | flops 805306368 | bytes 23068672 | tf_op jit(solution)/shard_map/pallas_call | solution.py:57
  112.1 129.0 %reduce-scatter.4.cloned.1.call-done = f32[12,32,128]{2,1,0:T(8,128)} async-done(((f32[192,32,128]{2,1,0:T(8,128)}), f32[12,32,128]{2,1,0:T(8,128)}) %reduce-scatter.4.cloned.1.call-update) | async-done | bytes 196624 | tf_op jit(solution)/shard_map/reduce_scatter | solution.py:118
  241.1 1.6 add_multiply_fusion.2
  242.8 69.1 %all-gather.6.cloned.1.call-done.flux_ref = f32[192,32,128]{2,1,0:T(8,128)} async-done(((f32[12,32,128]{2,1,0:T(8,128)}), f32[192,32,128]{2,1,0:T(8,128)}) %all-gather.6.cloned.1.call-update) | async-done | bytes 3145744 | tf_op jit(solution)/shard_map/all_gather | solution.py:116
  311.9 1.9 copy-done.3
  313.8 17.7 %shard_map.96 = f32[192,32,128]{2,1,0:T(8,128)} custom-call(s32[256]{0:T(256)S(1)} %get-tuple-element.11.row_ref, s32[256]{0:T(256)S(1)} %get-tuple-element.10.col_ref, f32[256]{0:T(256)S(1)} %compare_convert_fusion.used_ref, f32[192,32,128]{2,1,0:T(8,128)S(1)} %copy-done.3, f32[128,128,128]{2,1,0:T(8,128)} %own_ref.5, ...), custom_call_target="tpu_custom_call" | custom-call | flops 805306368 | bytes 23068672 | tf_op jit(solution)/shard_map/pallas_call | solution.py:57
  331.6 129.0 %reduce-scatter.6.cloned.1.call-done = f32[12,32,128]{2,1,0:T(8,128)} async-done(((f32[192,32,128]{2,1,0:T(8,128)}), f32[12,32,128]{2,1,0:T(8,128)}) %reduce-scatter.6.cloned.1.call-update) | async-done | bytes 196624 | tf_op jit(solution)/shard_map/reduce_scatter | solution.py:118
  460.6 1.6 add_multiply_fusion.1
  462.4 68.8 %all-gather.8.cloned.1.call-done.flux_ref = f32[192,32,128]{2,1,0:T(8,128)} async-done(((f32[12,32,128]{2,1,0:T(8,128)}), f32[192,32,128]{2,1,0:T(8,128)}) %all-gather.8.cloned.1.call-update) | async-done | bytes 3145744 | tf_op jit(solution)/shard_map/all_gather | solution.py:116
  531.2 1.9 copy-done.2
  533.1 17.7 %shard_map.97 = f32[192,32,128]{2,1,0:T(8,128)} custom-call(s32[256]{0:T(256)S(1)} %get-tuple-element.11.row_ref, s32[256]{0:T(256)S(1)} %get-tuple-element.10.col_ref, f32[256]{0:T(256)S(1)} %compare_convert_fusion.used_ref, f32[192,32,128]{2,1,0:T(8,128)S(1)} %copy-done.2, f32[128,128,128]{2,1,0:T(8,128)} %own_ref.5, ...), custom_call_target="tpu_custom_call" | custom-call | flops 805306368 | bytes 23068672 | tf_op jit(solution)/shard_map/pallas_call | solution.py:57
  550.8 129.0 %reduce-scatter.8.cloned.1.call-done = f32[12,32,128]{2,1,0:T(8,128)} async-done(((f32[192,32,128]{2,1,0:T(8,128)}), f32[12,32,128]{2,1,0:T(8,128)}) %reduce-scatter.8.cloned.1.call-update) | async-done | bytes 196624 | tf_op jit(solution)/shard_map/reduce_scatter | solution.py:118
  679.9 1.0 add_multiply_fusion
  680.9 0.1 collective-permute-start.3
  681.0 0.6 reduce_sum.19
  681.6 0.7 collective-permute-done.3
  682.3 0.7 copy_bitcast_fusion
  683.0 0.1 fusion
  683.1 40.5 %all-reduce = (f32[64]{0:T(128)S(1)}, f32[]{:T(128)}) all-reduce(f32[64]{0:T(128)S(1)} %fusion, f32[]{:T(128)} %reduce_sum.19), channel_id=1, replica_groups=mesh['row'=8,'x'=2,'core'=2] {'row','x','core'}, use_global_device_ids=true, to_apply=%region_4.5 | all-reduce | flops 65 | bytes 520 | tf_op jit(solution)/shard_map/psum | solution.py:128
  723.6 1.1 broadcast_divide_fusion
  (30 shorter events, 0.5 us)
Async XLA Ops:
  7.2 0.9 copy-start
  7.2 85.2 %all-gather.4.cloned.1.call-start = ((), (), s32[]{:S(2)}) async-start(), calls=%async_computation.3 | async-start | bytes 3342336 | tf_op jit(solution)/shard_map/all_gather | solution.py:116
  7.2 85.2 %collective-permute-start.2 = (f32[128,128,128]{2,1,0:T(8,128)}, f32[128,128,128]{2,1,0:T(8,128)}, u32[]{:S(2)}, u32[]{:S(2)}) collective-permute-start(f32[128,128,128]{2,1,0:T(8,128)} %own_ref.5), channel_id=1, source_target_pairs={{0,1},{1,0},{2,3},{3,2},{4,5},{5,4},{6,7},{7,6},{8,9},{9,8},{10,11... | collective-permute-start | bytes 25165832 | tf_op jit(solution)/shard_map/ppermute | solution.py:88
  8.8 11.9 %collective-permute-start = (f32[6,40,128]{2,1,0:T(8,128)S(1)}, f32[6,40,128]{2,1,0:T(8,128)S(1)}, u32[]{:S(2)}, u32[]{:S(2)}) collective-permute-start(f32[6,40,128]{2,1,0:T(8,128)S(1)} %pad_maximum_fusion.2), channel_id=1, source_target_pairs={{0,1},{1,0},{2,3},{3,2},{4,5},{5,4},{6,7},{7,6},{8,9},{9,8},{10,11... | collective-permute-start | bytes 368648 | tf_op jit(solution)/shard_map/ppermute | solution.py:110
  21.5 219.6 %reduce-scatter.4.cloned.1.call-start = ((), (), s32[]{:S(2)}) async-start(), calls=%async_computation.4 | async-start | bytes 3342336 | tf_op jit(solution)/shard_map/reduce_scatter | solution.py:118
  22.9 1.3 collective-permute-start.1
  92.4 1.9 copy-start.1
  112.0 199.9 %all-gather.6.cloned.1.call-start = ((), (), s32[]{:S(2)}) async-start(), calls=%async_computation.5 | async-start | bytes 3342336 | tf_op jit(solution)/shard_map/all_gather | solution.py:116
  242.7 217.9 %reduce-scatter.6.cloned.1.call-start = ((), (), s32[]{:S(2)}) async-start(), calls=%async_computation.6 | async-start | bytes 3342336 | tf_op jit(solution)/shard_map/reduce_scatter | solution.py:118
  311.9 1.9 copy-start.3
  331.5 199.7 %all-gather.8.cloned.1.call-start = ((), (), s32[]{:S(2)}) async-start(), calls=%async_computation.7 | async-start | bytes 3342336 | tf_op jit(solution)/shard_map/all_gather | solution.py:116
  462.3 217.6 %reduce-scatter.8.cloned.1.call-start = ((), (), s32[]{:S(2)}) async-start(), calls=%async_computation.8 | async-start | bytes 3342336 | tf_op jit(solution)/shard_map/reduce_scatter | solution.py:118
  531.2 1.9 copy-start.2
  550.8 130.1 %copy-start.4 = (f32[768]{0:T(1024)S(1)}, f32[768]{0:T(1024)}, u32[]{:S(2)}) copy-start(f32[768]{0:T(1024)} %param.15) | copy-start | bytes 9220
  680.9 1.4 collective-permute-start.3
Sparse Core Ops, SparseCore 0:
  21.6 70.7 all-gather.3
  112.2 128.8 reduce-scatter.3
  244.4 67.4 all-gather.5
  331.7 128.9 reduce-scatter.5
  463.8 67.3 all-gather.7
  551.0 128.8 reduce-scatter.7

commit v2 on v1

--- a/solution.py
+++ b/solution.py
@@ -15,14 +15,70 @@
 CHIPS = ("row", "x")
 ALL = ("row", "x", "core")
 DIMS = (((1,), (1,)), ((), ()))
-
-
-def apply_kernel(length, row_ref, col_ref, used_ref, flux_ref, own_ref, other_ref, out_ref):
+ORDERS = (("z", "x", "y"), ("z", "y", "x"), ("x", "y", "z"))
+
+
+def sizes_of(n_rows, n_x):
+    y = max(n for n in range(1, n_rows + 1) if n_rows % n == 0 and n * n <= n_rows)
+    return {"z": n_rows // y, "y": y, "x": n_x}
+
+
+def chip_of(sizes, z, y, x):
+    return (z * sizes["y"] + y) * sizes["x"] + x
+
+
+def shift(sizes, array, axis, by):
+    pairs = []
+    for z in range(sizes["z"]):
+        for y in range(sizes["y"]):
+            for x in range(sizes["x"]):
+                at = {"z": z, "y": y, "x": x}
+                to = dict(at, **{axis: (at[axis] + by) % sizes[axis]})
+                pairs.append((chip_of(sizes, **at), chip_of(sizes, **to)))
+    return lax.ppermute(array, CHIPS, pairs)
+
+
+def gather(sizes, block, order):
+    for axis in order[:-1]:
+        block = jnp.concatenate(
+            [block] + [shift(sizes, block, axis, j) for j in range(1, sizes[axis])], axis=0
+        )
+    axis = order[-1]
+    return [block] + [shift(sizes, block, axis, j) for j in range(1, sizes[axis])]
+
+
+def reduce(sizes, pieces, order):
+    for place in range(len(order) - 1, -1, -1):
+        axis = order[place]
+        got = [shift(sizes, pieces[j], axis, j) for j in range(1, sizes[axis])]
+        if place == 0:
+            return sum(got, pieces[0])
+        count = sizes[order[place - 1]]
+        length = pieces[0].shape[0] // count
+        pieces = [
+            sum([g[k * length : (k + 1) * length] for g in got], pieces[0][k * length : (k + 1) * length])
+            for k in range(count)
+        ]
+
+
+def apply_kernel(length, counts, row_ref, col_ref, used_ref, own_ref, other_ref, *refs):
     step = pl.program_id(0)
+    pieces = len(counts)
+    given, outs = refs[:pieces], refs[pieces : 2 * pieces]
+    flux_ref, sum_ref, sem = refs[2 * pieces :]
+    starts = [sum(counts[:k]) for k in range(pieces)]
 
     @pl.when(step == 0)
     def _():
-        out_ref[...] = jnp.zeros_like(out_ref)
+        copies = [
+            pltpu.make_async_copy(given[k], flux_ref.at[pl.ds(starts[k], counts[k])], sem.at[k])
+            for k in range(pieces)
+        ]
+        for copy in copies:
+            copy.start()
+        sum_ref[...] = jnp.zeros_like(sum_ref)
+        for copy in copies:
+            copy.wait()
 
     def add_tile(tile, slot):
         flux = flux_ref[col_ref[slot]] * used_ref[slot]
@@ -38,7 +94,7 @@
         )
         low = lax.dot_general(flux_high, tile_low, DIMS, preferred_element_type=jnp.float32)
         temps = flux.shape[0]
-        out_ref[row_ref[slot]] += both[:temps] + (both[temps:] + low)
+        sum_ref[row_ref[slot]] += both[:temps] + (both[temps:] + low)
 
     for part, ref in enumerate((own_ref, other_ref)):
         base = part * length + step * STEP
@@ -48,20 +104,38 @@
             for k in range(UNROLL):
                 add_tile(ref[group * UNROLL + k], base + group * UNROLL + k)
 
-
-def apply_tiles(row, col, used, flux, own, other):
+    @pl.when(step == pl.num_programs(0) - 1)
+    def _():
+        copies = [
+            pltpu.make_async_copy(sum_ref.at[pl.ds(starts[k], counts[k])], outs[k], sem.at[k])
+            for k in range(pieces)
+        ]
+        for copy in copies:
+            copy.start()
+        for copy in copies:
+            copy.wait()
+
+
+def apply_tiles(row, col, used, own, other, pieces):
     length, size, _ = own.shape
-    num, temps, _ = flux.shape
-    whole = pl.BlockSpec((num, temps, size), lambda i, *_: (0, 0, 0))
+    counts = [piece.shape[0] for piece in pieces]
+    temps = pieces[0].shape[1]
+    num = sum(counts)
     some = pl.BlockSpec((STEP, size, size), lambda i, *_: (i, 0, 0))
+    anywhere = pl.BlockSpec(memory_space=pl.ANY)
     return pl.pallas_call(
-        functools.partial(apply_kernel, length),
-        out_shape=jax.ShapeDtypeStruct(flux.shape, jnp.float32),
+        functools.partial(apply_kernel, length, counts),
+        out_shape=[jax.ShapeDtypeStruct(piece.shape, jnp.float32) for piece in pieces],
         grid_spec=pltpu.PrefetchScalarGridSpec(
             num_scalar_prefetch=3,
             grid=(length // STEP,),
-            in_specs=[whole, some, some],
-            out_specs=whole,
+            in_specs=[some, some] + [anywhere] * len(pieces),
+            out_specs=[anywhere] * len(pieces),
+            scratch_shapes=[
+                pltpu.VMEM((num, temps, size), jnp.float32),
+                pltpu.VMEM((num, temps, size), jnp.float32),
+                pltpu.SemaphoreType.DMA((len(pieces),)),
+            ],
         ),
         compiler_params=pltpu.CompilerParams(vmem_limit_bytes=40 * 1024 * 1024),
         cost_estimate=pl.CostEstimate(
@@ -69,7 +143,7 @@
             bytes_accessed=4 * (2 * length * size * size + 2 * num * temps * size),
             transcendentals=0,
         ),
-    )(row, col, used, flux, own, other)
+    )(row, col, used, own, other, *pieces)
 
 
 def shards(
@@ -77,20 +151,46 @@
 ):
     n_cols = lax.axis_size("x") * CORES
     n_rows = lax.axis_size("row")
+    sizes = sizes_of(n_rows, n_cols // CORES)
     length, size, _ = tile_values.shape
     modes, columns = driving.shape
     per = modes // size
+    chip_tiles = CORES * per
     num = n_rows * n_cols * per
     half = columns // CORES
     core = lax.axis_index("core")
+    row_at = lax.axis_index("row")
+    here = {"z": row_at // sizes["y"], "y": row_at % sizes["y"], "x": lax.axis_index("x")}
     swap = [(0, 1), (1, 0)]
+
+    last = chip_tiles // 4
+    first = (chip_tiles - last) // 2
+    bounds = (0, first, chip_tiles - last, chip_tiles)
+    parts = [(bounds[k], bounds[k + 1]) for k in range(len(ORDERS))]
+
+    def place(tile, sign):
+        chip, inside = tile // chip_tiles, tile % chip_tiles
+        at = {
+            "z": chip // (sizes["y"] * sizes["x"]),
+            "y": (chip // sizes["x"]) % sizes["y"],
+            "x": chip % sizes["x"],
+        }
+        away = {a: (sign * (at[a] - here[a]) + sizes[a]) % sizes[a] for a in sizes}
+        out = jnp.zeros_like(tile)
+        chips = n_rows * n_cols // CORES
+        for order, (low, high) in zip(ORDERS, parts):
+            inner, middle, outer = order
+            slot = (away[outer] * sizes[middle] + away[middle]) * sizes[inner] + away[inner]
+            slot = chips * low + slot * (high - low) + inside - low
+            out = jnp.where((inside >= low) & (inside < high), slot, out)
+        return out
 
     other_values = lax.ppermute(tile_values, "core", swap)
     owners = tile_owner[:, 0]
     row = (owners // n_cols) * (n_cols * per) + tile_row
     col = ((tile_col // per) * n_cols + owners % n_cols) * per + tile_col % per
     used = jnp.arange(length, dtype=jnp.int32) < tile_count[0]
-    places = jnp.where(used, row * num + col, -1)
+    places = jnp.where(used, place(row, 1) * num + place(col, -1), -1)
     places = jnp.concatenate([places, lax.ppermute(places, "core", swap)])
     is_used = places >= 0
     places = jnp.where(is_used, places, 0)
@@ -111,12 +211,18 @@
     drive_half = by_core(mine, got[:, :half])
     relax_both = by_core(relax, got[:, half : half + 1])
 
-    flux = relax_both * drive_half
+    drives = [drive_half[a:b] for a, b in parts]
+    relaxes = [relax_both[a:b] for a, b in parts]
+    fluxes = [r * d for r, d in zip(relaxes, drives)]
     for sweep in range(ITERS):
-        panel = lax.all_gather(flux, CHIPS, axis=0, tiled=True)
-        partial_sum = apply_tiles(row, col, used, panel, tile_values, other_values)
-        summed = lax.psum_scatter(partial_sum, CHIPS, scatter_dimension=0, tiled=True)
-        flux = relax_both * (drive_half + summed)
+        pieces = [gather(sizes, flux, order) for flux, order in zip(fluxes, ORDERS)]
+        sums = apply_tiles(row, col, used, tile_values, other_values, sum(pieces, []))
+        fluxes, done = [], 0
+        for order, piece, d, r in zip(ORDERS, pieces, drives, relaxes):
+            summed = reduce(sizes, sums[done : done + len(piece)], order)
+            done += len(piece)
+            fluxes.append(r * (d + summed))
+    flux = jnp.concatenate(fluxes, axis=0)
     first, second = flux[:per], flux[per:]
     mine = jnp.where(core == 0, first, second)
     got = lax.ppermute(jnp.where(core == 0, second, first), "core", swap)

time: 732 us -> 408 us (0.56)
  waiting for transfers between devices: 606 us -> 164 us
  starting transfers between devices: 1.79 us -> 136 us
  between operations: 14.8 us -> 1.78 us
    reduce_scatter x3 -> x0, waiting for transfers between devices: 387 us -> none  [shards(): lax.psum_scatter(partial_sum, CHIPS, scatter_dimension=0, tiled=True)]
    all_gather x3 -> x0, waiting for transfers between devices: 206 us -> none  [shards(): panel = lax.all_gather(flux, CHIPS, axis=0, tiled=True)]
    ppermute x0 -> x90, waiting for transfers between devices: none -> 152 us  [shift(): return lax.ppermute(array, CHIPS, pairs)]
    ppermute x0 -> x90, starting transfers between devices: none -> 135 us  [shift(): return lax.ppermute(array, CHIPS, pairs)]
  transfers between devices with their start and end apart: 10 -> 94, of which waited for: 9 -> 50; matrix products, arithmetic and copies ran while one was open for 0% -> 1% of each run, Pallas kernels for 0% -> 0%
where the time goes in v2:
time: 408 us; the launch traced here: 407 us
  waiting for transfers between devices  164 us (40%)
  starting transfers between devices  136 us (33%)
  Pallas kernels  58.3 us (14%)
  blocking collectives  40.1 us (10%)
  other arithmetic  4.84 us (1%)
    ppermute x90, waiting for transfers between devices, shift(): return lax.ppermute(array, CHIPS, pairs)  152 us
    ppermute x90, starting transfers between devices, shift(): return lax.ppermute(array, CHIPS, pairs)  135 us
    pallas_call x3, Pallas kernels, apply_tiles(): pl.pallas_call(functools.partial(apply_kernel, length, counts), out_shape...  58.3 us
    psum x1, blocking collectives, shards(): weighted, weight_sum = lax.psum((weighted_local, jnp.sum(heat_weight)), ALL)  40.1 us
    ppermute x1, waiting for transfers between devices, shards(): got = lax.ppermute(packed, 'core', swap)  9.94 us
  transfers between devices with their start and end apart: 94, of which 50 were waited for; matrix products, arithmetic and copies ran while one was open for 1% of the time, Pallas kernels for 0%

profile of v2, /device:TPU:0, one launch (start us, length us, event | category | flops | bytes accessed | tf_op | source)
XLA Modules:
  0.0 407.3 jit_solution(17673805189487837144)
XLA Ops:
  4.2 9.9 %collective-permute-done = f32[6,40,128]{2,1,0:T(8,128)S(1)} collective-permute-done((f32[6,40,128]{2,1,0:T(8,128)S(1)}, f32[6,40,128]{2,1,0:T(8,128)S(1)}, u32[]{:S(2)}, u32[]{:S(2)}) %collective-permute-start) | collective-permute-done | bytes 122912 | tf_op jit(solution)/shard_map/ppermute | solution.py:210
  14.2 5.0 %collective-permute-start.10 = (f32[5,32,128]{2,1,0:T(8,128)S(1)}, f32[5,32,128]{2,1,0:T(8,128)S(1)}, u32[]{:S(2)}, u32[]{:S(2)}) collective-permute-start(f32[5,32,128]{2,1,0:T(8,128)S(1)} %get-tuple-element.61), channel_id=1, source_target_pairs={{0,24},{2,26},{4,28},{6,30},{8,0},{10,2},{12,4},{14,6},{16,8},{18,... | collective-permute-start | bytes 245768 | tf_op jit(solution)/shard_map/ppermute | solution.py:38
  24.4 3.4 collective-permute-start.3
  31.5 4.5 %collective-permute-done.4 = f32[4,32,128]{2,1,0:T(8,128)S(1)} collective-permute-done((f32[4,32,128]{2,1,0:T(8,128)S(1)}, f32[4,32,128]{2,1,0:T(8,128)S(1)}, u32[]{:S(2)}, u32[]{:S(2)}) %collective-permute-start.4) | collective-permute-done | bytes 65568 | tf_op jit(solution)/shard_map/ppermute | solution.py:38
  36.8 3.4 collective-permute-done.5
  44.0 8.9 %collective-permute-done.11 = f32[20,32,128]{2,1,0:T(8,128)S(1)} collective-permute-done((f32[20,32,128]{2,1,0:T(8,128)S(1)}, f32[20,32,128]{2,1,0:T(8,128)S(1)}, u32[]{:S(2)}, u32[]{:S(2)}) %collective-permute-start.11) | collective-permute-done | bytes 327712 | tf_op jit(solution)/shard_map/ppermute | solution.py:38
  57.2 4.8 %collective-permute-done.15.refs_5_ = f32[12,32,128]{2,1,0:T(8,128)S(1)} collective-permute-done((f32[12,32,128]{2,1,0:T(8,128)S(1)}, f32[12,32,128]{2,1,0:T(8,128)S(1)}, u32[]{:S(2)}, u32[]{:S(2)}) %collective-permute-start.15) | collective-permute-done | bytes 196640 | tf_op jit(solution)/shard_map/ppermute | solution.py:38
  62.1 7.8 %collective-permute-done.16.refs_6_ = f32[12,32,128]{2,1,0:T(8,128)S(1)} collective-permute-done((f32[12,32,128]{2,1,0:T(8,128)S(1)}, f32[12,32,128]{2,1,0:T(8,128)S(1)}, u32[]{:S(2)}, u32[]{:S(2)}) %collective-permute-start.16) | collective-permute-done | bytes 196640 | tf_op jit(solution)/shard_map/ppermute | solution.py:38
  71.6 19.4 %shard_map.95 = (f32[32,32,128]{2,1,0:T(8,128)S(1)}, f32[32,32,128]{2,1,0:T(8,128)S(1)}, f32[40,32,128]{2,1,0:T(8,128)S(1)}, f32[40,32,128]{2,1,0:T(8,128)S(1)},...) custom-call(s32[256]{0:T(256)S(1)} %get-tuple-element.108.row_ref, ...), custom_call_target="tpu_custom_call" | custom-call | flops 805306368 | bytes 23068672 | tf_op jit(solution)/shard_map/pallas_call | solution.py:126
  92.4 3.0 collective-permute-start.38
  102.1 7.2 %collective-permute-done.39 = f32[12,32,128]{2,1,0:T(8,128)S(1)} collective-permute-done((f32[12,32,128]{2,1,0:T(8,128)S(1)}, f32[12,32,128]{2,1,0:T(8,128)S(1)}, u32[]{:S(2)}, u32[]{:S(2)}) %collective-permute-start.39) | collective-permute-done | bytes 196640 | tf_op jit(solution)/shard_map/ppermute | solution.py:38
  116.1 4.0 collective-permute-done.19
  120.1 3.7 collective-permute-start.20
  140.5 2.8 collective-permute-start.31
  146.0 4.1 %collective-permute-done.31 = f32[5,32,128]{2,1,0:T(8,128)S(1)} collective-permute-done((f32[5,32,128]{2,1,0:T(8,128)S(1)}, f32[5,32,128]{2,1,0:T(8,128)S(1)}, u32[]{:S(2)}, u32[]{:S(2)}) %collective-permute-start.31) | collective-permute-done | bytes 81952 | tf_op jit(solution)/shard_map/ppermute | solution.py:38
  160.5 9.3 %collective-permute-done.36 = f32[20,32,128]{2,1,0:T(8,128)S(1)} collective-permute-done((f32[20,32,128]{2,1,0:T(8,128)S(1)}, f32[20,32,128]{2,1,0:T(8,128)S(1)}, u32[]{:S(2)}, u32[]{:S(2)}) %collective-permute-start.36) | collective-permute-done | bytes 327712 | tf_op jit(solution)/shard_map/ppermute | solution.py:38
  172.2 8.1 %collective-permute-done.44 = f32[6,32,128]{2,1,0:T(8,128)S(1)} collective-permute-done((f32[6,32,128]{2,1,0:T(8,128)S(1)}, f32[6,32,128]{2,1,0:T(8,128)S(1)}, u32[]{:S(2)}, u32[]{:S(2)}) %collective-permute-start.44) | collective-permute-done | bytes 98336 | tf_op jit(solution)/shard_map/ppermute | solution.py:38
  184.2 3.8 collective-permute-done.45.refs_5_
  188.0 4.0 collective-permute-done.46.refs_6_
  192.0 19.4 %shard_map.96 = (f32[32,32,128]{2,1,0:T(8,128)S(1)}, f32[32,32,128]{2,1,0:T(8,128)S(1)}, f32[40,32,128]{2,1,0:T(8,128)S(1)}, f32[40,32,128]{2,1,0:T(8,128)S(1)},...) custom-call(s32[256]{0:T(256)S(1)} %get-tuple-element.108.row_ref, ...), custom_call_target="tpu_custom_call" | custom-call | flops 805306368 | bytes 23068672 | tf_op jit(solution)/shard_map/pallas_call | solution.py:126
  220.4 6.5 %collective-permute-done.69 = f32[12,32,128]{2,1,0:T(8,128)S(1)} collective-permute-done((f32[12,32,128]{2,1,0:T(8,128)S(1)}, f32[12,32,128]{2,1,0:T(8,128)S(1)}, u32[]{:S(2)}, u32[]{:S(2)}) %collective-permute-start.69) | collective-permute-done | bytes 196640 | tf_op jit(solution)/shard_map/ppermute | solution.py:38
  234.2 3.8 collective-permute-start.50
  272.6 6.0 %collective-permute-done.66 = f32[20,32,128]{2,1,0:T(8,128)S(1)} collective-permute-done((f32[20,32,128]{2,1,0:T(8,128)S(1)}, f32[20,32,128]{2,1,0:T(8,128)S(1)}, u32[]{:S(2)}, u32[]{:S(2)}) %collective-permute-start.66) | collective-permute-done | bytes 327712 | tf_op jit(solution)/shard_map/ppermute | solution.py:38
  282.1 8.1 %collective-permute-done.74 = f32[6,32,128]{2,1,0:T(8,128)S(1)} collective-permute-done((f32[6,32,128]{2,1,0:T(8,128)S(1)}, f32[6,32,128]{2,1,0:T(8,128)S(1)}, u32[]{:S(2)}, u32[]{:S(2)}) %collective-permute-start.74) | collective-permute-done | bytes 98336 | tf_op jit(solution)/shard_map/ppermute | solution.py:38
  294.1 3.8 collective-permute-done.75.refs_5_
  297.9 4.0 collective-permute-done.76.refs_6_
  302.0 19.4 %shard_map.97 = (f32[32,32,128]{2,1,0:T(8,128)S(1)}, f32[32,32,128]{2,1,0:T(8,128)S(1)}, f32[40,32,128]{2,1,0:T(8,128)S(1)}, f32[40,32,128]{2,1,0:T(8,128)S(1)},...) custom-call(s32[256]{0:T(256)S(1)} %get-tuple-element.108.row_ref, ...), custom_call_target="tpu_custom_call" | custom-call | flops 805306368 | bytes 23068672 | tf_op jit(solution)/shard_map/pallas_call | solution.py:126
  326.6 5.9 %collective-permute-start.78 = (f32[32,32,128]{2,1,0:T(8,128)S(1)}, f32[32,32,128]{2,1,0:T(8,128)S(1)}, u32[]{:S(2)}, u32[]{:S(2)}) collective-permute-start(f32[32,32,128]{2,1,0:T(8,128)S(1)} %get-tuple-element.43), channel_id=1, source_target_pairs={{0,4},{2,6},{4,0},{6,2},{8,12},{10,14},{12,8},{14,10},{16,20},{18,... | collective-permute-start | bytes 1572872 | tf_op jit(solution)/shard_map/ppermute | solution.py:38
  332.5 5.3 %collective-permute-done.89 = f32[12,32,128]{2,1,0:T(8,128)S(1)} collective-permute-done((f32[12,32,128]{2,1,0:T(8,128)S(1)}, f32[12,32,128]{2,1,0:T(8,128)S(1)}, u32[]{:S(2)}, u32[]{:S(2)}) %collective-permute-start.89) | collective-permute-done | bytes 196640 | tf_op jit(solution)/shard_map/ppermute | solution.py:38
  347.1 2.9 collective-permute-done.79
  350.0 3.3 collective-permute-start.80
  366.1 40.1 %all-reduce = (f32[64]{0:T(128)S(1)}, f32[]{:T(128)}) all-reduce(f32[64]{0:T(128)S(1)} %fusion, f32[]{:T(128)} %reduce_sum.19), channel_id=1, replica_groups=mesh['row'=8,'x'=2,'core'=2] {'row','x','core'}, use_global_device_ids=true, to_apply=%region_1.2 | all-reduce | flops 65 | bytes 520 | tf_op jit(solution)/shard_map/psum | solution.py:234
  (251 shorter events, 159.8 us)
Async XLA Ops:
  0.6 71.0 %collective-permute-start.2 = (f32[128,128,128]{2,1,0:T(8,128)}, f32[128,128,128]{2,1,0:T(8,128)}, u32[]{:S(2)}, u32[]{:S(2)}) collective-permute-start(f32[128,128,128]{2,1,0:T(8,128)} %own_ref.5), channel_id=1, source_target_pairs={{0,1},{1,0},{2,3},{3,2},{4,5},{5,4},{6,7},{7,6},{8,9},{9,8},{10,11... | collective-permute-start | bytes 25165832 | tf_op jit(solution)/shard_map/ppermute | solution.py:188
  2.3 11.8 %collective-permute-start = (f32[6,40,128]{2,1,0:T(8,128)S(1)}, f32[6,40,128]{2,1,0:T(8,128)S(1)}, u32[]{:S(2)}, u32[]{:S(2)}) collective-permute-start(f32[6,40,128]{2,1,0:T(8,128)S(1)} %pad_maximum_fusion.10), channel_id=1, source_target_pairs={{0,1},{1,0},{2,3},{3,2},{4,5},{5,4},{6,7},{7,6},{8,9},{9,8},{10,11... | collective-permute-start | bytes 368648 | tf_op jit(solution)/shard_map/ppermute | solution.py:210
  14.2 27.6 %collective-permute-start.10 = (f32[5,32,128]{2,1,0:T(8,128)S(1)}, f32[5,32,128]{2,1,0:T(8,128)S(1)}, u32[]{:S(2)}, u32[]{:S(2)}) collective-permute-start(f32[5,32,128]{2,1,0:T(8,128)S(1)} %get-tuple-element.61), channel_id=1, source_target_pairs={{0,24},{2,26},{4,28},{6,30},{8,0},{10,2},{12,4},{14,6},{16,8},{18,... | collective-permute-start | bytes 245768 | tf_op jit(solution)/shard_map/ppermute | solution.py:38
  19.2 24.1 %collective-permute-start.8 = (f32[5,32,128]{2,1,0:T(8,128)S(1)}, f32[5,32,128]{2,1,0:T(8,128)S(1)}, u32[]{:S(2)}, u32[]{:S(2)}) collective-permute-start(f32[5,32,128]{2,1,0:T(8,128)S(1)} %get-tuple-element.61), channel_id=1, source_target_pairs={{0,8},{2,10},{4,12},{6,14},{8,16},{10,18},{12,20},{14,22},{16,24},... | collective-permute-start | bytes 245768 | tf_op jit(solution)/shard_map/ppermute | solution.py:38
  19.2 24.1 %collective-permute-start.9 = (f32[5,32,128]{2,1,0:T(8,128)S(1)}, f32[5,32,128]{2,1,0:T(8,128)S(1)}, u32[]{:S(2)}, u32[]{:S(2)}) collective-permute-start(f32[5,32,128]{2,1,0:T(8,128)S(1)} %get-tuple-element.61), channel_id=1, source_target_pairs={{0,16},{2,18},{4,20},{6,22},{8,24},{10,26},{12,28},{14,30},{16,0},... | collective-permute-start | bytes 245768 | tf_op jit(solution)/shard_map/ppermute | solution.py:38
  40.2 13.6 %collective-permute-start.14 = (f32[6,32,128]{2,1,0:T(8,128)S(1)}, f32[6,32,128]{2,1,0:T(8,128)S(1)}, u32[]{:S(2)}, u32[]{:S(2)}) collective-permute-start(f32[6,32,128]{2,1,0:T(8,128)S(1)} %pad_maximum_fusion.13), channel_id=1, source_target_pairs={{0,4},{2,6},{4,0},{6,2},{8,12},{10,14},{12,8},{14,10},{16,20},{18,... | collective-permute-start | bytes 294920 | tf_op jit(solution)/shard_map/ppermute | solution.py:38
  52.9 18.7 %collective-permute-start.12 = (f32[40,32,128]{2,1,0:T(8,128)S(1)}, f32[40,32,128]{2,1,0:T(8,128)S(1)}, u32[]{:S(2)}, u32[]{:S(2)}) collective-permute-start(f32[40,32,128]{2,1,0:T(8,128)S(1)} %constant_dynamic-update-slice_fusion.5.refs_2_), channel_id=1, source_target_pairs={{0,2},{2,0},{4,6},{6,4},{8,10},{10,8},{12,14},{14,12},{16,18},{18,... | collective-permute-start | bytes 1966088 | tf_op jit(solution)/shard_map/ppermute | solution.py:38
  53.0 18.6 %collective-permute-start.7 = (f32[32,32,128]{2,1,0:T(8,128)S(1)}, f32[32,32,128]{2,1,0:T(8,128)S(1)}, u32[]{:S(2)}, u32[]{:S(2)}) collective-permute-start(f32[32,32,128]{2,1,0:T(8,128)S(1)} %constant_dynamic-update-slice_fusion.refs_0_), channel_id=1, source_target_pairs={{0,4},{2,6},{4,0},{6,2},{8,12},{10,14},{12,8},{14,10},{16,20},{18,... | collective-permute-start | bytes 1572872 | tf_op jit(solution)/shard_map/ppermute | solution.py:38
  56.9 13.0 %collective-permute-start.16 = (f32[12,32,128]{2,1,0:T(8,128)S(1)}, f32[12,32,128]{2,1,0:T(8,128)S(1)}, u32[]{:S(2)}, u32[]{:S(2)}) collective-permute-start(f32[12,32,128]{2,1,0:T(8,128)S(1)} %pad_maximum_fusion.6.refs_4_), channel_id=1, source_target_pairs={{0,16},{2,18},{4,20},{6,22},{8,24},{10,26},{12,28},{14,30},{16,0},... | collective-permute-start | bytes 589832 | tf_op jit(solution)/shard_map/ppermute | solution.py:38
  91.1 19.1 %collective-permute-start.18 = (f32[32,32,128]{2,1,0:T(8,128)S(1)}, f32[32,32,128]{2,1,0:T(8,128)S(1)}, u32[]{:S(2)}, u32[]{:S(2)}) collective-permute-start(f32[32,32,128]{2,1,0:T(8,128)S(1)} %get-tuple-element.27), channel_id=1, source_target_pairs={{0,4},{2,6},{4,0},{6,2},{8,12},{10,14},{12,8},{14,10},{16,20},{18,... | collective-permute-start | bytes 1572872 | tf_op jit(solution)/shard_map/ppermute | solution.py:38
  95.4 13.9 %collective-permute-start.39 = (f32[12,32,128]{2,1,0:T(8,128)S(1)}, f32[12,32,128]{2,1,0:T(8,128)S(1)}, u32[]{:S(2)}, u32[]{:S(2)}) collective-permute-start(f32[12,32,128]{2,1,0:T(8,128)S(1)} %get-tuple-element.32), channel_id=1, source_target_pairs={{0,16},{2,18},{4,20},{6,22},{8,24},{10,26},{12,28},{14,30},{16,0},... | collective-permute-start | bytes 589832 | tf_op jit(solution)/shard_map/ppermute | solution.py:38
  96.5 12.8 %collective-permute-start.40 = (f32[12,32,128]{2,1,0:T(8,128)S(1)}, f32[12,32,128]{2,1,0:T(8,128)S(1)}, u32[]{:S(2)}, u32[]{:S(2)}) collective-permute-start(f32[12,32,128]{2,1,0:T(8,128)S(1)} %get-tuple-element.33), channel_id=1, source_target_pairs={{0,24},{2,26},{4,28},{6,30},{8,0},{10,2},{12,4},{14,6},{16,8},{18,... | collective-permute-start | bytes 589832 | tf_op jit(solution)/shard_map/ppermute | solution.py:38
  97.8 28.5 %collective-permute-start.28 = (f32[40,32,128]{2,1,0:T(8,128)S(1)}, f32[40,32,128]{2,1,0:T(8,128)S(1)}, u32[]{:S(2)}, u32[]{:S(2)}) collective-permute-start(f32[40,32,128]{2,1,0:T(8,128)S(1)} %get-tuple-element.29), channel_id=1, source_target_pairs={{0,2},{2,0},{4,6},{6,4},{8,10},{10,8},{12,14},{14,12},{16,18},{18,... | collective-permute-start | bytes 1966088 | tf_op jit(solution)/shard_map/ppermute | solution.py:38
  114.1 19.9 %collective-permute-start.42 = (f32[3,32,128]{2,1,0:T(8,128)S(1)}, f32[3,32,128]{2,1,0:T(8,128)S(1)}, u32[]{:S(2)}, u32[]{:S(2)}) collective-permute-start(f32[3,32,128]{2,1,0:T(8,128)S(1)} %slice_add_fusion.58), channel_id=1, source_target_pairs={{0,2},{2,0},{4,6},{6,4},{8,10},{10,8},{12,14},{14,12},{16,18},{18,... | collective-permute-start | bytes 147464 | tf_op jit(solution)/shard_map/ppermute | solution.py:38
  126.3 13.2 %collective-permute-start.29 = (f32[20,32,128]{2,1,0:T(8,128)S(1)}, f32[20,32,128]{2,1,0:T(8,128)S(1)}, u32[]{:S(2)}, u32[]{:S(2)}) collective-permute-start(f32[20,32,128]{2,1,0:T(8,128)S(1)} %get-tuple-element.70), channel_id=1, source_target_pairs={{0,4},{2,6},{4,0},{6,2},{8,12},{10,14},{12,8},{14,10},{16,20},{18,... | collective-permute-start | bytes 983048 | tf_op jit(solution)/shard_map/ppermute | solution.py:38
  134.0 37.4 %collective-permute-start.43 = (f32[3,32,128]{2,1,0:T(8,128)S(1)}, f32[3,32,128]{2,1,0:T(8,128)S(1)}, u32[]{:S(2)}, u32[]{:S(2)}) collective-permute-start(f32[3,32,128]{2,1,0:T(8,128)S(1)} %fusion.42), channel_id=1, source_target_pairs={{0,2},{2,0},{4,6},{6,4},{8,10},{10,8},{12,14},{14,12},{16,18},{18,... | collective-permute-start | bytes 147464 | tf_op jit(solution)/shard_map/ppermute | solution.py:38
  137.8 32.1 %collective-permute-start.26 = (f32[16,32,128]{2,1,0:T(8,128)S(1)}, f32[16,32,128]{2,1,0:T(8,128)S(1)}, u32[]{:S(2)}, u32[]{:S(2)}) collective-permute-start(f32[16,32,128]{2,1,0:T(8,128)S(1)} %pad_maximum_fusion.4), channel_id=1, source_target_pairs={{0,2},{2,0},{4,6},{6,4},{8,10},{10,8},{12,14},{14,12},{16,18},{18,... | collective-permute-start | bytes 786440 | tf_op jit(solution)/shard_map/ppermute | solution.py:38
  169.8 22.2 %collective-permute-start.37 = (f32[40,32,128]{2,1,0:T(8,128)S(1)}, f32[40,32,128]{2,1,0:T(8,128)S(1)}, u32[]{:S(2)}, u32[]{:S(2)}) collective-permute-start(f32[40,32,128]{2,1,0:T(8,128)S(1)} %constant_dynamic-update-slice_fusion.15.refs_2_), channel_id=1, source_target_pairs={{0,2},{2,0},{4,6},{6,4},{8,10},{10,8},{12,14},{14,12},{16,18},{18,... | collective-permute-start | bytes 1966088 | tf_op jit(solution)/shard_map/ppermute | solution.py:38
  170.0 22.1 %collective-permute-start.27 = (f32[32,32,128]{2,1,0:T(8,128)S(1)}, f32[32,32,128]{2,1,0:T(8,128)S(1)}, u32[]{:S(2)}, u32[]{:S(2)}) collective-permute-start(f32[32,32,128]{2,1,0:T(8,128)S(1)} %constant_dynamic-update-slice_fusion.10.refs_0_), channel_id=1, source_target_pairs={{0,4},{2,6},{4,0},{6,2},{8,12},{10,14},{12,8},{14,10},{16,20},{18,... | collective-permute-start | bytes 1572872 | tf_op jit(solution)/shard_map/ppermute | solution.py:38
  211.5 15.8 %collective-permute-start.48 = (f32[32,32,128]{2,1,0:T(8,128)S(1)}, f32[32,32,128]{2,1,0:T(8,128)S(1)}, u32[]{:S(2)}, u32[]{:S(2)}) collective-permute-start(f32[32,32,128]{2,1,0:T(8,128)S(1)} %get-tuple-element.35), channel_id=1, source_target_pairs={{0,4},{2,6},{4,0},{6,2},{8,12},{10,14},{12,8},{14,10},{16,20},{18,... | collective-permute-start | bytes 1572872 | tf_op jit(solution)/shard_map/ppermute | solution.py:38
  215.5 11.4 %collective-permute-start.69 = (f32[12,32,128]{2,1,0:T(8,128)S(1)}, f32[12,32,128]{2,1,0:T(8,128)S(1)}, u32[]{:S(2)}, u32[]{:S(2)}) collective-permute-start(f32[12,32,128]{2,1,0:T(8,128)S(1)} %get-tuple-element.40), channel_id=1, source_target_pairs={{0,16},{2,18},{4,20},{6,22},{8,24},{10,26},{12,28},{14,30},{16,0},... | collective-permute-start | bytes 589832 | tf_op jit(solution)/shard_map/ppermute | solution.py:38
  217.9 22.6 %collective-permute-start.58 = (f32[40,32,128]{2,1,0:T(8,128)S(1)}, f32[40,32,128]{2,1,0:T(8,128)S(1)}, u32[]{:S(2)}, u32[]{:S(2)}) collective-permute-start(f32[40,32,128]{2,1,0:T(8,128)S(1)} %get-tuple-element.37), channel_id=1, source_target_pairs={{0,2},{2,0},{4,6},{6,4},{8,10},{10,8},{12,14},{14,12},{16,18},{18,... | collective-permute-start | bytes 1966088 | tf_op jit(solution)/shard_map/ppermute | solution.py:38
  231.6 17.2 %collective-permute-start.72 = (f32[3,32,128]{2,1,0:T(8,128)S(1)}, f32[3,32,128]{2,1,0:T(8,128)S(1)}, u32[]{:S(2)}, u32[]{:S(2)}) collective-permute-start(f32[3,32,128]{2,1,0:T(8,128)S(1)} %slice_add_fusion.56), channel_id=1, source_target_pairs={{0,2},{2,0},{4,6},{6,4},{8,10},{10,8},{12,14},{14,12},{16,18},{18,... | collective-permute-start | bytes 147464 | tf_op jit(solution)/shard_map/ppermute | solution.py:38
  240.6 14.0 %collective-permute-start.59 = (f32[20,32,128]{2,1,0:T(8,128)S(1)}, f32[20,32,128]{2,1,0:T(8,128)S(1)}, u32[]{:S(2)}, u32[]{:S(2)}) collective-permute-start(f32[20,32,128]{2,1,0:T(8,128)S(1)} %get-tuple-element.68), channel_id=1, source_target_pairs={{0,4},{2,6},{4,0},{6,2},{8,12},{10,14},{12,8},{14,10},{16,20},{18,... | collective-permute-start | bytes 983048 | tf_op jit(solution)/shard_map/ppermute | solution.py:38
  248.9 32.7 %collective-permute-start.73 = (f32[3,32,128]{2,1,0:T(8,128)S(1)}, f32[3,32,128]{2,1,0:T(8,128)S(1)}, u32[]{:S(2)}, u32[]{:S(2)}) collective-permute-start(f32[3,32,128]{2,1,0:T(8,128)S(1)} %fusion.39), channel_id=1, source_target_pairs={{0,2},{2,0},{4,6},{6,4},{8,10},{10,8},{12,14},{14,12},{16,18},{18,... | collective-permute-start | bytes 147464 | tf_op jit(solution)/shard_map/ppermute | solution.py:38
  253.7 26.2 %collective-permute-start.56 = (f32[16,32,128]{2,1,0:T(8,128)S(1)}, f32[16,32,128]{2,1,0:T(8,128)S(1)}, u32[]{:S(2)}, u32[]{:S(2)}) collective-permute-start(f32[16,32,128]{2,1,0:T(8,128)S(1)} %pad_maximum_fusion.5), channel_id=1, source_target_pairs={{0,2},{2,0},{4,6},{6,4},{8,10},{10,8},{12,14},{14,12},{16,18},{18,... | collective-permute-start | bytes 786440 | tf_op jit(solution)/shard_map/ppermute | solution.py:38
  278.7 23.3 %collective-permute-start.67 = (f32[40,32,128]{2,1,0:T(8,128)S(1)}, f32[40,32,128]{2,1,0:T(8,128)S(1)}, u32[]{:S(2)}, u32[]{:S(2)}) collective-permute-start(f32[40,32,128]{2,1,0:T(8,128)S(1)} %constant_dynamic-update-slice_fusion.25.refs_2_), channel_id=1, source_target_pairs={{0,2},{2,0},{4,6},{6,4},{8,10},{10,8},{12,14},{14,12},{16,18},{18,... | collective-permute-start | bytes 1966088 | tf_op jit(solution)/shard_map/ppermute | solution.py:38
  279.9 22.1 %collective-permute-start.57 = (f32[32,32,128]{2,1,0:T(8,128)S(1)}, f32[32,32,128]{2,1,0:T(8,128)S(1)}, u32[]{:S(2)}, u32[]{:S(2)}) collective-permute-start(f32[32,32,128]{2,1,0:T(8,128)S(1)} %constant_dynamic-update-slice_fusion.20.refs_0_), channel_id=1, source_target_pairs={{0,4},{2,6},{4,0},{6,2},{8,12},{10,14},{12,8},{14,10},{16,20},{18,... | collective-permute-start | bytes 1572872 | tf_op jit(solution)/shard_map/ppermute | solution.py:38
  324.2 13.6 %collective-permute-start.89 = (f32[12,32,128]{2,1,0:T(8,128)S(1)}, f32[12,32,128]{2,1,0:T(8,128)S(1)}, u32[]{:S(2)}, u32[]{:S(2)}) collective-permute-start(f32[12,32,128]{2,1,0:T(8,128)S(1)} %get-tuple-element.48), channel_id=1, source_target_pairs={{0,16},{2,18},{4,20},{6,22},{8,24},{10,26},{12,28},{14,30},{16,0},... | collective-permute-start | bytes 589832 | tf_op jit(solution)/shard_map/ppermute | solution.py:38
  325.0 12.8 %collective-permute-start.90 = (f32[12,32,128]{2,1,0:T(8,128)S(1)}, f32[12,32,128]{2,1,0:T(8,128)S(1)}, u32[]{:S(2)}, u32[]{:S(2)}) collective-permute-start(f32[12,32,128]{2,1,0:T(8,128)S(1)} %get-tuple-element.49), channel_id=1, source_target_pairs={{0,24},{2,26},{4,28},{6,30},{8,0},{10,2},{12,4},{14,6},{16,8},{18,... | collective-permute-start | bytes 589832 | tf_op jit(solution)/shard_map/ppermute | solution.py:38
  326.6 16.9 %collective-permute-start.78 = (f32[32,32,128]{2,1,0:T(8,128)S(1)}, f32[32,32,128]{2,1,0:T(8,128)S(1)}, u32[]{:S(2)}, u32[]{:S(2)}) collective-permute-start(f32[32,32,128]{2,1,0:T(8,128)S(1)} %get-tuple-element.43), channel_id=1, source_target_pairs={{0,4},{2,6},{4,0},{6,2},{8,12},{10,14},{12,8},{14,10},{16,20},{18,... | collective-permute-start | bytes 1572872 | tf_op jit(solution)/shard_map/ppermute | solution.py:38
  332.5 12.4 %collective-permute-start.83 = (f32[40,32,128]{2,1,0:T(8,128)S(1)}, f32[40,32,128]{2,1,0:T(8,128)S(1)}, u32[]{:S(2)}, u32[]{:S(2)}) collective-permute-start(f32[40,32,128]{2,1,0:T(8,128)S(1)} %get-tuple-element.45), channel_id=1, source_target_pairs={{0,2},{2,0},{4,6},{6,4},{8,10},{10,8},{12,14},{14,12},{16,18},{18,... | collective-permute-start | bytes 1966088 | tf_op jit(solution)/shard_map/ppermute | solution.py:38
  (64 other events, 510.7 us)

commit v3 on v2

v3 whole, which is shorter than its diff:
```python
import functools

import jax
import jax.numpy as jnp
from jax import lax
from jax.experimental import pallas as pl
from jax.experimental.pallas import tpu as pltpu
from jax.sharding import Mesh
from jax.sharding import PartitionSpec as P

ITERS = 3
CORES = 2
STEP = 16
UNROLL = 8
CHIPS = ("row", "x")
ALL = ("row", "x", "core")
DIMS = (((1,), (1,)), ((), ()))
ORDERS = (("z", "x", "y"), ("z", "y", "x"), ("x", "y", "z"))


def sizes_of(n_rows, n_x):
    y = max(n for n in range(1, n_rows + 1) if n_rows % n == 0 and n * n <= n_rows)
    return {"z": n_rows // y, "y": y, "x": n_x}


def chip_of(sizes, z, y, x):
    return (z * sizes["y"] + y) * sizes["x"] + x


def shift(sizes, array, axis, by):
    pairs = []
    for z in range(sizes["z"]):
        for y in range(sizes["y"]):
            for x in range(sizes["x"]):
                at = {"z": z, "y": y, "x": x}
                to = dict(at, **{axis: (at[axis] + by) % sizes[axis]})
                pairs.append((chip_of(sizes, **at), chip_of(sizes, **to)))
    return lax.ppermute(array, CHIPS, pairs)


def shifts(sizes, block, axis):
    return [block] + [shift(sizes, block, axis, j) for j in range(1, sizes[axis])]


def gather(sizes, flux, bounds):
    first, second, last = bounds
    blocks = shifts(sizes, flux[:second], "z")
    pieces = []
    for (low, high), (_, middle, outer) in zip(((0, first), (first, second)), ORDERS):
        block = jnp.concatenate([b[low:high] for b in blocks], axis=0)
        block = jnp.concatenate(shifts(sizes, block, middle), axis=0)
        pieces.append(shifts(sizes, block, outer))
    block = flux[second:last]
    for axis in ORDERS[2][:2]:
        block = jnp.concatenate(shifts(sizes, block, axis), axis=0)
    pieces.append(shifts(sizes, block, ORDERS[2][2]))
    return pieces


def fold(sizes, pieces, axis, count):
    got = [shift(sizes, pieces[j], axis, j) for j in range(1, sizes[axis])]
    length = pieces[0].shape[0] // count
    return [
        sum([g[k * length : (k + 1) * length] for g in got], pieces[0][k * length : (k + 1) * length])
        for k in range(count)
    ]


def reduce(sizes, pieces):
    inner, middle, outer = ORDERS[2]
    blocks = fold(sizes, pieces[2], outer, sizes[middle])
    blocks = fold(sizes, blocks, middle, sizes[inner])
    tail = fold(sizes, blocks, inner, 1)[0]
    halves = []
    for piece, (inner, middle, outer) in zip(pieces, ORDERS[:2]):
        blocks = fold(sizes, piece, outer, sizes[middle])
        halves.append(fold(sizes, blocks, middle, sizes[inner]))
    head = fold(sizes, [jnp.concatenate(pair, axis=0) for pair in zip(*halves)], "z", 1)[0]
    return jnp.concatenate([head, tail], axis=0)


def split_kernel(tile_ref, pair_ref):
    size = tile_ref.shape[1]

    @pl.loop(0, STEP // UNROLL)
    def _(group):
        for k in range(UNROLL):
            tile = jnp.transpose(tile_ref[group * UNROLL + k])
            high = tile.astype(jnp.bfloat16)
            low = (tile - high.astype(jnp.float32)).astype(jnp.bfloat16)
            pair_ref[group * UNROLL + k, :size] = high
            pair_ref[group * UNROLL + k, size:] = low


def split_tiles(tiles):
    length, size, _ = tiles.shape
    return pl.pallas_call(
        split_kernel,
        out_shape=jax.ShapeDtypeStruct((length, 2 * size, size), jnp.bfloat16),
        grid=(length // STEP,),
        in_specs=[pl.BlockSpec((STEP, size, size), lambda i: (i, 0, 0))],
        out_specs=pl.BlockSpec((STEP, 2 * size, size), lambda i: (i, 0, 0)),
        compiler_params=pltpu.CompilerParams(vmem_limit_bytes=40 * 1024 * 1024),
        cost_estimate=pl.CostEstimate(
            flops=3 * length * size * size, bytes_accessed=8 * length * size * size, transcendentals=0
        ),
    )(tiles)


def apply_kernel(length, counts, weighs, row_ref, col_ref, used_ref, own_ref, other_ref, *refs):
    step = pl.program_id(0)
    pieces = len(counts)
    weight_ref, refs = (refs[0], refs[1:]) if weighs else (None, refs)
    given, outs, refs = refs[:pieces], refs[pieces : 2 * pieces], refs[2 * pieces :]
    weighted_ref, refs = (refs[0], refs[1:]) if weighs else (None, refs)
    flux_ref, sum_ref, sem = refs
    starts = [sum(counts[:k]) for k in range(pieces)]

    @pl.when(step == 0)
    def _():
        copies = [
            pltpu.make_async_copy(given[k], flux_ref.at[pl.ds(starts[k], counts[k])], sem.at[k])
            for k in range(pieces)
        ]
        for copy in copies:
            copy.start()
        sum_ref[...] = jnp.zeros_like(sum_ref)
        for copy in copies:
            copy.wait()

    def add_tile(pair, slot):
        flux = flux_ref[col_ref[slot]] * used_ref[slot]
        high = flux.astype(jnp.bfloat16)
        low = (flux - high.astype(jnp.float32)).astype(jnp.bfloat16)
        left = jnp.concatenate([high, low], axis=0)
        both = jnp.dot(
            jnp.concatenate([left, left], axis=1), pair, preferred_element_type=jnp.float32
        )
        temps = flux.shape[0]
        sum_ref[row_ref[slot]] += both[:temps] + both[temps:]

    for part, ref in enumerate((own_ref, other_ref)):
        base = part * length + step * STEP

        @pl.loop(0, STEP // UNROLL)
        def _(group):
            for k in range(UNROLL):
                add_tile(ref[group * UNROLL + k], base + group * UNROLL + k)

    @pl.when(step == pl.num_programs(0) - 1)
    def _():
        copies = [
            pltpu.make_async_copy(sum_ref.at[pl.ds(starts[k], counts[k])], outs[k], sem.at[k])
            for k in range(pieces)
        ]
        for copy in copies:
            copy.start()
        if weighs:

            def weigh(k, total):
                return total + sum_ref[k] * weight_ref[k]

            weighted_ref[...] = lax.fori_loop(
                0, sum(counts), weigh, jnp.zeros(weighted_ref.shape, jnp.float32)
            )
        for copy in copies:
            copy.wait()


def apply_tiles(row, col, used, own, other, pieces, weights=None):
    length, _, size = own.shape
    counts = [piece.shape[0] for piece in pieces]
    temps = pieces[0].shape[1]
    num = sum(counts)
    some = pl.BlockSpec((STEP, 2 * size, size), lambda i, *_: (i, 0, 0))
    anywhere = pl.BlockSpec(memory_space=pl.ANY)
    weighs = weights is not None
    out_shape = [jax.ShapeDtypeStruct(piece.shape, jnp.float32) for piece in pieces]
    in_specs, out_specs, given = [some, some], [anywhere] * len(pieces), []
    if weighs:
        in_specs.append(pl.BlockSpec((num, 1, size), lambda i, *_: (0, 0, 0)))
        out_specs.append(pl.BlockSpec((temps, size), lambda i, *_: (0, 0)))
        out_shape.append(jax.ShapeDtypeStruct((temps, size), jnp.float32))
        given.append(weights)
    return pl.pallas_call(
        functools.partial(apply_kernel, length, counts, weighs),
        out_shape=out_shape,
        grid_spec=pltpu.PrefetchScalarGridSpec(
            num_scalar_prefetch=3,
            grid=(length // STEP,),
            in_specs=in_specs + [anywhere] * len(pieces),
            out_specs=out_specs,
            scratch_shapes=[
                pltpu.VMEM((num, temps, size), jnp.float32),
                pltpu.VMEM((num, temps, size), jnp.float32),
                pltpu.SemaphoreType.DMA((len(pieces),)),
            ],
        ),
        compiler_params=pltpu.CompilerParams(vmem_limit_bytes=40 * 1024 * 1024),
        cost_estimate=pl.CostEstimate(
            flops=2 * 2 * length * size * size * temps * 4,
            bytes_accessed=4 * (2 * length * size * size + 2 * num * temps * size),
            transcendentals=0,
        ),
    )(row, col, used, own, other, *given, *pieces)


def shards(
    tile_values, tile_owner, tile_row, tile_col, tile_count, relaxation, driving, heat_weight
):
    n_cols = lax.axis_size("x") * CORES
    n_rows = lax.axis_size("row")
    sizes = sizes_of(n_rows, n_cols // CORES)
    length, size, _ = tile_values.shape
    modes, columns = driving.shape
    per = modes // size
    chip_tiles = CORES * per
    num = n_rows * n_cols * per
    half = columns // CORES
    core = lax.axis_index("core")
    row_at = lax.axis_index("row")
    here = {"z": row_at // sizes["y"], "y": row_at % sizes["y"], "x": lax.axis_index("x")}
    swap = [(0, 1), (1, 0)]

    chips = n_rows * n_cols // CORES

    second = chip_tiles - max(1, chip_tiles // 6)
    bounds = (second // 2, second, chip_tiles)
    parts = ((0, second // 2), (second // 2, second), (second, chip_tiles))

    def place(tile, sign):
        chip, inside = tile // chip_tiles, tile % chip_tiles
        at = {
            "z": chip // (sizes["y"] * sizes["x"]),
            "y": (chip // sizes["x"]) % sizes["y"],
            "x": chip % sizes["x"],
        }
        away = {a: (sign * (at[a] - here[a]) + sizes[a]) % sizes[a] for a in sizes}
        out = jnp.zeros_like(tile)
        for order, (low, high) in zip(ORDERS, parts):
            inner, middle, outer = order
            slot = (away[outer] * sizes[middle] + away[middle]) * sizes[inner] + away[inner]
            slot = chips * low + slot * (high - low) + inside - low
            out = jnp.where((inside >= low) & (inside < high), slot, out)
        return out

    def placed_tiles():
        out = []
        for order, (low, high) in zip(ORDERS, parts):
            inner, middle, outer = order
            at = {}
            for axis, across in ((outer, 0), (middle, 1), (inner, 2)):
                steps = jnp.arange(sizes[axis], dtype=jnp.int32).reshape(
                    [-1 if k == across else 1 for k in range(4)]
                )
                at[axis] = (here[axis] + steps) % sizes[axis]
            tiles = chip_of(sizes, **at) * chip_tiles + jnp.arange(low, high, dtype=jnp.int32)
            out.append(tiles.reshape(-1))
        return jnp.concatenate(out)

    other_values = lax.ppermute(tile_values, "core", swap)
    owners = tile_owner[:, 0]
    row = (owners // n_cols) * (n_cols * per) + tile_row
    col = ((tile_col // per) * n_cols + owners % n_cols) * per + tile_col % per
    used = jnp.arange(length, dtype=jnp.int32) < tile_count[0]
    places = jnp.where(used, place(row, 1) * num + place(col, -1), -1)
    places = jnp.concatenate([places, lax.ppermute(places, "core", swap)])
    is_used = places >= 0
    places = jnp.where(is_used, places, 0)
    row, col, used = places // num, places % num, is_used.astype(jnp.float32)

    def by_core(own, other):
        return jnp.concatenate(
            [jnp.where(core == 0, own, other), jnp.where(core == 0, other, own)], axis=0
        )

    drive = jnp.transpose(driving.reshape(per, size, columns), (0, 2, 1))
    relax = relaxation.reshape(per, 1, size)
    heat = heat_weight.reshape(per, 1, size)
    low, high = drive[:, :half], drive[:, half:]
    mine = jnp.where(core == 0, low, high)
    theirs = jnp.where(core == 0, high, low)
    packed = [theirs, jnp.broadcast_to(relax, (per, 8, size)), jnp.broadcast_to(heat, (per, 8, size))]
    got = lax.ppermute(jnp.concatenate(packed, axis=1), "core", swap)
    drive_half = by_core(mine, got[:, :half])
    relax_both = by_core(relax, got[:, half : half + 1])
    heat_both = by_core(heat, got[:, half + 8 : half + 9])

    own = split_tiles(tile_values)
    other = split_tiles(other_values)
    flux = relax_both * drive_half
    weighted_own = jnp.sum(heat_both * flux, axis=(0, 2))
    heats = lax.all_gather(jnp.concatenate([heat, heat * relax], axis=1), ALL, axis=0, tiled=True)
    weight_sum = jnp.sum(heats[:, 0])
    weights = heats[:, 1:][placed_tiles()]
    for sweep in range(ITERS):
        pieces = gather(sizes, flux, bounds)
        counts = [len(piece) for piece in pieces]
        last = sweep == ITERS - 1
        sums = apply_tiles(row, col, used, own, other, sum(pieces, []), weights if last else None)
        if last:
            *sums, weighted = sums
            weighted = weighted_own + jnp.sum(weighted, axis=1)
            weighted = jnp.pad(weighted[None], ((0, 0), (0, size - half)))
            weighted = lax.all_gather(weighted, ALL, axis=0, tiled=True)
            weighted = jnp.sum(weighted.reshape(chips, CORES, size), axis=0)[:, :half]
        sums = [sums[sum(counts[:k]) : sum(counts[: k + 1])] for k in range(len(counts))]
        flux = relax_both * (drive_half + reduce(sizes, sums))
    first, second = flux[:per], flux[per:]
    mine = jnp.where(core == 0, first, second)
    got = lax.ppermute(jnp.where(core == 0, second, first), "core", swap)
    both = jnp.concatenate(
        [jnp.where(core == 0, mine, got), jnp.where(core == 0, got, mine)], axis=1
    )
    mode_flux = jnp.transpose(both, (0, 2, 1)).reshape(modes, columns)
    return (mode_flux, weighted.reshape(columns) / weight_sum)


def solution(mesh):
    n_rows, n_cols = mesh.shape["row"], mesh.shape["col"]
    chips = Mesh(mesh.devices.reshape(n_rows, n_cols // CORES, CORES), ALL)
    placed = (
        P(ALL, None, None),
        P(ALL, None),
        P(ALL),
        P(ALL),
        P(ALL),
        P(ALL),
        P(ALL, None),
        P(ALL),
    )
    return jax.shard_map(
        shards,
        mesh=chips,
        in_specs=placed,
        out_specs=(P(ALL, None), P()),
        check_vma=False,
    )
```

time: 408 us -> 418 us (1.025)
  blocking collectives: 40.1 us -> 87.9 us
  waiting for transfers between devices: 164 us -> 123 us
  starting transfers between devices: 136 us -> 98.7 us
  local copies, waits for them, and re-layouts: 2.08 us -> 29 us
  other arithmetic: 4.84 us -> 12.7 us
    all_gather x0 -> x2, blocking collectives: none -> 87.9 us  [the longest x1 44.2 us: shards(): lax.all_gather(jnp.concatenate([heat, heat * relax], axis=1), ALL, axis=0...]
    psum x1 -> x0, blocking collectives: 40.1 us -> none  [shards(): weighted, weight_sum = lax.psum((weighted_local, jnp.sum(heat_weight)), ALL)]
    ppermute x90 -> x72, waiting for transfers between devices: 152 us -> 114 us  [shift(): return lax.ppermute(array, CHIPS, pairs)]
    ppermute x90 -> x72, starting transfers between devices: 135 us -> 97.5 us  [shift(): return lax.ppermute(array, CHIPS, pairs)]
    unnamed x24 -> x73, local copies, waits for them, and re-layouts: 0.55 us -> 21.9 us
    pallas_call x3 -> x5, Pallas kernels: 58.3 us -> 60.8 us  [the longest x3 46.3 us: apply_tiles(): pl.pallas_call(functools.partial(apply_kernel, length, counts, weighs), o...]
  transfers between devices with their start and end apart: 94 -> 76, of which waited for: 50 -> 38; matrix products, arithmetic and copies ran while one was open for 1% -> 4% of each run, Pallas kernels for 0% -> 4%
where the time goes in v3:
time: 418 us; the launch traced here: 414 us
  waiting for transfers between devices  123 us (29%)
  starting transfers between devices  98.7 us (24%)
  blocking collectives  87.9 us (21%)
  Pallas kernels  60.8 us (15%)
  local copies, waits for them, and re-layouts  29 us (7%)
  other arithmetic  12.7 us (3%)
    ppermute x72, waiting for transfers between devices, shift(): return lax.ppermute(array, CHIPS, pairs)  114 us
    ppermute x72, starting transfers between devices, shift(): return lax.ppermute(array, CHIPS, pairs)  97.5 us
    pallas_call x3, Pallas kernels, apply_tiles(): pl.pallas_call(functools.partial(apply_kernel, length, counts, weighs), o...  46.3 us
    all_gather x1, blocking collectives, shards(): lax.all_gather(jnp.concatenate([heat, heat * relax], axis=1), ALL, axis=0...  44.2 us
    all_gather x1, blocking collectives, shards(): weighted = lax.all_gather(weighted, ALL, axis=0, tiled=True)  43.7 us
    unnamed x73, local copies, waits for them, and re-layouts  21.9 us
    pallas_call x2, Pallas kernels, split_tiles(): pl.pallas_call(split_kernel, out_shape=jax.ShapeDtypeStruct((length, 2 *...  14.5 us
    ppermute x1, waiting for transfers between devices, shards(): got = lax.ppermute(jnp.concatenate(packed, axis=1), 'core', swap)  8.59 us
  transfers between devices with their start and end apart: 76, of which 38 were waited for; matrix products, arithmetic and copies ran while one was open for 4% of the time, Pallas kernels for 4%

profile of v3, /device:TPU:0, one launch (start us, length us, event | category | flops | bytes accessed | tf_op | source)
XLA Modules:
  0.0 413.9 jit_solution(2415467023656045489)
XLA Ops:
  5.6 8.6 %collective-permute-done = f32[6,48,128]{2,1,0:T(8,128)S(1)} collective-permute-done((f32[6,48,128]{2,1,0:T(8,128)S(1)}, f32[6,48,128]{2,1,0:T(8,128)S(1)}, u32[]{:S(2)}, u32[]{:S(2)}) %collective-permute-start) | collective-permute-done | bytes 147488 | tf_op jit(solution)/shard_map/ppermute | solution.py:284
  22.5 3.1 collective-permute-done.3
  25.6 6.5 %collective-permute-done.4 = f32[10,32,128]{2,1,0:T(8,128)S(1)} collective-permute-done((f32[10,32,128]{2,1,0:T(8,128)S(1)}, f32[10,32,128]{2,1,0:T(8,128)S(1)}, u32[]{:S(2)}, u32[]{:S(2)}) %collective-permute-start.4) | collective-permute-done | bytes 163872 | tf_op jit(solution)/shard_map/ppermute | solution.py:38
  36.9 5.0 %collective-permute-done.8 = f32[20,32,128]{2,1,0:T(8,128)S(1)} collective-permute-done((f32[20,32,128]{2,1,0:T(8,128)S(1)}, f32[20,32,128]{2,1,0:T(8,128)S(1)}, u32[]{:S(2)}, u32[]{:S(2)}) %collective-permute-start.8) | collective-permute-done | bytes 327712 | tf_op jit(solution)/shard_map/ppermute | solution.py:38
  45.1 7.2 %shard_map.95.own_ref = bf16[128,256,128]{2,1,0:T(8,128)(2,1)S(1)} custom-call(f32[128,128,128]{2,1,0:T(8,128)} %tile_ref.1), custom_call_target="tpu_custom_call" | custom-call | flops 6291456 | bytes 16777216 | tf_op jit(solution)/shard_map/pallas_call | solution.py:97
  52.3 3.3 copy-done.2
  56.4 4.0 collective-permute-done.11
  60.4 4.2 %collective-permute-start.12 = (f32[8,32,128]{2,1,0:T(8,128)S(1)}, f32[8,32,128]{2,1,0:T(8,128)S(1)}, u32[]{:S(2)}, u32[]{:S(2)}) collective-permute-start(f32[8,32,128]{2,1,0:T(8,128)S(1)} %pad_maximum_fusion.17.refs_4_), channel_id=1, source_target_pairs={{0,8},{2,10},{4,12},{6,14},{8,16},{10,18},{12,20},{14,22},{16,24},... | collective-permute-start | bytes 393224 | tf_op jit(solution)/shard_map/ppermute | solution.py:38
  67.1 7.3 %shard_map.96.other_ref = bf16[128,256,128]{2,1,0:T(8,128)(2,1)S(1)} custom-call(f32[128,128,128]{2,1,0:T(8,128)} %collective-permute-done.2.tile_ref), custom_call_target="tpu_custom_call" | custom-call | flops 6291456 | bytes 16777216 | tf_op jit(solution)/shard_map/pallas_call | solution.py:97
  74.3 3.3 copy-done.3
  77.7 15.3 %shard_map.97 = (f32[40,32,128]{2,1,0:T(8,128)S(1)}, f32[40,32,128]{2,1,0:T(8,128)S(1)}, f32[40,32,128]{2,1,0:T(8,128)S(1)}, f32[40,32,128]{2,1,0:T(8,128)S(1)},...) custom-call(s32[256]{0:T(256)S(1)} %get-tuple-element.160.row_ref, ...), custom_call_target="tpu_custom_call" | custom-call | flops 1073741824 | bytes 23068672 | tf_op jit(solution)/shard_map/pallas_call | solution.py:185
  99.1 3.2 collective-permute-done.22
  121.6 3.8 collective-permute-done.19
  125.4 4.9 %collective-permute-done.20 = f32[10,32,128]{2,1,0:T(8,128)S(1)} collective-permute-done((f32[10,32,128]{2,1,0:T(8,128)S(1)}, f32[10,32,128]{2,1,0:T(8,128)S(1)}, u32[]{:S(2)}, u32[]{:S(2)}) %collective-permute-start.20) | collective-permute-done | bytes 163872 | tf_op jit(solution)/shard_map/ppermute | solution.py:38
  130.4 4.3 %collective-permute-start.27 = (f32[10,32,128]{2,1,0:T(8,128)S(1)}, f32[10,32,128]{2,1,0:T(8,128)S(1)}, u32[]{:S(2)}, u32[]{:S(2)}) collective-permute-start(f32[10,32,128]{2,1,0:T(8,128)S(1)} %slice.646), channel_id=1, source_target_pairs={{0,8},{2,10},{4,12},{6,14},{8,16},{10,18},{12,20},{14,22},{16,24},... | collective-permute-start | bytes 491528 | tf_op jit(solution)/shard_map/ppermute | solution.py:38
  139.7 5.0 %collective-permute-done.28 = f32[10,32,128]{2,1,0:T(8,128)S(1)} collective-permute-done((f32[10,32,128]{2,1,0:T(8,128)S(1)}, f32[10,32,128]{2,1,0:T(8,128)S(1)}, u32[]{:S(2)}, u32[]{:S(2)}) %collective-permute-start.28) | collective-permute-done | bytes 163872 | tf_op jit(solution)/shard_map/ppermute | solution.py:38
  148.1 4.5 %collective-permute-done.32 = f32[20,32,128]{2,1,0:T(8,128)S(1)} collective-permute-done((f32[20,32,128]{2,1,0:T(8,128)S(1)}, f32[20,32,128]{2,1,0:T(8,128)S(1)}, u32[]{:S(2)}, u32[]{:S(2)}) %collective-permute-start.32) | collective-permute-done | bytes 327712 | tf_op jit(solution)/shard_map/ppermute | solution.py:38
  156.9 3.4 collective-permute-start.36
  160.2 3.2 collective-permute-start.37
  174.1 15.0 %shard_map.98 = (f32[40,32,128]{2,1,0:T(8,128)S(1)}, f32[40,32,128]{2,1,0:T(8,128)}, f32[40,32,128]{2,1,0:T(8,128)S(1)}, f32[40,32,128]{2,1,0:T(8,128)}, f32[8,3...) custom-call(s32[256]{0:T(256)S(1)} %get-tuple-element.160.row_ref, ...), custom_call_target="tpu_custom_call" | custom-call | flops 1073741824 | bytes 23068672 | tf_op jit(solution)/shard_map/pallas_call | solution.py:185
  220.1 6.8 %collective-permute-done.44 = f32[10,32,128]{2,1,0:T(8,128)S(1)} collective-permute-done((f32[10,32,128]{2,1,0:T(8,128)S(1)}, f32[10,32,128]{2,1,0:T(8,128)S(1)}, u32[]{:S(2)}, u32[]{:S(2)}) %collective-permute-start.44) | collective-permute-done | bytes 163872 | tf_op jit(solution)/shard_map/ppermute | solution.py:38
  232.5 3.7 collective-permute-done.51
  236.2 4.7 %collective-permute-done.52 = f32[10,32,128]{2,1,0:T(8,128)S(1)} collective-permute-done((f32[10,32,128]{2,1,0:T(8,128)S(1)}, f32[10,32,128]{2,1,0:T(8,128)S(1)}, u32[]{:S(2)}, u32[]{:S(2)}) %collective-permute-start.52) | collective-permute-done | bytes 163872 | tf_op jit(solution)/shard_map/ppermute | solution.py:38
  254.3 44.2 %all_gather.6 = f32[192,2,128]{2,1,0:T(2,128)S(1)} all-gather(f32[6,2,128]{2,1,0:T(2,128)S(1)} %pad_maximum_fusion.24), channel_id=1, replica_groups=mesh['row'=8,'x'=2,'core'=2] {'row','x','core'}, dimensions={0}, use_global_device_ids=true | all-gather | bytes 202752 | tf_op jit(solution)/shard_map/all_gather | solution.py:293
  298.7 3.7 collective-permute-start.62
  307.5 4.0 collective-permute-done.61.refs_7_
  319.3 16.0 %shard_map.99 = (f32[40,32,128]{2,1,0:T(8,128)S(1)}, f32[40,32,128]{2,1,0:T(8,128)}, f32[40,32,128]{2,1,0:T(8,128)S(1)}, f32[40,32,128]{2,1,0:T(8,128)}, f32[8,3...) custom-call(s32[256]{0:T(256)S(1)} %get-tuple-element.160.row_ref, ...), custom_call_target="tpu_custom_call" | custom-call | flops 1073741824 | bytes 23068672 | tf_op jit(solution)/shard_map/pallas_call | solution.py:185
  340.8 43.7 %all-gather = f32[32,1,128]{2,1,0:T(1,128)S(1)} all-gather(f32[1,1,128]{2,1,0:T(1,128)S(1)} %pad_bitcast_fusion), channel_id=1, replica_groups=mesh['row'=8,'x'=2,'core'=2] {'row','x','core'}, dimensions={0}, use_global_device_ids=true | all-gather | bytes 16896 | tf_op jit(solution)/shard_map/all_gather | solution.py:305
  391.1 6.0 %collective-permute-done.64 = f32[20,32,128]{2,1,0:T(8,128)S(1)} collective-permute-done((f32[20,32,128]{2,1,0:T(8,128)S(1)}, f32[20,32,128]{2,1,0:T(8,128)S(1)}, u32[]{:S(2)}, u32[]{:S(2)}) %collective-permute-start.64) | collective-permute-done | bytes 327712 | tf_op jit(solution)/shard_map/ppermute | solution.py:38
  397.6 3.7 collective-permute-start.69
  401.3 5.0 %collective-permute-done.67 = f32[10,32,128]{2,1,0:T(8,128)S(1)} collective-permute-done((f32[10,32,128]{2,1,0:T(8,128)S(1)}, f32[10,32,128]{2,1,0:T(8,128)S(1)}, u32[]{:S(2)}, u32[]{:S(2)}) %collective-permute-start.67) | collective-permute-done | bytes 163872 | tf_op jit(solution)/shard_map/ppermute | solution.py:38
  406.3 5.4 %collective-permute-done.68 = f32[10,32,128]{2,1,0:T(8,128)S(1)} collective-permute-done((f32[10,32,128]{2,1,0:T(8,128)S(1)}, f32[10,32,128]{2,1,0:T(8,128)S(1)}, u32[]{:S(2)}, u32[]{:S(2)}) %collective-permute-start.68) | collective-permute-done | bytes 163872 | tf_op jit(solution)/shard_map/ppermute | solution.py:38
  (313 shorter events, 149.7 us)
Async XLA Ops:
  0.6 64.4 %collective-permute-start.2 = (f32[128,128,128]{2,1,0:T(8,128)}, f32[128,128,128]{2,1,0:T(8,128)}, u32[]{:S(2)}, u32[]{:S(2)}) collective-permute-start(f32[128,128,128]{2,1,0:T(8,128)} %tile_ref.1), channel_id=1, source_target_pairs={{0,1},{1,0},{2,3},{3,2},{4,5},{5,4},{6,7},{7,6},{8,9},{9,8},{10,11... | collective-permute-start | bytes 25165832 | tf_op jit(solution)/shard_map/ppermute | solution.py:261
  3.0 11.2 %collective-permute-start = (f32[6,48,128]{2,1,0:T(8,128)S(1)}, f32[6,48,128]{2,1,0:T(8,128)S(1)}, u32[]{:S(2)}, u32[]{:S(2)}) collective-permute-start(f32[6,48,128]{2,1,0:T(8,128)S(1)} %pad_maximum_fusion.16), channel_id=1, source_target_pairs={{0,1},{1,0},{2,3},{3,2},{4,5},{5,4},{6,7},{7,6},{8,9},{9,8},{10,11... | collective-permute-start | bytes 442376 | tf_op jit(solution)/shard_map/ppermute | solution.py:284
  18.5 13.6 %collective-permute-start.4 = (f32[10,32,128]{2,1,0:T(8,128)S(1)}, f32[10,32,128]{2,1,0:T(8,128)S(1)}, u32[]{:S(2)}, u32[]{:S(2)}) collective-permute-start(f32[10,32,128]{2,1,0:T(8,128)S(1)} %slice.606), channel_id=1, source_target_pairs={{0,16},{2,18},{4,20},{6,22},{8,24},{10,26},{12,28},{14,30},{16,0},... | collective-permute-start | bytes 491528 | tf_op jit(solution)/shard_map/ppermute | solution.py:38
  21.1 11.1 %collective-permute-start.5 = (f32[10,32,128]{2,1,0:T(8,128)S(1)}, f32[10,32,128]{2,1,0:T(8,128)S(1)}, u32[]{:S(2)}, u32[]{:S(2)}) collective-permute-start(f32[10,32,128]{2,1,0:T(8,128)S(1)} %slice.606), channel_id=1, source_target_pairs={{0,24},{2,26},{4,28},{6,30},{8,0},{10,2},{12,4},{14,6},{16,8},{18,... | collective-permute-start | bytes 491528 | tf_op jit(solution)/shard_map/ppermute | solution.py:38
  36.2 28.4 %collective-permute-start.1 = (s32[128]{0:T(128)S(1)}, s32[128]{0:T(128)S(1)}, u32[]{:S(2)}, u32[]{:S(2)}) collective-permute-start(s32[128]{0:T(128)S(1)} %compare_select_fusion.24), channel_id=1, source_target_pairs={{0,1},{1,0},{2,3},{3,2},{4,5},{5,4},{6,7},{7,6},{8,9},{9,8},{10,11... | collective-permute-start | bytes 1544 | tf_op jit(solution)/shard_map/ppermute | solution.py:267
  36.3 19.4 %collective-permute-start.10 = (f32[2,32,128]{2,1,0:T(8,128)S(1)}, f32[2,32,128]{2,1,0:T(8,128)S(1)}, u32[]{:S(2)}, u32[]{:S(2)}) collective-permute-start(f32[2,32,128]{2,1,0:T(8,128)S(1)} %slice.614), channel_id=1, source_target_pairs={{0,2},{2,0},{4,6},{6,4},{8,10},{10,8},{12,14},{14,12},{16,18},{18,... | collective-permute-start | bytes 98312 | tf_op jit(solution)/shard_map/ppermute | solution.py:38
  41.9 35.8 %collective-permute-start.9 = (f32[40,32,128]{2,1,0:T(8,128)S(1)}, f32[40,32,128]{2,1,0:T(8,128)S(1)}, u32[]{:S(2)}, u32[]{:S(2)}) collective-permute-start(f32[40,32,128]{2,1,0:T(8,128)S(1)} %constant_dynamic-update-slice_fusion.5.refs_2_), channel_id=1, source_target_pairs={{0,2},{2,0},{4,6},{6,4},{8,10},{10,8},{12,14},{14,12},{16,18},{18,... | collective-permute-start | bytes 1966088 | tf_op jit(solution)/shard_map/ppermute | solution.py:38
  43.6 34.1 %collective-permute-start.7 = (f32[40,32,128]{2,1,0:T(8,128)S(1)}, f32[40,32,128]{2,1,0:T(8,128)S(1)}, u32[]{:S(2)}, u32[]{:S(2)}) collective-permute-start(f32[40,32,128]{2,1,0:T(8,128)S(1)} %constant_dynamic-update-slice_fusion.refs_0_), channel_id=1, source_target_pairs={{0,4},{2,6},{4,0},{6,2},{8,12},{10,14},{12,8},{14,10},{16,20},{18,... | collective-permute-start | bytes 1966088 | tf_op jit(solution)/shard_map/ppermute | solution.py:38
  60.4 17.3 %collective-permute-start.12 = (f32[8,32,128]{2,1,0:T(8,128)S(1)}, f32[8,32,128]{2,1,0:T(8,128)S(1)}, u32[]{:S(2)}, u32[]{:S(2)}) collective-permute-start(f32[8,32,128]{2,1,0:T(8,128)S(1)} %pad_maximum_fusion.17.refs_4_), channel_id=1, source_target_pairs={{0,8},{2,10},{4,12},{6,14},{8,16},{10,18},{12,20},{14,22},{16,24},... | collective-permute-start | bytes 393224 | tf_op jit(solution)/shard_map/ppermute | solution.py:38
  64.6 13.1 %collective-permute-start.13 = (f32[8,32,128]{2,1,0:T(8,128)S(1)}, f32[8,32,128]{2,1,0:T(8,128)S(1)}, u32[]{:S(2)}, u32[]{:S(2)}) collective-permute-start(f32[8,32,128]{2,1,0:T(8,128)S(1)} %pad_maximum_fusion.17.refs_4_), channel_id=1, source_target_pairs={{0,16},{2,18},{4,20},{6,22},{8,24},{10,26},{12,28},{14,30},{16,0},... | collective-permute-start | bytes 393224 | tf_op jit(solution)/shard_map/ppermute | solution.py:38
  65.1 12.6 %collective-permute-start.14 = (f32[8,32,128]{2,1,0:T(8,128)S(1)}, f32[8,32,128]{2,1,0:T(8,128)S(1)}, u32[]{:S(2)}, u32[]{:S(2)}) collective-permute-start(f32[8,32,128]{2,1,0:T(8,128)S(1)} %pad_maximum_fusion.17.refs_4_), channel_id=1, source_target_pairs={{0,24},{2,26},{4,28},{6,30},{8,0},{10,2},{12,4},{14,6},{16,8},{18,... | collective-permute-start | bytes 393224 | tf_op jit(solution)/shard_map/ppermute | solution.py:38
  93.0 15.4 %collective-permute-start.15 = (f32[40,32,128]{2,1,0:T(8,128)S(1)}, f32[40,32,128]{2,1,0:T(8,128)S(1)}, u32[]{:S(2)}, u32[]{:S(2)}) collective-permute-start(f32[40,32,128]{2,1,0:T(8,128)S(1)} %get-tuple-element.28), channel_id=1, source_target_pairs={{0,4},{2,6},{4,0},{6,2},{8,12},{10,14},{12,8},{14,10},{16,20},{18,... | collective-permute-start | bytes 1966088 | tf_op jit(solution)/shard_map/ppermute | solution.py:38
  94.6 15.6 %collective-permute-start.17 = (f32[40,32,128]{2,1,0:T(8,128)S(1)}, f32[40,32,128]{2,1,0:T(8,128)S(1)}, u32[]{:S(2)}, u32[]{:S(2)}) collective-permute-start(f32[40,32,128]{2,1,0:T(8,128)S(1)} %get-tuple-element.30), channel_id=1, source_target_pairs={{0,2},{2,0},{4,6},{6,4},{8,10},{10,8},{12,14},{14,12},{16,18},{18,... | collective-permute-start | bytes 1966088 | tf_op jit(solution)/shard_map/ppermute | solution.py:38
  118.8 11.5 %collective-permute-start.20 = (f32[10,32,128]{2,1,0:T(8,128)S(1)}, f32[10,32,128]{2,1,0:T(8,128)S(1)}, u32[]{:S(2)}, u32[]{:S(2)}) collective-permute-start(f32[10,32,128]{2,1,0:T(8,128)S(1)} %pad_maximum_fusion.8), channel_id=1, source_target_pairs={{0,16},{2,18},{4,20},{6,22},{8,24},{10,26},{12,28},{14,30},{16,0},... | collective-permute-start | bytes 491528 | tf_op jit(solution)/shard_map/ppermute | solution.py:38
  152.6 17.7 %collective-permute-start.33 = (f32[40,32,128]{2,1,0:T(8,128)S(1)}, f32[40,32,128]{2,1,0:T(8,128)S(1)}, u32[]{:S(2)}, u32[]{:S(2)}) collective-permute-start(f32[40,32,128]{2,1,0:T(8,128)S(1)} %constant_dynamic-update-slice_fusion.15.refs_2_), channel_id=1, source_target_pairs={{0,2},{2,0},{4,6},{6,4},{8,10},{10,8},{12,14},{14,12},{16,18},{18,... | collective-permute-start | bytes 1966088 | tf_op jit(solution)/shard_map/ppermute | solution.py:38
  155.0 15.3 %collective-permute-start.31 = (f32[40,32,128]{2,1,0:T(8,128)S(1)}, f32[40,32,128]{2,1,0:T(8,128)S(1)}, u32[]{:S(2)}, u32[]{:S(2)}) collective-permute-start(f32[40,32,128]{2,1,0:T(8,128)S(1)} %constant_dynamic-update-slice_fusion.10.refs_0_), channel_id=1, source_target_pairs={{0,4},{2,6},{4,0},{6,2},{8,12},{10,14},{12,8},{14,10},{16,20},{18,... | collective-permute-start | bytes 1966088 | tf_op jit(solution)/shard_map/ppermute | solution.py:38
  189.7 14.7 %collective-permute-start.39 = (f32[40,32,128]{2,1,0:T(8,128)}, f32[40,32,128]{2,1,0:T(8,128)S(1)}, u32[]{:S(2)}, u32[]{:S(2)}) collective-permute-start(f32[40,32,128]{2,1,0:T(8,128)} %get-tuple-element.36), channel_id=1, source_target_pairs={{0,4},{2,6},{4,0},{6,2},{8,12},{10,14},{12,8},{14,10},{16,20},{18,... | collective-permute-start | bytes 1966088 | tf_op jit(solution)/shard_map/ppermute | solution.py:38
  190.6 14.8 %collective-permute-start.41 = (f32[40,32,128]{2,1,0:T(8,128)}, f32[40,32,128]{2,1,0:T(8,128)S(1)}, u32[]{:S(2)}, u32[]{:S(2)}) collective-permute-start(f32[40,32,128]{2,1,0:T(8,128)} %get-tuple-element.38), channel_id=1, source_target_pairs={{0,2},{2,0},{4,6},{6,4},{8,10},{10,8},{12,14},{14,12},{16,18},{18,... | collective-permute-start | bytes 1966088 | tf_op jit(solution)/shard_map/ppermute | solution.py:38
  214.9 11.9 %collective-permute-start.44 = (f32[10,32,128]{2,1,0:T(8,128)S(1)}, f32[10,32,128]{2,1,0:T(8,128)S(1)}, u32[]{:S(2)}, u32[]{:S(2)}) collective-permute-start(f32[10,32,128]{2,1,0:T(8,128)S(1)} %pad_maximum_fusion.11), channel_id=1, source_target_pairs={{0,16},{2,18},{4,20},{6,22},{8,24},{10,26},{12,28},{14,30},{16,0},... | collective-permute-start | bytes 491528 | tf_op jit(solution)/shard_map/ppermute | solution.py:38
  248.3 64.6 %collective-permute-start.57 = (f32[40,32,128]{2,1,0:T(8,128)S(1)}, f32[40,32,128]{2,1,0:T(8,128)S(1)}, u32[]{:S(2)}, u32[]{:S(2)}) collective-permute-start(f32[40,32,128]{2,1,0:T(8,128)S(1)} %constant_dynamic-update-slice_fusion.25.refs_3_), channel_id=1, source_target_pairs={{0,2},{2,0},{4,6},{6,4},{8,10},{10,8},{12,14},{14,12},{16,18},{18,... | collective-permute-start | bytes 1966088 | tf_op jit(solution)/shard_map/ppermute | solution.py:38
  251.4 61.4 %collective-permute-start.55 = (f32[40,32,128]{2,1,0:T(8,128)S(1)}, f32[40,32,128]{2,1,0:T(8,128)S(1)}, u32[]{:S(2)}, u32[]{:S(2)}) collective-permute-start(f32[40,32,128]{2,1,0:T(8,128)S(1)} %constant_dynamic-update-slice_fusion.20.refs_1_), channel_id=1, source_target_pairs={{0,4},{2,6},{4,0},{6,2},{8,12},{10,14},{12,8},{14,10},{16,20},{18,... | collective-permute-start | bytes 1966088 | tf_op jit(solution)/shard_map/ppermute | solution.py:38
  252.9 45.6 %collective-permute-start.59 = (f32[4,32,128]{2,1,0:T(8,128)S(1)}, f32[4,32,128]{2,1,0:T(8,128)S(1)}, u32[]{:S(2)}, u32[]{:S(2)}) collective-permute-start(f32[4,32,128]{2,1,0:T(8,128)S(1)} %pad_maximum_fusion.22), channel_id=1, source_target_pairs={{0,4},{2,6},{4,0},{6,2},{8,12},{10,14},{12,8},{14,10},{16,20},{18,... | collective-permute-start | bytes 196616 | tf_op jit(solution)/shard_map/ppermute | solution.py:38
  298.6 12.9 %collective-permute-start.61 = (f32[8,32,128]{2,1,0:T(8,128)S(1)}, f32[8,32,128]{2,1,0:T(8,128)S(1)}, u32[]{:S(2)}, u32[]{:S(2)}) collective-permute-start(f32[8,32,128]{2,1,0:T(8,128)S(1)} %pad_maximum_fusion.19.refs_5_), channel_id=1, source_target_pairs={{0,16},{2,18},{4,20},{6,22},{8,24},{10,26},{12,28},{14,30},{16,0},... | collective-permute-start | bytes 393224 | tf_op jit(solution)/shard_map/ppermute | solution.py:38
  298.7 13.5 %collective-permute-start.62 = (f32[8,32,128]{2,1,0:T(8,128)S(1)}, f32[8,32,128]{2,1,0:T(8,128)S(1)}, u32[]{:S(2)}, u32[]{:S(2)}) collective-permute-start(f32[8,32,128]{2,1,0:T(8,128)S(1)} %pad_maximum_fusion.19.refs_5_), channel_id=1, source_target_pairs={{0,24},{2,26},{4,28},{6,30},{8,0},{10,2},{12,4},{14,6},{16,8},{18,... | collective-permute-start | bytes 393224 | tf_op jit(solution)/shard_map/ppermute | solution.py:38
  336.0 49.6 %collective-permute-start.63 = (f32[40,32,128]{2,1,0:T(8,128)}, f32[40,32,128]{2,1,0:T(8,128)}, u32[]{:S(2)}, u32[]{:S(2)}) collective-permute-start(f32[40,32,128]{2,1,0:T(8,128)} %get-tuple-element.44), channel_id=1, source_target_pairs={{0,4},{2,6},{4,0},{6,2},{8,12},{10,14},{12,8},{14,10},{16,20},{18,... | collective-permute-start | bytes 1966088 | tf_op jit(solution)/shard_map/ppermute | solution.py:38
  336.0 50.9 %collective-permute-start.65 = (f32[40,32,128]{2,1,0:T(8,128)}, f32[40,32,128]{2,1,0:T(8,128)S(1)}, u32[]{:S(2)}, u32[]{:S(2)}) collective-permute-start(f32[40,32,128]{2,1,0:T(8,128)} %get-tuple-element.46), channel_id=1, source_target_pairs={{0,2},{2,0},{4,6},{6,4},{8,10},{10,8},{12,14},{14,12},{16,18},{18,... | collective-permute-start | bytes 1966088 | tf_op jit(solution)/shard_map/ppermute | solution.py:38
  336.1 48.5 %collective-permute-start.70 = (f32[8,32,128]{2,1,0:T(8,128)}, f32[8,32,128]{2,1,0:T(8,128)S(1)}, u32[]{:S(2)}, u32[]{:S(2)}) collective-permute-start(f32[8,32,128]{2,1,0:T(8,128)} %get-tuple-element.48), channel_id=1, source_target_pairs={{0,8},{2,10},{4,12},{6,14},{8,16},{10,18},{12,20},{14,22},{16,24},... | collective-permute-start | bytes 393224 | tf_op jit(solution)/shard_map/ppermute | solution.py:38
  338.2 46.3 %collective-permute-start.71 = (f32[8,32,128]{2,1,0:T(8,128)}, f32[8,32,128]{2,1,0:T(8,128)S(1)}, u32[]{:S(2)}, u32[]{:S(2)}) collective-permute-start(f32[8,32,128]{2,1,0:T(8,128)} %get-tuple-element.49), channel_id=1, source_target_pairs={{0,16},{2,18},{4,20},{6,22},{8,24},{10,26},{12,28},{14,30},{16,0},... | collective-permute-start | bytes 393224 | tf_op jit(solution)/shard_map/ppermute | solution.py:38
  339.5 45.1 %collective-permute-start.72 = (f32[8,32,128]{2,1,0:T(8,128)}, f32[8,32,128]{2,1,0:T(8,128)S(1)}, u32[]{:S(2)}, u32[]{:S(2)}) collective-permute-start(f32[8,32,128]{2,1,0:T(8,128)} %get-tuple-element.50), channel_id=1, source_target_pairs={{0,24},{2,26},{4,28},{6,30},{8,0},{10,2},{12,4},{14,6},{16,8},{18,... | collective-permute-start | bytes 393224 | tf_op jit(solution)/shard_map/ppermute | solution.py:38
  389.9 11.4 %collective-permute-start.74 = (f32[2,32,128]{2,1,0:T(8,128)S(1)}, f32[2,32,128]{2,1,0:T(8,128)S(1)}, u32[]{:S(2)}, u32[]{:S(2)}) collective-permute-start(f32[2,32,128]{2,1,0:T(8,128)S(1)} %slice_add_fusion.54), channel_id=1, source_target_pairs={{0,2},{2,0},{4,6},{6,4},{8,10},{10,8},{12,14},{14,12},{16,18},{18,... | collective-permute-start | bytes 98312 | tf_op jit(solution)/shard_map/ppermute | solution.py:38
  397.3 14.3 %collective-permute-start.68 = (f32[10,32,128]{2,1,0:T(8,128)S(1)}, f32[10,32,128]{2,1,0:T(8,128)S(1)}, u32[]{:S(2)}, u32[]{:S(2)}) collective-permute-start(f32[10,32,128]{2,1,0:T(8,128)S(1)} %pad_maximum_fusion.14), channel_id=1, source_target_pairs={{0,16},{2,18},{4,20},{6,22},{8,24},{10,26},{12,28},{14,30},{16,0},... | collective-permute-start | bytes 491528 | tf_op jit(solution)/shard_map/ppermute | solution.py:38
  397.6 14.1 %collective-permute-start.69 = (f32[10,32,128]{2,1,0:T(8,128)S(1)}, f32[10,32,128]{2,1,0:T(8,128)S(1)}, u32[]{:S(2)}, u32[]{:S(2)}) collective-permute-start(f32[10,32,128]{2,1,0:T(8,128)S(1)} %pad_maximum_fusion.15), channel_id=1, source_target_pairs={{0,24},{2,26},{4,28},{6,30},{8,0},{10,2},{12,4},{14,6},{16,8},{18,... | collective-permute-start | bytes 491528 | tf_op jit(solution)/shard_map/ppermute | solution.py:38
  (79 other events, 1278.3 us)

commit v4 on v2

v4 whole, which is shorter than its diff:
```python
import functools

import jax
import jax.numpy as jnp
from jax import lax
from jax.experimental import pallas as pl
from jax.experimental.pallas import tpu as pltpu
from jax.sharding import Mesh
from jax.sharding import PartitionSpec as P

ITERS = 3
CORES = 2
STEP = 16
UNROLL = 8
VMEM = 60 * 1024 * 1024
PLANE = ("y", "x")
CHIPS = ("z", "y", "x")
ALL = ("z", "y", "x", "core")


def depth_of(n_rows):
    return min(n for n in range(1, n_rows + 1) if n_rows % n == 0 and n * n >= n_rows)


def exchange(blocks, axes):
    return lax.all_to_all(blocks, axes, split_axis=0, concat_axis=0, tiled=True)


def spread(block, axes):
    return exchange(jnp.concatenate([block] * lax.axis_size(axes), axis=0), axes)


def fold(blocks, axes):
    got = exchange(blocks, axes)
    return jnp.sum(got.reshape((lax.axis_size(axes), -1) + got.shape[1:]), axis=0)


def after(value, *others):
    return lax.optimization_barrier((value,) + others)[0]


def split_kernel(tile_ref, pair_ref):
    size = tile_ref.shape[1]

    @pl.loop(0, STEP // UNROLL)
    def _(group):
        for k in range(UNROLL):
            tile = jnp.transpose(tile_ref[group * UNROLL + k])
            high = tile.astype(jnp.bfloat16)
            low = (tile - high.astype(jnp.float32)).astype(jnp.bfloat16)
            pair_ref[group * UNROLL + k, :size] = high
            pair_ref[group * UNROLL + k, size:] = low


def split_tiles(tiles):
    length, size, _ = tiles.shape
    return pl.pallas_call(
        split_kernel,
        out_shape=jax.ShapeDtypeStruct((length, 2 * size, size), jnp.bfloat16),
        grid=(length // STEP,),
        in_specs=[pl.BlockSpec((STEP, size, size), lambda i: (i, 0, 0))],
        out_specs=pl.BlockSpec((STEP, 2 * size, size), lambda i: (i, 0, 0)),
        compiler_params=pltpu.CompilerParams(vmem_limit_bytes=VMEM),
        cost_estimate=pl.CostEstimate(
            flops=3 * length * size * size, bytes_accessed=8 * length * size * size, transcendentals=0
        ),
    )(tiles)


def apply_kernel(length, counts, row_ref, col_ref, used_ref, own_ref, other_ref, *refs):
    step = pl.program_id(0)
    pieces = len(counts)
    given, outs = refs[:pieces], refs[pieces : 2 * pieces]
    flux_ref, sum_ref, sem = refs[2 * pieces :]
    starts = [sum(counts[:k]) for k in range(pieces)]

    @pl.when(step == 0)
    def _():
        copies = [
            pltpu.make_async_copy(given[k], flux_ref.at[pl.ds(starts[k], counts[k])], sem.at[k])
            for k in range(pieces)
        ]
        for copy in copies:
            copy.start()
        sum_ref[...] = jnp.zeros_like(sum_ref)
        for copy in copies:
            copy.wait()

    def add_tile(pair, slot):
        flux = flux_ref[col_ref[slot]] * used_ref[slot]
        high = flux.astype(jnp.bfloat16)
        low = (flux - high.astype(jnp.float32)).astype(jnp.bfloat16)
        left = jnp.concatenate([high, low], axis=0)
        both = jnp.dot(
            jnp.concatenate([left, left], axis=1), pair, preferred_element_type=jnp.float32
        )
        temps = flux.shape[0]
        sum_ref[row_ref[slot]] += both[:temps] + both[temps:]

    for part, ref in enumerate((own_ref, other_ref)):
        base = part * length + step * STEP

        @pl.loop(0, STEP // UNROLL)
        def _(group):
            for k in range(UNROLL):
                add_tile(ref[group * UNROLL + k], base + group * UNROLL + k)

    @pl.when(step == pl.num_programs(0) - 1)
    def _():
        copies = [
            pltpu.make_async_copy(sum_ref.at[pl.ds(starts[k], counts[k])], outs[k], sem.at[k])
            for k in range(pieces)
        ]
        for copy in copies:
            copy.start()
        for copy in copies:
            copy.wait()


def apply_tiles(row, col, used, own, other, pieces):
    length, _, size = own.shape
    counts = [piece.shape[0] for piece in pieces]
    temps = pieces[0].shape[1]
    num = sum(counts)
    some = pl.BlockSpec((STEP, 2 * size, size), lambda i, *_: (i, 0, 0))
    anywhere = pl.BlockSpec(memory_space=pl.ANY)
    return pl.pallas_call(
        functools.partial(apply_kernel, length, counts),
        out_shape=[jax.ShapeDtypeStruct(piece.shape, jnp.float32) for piece in pieces],
        grid_spec=pltpu.PrefetchScalarGridSpec(
            num_scalar_prefetch=3,
            grid=(length // STEP,),
            in_specs=[some, some] + [anywhere] * len(pieces),
            out_specs=[anywhere] * len(pieces),
            scratch_shapes=[
                pltpu.VMEM((num, temps, size), jnp.float32),
                pltpu.VMEM((num, temps, size), jnp.float32),
                pltpu.SemaphoreType.DMA((len(pieces),)),
            ],
        ),
        compiler_params=pltpu.CompilerParams(vmem_limit_bytes=VMEM),
        cost_estimate=pl.CostEstimate(
            flops=2 * 2 * length * size * size * temps * 4,
            bytes_accessed=4 * (2 * length * size * size + 2 * num * temps * size),
            transcendentals=0,
        ),
    )(row, col, used, own, other, *pieces)


def shards(
    tile_values, tile_owner, tile_row, tile_col, tile_count, relaxation, driving, heat_weight
):
    n_cols = lax.axis_size("x") * CORES
    planes, plane = lax.axis_size("z"), lax.axis_size(PLANE)
    chips = planes * plane
    length, size, _ = tile_values.shape
    modes, columns = driving.shape
    per = modes // size
    chip_tiles = CORES * per
    num = chips * chip_tiles
    half = columns // CORES
    core = lax.axis_index("core")
    swap = [(0, 1), (1, 0)]

    second = chip_tiles - max(1, chip_tiles // 6)
    bounds = (0, second // 2, second, chip_tiles)
    parts = list(zip(bounds[:-1], bounds[1:]))

    def place(tile):
        chip, inside = tile // chip_tiles, tile % chip_tiles
        z, at = chip // plane, chip % plane
        out = jnp.zeros_like(tile)
        for k, (low, high) in enumerate(parts):
            slot = z * plane + at if k == 2 else at * planes + z
            slot = chips * low + slot * (high - low) + inside - low
            out = jnp.where((inside >= low) & (inside < high), slot, out)
        return out

    other_values = lax.ppermute(tile_values, "core", swap)
    owners = tile_owner[:, 0]
    row = (owners // n_cols) * (n_cols * per) + tile_row
    col = ((tile_col // per) * n_cols + owners % n_cols) * per + tile_col % per
    used = jnp.arange(length, dtype=jnp.int32) < tile_count[0]
    places = jnp.where(used, place(row) * num + place(col), -1)
    places = jnp.concatenate([places, lax.ppermute(places, "core", swap)])
    is_used = places >= 0
    places = jnp.where(is_used, places, 0)
    row, col, used = places // num, places % num, is_used.astype(jnp.float32)

    def by_core(own, other):
        return jnp.concatenate(
            [jnp.where(core == 0, own, other), jnp.where(core == 0, other, own)], axis=0
        )

    drive = jnp.transpose(driving.reshape(per, size, columns), (0, 2, 1))
    relax = relaxation.reshape(per, 1, size)
    heat = heat_weight.reshape(per, 1, size)
    low, high = drive[:, :half], drive[:, half:]
    mine = jnp.where(core == 0, low, high)
    theirs = jnp.where(core == 0, high, low)
    packed = [theirs, jnp.broadcast_to(relax, (per, 8, size)), jnp.broadcast_to(heat, (per, 8, size))]
    got = lax.ppermute(jnp.concatenate(packed, axis=1), "core", swap)
    drive_half = by_core(mine, got[:, :half])
    relax_both = by_core(relax, got[:, half : half + 1])
    heat_both = by_core(heat, got[:, half + 8 : half + 9])

    own = split_tiles(tile_values)
    other = split_tiles(other_values)
    drives = [drive_half[low:high] for low, high in parts]
    relaxes = [relax_both[low:high] for low, high in parts]
    fluxes = [r * d for r, d in zip(relaxes, drives)]
    for sweep in range(ITERS):
        by_z = [spread(flux, "z") for flux in fluxes[:2]]
        by_plane = spread(fluxes[2], PLANE)
        first = spread(by_z[0], PLANE)
        third = spread(after(by_plane, by_z[1]), "z")
        second = spread(after(by_z[1], first), PLANE)
        sums = apply_tiles(row, col, used, own, other, [first, second, third])
        third = fold(sums[2], "z")
        first = fold(sums[0], PLANE)
        second = fold(after(sums[1], first), PLANE)
        summed = [fold(first, "z"), fold(second, "z"), fold(third, PLANE)]
        fluxes = [r * (d + s) for r, d, s in zip(relaxes, drives, summed)]
    flux = jnp.concatenate(fluxes, axis=0)
    weighted = jnp.sum(heat_both * flux, axis=(0, 2))
    totals = jnp.concatenate([weighted, jnp.sum(heat).reshape(1)])
    totals = spread(jnp.pad(totals[None], ((0, 0), (0, size - half - 1))), ALL)
    totals = jnp.sum(totals.reshape(chips, CORES, size), axis=0)
    conductivity = totals[:, :half].reshape(columns) / jnp.sum(totals[:, half])
    first, second = flux[:per], flux[per:]
    mine = jnp.where(core == 0, first, second)
    got = lax.ppermute(jnp.where(core == 0, second, first), "core", swap)
    both = jnp.concatenate(
        [jnp.where(core == 0, mine, got), jnp.where(core == 0, got, mine)], axis=1
    )
    mode_flux = jnp.transpose(both, (0, 2, 1)).reshape(modes, columns)
    return (mode_flux, conductivity)


def solution(mesh):
    n_rows, n_cols = mesh.shape["row"], mesh.shape["col"]
    planes = depth_of(n_rows)
    chips = Mesh(mesh.devices.reshape(planes, n_rows // planes, n_cols // CORES, CORES), ALL)
    placed = (
        P(ALL, None, None),
        P(ALL, None),
        P(ALL),
        P(ALL),
        P(ALL),
        P(ALL),
        P(ALL, None),
        P(ALL),
    )
    return jax.shard_map(
        shards,
        mesh=chips,
        in_specs=placed,
        out_specs=(P(ALL, None), P()),
        check_vma=False,
    )
```

time: 408 us -> 578 us (1.42)
  blocking collectives: 40.1 us -> 137 us
  waiting for transfers between devices: 164 us -> 232 us
  starting transfers between devices: 136 us -> 102 us
  other arithmetic: 4.84 us -> 28.2 us
  Pallas kernels: 58.3 us -> 67.1 us
    all_to_all x0 -> x27, waiting for transfers between devices: none -> 222 us  [exchange(): return lax.all_to_all(blocks, axes, split_axis=0, concat_axis=0, tiled=True)]
    ppermute x91 -> x1, waiting for transfers between devices: 162 us -> 9.25 us  [shards(): got = lax.ppermute(jnp.concatenate(packed, axis=1), 'core', swap)]
    all_to_all x0 -> x10, blocking collectives: none -> 137 us  [exchange(): return lax.all_to_all(blocks, axes, split_axis=0, concat_axis=0, tiled=True)]
    ppermute x91 -> x1, starting transfers between devices: 135 us -> 0.52 us  [shards(): got = lax.ppermute(jnp.concatenate(packed, axis=1), 'core', swap)]
    all_to_all x0 -> x27, starting transfers between devices: none -> 100 us  [exchange(): return lax.all_to_all(blocks, axes, split_axis=0, concat_axis=0, tiled=True)]
    psum x1 -> x0, blocking collectives: 40.1 us -> none  [shards(): weighted, weight_sum = lax.psum((weighted_local, jnp.sum(heat_weight)), ALL)]
    pallas_call x0 -> x2, Pallas kernels: none -> 20.6 us  [split_tiles(): pl.pallas_call(split_kernel, out_shape=jax.ShapeDtypeStruct((length, 2 *...]
    concatenate x13 -> x19, other arithmetic: 0.2 us -> 17.2 us  [the longest x18 17.2 us: spread(): jnp.concatenate([block] * lax.axis_size(axes), axis=0)]
  transfers between devices with their start and end apart: 94 -> 31, of which waited for: 50 -> 27; matrix products, arithmetic and copies ran while one was open for 1% -> 5% of each run, Pallas kernels for 0% -> 4%
where the time goes in v4:
time: 578 us; the launch traced here: 575 us
  waiting for transfers between devices  232 us (40%)
  blocking collectives  137 us (24%)
  starting transfers between devices  102 us (18%)
  Pallas kernels  67.1 us (12%)
  other arithmetic  28.2 us (5%)
  local copies, waits for them, and re-layouts  7.77 us (1%)
    all_to_all x27, waiting for transfers between devices, exchange(): return lax.all_to_all(blocks, axes, split_axis=0, concat_axis=0, tiled=True)  222 us
    all_to_all x10, blocking collectives, exchange(): return lax.all_to_all(blocks, axes, split_axis=0, concat_axis=0, tiled=True)  137 us
    all_to_all x27, starting transfers between devices, exchange(): return lax.all_to_all(blocks, axes, split_axis=0, concat_axis=0, tiled=True)  100 us
    pallas_call x3, Pallas kernels, apply_tiles(): pl.pallas_call(functools.partial(apply_kernel, length, counts), out_shape...  46.5 us
    pallas_call x2, Pallas kernels, split_tiles(): pl.pallas_call(split_kernel, out_shape=jax.ShapeDtypeStruct((length, 2 *...  20.6 us
    concatenate x18, other arithmetic, spread(): jnp.concatenate([block] * lax.axis_size(axes), axis=0)  17.2 us
  transfers between devices with their start and end apart: 31, of which 27 were waited for; matrix products, arithmetic and copies ran while one was open for 5% of the time, Pallas kernels for 4%

profile of v4, /device:TPU:0, one launch (start us, length us, event | category | flops | bytes accessed | tf_op | source)
XLA Modules:
  0.0 574.9 jit_solution(18415081937347295821)
XLA Ops:
  4.9 9.2 %collective-permute-done = f32[6,48,128]{2,1,0:T(8,128)S(1)} collective-permute-done((f32[6,48,128]{2,1,0:T(8,128)S(1)}, f32[6,48,128]{2,1,0:T(8,128)S(1)}, u32[]{:S(2)}, u32[]{:S(2)}) %collective-permute-start) | collective-permute-done | bytes 147488 | tf_op jit(solution)/shard_map/ppermute | solution.py:202
  30.6 8.4 %all-to-all-done = f32[20,32,128]{2,1,0:T(8,128)S(1)} async-done(((f32[20,32,128]{2,1,0:T(8,128)}), f32[20,32,128]{2,1,0:T(8,128)S(1)}, u32[]{:S(2)}, u32[]{:S(2)}) %all-to-all-start) | async-done | bytes 327712 | tf_op jit(solution)/shard_map/all_to_all | solution.py:26
  43.7 7.4 %all-to-all-done.2 = f32[20,32,128]{2,1,0:T(8,128)S(1)} async-done(((f32[20,32,128]{2,1,0:T(8,128)}), f32[20,32,128]{2,1,0:T(8,128)S(1)}, u32[]{:S(2)}, u32[]{:S(2)}) %all-to-all-start.2) | async-done | bytes 327712 | tf_op jit(solution)/shard_map/all_to_all | solution.py:26
  55.5 11.5 %all-to-all-done.1.refs_0_ = f32[80,32,128]{2,1,0:T(8,128)S(1)} async-done(((f32[80,32,128]{2,1,0:T(8,128)}), f32[80,32,128]{2,1,0:T(8,128)S(1)}, u32[]{:S(2)}, u32[]{:S(2)}) %all-to-all-start.1) | async-done | bytes 1310752 | tf_op jit(solution)/shard_map/all_to_all | solution.py:26
  73.9 12.4 %all-to-all-done.5.refs_2_ = f32[32,32,128]{2,1,0:T(8,128)S(1)} async-done(((f32[32,32,128]{2,1,0:T(8,128)}), f32[32,32,128]{2,1,0:T(8,128)S(1)}, u32[]{:S(2)}, u32[]{:S(2)}) %all-to-all-start.5) | async-done | bytes 524320 | tf_op jit(solution)/shard_map/all_to_all | solution.py:26
  91.4 10.3 %shard_map.95.own_ref = bf16[128,256,128]{2,1,0:T(8,128)(2,1)} custom-call(f32[128,128,128]{2,1,0:T(8,128)} %tile_ref.1), custom_call_target="tpu_custom_call" | custom-call | flops 6291456 | bytes 16777216 | tf_op jit(solution)/shard_map/pallas_call | solution.py:57
  102.9 10.3 %shard_map.96.other_ref = bf16[128,256,128]{2,1,0:T(8,128)(2,1)} custom-call(f32[128,128,128]{2,1,0:T(8,128)} %collective-permute-done.2.tile_ref), custom_call_target="tpu_custom_call" | custom-call | flops 6291456 | bytes 16777216 | tf_op jit(solution)/shard_map/pallas_call | solution.py:57
  114.2 15.5 %shard_map.97 = (f32[80,32,128]{2,1,0:T(8,128)}, f32[80,32,128]{2,1,0:T(8,128)}, f32[32,32,128]{2,1,0:T(8,128)}) custom-call(s32[256]{0:T(256)} %get-tuple-element.54.row_ref, s32[256]{0:T(256)} %get-tuple-element.53.col_ref, f32[256]{0:T(256)} %compare_convert_fusion.used_ref, bf16[128,256,128]{2,1,0:T(8,128)(2,1)} %shard_map.95.own_ref, ...), custom_call_target="tpu_custom_call" | custom-call | flops 1073741824 | bytes 23068672 | tf_op jit(solution)/shard_map/pallas_call | solution.py:127
  129.7 18.9 %all_to_all.186 = f32[32,32,128]{2,1,0:T(8,128)S(1)} all-to-all(f32[32,32,128]{2,1,0:T(8,128)} %get-tuple-element.26), channel_id=1, replica_groups=mesh['z'=4,'y'=2,'x'=2,'core'=2] {'z'}, dimensions={0} | all-to-all | bytes 1048576 | tf_op jit(solution)/shard_map/all_to_all | solution.py:26
  148.7 9.0 %all_to_all.187 = f32[8,32,128]{2,1,0:T(8,128)S(1)} all-to-all(f32[8,32,128]{2,1,0:T(8,128)S(1)} %reduce_sum.202), channel_id=1, replica_groups=mesh['z'=4,'y'=2,'x'=2,'core'=2] {'y','x'}, dimensions={0} | all-to-all | bytes 262144 | tf_op jit(solution)/shard_map/all_to_all | solution.py:26
  161.9 14.1 %all-to-all-done.6 = f32[80,32,128]{2,1,0:T(8,128)S(1)} async-done(((f32[80,32,128]{2,1,0:T(8,128)}), f32[80,32,128]{2,1,0:T(8,128)S(1)}, u32[]{:S(2)}, u32[]{:S(2)}) %all-to-all-start.6) | async-done | bytes 1310752 | tf_op jit(solution)/shard_map/all_to_all | solution.py:26
  184.3 17.7 %all_to_all.188 = f32[80,32,128]{2,1,0:T(8,128)S(1)} all-to-all(f32[80,32,128]{2,1,0:T(8,128)S(1)} %copy-done.9), channel_id=1, replica_groups=mesh['z'=4,'y'=2,'x'=2,'core'=2] {'y','x'}, dimensions={0} | all-to-all | bytes 2621440 | tf_op jit(solution)/shard_map/all_to_all | solution.py:26
  228.1 8.5 %all-to-all-done.8 = f32[20,32,128]{2,1,0:T(8,128)S(1)} async-done(((f32[20,32,128]{2,1,0:T(8,128)}), f32[20,32,128]{2,1,0:T(8,128)S(1)}, u32[]{:S(2)}, u32[]{:S(2)}) %all-to-all-start.8) | async-done | bytes 327712 | tf_op jit(solution)/shard_map/all_to_all | solution.py:26
  253.5 10.0 %all-to-all-done.9.refs_0_ = f32[80,32,128]{2,1,0:T(8,128)S(1)} async-done(((f32[80,32,128]{2,1,0:T(8,128)}), f32[80,32,128]{2,1,0:T(8,128)S(1)}, u32[]{:S(2)}, u32[]{:S(2)}) %all-to-all-start.9) | async-done | bytes 1310752 | tf_op jit(solution)/shard_map/all_to_all | solution.py:26
  268.6 8.7 %all-to-all-done.17.refs_2_ = f32[32,32,128]{2,1,0:T(8,128)S(1)} async-done(((f32[32,32,128]{2,1,0:T(8,128)}), f32[32,32,128]{2,1,0:T(8,128)S(1)}, u32[]{:S(2)}, u32[]{:S(2)}) %all-to-all-start.17) | async-done | bytes 524320 | tf_op jit(solution)/shard_map/all_to_all | solution.py:26
  277.3 14.5 %all_to_all.189.refs_1_ = f32[80,32,128]{2,1,0:T(8,128)} all-to-all(f32[80,32,128]{2,1,0:T(8,128)S(1)} %pad_maximum_fusion.3), channel_id=1, replica_groups=mesh['z'=4,'y'=2,'x'=2,'core'=2] {'y','x'}, dimensions={0} | all-to-all | bytes 2621440 | tf_op jit(solution)/shard_map/all_to_all | solution.py:26
  291.8 15.5 %shard_map.98 = (f32[80,32,128]{2,1,0:T(8,128)}, f32[80,32,128]{2,1,0:T(8,128)}, f32[32,32,128]{2,1,0:T(8,128)}) custom-call(s32[256]{0:T(256)} %get-tuple-element.54.row_ref, s32[256]{0:T(256)} %get-tuple-element.53.col_ref, f32[256]{0:T(256)} %compare_convert_fusion.used_ref, bf16[128,256,128]{2,1,0:T(8,128)(2,1)} %shard_map.95.own_ref, ...), custom_call_target="tpu_custom_call" | custom-call | flops 1073741824 | bytes 23068672 | tf_op jit(solution)/shard_map/pallas_call | solution.py:127
  307.3 13.7 %all_to_all.190 = f32[32,32,128]{2,1,0:T(8,128)S(1)} all-to-all(f32[32,32,128]{2,1,0:T(8,128)} %get-tuple-element.32), channel_id=1, replica_groups=mesh['z'=4,'y'=2,'x'=2,'core'=2] {'z'}, dimensions={0} | all-to-all | bytes 1048576 | tf_op jit(solution)/shard_map/all_to_all | solution.py:26
  321.1 7.4 %all_to_all.191 = f32[8,32,128]{2,1,0:T(8,128)S(1)} all-to-all(f32[8,32,128]{2,1,0:T(8,128)S(1)} %reduce_sum.208), channel_id=1, replica_groups=mesh['z'=4,'y'=2,'x'=2,'core'=2] {'y','x'}, dimensions={0} | all-to-all | bytes 262144 | tf_op jit(solution)/shard_map/all_to_all | solution.py:26
  332.8 14.6 %all-to-all-done.18 = f32[80,32,128]{2,1,0:T(8,128)S(1)} async-done(((f32[80,32,128]{2,1,0:T(8,128)}), f32[80,32,128]{2,1,0:T(8,128)S(1)}, u32[]{:S(2)}, u32[]{:S(2)}) %all-to-all-start.18) | async-done | bytes 1310752 | tf_op jit(solution)/shard_map/all_to_all | solution.py:26
  355.7 13.8 %all_to_all.192 = f32[80,32,128]{2,1,0:T(8,128)S(1)} all-to-all(f32[80,32,128]{2,1,0:T(8,128)S(1)} %copy-done.10), channel_id=1, replica_groups=mesh['z'=4,'y'=2,'x'=2,'core'=2] {'y','x'}, dimensions={0} | all-to-all | bytes 2621440 | tf_op jit(solution)/shard_map/all_to_all | solution.py:26
  373.8 10.0 %all-to-all-done.19 = f32[20,32,128]{2,1,0:T(8,128)S(1)} async-done(((f32[20,32,128]{2,1,0:T(8,128)}), f32[20,32,128]{2,1,0:T(8,128)S(1)}, u32[]{:S(2)}, u32[]{:S(2)}) %all-to-all-start.19) | async-done | bytes 327712 | tf_op jit(solution)/shard_map/all_to_all | solution.py:26
  388.0 9.2 %all-to-all-done.23 = f32[20,32,128]{2,1,0:T(8,128)S(1)} async-done(((f32[20,32,128]{2,1,0:T(8,128)}), f32[20,32,128]{2,1,0:T(8,128)S(1)}, u32[]{:S(2)}, u32[]{:S(2)}) %all-to-all-start.23) | async-done | bytes 327712 | tf_op jit(solution)/shard_map/all_to_all | solution.py:26
  412.8 11.5 %all-to-all-done.24 = f32[20,32,128]{2,1,0:T(8,128)S(1)} async-done(((f32[20,32,128]{2,1,0:T(8,128)}), f32[20,32,128]{2,1,0:T(8,128)S(1)}, u32[]{:S(2)}, u32[]{:S(2)}) %all-to-all-start.24) | async-done | bytes 327712 | tf_op jit(solution)/shard_map/all_to_all | solution.py:26
  429.4 15.6 %all-to-all-done.21.refs_0_ = f32[80,32,128]{2,1,0:T(8,128)S(1)} async-done(((f32[80,32,128]{2,1,0:T(8,128)}), f32[80,32,128]{2,1,0:T(8,128)S(1)}, u32[]{:S(2)}, u32[]{:S(2)}) %all-to-all-start.21) | async-done | bytes 1310752 | tf_op jit(solution)/shard_map/all_to_all | solution.py:26
  450.0 8.7 %all-to-all-done.29.refs_2_ = f32[32,32,128]{2,1,0:T(8,128)S(1)} async-done(((f32[32,32,128]{2,1,0:T(8,128)}), f32[32,32,128]{2,1,0:T(8,128)S(1)}, u32[]{:S(2)}, u32[]{:S(2)}) %all-to-all-start.29) | async-done | bytes 524320 | tf_op jit(solution)/shard_map/all_to_all | solution.py:26
  458.7 14.5 %all_to_all.193.refs_1_ = f32[80,32,128]{2,1,0:T(8,128)} all-to-all(f32[80,32,128]{2,1,0:T(8,128)S(1)} %pad_maximum_fusion.5), channel_id=1, replica_groups=mesh['z'=4,'y'=2,'x'=2,'core'=2] {'y','x'}, dimensions={0} | all-to-all | bytes 2621440 | tf_op jit(solution)/shard_map/all_to_all | solution.py:26
  473.2 15.5 %shard_map.99 = (f32[80,32,128]{2,1,0:T(8,128)}, f32[80,32,128]{2,1,0:T(8,128)}, f32[32,32,128]{2,1,0:T(8,128)}) custom-call(s32[256]{0:T(256)} %get-tuple-element.54.row_ref, s32[256]{0:T(256)} %get-tuple-element.53.col_ref, f32[256]{0:T(256)} %compare_convert_fusion.used_ref, bf16[128,256,128]{2,1,0:T(8,128)(2,1)} %shard_map.95.own_ref, ...), custom_call_target="tpu_custom_call" | custom-call | flops 1073741824 | bytes 23068672 | tf_op jit(solution)/shard_map/pallas_call | solution.py:127
  488.7 13.7 %all_to_all.194 = f32[32,32,128]{2,1,0:T(8,128)S(1)} all-to-all(f32[32,32,128]{2,1,0:T(8,128)} %get-tuple-element.37), channel_id=1, replica_groups=mesh['z'=4,'y'=2,'x'=2,'core'=2] {'z'}, dimensions={0} | all-to-all | bytes 1048576 | tf_op jit(solution)/shard_map/all_to_all | solution.py:26
  506.7 10.1 %all-to-all-done.30 = f32[80,32,128]{2,1,0:T(8,128)S(1)} async-done(((f32[80,32,128]{2,1,0:T(8,128)}), f32[80,32,128]{2,1,0:T(8,128)S(1)}, u32[]{:S(2)}, u32[]{:S(2)}) %all-to-all-start.30) | async-done | bytes 1310752 | tf_op jit(solution)/shard_map/all_to_all | solution.py:26
  525.1 13.8 %all_to_all.195 = f32[80,32,128]{2,1,0:T(8,128)S(1)} all-to-all(f32[80,32,128]{2,1,0:T(8,128)S(1)} %copy-done.11), channel_id=1, replica_groups=mesh['z'=4,'y'=2,'x'=2,'core'=2] {'y','x'}, dimensions={0} | all-to-all | bytes 2621440 | tf_op jit(solution)/shard_map/all_to_all | solution.py:26
  553.3 7.2 %all-to-all-done.33 = f32[20,32,128]{2,1,0:T(8,128)S(1)} async-done(((f32[20,32,128]{2,1,0:T(8,128)}), f32[20,32,128]{2,1,0:T(8,128)S(1)}, u32[]{:S(2)}, u32[]{:S(2)}) %all-to-all-start.33) | async-done | bytes 327712 | tf_op jit(solution)/shard_map/all_to_all | solution.py:26
  (157 shorter events, 192.0 us)
Async XLA Ops:
  0.6 102.2 %collective-permute-start.2 = (f32[128,128,128]{2,1,0:T(8,128)}, f32[128,128,128]{2,1,0:T(8,128)}, u32[]{:S(2)}, u32[]{:S(2)}) collective-permute-start(f32[128,128,128]{2,1,0:T(8,128)} %tile_ref.1), channel_id=1, source_target_pairs={{0,1},{1,0},{2,3},{3,2},{4,5},{5,4},{6,7},{7,6},{8,9},{9,8},{10,11... | collective-permute-start | bytes 25165832 | tf_op jit(solution)/shard_map/ppermute | solution.py:179
  3.0 11.2 %collective-permute-start = (f32[6,48,128]{2,1,0:T(8,128)S(1)}, f32[6,48,128]{2,1,0:T(8,128)S(1)}, u32[]{:S(2)}, u32[]{:S(2)}) collective-permute-start(f32[6,48,128]{2,1,0:T(8,128)S(1)} %pad_maximum_fusion.15), channel_id=1, source_target_pairs={{0,1},{1,0},{2,3},{3,2},{4,5},{5,4},{6,7},{7,6},{8,9},{9,8},{10,11... | collective-permute-start | bytes 442376 | tf_op jit(solution)/shard_map/ppermute | solution.py:202
  14.9 10.1 %all-to-all-start.4 = ((f32[8,32,128]{2,1,0:T(8,128)}), f32[8,32,128]{2,1,0:T(8,128)S(1)}, u32[]{:S(2)}, u32[]{:S(2)}) async-start(f32[8,32,128]{2,1,0:T(8,128)} %pad_maximum_fusion.16), calls=%async_computation.4 | async-start | bytes 262144 | tf_op jit(solution)/shard_map/all_to_all | solution.py:26
  25.0 14.0 %all-to-all-start = ((f32[20,32,128]{2,1,0:T(8,128)}), f32[20,32,128]{2,1,0:T(8,128)S(1)}, u32[]{:S(2)}, u32[]{:S(2)}) async-start(f32[20,32,128]{2,1,0:T(8,128)} %pad_maximum_fusion.9), calls=%async_computation | async-start | bytes 655360 | tf_op jit(solution)/shard_map/all_to_all | solution.py:26
  39.0 12.1 %all-to-all-start.2 = ((f32[20,32,128]{2,1,0:T(8,128)}), f32[20,32,128]{2,1,0:T(8,128)S(1)}, u32[]{:S(2)}, u32[]{:S(2)}) async-start(f32[20,32,128]{2,1,0:T(8,128)} %pad_maximum_fusion.10), calls=%async_computation.2 | async-start | bytes 655360 | tf_op jit(solution)/shard_map/all_to_all | solution.py:26
  51.1 15.9 %all-to-all-start.1 = ((f32[80,32,128]{2,1,0:T(8,128)}), f32[80,32,128]{2,1,0:T(8,128)S(1)}, u32[]{:S(2)}, u32[]{:S(2)}) async-start(f32[80,32,128]{2,1,0:T(8,128)} %pad_maximum_fusion), calls=%async_computation.1 | async-start | bytes 2621440 | tf_op jit(solution)/shard_map/all_to_all | solution.py:26
  67.0 19.3 %all-to-all-start.5 = ((f32[32,32,128]{2,1,0:T(8,128)}), f32[32,32,128]{2,1,0:T(8,128)S(1)}, u32[]{:S(2)}, u32[]{:S(2)}) async-start(f32[32,32,128]{2,1,0:T(8,128)} %pad_maximum_fusion.6), calls=%async_computation.5 | async-start | bytes 1048576 | tf_op jit(solution)/shard_map/all_to_all | solution.py:26
  87.1 26.1 %all-to-all-start.3 = ((f32[80,32,128]{2,1,0:T(8,128)}), f32[80,32,128]{2,1,0:T(8,128)S(1)}, u32[]{:S(2)}, u32[]{:S(2)}) async-start(f32[80,32,128]{2,1,0:T(8,128)} %pad_maximum_fusion.1), calls=%async_computation.3 | async-start | bytes 2621440 | tf_op jit(solution)/shard_map/all_to_all | solution.py:26
  91.4 10.4 %collective-permute-start.1 = (s32[128]{0:T(128)S(1)}, s32[128]{0:T(128)S(1)}, u32[]{:S(2)}, u32[]{:S(2)}) collective-permute-start(s32[128]{0:T(128)S(1)} %compare_select_fusion.1), channel_id=1, source_target_pairs={{0,1},{1,0},{2,3},{3,2},{4,5},{5,4},{6,7},{7,6},{8,9},{9,8},{10,11... | collective-permute-start | bytes 1544 | tf_op jit(solution)/shard_map/ppermute | solution.py:185
  157.6 18.4 %all-to-all-start.6 = ((f32[80,32,128]{2,1,0:T(8,128)}), f32[80,32,128]{2,1,0:T(8,128)S(1)}, u32[]{:S(2)}, u32[]{:S(2)}) async-start(f32[80,32,128]{2,1,0:T(8,128)} %get-tuple-element.22), calls=%async_computation.6 | async-start | bytes 2621440 | tf_op jit(solution)/shard_map/all_to_all | solution.py:26
  176.0 8.3 %all-to-all-start.16 = ((f32[8,32,128]{2,1,0:T(8,128)}), f32[8,32,128]{2,1,0:T(8,128)S(1)}, u32[]{:S(2)}, u32[]{:S(2)}) async-start(f32[8,32,128]{2,1,0:T(8,128)} %pad_maximum_fusion.17), calls=%async_computation.16 | async-start | bytes 262144 | tf_op jit(solution)/shard_map/all_to_all | solution.py:26
  202.0 10.7 %all-to-all-start.7 = ((f32[20,32,128]{2,1,0:T(8,128)}), f32[20,32,128]{2,1,0:T(8,128)S(1)}, u32[]{:S(2)}, u32[]{:S(2)}) async-start(f32[20,32,128]{2,1,0:T(8,128)} %reduce_sum.198), calls=%async_computation.7 | async-start | bytes 655360 | tf_op jit(solution)/shard_map/all_to_all | solution.py:26
  212.7 10.9 %all-to-all-start.11 = ((f32[20,32,128]{2,1,0:T(8,128)}), f32[20,32,128]{2,1,0:T(8,128)S(1)}, u32[]{:S(2)}, u32[]{:S(2)}) async-start(f32[20,32,128]{2,1,0:T(8,128)} %reduce_sum.200), calls=%async_computation.11 | async-start | bytes 655360 | tf_op jit(solution)/shard_map/all_to_all | solution.py:26
  223.6 12.9 %all-to-all-start.8 = ((f32[20,32,128]{2,1,0:T(8,128)}), f32[20,32,128]{2,1,0:T(8,128)S(1)}, u32[]{:S(2)}, u32[]{:S(2)}) async-start(f32[20,32,128]{2,1,0:T(8,128)} %pad_maximum_fusion.11), calls=%async_computation.8 | async-start | bytes 655360 | tf_op jit(solution)/shard_map/all_to_all | solution.py:26
  236.6 11.8 %all-to-all-start.12 = ((f32[20,32,128]{2,1,0:T(8,128)}), f32[20,32,128]{2,1,0:T(8,128)S(1)}, u32[]{:S(2)}, u32[]{:S(2)}) async-start(f32[20,32,128]{2,1,0:T(8,128)} %pad_maximum_fusion.12), calls=%async_computation.12 | async-start | bytes 655360 | tf_op jit(solution)/shard_map/all_to_all | solution.py:26
  249.1 14.3 %all-to-all-start.9 = ((f32[80,32,128]{2,1,0:T(8,128)}), f32[80,32,128]{2,1,0:T(8,128)S(1)}, u32[]{:S(2)}, u32[]{:S(2)}) async-start(f32[80,32,128]{2,1,0:T(8,128)} %pad_maximum_fusion.2), calls=%async_computation.9 | async-start | bytes 2621440 | tf_op jit(solution)/shard_map/all_to_all | solution.py:26
  263.4 13.9 %all-to-all-start.17 = ((f32[32,32,128]{2,1,0:T(8,128)}), f32[32,32,128]{2,1,0:T(8,128)S(1)}, u32[]{:S(2)}, u32[]{:S(2)}) async-start(f32[32,32,128]{2,1,0:T(8,128)} %pad_maximum_fusion.7), calls=%async_computation.17 | async-start | bytes 1048576 | tf_op jit(solution)/shard_map/all_to_all | solution.py:26
  328.5 18.9 %all-to-all-start.18 = ((f32[80,32,128]{2,1,0:T(8,128)}), f32[80,32,128]{2,1,0:T(8,128)S(1)}, u32[]{:S(2)}, u32[]{:S(2)}) async-start(f32[80,32,128]{2,1,0:T(8,128)} %get-tuple-element.28), calls=%async_computation.18 | async-start | bytes 2621440 | tf_op jit(solution)/shard_map/all_to_all | solution.py:26
  332.1 23.6 %copy-start.10 = (f32[80,32,128]{2,1,0:T(8,128)S(1)}, f32[80,32,128]{2,1,0:T(8,128)}, u32[]{:S(2)}) copy-start(f32[80,32,128]{2,1,0:T(8,128)} %get-tuple-element.30) | copy-start | bytes 3932164
  347.4 8.3 %all-to-all-start.28 = ((f32[8,32,128]{2,1,0:T(8,128)}), f32[8,32,128]{2,1,0:T(8,128)S(1)}, u32[]{:S(2)}, u32[]{:S(2)}) async-start(f32[8,32,128]{2,1,0:T(8,128)} %pad_maximum_fusion.18), calls=%async_computation.28 | async-start | bytes 262144 | tf_op jit(solution)/shard_map/all_to_all | solution.py:26
  369.5 14.3 %all-to-all-start.19 = ((f32[20,32,128]{2,1,0:T(8,128)}), f32[20,32,128]{2,1,0:T(8,128)S(1)}, u32[]{:S(2)}, u32[]{:S(2)}) async-start(f32[20,32,128]{2,1,0:T(8,128)} %reduce_sum.204), calls=%async_computation.19 | async-start | bytes 655360 | tf_op jit(solution)/shard_map/all_to_all | solution.py:26
  383.7 13.5 %all-to-all-start.23 = ((f32[20,32,128]{2,1,0:T(8,128)}), f32[20,32,128]{2,1,0:T(8,128)S(1)}, u32[]{:S(2)}, u32[]{:S(2)}) async-start(f32[20,32,128]{2,1,0:T(8,128)} %reduce_sum.206), calls=%async_computation.23 | async-start | bytes 655360 | tf_op jit(solution)/shard_map/all_to_all | solution.py:26
  397.2 10.7 %all-to-all-start.20 = ((f32[20,32,128]{2,1,0:T(8,128)}), f32[20,32,128]{2,1,0:T(8,128)S(1)}, u32[]{:S(2)}, u32[]{:S(2)}) async-start(f32[20,32,128]{2,1,0:T(8,128)} %pad_maximum_fusion.13), calls=%async_computation.20 | async-start | bytes 655360 | tf_op jit(solution)/shard_map/all_to_all | solution.py:26
  407.9 16.3 %all-to-all-start.24 = ((f32[20,32,128]{2,1,0:T(8,128)}), f32[20,32,128]{2,1,0:T(8,128)S(1)}, u32[]{:S(2)}, u32[]{:S(2)}) async-start(f32[20,32,128]{2,1,0:T(8,128)} %pad_maximum_fusion.14), calls=%async_computation.24 | async-start | bytes 655360 | tf_op jit(solution)/shard_map/all_to_all | solution.py:26
  425.0 20.0 %all-to-all-start.21 = ((f32[80,32,128]{2,1,0:T(8,128)}), f32[80,32,128]{2,1,0:T(8,128)S(1)}, u32[]{:S(2)}, u32[]{:S(2)}) async-start(f32[80,32,128]{2,1,0:T(8,128)} %pad_maximum_fusion.4), calls=%async_computation.21 | async-start | bytes 2621440 | tf_op jit(solution)/shard_map/all_to_all | solution.py:26
  445.0 13.7 %all-to-all-start.29 = ((f32[32,32,128]{2,1,0:T(8,128)}), f32[32,32,128]{2,1,0:T(8,128)S(1)}, u32[]{:S(2)}, u32[]{:S(2)}) async-start(f32[32,32,128]{2,1,0:T(8,128)} %pad_maximum_fusion.8), calls=%async_computation.29 | async-start | bytes 1048576 | tf_op jit(solution)/shard_map/all_to_all | solution.py:26
  502.4 14.3 %all-to-all-start.30 = ((f32[80,32,128]{2,1,0:T(8,128)}), f32[80,32,128]{2,1,0:T(8,128)S(1)}, u32[]{:S(2)}, u32[]{:S(2)}) async-start(f32[80,32,128]{2,1,0:T(8,128)} %get-tuple-element.34), calls=%async_computation.30 | async-start | bytes 2621440 | tf_op jit(solution)/shard_map/all_to_all | solution.py:26
  516.8 8.3 %all-to-all-start.35 = ((f32[8,32,128]{2,1,0:T(8,128)}), f32[8,32,128]{2,1,0:T(8,128)S(1)}, u32[]{:S(2)}, u32[]{:S(2)}) async-start(f32[8,32,128]{2,1,0:T(8,128)} %reduce_sum.214), calls=%async_computation.35 | async-start | bytes 262144 | tf_op jit(solution)/shard_map/all_to_all | solution.py:26
  538.9 10.7 %all-to-all-start.31 = ((f32[20,32,128]{2,1,0:T(8,128)}), f32[20,32,128]{2,1,0:T(8,128)S(1)}, u32[]{:S(2)}, u32[]{:S(2)}) async-start(f32[20,32,128]{2,1,0:T(8,128)} %reduce_sum.210), calls=%async_computation.31 | async-start | bytes 655360 | tf_op jit(solution)/shard_map/all_to_all | solution.py:26
  549.6 10.9 %all-to-all-start.33 = ((f32[20,32,128]{2,1,0:T(8,128)}), f32[20,32,128]{2,1,0:T(8,128)S(1)}, u32[]{:S(2)}, u32[]{:S(2)}) async-start(f32[20,32,128]{2,1,0:T(8,128)} %reduce_sum.212), calls=%async_computation.33 | async-start | bytes 655360 | tf_op jit(solution)/shard_map/all_to_all | solution.py:26
  562.1 10.1 %all-to-all-start.36 = ((f32[32,1,128]{2,1,0:T(1,128)}), f32[32,1,128]{2,1,0:T(1,128)S(1)}, u32[]{:S(2)}, u32[]{:S(2)}) async-start(f32[32,1,128]{2,1,0:T(1,128)} %concatenate.115), calls=%async_computation.36 | async-start | bytes 32768 | tf_op jit(solution)/shard_map/all_to_all | solution.py:26
  565.1 9.0 %collective-permute-start.3 = (f32[6,32,128]{2,1,0:T(8,128)S(1)}, f32[6,32,128]{2,1,0:T(8,128)S(1)}, u32[]{:S(2)}, u32[]{:S(2)}) collective-permute-start(f32[6,32,128]{2,1,0:T(8,128)S(1)} %fusion.2), channel_id=1, source_target_pairs={{0,1},{1,0},{2,3},{3,2},{4,5},{5,4},{6,7},{7,6},{8,9},{9,8},{10,11... | collective-permute-start | bytes 294920 | tf_op jit(solution)/shard_map/ppermute | solution.py:232
  (17 other events, 187.8 us)

commit v5 on v4

--- a/solution.py
+++ b/solution.py
@@ -13,30 +13,81 @@
 STEP = 16
 UNROLL = 8
 VMEM = 60 * 1024 * 1024
-PLANE = ("y", "x")
 CHIPS = ("z", "y", "x")
 ALL = ("z", "y", "x", "core")
+NEAR = ("x", "y", "z")
+GROUPS = 2
 
 
 def depth_of(n_rows):
     return min(n for n in range(1, n_rows + 1) if n_rows % n == 0 and n * n >= n_rows)
 
 
-def exchange(blocks, axes):
-    return lax.all_to_all(blocks, axes, split_axis=0, concat_axis=0, tiled=True)
-
-
-def spread(block, axes):
-    return exchange(jnp.concatenate([block] * lax.axis_size(axes), axis=0), axes)
-
-
-def fold(blocks, axes):
-    got = exchange(blocks, axes)
-    return jnp.sum(got.reshape((lax.axis_size(axes), -1) + got.shape[1:]), axis=0)
+def far_steps():
+    return [(a, 1 << k) for a in NEAR for k in range(1, lax.axis_size(a).bit_length() - 1)]
+
+
+def near_steps(part):
+    turn = part % len(NEAR)
+    return [(a, 1) for a in NEAR[turn:] + NEAR[:turn]]
+
+
+def swap(array, step):
+    axis, distance = step
+    pairs = [(i, i ^ distance) for i in range(lax.axis_size(axis))]
+    return lax.ppermute(array, axis, pairs)
 
 
 def after(value, *others):
     return lax.optimization_barrier((value,) + others)[0]
+
+
+def halves(array):
+    middle = array.shape[0] // 2
+    return array[:middle], array[middle:]
+
+
+def gather(flux, bounds, part, held=None):
+    blocks = [flux]
+    for step in reversed(far_steps()):
+        send = blocks[0] if len(blocks) == 1 else jnp.concatenate(blocks, axis=0)
+        got = swap(send if held is None else after(send, held), step)
+        held = got if held is None else held
+        blocks = blocks + jnp.split(got, len(blocks))
+    pieces = []
+    for k, (low, high) in enumerate(bounds):
+        block = jnp.concatenate([b[low:high] for b in blocks], axis=0)
+        steps = near_steps(part + k)
+        for step in reversed(steps[1:]):
+            block = jnp.concatenate([block, swap(block, step)], axis=0)
+        pieces.append((block, swap(block, steps[0])))
+    return pieces, got
+
+
+def reduce(pieces, part, held=None):
+    ends, firsts = [], []
+    for k, (keep, send) in enumerate(pieces):
+        if held is not None:
+            send = after(send, held[k])
+        steps = near_steps(part + k)
+        got = swap(send, steps[0])
+        firsts.append(got)
+        for step in steps[1:]:
+            keep, send = [k + g for k, g in zip(halves(keep), halves(got))]
+            got = swap(send, step)
+        ends.append((keep, got))
+    far = far_steps()
+    blocks = [
+        [k + g for k, g in zip(jnp.split(keep, 1 << len(far)), jnp.split(got, 1 << len(far)))]
+        for keep, got in ends
+    ]
+    blocks = [jnp.concatenate(group, axis=0) for group in zip(*blocks)]
+    for step in far:
+        middle = len(blocks) // 2
+        send = blocks[middle:]
+        got = swap(jnp.concatenate(send, axis=0) if middle > 1 else send[0], step)
+        blocks = [b + g for b, g in zip(blocks[:middle], jnp.split(got, middle))]
+    return blocks[0], firsts
 
 
 def split_kernel(tile_ref, pair_ref):
@@ -151,8 +202,7 @@
     tile_values, tile_owner, tile_row, tile_col, tile_count, relaxation, driving, heat_weight
 ):
     n_cols = lax.axis_size("x") * CORES
-    planes, plane = lax.axis_size("z"), lax.axis_size(PLANE)
-    chips = planes * plane
+    chips = lax.axis_size(CHIPS)
     length, size, _ = tile_values.shape
     modes, columns = driving.shape
     per = modes // size
@@ -160,29 +210,33 @@
     num = chips * chip_tiles
     half = columns // CORES
     core = lax.axis_index("core")
-    swap = [(0, 1), (1, 0)]
-
-    second = chip_tiles - max(1, chip_tiles // 6)
-    bounds = (0, second // 2, second, chip_tiles)
-    parts = list(zip(bounds[:-1], bounds[1:]))
+    cores = ("core", 1)
+
+    count = GROUPS * len(NEAR)
+    edges = [chip_tiles * k // count for k in range(count + 1)]
 
     def place(tile):
         chip, inside = tile // chip_tiles, tile % chip_tiles
-        z, at = chip // plane, chip % plane
+        away, width = {}, 1
+        for axis in reversed(CHIPS):
+            n = lax.axis_size(axis)
+            away[axis] = ((chip // width) % n) ^ lax.axis_index(axis)
+            width *= n
         out = jnp.zeros_like(tile)
-        for k, (low, high) in enumerate(parts):
-            slot = z * plane + at if k == 2 else at * planes + z
-            slot = chips * low + slot * (high - low) + inside - low
-            out = jnp.where((inside >= low) & (inside < high), slot, out)
+        for part in range(count):
+            slot = jnp.zeros_like(tile)
+            for axis, distance in near_steps(part) + far_steps():
+                slot = 2 * slot + (away[axis] // distance) % 2
+            slot = chips * edges[part] + slot * (edges[part + 1] - edges[part]) + inside - edges[part]
+            out = jnp.where(inside >= edges[part], slot, out)
         return out
 
-    other_values = lax.ppermute(tile_values, "core", swap)
     owners = tile_owner[:, 0]
     row = (owners // n_cols) * (n_cols * per) + tile_row
     col = ((tile_col // per) * n_cols + owners % n_cols) * per + tile_col % per
     used = jnp.arange(length, dtype=jnp.int32) < tile_count[0]
     places = jnp.where(used, place(row) * num + place(col), -1)
-    places = jnp.concatenate([places, lax.ppermute(places, "core", swap)])
+    places = jnp.concatenate([places, swap(places, cores)])
     is_used = places >= 0
     places = jnp.where(is_used, places, 0)
     row, col, used = places // num, places % num, is_used.astype(jnp.float32)
@@ -199,37 +253,44 @@
     mine = jnp.where(core == 0, low, high)
     theirs = jnp.where(core == 0, high, low)
     packed = [theirs, jnp.broadcast_to(relax, (per, 8, size)), jnp.broadcast_to(heat, (per, 8, size))]
-    got = lax.ppermute(jnp.concatenate(packed, axis=1), "core", swap)
+    got = swap(jnp.concatenate(packed, axis=1), cores)
+    other_values = swap(after(tile_values, got), cores)
     drive_half = by_core(mine, got[:, :half])
     relax_both = by_core(relax, got[:, half : half + 1])
     heat_both = by_core(heat, got[:, half + 8 : half + 9])
 
     own = split_tiles(tile_values)
     other = split_tiles(other_values)
-    drives = [drive_half[low:high] for low, high in parts]
-    relaxes = [relax_both[low:high] for low, high in parts]
-    fluxes = [r * d for r, d in zip(relaxes, drives)]
+    groups = []
+    for g in range(GROUPS):
+        part = g * len(NEAR)
+        low, high = edges[part], edges[part + len(NEAR)]
+        bounds = [(edges[part + k] - low, edges[part + k + 1] - low) for k in range(len(NEAR))]
+        groups.append((part, bounds, relax_both[low:high], drive_half[low:high]))
+    fluxes = [relax * drive for _, _, relax, drive in groups]
     for sweep in range(ITERS):
-        by_z = [spread(flux, "z") for flux in fluxes[:2]]
-        by_plane = spread(fluxes[2], PLANE)
-        first = spread(by_z[0], PLANE)
-        third = spread(after(by_plane, by_z[1]), "z")
-        second = spread(after(by_z[1], first), PLANE)
-        sums = apply_tiles(row, col, used, own, other, [first, second, third])
-        third = fold(sums[2], "z")
-        first = fold(sums[0], PLANE)
-        second = fold(after(sums[1], first), PLANE)
-        summed = [fold(first, "z"), fold(second, "z"), fold(third, PLANE)]
-        fluxes = [r * (d + s) for r, d, s in zip(relaxes, drives, summed)]
+        pieces, held = [], None
+        for (part, bounds, _, _), flux in zip(groups, fluxes):
+            gathered, held = gather(flux, bounds, part, held if sweep == 0 else None)
+            pieces.extend(gathered)
+        sums = apply_tiles(row, col, used, own, other, [p for pair in pieces for p in pair])
+        pairs = list(zip(sums[0::2], sums[1::2]))
+        fluxes, held = [], None
+        for part, _, relax, drive in groups:
+            summed, held = reduce(pairs[part : part + len(NEAR)], part, held)
+            fluxes.append(relax * (drive + summed))
     flux = jnp.concatenate(fluxes, axis=0)
     weighted = jnp.sum(heat_both * flux, axis=(0, 2))
     totals = jnp.concatenate([weighted, jnp.sum(heat).reshape(1)])
-    totals = spread(jnp.pad(totals[None], ((0, 0), (0, size - half - 1))), ALL)
+    totals = jnp.pad(totals[None], ((0, 0), (0, size - half - 1)))
+    totals = lax.all_to_all(
+        jnp.broadcast_to(totals, (chips * CORES, size)), ALL, split_axis=0, concat_axis=0, tiled=True
+    )
     totals = jnp.sum(totals.reshape(chips, CORES, size), axis=0)
     conductivity = totals[:, :half].reshape(columns) / jnp.sum(totals[:, half])
     first, second = flux[:per], flux[per:]
     mine = jnp.where(core == 0, first, second)
-    got = lax.ppermute(jnp.where(core == 0, second, first), "core", swap)
+    got = swap(jnp.where(core == 0, second, first), cores)
     both = jnp.concatenate(
         [jnp.where(core == 0, mine, got), jnp.where(core == 0, got, mine)], axis=1
     )

time: 578 us -> 381 us (0.66)
  blocking collectives: 137 us -> 0 us
  waiting for transfers between devices: 232 us -> 142 us
  starting transfers between devices: 102 us -> 134 us
    all_to_all x27 -> x1, waiting for transfers between devices: 222 us -> 6.76 us  [shards(): lax.all_to_all(jnp.broadcast_to(totals, (chips * CORES, size)), ALL, spli...]
    all_to_all x10 -> x0, blocking collectives: 137 us -> none  [exchange(): return lax.all_to_all(blocks, axes, split_axis=0, concat_axis=0, tiled=True)]
    ppermute x4 -> x124, starting transfers between devices: 1.42 us -> 131 us  [swap(): return lax.ppermute(array, axis, pairs)]
    ppermute x4 -> x124, waiting for transfers between devices: 9.26 us -> 135 us  [swap(): return lax.ppermute(array, axis, pairs)]
    all_to_all x27 -> x1, starting transfers between devices: 100 us -> 3.37 us  [shards(): lax.all_to_all(jnp.broadcast_to(totals, (chips * CORES, size)), ALL, spli...]
    add x0 -> x54, other arithmetic: none -> 18.7 us  [the longest x36 18.5 us: reduce(): keep, send = [k + g for k, g in zip(halves(keep), halves(got))]]
    concatenate x19 -> x61, other arithmetic: 17.2 us -> 0.67 us  [the longest x36 0.5 us: gather(): block = jnp.concatenate([block, swap(block, step)], axis=0)]
    reduce_sum x18 -> x0, other arithmetic: 6.09 us -> none  [fold(): jnp.sum(got.reshape((lax.axis_size(axes), -1) + got.shape[1:]), axis=0)]
  transfers between devices with their start and end apart: 31 -> 125, of which waited for: 27 -> 63; matrix products, arithmetic and copies ran while one was open for 5% -> 7% of each run, Pallas kernels for 4% -> 5%
where the time goes in v5:
time: 381 us; the launch traced here: 379 us
  waiting for transfers between devices  142 us (37%)
  starting transfers between devices  134 us (35%)
  Pallas kernels  67.7 us (18%)
  other arithmetic  25 us (7%)
  local copies, waits for them, and re-layouts  7.54 us (2%)
    ppermute x124, waiting for transfers between devices, swap(): return lax.ppermute(array, axis, pairs)  135 us
    ppermute x124, starting transfers between devices, swap(): return lax.ppermute(array, axis, pairs)  131 us
    pallas_call x3, Pallas kernels, apply_tiles(): pl.pallas_call(functools.partial(apply_kernel, length, counts), out_shape...  47.2 us
    pallas_call x2, Pallas kernels, split_tiles(): pl.pallas_call(split_kernel, out_shape=jax.ShapeDtypeStruct((length, 2 *...  20.5 us
    add x36, other arithmetic, reduce(): keep, send = [k + g for k, g in zip(halves(keep), halves(got))]  18.5 us
  transfers between devices with their start and end apart: 125, of which 63 were waited for; matrix products, arithmetic and copies ran while one was open for 7% of the time, Pallas kernels for 5%

profile of v5, /device:TPU:0, one launch (start us, length us, event | category | flops | bytes accessed | tf_op | source)
XLA Modules:
  0.0 378.9 jit_solution(4751423438195483460)
XLA Ops:
  8.0 4.0 %collective-permute-start.3 = (f32[6,32,128]{2,1,0:T(8,128)S(1)}, f32[6,32,128]{2,1,0:T(8,128)S(1)}, u32[]{:S(2)}, u32[]{:S(2)}) collective-permute-start(f32[6,32,128]{2,1,0:T(8,128)S(1)} %get-tuple-element.139), channel_id=1, source_target_pairs={{0,16},{8,24},{16,0},{24,8},{1,17},{9,25},{17,1},{25,9},{2,18},{10... | collective-permute-start | bytes 294920 | tf_op jit(solution)/shard_map/ppermute | solution.py:38
  12.0 5.2 %collective-permute-done.3 = f32[6,32,128]{2,1,0:T(8,128)S(1)} collective-permute-done((f32[6,32,128]{2,1,0:T(8,128)S(1)}, f32[6,32,128]{2,1,0:T(8,128)S(1)}, u32[]{:S(2)}, u32[]{:S(2)}) %collective-permute-start.3) | collective-permute-done | bytes 98336 | tf_op jit(solution)/shard_map/ppermute | solution.py:38
  19.5 3.5 collective-permute-start.4
  28.7 3.5 collective-permute-start.14
  35.4 3.4 collective-permute-done.17
  39.2 4.0 %collective-permute-done.20 = f32[4,32,128]{2,1,0:T(8,128)S(1)} collective-permute-done((f32[4,32,128]{2,1,0:T(8,128)S(1)}, f32[4,32,128]{2,1,0:T(8,128)S(1)}, u32[]{:S(2)}, u32[]{:S(2)}) %collective-permute-start.20) | collective-permute-done | bytes 65568 | tf_op jit(solution)/shard_map/ppermute | solution.py:38
  46.3 3.4 collective-permute-done.8
  60.2 10.3 %shard_map.95.own_ref = bf16[128,256,128]{2,1,0:T(8,128)(2,1)} custom-call(f32[128,128,128]{2,1,0:T(8,128)} %tile_ref.1), custom_call_target="tpu_custom_call" | custom-call | flops 6291456 | bytes 16777216 | tf_op jit(solution)/shard_map/pallas_call | solution.py:108
  71.7 10.3 %shard_map.96.other_ref = bf16[128,256,128]{2,1,0:T(8,128)(2,1)} custom-call(f32[128,128,128]{2,1,0:T(8,128)} %collective-permute-done.2.tile_ref), custom_call_target="tpu_custom_call" | custom-call | flops 6291456 | bytes 16777216 | tf_op jit(solution)/shard_map/pallas_call | solution.py:108
  83.1 15.6 %shard_map.97 = (f32[16,32,128]{2,1,0:T(8,128)}, f32[16,32,128]{2,1,0:T(8,128)}, f32[16,32,128]{2,1,0:T(8,128)}, f32[16,32,128]{2,1,0:T(8,128)}, f32[16,32,128]{...) custom-call(s32[256]{0:T(256)} %get-tuple-element.258.row_ref, ...), custom_call_target="tpu_custom_call" | custom-call | flops 1073741824 | bytes 23068672 | tf_op jit(solution)/shard_map/pallas_call | solution.py:178
  116.8 2.8 collective-permute-done.27
  119.8 2.9 collective-permute-done.30
  133.9 2.8 collective-permute-start.50
  137.5 7.6 %collective-permute-done.33 = f32[6,32,128]{2,1,0:T(8,128)S(1)} collective-permute-done((f32[6,32,128]{2,1,0:T(8,128)S(1)}, f32[6,32,128]{2,1,0:T(8,128)S(1)}, u32[]{:S(2)}, u32[]{:S(2)}) %collective-permute-start.33) | collective-permute-done | bytes 98336 | tf_op jit(solution)/shard_map/ppermute | solution.py:38
  156.7 4.0 %collective-permute-done.52 = f32[6,32,128]{2,1,0:T(8,128)S(1)} collective-permute-done((f32[6,32,128]{2,1,0:T(8,128)S(1)}, f32[6,32,128]{2,1,0:T(8,128)S(1)}, u32[]{:S(2)}, u32[]{:S(2)}) %collective-permute-start.52) | collective-permute-done | bytes 98336 | tf_op jit(solution)/shard_map/ppermute | solution.py:38
  184.4 4.8 %collective-permute-done.62.refs_11_ = f32[16,32,128]{2,1,0:T(8,128)S(1)} collective-permute-done((f32[16,32,128]{2,1,0:T(8,128)S(1)}, f32[16,32,128]{2,1,0:T(8,128)S(1)}, u32[]{:S(2)}, u32[]{:S(2)}) %collective-permute-start.62) | collective-permute-done | bytes 262176 | tf_op jit(solution)/shard_map/ppermute | solution.py:38
  191.3 15.7 %shard_map.98 = (f32[16,32,128]{2,1,0:T(8,128)}, f32[16,32,128]{2,1,0:T(8,128)}, f32[16,32,128]{2,1,0:T(8,128)}, f32[16,32,128]{2,1,0:T(8,128)}, f32[16,32,128]{...) custom-call(s32[256]{0:T(256)} %get-tuple-element.258.row_ref, ...), custom_call_target="tpu_custom_call" | custom-call | flops 1073741824 | bytes 23068672 | tf_op jit(solution)/shard_map/pallas_call | solution.py:178
  210.4 4.7 %collective-permute-done.63 = f32[16,32,128]{2,1,0:T(8,128)S(1)} collective-permute-done((f32[16,32,128]{2,1,0:T(8,128)}, f32[16,32,128]{2,1,0:T(8,128)S(1)}, u32[]{:S(2)}, u32[]{:S(2)}) %collective-permute-start.63) | collective-permute-done | bytes 262176 | tf_op jit(solution)/shard_map/ppermute | solution.py:38
  225.8 2.5 collective-permute-done.67
  230.8 2.9 collective-permute-done.65
  235.2 2.7 collective-permute-done.71
  245.9 5.7 %collective-permute-done.73 = f32[6,32,128]{2,1,0:T(8,128)S(1)} collective-permute-done((f32[6,32,128]{2,1,0:T(8,128)S(1)}, f32[6,32,128]{2,1,0:T(8,128)S(1)}, u32[]{:S(2)}, u32[]{:S(2)}) %collective-permute-start.73) | collective-permute-done | bytes 98336 | tf_op jit(solution)/shard_map/ppermute | solution.py:38
  263.9 3.0 collective-permute-done.92
  273.2 2.7 collective-permute-start.100
  275.9 4.1 %collective-permute-done.100 = f32[4,32,128]{2,1,0:T(8,128)S(1)} collective-permute-done((f32[4,32,128]{2,1,0:T(8,128)S(1)}, f32[4,32,128]{2,1,0:T(8,128)S(1)}, u32[]{:S(2)}, u32[]{:S(2)}) %collective-permute-start.100) | collective-permute-done | bytes 65568 | tf_op jit(solution)/shard_map/ppermute | solution.py:38
  281.7 3.4 collective-permute-done.94
  286.8 3.6 collective-permute-done.98
  293.1 3.7 collective-permute-done.102.refs_11_
  299.1 15.8 %shard_map.99 = (f32[16,32,128]{2,1,0:T(8,128)}, f32[16,32,128]{2,1,0:T(8,128)}, f32[16,32,128]{2,1,0:T(8,128)}, f32[16,32,128]{2,1,0:T(8,128)}, f32[16,32,128]{...) custom-call(s32[256]{0:T(256)} %get-tuple-element.258.row_ref, ...), custom_call_target="tpu_custom_call" | custom-call | flops 1073741824 | bytes 23068672 | tf_op jit(solution)/shard_map/pallas_call | solution.py:178
  359.4 4.8 %collective-permute-done.122 = f32[6,32,128]{2,1,0:T(8,128)S(1)} collective-permute-done((f32[6,32,128]{2,1,0:T(8,128)S(1)}, f32[6,32,128]{2,1,0:T(8,128)S(1)}, u32[]{:S(2)}, u32[]{:S(2)}) %collective-permute-start.122) | collective-permute-done | bytes 98336 | tf_op jit(solution)/shard_map/ppermute | solution.py:38
  365.7 3.4 all-to-all-start
  369.4 6.8 %all-to-all-done = f32[32,1,128]{2,1,0:T(1,128)S(1)} async-done(((f32[32,1,128]{2,1,0:T(1,128)}), f32[32,1,128]{2,1,0:T(1,128)S(1)}, u32[]{:S(2)}, u32[]{:S(2)}) %all-to-all-start) | async-done | bytes 16416 | tf_op jit(solution)/shard_map/all_to_all | solution.py:286
  (458 shorter events, 203.0 us)
Async XLA Ops:
  4.5 55.4 %collective-permute-start.2 = (f32[128,128,128]{2,1,0:T(8,128)}, f32[128,128,128]{2,1,0:T(8,128)}, u32[]{:S(2)}, u32[]{:S(2)}) collective-permute-start(f32[128,128,128]{2,1,0:T(8,128)} %tile_ref.1), channel_id=1, source_target_pairs={{0,1},{1,0},{2,3},{3,2},{4,5},{5,4},{6,7},{7,6},{8,9},{9,8},{10,11... | collective-permute-start | bytes 25165832 | tf_op jit(solution)/shard_map/ppermute | solution.py:38
  6.3 49.1 %collective-permute-start.1 = (s32[128]{0:T(128)S(1)}, s32[128]{0:T(128)S(1)}, u32[]{:S(2)}, u32[]{:S(2)}) collective-permute-start(s32[128]{0:T(128)S(1)} %compare_select_fusion.33), channel_id=1, source_target_pairs={{0,1},{1,0},{2,3},{3,2},{4,5},{5,4},{6,7},{7,6},{8,9},{9,8},{10,11... | collective-permute-start | bytes 1544 | tf_op jit(solution)/shard_map/ppermute | solution.py:38
  25.6 19.4 %collective-permute-start.11 = (f32[8,32,128]{2,1,0:T(8,128)S(1)}, f32[8,32,128]{2,1,0:T(8,128)S(1)}, u32[]{:S(2)}, u32[]{:S(2)}) collective-permute-start(f32[8,32,128]{2,1,0:T(8,128)S(1)} %pad_maximum_fusion.21), channel_id=1, source_target_pairs={{0,2},{2,0},{1,3},{3,1},{4,6},{6,4},{5,7},{7,5},{8,10},{10,8},{9,1... | collective-permute-start | bytes 393224 | tf_op jit(solution)/shard_map/ppermute | solution.py:38
  27.3 18.4 %collective-permute-start.5 = (f32[8,32,128]{2,1,0:T(8,128)S(1)}, f32[8,32,128]{2,1,0:T(8,128)S(1)}, u32[]{:S(2)}, u32[]{:S(2)}) collective-permute-start(f32[8,32,128]{2,1,0:T(8,128)S(1)} %pad_maximum_fusion.19), channel_id=1, source_target_pairs={{0,4},{4,0},{1,5},{5,1},{2,6},{6,2},{3,7},{7,3},{8,12},{12,8},{9,1... | collective-permute-start | bytes 393224 | tf_op jit(solution)/shard_map/ppermute | solution.py:38
  51.9 30.1 %collective-permute-start.6 = (f32[16,32,128]{2,1,0:T(8,128)S(1)}, f32[16,32,128]{2,1,0:T(8,128)S(1)}, u32[]{:S(2)}, u32[]{:S(2)}) collective-permute-start(f32[16,32,128]{2,1,0:T(8,128)S(1)} %pad_maximum_fusion.refs_0_), channel_id=1, source_target_pairs={{0,2},{2,0},{1,3},{3,1},{4,6},{6,4},{5,7},{7,5},{8,10},{10,8},{9,1... | collective-permute-start | bytes 786440 | tf_op jit(solution)/shard_map/ppermute | solution.py:38
  54.7 27.4 %collective-permute-start.9 = (f32[16,32,128]{2,1,0:T(8,128)S(1)}, f32[16,32,128]{2,1,0:T(8,128)S(1)}, u32[]{:S(2)}, u32[]{:S(2)}) collective-permute-start(f32[16,32,128]{2,1,0:T(8,128)S(1)} %pad_maximum_fusion.1.refs_2_), channel_id=1, source_target_pairs={{0,4},{4,0},{1,5},{5,1},{2,6},{6,2},{3,7},{7,3},{8,12},{12,8},{9,1... | collective-permute-start | bytes 786440 | tf_op jit(solution)/shard_map/ppermute | solution.py:38
  55.4 26.6 %collective-permute-start.16 = (f32[16,32,128]{2,1,0:T(8,128)S(1)}, f32[16,32,128]{2,1,0:T(8,128)S(1)}, u32[]{:S(2)}, u32[]{:S(2)}) collective-permute-start(f32[16,32,128]{2,1,0:T(8,128)S(1)} %pad_maximum_fusion.3.refs_6_), channel_id=1, source_target_pairs={{0,2},{2,0},{1,3},{3,1},{4,6},{6,4},{5,7},{7,5},{8,10},{10,8},{9,1... | collective-permute-start | bytes 786440 | tf_op jit(solution)/shard_map/ppermute | solution.py:38
  58.8 23.2 %collective-permute-start.19 = (f32[16,32,128]{2,1,0:T(8,128)S(1)}, f32[16,32,128]{2,1,0:T(8,128)S(1)}, u32[]{:S(2)}, u32[]{:S(2)}) collective-permute-start(f32[16,32,128]{2,1,0:T(8,128)S(1)} %pad_maximum_fusion.4.refs_8_), channel_id=1, source_target_pairs={{0,4},{4,0},{1,5},{5,1},{2,6},{6,2},{3,7},{7,3},{8,12},{12,8},{9,1... | collective-permute-start | bytes 786440 | tf_op jit(solution)/shard_map/ppermute | solution.py:38
  60.0 22.1 %collective-permute-start.22 = (f32[16,32,128]{2,1,0:T(8,128)S(1)}, f32[16,32,128]{2,1,0:T(8,128)S(1)}, u32[]{:S(2)}, u32[]{:S(2)}) collective-permute-start(f32[16,32,128]{2,1,0:T(8,128)S(1)} %pad_maximum_fusion.5.refs_10_), channel_id=1, source_target_pairs={{0,8},{8,0},{16,24},{24,16},{1,9},{9,1},{17,25},{25,17},{2,10},{10... | collective-permute-start | bytes 786440 | tf_op jit(solution)/shard_map/ppermute | solution.py:38
  105.7 23.6 %collective-permute-start.43 = (f32[16,32,128]{2,1,0:T(8,128)}, f32[16,32,128]{2,1,0:T(8,128)S(1)}, u32[]{:S(2)}, u32[]{:S(2)}) collective-permute-start(f32[16,32,128]{2,1,0:T(8,128)} %get-tuple-element.59), channel_id=1, source_target_pairs={{0,2},{2,0},{1,3},{3,1},{4,6},{6,4},{5,7},{7,5},{8,10},{10,8},{9,1... | collective-permute-start | bytes 786440 | tf_op jit(solution)/shard_map/ppermute | solution.py:38
  108.1 23.1 %collective-permute-start.46 = (f32[16,32,128]{2,1,0:T(8,128)}, f32[16,32,128]{2,1,0:T(8,128)S(1)}, u32[]{:S(2)}, u32[]{:S(2)}) collective-permute-start(f32[16,32,128]{2,1,0:T(8,128)} %get-tuple-element.62), channel_id=1, source_target_pairs={{0,4},{4,0},{1,5},{5,1},{2,6},{6,2},{3,7},{7,3},{8,12},{12,8},{9,1... | collective-permute-start | bytes 786440 | tf_op jit(solution)/shard_map/ppermute | solution.py:38
  108.8 24.1 %collective-permute-start.49 = (f32[16,32,128]{2,1,0:T(8,128)}, f32[16,32,128]{2,1,0:T(8,128)S(1)}, u32[]{:S(2)}, u32[]{:S(2)}) collective-permute-start(f32[16,32,128]{2,1,0:T(8,128)} %get-tuple-element.65), channel_id=1, source_target_pairs={{0,8},{8,0},{16,24},{24,16},{1,9},{9,1},{17,25},{25,17},{2,10},{10... | collective-permute-start | bytes 786440 | tf_op jit(solution)/shard_map/ppermute | solution.py:38
  130.4 15.2 %collective-permute-start.44 = (f32[8,32,128]{2,1,0:T(8,128)S(1)}, f32[8,32,128]{2,1,0:T(8,128)S(1)}, u32[]{:S(2)}, u32[]{:S(2)}) collective-permute-start(f32[8,32,128]{2,1,0:T(8,128)S(1)} %get-tuple-element.128), channel_id=1, source_target_pairs={{0,4},{4,0},{1,5},{5,1},{2,6},{6,2},{3,7},{7,3},{8,12},{12,8},{9,1... | collective-permute-start | bytes 393224 | tf_op jit(solution)/shard_map/ppermute | solution.py:38
  132.2 13.9 %collective-permute-start.47 = (f32[8,32,128]{2,1,0:T(8,128)S(1)}, f32[8,32,128]{2,1,0:T(8,128)S(1)}, u32[]{:S(2)}, u32[]{:S(2)}) collective-permute-start(f32[8,32,128]{2,1,0:T(8,128)S(1)} %get-tuple-element.130), channel_id=1, source_target_pairs={{0,8},{8,0},{16,24},{24,16},{1,9},{9,1},{17,25},{25,17},{2,10},{10... | collective-permute-start | bytes 393224 | tf_op jit(solution)/shard_map/ppermute | solution.py:38
  133.9 13.9 %collective-permute-start.50 = (f32[8,32,128]{2,1,0:T(8,128)S(1)}, f32[8,32,128]{2,1,0:T(8,128)S(1)}, u32[]{:S(2)}, u32[]{:S(2)}) collective-permute-start(f32[8,32,128]{2,1,0:T(8,128)S(1)} %get-tuple-element.132), channel_id=1, source_target_pairs={{0,2},{2,0},{1,3},{3,1},{4,6},{6,4},{5,7},{7,5},{8,10},{10,8},{9,1... | collective-permute-start | bytes 393224 | tf_op jit(solution)/shard_map/ppermute | solution.py:38
  152.0 11.9 %collective-permute-start.38 = (f32[8,32,128]{2,1,0:T(8,128)S(1)}, f32[8,32,128]{2,1,0:T(8,128)S(1)}, u32[]{:S(2)}, u32[]{:S(2)}) collective-permute-start(f32[8,32,128]{2,1,0:T(8,128)S(1)} %pad_maximum_fusion.26), channel_id=1, source_target_pairs={{0,8},{8,0},{16,24},{24,16},{1,9},{9,1},{17,25},{25,17},{2,10},{10... | collective-permute-start | bytes 393224 | tf_op jit(solution)/shard_map/ppermute | solution.py:38
  162.1 21.3 %collective-permute-start.42 = (f32[16,32,128]{2,1,0:T(8,128)S(1)}, f32[16,32,128]{2,1,0:T(8,128)S(1)}, u32[]{:S(2)}, u32[]{:S(2)}) collective-permute-start(f32[16,32,128]{2,1,0:T(8,128)S(1)} %pad_maximum_fusion.8.refs_4_), channel_id=1, source_target_pairs={{0,8},{8,0},{16,24},{24,16},{1,9},{9,1},{17,25},{25,17},{2,10},{10... | collective-permute-start | bytes 786440 | tf_op jit(solution)/shard_map/ppermute | solution.py:38
  164.0 20.4 %collective-permute-start.39 = (f32[16,32,128]{2,1,0:T(8,128)S(1)}, f32[16,32,128]{2,1,0:T(8,128)S(1)}, u32[]{:S(2)}, u32[]{:S(2)}) collective-permute-start(f32[16,32,128]{2,1,0:T(8,128)S(1)} %pad_maximum_fusion.7.refs_2_), channel_id=1, source_target_pairs={{0,4},{4,0},{1,5},{5,1},{2,6},{6,2},{3,7},{7,3},{8,12},{12,8},{9,1... | collective-permute-start | bytes 786440 | tf_op jit(solution)/shard_map/ppermute | solution.py:38
  165.3 19.1 %collective-permute-start.36 = (f32[16,32,128]{2,1,0:T(8,128)S(1)}, f32[16,32,128]{2,1,0:T(8,128)S(1)}, u32[]{:S(2)}, u32[]{:S(2)}) collective-permute-start(f32[16,32,128]{2,1,0:T(8,128)S(1)} %pad_maximum_fusion.6.refs_0_), channel_id=1, source_target_pairs={{0,2},{2,0},{1,3},{3,1},{4,6},{6,4},{5,7},{7,5},{8,10},{10,8},{9,1... | collective-permute-start | bytes 786440 | tf_op jit(solution)/shard_map/ppermute | solution.py:38
  215.1 25.0 %collective-permute-start.83 = (f32[16,32,128]{2,1,0:T(8,128)}, f32[16,32,128]{2,1,0:T(8,128)S(1)}, u32[]{:S(2)}, u32[]{:S(2)}) collective-permute-start(f32[16,32,128]{2,1,0:T(8,128)} %get-tuple-element.74), channel_id=1, source_target_pairs={{0,2},{2,0},{1,3},{3,1},{4,6},{6,4},{5,7},{7,5},{8,10},{10,8},{9,1... | collective-permute-start | bytes 786440 | tf_op jit(solution)/shard_map/ppermute | solution.py:38
  216.6 25.2 %collective-permute-start.86 = (f32[16,32,128]{2,1,0:T(8,128)}, f32[16,32,128]{2,1,0:T(8,128)S(1)}, u32[]{:S(2)}, u32[]{:S(2)}) collective-permute-start(f32[16,32,128]{2,1,0:T(8,128)} %get-tuple-element.77), channel_id=1, source_target_pairs={{0,4},{4,0},{1,5},{5,1},{2,6},{6,2},{3,7},{7,3},{8,12},{12,8},{9,1... | collective-permute-start | bytes 786440 | tf_op jit(solution)/shard_map/ppermute | solution.py:38
  217.9 25.6 %collective-permute-start.89 = (f32[16,32,128]{2,1,0:T(8,128)}, f32[16,32,128]{2,1,0:T(8,128)S(1)}, u32[]{:S(2)}, u32[]{:S(2)}) collective-permute-start(f32[16,32,128]{2,1,0:T(8,128)} %get-tuple-element.80), channel_id=1, source_target_pairs={{0,8},{8,0},{16,24},{24,16},{1,9},{9,1},{17,25},{25,17},{2,10},{10... | collective-permute-start | bytes 786440 | tf_op jit(solution)/shard_map/ppermute | solution.py:38
  241.1 12.7 %collective-permute-start.84 = (f32[8,32,128]{2,1,0:T(8,128)S(1)}, f32[8,32,128]{2,1,0:T(8,128)S(1)}, u32[]{:S(2)}, u32[]{:S(2)}) collective-permute-start(f32[8,32,128]{2,1,0:T(8,128)S(1)} %get-tuple-element.116), channel_id=1, source_target_pairs={{0,4},{4,0},{1,5},{5,1},{2,6},{6,2},{3,7},{7,3},{8,12},{12,8},{9,1... | collective-permute-start | bytes 393224 | tf_op jit(solution)/shard_map/ppermute | solution.py:38
  242.8 13.4 %collective-permute-start.87 = (f32[8,32,128]{2,1,0:T(8,128)S(1)}, f32[8,32,128]{2,1,0:T(8,128)S(1)}, u32[]{:S(2)}, u32[]{:S(2)}) collective-permute-start(f32[8,32,128]{2,1,0:T(8,128)S(1)} %get-tuple-element.118), channel_id=1, source_target_pairs={{0,8},{8,0},{16,24},{24,16},{1,9},{9,1},{17,25},{25,17},{2,10},{10... | collective-permute-start | bytes 393224 | tf_op jit(solution)/shard_map/ppermute | solution.py:38
  244.5 11.8 %collective-permute-start.90 = (f32[8,32,128]{2,1,0:T(8,128)S(1)}, f32[8,32,128]{2,1,0:T(8,128)S(1)}, u32[]{:S(2)}, u32[]{:S(2)}) collective-permute-start(f32[8,32,128]{2,1,0:T(8,128)S(1)} %get-tuple-element.120), channel_id=1, source_target_pairs={{0,2},{2,0},{1,3},{3,1},{4,6},{6,4},{5,7},{7,5},{8,10},{10,8},{9,1... | collective-permute-start | bytes 393224 | tf_op jit(solution)/shard_map/ppermute | solution.py:38
  268.3 23.5 %collective-permute-start.82 = (f32[16,32,128]{2,1,0:T(8,128)S(1)}, f32[16,32,128]{2,1,0:T(8,128)S(1)}, u32[]{:S(2)}, u32[]{:S(2)}) collective-permute-start(f32[16,32,128]{2,1,0:T(8,128)S(1)} %pad_maximum_fusion.14.refs_4_), channel_id=1, source_target_pairs={{0,8},{8,0},{16,24},{24,16},{1,9},{9,1},{17,25},{25,17},{2,10},{10... | collective-permute-start | bytes 786440 | tf_op jit(solution)/shard_map/ppermute | solution.py:38
  270.8 22.2 %collective-permute-start.79 = (f32[16,32,128]{2,1,0:T(8,128)S(1)}, f32[16,32,128]{2,1,0:T(8,128)S(1)}, u32[]{:S(2)}, u32[]{:S(2)}) collective-permute-start(f32[16,32,128]{2,1,0:T(8,128)S(1)} %pad_maximum_fusion.13.refs_2_), channel_id=1, source_target_pairs={{0,4},{4,0},{1,5},{5,1},{2,6},{6,2},{3,7},{7,3},{8,12},{12,8},{9,1... | collective-permute-start | bytes 786440 | tf_op jit(solution)/shard_map/ppermute | solution.py:38
  271.7 21.3 %collective-permute-start.76 = (f32[16,32,128]{2,1,0:T(8,128)S(1)}, f32[16,32,128]{2,1,0:T(8,128)S(1)}, u32[]{:S(2)}, u32[]{:S(2)}) collective-permute-start(f32[16,32,128]{2,1,0:T(8,128)S(1)} %pad_maximum_fusion.12.refs_0_), channel_id=1, source_target_pairs={{0,2},{2,0},{1,3},{3,1},{4,6},{6,4},{5,7},{7,5},{8,10},{10,8},{9,1... | collective-permute-start | bytes 786440 | tf_op jit(solution)/shard_map/ppermute | solution.py:38
  321.6 21.4 %collective-permute-start.113 = (f32[16,32,128]{2,1,0:T(8,128)}, f32[16,32,128]{2,1,0:T(8,128)S(1)}, u32[]{:S(2)}, u32[]{:S(2)}) collective-permute-start(f32[16,32,128]{2,1,0:T(8,128)} %get-tuple-element.89), channel_id=1, source_target_pairs={{0,2},{2,0},{1,3},{3,1},{4,6},{6,4},{5,7},{7,5},{8,10},{10,8},{9,1... | collective-permute-start | bytes 786440 | tf_op jit(solution)/shard_map/ppermute | solution.py:38
  322.7 22.5 %collective-permute-start.116 = (f32[16,32,128]{2,1,0:T(8,128)}, f32[16,32,128]{2,1,0:T(8,128)S(1)}, u32[]{:S(2)}, u32[]{:S(2)}) collective-permute-start(f32[16,32,128]{2,1,0:T(8,128)} %get-tuple-element.92), channel_id=1, source_target_pairs={{0,4},{4,0},{1,5},{5,1},{2,6},{6,2},{3,7},{7,3},{8,12},{12,8},{9,1... | collective-permute-start | bytes 786440 | tf_op jit(solution)/shard_map/ppermute | solution.py:38
  323.4 23.7 %collective-permute-start.119 = (f32[16,32,128]{2,1,0:T(8,128)}, f32[16,32,128]{2,1,0:T(8,128)S(1)}, u32[]{:S(2)}, u32[]{:S(2)}) collective-permute-start(f32[16,32,128]{2,1,0:T(8,128)} %get-tuple-element.95), channel_id=1, source_target_pairs={{0,8},{8,0},{16,24},{24,16},{1,9},{9,1},{17,25},{25,17},{2,10},{10... | collective-permute-start | bytes 786440 | tf_op jit(solution)/shard_map/ppermute | solution.py:38
  342.4 17.0 %collective-permute-start.112 = (f32[6,32,128]{2,1,0:T(8,128)S(1)}, f32[6,32,128]{2,1,0:T(8,128)S(1)}, u32[]{:S(2)}, u32[]{:S(2)}) collective-permute-start(f32[6,32,128]{2,1,0:T(8,128)S(1)} %pad_maximum_fusion.41), channel_id=1, source_target_pairs={{0,16},{8,24},{16,0},{24,8},{1,17},{9,25},{17,1},{25,9},{2,18},{10... | collective-permute-start | bytes 294920 | tf_op jit(solution)/shard_map/ppermute | solution.py:38
  (132 other events, 1076.2 us)

commit v6 on v5

--- a/solution.py
+++ b/solution.py
@@ -16,7 +16,7 @@
 CHIPS = ("z", "y", "x")
 ALL = ("z", "y", "x", "core")
 NEAR = ("x", "y", "z")
-GROUPS = 2
+GROUPS = 1
 
 
 def depth_of(n_rows):

time: 381 us -> 325 us (0.85)
  starting transfers between devices: 134 us -> 72.2 us
  waiting for transfers between devices: 142 us -> 157 us
  other arithmetic: 25 us -> 16.8 us
    ppermute x124 -> x64, starting transfers between devices: 131 us -> 69.7 us  [swap(): return lax.ppermute(array, axis, pairs)]
    ppermute x124 -> x64, waiting for transfers between devices: 135 us -> 151 us  [swap(): return lax.ppermute(array, axis, pairs)]
    add x36 -> x18, other arithmetic: 18.5 us -> 10.4 us  [reduce(): keep, send = [k + g for k, g in zip(halves(keep), halves(got))]]
  transfers between devices with their start and end apart: 125 -> 65, of which waited for: 63 -> 46; matrix products, arithmetic and copies ran while one was open for 7% -> 5% of each run, Pallas kernels for 5% -> 6%
where the time goes in v6:
time: 325 us; the launch traced here: 323 us
  waiting for transfers between devices  157 us (48%)
  starting transfers between devices  72.2 us (22%)
  Pallas kernels  67.4 us (21%)
  other arithmetic  16.8 us (5%)
  local copies, waits for them, and re-layouts  7.78 us (2%)
    ppermute x64, waiting for transfers between devices, swap(): return lax.ppermute(array, axis, pairs)  151 us
    ppermute x64, starting transfers between devices, swap(): return lax.ppermute(array, axis, pairs)  69.7 us
    pallas_call x3, Pallas kernels, apply_tiles(): pl.pallas_call(functools.partial(apply_kernel, length, counts), out_shape...  46.8 us
    pallas_call x2, Pallas kernels, split_tiles(): pl.pallas_call(split_kernel, out_shape=jax.ShapeDtypeStruct((length, 2 *...  20.5 us
    add x18, other arithmetic, reduce(): keep, send = [k + g for k, g in zip(halves(keep), halves(got))]  10.4 us
    all_to_all x1, waiting for transfers between devices, shards(): lax.all_to_all(jnp.broadcast_to(totals, (chips * CORES, size)), ALL, spli...  6.78 us
  transfers between devices with their start and end apart: 65, of which 46 were waited for; matrix products, arithmetic and copies ran while one was open for 5% of the time, Pallas kernels for 6%

profile of v6, /device:TPU:0, one launch (start us, length us, event | category | flops | bytes accessed | tf_op | source)
XLA Modules:
  0.0 323.5 jit_solution(11627333177126196965)
XLA Ops:
  6.4 3.8 %collective-permute-start.3 = (f32[12,32,128]{2,1,0:T(8,128)S(1)}, f32[12,32,128]{2,1,0:T(8,128)S(1)}, u32[]{:S(2)}, u32[]{:S(2)}) collective-permute-start(f32[12,32,128]{2,1,0:T(8,128)S(1)} %broadcast_multiply_fusion), channel_id=1, source_target_pairs={{0,16},{8,24},{16,0},{24,8},{1,17},{9,25},{17,1},{25,9},{2,18},{10... | collective-permute-start | bytes 589832 | tf_op jit(solution)/shard_map/ppermute | solution.py:38
  10.2 9.6 %collective-permute-done.3 = f32[12,32,128]{2,1,0:T(8,128)S(1)} collective-permute-done((f32[12,32,128]{2,1,0:T(8,128)S(1)}, f32[12,32,128]{2,1,0:T(8,128)S(1)}, u32[]{:S(2)}, u32[]{:S(2)}) %collective-permute-start.3) | collective-permute-done | bytes 196640 | tf_op jit(solution)/shard_map/ppermute | solution.py:38
  28.7 4.3 %collective-permute-done.4 = f32[8,32,128]{2,1,0:T(8,128)S(1)} collective-permute-done((f32[8,32,128]{2,1,0:T(8,128)S(1)}, f32[8,32,128]{2,1,0:T(8,128)S(1)}, u32[]{:S(2)}, u32[]{:S(2)}) %collective-permute-start.4) | collective-permute-done | bytes 131104 | tf_op jit(solution)/shard_map/ppermute | solution.py:38
  35.9 2.7 collective-permute-done.8
  44.6 10.3 %shard_map.95.own_ref = bf16[128,256,128]{2,1,0:T(8,128)(2,1)} custom-call(f32[128,128,128]{2,1,0:T(8,128)} %tile_ref.1), custom_call_target="tpu_custom_call" | custom-call | flops 6291456 | bytes 16777216 | tf_op jit(solution)/shard_map/pallas_call | solution.py:108
  56.0 10.3 %shard_map.96.other_ref = bf16[128,256,128]{2,1,0:T(8,128)(2,1)} custom-call(f32[128,128,128]{2,1,0:T(8,128)} %collective-permute-done.2.tile_ref), custom_call_target="tpu_custom_call" | custom-call | flops 6291456 | bytes 16777216 | tf_op jit(solution)/shard_map/pallas_call | solution.py:108
  67.4 15.6 %shard_map.97 = (f32[32,32,128]{2,1,0:T(8,128)}, f32[32,32,128]{2,1,0:T(8,128)}, f32[32,32,128]{2,1,0:T(8,128)}, f32[32,32,128]{2,1,0:T(8,128)}, f32[32,32,128]{2,1,0:T(8,128)}, /*index=5*/f32[32,32,128]{2,1,0:T(8,128)}) custom-call(s32[256]{0:T(256)} %get-tuple-element.125.row_ref, s32[256]{0:T(256)} %get-tuple-element.124.col_ref, ...), custom_call_target="tpu_custom_call" | custom-call | flops 1073741824 | bytes 23068672 | tf_op jit(solution)/shard_map/pallas_call | solution.py:178
  86.7 11.0 %collective-permute-done.13 = f32[32,32,128]{2,1,0:T(8,128)S(1)} collective-permute-done((f32[32,32,128]{2,1,0:T(8,128)}, f32[32,32,128]{2,1,0:T(8,128)S(1)}, u32[]{:S(2)}, u32[]{:S(2)}) %collective-permute-start.13) | collective-permute-done | bytes 524320 | tf_op jit(solution)/shard_map/ppermute | solution.py:38
  107.4 2.2 collective-permute-done.17
  111.9 2.8 collective-permute-done.18
  116.5 3.6 %collective-permute-start.22 = (f32[12,32,128]{2,1,0:T(8,128)S(1)}, f32[12,32,128]{2,1,0:T(8,128)S(1)}, u32[]{:S(2)}, u32[]{:S(2)}) collective-permute-start(f32[12,32,128]{2,1,0:T(8,128)S(1)} %pad_maximum_fusion.19), channel_id=1, source_target_pairs={{0,16},{8,24},{16,0},{24,8},{1,17},{9,25},{17,1},{25,9},{2,18},{10... | collective-permute-start | bytes 589832 | tf_op jit(solution)/shard_map/ppermute | solution.py:38
  120.2 8.8 %collective-permute-done.22 = f32[12,32,128]{2,1,0:T(8,128)S(1)} collective-permute-done((f32[12,32,128]{2,1,0:T(8,128)S(1)}, f32[12,32,128]{2,1,0:T(8,128)S(1)}, u32[]{:S(2)}, u32[]{:S(2)}) %collective-permute-start.22) | collective-permute-done | bytes 196640 | tf_op jit(solution)/shard_map/ppermute | solution.py:38
  129.1 8.6 %collective-permute-done.23 = f32[12,32,128]{2,1,0:T(8,128)S(1)} collective-permute-done((f32[12,32,128]{2,1,0:T(8,128)S(1)}, f32[12,32,128]{2,1,0:T(8,128)S(1)}, u32[]{:S(2)}, u32[]{:S(2)}) %collective-permute-start.23) | collective-permute-done | bytes 196640 | tf_op jit(solution)/shard_map/ppermute | solution.py:38
  139.4 4.2 %collective-permute-done.30 = f32[8,32,128]{2,1,0:T(8,128)S(1)} collective-permute-done((f32[8,32,128]{2,1,0:T(8,128)S(1)}, f32[8,32,128]{2,1,0:T(8,128)S(1)}, u32[]{:S(2)}, u32[]{:S(2)}) %collective-permute-start.30) | collective-permute-done | bytes 131104 | tf_op jit(solution)/shard_map/ppermute | solution.py:38
  145.9 3.5 %collective-permute-done.24 = f32[8,32,128]{2,1,0:T(8,128)S(1)} collective-permute-done((f32[8,32,128]{2,1,0:T(8,128)S(1)}, f32[8,32,128]{2,1,0:T(8,128)S(1)}, u32[]{:S(2)}, u32[]{:S(2)}) %collective-permute-start.24) | collective-permute-done | bytes 131104 | tf_op jit(solution)/shard_map/ppermute | solution.py:38
  157.3 3.9 %collective-permute-done.32.refs_5_ = f32[32,32,128]{2,1,0:T(8,128)S(1)} collective-permute-done((f32[32,32,128]{2,1,0:T(8,128)S(1)}, f32[32,32,128]{2,1,0:T(8,128)S(1)}, u32[]{:S(2)}, u32[]{:S(2)}) %collective-permute-start.32) | collective-permute-done | bytes 524320 | tf_op jit(solution)/shard_map/ppermute | solution.py:38
  161.5 3.6 %collective-permute-done.26.refs_1_ = f32[32,32,128]{2,1,0:T(8,128)S(1)} collective-permute-done((f32[32,32,128]{2,1,0:T(8,128)S(1)}, f32[32,32,128]{2,1,0:T(8,128)S(1)}, u32[]{:S(2)}, u32[]{:S(2)}) %collective-permute-start.26) | collective-permute-done | bytes 524320 | tf_op jit(solution)/shard_map/ppermute | solution.py:38
  166.0 15.5 %shard_map.98 = (f32[32,32,128]{2,1,0:T(8,128)}, f32[32,32,128]{2,1,0:T(8,128)}, f32[32,32,128]{2,1,0:T(8,128)}, f32[32,32,128]{2,1,0:T(8,128)}, f32[32,32,128]{2,1,0:T(8,128)}, /*index=5*/f32[32,32,128]{2,1,0:T(8,128)}) custom-call(s32[256]{0:T(256)} %get-tuple-element.125.row_ref, s32[256]{0:T(256)} %get-tuple-element.124.col_ref, ...), custom_call_target="tpu_custom_call" | custom-call | flops 1073741824 | bytes 23068672 | tf_op jit(solution)/shard_map/pallas_call | solution.py:178
  184.0 11.2 %collective-permute-done.33 = f32[32,32,128]{2,1,0:T(8,128)S(1)} collective-permute-done((f32[32,32,128]{2,1,0:T(8,128)}, f32[32,32,128]{2,1,0:T(8,128)S(1)}, u32[]{:S(2)}, u32[]{:S(2)}) %collective-permute-start.33) | collective-permute-done | bytes 524320 | tf_op jit(solution)/shard_map/ppermute | solution.py:38
  203.0 2.9 collective-permute-done.37
  213.4 7.0 %collective-permute-done.42 = f32[12,32,128]{2,1,0:T(8,128)S(1)} collective-permute-done((f32[12,32,128]{2,1,0:T(8,128)S(1)}, f32[12,32,128]{2,1,0:T(8,128)S(1)}, u32[]{:S(2)}, u32[]{:S(2)}) %collective-permute-start.42) | collective-permute-done | bytes 196640 | tf_op jit(solution)/shard_map/ppermute | solution.py:38
  220.6 8.0 %collective-permute-done.43 = f32[12,32,128]{2,1,0:T(8,128)S(1)} collective-permute-done((f32[12,32,128]{2,1,0:T(8,128)S(1)}, f32[12,32,128]{2,1,0:T(8,128)S(1)}, u32[]{:S(2)}, u32[]{:S(2)}) %collective-permute-start.43) | collective-permute-done | bytes 196640 | tf_op jit(solution)/shard_map/ppermute | solution.py:38
  237.7 2.9 collective-permute-done.44
  247.4 3.9 %collective-permute-done.52.refs_5_ = f32[32,32,128]{2,1,0:T(8,128)S(1)} collective-permute-done((f32[32,32,128]{2,1,0:T(8,128)S(1)}, f32[32,32,128]{2,1,0:T(8,128)S(1)}, u32[]{:S(2)}, u32[]{:S(2)}) %collective-permute-start.52) | collective-permute-done | bytes 524320 | tf_op jit(solution)/shard_map/ppermute | solution.py:38
  252.7 5.2 %collective-permute-done.46.refs_1_ = f32[32,32,128]{2,1,0:T(8,128)S(1)} collective-permute-done((f32[32,32,128]{2,1,0:T(8,128)S(1)}, f32[32,32,128]{2,1,0:T(8,128)S(1)}, u32[]{:S(2)}, u32[]{:S(2)}) %collective-permute-start.46) | collective-permute-done | bytes 524320 | tf_op jit(solution)/shard_map/ppermute | solution.py:38
  258.7 15.7 %shard_map.99 = (f32[32,32,128]{2,1,0:T(8,128)}, f32[32,32,128]{2,1,0:T(8,128)}, f32[32,32,128]{2,1,0:T(8,128)}, f32[32,32,128]{2,1,0:T(8,128)}, f32[32,32,128]{2,1,0:T(8,128)}, /*index=5*/f32[32,32,128]{2,1,0:T(8,128)}) custom-call(s32[256]{0:T(256)} %get-tuple-element.125.row_ref, s32[256]{0:T(256)} %get-tuple-element.124.col_ref, ...), custom_call_target="tpu_custom_call" | custom-call | flops 1073741824 | bytes 23068672 | tf_op jit(solution)/shard_map/pallas_call | solution.py:178
  275.1 2.6 collective-permute-start.59
  277.7 6.1 %collective-permute-done.53 = f32[32,32,128]{2,1,0:T(8,128)S(1)} collective-permute-done((f32[32,32,128]{2,1,0:T(8,128)}, f32[32,32,128]{2,1,0:T(8,128)S(1)}, u32[]{:S(2)}, u32[]{:S(2)}) %collective-permute-start.53) | collective-permute-done | bytes 524320 | tf_op jit(solution)/shard_map/ppermute | solution.py:38
  298.3 2.6 collective-permute-done.61
  302.4 7.3 %collective-permute-done.62 = f32[12,32,128]{2,1,0:T(8,128)S(1)} collective-permute-done((f32[12,32,128]{2,1,0:T(8,128)S(1)}, f32[12,32,128]{2,1,0:T(8,128)S(1)}, u32[]{:S(2)}, u32[]{:S(2)}) %collective-permute-start.62) | collective-permute-done | bytes 196640 | tf_op jit(solution)/shard_map/ppermute | solution.py:38
  311.2 2.5 all-to-all-start
  314.0 6.8 %all-to-all-done = f32[32,1,128]{2,1,0:T(1,128)S(1)} async-done(((f32[32,1,128]{2,1,0:T(1,128)}), f32[32,1,128]{2,1,0:T(1,128)S(1)}, u32[]{:S(2)}, u32[]{:S(2)}) %all-to-all-start) | async-done | bytes 16416 | tf_op jit(solution)/shard_map/all_to_all | solution.py:286
  (239 shorter events, 112.4 us)
Async XLA Ops:
  4.5 51.5 %collective-permute-start.2 = (f32[128,128,128]{2,1,0:T(8,128)}, f32[128,128,128]{2,1,0:T(8,128)}, u32[]{:S(2)}, u32[]{:S(2)}) collective-permute-start(f32[128,128,128]{2,1,0:T(8,128)} %tile_ref.1), channel_id=1, source_target_pairs={{0,1},{1,0},{2,3},{3,2},{4,5},{5,4},{6,7},{7,6},{8,9},{9,8},{10,11... | collective-permute-start | bytes 25165832 | tf_op jit(solution)/shard_map/ppermute | solution.py:38
  6.4 13.4 %collective-permute-start.3 = (f32[12,32,128]{2,1,0:T(8,128)S(1)}, f32[12,32,128]{2,1,0:T(8,128)S(1)}, u32[]{:S(2)}, u32[]{:S(2)}) collective-permute-start(f32[12,32,128]{2,1,0:T(8,128)S(1)} %broadcast_multiply_fusion), channel_id=1, source_target_pairs={{0,16},{8,24},{16,0},{24,8},{1,17},{9,25},{17,1},{25,9},{2,18},{10... | collective-permute-start | bytes 589832 | tf_op jit(solution)/shard_map/ppermute | solution.py:38
  25.1 9.5 %collective-permute-start.11 = (f32[16,32,128]{2,1,0:T(8,128)S(1)}, f32[16,32,128]{2,1,0:T(8,128)S(1)}, u32[]{:S(2)}, u32[]{:S(2)}) collective-permute-start(f32[16,32,128]{2,1,0:T(8,128)S(1)} %pad_maximum_fusion.11), channel_id=1, source_target_pairs={{0,2},{2,0},{1,3},{3,1},{4,6},{6,4},{5,7},{7,5},{8,10},{10,8},{9,1... | collective-permute-start | bytes 786440 | tf_op jit(solution)/shard_map/ppermute | solution.py:38
  27.8 10.8 %collective-permute-start.8 = (f32[16,32,128]{2,1,0:T(8,128)S(1)}, f32[16,32,128]{2,1,0:T(8,128)S(1)}, u32[]{:S(2)}, u32[]{:S(2)}) collective-permute-start(f32[16,32,128]{2,1,0:T(8,128)S(1)} %pad_maximum_fusion.10), channel_id=1, source_target_pairs={{0,8},{8,0},{16,24},{24,16},{1,9},{9,1},{17,25},{25,17},{2,10},{10... | collective-permute-start | bytes 786440 | tf_op jit(solution)/shard_map/ppermute | solution.py:38
  33.0 9.2 %collective-permute-start.5 = (f32[16,32,128]{2,1,0:T(8,128)S(1)}, f32[16,32,128]{2,1,0:T(8,128)S(1)}, u32[]{:S(2)}, u32[]{:S(2)}) collective-permute-start(f32[16,32,128]{2,1,0:T(8,128)S(1)} %pad_maximum_fusion.9), channel_id=1, source_target_pairs={{0,4},{4,0},{1,5},{5,1},{2,6},{6,2},{3,7},{7,3},{8,12},{12,8},{9,1... | collective-permute-start | bytes 786440 | tf_op jit(solution)/shard_map/ppermute | solution.py:38
  34.6 31.7 %collective-permute-start.12 = (f32[32,32,128]{2,1,0:T(8,128)S(1)}, f32[32,32,128]{2,1,0:T(8,128)S(1)}, u32[]{:S(2)}, u32[]{:S(2)}) collective-permute-start(f32[32,32,128]{2,1,0:T(8,128)S(1)} %pad_maximum_fusion.2.refs_4_), channel_id=1, source_target_pairs={{0,8},{8,0},{16,24},{24,16},{1,9},{9,1},{17,25},{25,17},{2,10},{10... | collective-permute-start | bytes 1572872 | tf_op jit(solution)/shard_map/ppermute | solution.py:38
  38.6 27.7 %collective-permute-start.9 = (f32[32,32,128]{2,1,0:T(8,128)S(1)}, f32[32,32,128]{2,1,0:T(8,128)S(1)}, u32[]{:S(2)}, u32[]{:S(2)}) collective-permute-start(f32[32,32,128]{2,1,0:T(8,128)S(1)} %pad_maximum_fusion.1.refs_2_), channel_id=1, source_target_pairs={{0,4},{4,0},{1,5},{5,1},{2,6},{6,2},{3,7},{7,3},{8,12},{12,8},{9,1... | collective-permute-start | bytes 1572872 | tf_op jit(solution)/shard_map/ppermute | solution.py:38
  42.3 24.0 %collective-permute-start.6 = (f32[32,32,128]{2,1,0:T(8,128)S(1)}, f32[32,32,128]{2,1,0:T(8,128)S(1)}, u32[]{:S(2)}, u32[]{:S(2)}) collective-permute-start(f32[32,32,128]{2,1,0:T(8,128)S(1)} %pad_maximum_fusion.refs_0_), channel_id=1, source_target_pairs={{0,2},{2,0},{1,3},{3,1},{4,6},{6,4},{5,7},{7,5},{8,10},{10,8},{9,1... | collective-permute-start | bytes 1572872 | tf_op jit(solution)/shard_map/ppermute | solution.py:38
  44.5 10.3 %collective-permute-start.1 = (s32[128]{0:T(128)S(1)}, s32[128]{0:T(128)S(1)}, u32[]{:S(2)}, u32[]{:S(2)}) collective-permute-start(s32[128]{0:T(128)S(1)} %compare_select_fusion.27), channel_id=1, source_target_pairs={{0,1},{1,0},{2,3},{3,2},{4,5},{5,4},{6,7},{7,6},{8,9},{9,8},{10,11... | collective-permute-start | bytes 1544 | tf_op jit(solution)/shard_map/ppermute | solution.py:38
  83.1 14.6 %collective-permute-start.13 = (f32[32,32,128]{2,1,0:T(8,128)}, f32[32,32,128]{2,1,0:T(8,128)S(1)}, u32[]{:S(2)}, u32[]{:S(2)}) collective-permute-start(f32[32,32,128]{2,1,0:T(8,128)} %get-tuple-element.23), channel_id=1, source_target_pairs={{0,2},{2,0},{1,3},{3,1},{4,6},{6,4},{5,7},{7,5},{8,10},{10,8},{9,1... | collective-permute-start | bytes 1572872 | tf_op jit(solution)/shard_map/ppermute | solution.py:38
  84.4 15.8 %collective-permute-start.16 = (f32[32,32,128]{2,1,0:T(8,128)}, f32[32,32,128]{2,1,0:T(8,128)S(1)}, u32[]{:S(2)}, u32[]{:S(2)}) collective-permute-start(f32[32,32,128]{2,1,0:T(8,128)} %get-tuple-element.25), channel_id=1, source_target_pairs={{0,4},{4,0},{1,5},{5,1},{2,6},{6,2},{3,7},{7,3},{8,12},{12,8},{9,1... | collective-permute-start | bytes 1572872 | tf_op jit(solution)/shard_map/ppermute | solution.py:38
  85.9 16.2 %collective-permute-start.19 = (f32[32,32,128]{2,1,0:T(8,128)}, f32[32,32,128]{2,1,0:T(8,128)S(1)}, u32[]{:S(2)}, u32[]{:S(2)}) collective-permute-start(f32[32,32,128]{2,1,0:T(8,128)} %get-tuple-element.27), channel_id=1, source_target_pairs={{0,8},{8,0},{16,24},{24,16},{1,9},{9,1},{17,25},{25,17},{2,10},{10... | collective-permute-start | bytes 1572872 | tf_op jit(solution)/shard_map/ppermute | solution.py:38
  116.5 12.4 %collective-permute-start.22 = (f32[12,32,128]{2,1,0:T(8,128)S(1)}, f32[12,32,128]{2,1,0:T(8,128)S(1)}, u32[]{:S(2)}, u32[]{:S(2)}) collective-permute-start(f32[12,32,128]{2,1,0:T(8,128)S(1)} %pad_maximum_fusion.19), channel_id=1, source_target_pairs={{0,16},{8,24},{16,0},{24,8},{1,17},{9,25},{17,1},{25,9},{2,18},{10... | collective-permute-start | bytes 589832 | tf_op jit(solution)/shard_map/ppermute | solution.py:38
  129.0 8.7 %collective-permute-start.23 = (f32[12,32,128]{2,1,0:T(8,128)S(1)}, f32[12,32,128]{2,1,0:T(8,128)S(1)}, u32[]{:S(2)}, u32[]{:S(2)}) collective-permute-start(f32[12,32,128]{2,1,0:T(8,128)S(1)} %fusion.1), channel_id=1, source_target_pairs={{0,16},{8,24},{16,0},{24,8},{1,17},{9,25},{17,1},{25,9},{2,18},{10... | collective-permute-start | bytes 589832 | tf_op jit(solution)/shard_map/ppermute | solution.py:38
  143.8 8.4 %collective-permute-start.28 = (f32[16,32,128]{2,1,0:T(8,128)S(1)}, f32[16,32,128]{2,1,0:T(8,128)S(1)}, u32[]{:S(2)}, u32[]{:S(2)}) collective-permute-start(f32[16,32,128]{2,1,0:T(8,128)S(1)} %pad_maximum_fusion.13), channel_id=1, source_target_pairs={{0,8},{8,0},{16,24},{24,16},{1,9},{9,1},{17,25},{25,17},{2,10},{10... | collective-permute-start | bytes 786440 | tf_op jit(solution)/shard_map/ppermute | solution.py:38
  152.0 9.2 %collective-permute-start.32 = (f32[32,32,128]{2,1,0:T(8,128)S(1)}, f32[32,32,128]{2,1,0:T(8,128)S(1)}, u32[]{:S(2)}, u32[]{:S(2)}) collective-permute-start(f32[32,32,128]{2,1,0:T(8,128)S(1)} %pad_maximum_fusion.5.refs_4_), channel_id=1, source_target_pairs={{0,8},{8,0},{16,24},{24,16},{1,9},{9,1},{17,25},{25,17},{2,10},{10... | collective-permute-start | bytes 1572872 | tf_op jit(solution)/shard_map/ppermute | solution.py:38
  152.3 9.2 %collective-permute-start.29 = (f32[32,32,128]{2,1,0:T(8,128)S(1)}, f32[32,32,128]{2,1,0:T(8,128)S(1)}, u32[]{:S(2)}, u32[]{:S(2)}) collective-permute-start(f32[32,32,128]{2,1,0:T(8,128)S(1)} %pad_maximum_fusion.4.refs_2_), channel_id=1, source_target_pairs={{0,4},{4,0},{1,5},{5,1},{2,6},{6,2},{3,7},{7,3},{8,12},{12,8},{9,1... | collective-permute-start | bytes 1572872 | tf_op jit(solution)/shard_map/ppermute | solution.py:38
  155.9 9.2 %collective-permute-start.26 = (f32[32,32,128]{2,1,0:T(8,128)S(1)}, f32[32,32,128]{2,1,0:T(8,128)S(1)}, u32[]{:S(2)}, u32[]{:S(2)}) collective-permute-start(f32[32,32,128]{2,1,0:T(8,128)S(1)} %pad_maximum_fusion.3.refs_0_), channel_id=1, source_target_pairs={{0,2},{2,0},{1,3},{3,1},{4,6},{6,4},{5,7},{7,5},{8,10},{10,8},{9,1... | collective-permute-start | bytes 1572872 | tf_op jit(solution)/shard_map/ppermute | solution.py:38
  181.5 13.7 %collective-permute-start.33 = (f32[32,32,128]{2,1,0:T(8,128)}, f32[32,32,128]{2,1,0:T(8,128)S(1)}, u32[]{:S(2)}, u32[]{:S(2)}) collective-permute-start(f32[32,32,128]{2,1,0:T(8,128)} %get-tuple-element.29), channel_id=1, source_target_pairs={{0,2},{2,0},{1,3},{3,1},{4,6},{6,4},{5,7},{7,5},{8,10},{10,8},{9,1... | collective-permute-start | bytes 1572872 | tf_op jit(solution)/shard_map/ppermute | solution.py:38
  182.9 14.9 %collective-permute-start.36 = (f32[32,32,128]{2,1,0:T(8,128)}, f32[32,32,128]{2,1,0:T(8,128)S(1)}, u32[]{:S(2)}, u32[]{:S(2)}) collective-permute-start(f32[32,32,128]{2,1,0:T(8,128)} %get-tuple-element.31), channel_id=1, source_target_pairs={{0,4},{4,0},{1,5},{5,1},{2,6},{6,2},{3,7},{7,3},{8,12},{12,8},{9,1... | collective-permute-start | bytes 1572872 | tf_op jit(solution)/shard_map/ppermute | solution.py:38
  183.7 15.4 %collective-permute-start.39 = (f32[32,32,128]{2,1,0:T(8,128)}, f32[32,32,128]{2,1,0:T(8,128)S(1)}, u32[]{:S(2)}, u32[]{:S(2)}) collective-permute-start(f32[32,32,128]{2,1,0:T(8,128)} %get-tuple-element.33), channel_id=1, source_target_pairs={{0,8},{8,0},{16,24},{24,16},{1,9},{9,1},{17,25},{25,17},{2,10},{10... | collective-permute-start | bytes 1572872 | tf_op jit(solution)/shard_map/ppermute | solution.py:38
  212.1 8.4 %collective-permute-start.42 = (f32[12,32,128]{2,1,0:T(8,128)S(1)}, f32[12,32,128]{2,1,0:T(8,128)S(1)}, u32[]{:S(2)}, u32[]{:S(2)}) collective-permute-start(f32[12,32,128]{2,1,0:T(8,128)S(1)} %pad_maximum_fusion.20), channel_id=1, source_target_pairs={{0,16},{8,24},{16,0},{24,8},{1,17},{9,25},{17,1},{25,9},{2,18},{10... | collective-permute-start | bytes 589832 | tf_op jit(solution)/shard_map/ppermute | solution.py:38
  233.7 8.4 %collective-permute-start.51 = (f32[16,32,128]{2,1,0:T(8,128)S(1)}, f32[16,32,128]{2,1,0:T(8,128)S(1)}, u32[]{:S(2)}, u32[]{:S(2)}) collective-permute-start(f32[16,32,128]{2,1,0:T(8,128)S(1)} %pad_maximum_fusion.17), channel_id=1, source_target_pairs={{0,2},{2,0},{1,3},{3,1},{4,6},{6,4},{5,7},{7,5},{8,10},{10,8},{9,1... | collective-permute-start | bytes 786440 | tf_op jit(solution)/shard_map/ppermute | solution.py:38
  242.1 9.2 %collective-permute-start.52 = (f32[32,32,128]{2,1,0:T(8,128)S(1)}, f32[32,32,128]{2,1,0:T(8,128)S(1)}, u32[]{:S(2)}, u32[]{:S(2)}) collective-permute-start(f32[32,32,128]{2,1,0:T(8,128)S(1)} %pad_maximum_fusion.8.refs_4_), channel_id=1, source_target_pairs={{0,8},{8,0},{16,24},{24,16},{1,9},{9,1},{17,25},{25,17},{2,10},{10... | collective-permute-start | bytes 1572872 | tf_op jit(solution)/shard_map/ppermute | solution.py:38
  243.4 9.2 %collective-permute-start.49 = (f32[32,32,128]{2,1,0:T(8,128)S(1)}, f32[32,32,128]{2,1,0:T(8,128)S(1)}, u32[]{:S(2)}, u32[]{:S(2)}) collective-permute-start(f32[32,32,128]{2,1,0:T(8,128)S(1)} %pad_maximum_fusion.7.refs_2_), channel_id=1, source_target_pairs={{0,4},{4,0},{1,5},{5,1},{2,6},{6,2},{3,7},{7,3},{8,12},{12,8},{9,1... | collective-permute-start | bytes 1572872 | tf_op jit(solution)/shard_map/ppermute | solution.py:38
  247.1 10.7 %collective-permute-start.46 = (f32[32,32,128]{2,1,0:T(8,128)S(1)}, f32[32,32,128]{2,1,0:T(8,128)S(1)}, u32[]{:S(2)}, u32[]{:S(2)}) collective-permute-start(f32[32,32,128]{2,1,0:T(8,128)S(1)} %pad_maximum_fusion.6.refs_0_), channel_id=1, source_target_pairs={{0,2},{2,0},{1,3},{3,1},{4,6},{6,4},{5,7},{7,5},{8,10},{10,8},{9,1... | collective-permute-start | bytes 1572872 | tf_op jit(solution)/shard_map/ppermute | solution.py:38
  274.4 9.5 %collective-permute-start.53 = (f32[32,32,128]{2,1,0:T(8,128)}, f32[32,32,128]{2,1,0:T(8,128)S(1)}, u32[]{:S(2)}, u32[]{:S(2)}) collective-permute-start(f32[32,32,128]{2,1,0:T(8,128)} %get-tuple-element.35), channel_id=1, source_target_pairs={{0,2},{2,0},{1,3},{3,1},{4,6},{6,4},{5,7},{7,5},{8,10},{10,8},{9,1... | collective-permute-start | bytes 1572872 | tf_op jit(solution)/shard_map/ppermute | solution.py:38
  274.5 11.2 %collective-permute-start.56 = (f32[32,32,128]{2,1,0:T(8,128)}, f32[32,32,128]{2,1,0:T(8,128)S(1)}, u32[]{:S(2)}, u32[]{:S(2)}) collective-permute-start(f32[32,32,128]{2,1,0:T(8,128)} %get-tuple-element.37), channel_id=1, source_target_pairs={{0,4},{4,0},{1,5},{5,1},{2,6},{6,2},{3,7},{7,3},{8,12},{12,8},{9,1... | collective-permute-start | bytes 1572872 | tf_op jit(solution)/shard_map/ppermute | solution.py:38
  275.1 13.2 %collective-permute-start.59 = (f32[32,32,128]{2,1,0:T(8,128)}, f32[32,32,128]{2,1,0:T(8,128)S(1)}, u32[]{:S(2)}, u32[]{:S(2)}) collective-permute-start(f32[32,32,128]{2,1,0:T(8,128)} %get-tuple-element.39), channel_id=1, source_target_pairs={{0,8},{8,0},{16,24},{24,16},{1,9},{9,1},{17,25},{25,17},{2,10},{10... | collective-permute-start | bytes 1572872 | tf_op jit(solution)/shard_map/ppermute | solution.py:38
  301.0 8.7 %collective-permute-start.62 = (f32[12,32,128]{2,1,0:T(8,128)S(1)}, f32[12,32,128]{2,1,0:T(8,128)S(1)}, u32[]{:S(2)}, u32[]{:S(2)}) collective-permute-start(f32[12,32,128]{2,1,0:T(8,128)S(1)} %pad_maximum_fusion.21), channel_id=1, source_target_pairs={{0,16},{8,24},{16,0},{24,8},{1,17},{9,25},{17,1},{25,9},{2,18},{10... | collective-permute-start | bytes 589832 | tf_op jit(solution)/shard_map/ppermute | solution.py:38
  311.2 9.6 %all-to-all-start = ((f32[32,1,128]{2,1,0:T(1,128)}), f32[32,1,128]{2,1,0:T(1,128)S(1)}, u32[]{:S(2)}, u32[]{:S(2)}) async-start(f32[32,1,128]{2,1,0:T(1,128)} %broadcast_in_dim.31), calls=%async_computation | async-start | bytes 32768 | tf_op jit(solution)/shard_map/all_to_all | solution.py:286
  313.8 9.0 %collective-permute-start.63 = (f32[6,32,128]{2,1,0:T(8,128)S(1)}, f32[6,32,128]{2,1,0:T(8,128)S(1)}, u32[]{:S(2)}, u32[]{:S(2)}) collective-permute-start(f32[6,32,128]{2,1,0:T(8,128)S(1)} %slice_select_fusion), channel_id=1, source_target_pairs={{0,1},{1,0},{2,3},{3,2},{4,5},{5,4},{6,7},{7,6},{8,9},{9,8},{10,11... | collective-permute-start | bytes 294920 | tf_op jit(solution)/shard_map/ppermute | solution.py:38
  (54 other events, 442.5 us)

commit v7 on v6

v7 whole, which is shorter than its diff:
```python
import functools

import jax
import jax.numpy as jnp
from jax import lax
from jax.experimental import pallas as pl
from jax.experimental.pallas import tpu as pltpu
from jax.sharding import Mesh
from jax.sharding import PartitionSpec as P

ITERS = 3
CORES = 2
STEP = 16
UNROLL = 8
CHUNK = 8
SLOTS = 8
VMEM = 60 * 1024 * 1024
CHIPS = ("z", "y", "x")
ALL = ("z", "y", "x", "core")
NEAR = ("x", "y", "z")


def depth_of(n_rows):
    return min(n for n in range(1, n_rows + 1) if n_rows % n == 0 and n * n >= n_rows)


def far_steps():
    return [(a, 1 << k) for a in NEAR for k in range(1, lax.axis_size(a).bit_length() - 1)]


def near_steps(part):
    turn = part % len(NEAR)
    return [(a, 1) for a in NEAR[turn:] + NEAR[:turn]]


def swap(array, step):
    axis, distance = step
    pairs = [(i, i ^ distance) for i in range(lax.axis_size(axis))]
    return lax.ppermute(array, axis, pairs)


def after(value, *others):
    return lax.optimization_barrier((value,) + others)[0]


def halves(array):
    middle = array.shape[0] // 2
    return array[:middle], array[middle:]


def gather_far(block, beside=None):
    blocks = [block]
    for step in reversed(far_steps()):
        got = swap(blocks[0] if len(blocks) == 1 else jnp.concatenate(blocks, axis=0), step)
        if beside is not None:
            got, beside = after(got, beside), None
        blocks = blocks + jnp.split(got, len(blocks))
    return blocks


def gather(flux, edges, beside=None):
    blocks = gather_far(flux, beside)
    pieces = []
    for part in range(len(NEAR)):
        block = jnp.concatenate([b[edges[part] : edges[part + 1]] for b in blocks], axis=0)
        steps = near_steps(part)
        for step in reversed(steps[1:]):
            block = jnp.concatenate([block, swap(block, step)], axis=0)
        pieces.append((block, swap(block, steps[0])))
    return pieces


def reduce_near(keeps, sends):
    far = 1 << len(far_steps())
    parts = []
    for part, (keep, send) in enumerate(zip(keeps, sends)):
        steps = near_steps(part)
        got = swap(send, steps[0])
        for step in steps[1:]:
            keep, send = [k + g for k, g in zip(halves(keep), halves(got))]
            got = swap(send, step)
        parts.append([k + g for k, g in zip(jnp.split(keep, far), jnp.split(got, far))])
    return [jnp.concatenate(group, axis=0) for group in zip(*parts)]


def reduce_far(blocks):
    for step in far_steps():
        middle = len(blocks) // 2
        send = blocks[middle:]
        got = swap(jnp.concatenate(send, axis=0) if middle > 1 else send[0], step)
        blocks = [b + g for b, g in zip(blocks[:middle], jnp.split(got, middle))]
    return blocks[0]


def split_kernel(tile_ref, *refs):
    pair_ref = refs[-1]
    size = tile_ref.shape[1]

    @pl.loop(0, STEP // UNROLL)
    def _(group):
        for k in range(UNROLL):
            tile = jnp.transpose(tile_ref[group * UNROLL + k])
            high = tile.astype(jnp.bfloat16)
            low = (tile - high.astype(jnp.float32)).astype(jnp.bfloat16)
            pair_ref[group * UNROLL + k, :size] = high
            pair_ref[group * UNROLL + k, size:] = low


def split_tiles(tiles, place, pairs=None):
    length, size, _ = tiles.shape
    steps = length // STEP
    given = [] if pairs is None else [pairs]
    return pl.pallas_call(
        split_kernel,
        out_shape=jax.ShapeDtypeStruct((CORES * length, 2 * size, size), jnp.bfloat16),
        grid=(steps,),
        in_specs=[pl.BlockSpec((STEP, size, size), lambda i: (i, 0, 0))]
        + [pl.BlockSpec(memory_space=pl.ANY)] * len(given),
        out_specs=pl.BlockSpec((STEP, 2 * size, size), lambda i: (place * steps + i, 0, 0)),
        input_output_aliases={1: 0} if given else {},
        compiler_params=pltpu.CompilerParams(vmem_limit_bytes=VMEM),
        cost_estimate=pl.CostEstimate(
            flops=3 * length * size * size, bytes_accessed=8 * length * size * size, transcendentals=0
        ),
    )(tiles, *given)


def apply_kernel(span, skip, counts, has_base, ends_ref, order_ref, row_ref, col_ref, pairs_ref, *refs):
    ends, refs = refs[: len(counts)], refs[len(counts) :]
    base_ref, refs = (refs[0], refs[1:]) if has_base else (None, refs)
    *outs, flux_ref, sum_ref, held_ref, sem, held_sem = refs
    total = order_ref.shape[0]
    start, stop = ends_ref[span], ends_ref[span + 1]
    chunks = (stop - start + CHUNK - 1) // CHUNK

    def fetch(chunk):
        slot = lax.rem(chunk, SLOTS)
        for k in range(CHUNK):
            at = jnp.minimum(start + chunk * CHUNK + k, total - 1)
            pltpu.make_async_copy(
                pairs_ref.at[order_ref[at]], held_ref.at[slot, k], held_sem.at[slot]
            ).start()

    copies = [
        pltpu.make_async_copy(
            piece, flux_ref.at[pl.ds(sum(counts[:k]), counts[k])], sem.at[k]
        )
        for k, piece in enumerate(ends)
    ]
    if has_base:
        copies.append(pltpu.make_async_copy(base_ref, sum_ref, sem.at[len(counts)]))
    for copy in copies:
        copy.start()
    for chunk in range(SLOTS - 1):

        @pl.when(chunk < chunks)
        def _():
            fetch(jnp.int32(chunk))

    if not has_base:
        sum_ref[...] = jnp.zeros_like(sum_ref)
    for copy in copies:
        copy.wait()

    @pl.loop(0, chunks)
    def _(chunk):
        slot = lax.rem(chunk, SLOTS)
        pltpu.make_async_copy(
            pairs_ref.at[pl.ds(0, CHUNK)], held_ref.at[slot], held_sem.at[slot]
        ).wait()

        @pl.when(chunk + SLOTS - 1 < chunks)
        def _():
            fetch(chunk + SLOTS - 1)

        products, rows = [], []
        for k in range(CHUNK):
            at = start + chunk * CHUNK + k
            valid = jnp.where(at < stop, 1.0, 0.0)
            at = jnp.minimum(at, stop - 1)
            flux = flux_ref[col_ref[at]] * valid
            high = flux.astype(jnp.bfloat16)
            low = (flux - high.astype(jnp.float32)).astype(jnp.bfloat16)
            left = jnp.concatenate([high, low], axis=0)
            both = jnp.dot(
                jnp.concatenate([left, left], axis=1),
                held_ref[slot, k],
                preferred_element_type=jnp.float32,
            )
            temps = flux.shape[0]
            products.append(both[:temps] + both[temps:])
            rows.append(row_ref[at] - skip)
        for row, product in zip(rows, products):
            sum_ref[row] += product

    sizes = [out.shape[0] for out in outs]
    copies = [
        pltpu.make_async_copy(sum_ref.at[pl.ds(sum(sizes[:k]), sizes[k])], out, sem.at[k])
        for k, out in enumerate(outs)
    ]
    for copy in copies:
        copy.start()
    for copy in copies:
        copy.wait()


def apply_tiles(span, skip, places, pairs, flux, sizes, share, base=None):
    total, _, size = pairs.shape
    counts = [piece.shape[0] for piece in flux]
    temps = flux[0].shape[1]
    anywhere = pl.BlockSpec(memory_space=pl.ANY)
    given = [pairs, *flux] + ([] if base is None else [base])
    return pl.pallas_call(
        functools.partial(apply_kernel, span, skip, counts, base is not None),
        out_shape=[jax.ShapeDtypeStruct((n, temps, size), jnp.float32) for n in sizes],
        grid_spec=pltpu.PrefetchScalarGridSpec(
            num_scalar_prefetch=4,
            grid=(),
            in_specs=[anywhere] * len(given),
            out_specs=[anywhere] * len(sizes),
            scratch_shapes=[
                pltpu.VMEM((sum(counts), temps, size), jnp.float32),
                pltpu.VMEM((sum(sizes), temps, size), jnp.float32),
                pltpu.VMEM((SLOTS, CHUNK) + pairs.shape[1:], jnp.bfloat16),
                pltpu.SemaphoreType.DMA((len(counts) + 1,)),
                pltpu.SemaphoreType.DMA((SLOTS,)),
            ],
        ),
        compiler_params=pltpu.CompilerParams(vmem_limit_bytes=VMEM),
        cost_estimate=pl.CostEstimate(
            flops=int(share * total * size * size * temps * 8),
            bytes_accessed=int(share * total * size * size * 4) + 8 * sum(sizes) * temps * size,
            transcendentals=0,
        ),
    )(*places, *given)


def shards(
    tile_values, tile_owner, tile_row, tile_col, tile_count, relaxation, driving, heat_weight
):
    n_cols = lax.axis_size("x") * CORES
    chips = lax.axis_size(CHIPS)
    length, size, _ = tile_values.shape
    modes, columns = driving.shape
    per = modes // size
    chip_tiles = CORES * per
    num = chips * chip_tiles
    half = columns // CORES
    core = lax.axis_index("core")
    cores = ("core", 1)

    edges = [chip_tiles * k // len(NEAR) for k in range(len(NEAR) + 1)]

    def place(tile):
        chip, inside = tile // chip_tiles, tile % chip_tiles
        away, width = {}, 1
        for axis in reversed(CHIPS):
            n = lax.axis_size(axis)
            away[axis] = ((chip // width) % n) ^ lax.axis_index(axis)
            width *= n
        side, out = jnp.zeros_like(tile), jnp.zeros_like(tile)
        for part in range(len(NEAR)):
            low, high = edges[part], edges[part + 1]
            (first, _), *steps = near_steps(part)
            slot = jnp.zeros_like(tile)
            for axis, distance in steps + far_steps():
                slot = 2 * slot + (away[axis] // distance) % 2
            slot = chips // 2 * low + slot * (high - low) + inside - low
            out = jnp.where(inside >= low, slot, out)
            side = jnp.where(inside >= low, away[first] % 2, side)
        return side, out

    owners = tile_owner[:, 0]
    row_side, row = place((owners // n_cols) * (n_cols * per) + tile_row)
    col_side, col = place(((tile_col // per) * n_cols + owners % n_cols) * per + tile_col % per)
    used = jnp.arange(length, dtype=jnp.int32) < tile_count[0]
    kind = jnp.where(used, jnp.where(col_side == 0, 0, 2 - row_side), 3)
    row = jnp.where(row_side == 1, row, row + num // 2)
    code = (kind * num + row) * num + col
    code = jnp.concatenate([code, swap(code, cores)])
    kind = code // (num * num)
    slots = jnp.arange(CORES * length, dtype=jnp.int32)
    key = kind * (CORES * length) + slots
    rank = jnp.sum((key[None, :] < key[:, None]).astype(jnp.int32), axis=1)
    ends = jnp.sum((kind[None, :] < jnp.arange(4, dtype=jnp.int32)[:, None]).astype(jnp.int32), axis=1)
    sorts = rank[None, :] == slots[:, None]
    order = jnp.sum(jnp.where(sorts, slots[None, :], 0), axis=1)
    code = jnp.sum(jnp.where(sorts, code[None, :] % (num * num), 0), axis=1)
    places = (ends, order, code // num, code % num)

    def by_core(own, other):
        return jnp.concatenate(
            [jnp.where(core == 0, own, other), jnp.where(core == 0, other, own)], axis=0
        )

    drive = jnp.transpose(driving.reshape(per, size, columns), (0, 2, 1))
    relax = relaxation.reshape(per, 1, size)
    heat = heat_weight.reshape(per, 1, size)
    low, high = drive[:, :half], drive[:, half:]
    mine = jnp.where(core == 0, low, high)
    theirs = jnp.where(core == 0, high, low)
    packed = [theirs, jnp.broadcast_to(relax, (per, 8, size)), jnp.broadcast_to(heat, (per, 8, size))]
    got = swap(jnp.concatenate(packed, axis=1), cores)
    other_values = swap(after(tile_values, got), cores)
    drive_half = by_core(mine, got[:, :half])
    relax_both = by_core(relax, got[:, half : half + 1])
    heat_both = by_core(heat, got[:, half + 8 : half + 9])

    pairs = split_tiles(tile_values, 0)
    beside = pairs
    heats = gather_far(heat_both * relax_both)
    flux = relax_both * drive_half
    sizes = [chips // 2 * (high - low) for low, high in zip(edges[:-1], edges[1:])]
    for sweep in range(ITERS):
        pieces = gather(flux, edges, beside)
        if sweep == 0:
            pairs, beside = split_tiles(other_values, 1, pairs), None
        near, far = [p for p, _ in pieces], [p for _, p in pieces]
        base = apply_tiles(0, 0, places, pairs, near, [num // 2, num // 2], 0.5)
        sends = apply_tiles(1, 0, places, pairs, far, sizes, 0.25, base[0])
        keeps = apply_tiles(2, num // 2, places, pairs, far, sizes, 0.25, base[1])
        blocks = reduce_near(keeps, sends)
        if sweep == ITERS - 1:
            weighted = sum(
                [jnp.sum(w * b, axis=(0, 2)) for w, b in zip(heats, blocks)],
                jnp.sum(heats[0] * drive_half, axis=(0, 2)),
            )
            totals = jnp.concatenate([weighted, jnp.sum(heat).reshape(1)])
            totals = jnp.pad(totals[None], ((0, 0), (0, size - half - 1)))
            totals = lax.all_to_all(
                jnp.broadcast_to(totals, (chips * CORES, size)), ALL, split_axis=0, concat_axis=0, tiled=True
            )
            totals = jnp.sum(totals.reshape(chips, CORES, size), axis=0)
            conductivity = totals[:, :half].reshape(columns) / jnp.sum(totals[:, half])
        flux = relax_both * (drive_half + reduce_far(blocks))
    first, second = flux[:per], flux[per:]
    mine = jnp.where(core == 0, first, second)
    got = swap(jnp.where(core == 0, second, first), cores)
    both = jnp.concatenate(
        [jnp.where(core == 0, mine, got), jnp.where(core == 0, got, mine)], axis=1
    )
    mode_flux = jnp.transpose(both, (0, 2, 1)).reshape(modes, columns)
    return (mode_flux, conductivity)


def solution(mesh):
    n_rows, n_cols = mesh.shape["row"], mesh.shape["col"]
    planes = depth_of(n_rows)
    chips = Mesh(mesh.devices.reshape(planes, n_rows // planes, n_cols // CORES, CORES), ALL)
    placed = (
        P(ALL, None, None),
        P(ALL, None),
        P(ALL),
        P(ALL),
        P(ALL),
        P(ALL),
        P(ALL, None),
        P(ALL),
    )
    return jax.shard_map(
        shards,
        mesh=chips,
        in_specs=placed,
        out_specs=(P(ALL, None), P()),
        check_vma=False,
    )
```

time: 325 us -> 312 us (0.960)
  waiting for transfers between devices: 157 us -> 116 us
  Pallas kernels: 67.4 us -> 86.8 us
  starting transfers between devices: 72.2 us -> 86.6 us
  other arithmetic: 16.8 us -> 11.9 us
    ppermute x64 -> x65, waiting for transfers between devices: 151 us -> 109 us  [swap(): return lax.ppermute(array, axis, pairs)]
    pallas_call x5 -> x11, Pallas kernels: 67.4 us -> 86.8 us  [the longest x9 66.3 us: apply_tiles(): pl.pallas_call(functools.partial(apply_kernel, span, skip, counts, base i...]
    ppermute x64 -> x65, starting transfers between devices: 69.7 us -> 83.1 us  [swap(): return lax.ppermute(array, axis, pairs)]
    add x27 -> x30, other arithmetic: 10.5 us -> 5.31 us  [the longest x18 4.34 us: reduce_near(): keep, send = [k + g for k, g in zip(halves(keep), halves(got))]]
  transfers between devices with their start and end apart: 65 -> 66, of which waited for: 46 -> 39; matrix products, arithmetic and copies ran while one was open for 5% -> 3% of each run, Pallas kernels for 6% -> 22%
where the time goes in v7:
time: 312 us; the launch traced here: 310 us
  waiting for transfers between devices  116 us (37%)
  Pallas kernels  86.8 us (28%)
  starting transfers between devices  86.6 us (28%)
  other arithmetic  11.9 us (4%)
  local copies, waits for them, and re-layouts  7.33 us (2%)
    ppermute x65, waiting for transfers between devices, swap(): return lax.ppermute(array, axis, pairs)  109 us
    ppermute x65, starting transfers between devices, swap(): return lax.ppermute(array, axis, pairs)  83.1 us
    pallas_call x9, Pallas kernels, apply_tiles(): pl.pallas_call(functools.partial(apply_kernel, span, skip, counts, base i...  66.3 us
    pallas_call x2, Pallas kernels, split_tiles(): pl.pallas_call(split_kernel, out_shape=jax.ShapeDtypeStruct((CORES * leng...  20.5 us
    all_to_all x1, waiting for transfers between devices, shards(): lax.all_to_all(jnp.broadcast_to(totals, (chips * CORES, size)), ALL, spli...  6.73 us
  transfers between devices with their start and end apart: 66, of which 39 were waited for; matrix products, arithmetic and copies ran while one was open for 3% of the time, Pallas kernels for 22%

profile of v7, /device:TPU:0, one launch (start us, length us, event | category | flops | bytes accessed | tf_op | source)
XLA Modules:
  0.0 310.4 jit_solution(13053805124653334555)
XLA Ops:
  6.6 10.2 %shard_map.95.refs_0_ = bf16[256,256,128]{2,1,0:T(8,128)(2,1)} custom-call(f32[128,128,128]{2,1,0:T(8,128)} %tile_ref.1), custom_call_target="tpu_custom_call" | custom-call | flops 6291456 | bytes 16777216 | tf_op jit(solution)/shard_map/pallas_call | solution.py:113
  16.9 4.0 %collective-permute-start.3 = (f32[12,32,128]{2,1,0:T(8,128)S(1)}, f32[12,32,128]{2,1,0:T(8,128)S(1)}, u32[]{:S(2)}, u32[]{:S(2)}) collective-permute-start(f32[12,32,128]{2,1,0:T(8,128)S(1)} %broadcast_multiply_fusion), channel_id=1, source_target_pairs={{0,16},{8,24},{16,0},{24,8},{1,17},{9,25},{17,1},{25,9},{2,18},{10... | collective-permute-start | bytes 589832 | tf_op jit(solution)/shard_map/ppermute | solution.py:39
  21.0 9.4 %collective-permute-done.3 = f32[12,32,128]{2,1,0:T(8,128)S(1)} collective-permute-done((f32[12,32,128]{2,1,0:T(8,128)S(1)}, f32[12,32,128]{2,1,0:T(8,128)S(1)}, u32[]{:S(2)}, u32[]{:S(2)}) %collective-permute-start.3) | collective-permute-done | bytes 196640 | tf_op jit(solution)/shard_map/ppermute | solution.py:39
  40.0 3.5 %collective-permute-done.5 = f32[16,32,128]{2,1,0:T(8,128)S(1)} collective-permute-done((f32[16,32,128]{2,1,0:T(8,128)S(1)}, f32[16,32,128]{2,1,0:T(8,128)S(1)}, u32[]{:S(2)}, u32[]{:S(2)}) %collective-permute-start.5) | collective-permute-done | bytes 262176 | tf_op jit(solution)/shard_map/ppermute | solution.py:39
  49.6 10.3 %shard_map.96.pairs_ref = bf16[256,256,128]{2,1,0:T(8,128)(2,1)} custom-call(f32[128,128,128]{2,1,0:T(8,128)} %collective-permute-done.2.tile_ref, bf16[256,256,128]{2,1,0:T(8,128)(2,1)} %shard_map.95.refs_0_), custom_call_target="tpu_custom_call", output_to_operand_aliasing={{}: (1, {})} | custom-call | flops 6291456 | bytes 16777216 | tf_op jit(solution)/shard_map/pallas_call | solution.py:113
  59.9 8.7 %shard_map.97 = (f32[96,32,128]{2,1,0:T(8,128)}, f32[96,32,128]{2,1,0:T(8,128)}) custom-call(s32[4]{0:T(128)} %convert_reduce_fusion.1.ends_ref, s32[256]{0:T(256)} %get-tuple-element.57.order_ref, s32[256]{0:T(256)} %get-tuple-element.146.row_ref, s32[256]{0:T(256)} %get-tuple-element.145.col_ref, bf16[256,256,128]{2,1,0:T(8,128)(2,1)} %shard_map.96.pairs_ref, ...), custom_call_target="tpu_custom_call" | custom-call | flops 536870912 | bytes 14680064 | tf_op jit(solution)/shard_map/pallas_call | solution.py:213
  69.8 6.5 %shard_map.99 = (f32[32,32,128]{2,1,0:T(8,128)}, f32[32,32,128]{2,1,0:T(8,128)}, f32[32,32,128]{2,1,0:T(8,128)}) custom-call(s32[4]{0:T(128)} %convert_reduce_fusion.1.ends_ref, s32[256]{0:T(256)} %get-tuple-element.57.order_ref, s32[256]{0:T(256)} %get-tuple-element.146.row_ref, s32[256]{0:T(256)} %get-tuple-element.145.col_ref, ...), custom_call_target="tpu_custom_call" | custom-call | flops 268435456 | bytes 7340032 | tf_op jit(solution)/shard_map/pallas_call | solution.py:213
  80.2 6.9 %shard_map.98 = (f32[32,32,128]{2,1,0:T(8,128)}, f32[32,32,128]{2,1,0:T(8,128)}, f32[32,32,128]{2,1,0:T(8,128)}) custom-call(s32[4]{0:T(128)} %convert_reduce_fusion.1.ends_ref, s32[256]{0:T(256)} %get-tuple-element.57.order_ref, s32[256]{0:T(256)} %get-tuple-element.146.row_ref, s32[256]{0:T(256)} %get-tuple-element.145.col_ref, ...), custom_call_target="tpu_custom_call" | custom-call | flops 268435456 | bytes 7340032 | tf_op jit(solution)/shard_map/pallas_call | solution.py:213
  104.5 4.3 %collective-permute-start.22 = (f32[12,32,128]{2,1,0:T(8,128)S(1)}, f32[12,32,128]{2,1,0:T(8,128)S(1)}, u32[]{:S(2)}, u32[]{:S(2)}) collective-permute-start(f32[12,32,128]{2,1,0:T(8,128)S(1)} %pad_maximum_fusion.19), channel_id=1, source_target_pairs={{0,16},{8,24},{16,0},{24,8},{1,17},{9,25},{17,1},{25,9},{2,18},{10... | collective-permute-start | bytes 589832 | tf_op jit(solution)/shard_map/ppermute | solution.py:39
  108.8 9.3 %collective-permute-done.22 = f32[12,32,128]{2,1,0:T(8,128)S(1)} collective-permute-done((f32[12,32,128]{2,1,0:T(8,128)S(1)}, f32[12,32,128]{2,1,0:T(8,128)S(1)}, u32[]{:S(2)}, u32[]{:S(2)}) %collective-permute-start.22) | collective-permute-done | bytes 196640 | tf_op jit(solution)/shard_map/ppermute | solution.py:39
  118.3 8.6 %collective-permute-done.23 = f32[12,32,128]{2,1,0:T(8,128)S(1)} collective-permute-done((f32[12,32,128]{2,1,0:T(8,128)S(1)}, f32[12,32,128]{2,1,0:T(8,128)S(1)}, u32[]{:S(2)}, u32[]{:S(2)}) %collective-permute-start.23) | collective-permute-done | bytes 196640 | tf_op jit(solution)/shard_map/ppermute | solution.py:39
  128.6 3.4 %collective-permute-done.24 = f32[8,32,128]{2,1,0:T(8,128)S(1)} collective-permute-done((f32[8,32,128]{2,1,0:T(8,128)S(1)}, f32[8,32,128]{2,1,0:T(8,128)S(1)}, u32[]{:S(2)}, u32[]{:S(2)}) %collective-permute-start.24) | collective-permute-done | bytes 131104 | tf_op jit(solution)/shard_map/ppermute | solution.py:39
  135.6 8.4 %collective-permute-done.30 = f32[8,32,128]{2,1,0:T(8,128)S(1)} collective-permute-done((f32[8,32,128]{2,1,0:T(8,128)S(1)}, f32[8,32,128]{2,1,0:T(8,128)S(1)}, u32[]{:S(2)}, u32[]{:S(2)}) %collective-permute-start.30) | collective-permute-done | bytes 131104 | tf_op jit(solution)/shard_map/ppermute | solution.py:39
  146.7 3.8 %collective-permute-done.31 = f32[16,32,128]{2,1,0:T(8,128)S(1)} collective-permute-done((f32[16,32,128]{2,1,0:T(8,128)S(1)}, f32[16,32,128]{2,1,0:T(8,128)S(1)}, u32[]{:S(2)}, u32[]{:S(2)}) %collective-permute-start.31) | collective-permute-done | bytes 262176 | tf_op jit(solution)/shard_map/ppermute | solution.py:39
  151.9 8.7 %shard_map.100 = (f32[96,32,128]{2,1,0:T(8,128)}, f32[96,32,128]{2,1,0:T(8,128)}) custom-call(s32[4]{0:T(128)} %convert_reduce_fusion.1.ends_ref, s32[256]{0:T(256)} %get-tuple-element.57.order_ref, s32[256]{0:T(256)} %get-tuple-element.146.row_ref, s32[256]{0:T(256)} %get-tuple-element.145.col_ref, bf16[256,256,128]{2,1,0:T(8,128)(2,1)} %shard_map.96.pairs_ref, ...), custom_call_target="tpu_custom_call" | custom-call | flops 536870912 | bytes 14680064 | tf_op jit(solution)/shard_map/pallas_call | solution.py:213
  163.1 6.5 %shard_map.102 = (f32[32,32,128]{2,1,0:T(8,128)}, f32[32,32,128]{2,1,0:T(8,128)}, f32[32,32,128]{2,1,0:T(8,128)}) custom-call(s32[4]{0:T(128)} %convert_reduce_fusion.1.ends_ref, s32[256]{0:T(256)} %get-tuple-element.57.order_ref, s32[256]{0:T(256)} %get-tuple-element.146.row_ref, s32[256]{0:T(256)} %get-tuple-element.145.col_ref, ...), custom_call_target="tpu_custom_call" | custom-call | flops 268435456 | bytes 7340032 | tf_op jit(solution)/shard_map/pallas_call | solution.py:213
  173.2 6.9 %shard_map.101 = (f32[32,32,128]{2,1,0:T(8,128)}, f32[32,32,128]{2,1,0:T(8,128)}, f32[32,32,128]{2,1,0:T(8,128)}) custom-call(s32[4]{0:T(128)} %convert_reduce_fusion.1.ends_ref, s32[256]{0:T(256)} %get-tuple-element.57.order_ref, s32[256]{0:T(256)} %get-tuple-element.146.row_ref, s32[256]{0:T(256)} %get-tuple-element.145.col_ref, ...), custom_call_target="tpu_custom_call" | custom-call | flops 268435456 | bytes 7340032 | tf_op jit(solution)/shard_map/pallas_call | solution.py:213
  196.6 2.9 collective-permute-start.42
  199.6 5.9 %collective-permute-done.42 = f32[12,32,128]{2,1,0:T(8,128)S(1)} collective-permute-done((f32[12,32,128]{2,1,0:T(8,128)S(1)}, f32[12,32,128]{2,1,0:T(8,128)S(1)}, u32[]{:S(2)}, u32[]{:S(2)}) %collective-permute-start.42) | collective-permute-done | bytes 196640 | tf_op jit(solution)/shard_map/ppermute | solution.py:39
  208.1 4.3 %collective-permute-done.43 = f32[12,32,128]{2,1,0:T(8,128)S(1)} collective-permute-done((f32[12,32,128]{2,1,0:T(8,128)S(1)}, f32[12,32,128]{2,1,0:T(8,128)S(1)}, u32[]{:S(2)}, u32[]{:S(2)}) %collective-permute-start.43) | collective-permute-done | bytes 196640 | tf_op jit(solution)/shard_map/ppermute | solution.py:39
  212.6 2.9 collective-permute-start.47
  215.4 3.5 %collective-permute-done.44 = f32[8,32,128]{2,1,0:T(8,128)S(1)} collective-permute-done((f32[8,32,128]{2,1,0:T(8,128)S(1)}, f32[8,32,128]{2,1,0:T(8,128)S(1)}, u32[]{:S(2)}, u32[]{:S(2)}) %collective-permute-start.44) | collective-permute-done | bytes 131104 | tf_op jit(solution)/shard_map/ppermute | solution.py:39
  221.3 5.6 %collective-permute-done.50 = f32[8,32,128]{2,1,0:T(8,128)S(1)} collective-permute-done((f32[8,32,128]{2,1,0:T(8,128)S(1)}, f32[8,32,128]{2,1,0:T(8,128)S(1)}, u32[]{:S(2)}, u32[]{:S(2)}) %collective-permute-start.50) | collective-permute-done | bytes 131104 | tf_op jit(solution)/shard_map/ppermute | solution.py:39
  230.3 3.8 %collective-permute-done.51 = f32[16,32,128]{2,1,0:T(8,128)S(1)} collective-permute-done((f32[16,32,128]{2,1,0:T(8,128)S(1)}, f32[16,32,128]{2,1,0:T(8,128)S(1)}, u32[]{:S(2)}, u32[]{:S(2)}) %collective-permute-start.51) | collective-permute-done | bytes 262176 | tf_op jit(solution)/shard_map/ppermute | solution.py:39
  234.9 8.7 %shard_map.103 = (f32[96,32,128]{2,1,0:T(8,128)}, f32[96,32,128]{2,1,0:T(8,128)}) custom-call(s32[4]{0:T(128)} %convert_reduce_fusion.1.ends_ref, s32[256]{0:T(256)} %get-tuple-element.57.order_ref, s32[256]{0:T(256)} %get-tuple-element.146.row_ref, s32[256]{0:T(256)} %get-tuple-element.145.col_ref, bf16[256,256,128]{2,1,0:T(8,128)(2,1)} %shard_map.96.pairs_ref, ...), custom_call_target="tpu_custom_call" | custom-call | flops 536870912 | bytes 14680064 | tf_op jit(solution)/shard_map/pallas_call | solution.py:213
  245.6 6.5 %shard_map.105 = (f32[32,32,128]{2,1,0:T(8,128)}, f32[32,32,128]{2,1,0:T(8,128)}, f32[32,32,128]{2,1,0:T(8,128)}) custom-call(s32[4]{0:T(128)} %convert_reduce_fusion.1.ends_ref, s32[256]{0:T(256)} %get-tuple-element.57.order_ref, s32[256]{0:T(256)} %get-tuple-element.146.row_ref, s32[256]{0:T(256)} %get-tuple-element.145.col_ref, ...), custom_call_target="tpu_custom_call" | custom-call | flops 268435456 | bytes 7340032 | tf_op jit(solution)/shard_map/pallas_call | solution.py:213
  254.1 3.2 %collective-permute-start.64 = (f32[12,1,128]{2,1,0:T(1,128)S(1)}, f32[12,1,128]{2,1,0:T(1,128)S(1)}, u32[]{:S(2)}, u32[]{:S(2)}) collective-permute-start(f32[12,1,128]{2,1,0:T(1,128)S(1)} %get-tuple-element.143), channel_id=1, source_target_pairs={{0,16},{8,24},{16,0},{24,8},{1,17},{9,25},{17,1},{25,9},{2,18},{10... | collective-permute-start | bytes 18440 | tf_op jit(solution)/shard_map/ppermute | solution.py:39
  258.0 4.6 %collective-permute-done.64 = f32[12,1,128]{2,1,0:T(1,128)S(1)} collective-permute-done((f32[12,1,128]{2,1,0:T(1,128)S(1)}, f32[12,1,128]{2,1,0:T(1,128)S(1)}, u32[]{:S(2)}, u32[]{:S(2)}) %collective-permute-start.64) | collective-permute-done | bytes 6176 | tf_op jit(solution)/shard_map/ppermute | solution.py:39
  263.3 6.9 %shard_map.104 = (f32[32,32,128]{2,1,0:T(8,128)}, f32[32,32,128]{2,1,0:T(8,128)}, f32[32,32,128]{2,1,0:T(8,128)}) custom-call(s32[4]{0:T(128)} %convert_reduce_fusion.1.ends_ref, s32[256]{0:T(256)} %get-tuple-element.57.order_ref, s32[256]{0:T(256)} %get-tuple-element.146.row_ref, s32[256]{0:T(256)} %get-tuple-element.145.col_ref, ...), custom_call_target="tpu_custom_call" | custom-call | flops 268435456 | bytes 7340032 | tf_op jit(solution)/shard_map/pallas_call | solution.py:213
  289.0 6.7 %collective-permute-done.62 = f32[12,32,128]{2,1,0:T(8,128)S(1)} collective-permute-done((f32[12,32,128]{2,1,0:T(8,128)S(1)}, f32[12,32,128]{2,1,0:T(8,128)S(1)}, u32[]{:S(2)}, u32[]{:S(2)}) %collective-permute-start.62) | collective-permute-done | bytes 196640 | tf_op jit(solution)/shard_map/ppermute | solution.py:39
  297.2 3.5 %all-to-all-start = ((f32[32,1,128]{2,1,0:T(1,128)}), f32[32,1,128]{2,1,0:T(1,128)S(1)}, u32[]{:S(2)}, u32[]{:S(2)}) async-start(f32[32,1,128]{2,1,0:T(1,128)} %broadcast_in_dim.60), calls=%async_computation | async-start | bytes 32768 | tf_op jit(solution)/shard_map/all_to_all | solution.py:330
  301.0 6.7 %all-to-all-done = f32[32,1,128]{2,1,0:T(1,128)S(1)} async-done(((f32[32,1,128]{2,1,0:T(1,128)}), f32[32,1,128]{2,1,0:T(1,128)S(1)}, u32[]{:S(2)}, u32[]{:S(2)}) %all-to-all-start) | async-done | bytes 16416 | tf_op jit(solution)/shard_map/all_to_all | solution.py:330
  (267 shorter events, 113.2 us)
Async XLA Ops:
  4.5 45.1 %collective-permute-start.2 = (f32[128,128,128]{2,1,0:T(8,128)}, f32[128,128,128]{2,1,0:T(8,128)}, u32[]{:S(2)}, u32[]{:S(2)}) collective-permute-start(f32[128,128,128]{2,1,0:T(8,128)} %tile_ref.1), channel_id=1, source_target_pairs={{0,1},{1,0},{2,3},{3,2},{4,5},{5,4},{6,7},{7,6},{8,9},{9,8},{10,11... | collective-permute-start | bytes 25165832 | tf_op jit(solution)/shard_map/ppermute | solution.py:39
  6.3 33.6 %collective-permute-start.1 = (s32[128]{0:T(128)S(1)}, s32[128]{0:T(128)S(1)}, u32[]{:S(2)}, u32[]{:S(2)}) collective-permute-start(s32[128]{0:T(128)S(1)} %fusion.6), channel_id=1, source_target_pairs={{0,1},{1,0},{2,3},{3,2},{4,5},{5,4},{6,7},{7,6},{8,9},{9,8},{10,11... | collective-permute-start | bytes 1544 | tf_op jit(solution)/shard_map/ppermute | solution.py:39
  16.9 13.4 %collective-permute-start.3 = (f32[12,32,128]{2,1,0:T(8,128)S(1)}, f32[12,32,128]{2,1,0:T(8,128)S(1)}, u32[]{:S(2)}, u32[]{:S(2)}) collective-permute-start(f32[12,32,128]{2,1,0:T(8,128)S(1)} %broadcast_multiply_fusion), channel_id=1, source_target_pairs={{0,16},{8,24},{16,0},{24,8},{1,17},{9,25},{17,1},{25,9},{2,18},{10... | collective-permute-start | bytes 589832 | tf_op jit(solution)/shard_map/ppermute | solution.py:39
  43.5 25.1 %collective-permute-start.6 = (f32[32,32,128]{2,1,0:T(8,128)S(1)}, f32[32,32,128]{2,1,0:T(8,128)S(1)}, u32[]{:S(2)}, u32[]{:S(2)}) collective-permute-start(f32[32,32,128]{2,1,0:T(8,128)S(1)} %pad_maximum_fusion.refs_0_), channel_id=1, source_target_pairs={{0,2},{2,0},{1,3},{3,1},{4,6},{6,4},{5,7},{7,5},{8,10},{10,8},{9,1... | collective-permute-start | bytes 1572872 | tf_op jit(solution)/shard_map/ppermute | solution.py:39
  44.2 24.5 %collective-permute-start.9 = (f32[32,32,128]{2,1,0:T(8,128)S(1)}, f32[32,32,128]{2,1,0:T(8,128)S(1)}, u32[]{:S(2)}, u32[]{:S(2)}) collective-permute-start(f32[32,32,128]{2,1,0:T(8,128)S(1)} %pad_maximum_fusion.1.refs_1_), channel_id=1, source_target_pairs={{0,4},{4,0},{1,5},{5,1},{2,6},{6,2},{3,7},{7,3},{8,12},{12,8},{9,1... | collective-permute-start | bytes 1572872 | tf_op jit(solution)/shard_map/ppermute | solution.py:39
  45.9 22.8 %collective-permute-start.12 = (f32[32,32,128]{2,1,0:T(8,128)S(1)}, f32[32,32,128]{2,1,0:T(8,128)S(1)}, u32[]{:S(2)}, u32[]{:S(2)}) collective-permute-start(f32[32,32,128]{2,1,0:T(8,128)S(1)} %pad_maximum_fusion.2.refs_2_), channel_id=1, source_target_pairs={{0,8},{8,0},{16,24},{24,16},{1,9},{9,1},{17,25},{25,17},{2,10},{10... | collective-permute-start | bytes 1572872 | tf_op jit(solution)/shard_map/ppermute | solution.py:39
  76.3 11.7 %collective-permute-start.19 = (f32[32,32,128]{2,1,0:T(8,128)}, f32[32,32,128]{2,1,0:T(8,128)S(1)}, u32[]{:S(2)}, u32[]{:S(2)}) collective-permute-start(f32[32,32,128]{2,1,0:T(8,128)} %get-tuple-element.37), channel_id=1, source_target_pairs={{0,8},{8,0},{16,24},{24,16},{1,9},{9,1},{17,25},{25,17},{2,10},{10... | collective-permute-start | bytes 1572872 | tf_op jit(solution)/shard_map/ppermute | solution.py:39
  78.3 12.8 %collective-permute-start.16 = (f32[32,32,128]{2,1,0:T(8,128)}, f32[32,32,128]{2,1,0:T(8,128)S(1)}, u32[]{:S(2)}, u32[]{:S(2)}) collective-permute-start(f32[32,32,128]{2,1,0:T(8,128)} %get-tuple-element.35), channel_id=1, source_target_pairs={{0,4},{4,0},{1,5},{5,1},{2,6},{6,2},{3,7},{7,3},{8,12},{12,8},{9,1... | collective-permute-start | bytes 1572872 | tf_op jit(solution)/shard_map/ppermute | solution.py:39
  79.1 12.5 %collective-permute-start.13 = (f32[32,32,128]{2,1,0:T(8,128)}, f32[32,32,128]{2,1,0:T(8,128)S(1)}, u32[]{:S(2)}, u32[]{:S(2)}) collective-permute-start(f32[32,32,128]{2,1,0:T(8,128)} %get-tuple-element.33), channel_id=1, source_target_pairs={{0,2},{2,0},{1,3},{3,1},{4,6},{6,4},{5,7},{7,5},{8,10},{10,8},{9,1... | collective-permute-start | bytes 1572872 | tf_op jit(solution)/shard_map/ppermute | solution.py:39
  104.5 13.6 %collective-permute-start.22 = (f32[12,32,128]{2,1,0:T(8,128)S(1)}, f32[12,32,128]{2,1,0:T(8,128)S(1)}, u32[]{:S(2)}, u32[]{:S(2)}) collective-permute-start(f32[12,32,128]{2,1,0:T(8,128)S(1)} %pad_maximum_fusion.19), channel_id=1, source_target_pairs={{0,16},{8,24},{16,0},{24,8},{1,17},{9,25},{17,1},{25,9},{2,18},{10... | collective-permute-start | bytes 589832 | tf_op jit(solution)/shard_map/ppermute | solution.py:39
  118.2 8.7 %collective-permute-start.23 = (f32[12,32,128]{2,1,0:T(8,128)S(1)}, f32[12,32,128]{2,1,0:T(8,128)S(1)}, u32[]{:S(2)}, u32[]{:S(2)}) collective-permute-start(f32[12,32,128]{2,1,0:T(8,128)S(1)} %fusion.1), channel_id=1, source_target_pairs={{0,16},{8,24},{16,0},{24,8},{1,17},{9,25},{17,1},{25,9},{2,18},{10... | collective-permute-start | bytes 589832 | tf_op jit(solution)/shard_map/ppermute | solution.py:39
  132.0 12.7 %collective-permute-start.25 = (f32[16,32,128]{2,1,0:T(8,128)S(1)}, f32[16,32,128]{2,1,0:T(8,128)S(1)}, u32[]{:S(2)}, u32[]{:S(2)}) collective-permute-start(f32[16,32,128]{2,1,0:T(8,128)S(1)} %pad_maximum_fusion.12), channel_id=1, source_target_pairs={{0,4},{4,0},{1,5},{5,1},{2,6},{6,2},{3,7},{7,3},{8,12},{12,8},{9,1... | collective-permute-start | bytes 786440 | tf_op jit(solution)/shard_map/ppermute | solution.py:39
  132.3 11.7 %collective-permute-start.30 = (f32[8,32,128]{2,1,0:T(8,128)S(1)}, f32[8,32,128]{2,1,0:T(8,128)S(1)}, u32[]{:S(2)}, u32[]{:S(2)}) collective-permute-start(f32[8,32,128]{2,1,0:T(8,128)S(1)} %pad_maximum_fusion.29), channel_id=1, source_target_pairs={{0,4},{4,0},{1,5},{5,1},{2,6},{6,2},{3,7},{7,3},{8,12},{12,8},{9,1... | collective-permute-start | bytes 393224 | tf_op jit(solution)/shard_map/ppermute | solution.py:39
  134.2 12.0 %collective-permute-start.28 = (f32[16,32,128]{2,1,0:T(8,128)S(1)}, f32[16,32,128]{2,1,0:T(8,128)S(1)}, u32[]{:S(2)}, u32[]{:S(2)}) collective-permute-start(f32[16,32,128]{2,1,0:T(8,128)S(1)} %pad_maximum_fusion.13), channel_id=1, source_target_pairs={{0,8},{8,0},{16,24},{24,16},{1,9},{9,1},{17,25},{25,17},{2,10},{10... | collective-permute-start | bytes 786440 | tf_op jit(solution)/shard_map/ppermute | solution.py:39
  144.7 15.9 %collective-permute-start.26 = (f32[32,32,128]{2,1,0:T(8,128)S(1)}, f32[32,32,128]{2,1,0:T(8,128)S(1)}, u32[]{:S(2)}, u32[]{:S(2)}) collective-permute-start(f32[32,32,128]{2,1,0:T(8,128)S(1)} %pad_maximum_fusion.3.refs_0_), channel_id=1, source_target_pairs={{0,2},{2,0},{1,3},{3,1},{4,6},{6,4},{5,7},{7,5},{8,10},{10,8},{9,1... | collective-permute-start | bytes 1572872 | tf_op jit(solution)/shard_map/ppermute | solution.py:39
  146.3 14.4 %collective-permute-start.29 = (f32[32,32,128]{2,1,0:T(8,128)S(1)}, f32[32,32,128]{2,1,0:T(8,128)S(1)}, u32[]{:S(2)}, u32[]{:S(2)}) collective-permute-start(f32[32,32,128]{2,1,0:T(8,128)S(1)} %pad_maximum_fusion.4.refs_1_), channel_id=1, source_target_pairs={{0,4},{4,0},{1,5},{5,1},{2,6},{6,2},{3,7},{7,3},{8,12},{12,8},{9,1... | collective-permute-start | bytes 1572872 | tf_op jit(solution)/shard_map/ppermute | solution.py:39
  150.5 11.7 %collective-permute-start.32 = (f32[32,32,128]{2,1,0:T(8,128)S(1)}, f32[32,32,128]{2,1,0:T(8,128)S(1)}, u32[]{:S(2)}, u32[]{:S(2)}) collective-permute-start(f32[32,32,128]{2,1,0:T(8,128)S(1)} %pad_maximum_fusion.5.refs_2_), channel_id=1, source_target_pairs={{0,8},{8,0},{16,24},{24,16},{1,9},{9,1},{17,25},{25,17},{2,10},{10... | collective-permute-start | bytes 1572872 | tf_op jit(solution)/shard_map/ppermute | solution.py:39
  169.6 10.9 %collective-permute-start.39 = (f32[32,32,128]{2,1,0:T(8,128)}, f32[32,32,128]{2,1,0:T(8,128)S(1)}, u32[]{:S(2)}, u32[]{:S(2)}) collective-permute-start(f32[32,32,128]{2,1,0:T(8,128)} %get-tuple-element.45), channel_id=1, source_target_pairs={{0,8},{8,0},{16,24},{24,16},{1,9},{9,1},{17,25},{25,17},{2,10},{10... | collective-permute-start | bytes 1572872 | tf_op jit(solution)/shard_map/ppermute | solution.py:39
  171.2 11.6 %collective-permute-start.36 = (f32[32,32,128]{2,1,0:T(8,128)}, f32[32,32,128]{2,1,0:T(8,128)S(1)}, u32[]{:S(2)}, u32[]{:S(2)}) collective-permute-start(f32[32,32,128]{2,1,0:T(8,128)} %get-tuple-element.43), channel_id=1, source_target_pairs={{0,4},{4,0},{1,5},{5,1},{2,6},{6,2},{3,7},{7,3},{8,12},{12,8},{9,1... | collective-permute-start | bytes 1572872 | tf_op jit(solution)/shard_map/ppermute | solution.py:39
  172.2 12.7 %collective-permute-start.33 = (f32[32,32,128]{2,1,0:T(8,128)}, f32[32,32,128]{2,1,0:T(8,128)S(1)}, u32[]{:S(2)}, u32[]{:S(2)}) collective-permute-start(f32[32,32,128]{2,1,0:T(8,128)} %get-tuple-element.41), channel_id=1, source_target_pairs={{0,2},{2,0},{1,3},{3,1},{4,6},{6,4},{5,7},{7,5},{8,10},{10,8},{9,1... | collective-permute-start | bytes 1572872 | tf_op jit(solution)/shard_map/ppermute | solution.py:39
  196.6 8.8 %collective-permute-start.42 = (f32[12,32,128]{2,1,0:T(8,128)S(1)}, f32[12,32,128]{2,1,0:T(8,128)S(1)}, u32[]{:S(2)}, u32[]{:S(2)}) collective-permute-start(f32[12,32,128]{2,1,0:T(8,128)S(1)} %pad_maximum_fusion.20), channel_id=1, source_target_pairs={{0,16},{8,24},{16,0},{24,8},{1,17},{9,25},{17,1},{25,9},{2,18},{10... | collective-permute-start | bytes 589832 | tf_op jit(solution)/shard_map/ppermute | solution.py:39
  219.0 10.7 %collective-permute-start.45 = (f32[16,32,128]{2,1,0:T(8,128)S(1)}, f32[16,32,128]{2,1,0:T(8,128)S(1)}, u32[]{:S(2)}, u32[]{:S(2)}) collective-permute-start(f32[16,32,128]{2,1,0:T(8,128)S(1)} %pad_maximum_fusion.15), channel_id=1, source_target_pairs={{0,4},{4,0},{1,5},{5,1},{2,6},{6,2},{3,7},{7,3},{8,12},{12,8},{9,1... | collective-permute-start | bytes 786440 | tf_op jit(solution)/shard_map/ppermute | solution.py:39
  221.2 8.7 %collective-permute-start.48 = (f32[16,32,128]{2,1,0:T(8,128)S(1)}, f32[16,32,128]{2,1,0:T(8,128)S(1)}, u32[]{:S(2)}, u32[]{:S(2)}) collective-permute-start(f32[16,32,128]{2,1,0:T(8,128)S(1)} %pad_maximum_fusion.16), channel_id=1, source_target_pairs={{0,8},{8,0},{16,24},{24,16},{1,9},{9,1},{17,25},{25,17},{2,10},{10... | collective-permute-start | bytes 786440 | tf_op jit(solution)/shard_map/ppermute | solution.py:39
  229.8 13.9 %collective-permute-start.46 = (f32[32,32,128]{2,1,0:T(8,128)S(1)}, f32[32,32,128]{2,1,0:T(8,128)S(1)}, u32[]{:S(2)}, u32[]{:S(2)}) collective-permute-start(f32[32,32,128]{2,1,0:T(8,128)S(1)} %pad_maximum_fusion.6.refs_0_), channel_id=1, source_target_pairs={{0,2},{2,0},{1,3},{3,1},{4,6},{6,4},{5,7},{7,5},{8,10},{10,8},{9,1... | collective-permute-start | bytes 1572872 | tf_op jit(solution)/shard_map/ppermute | solution.py:39
  229.9 14.7 %collective-permute-start.49 = (f32[32,32,128]{2,1,0:T(8,128)S(1)}, f32[32,32,128]{2,1,0:T(8,128)S(1)}, u32[]{:S(2)}, u32[]{:S(2)}) collective-permute-start(f32[32,32,128]{2,1,0:T(8,128)S(1)} %pad_maximum_fusion.7.refs_1_), channel_id=1, source_target_pairs={{0,4},{4,0},{1,5},{5,1},{2,6},{6,2},{3,7},{7,3},{8,12},{12,8},{9,1... | collective-permute-start | bytes 1572872 | tf_op jit(solution)/shard_map/ppermute | solution.py:39
  234.1 10.5 %collective-permute-start.52 = (f32[32,32,128]{2,1,0:T(8,128)S(1)}, f32[32,32,128]{2,1,0:T(8,128)S(1)}, u32[]{:S(2)}, u32[]{:S(2)}) collective-permute-start(f32[32,32,128]{2,1,0:T(8,128)S(1)} %pad_maximum_fusion.8.refs_2_), channel_id=1, source_target_pairs={{0,8},{8,0},{16,24},{24,16},{1,9},{9,1},{17,25},{25,17},{2,10},{10... | collective-permute-start | bytes 1572872 | tf_op jit(solution)/shard_map/ppermute | solution.py:39
  252.1 18.0 %collective-permute-start.59 = (f32[32,32,128]{2,1,0:T(8,128)}, f32[32,32,128]{2,1,0:T(8,128)S(1)}, u32[]{:S(2)}, u32[]{:S(2)}) collective-permute-start(f32[32,32,128]{2,1,0:T(8,128)} %get-tuple-element.53), channel_id=1, source_target_pairs={{0,8},{8,0},{16,24},{24,16},{1,9},{9,1},{17,25},{25,17},{2,10},{10... | collective-permute-start | bytes 1572872 | tf_op jit(solution)/shard_map/ppermute | solution.py:39
  254.1 18.9 %collective-permute-start.56 = (f32[32,32,128]{2,1,0:T(8,128)}, f32[32,32,128]{2,1,0:T(8,128)S(1)}, u32[]{:S(2)}, u32[]{:S(2)}) collective-permute-start(f32[32,32,128]{2,1,0:T(8,128)} %get-tuple-element.51), channel_id=1, source_target_pairs={{0,4},{4,0},{1,5},{5,1},{2,6},{6,2},{3,7},{7,3},{8,12},{12,8},{9,1... | collective-permute-start | bytes 1572872 | tf_op jit(solution)/shard_map/ppermute | solution.py:39
  262.6 12.7 %collective-permute-start.53 = (f32[32,32,128]{2,1,0:T(8,128)}, f32[32,32,128]{2,1,0:T(8,128)S(1)}, u32[]{:S(2)}, u32[]{:S(2)}) collective-permute-start(f32[32,32,128]{2,1,0:T(8,128)} %get-tuple-element.49), channel_id=1, source_target_pairs={{0,2},{2,0},{1,3},{3,1},{4,6},{6,4},{5,7},{7,5},{8,10},{10,8},{9,1... | collective-permute-start | bytes 1572872 | tf_op jit(solution)/shard_map/ppermute | solution.py:39
  287.0 8.7 %collective-permute-start.62 = (f32[12,32,128]{2,1,0:T(8,128)S(1)}, f32[12,32,128]{2,1,0:T(8,128)S(1)}, u32[]{:S(2)}, u32[]{:S(2)}) collective-permute-start(f32[12,32,128]{2,1,0:T(8,128)S(1)} %get-tuple-element.120), channel_id=1, source_target_pairs={{0,16},{8,24},{16,0},{24,8},{1,17},{9,25},{17,1},{25,9},{2,18},{10... | collective-permute-start | bytes 589832 | tf_op jit(solution)/shard_map/ppermute | solution.py:39
  297.2 10.6 %all-to-all-start = ((f32[32,1,128]{2,1,0:T(1,128)}), f32[32,1,128]{2,1,0:T(1,128)S(1)}, u32[]{:S(2)}, u32[]{:S(2)}) async-start(f32[32,1,128]{2,1,0:T(1,128)} %broadcast_in_dim.60), calls=%async_computation | async-start | bytes 32768 | tf_op jit(solution)/shard_map/all_to_all | solution.py:330
  300.7 9.0 %collective-permute-start.63 = (f32[6,32,128]{2,1,0:T(8,128)S(1)}, f32[6,32,128]{2,1,0:T(8,128)S(1)}, u32[]{:S(2)}, u32[]{:S(2)}) collective-permute-start(f32[6,32,128]{2,1,0:T(8,128)S(1)} %slice_select_fusion), channel_id=1, source_target_pairs={{0,1},{1,0},{2,3},{3,2},{4,5},{5,4},{6,7},{7,6},{8,9},{9,8},{10,11... | collective-permute-start | bytes 294920 | tf_op jit(solution)/shard_map/ppermute | solution.py:39
  (62 other events, 360.6 us)

commit v8 on v7

--- a/solution.py
+++ b/solution.py
@@ -14,7 +14,7 @@
 UNROLL = 8
 CHUNK = 8
 SLOTS = 8
-VMEM = 60 * 1024 * 1024
+VMEM = 16 * 1024 * 1024
 CHIPS = ("z", "y", "x")
 ALL = ("z", "y", "x", "core")
 NEAR = ("x", "y", "z")
@@ -53,16 +53,18 @@
     for step in reversed(far_steps()):
         got = swap(blocks[0] if len(blocks) == 1 else jnp.concatenate(blocks, axis=0), step)
         if beside is not None:
-            got, beside = after(got, beside), None
+            got, beside = after(got, *beside), None
         blocks = blocks + jnp.split(got, len(blocks))
     return blocks
 
 
 def gather(flux, edges, beside=None):
     blocks = gather_far(flux, beside)
+    starts = [
+        jnp.concatenate([b[low:high] for b in blocks], axis=0) for low, high in zip(edges[:-1], edges[1:])
+    ]
     pieces = []
-    for part in range(len(NEAR)):
-        block = jnp.concatenate([b[edges[part] : edges[part + 1]] for b in blocks], axis=0)
+    for part, block in enumerate(lax.optimization_barrier(starts)):
         steps = near_steps(part)
         for step in reversed(steps[1:]):
             block = jnp.concatenate([block, swap(block, step)], axis=0)
@@ -115,7 +117,7 @@
         out_shape=jax.ShapeDtypeStruct((CORES * length, 2 * size, size), jnp.bfloat16),
         grid=(steps,),
         in_specs=[pl.BlockSpec((STEP, size, size), lambda i: (i, 0, 0))]
-        + [pl.BlockSpec(memory_space=pl.ANY)] * len(given),
+        + [pl.BlockSpec(memory_space=pltpu.HBM)] * len(given),
         out_specs=pl.BlockSpec((STEP, 2 * size, size), lambda i: (place * steps + i, 0, 0)),
         input_output_aliases={1: 0} if given else {},
         compiler_params=pltpu.CompilerParams(vmem_limit_bytes=VMEM),
@@ -208,7 +210,7 @@
     total, _, size = pairs.shape
     counts = [piece.shape[0] for piece in flux]
     temps = flux[0].shape[1]
-    anywhere = pl.BlockSpec(memory_space=pl.ANY)
+    anywhere = pl.BlockSpec(memory_space=pltpu.HBM)
     given = [pairs, *flux] + ([] if base is None else [base])
     return pl.pallas_call(
         functools.partial(apply_kernel, span, skip, counts, base is not None),
@@ -306,10 +308,10 @@
     relax_both = by_core(relax, got[:, half : half + 1])
     heat_both = by_core(heat, got[:, half + 8 : half + 9])
 
-    pairs = split_tiles(tile_values, 0)
-    beside = pairs
+    flux = relax_both * drive_half
+    pairs = split_tiles(after(tile_values, flux), 0)
     heats = gather_far(heat_both * relax_both)
-    flux = relax_both * drive_half
+    beside = (pairs, *heats)
     sizes = [chips // 2 * (high - low) for low, high in zip(edges[:-1], edges[1:])]
     for sweep in range(ITERS):
         pieces = gather(flux, edges, beside)
@@ -332,7 +334,10 @@
             )
             totals = jnp.sum(totals.reshape(chips, CORES, size), axis=0)
             conductivity = totals[:, :half].reshape(columns) / jnp.sum(totals[:, half])
-        flux = relax_both * (drive_half + reduce_far(blocks))
+        summed = reduce_far(blocks)
+        if sweep == ITERS - 1:
+            summed = after(summed, conductivity)
+        flux = relax_both * (drive_half + summed)
     first, second = flux[:per], flux[per:]
     mine = jnp.where(core == 0, first, second)
     got = swap(jnp.where(core == 0, second, first), cores)

time: 312 us -> 311 us (level)
  Pallas kernels: 86.8 us -> 104 us
  starting transfers between devices: 86.6 us -> 71.2 us
  blocking collectives: 0 us -> 10.7 us
  waiting for transfers between devices: 116 us -> 108 us
  other arithmetic: 11.9 us -> 8.08 us
    pallas_call x9, Pallas kernels: 66.3 us -> 92.9 us  [apply_tiles(): pl.pallas_call(functools.partial(apply_kernel, span, skip, counts, base i...]
    ppermute x65, starting transfers between devices: 83.1 us -> 71.2 us  [swap(): return lax.ppermute(array, axis, pairs)]
    all_to_all x0 -> x1, blocking collectives: none -> 10.7 us  [shards(): lax.all_to_all(jnp.broadcast_to(totals, (chips * CORES, size)), ALL, spli...]
    pallas_call x2, Pallas kernels: 20.5 us -> 10.6 us  [split_tiles(): pl.pallas_call(split_kernel, out_shape=jax.ShapeDtypeStruct((CORES * leng...]
    all_to_all x1 -> x0, waiting for transfers between devices: 6.73 us -> none  [shards(): lax.all_to_all(jnp.broadcast_to(totals, (chips * CORES, size)), ALL, spli...]
    all_to_all x1 -> x0, starting transfers between devices: 3.5 us -> none  [shards(): lax.all_to_all(jnp.broadcast_to(totals, (chips * CORES, size)), ALL, spli...]
    add x18, other arithmetic: 4.34 us -> 1.05 us  [reduce_near(): keep, send = [k + g for k, g in zip(halves(keep), halves(got))]]
  transfers between devices with their start and end apart: 66 -> 65, of which waited for: 39 -> 34; matrix products, arithmetic and copies ran while one was open for 3% -> 2% of each run, Pallas kernels for 22% -> 26%
where the time goes in v8:
time: 311 us; the launch traced here: 310 us
  waiting for transfers between devices  108 us (35%)
  Pallas kernels  104 us (33%)
  starting transfers between devices  71.2 us (23%)
  blocking collectives  10.7 us (3%)
  other arithmetic  8.08 us (3%)
  local copies, waits for them, and re-layouts  6.76 us (2%)
    ppermute x65, waiting for transfers between devices, swap(): return lax.ppermute(array, axis, pairs)  108 us
    pallas_call x9, Pallas kernels, apply_tiles(): pl.pallas_call(functools.partial(apply_kernel, span, skip, counts, base i...  92.9 us
    ppermute x65, starting transfers between devices, swap(): return lax.ppermute(array, axis, pairs)  71.2 us
    all_to_all x1, blocking collectives, shards(): lax.all_to_all(jnp.broadcast_to(totals, (chips * CORES, size)), ALL, spli...  10.7 us
    pallas_call x2, Pallas kernels, split_tiles(): pl.pallas_call(split_kernel, out_shape=jax.ShapeDtypeStruct((CORES * leng...  10.6 us
  transfers between devices with their start and end apart: 65, of which 34 were waited for; matrix products, arithmetic and copies ran while one was open for 2% of the time, Pallas kernels for 26%

profile of v8, /device:TPU:0, one launch (start us, length us, event | category | flops | bytes accessed | tf_op | source)
XLA Modules:
  0.0 310.1 jit_solution(18282948853671588125)
XLA Ops:
  6.5 11.2 %collective-permute-done.1 = s32[128]{0:T(128)S(1)} collective-permute-done((s32[128]{0:T(128)S(1)}, s32[128]{0:T(128)S(1)}, u32[]{:S(2)}, u32[]{:S(2)}) %collective-permute-start.1) | collective-permute-done | bytes 544 | tf_op jit(solution)/shard_map/ppermute | solution.py:39
  19.2 4.0 %collective-permute-start.3 = (f32[12,32,128]{2,1,0:T(8,128)S(1)}, f32[12,32,128]{2,1,0:T(8,128)S(1)}, u32[]{:S(2)}, u32[]{:S(2)}) collective-permute-start(f32[12,32,128]{2,1,0:T(8,128)S(1)} %broadcast_multiply_fusion), channel_id=1, source_target_pairs={{0,16},{8,24},{16,0},{24,8},{1,17},{9,25},{17,1},{25,9},{2,18},{10... | collective-permute-start | bytes 589832 | tf_op jit(solution)/shard_map/ppermute | solution.py:39
  23.3 3.4 %copy-done.2 = f32[128,128,128]{2,1,0:T(8,128)S(1)} copy-done((f32[128,128,128]{2,1,0:T(8,128)S(1)}, f32[128,128,128]{2,1,0:T(8,128)}, u32[]{:S(2)}) %copy-start.2) | copy-done | bytes 8388632
  26.6 3.4 %shard_map.95.refs_0_ = bf16[256,256,128]{2,1,0:T(8,128)(2,1)S(1)} custom-call(f32[128,128,128]{2,1,0:T(8,128)S(1)} %copy-done.2), custom_call_target="tpu_custom_call" | custom-call | flops 6291456 | bytes 16777216 | tf_op jit(solution)/shard_map/pallas_call | solution.py:115
  42.6 3.5 %collective-permute-done.6 = f32[16,32,128]{2,1,0:T(8,128)S(1)} collective-permute-done((f32[16,32,128]{2,1,0:T(8,128)S(1)}, f32[16,32,128]{2,1,0:T(8,128)S(1)}, u32[]{:S(2)}, u32[]{:S(2)}) %collective-permute-start.6) | collective-permute-done | bytes 262176 | tf_op jit(solution)/shard_map/ppermute | solution.py:39
  50.5 7.3 %shard_map.96.pairs_ref = bf16[256,256,128]{2,1,0:T(8,128)(2,1)S(1)} custom-call(f32[128,128,128]{2,1,0:T(8,128)} %collective-permute-done.2.tile_ref, bf16[256,256,128]{2,1,0:T(8,128)(2,1)S(1)} %shard_map.95.refs_0_), custom_call_target="tpu_custom_call", output_to_operand_aliasing={{}: (1, {})} | custom-call | flops 6291456 | bytes 16777216 | tf_op jit(solution)/shard_map/pallas_call | solution.py:115
  57.8 14.6 %shard_map.97 = (f32[96,32,128]{2,1,0:T(8,128)S(1)}, f32[96,32,128]{2,1,0:T(8,128)S(1)}) custom-call(s32[4]{0:T(128)S(1)} %convert_reduce_fusion.1.ends_ref, s32[256]{0:T(256)S(1)} %get-tuple-element.79.order_ref, s32[256]{0:T(256)S(1)} %get-tuple-element.171.row_ref, s32[256]{0:T(256)S(1)} %get-tuple-element.170.col_ref, ...), custom_call_target="tpu_custom_call" | custom-call | flops 536870912 | bytes 14680064 | tf_op jit(solution)/shard_map/pallas_call | solution.py:215
  72.4 7.7 %shard_map.99 = (f32[32,32,128]{2,1,0:T(8,128)S(1)}, f32[32,32,128]{2,1,0:T(8,128)S(1)}, f32[32,32,128]{2,1,0:T(8,128)S(1)}) custom-call(s32[4]{0:T(128)S(1)} %convert_reduce_fusion.1.ends_ref, s32[256]{0:T(256)S(1)} %get-tuple-element.79.order_ref, s32[256]{0:T(256)S(1)} %get-tuple-element.171.row_ref, s32[256]{0:T(256)S(1)} %get-tuple-element.170.col_ref, ...), custom_call_target="tpu_custom_call" | custom-call | flops 268435456 | bytes 7340032 | tf_op jit(solution)/shard_map/pallas_call | solution.py:215
  80.1 3.4 %collective-permute-start.20 = (f32[32,32,128]{2,1,0:T(8,128)S(1)}, f32[32,32,128]{2,1,0:T(8,128)S(1)}, u32[]{:S(2)}, u32[]{:S(2)}) collective-permute-start(f32[32,32,128]{2,1,0:T(8,128)S(1)} %get-tuple-element.52), channel_id=1, source_target_pairs={{0,8},{8,0},{16,24},{24,16},{1,9},{9,1},{17,25},{25,17},{2,10},{10... | collective-permute-start | bytes 1572872 | tf_op jit(solution)/shard_map/ppermute | solution.py:39
  85.1 8.7 %shard_map.98 = (f32[32,32,128]{2,1,0:T(8,128)S(1)}, f32[32,32,128]{2,1,0:T(8,128)S(1)}, f32[32,32,128]{2,1,0:T(8,128)S(1)}) custom-call(s32[4]{0:T(128)S(1)} %convert_reduce_fusion.1.ends_ref, s32[256]{0:T(256)S(1)} %get-tuple-element.79.order_ref, s32[256]{0:T(256)S(1)} %get-tuple-element.171.row_ref, s32[256]{0:T(256)S(1)} %get-tuple-element.170.col_ref, ...), custom_call_target="tpu_custom_call" | custom-call | flops 268435456 | bytes 7340032 | tf_op jit(solution)/shard_map/pallas_call | solution.py:215
  96.0 3.2 %collective-permute-start.15 = (f32[16,32,128]{2,1,0:T(8,128)S(1)}, f32[16,32,128]{2,1,0:T(8,128)S(1)}, u32[]{:S(2)}, u32[]{:S(2)}) collective-permute-start(f32[16,32,128]{2,1,0:T(8,128)S(1)} %get-tuple-element.95), channel_id=1, source_target_pairs={{0,4},{4,0},{1,5},{5,1},{2,6},{6,2},{3,7},{7,3},{8,12},{12,8},{9,1... | collective-permute-start | bytes 786440 | tf_op jit(solution)/shard_map/ppermute | solution.py:39
  107.1 3.0 collective-permute-done.16
  110.1 4.2 %collective-permute-start.23 = (f32[12,32,128]{2,1,0:T(8,128)S(1)}, f32[12,32,128]{2,1,0:T(8,128)S(1)}, u32[]{:S(2)}, u32[]{:S(2)}) collective-permute-start(f32[12,32,128]{2,1,0:T(8,128)S(1)} %pad_maximum_fusion.10), channel_id=1, source_target_pairs={{0,16},{8,24},{16,0},{24,8},{1,17},{9,25},{17,1},{25,9},{2,18},{10... | collective-permute-start | bytes 589832 | tf_op jit(solution)/shard_map/ppermute | solution.py:39
  114.3 9.7 %collective-permute-done.23 = f32[12,32,128]{2,1,0:T(8,128)S(1)} collective-permute-done((f32[12,32,128]{2,1,0:T(8,128)S(1)}, f32[12,32,128]{2,1,0:T(8,128)S(1)}, u32[]{:S(2)}, u32[]{:S(2)}) %collective-permute-start.23) | collective-permute-done | bytes 196640 | tf_op jit(solution)/shard_map/ppermute | solution.py:39
  124.1 8.4 %collective-permute-done.24 = f32[12,32,128]{2,1,0:T(8,128)S(1)} collective-permute-done((f32[12,32,128]{2,1,0:T(8,128)S(1)}, f32[12,32,128]{2,1,0:T(8,128)S(1)}, u32[]{:S(2)}, u32[]{:S(2)}) %collective-permute-start.24) | collective-permute-done | bytes 196640 | tf_op jit(solution)/shard_map/ppermute | solution.py:39
  134.2 3.5 %collective-permute-done.25 = f32[8,32,128]{2,1,0:T(8,128)S(1)} collective-permute-done((f32[8,32,128]{2,1,0:T(8,128)S(1)}, f32[8,32,128]{2,1,0:T(8,128)S(1)}, u32[]{:S(2)}, u32[]{:S(2)}) %collective-permute-start.25) | collective-permute-done | bytes 131104 | tf_op jit(solution)/shard_map/ppermute | solution.py:39
  141.5 5.2 %collective-permute-done.26 = f32[16,32,128]{2,1,0:T(8,128)S(1)} collective-permute-done((f32[16,32,128]{2,1,0:T(8,128)S(1)}, f32[16,32,128]{2,1,0:T(8,128)S(1)}, u32[]{:S(2)}, u32[]{:S(2)}) %collective-permute-start.26) | collective-permute-done | bytes 262176 | tf_op jit(solution)/shard_map/ppermute | solution.py:39
  149.2 14.6 %shard_map.100 = (f32[96,32,128]{2,1,0:T(8,128)S(1)}, f32[96,32,128]{2,1,0:T(8,128)S(1)}) custom-call(s32[4]{0:T(128)S(1)} %convert_reduce_fusion.1.ends_ref, s32[256]{0:T(256)S(1)} %get-tuple-element.79.order_ref, s32[256]{0:T(256)S(1)} %get-tuple-element.171.row_ref, s32[256]{0:T(256)S(1)} %get-tuple-element.170.col_ref, ...), custom_call_target="tpu_custom_call" | custom-call | flops 536870912 | bytes 14680064 | tf_op jit(solution)/shard_map/pallas_call | solution.py:215
  163.8 7.7 %shard_map.102 = (f32[32,32,128]{2,1,0:T(8,128)S(1)}, f32[32,32,128]{2,1,0:T(8,128)S(1)}, f32[32,32,128]{2,1,0:T(8,128)S(1)}) custom-call(s32[4]{0:T(128)S(1)} %convert_reduce_fusion.1.ends_ref, s32[256]{0:T(256)S(1)} %get-tuple-element.79.order_ref, s32[256]{0:T(256)S(1)} %get-tuple-element.171.row_ref, s32[256]{0:T(256)S(1)} %get-tuple-element.170.col_ref, ...), custom_call_target="tpu_custom_call" | custom-call | flops 268435456 | bytes 7340032 | tf_op jit(solution)/shard_map/pallas_call | solution.py:215
  171.5 4.4 %collective-permute-start.40 = (f32[32,32,128]{2,1,0:T(8,128)S(1)}, f32[32,32,128]{2,1,0:T(8,128)S(1)}, u32[]{:S(2)}, u32[]{:S(2)}) collective-permute-start(f32[32,32,128]{2,1,0:T(8,128)S(1)} %get-tuple-element.63), channel_id=1, source_target_pairs={{0,8},{8,0},{16,24},{24,16},{1,9},{9,1},{17,25},{25,17},{2,10},{10... | collective-permute-start | bytes 1572872 | tf_op jit(solution)/shard_map/ppermute | solution.py:39
  176.3 8.8 %shard_map.101 = (f32[32,32,128]{2,1,0:T(8,128)S(1)}, f32[32,32,128]{2,1,0:T(8,128)S(1)}, f32[32,32,128]{2,1,0:T(8,128)S(1)}) custom-call(s32[4]{0:T(128)S(1)} %convert_reduce_fusion.1.ends_ref, s32[256]{0:T(256)S(1)} %get-tuple-element.79.order_ref, s32[256]{0:T(256)S(1)} %get-tuple-element.171.row_ref, s32[256]{0:T(256)S(1)} %get-tuple-element.170.col_ref, ...), custom_call_target="tpu_custom_call" | custom-call | flops 268435456 | bytes 7340032 | tf_op jit(solution)/shard_map/pallas_call | solution.py:215
  204.2 7.8 %collective-permute-done.43 = f32[12,32,128]{2,1,0:T(8,128)S(1)} collective-permute-done((f32[12,32,128]{2,1,0:T(8,128)S(1)}, f32[12,32,128]{2,1,0:T(8,128)S(1)}, u32[]{:S(2)}, u32[]{:S(2)}) %collective-permute-start.43) | collective-permute-done | bytes 196640 | tf_op jit(solution)/shard_map/ppermute | solution.py:39
  212.1 7.7 %collective-permute-done.44 = f32[12,32,128]{2,1,0:T(8,128)S(1)} collective-permute-done((f32[12,32,128]{2,1,0:T(8,128)S(1)}, f32[12,32,128]{2,1,0:T(8,128)S(1)}, u32[]{:S(2)}, u32[]{:S(2)}) %collective-permute-start.44) | collective-permute-done | bytes 196640 | tf_op jit(solution)/shard_map/ppermute | solution.py:39
  221.0 5.2 %collective-permute-done.45 = f32[8,32,128]{2,1,0:T(8,128)S(1)} collective-permute-done((f32[8,32,128]{2,1,0:T(8,128)S(1)}, f32[8,32,128]{2,1,0:T(8,128)S(1)}, u32[]{:S(2)}, u32[]{:S(2)}) %collective-permute-start.45) | collective-permute-done | bytes 131104 | tf_op jit(solution)/shard_map/ppermute | solution.py:39
  227.7 5.0 %collective-permute-done.46 = f32[16,32,128]{2,1,0:T(8,128)S(1)} collective-permute-done((f32[16,32,128]{2,1,0:T(8,128)S(1)}, f32[16,32,128]{2,1,0:T(8,128)S(1)}, u32[]{:S(2)}, u32[]{:S(2)}) %collective-permute-start.46) | collective-permute-done | bytes 262176 | tf_op jit(solution)/shard_map/ppermute | solution.py:39
  235.1 14.6 %shard_map.103 = (f32[96,32,128]{2,1,0:T(8,128)S(1)}, f32[96,32,128]{2,1,0:T(8,128)S(1)}) custom-call(s32[4]{0:T(128)S(1)} %convert_reduce_fusion.1.ends_ref, s32[256]{0:T(256)S(1)} %get-tuple-element.79.order_ref, s32[256]{0:T(256)S(1)} %get-tuple-element.171.row_ref, s32[256]{0:T(256)S(1)} %get-tuple-element.170.col_ref, ...), custom_call_target="tpu_custom_call" | custom-call | flops 536870912 | bytes 14680064 | tf_op jit(solution)/shard_map/pallas_call | solution.py:215
  249.7 7.7 %shard_map.105 = (f32[32,32,128]{2,1,0:T(8,128)S(1)}, f32[32,32,128]{2,1,0:T(8,128)S(1)}, f32[32,32,128]{2,1,0:T(8,128)S(1)}) custom-call(s32[4]{0:T(128)S(1)} %convert_reduce_fusion.1.ends_ref, s32[256]{0:T(256)S(1)} %get-tuple-element.79.order_ref, s32[256]{0:T(256)S(1)} %get-tuple-element.171.row_ref, s32[256]{0:T(256)S(1)} %get-tuple-element.170.col_ref, ...), custom_call_target="tpu_custom_call" | custom-call | flops 268435456 | bytes 7340032 | tf_op jit(solution)/shard_map/pallas_call | solution.py:215
  257.4 4.8 %collective-permute-start.60 = (f32[32,32,128]{2,1,0:T(8,128)S(1)}, f32[32,32,128]{2,1,0:T(8,128)S(1)}, u32[]{:S(2)}, u32[]{:S(2)}) collective-permute-start(f32[32,32,128]{2,1,0:T(8,128)S(1)} %get-tuple-element.74), channel_id=1, source_target_pairs={{0,8},{8,0},{16,24},{24,16},{1,9},{9,1},{17,25},{25,17},{2,10},{10... | collective-permute-start | bytes 1572872 | tf_op jit(solution)/shard_map/ppermute | solution.py:39
  262.2 8.7 %shard_map.104 = (f32[32,32,128]{2,1,0:T(8,128)S(1)}, f32[32,32,128]{2,1,0:T(8,128)S(1)}, f32[32,32,128]{2,1,0:T(8,128)S(1)}) custom-call(s32[4]{0:T(128)S(1)} %convert_reduce_fusion.1.ends_ref, s32[256]{0:T(256)S(1)} %get-tuple-element.79.order_ref, s32[256]{0:T(256)S(1)} %get-tuple-element.171.row_ref, s32[256]{0:T(256)S(1)} %get-tuple-element.170.col_ref, ...), custom_call_target="tpu_custom_call" | custom-call | flops 268435456 | bytes 7340032 | tf_op jit(solution)/shard_map/pallas_call | solution.py:215
  274.5 3.5 %collective-permute-done.61 = f32[16,32,128]{2,1,0:T(8,128)S(1)} collective-permute-done((f32[16,32,128]{2,1,0:T(8,128)S(1)}, f32[16,32,128]{2,1,0:T(8,128)S(1)}, u32[]{:S(2)}, u32[]{:S(2)}) %collective-permute-start.61) | collective-permute-done | bytes 262176 | tf_op jit(solution)/shard_map/ppermute | solution.py:39
  288.3 6.1 %collective-permute-done.63 = f32[12,32,128]{2,1,0:T(8,128)S(1)} collective-permute-done((f32[12,32,128]{2,1,0:T(8,128)S(1)}, f32[12,32,128]{2,1,0:T(8,128)S(1)}, u32[]{:S(2)}, u32[]{:S(2)}) %collective-permute-start.63) | collective-permute-done | bytes 196640 | tf_op jit(solution)/shard_map/ppermute | solution.py:39
  295.3 10.7 %all_to_all.6 = f32[32,1,128]{2,1,0:T(1,128)S(1)} all-to-all(f32[32,1,128]{2,1,0:T(1,128)S(1)} %broadcast_in_dim.60), channel_id=1, replica_groups=mesh['z'=4,'y'=2,'x'=2,'core'=2] {'z','y','x','core'}, dimensions={0} | all-to-all | bytes 32768 | tf_op jit(solution)/shard_map/all_to_all | solution.py:332
  (233 shorter events, 86.7 us)
Async XLA Ops:
  4.5 46.0 %collective-permute-start.2 = (f32[128,128,128]{2,1,0:T(8,128)}, f32[128,128,128]{2,1,0:T(8,128)}, u32[]{:S(2)}, u32[]{:S(2)}) collective-permute-start(f32[128,128,128]{2,1,0:T(8,128)} %tile_ref), channel_id=1, source_target_pairs={{0,1},{1,0},{2,3},{3,2},{4,5},{5,4},{6,7},{7,6},{8,9},{9,8},{10,11... | collective-permute-start | bytes 25165832 | tf_op jit(solution)/shard_map/ppermute | solution.py:39
  6.3 11.4 %collective-permute-start.1 = (s32[128]{0:T(128)S(1)}, s32[128]{0:T(128)S(1)}, u32[]{:S(2)}, u32[]{:S(2)}) collective-permute-start(s32[128]{0:T(128)S(1)} %fusion.8), channel_id=1, source_target_pairs={{0,1},{1,0},{2,3},{3,2},{4,5},{5,4},{6,7},{7,6},{8,9},{9,8},{10,11... | collective-permute-start | bytes 1544 | tf_op jit(solution)/shard_map/ppermute | solution.py:39
  19.2 13.8 %collective-permute-start.3 = (f32[12,32,128]{2,1,0:T(8,128)S(1)}, f32[12,32,128]{2,1,0:T(8,128)S(1)}, u32[]{:S(2)}, u32[]{:S(2)}) collective-permute-start(f32[12,32,128]{2,1,0:T(8,128)S(1)} %broadcast_multiply_fusion), channel_id=1, source_target_pairs={{0,16},{8,24},{16,0},{24,8},{1,17},{9,25},{17,1},{25,9},{2,18},{10... | collective-permute-start | bytes 589832 | tf_op jit(solution)/shard_map/ppermute | solution.py:39
  23.2 9.8 %collective-permute-start.4 = (f32[12,1,128]{2,0,1:T(8,128)S(1)}, f32[12,1,128]{2,0,1:T(8,128)S(1)}, u32[]{:S(2)}, u32[]{:S(2)}) collective-permute-start(f32[12,1,128]{2,0,1:T(8,128)S(1)} %get-tuple-element.164), channel_id=1, source_target_pairs={{0,16},{8,24},{16,0},{24,8},{1,17},{9,25},{17,1},{25,9},{2,18},{10... | collective-permute-start | bytes 18440 | tf_op jit(solution)/shard_map/ppermute | solution.py:39
  38.2 7.9 %collective-permute-start.6 = (f32[16,32,128]{2,1,0:T(8,128)S(1)}, f32[16,32,128]{2,1,0:T(8,128)S(1)}, u32[]{:S(2)}, u32[]{:S(2)}) collective-permute-start(f32[16,32,128]{2,1,0:T(8,128)S(1)} %pad_maximum_fusion), channel_id=1, source_target_pairs={{0,4},{4,0},{1,5},{5,1},{2,6},{6,2},{3,7},{7,3},{8,12},{12,8},{9,1... | collective-permute-start | bytes 786440 | tf_op jit(solution)/shard_map/ppermute | solution.py:39
  46.1 26.2 %collective-permute-start.7 = (f32[32,32,128]{2,1,0:T(8,128)S(1)}, f32[32,32,128]{2,1,0:T(8,128)S(1)}, u32[]{:S(2)}, u32[]{:S(2)}) collective-permute-start(f32[32,32,128]{2,1,0:T(8,128)S(1)} %constant_dynamic-update-slice_fusion.refs_0_), channel_id=1, source_target_pairs={{0,2},{2,0},{1,3},{3,1},{4,6},{6,4},{5,7},{7,5},{8,10},{10,8},{9,1... | collective-permute-start | bytes 1572872 | tf_op jit(solution)/shard_map/ppermute | solution.py:39
  46.8 25.6 %collective-permute-start.10 = (f32[32,32,128]{2,1,0:T(8,128)S(1)}, f32[32,32,128]{2,1,0:T(8,128)S(1)}, u32[]{:S(2)}, u32[]{:S(2)}) collective-permute-start(f32[32,32,128]{2,1,0:T(8,128)S(1)} %constant_dynamic-update-slice_fusion.3.refs_1_), channel_id=1, source_target_pairs={{0,4},{4,0},{1,5},{5,1},{2,6},{6,2},{3,7},{7,3},{8,12},{12,8},{9,1... | collective-permute-start | bytes 1572872 | tf_op jit(solution)/shard_map/ppermute | solution.py:39
  48.5 23.9 %collective-permute-start.13 = (f32[32,32,128]{2,1,0:T(8,128)S(1)}, f32[32,32,128]{2,1,0:T(8,128)S(1)}, u32[]{:S(2)}, u32[]{:S(2)}) collective-permute-start(f32[32,32,128]{2,1,0:T(8,128)S(1)} %constant_dynamic-update-slice_fusion.6.refs_2_), channel_id=1, source_target_pairs={{0,8},{8,0},{16,24},{24,16},{1,9},{9,1},{17,25},{25,17},{2,10},{10... | collective-permute-start | bytes 1572872 | tf_op jit(solution)/shard_map/ppermute | solution.py:39
  80.1 13.7 %collective-permute-start.20 = (f32[32,32,128]{2,1,0:T(8,128)S(1)}, f32[32,32,128]{2,1,0:T(8,128)S(1)}, u32[]{:S(2)}, u32[]{:S(2)}) collective-permute-start(f32[32,32,128]{2,1,0:T(8,128)S(1)} %get-tuple-element.52), channel_id=1, source_target_pairs={{0,8},{8,0},{16,24},{24,16},{1,9},{9,1},{17,25},{25,17},{2,10},{10... | collective-permute-start | bytes 1572872 | tf_op jit(solution)/shard_map/ppermute | solution.py:39
  83.6 11.8 %collective-permute-start.17 = (f32[32,32,128]{2,1,0:T(8,128)S(1)}, f32[32,32,128]{2,1,0:T(8,128)S(1)}, u32[]{:S(2)}, u32[]{:S(2)}) collective-permute-start(f32[32,32,128]{2,1,0:T(8,128)S(1)} %get-tuple-element.50), channel_id=1, source_target_pairs={{0,4},{4,0},{1,5},{5,1},{2,6},{6,2},{3,7},{7,3},{8,12},{12,8},{9,1... | collective-permute-start | bytes 1572872 | tf_op jit(solution)/shard_map/ppermute | solution.py:39
  84.9 10.9 %collective-permute-start.14 = (f32[32,32,128]{2,1,0:T(8,128)S(1)}, f32[32,32,128]{2,1,0:T(8,128)S(1)}, u32[]{:S(2)}, u32[]{:S(2)}) collective-permute-start(f32[32,32,128]{2,1,0:T(8,128)S(1)} %get-tuple-element.48), channel_id=1, source_target_pairs={{0,2},{2,0},{1,3},{3,1},{4,6},{6,4},{5,7},{7,5},{8,10},{10,8},{9,1... | collective-permute-start | bytes 1572872 | tf_op jit(solution)/shard_map/ppermute | solution.py:39
  96.0 8.4 %collective-permute-start.15 = (f32[16,32,128]{2,1,0:T(8,128)S(1)}, f32[16,32,128]{2,1,0:T(8,128)S(1)}, u32[]{:S(2)}, u32[]{:S(2)}) collective-permute-start(f32[16,32,128]{2,1,0:T(8,128)S(1)} %get-tuple-element.95), channel_id=1, source_target_pairs={{0,4},{4,0},{1,5},{5,1},{2,6},{6,2},{3,7},{7,3},{8,12},{12,8},{9,1... | collective-permute-start | bytes 786440 | tf_op jit(solution)/shard_map/ppermute | solution.py:39
  110.1 13.8 %collective-permute-start.23 = (f32[12,32,128]{2,1,0:T(8,128)S(1)}, f32[12,32,128]{2,1,0:T(8,128)S(1)}, u32[]{:S(2)}, u32[]{:S(2)}) collective-permute-start(f32[12,32,128]{2,1,0:T(8,128)S(1)} %pad_maximum_fusion.10), channel_id=1, source_target_pairs={{0,16},{8,24},{16,0},{24,8},{1,17},{9,25},{17,1},{25,9},{2,18},{10... | collective-permute-start | bytes 589832 | tf_op jit(solution)/shard_map/ppermute | solution.py:39
  124.0 8.5 %collective-permute-start.24 = (f32[12,32,128]{2,1,0:T(8,128)S(1)}, f32[12,32,128]{2,1,0:T(8,128)S(1)}, u32[]{:S(2)}, u32[]{:S(2)}) collective-permute-start(f32[12,32,128]{2,1,0:T(8,128)S(1)} %fusion.1), channel_id=1, source_target_pairs={{0,16},{8,24},{16,0},{24,8},{1,17},{9,25},{17,1},{25,9},{2,18},{10... | collective-permute-start | bytes 589832 | tf_op jit(solution)/shard_map/ppermute | solution.py:39
  133.2 8.1 %collective-permute-start.31 = (f32[8,32,128]{2,1,0:T(8,128)S(1)}, f32[8,32,128]{2,1,0:T(8,128)S(1)}, u32[]{:S(2)}, u32[]{:S(2)}) collective-permute-start(f32[8,32,128]{2,1,0:T(8,128)S(1)} %pad_maximum_fusion.20), channel_id=1, source_target_pairs={{0,4},{4,0},{1,5},{5,1},{2,6},{6,2},{3,7},{7,3},{8,12},{12,8},{9,1... | collective-permute-start | bytes 393224 | tf_op jit(solution)/shard_map/ppermute | solution.py:39
  137.7 9.0 %collective-permute-start.26 = (f32[16,32,128]{2,1,0:T(8,128)S(1)}, f32[16,32,128]{2,1,0:T(8,128)S(1)}, u32[]{:S(2)}, u32[]{:S(2)}) collective-permute-start(f32[16,32,128]{2,1,0:T(8,128)S(1)} %pad_maximum_fusion.3), channel_id=1, source_target_pairs={{0,4},{4,0},{1,5},{5,1},{2,6},{6,2},{3,7},{7,3},{8,12},{12,8},{9,1... | collective-permute-start | bytes 786440 | tf_op jit(solution)/shard_map/ppermute | solution.py:39
  146.7 17.1 %collective-permute-start.27 = (f32[32,32,128]{2,1,0:T(8,128)S(1)}, f32[32,32,128]{2,1,0:T(8,128)S(1)}, u32[]{:S(2)}, u32[]{:S(2)}) collective-permute-start(f32[32,32,128]{2,1,0:T(8,128)S(1)} %constant_dynamic-update-slice_fusion.9.refs_0_), channel_id=1, source_target_pairs={{0,2},{2,0},{1,3},{3,1},{4,6},{6,4},{5,7},{7,5},{8,10},{10,8},{9,1... | collective-permute-start | bytes 1572872 | tf_op jit(solution)/shard_map/ppermute | solution.py:39
  147.1 16.7 %collective-permute-start.30 = (f32[32,32,128]{2,1,0:T(8,128)S(1)}, f32[32,32,128]{2,1,0:T(8,128)S(1)}, u32[]{:S(2)}, u32[]{:S(2)}) collective-permute-start(f32[32,32,128]{2,1,0:T(8,128)S(1)} %constant_dynamic-update-slice_fusion.12.refs_1_), channel_id=1, source_target_pairs={{0,4},{4,0},{1,5},{5,1},{2,6},{6,2},{3,7},{7,3},{8,12},{12,8},{9,1... | collective-permute-start | bytes 1572872 | tf_op jit(solution)/shard_map/ppermute | solution.py:39
  148.5 15.2 %collective-permute-start.33 = (f32[32,32,128]{2,1,0:T(8,128)S(1)}, f32[32,32,128]{2,1,0:T(8,128)S(1)}, u32[]{:S(2)}, u32[]{:S(2)}) collective-permute-start(f32[32,32,128]{2,1,0:T(8,128)S(1)} %constant_dynamic-update-slice_fusion.15.refs_2_), channel_id=1, source_target_pairs={{0,8},{8,0},{16,24},{24,16},{1,9},{9,1},{17,25},{25,17},{2,10},{10... | collective-permute-start | bytes 1572872 | tf_op jit(solution)/shard_map/ppermute | solution.py:39
  171.5 13.7 %collective-permute-start.40 = (f32[32,32,128]{2,1,0:T(8,128)S(1)}, f32[32,32,128]{2,1,0:T(8,128)S(1)}, u32[]{:S(2)}, u32[]{:S(2)}) collective-permute-start(f32[32,32,128]{2,1,0:T(8,128)S(1)} %get-tuple-element.63), channel_id=1, source_target_pairs={{0,8},{8,0},{16,24},{24,16},{1,9},{9,1},{17,25},{25,17},{2,10},{10... | collective-permute-start | bytes 1572872 | tf_op jit(solution)/shard_map/ppermute | solution.py:39
  175.8 11.0 %collective-permute-start.37 = (f32[32,32,128]{2,1,0:T(8,128)S(1)}, f32[32,32,128]{2,1,0:T(8,128)S(1)}, u32[]{:S(2)}, u32[]{:S(2)}) collective-permute-start(f32[32,32,128]{2,1,0:T(8,128)S(1)} %get-tuple-element.61), channel_id=1, source_target_pairs={{0,4},{4,0},{1,5},{5,1},{2,6},{6,2},{3,7},{7,3},{8,12},{12,8},{9,1... | collective-permute-start | bytes 1572872 | tf_op jit(solution)/shard_map/ppermute | solution.py:39
  175.8 11.3 %collective-permute-start.34 = (f32[32,32,128]{2,1,0:T(8,128)S(1)}, f32[32,32,128]{2,1,0:T(8,128)S(1)}, u32[]{:S(2)}, u32[]{:S(2)}) collective-permute-start(f32[32,32,128]{2,1,0:T(8,128)S(1)} %get-tuple-element.59), channel_id=1, source_target_pairs={{0,2},{2,0},{1,3},{3,1},{4,6},{6,4},{5,7},{7,5},{8,10},{10,8},{9,1... | collective-permute-start | bytes 1572872 | tf_op jit(solution)/shard_map/ppermute | solution.py:39
  187.0 8.5 %collective-permute-start.38 = (f32[16,32,128]{2,1,0:T(8,128)S(1)}, f32[16,32,128]{2,1,0:T(8,128)S(1)}, u32[]{:S(2)}, u32[]{:S(2)}) collective-permute-start(f32[16,32,128]{2,1,0:T(8,128)S(1)} %get-tuple-element.91), channel_id=1, source_target_pairs={{0,8},{8,0},{16,24},{24,16},{1,9},{9,1},{17,25},{25,17},{2,10},{10... | collective-permute-start | bytes 786440 | tf_op jit(solution)/shard_map/ppermute | solution.py:39
  187.2 8.8 %collective-permute-start.35 = (f32[16,32,128]{2,1,0:T(8,128)S(1)}, f32[16,32,128]{2,1,0:T(8,128)S(1)}, u32[]{:S(2)}, u32[]{:S(2)}) collective-permute-start(f32[16,32,128]{2,1,0:T(8,128)S(1)} %get-tuple-element.89), channel_id=1, source_target_pairs={{0,4},{4,0},{1,5},{5,1},{2,6},{6,2},{3,7},{7,3},{8,12},{12,8},{9,1... | collective-permute-start | bytes 786440 | tf_op jit(solution)/shard_map/ppermute | solution.py:39
  203.2 8.8 %collective-permute-start.43 = (f32[12,32,128]{2,1,0:T(8,128)S(1)}, f32[12,32,128]{2,1,0:T(8,128)S(1)}, u32[]{:S(2)}, u32[]{:S(2)}) collective-permute-start(f32[12,32,128]{2,1,0:T(8,128)S(1)} %pad_maximum_fusion.11), channel_id=1, source_target_pairs={{0,16},{8,24},{16,0},{24,8},{1,17},{9,25},{17,1},{25,9},{2,18},{10... | collective-permute-start | bytes 589832 | tf_op jit(solution)/shard_map/ppermute | solution.py:39
  232.7 16.9 %collective-permute-start.47 = (f32[32,32,128]{2,1,0:T(8,128)S(1)}, f32[32,32,128]{2,1,0:T(8,128)S(1)}, u32[]{:S(2)}, u32[]{:S(2)}) collective-permute-start(f32[32,32,128]{2,1,0:T(8,128)S(1)} %constant_dynamic-update-slice_fusion.18.refs_0_), channel_id=1, source_target_pairs={{0,2},{2,0},{1,3},{3,1},{4,6},{6,4},{5,7},{7,5},{8,10},{10,8},{9,1... | collective-permute-start | bytes 1572872 | tf_op jit(solution)/shard_map/ppermute | solution.py:39
  233.1 16.6 %collective-permute-start.50 = (f32[32,32,128]{2,1,0:T(8,128)S(1)}, f32[32,32,128]{2,1,0:T(8,128)S(1)}, u32[]{:S(2)}, u32[]{:S(2)}) collective-permute-start(f32[32,32,128]{2,1,0:T(8,128)S(1)} %constant_dynamic-update-slice_fusion.21.refs_1_), channel_id=1, source_target_pairs={{0,4},{4,0},{1,5},{5,1},{2,6},{6,2},{3,7},{7,3},{8,12},{12,8},{9,1... | collective-permute-start | bytes 1572872 | tf_op jit(solution)/shard_map/ppermute | solution.py:39
  234.9 14.8 %collective-permute-start.53 = (f32[32,32,128]{2,1,0:T(8,128)S(1)}, f32[32,32,128]{2,1,0:T(8,128)S(1)}, u32[]{:S(2)}, u32[]{:S(2)}) collective-permute-start(f32[32,32,128]{2,1,0:T(8,128)S(1)} %constant_dynamic-update-slice_fusion.24.refs_2_), channel_id=1, source_target_pairs={{0,8},{8,0},{16,24},{24,16},{1,9},{9,1},{17,25},{25,17},{2,10},{10... | collective-permute-start | bytes 1572872 | tf_op jit(solution)/shard_map/ppermute | solution.py:39
  257.4 14.1 %collective-permute-start.60 = (f32[32,32,128]{2,1,0:T(8,128)S(1)}, f32[32,32,128]{2,1,0:T(8,128)S(1)}, u32[]{:S(2)}, u32[]{:S(2)}) collective-permute-start(f32[32,32,128]{2,1,0:T(8,128)S(1)} %get-tuple-element.74), channel_id=1, source_target_pairs={{0,8},{8,0},{16,24},{24,16},{1,9},{9,1},{17,25},{25,17},{2,10},{10... | collective-permute-start | bytes 1572872 | tf_op jit(solution)/shard_map/ppermute | solution.py:39
  262.2 9.9 %collective-permute-start.57 = (f32[32,32,128]{2,1,0:T(8,128)S(1)}, f32[32,32,128]{2,1,0:T(8,128)S(1)}, u32[]{:S(2)}, u32[]{:S(2)}) collective-permute-start(f32[32,32,128]{2,1,0:T(8,128)S(1)} %get-tuple-element.72), channel_id=1, source_target_pairs={{0,4},{4,0},{1,5},{5,1},{2,6},{6,2},{3,7},{7,3},{8,12},{12,8},{9,1... | collective-permute-start | bytes 1572872 | tf_op jit(solution)/shard_map/ppermute | solution.py:39
  262.2 11.6 %collective-permute-start.54 = (f32[32,32,128]{2,1,0:T(8,128)S(1)}, f32[32,32,128]{2,1,0:T(8,128)S(1)}, u32[]{:S(2)}, u32[]{:S(2)}) collective-permute-start(f32[32,32,128]{2,1,0:T(8,128)S(1)} %get-tuple-element.70), channel_id=1, source_target_pairs={{0,2},{2,0},{1,3},{3,1},{4,6},{6,4},{5,7},{7,5},{8,10},{10,8},{9,1... | collective-permute-start | bytes 1572872 | tf_op jit(solution)/shard_map/ppermute | solution.py:39
  285.6 8.7 %collective-permute-start.63 = (f32[12,32,128]{2,1,0:T(8,128)S(1)}, f32[12,32,128]{2,1,0:T(8,128)S(1)}, u32[]{:S(2)}, u32[]{:S(2)}) collective-permute-start(f32[12,32,128]{2,1,0:T(8,128)S(1)} %get-tuple-element.142), channel_id=1, source_target_pairs={{0,16},{8,24},{16,0},{24,8},{1,17},{9,25},{17,1},{25,9},{2,18},{10... | collective-permute-start | bytes 589832 | tf_op jit(solution)/shard_map/ppermute | solution.py:39
  (37 other events, 234.5 us)

commit v9 on v8

--- a/solution.py
+++ b/solution.py
@@ -14,7 +14,7 @@
 UNROLL = 8
 CHUNK = 8
 SLOTS = 8
-VMEM = 16 * 1024 * 1024
+VMEM = 60 * 1024 * 1024
 CHIPS = ("z", "y", "x")
 ALL = ("z", "y", "x", "core")
 NEAR = ("x", "y", "z")
@@ -48,18 +48,15 @@
     return array[:middle], array[middle:]
 
 
-def gather_far(block, beside=None):
+def gather_far(block):
     blocks = [block]
     for step in reversed(far_steps()):
         got = swap(blocks[0] if len(blocks) == 1 else jnp.concatenate(blocks, axis=0), step)
-        if beside is not None:
-            got, beside = after(got, *beside), None
         blocks = blocks + jnp.split(got, len(blocks))
     return blocks
 
 
-def gather(flux, edges, beside=None):
-    blocks = gather_far(flux, beside)
+def gather_near(blocks, edges):
     starts = [
         jnp.concatenate([b[low:high] for b in blocks], axis=0) for low, high in zip(edges[:-1], edges[1:])
     ]
@@ -78,10 +75,14 @@
     for part, (keep, send) in enumerate(zip(keeps, sends)):
         steps = near_steps(part)
         got = swap(send, steps[0])
+        terms = [keep]
         for step in steps[1:]:
-            keep, send = [k + g for k, g in zip(halves(keep), halves(got))]
-            got = swap(send, step)
-        parts.append([k + g for k, g in zip(jnp.split(keep, far), jnp.split(got, far))])
+            terms.append(got)
+            got = swap(sum([halves(t)[1] for t in terms[1:]], halves(terms[0])[1]), step)
+            *terms, got = lax.optimization_barrier((*terms, got))
+            terms = [halves(t)[0] for t in terms]
+        terms = [jnp.split(t, far) for t in (*terms, got)]
+        parts.append([sum(t[1:], t[0]) for t in zip(*terms)])
     return [jnp.concatenate(group, axis=0) for group in zip(*parts)]
 
 
@@ -92,6 +93,15 @@
         got = swap(jnp.concatenate(send, axis=0) if middle > 1 else send[0], step)
         blocks = [b + g for b, g in zip(blocks[:middle], jnp.split(got, middle))]
     return blocks[0]
+
+
+def sum_far(blocks):
+    count = len(blocks)
+    for place, step in enumerate(far_steps()):
+        bit = count >> (place + 1)
+        got = jnp.split(swap(jnp.concatenate(blocks, axis=0), step), count)
+        blocks = [b + got[k ^ bit] for k, b in enumerate(blocks)]
+    return blocks
 
 
 def split_kernel(tile_ref, *refs):
@@ -279,7 +289,8 @@
     kind = jnp.where(used, jnp.where(col_side == 0, 0, 2 - row_side), 3)
     row = jnp.where(row_side == 1, row, row + num // 2)
     code = (kind * num + row) * num + col
-    code = jnp.concatenate([code, swap(code, cores)])
+    other_code = swap(code, cores)
+    code = jnp.concatenate([code, other_code])
     kind = code // (num * num)
     slots = jnp.arange(CORES * length, dtype=jnp.int32)
     key = kind * (CORES * length) + slots
@@ -303,41 +314,43 @@
     theirs = jnp.where(core == 0, high, low)
     packed = [theirs, jnp.broadcast_to(relax, (per, 8, size)), jnp.broadcast_to(heat, (per, 8, size))]
     got = swap(jnp.concatenate(packed, axis=1), cores)
-    other_values = swap(after(tile_values, got), cores)
+    tile_values = after(tile_values, got, other_code)
+    other_values = swap(tile_values, cores)
     drive_half = by_core(mine, got[:, :half])
     relax_both = by_core(relax, got[:, half : half + 1])
     heat_both = by_core(heat, got[:, half + 8 : half + 9])
 
-    flux = relax_both * drive_half
-    pairs = split_tiles(after(tile_values, flux), 0)
-    heats = gather_far(heat_both * relax_both)
-    beside = (pairs, *heats)
+    drives = gather_far(drive_half)
+    small = gather_far(jnp.concatenate([relax_both, heat_both * relax_both], axis=1))
+    relaxes, heats = [s[:, :1] for s in small], [s[:, 1:] for s in small]
+    pairs = split_tiles(tile_values, 0)
+    drives[-1] = after(drives[-1], pairs)
+    fluxes = [r * d for r, d in zip(relaxes, drives)]
     sizes = [chips // 2 * (high - low) for low, high in zip(edges[:-1], edges[1:])]
     for sweep in range(ITERS):
-        pieces = gather(flux, edges, beside)
+        pieces = gather_near(fluxes, edges)
         if sweep == 0:
-            pairs, beside = split_tiles(other_values, 1, pairs), None
+            pairs = split_tiles(other_values, 1, pairs)
         near, far = [p for p, _ in pieces], [p for _, p in pieces]
         base = apply_tiles(0, 0, places, pairs, near, [num // 2, num // 2], 0.5)
         sends = apply_tiles(1, 0, places, pairs, far, sizes, 0.25, base[0])
         keeps = apply_tiles(2, num // 2, places, pairs, far, sizes, 0.25, base[1])
         blocks = reduce_near(keeps, sends)
-        if sweep == ITERS - 1:
-            weighted = sum(
-                [jnp.sum(w * b, axis=(0, 2)) for w, b in zip(heats, blocks)],
-                jnp.sum(heats[0] * drive_half, axis=(0, 2)),
-            )
-            totals = jnp.concatenate([weighted, jnp.sum(heat).reshape(1)])
-            totals = jnp.pad(totals[None], ((0, 0), (0, size - half - 1)))
-            totals = lax.all_to_all(
-                jnp.broadcast_to(totals, (chips * CORES, size)), ALL, split_axis=0, concat_axis=0, tiled=True
-            )
-            totals = jnp.sum(totals.reshape(chips, CORES, size), axis=0)
-            conductivity = totals[:, :half].reshape(columns) / jnp.sum(totals[:, half])
-        summed = reduce_far(blocks)
-        if sweep == ITERS - 1:
-            summed = after(summed, conductivity)
-        flux = relax_both * (drive_half + summed)
+        if sweep < ITERS - 1:
+            fluxes = [r * (d + s) for r, d, s in zip(relaxes, drives, sum_far(blocks))]
+    weighted = sum(
+        [jnp.sum(w * b, axis=(0, 2)) for w, b in zip(heats, blocks)],
+        jnp.sum(heats[0] * drive_half, axis=(0, 2)),
+    )
+    totals = jnp.concatenate([weighted, jnp.sum(heat).reshape(1)])
+    totals = jnp.pad(totals[None], ((0, 0), (0, size - half - 1)))
+    *blocks, totals = lax.optimization_barrier((*blocks, totals))
+    totals = lax.all_to_all(
+        jnp.broadcast_to(totals, (chips * CORES, size)), ALL, split_axis=0, concat_axis=0, tiled=True
+    )
+    totals = jnp.sum(totals.reshape(chips, CORES, size), axis=0)
+    conductivity = totals[:, :half].reshape(columns) / jnp.sum(totals[:, half])
+    flux = relax_both * (drive_half + after(reduce_far(blocks), conductivity))
     first, second = flux[:per], flux[per:]
     mine = jnp.where(core == 0, first, second)
     got = swap(jnp.where(core == 0, second, first), cores)

time: 311 us -> 278 us (0.89)
  waiting for transfers between devices: 108 us -> 76.7 us
  Pallas kernels: 104 us -> 89.7 us
  other arithmetic: 8.08 us -> 19.8 us
  blocking collectives: 10.7 us -> 0 us
  starting transfers between devices: 71.2 us -> 79.6 us
    ppermute x65 -> x63, waiting for transfers between devices: 108 us -> 72.3 us  [swap(): return lax.ppermute(array, axis, pairs)]
    pallas_call x9, Pallas kernels: 92.9 us -> 69.1 us  [apply_tiles(): pl.pallas_call(functools.partial(apply_kernel, span, skip, counts, base i...]
    all_to_all x1 -> x0, blocking collectives: 10.7 us -> none  [shards(): lax.all_to_all(jnp.broadcast_to(totals, (chips * CORES, size)), ALL, spli...]
    pallas_call x2, Pallas kernels: 10.6 us -> 20.6 us  [split_tiles(): pl.pallas_call(split_kernel, out_shape=jax.ShapeDtypeStruct((CORES * leng...]
    add x27 -> x22, other arithmetic: 1.22 us -> 10.8 us  [the longest x18 8.89 us: reduce_near(): sum([halves(t)[1] for t in terms[1:]], halves(terms[0])[1])]
    ppermute x65 -> x63, starting transfers between devices: 71.2 us -> 76 us  [swap(): return lax.ppermute(array, axis, pairs)]
    all_to_all x0 -> x1, waiting for transfers between devices: none -> 4.41 us  [shards(): lax.all_to_all(jnp.broadcast_to(totals, (chips * CORES, size)), ALL, spli...]
    all_to_all x0 -> x1, starting transfers between devices: none -> 3.6 us  [shards(): lax.all_to_all(jnp.broadcast_to(totals, (chips * CORES, size)), ALL, spli...]
  transfers between devices with their start and end apart: 65 -> 64, of which waited for: 34 -> 34; matrix products, arithmetic and copies ran while one was open for 2% -> 6% of each run, Pallas kernels for 26% -> 25%
where the time goes in v9:
time: 278 us
  Pallas kernels  89.7 us (32%)
  starting transfers between devices  79.6 us (29%)
  waiting for transfers between devices  76.7 us (28%)
  other arithmetic  19.8 us (7%)
  local copies, waits for them, and re-layouts  9.17 us (3%)
    ppermute x63, starting transfers between devices, swap(): return lax.ppermute(array, axis, pairs)  76 us
    ppermute x63, waiting for transfers between devices, swap(): return lax.ppermute(array, axis, pairs)  72.3 us
    pallas_call x9, Pallas kernels, apply_tiles(): pl.pallas_call(functools.partial(apply_kernel, span, skip, counts, base i...  69.1 us
    pallas_call x2, Pallas kernels, split_tiles(): pl.pallas_call(split_kernel, out_shape=jax.ShapeDtypeStruct((CORES * leng...  20.6 us
    add x18, other arithmetic, reduce_near(): sum([halves(t)[1] for t in terms[1:]], halves(terms[0])[1])  8.89 us
  transfers between devices with their start and end apart: 64, of which 34 were waited for; matrix products, arithmetic and copies ran while one was open for 6% of the time, Pallas kernels for 25%

profile of v9, /device:TPU:0, one launch (start us, length us, event | category | flops | bytes accessed | tf_op | source)
XLA Modules:
  0.0 277.5 jit_solution(7378679363505588947)
XLA Ops:
  8.4 3.9 %collective-permute-start.4 = (f32[12,32,128]{2,1,0:T(8,128)S(1)}, f32[12,32,128]{2,1,0:T(8,128)S(1)}, u32[]{:S(2)}, u32[]{:S(2)}) collective-permute-start(f32[12,32,128]{2,1,0:T(8,128)S(1)} %get-tuple-element.272), channel_id=1, source_target_pairs={{0,16},{8,24},{16,0},{24,8},{1,17},{9,25},{17,1},{25,9},{2,18},{10... | collective-permute-start | bytes 589832 | tf_op jit(solution)/shard_map/ppermute | solution.py:39
  12.4 10.3 %shard_map.95.refs_0_ = bf16[256,256,128]{2,1,0:T(8,128)(2,1)} custom-call(f32[128,128,128]{2,1,0:T(8,128)} %tile_ref), custom_call_target="tpu_custom_call" | custom-call | flops 6291456 | bytes 16777216 | tf_op jit(solution)/shard_map/pallas_call | solution.py:125
  33.7 3.8 %collective-permute-done.6 = f32[16,32,128]{2,1,0:T(8,128)S(1)} collective-permute-done((f32[16,32,128]{2,1,0:T(8,128)S(1)}, f32[16,32,128]{2,1,0:T(8,128)S(1)}, u32[]{:S(2)}, u32[]{:S(2)}) %collective-permute-start.6) | collective-permute-done | bytes 262176 | tf_op jit(solution)/shard_map/ppermute | solution.py:39
  42.9 10.3 %shard_map.96.pairs_ref = bf16[256,256,128]{2,1,0:T(8,128)(2,1)} custom-call(f32[128,128,128]{2,1,0:T(8,128)} %collective-permute-done.2.tile_ref, bf16[256,256,128]{2,1,0:T(8,128)(2,1)} %shard_map.95.refs_0_), custom_call_target="tpu_custom_call", output_to_operand_aliasing={{}: (1, {})} | custom-call | flops 6291456 | bytes 16777216 | tf_op jit(solution)/shard_map/pallas_call | solution.py:125
  53.2 9.0 %shard_map.97 = (f32[96,32,128]{2,1,0:T(8,128)}, f32[96,32,128]{2,1,0:T(8,128)}) custom-call(s32[4]{0:T(128)} %convert_reduce_fusion.1.ends_ref, s32[256]{0:T(256)} %get-tuple-element.209.order_ref, s32[256]{0:T(256)} %get-tuple-element.285.row_ref, s32[256]{0:T(256)} %get-tuple-element.284.col_ref, bf16[256,256,128]{2,1,0:T(8,128)(2,1)} %shard_map.96.pairs_ref, ...), custom_call_target="tpu_custom_call" | custom-call | flops 536870912 | bytes 14680064 | tf_op jit(solution)/shard_map/pallas_call | solution.py:225
  63.4 6.9 %shard_map.99 = (f32[32,32,128]{2,1,0:T(8,128)}, f32[32,32,128]{2,1,0:T(8,128)}, f32[32,32,128]{2,1,0:T(8,128)}) custom-call(s32[4]{0:T(128)} %convert_reduce_fusion.1.ends_ref, s32[256]{0:T(256)} %get-tuple-element.209.order_ref, s32[256]{0:T(256)} %get-tuple-element.285.row_ref, s32[256]{0:T(256)} %get-tuple-element.284.col_ref, ...), custom_call_target="tpu_custom_call" | custom-call | flops 268435456 | bytes 7340032 | tf_op jit(solution)/shard_map/pallas_call | solution.py:225
  71.2 2.3 collective-permute-start.17
  73.8 7.2 %shard_map.98 = (f32[32,32,128]{2,1,0:T(8,128)}, f32[32,32,128]{2,1,0:T(8,128)}, f32[32,32,128]{2,1,0:T(8,128)}) custom-call(s32[4]{0:T(128)} %convert_reduce_fusion.1.ends_ref, s32[256]{0:T(256)} %get-tuple-element.209.order_ref, s32[256]{0:T(256)} %get-tuple-element.285.row_ref, s32[256]{0:T(256)} %get-tuple-element.284.col_ref, ...), custom_call_target="tpu_custom_call" | custom-call | flops 268435456 | bytes 7340032 | tf_op jit(solution)/shard_map/pallas_call | solution.py:225
  84.8 2.1 collective-permute-start.18
  94.5 2.8 %collective-permute-done.19 = f32[8,32,128]{2,1,0:T(8,128)S(1)} collective-permute-done((f32[8,32,128]{2,1,0:T(8,128)S(1)}, f32[8,32,128]{2,1,0:T(8,128)S(1)}, u32[]{:S(2)}, u32[]{:S(2)}) %collective-permute-start.19) | collective-permute-done | bytes 131104 | tf_op jit(solution)/shard_map/ppermute | solution.py:39
  99.0 2.3 collective-permute-start.23
  101.4 11.3 %collective-permute-done.23 = f32[24,32,128]{2,1,0:T(8,128)S(1)} collective-permute-done((f32[24,32,128]{2,1,0:T(8,128)S(1)}, f32[24,32,128]{2,1,0:T(8,128)S(1)}, u32[]{:S(2)}, u32[]{:S(2)}) %collective-permute-start.23) | collective-permute-done | bytes 393248 | tf_op jit(solution)/shard_map/ppermute | solution.py:39
  116.1 2.4 collective-permute-done.24
  122.2 3.2 %collective-permute-done.25 = f32[16,32,128]{2,1,0:T(8,128)S(1)} collective-permute-done((f32[16,32,128]{2,1,0:T(8,128)S(1)}, f32[16,32,128]{2,1,0:T(8,128)S(1)}, u32[]{:S(2)}, u32[]{:S(2)}) %collective-permute-start.25) | collective-permute-done | bytes 262176 | tf_op jit(solution)/shard_map/ppermute | solution.py:39
  125.4 2.5 collective-permute-start.26
  127.9 2.5 collective-permute-start.29
  131.4 9.0 %shard_map.100 = (f32[96,32,128]{2,1,0:T(8,128)}, f32[96,32,128]{2,1,0:T(8,128)}) custom-call(s32[4]{0:T(128)} %convert_reduce_fusion.1.ends_ref, s32[256]{0:T(256)} %get-tuple-element.209.order_ref, s32[256]{0:T(256)} %get-tuple-element.285.row_ref, s32[256]{0:T(256)} %get-tuple-element.284.col_ref, bf16[256,256,128]{2,1,0:T(8,128)(2,1)} %shard_map.96.pairs_ref, ...), custom_call_target="tpu_custom_call" | custom-call | flops 536870912 | bytes 14680064 | tf_op jit(solution)/shard_map/pallas_call | solution.py:225
  141.6 6.9 %shard_map.102 = (f32[32,32,128]{2,1,0:T(8,128)}, f32[32,32,128]{2,1,0:T(8,128)}, f32[32,32,128]{2,1,0:T(8,128)}) custom-call(s32[4]{0:T(128)} %convert_reduce_fusion.1.ends_ref, s32[256]{0:T(256)} %get-tuple-element.209.order_ref, s32[256]{0:T(256)} %get-tuple-element.285.row_ref, s32[256]{0:T(256)} %get-tuple-element.284.col_ref, ...), custom_call_target="tpu_custom_call" | custom-call | flops 268435456 | bytes 7340032 | tf_op jit(solution)/shard_map/pallas_call | solution.py:225
  149.6 2.6 collective-permute-start.36
  152.2 7.2 %shard_map.101 = (f32[32,32,128]{2,1,0:T(8,128)}, f32[32,32,128]{2,1,0:T(8,128)}, f32[32,32,128]{2,1,0:T(8,128)}) custom-call(s32[4]{0:T(128)} %convert_reduce_fusion.1.ends_ref, s32[256]{0:T(256)} %get-tuple-element.209.order_ref, s32[256]{0:T(256)} %get-tuple-element.285.row_ref, s32[256]{0:T(256)} %get-tuple-element.284.col_ref, ...), custom_call_target="tpu_custom_call" | custom-call | flops 268435456 | bytes 7340032 | tf_op jit(solution)/shard_map/pallas_call | solution.py:225
  165.9 2.5 collective-permute-done.34
  177.4 4.8 %collective-permute-start.42 = (f32[24,32,128]{2,1,0:T(8,128)S(1)}, f32[24,32,128]{2,1,0:T(8,128)S(1)}, u32[]{:S(2)}, u32[]{:S(2)}) collective-permute-start(f32[24,32,128]{2,1,0:T(8,128)S(1)} %get-tuple-element.210), channel_id=1, source_target_pairs={{0,16},{8,24},{16,0},{24,8},{1,17},{9,25},{17,1},{25,9},{2,18},{10... | collective-permute-start | bytes 1179656 | tf_op jit(solution)/shard_map/ppermute | solution.py:39
  182.2 9.1 %collective-permute-done.42 = f32[24,32,128]{2,1,0:T(8,128)S(1)} collective-permute-done((f32[24,32,128]{2,1,0:T(8,128)S(1)}, f32[24,32,128]{2,1,0:T(8,128)S(1)}, u32[]{:S(2)}, u32[]{:S(2)}) %collective-permute-start.42) | collective-permute-done | bytes 393248 | tf_op jit(solution)/shard_map/ppermute | solution.py:39
  193.2 3.4 %collective-permute-done.43 = f32[8,32,128]{2,1,0:T(8,128)S(1)} collective-permute-done((f32[8,32,128]{2,1,0:T(8,128)S(1)}, f32[8,32,128]{2,1,0:T(8,128)S(1)}, u32[]{:S(2)}, u32[]{:S(2)}) %collective-permute-start.43) | collective-permute-done | bytes 131104 | tf_op jit(solution)/shard_map/ppermute | solution.py:39
  201.4 4.5 %collective-permute-done.44 = f32[16,32,128]{2,1,0:T(8,128)S(1)} collective-permute-done((f32[16,32,128]{2,1,0:T(8,128)S(1)}, f32[16,32,128]{2,1,0:T(8,128)S(1)}, u32[]{:S(2)}, u32[]{:S(2)}) %collective-permute-start.44) | collective-permute-done | bytes 262176 | tf_op jit(solution)/shard_map/ppermute | solution.py:39
  208.0 9.0 %shard_map.103 = (f32[96,32,128]{2,1,0:T(8,128)}, f32[96,32,128]{2,1,0:T(8,128)}) custom-call(s32[4]{0:T(128)} %convert_reduce_fusion.1.ends_ref, s32[256]{0:T(256)} %get-tuple-element.209.order_ref, s32[256]{0:T(256)} %get-tuple-element.285.row_ref, s32[256]{0:T(256)} %get-tuple-element.284.col_ref, bf16[256,256,128]{2,1,0:T(8,128)(2,1)} %shard_map.96.pairs_ref, ...), custom_call_target="tpu_custom_call" | custom-call | flops 536870912 | bytes 14680064 | tf_op jit(solution)/shard_map/pallas_call | solution.py:225
  218.2 6.9 %shard_map.105 = (f32[32,32,128]{2,1,0:T(8,128)}, f32[32,32,128]{2,1,0:T(8,128)}, f32[32,32,128]{2,1,0:T(8,128)}) custom-call(s32[4]{0:T(128)} %convert_reduce_fusion.1.ends_ref, s32[256]{0:T(256)} %get-tuple-element.209.order_ref, s32[256]{0:T(256)} %get-tuple-element.285.row_ref, s32[256]{0:T(256)} %get-tuple-element.284.col_ref, ...), custom_call_target="tpu_custom_call" | custom-call | flops 268435456 | bytes 7340032 | tf_op jit(solution)/shard_map/pallas_call | solution.py:225
  229.0 7.2 %shard_map.104 = (f32[32,32,128]{2,1,0:T(8,128)}, f32[32,32,128]{2,1,0:T(8,128)}, f32[32,32,128]{2,1,0:T(8,128)}) custom-call(s32[4]{0:T(128)} %convert_reduce_fusion.1.ends_ref, s32[256]{0:T(256)} %get-tuple-element.209.order_ref, s32[256]{0:T(256)} %get-tuple-element.285.row_ref, s32[256]{0:T(256)} %get-tuple-element.284.col_ref, ...), custom_call_target="tpu_custom_call" | custom-call | flops 268435456 | bytes 7340032 | tf_op jit(solution)/shard_map/pallas_call | solution.py:225
  259.2 3.6 %all-to-all-start = ((f32[32,1,128]{2,1,0:T(1,128)}), f32[32,1,128]{2,1,0:T(1,128)S(1)}, u32[]{:S(2)}, u32[]{:S(2)}) async-start(f32[32,1,128]{2,1,0:T(1,128)} %broadcast_in_dim.60), calls=%async_computation | async-start | bytes 32768 | tf_op jit(solution)/shard_map/all_to_all | solution.py:348
  262.8 2.7 collective-permute-start.61
  265.6 4.4 %all-to-all-done = f32[32,1,128]{2,1,0:T(1,128)S(1)} async-done(((f32[32,1,128]{2,1,0:T(1,128)}), f32[32,1,128]{2,1,0:T(1,128)S(1)}, u32[]{:S(2)}, u32[]{:S(2)}) %all-to-all-start) | async-done | bytes 16416 | tf_op jit(solution)/shard_map/all_to_all | solution.py:348
  271.9 3.4 %collective-permute-done.61 = f32[12,32,128]{2,1,0:T(8,128)S(1)} collective-permute-done((f32[12,32,128]{2,1,0:T(8,128)S(1)}, f32[12,32,128]{2,1,0:T(8,128)S(1)}, u32[]{:S(2)}, u32[]{:S(2)}) %collective-permute-start.61) | collective-permute-done | bytes 196640 | tf_op jit(solution)/shard_map/ppermute | solution.py:39
  (336 shorter events, 105.2 us)
Async XLA Ops:
  6.1 36.8 %collective-permute-start.2 = (f32[128,128,128]{2,1,0:T(8,128)}, f32[128,128,128]{2,1,0:T(8,128)}, u32[]{:S(2)}, u32[]{:S(2)}) collective-permute-start(f32[128,128,128]{2,1,0:T(8,128)} %tile_ref), channel_id=1, source_target_pairs={{0,1},{1,0},{2,3},{3,2},{4,5},{5,4},{6,7},{7,6},{8,9},{9,8},{10,11... | collective-permute-start | bytes 25165832 | tf_op jit(solution)/shard_map/ppermute | solution.py:39
  8.4 14.9 %collective-permute-start.4 = (f32[12,32,128]{2,1,0:T(8,128)S(1)}, f32[12,32,128]{2,1,0:T(8,128)S(1)}, u32[]{:S(2)}, u32[]{:S(2)}) collective-permute-start(f32[12,32,128]{2,1,0:T(8,128)S(1)} %get-tuple-element.272), channel_id=1, source_target_pairs={{0,16},{8,24},{16,0},{24,8},{1,17},{9,25},{17,1},{25,9},{2,18},{10... | collective-permute-start | bytes 589832 | tf_op jit(solution)/shard_map/ppermute | solution.py:39
  12.3 10.4 %collective-permute-start.3 = (f32[12,2,128]{2,0,1:T(8,128)S(1)}, f32[12,2,128]{2,0,1:T(8,128)S(1)}, u32[]{:S(2)}, u32[]{:S(2)}) collective-permute-start(f32[12,2,128]{2,0,1:T(8,128)S(1)} %pad_maximum_fusion.22), channel_id=1, source_target_pairs={{0,16},{8,24},{16,0},{24,8},{1,17},{9,25},{17,1},{25,9},{2,18},{10... | collective-permute-start | bytes 36872 | tf_op jit(solution)/shard_map/ppermute | solution.py:39
  28.8 8.7 %collective-permute-start.6 = (f32[16,32,128]{2,1,0:T(8,128)S(1)}, f32[16,32,128]{2,1,0:T(8,128)S(1)}, u32[]{:S(2)}, u32[]{:S(2)}) collective-permute-start(f32[16,32,128]{2,1,0:T(8,128)S(1)} %pad_maximum_fusion), channel_id=1, source_target_pairs={{0,4},{4,0},{1,5},{5,1},{2,6},{6,2},{3,7},{7,3},{8,12},{12,8},{9,1... | collective-permute-start | bytes 786440 | tf_op jit(solution)/shard_map/ppermute | solution.py:39
  30.4 7.7 %collective-permute-start.9 = (f32[16,32,128]{2,1,0:T(8,128)S(1)}, f32[16,32,128]{2,1,0:T(8,128)S(1)}, u32[]{:S(2)}, u32[]{:S(2)}) collective-permute-start(f32[16,32,128]{2,1,0:T(8,128)S(1)} %pad_maximum_fusion.1), channel_id=1, source_target_pairs={{0,8},{8,0},{16,24},{24,16},{1,9},{9,1},{17,25},{25,17},{2,10},{10... | collective-permute-start | bytes 786440 | tf_op jit(solution)/shard_map/ppermute | solution.py:39
  37.5 24.7 %collective-permute-start.7 = (f32[32,32,128]{2,1,0:T(8,128)S(1)}, f32[32,32,128]{2,1,0:T(8,128)S(1)}, u32[]{:S(2)}, u32[]{:S(2)}) collective-permute-start(f32[32,32,128]{2,1,0:T(8,128)S(1)} %constant_dynamic-update-slice_fusion.refs_0_), channel_id=1, source_target_pairs={{0,2},{2,0},{1,3},{3,1},{4,6},{6,4},{5,7},{7,5},{8,10},{10,8},{9,1... | collective-permute-start | bytes 1572872 | tf_op jit(solution)/shard_map/ppermute | solution.py:39
  38.2 24.1 %collective-permute-start.10 = (f32[32,32,128]{2,1,0:T(8,128)S(1)}, f32[32,32,128]{2,1,0:T(8,128)S(1)}, u32[]{:S(2)}, u32[]{:S(2)}) collective-permute-start(f32[32,32,128]{2,1,0:T(8,128)S(1)} %constant_dynamic-update-slice_fusion.3.refs_1_), channel_id=1, source_target_pairs={{0,4},{4,0},{1,5},{5,1},{2,6},{6,2},{3,7},{7,3},{8,12},{12,8},{9,1... | collective-permute-start | bytes 1572872 | tf_op jit(solution)/shard_map/ppermute | solution.py:39
  40.5 21.7 %collective-permute-start.13 = (f32[32,32,128]{2,1,0:T(8,128)S(1)}, f32[32,32,128]{2,1,0:T(8,128)S(1)}, u32[]{:S(2)}, u32[]{:S(2)}) collective-permute-start(f32[32,32,128]{2,1,0:T(8,128)S(1)} %constant_dynamic-update-slice_fusion.6.refs_2_), channel_id=1, source_target_pairs={{0,8},{8,0},{16,24},{24,16},{1,9},{9,1},{17,25},{25,17},{2,10},{10... | collective-permute-start | bytes 1572872 | tf_op jit(solution)/shard_map/ppermute | solution.py:39
  70.3 11.2 %collective-permute-start.14 = (f32[32,32,128]{2,1,0:T(8,128)}, f32[32,32,128]{2,1,0:T(8,128)S(1)}, u32[]{:S(2)}, u32[]{:S(2)}) collective-permute-start(f32[32,32,128]{2,1,0:T(8,128)} %get-tuple-element.112), channel_id=1, source_target_pairs={{0,2},{2,0},{1,3},{3,1},{4,6},{6,4},{5,7},{7,5},{8,10},{10,8},{9,1... | collective-permute-start | bytes 1572872 | tf_op jit(solution)/shard_map/ppermute | solution.py:39
  71.2 12.6 %collective-permute-start.17 = (f32[32,32,128]{2,1,0:T(8,128)}, f32[32,32,128]{2,1,0:T(8,128)S(1)}, u32[]{:S(2)}, u32[]{:S(2)}) collective-permute-start(f32[32,32,128]{2,1,0:T(8,128)} %get-tuple-element.121), channel_id=1, source_target_pairs={{0,4},{4,0},{1,5},{5,1},{2,6},{6,2},{3,7},{7,3},{8,12},{12,8},{9,1... | collective-permute-start | bytes 1572872 | tf_op jit(solution)/shard_map/ppermute | solution.py:39
  73.5 13.4 %collective-permute-start.20 = (f32[32,32,128]{2,1,0:T(8,128)}, f32[32,32,128]{2,1,0:T(8,128)S(1)}, u32[]{:S(2)}, u32[]{:S(2)}) collective-permute-start(f32[32,32,128]{2,1,0:T(8,128)} %get-tuple-element.130), channel_id=1, source_target_pairs={{0,8},{8,0},{16,24},{24,16},{1,9},{9,1},{17,25},{25,17},{2,10},{10... | collective-permute-start | bytes 1572872 | tf_op jit(solution)/shard_map/ppermute | solution.py:39
  99.0 13.6 %collective-permute-start.23 = (f32[24,32,128]{2,1,0:T(8,128)S(1)}, f32[24,32,128]{2,1,0:T(8,128)S(1)}, u32[]{:S(2)}, u32[]{:S(2)}) collective-permute-start(f32[24,32,128]{2,1,0:T(8,128)S(1)} %get-tuple-element.222), channel_id=1, source_target_pairs={{0,16},{8,24},{16,0},{24,8},{1,17},{9,25},{17,1},{25,9},{2,18},{10... | collective-permute-start | bytes 1179656 | tf_op jit(solution)/shard_map/ppermute | solution.py:39
  119.7 8.1 %collective-permute-start.28 = (f32[16,32,128]{2,1,0:T(8,128)S(1)}, f32[16,32,128]{2,1,0:T(8,128)S(1)}, u32[]{:S(2)}, u32[]{:S(2)}) collective-permute-start(f32[16,32,128]{2,1,0:T(8,128)S(1)} %pad_maximum_fusion.4), channel_id=1, source_target_pairs={{0,8},{8,0},{16,24},{24,16},{1,9},{9,1},{17,25},{25,17},{2,10},{10... | collective-permute-start | bytes 786440 | tf_op jit(solution)/shard_map/ppermute | solution.py:39
  120.8 9.7 %collective-permute-start.31 = (f32[16,32,128]{2,1,0:T(8,128)S(1)}, f32[16,32,128]{2,1,0:T(8,128)S(1)}, u32[]{:S(2)}, u32[]{:S(2)}) collective-permute-start(f32[16,32,128]{2,1,0:T(8,128)S(1)} %pad_maximum_fusion.5), channel_id=1, source_target_pairs={{0,2},{2,0},{1,3},{3,1},{4,6},{6,4},{5,7},{7,5},{8,10},{10,8},{9,1... | collective-permute-start | bytes 786440 | tf_op jit(solution)/shard_map/ppermute | solution.py:39
  125.4 15.0 %collective-permute-start.26 = (f32[32,32,128]{2,1,0:T(8,128)S(1)}, f32[32,32,128]{2,1,0:T(8,128)S(1)}, u32[]{:S(2)}, u32[]{:S(2)}) collective-permute-start(f32[32,32,128]{2,1,0:T(8,128)S(1)} %constant_dynamic-update-slice_fusion.15.refs_0_), channel_id=1, source_target_pairs={{0,2},{2,0},{1,3},{3,1},{4,6},{6,4},{5,7},{7,5},{8,10},{10,8},{9,1... | collective-permute-start | bytes 1572872 | tf_op jit(solution)/shard_map/ppermute | solution.py:39
  127.9 12.5 %collective-permute-start.29 = (f32[32,32,128]{2,1,0:T(8,128)S(1)}, f32[32,32,128]{2,1,0:T(8,128)S(1)}, u32[]{:S(2)}, u32[]{:S(2)}) collective-permute-start(f32[32,32,128]{2,1,0:T(8,128)S(1)} %constant_dynamic-update-slice_fusion.18.refs_1_), channel_id=1, source_target_pairs={{0,4},{4,0},{1,5},{5,1},{2,6},{6,2},{3,7},{7,3},{8,12},{12,8},{9,1... | collective-permute-start | bytes 1572872 | tf_op jit(solution)/shard_map/ppermute | solution.py:39
  130.5 9.9 %collective-permute-start.32 = (f32[32,32,128]{2,1,0:T(8,128)S(1)}, f32[32,32,128]{2,1,0:T(8,128)S(1)}, u32[]{:S(2)}, u32[]{:S(2)}) collective-permute-start(f32[32,32,128]{2,1,0:T(8,128)S(1)} %constant_dynamic-update-slice_fusion.21.refs_2_), channel_id=1, source_target_pairs={{0,8},{8,0},{16,24},{24,16},{1,9},{9,1},{17,25},{25,17},{2,10},{10... | collective-permute-start | bytes 1572872 | tf_op jit(solution)/shard_map/ppermute | solution.py:39
  148.5 10.9 %collective-permute-start.33 = (f32[32,32,128]{2,1,0:T(8,128)}, f32[32,32,128]{2,1,0:T(8,128)S(1)}, u32[]{:S(2)}, u32[]{:S(2)}) collective-permute-start(f32[32,32,128]{2,1,0:T(8,128)} %get-tuple-element.144), channel_id=1, source_target_pairs={{0,2},{2,0},{1,3},{3,1},{4,6},{6,4},{5,7},{7,5},{8,10},{10,8},{9,1... | collective-permute-start | bytes 1572872 | tf_op jit(solution)/shard_map/ppermute | solution.py:39
  149.6 12.7 %collective-permute-start.36 = (f32[32,32,128]{2,1,0:T(8,128)}, f32[32,32,128]{2,1,0:T(8,128)S(1)}, u32[]{:S(2)}, u32[]{:S(2)}) collective-permute-start(f32[32,32,128]{2,1,0:T(8,128)} %get-tuple-element.153), channel_id=1, source_target_pairs={{0,4},{4,0},{1,5},{5,1},{2,6},{6,2},{3,7},{7,3},{8,12},{12,8},{9,1... | collective-permute-start | bytes 1572872 | tf_op jit(solution)/shard_map/ppermute | solution.py:39
  152.2 13.5 %collective-permute-start.39 = (f32[32,32,128]{2,1,0:T(8,128)}, f32[32,32,128]{2,1,0:T(8,128)S(1)}, u32[]{:S(2)}, u32[]{:S(2)}) collective-permute-start(f32[32,32,128]{2,1,0:T(8,128)} %get-tuple-element.162), channel_id=1, source_target_pairs={{0,8},{8,0},{16,24},{24,16},{1,9},{9,1},{17,25},{25,17},{2,10},{10... | collective-permute-start | bytes 1572872 | tf_op jit(solution)/shard_map/ppermute | solution.py:39
  160.5 7.8 %collective-permute-start.34 = (f32[16,32,128]{2,1,0:T(8,128)S(1)}, f32[16,32,128]{2,1,0:T(8,128)S(1)}, u32[]{:S(2)}, u32[]{:S(2)}) collective-permute-start(f32[16,32,128]{2,1,0:T(8,128)S(1)} %slice_add_fusion.5), channel_id=1, source_target_pairs={{0,4},{4,0},{1,5},{5,1},{2,6},{6,2},{3,7},{7,3},{8,12},{12,8},{9,1... | collective-permute-start | bytes 786440 | tf_op jit(solution)/shard_map/ppermute | solution.py:39
  177.4 13.8 %collective-permute-start.42 = (f32[24,32,128]{2,1,0:T(8,128)S(1)}, f32[24,32,128]{2,1,0:T(8,128)S(1)}, u32[]{:S(2)}, u32[]{:S(2)}) collective-permute-start(f32[24,32,128]{2,1,0:T(8,128)S(1)} %get-tuple-element.210), channel_id=1, source_target_pairs={{0,16},{8,24},{16,0},{24,8},{1,17},{9,25},{17,1},{25,9},{2,18},{10... | collective-permute-start | bytes 1179656 | tf_op jit(solution)/shard_map/ppermute | solution.py:39
  196.6 9.3 %collective-permute-start.44 = (f32[16,32,128]{2,1,0:T(8,128)S(1)}, f32[16,32,128]{2,1,0:T(8,128)S(1)}, u32[]{:S(2)}, u32[]{:S(2)}) collective-permute-start(f32[16,32,128]{2,1,0:T(8,128)S(1)} %pad_maximum_fusion.6), channel_id=1, source_target_pairs={{0,4},{4,0},{1,5},{5,1},{2,6},{6,2},{3,7},{7,3},{8,12},{12,8},{9,1... | collective-permute-start | bytes 786440 | tf_op jit(solution)/shard_map/ppermute | solution.py:39
  198.2 8.8 %collective-permute-start.47 = (f32[16,32,128]{2,1,0:T(8,128)S(1)}, f32[16,32,128]{2,1,0:T(8,128)S(1)}, u32[]{:S(2)}, u32[]{:S(2)}) collective-permute-start(f32[16,32,128]{2,1,0:T(8,128)S(1)} %pad_maximum_fusion.7), channel_id=1, source_target_pairs={{0,8},{8,0},{16,24},{24,16},{1,9},{9,1},{17,25},{25,17},{2,10},{10... | collective-permute-start | bytes 786440 | tf_op jit(solution)/shard_map/ppermute | solution.py:39
  205.9 11.1 %collective-permute-start.45 = (f32[32,32,128]{2,1,0:T(8,128)S(1)}, f32[32,32,128]{2,1,0:T(8,128)S(1)}, u32[]{:S(2)}, u32[]{:S(2)}) collective-permute-start(f32[32,32,128]{2,1,0:T(8,128)S(1)} %constant_dynamic-update-slice_fusion.30.refs_0_), channel_id=1, source_target_pairs={{0,2},{2,0},{1,3},{3,1},{4,6},{6,4},{5,7},{7,5},{8,10},{10,8},{9,1... | collective-permute-start | bytes 1572872 | tf_op jit(solution)/shard_map/ppermute | solution.py:39
  207.1 10.0 %collective-permute-start.48 = (f32[32,32,128]{2,1,0:T(8,128)S(1)}, f32[32,32,128]{2,1,0:T(8,128)S(1)}, u32[]{:S(2)}, u32[]{:S(2)}) collective-permute-start(f32[32,32,128]{2,1,0:T(8,128)S(1)} %constant_dynamic-update-slice_fusion.33.refs_1_), channel_id=1, source_target_pairs={{0,4},{4,0},{1,5},{5,1},{2,6},{6,2},{3,7},{7,3},{8,12},{12,8},{9,1... | collective-permute-start | bytes 1572872 | tf_op jit(solution)/shard_map/ppermute | solution.py:39
  207.2 9.9 %collective-permute-start.51 = (f32[32,32,128]{2,1,0:T(8,128)S(1)}, f32[32,32,128]{2,1,0:T(8,128)S(1)}, u32[]{:S(2)}, u32[]{:S(2)}) collective-permute-start(f32[32,32,128]{2,1,0:T(8,128)S(1)} %constant_dynamic-update-slice_fusion.36.refs_2_), channel_id=1, source_target_pairs={{0,8},{8,0},{16,24},{24,16},{1,9},{9,1},{17,25},{25,17},{2,10},{10... | collective-permute-start | bytes 1572872 | tf_op jit(solution)/shard_map/ppermute | solution.py:39
  225.1 12.1 %collective-permute-start.58 = (f32[32,32,128]{2,1,0:T(8,128)}, f32[32,32,128]{2,1,0:T(8,128)S(1)}, u32[]{:S(2)}, u32[]{:S(2)}) collective-permute-start(f32[32,32,128]{2,1,0:T(8,128)} %get-tuple-element.194), channel_id=1, source_target_pairs={{0,8},{8,0},{16,24},{24,16},{1,9},{9,1},{17,25},{25,17},{2,10},{10... | collective-permute-start | bytes 1572872 | tf_op jit(solution)/shard_map/ppermute | solution.py:39
  226.4 13.6 %collective-permute-start.55 = (f32[32,32,128]{2,1,0:T(8,128)}, f32[32,32,128]{2,1,0:T(8,128)S(1)}, u32[]{:S(2)}, u32[]{:S(2)}) collective-permute-start(f32[32,32,128]{2,1,0:T(8,128)} %get-tuple-element.185), channel_id=1, source_target_pairs={{0,4},{4,0},{1,5},{5,1},{2,6},{6,2},{3,7},{7,3},{8,12},{12,8},{9,1... | collective-permute-start | bytes 1572872 | tf_op jit(solution)/shard_map/ppermute | solution.py:39
  227.9 14.6 %collective-permute-start.52 = (f32[32,32,128]{2,1,0:T(8,128)}, f32[32,32,128]{2,1,0:T(8,128)S(1)}, u32[]{:S(2)}, u32[]{:S(2)}) collective-permute-start(f32[32,32,128]{2,1,0:T(8,128)} %get-tuple-element.176), channel_id=1, source_target_pairs={{0,2},{2,0},{1,3},{3,1},{4,6},{6,4},{5,7},{7,5},{8,10},{10,8},{9,1... | collective-permute-start | bytes 1572872 | tf_op jit(solution)/shard_map/ppermute | solution.py:39
  259.2 10.8 %all-to-all-start = ((f32[32,1,128]{2,1,0:T(1,128)}), f32[32,1,128]{2,1,0:T(1,128)S(1)}, u32[]{:S(2)}, u32[]{:S(2)}) async-start(f32[32,1,128]{2,1,0:T(1,128)} %broadcast_in_dim.60), calls=%async_computation | async-start | bytes 32768 | tf_op jit(solution)/shard_map/all_to_all | solution.py:348
  262.8 12.5 %collective-permute-start.61 = (f32[12,32,128]{2,1,0:T(8,128)S(1)}, f32[12,32,128]{2,1,0:T(8,128)S(1)}, u32[]{:S(2)}, u32[]{:S(2)}) collective-permute-start(f32[12,32,128]{2,1,0:T(8,128)S(1)} %get-tuple-element.203), channel_id=1, source_target_pairs={{0,16},{8,24},{16,0},{24,8},{1,17},{9,25},{17,1},{25,9},{2,18},{10... | collective-permute-start | bytes 589832 | tf_op jit(solution)/shard_map/ppermute | solution.py:39
  (77 other events, 445.5 us)

commit v10 on v9

--- a/solution.py
+++ b/solution.py
@@ -2,6 +2,7 @@
 
 import jax
 import jax.numpy as jnp
+import numpy as np
 from jax import lax
 from jax.experimental import pallas as pl
 from jax.experimental.pallas import tpu as pltpu
@@ -14,10 +15,12 @@
 UNROLL = 8
 CHUNK = 8
 SLOTS = 8
+SPANS = 4
 VMEM = 60 * 1024 * 1024
 CHIPS = ("z", "y", "x")
 ALL = ("z", "y", "x", "core")
-NEAR = ("x", "y", "z")
+AXES = ("x", "y", "z")
+PARTS = ((2, ("xzy", "yxz")), (1, ("zyx", "zyx")))
 
 
 def depth_of(n_rows):
@@ -25,18 +28,26 @@
 
 
 def far_steps():
-    return [(a, 1 << k) for a in NEAR for k in range(1, lax.axis_size(a).bit_length() - 1)]
+    return [(a + a, 1 << k) for a in AXES for k in range(1, lax.axis_size(a).bit_length() - 1)]
 
 
 def near_steps(part):
-    turn = part % len(NEAR)
-    return [(a, 1) for a in NEAR[turn:] + NEAR[:turn]]
+    return [(axes, 1) for axes in zip(*PARTS[part][1])]
 
 
 def swap(array, step):
-    axis, distance = step
-    pairs = [(i, i ^ distance) for i in range(lax.axis_size(axis))]
-    return lax.ppermute(array, axis, pairs)
+    axes, distance = step
+    sizes = [lax.axis_size(a) for a in CHIPS]
+    pairs = []
+    for at in np.ndindex(*sizes, CORES):
+        to = list(at)
+        to[CHIPS.index(axes[at[-1]])] ^= distance
+        pairs.append([int(np.ravel_multi_index(i, sizes + [CORES])) for i in (at, to)])
+    return lax.ppermute(array, ALL, pairs)
+
+
+def swap_cores(array):
+    return lax.ppermute(array, "core", [(0, 1), (1, 0)])
 
 
 def after(value, *others):
@@ -60,10 +71,13 @@
     starts = [
         jnp.concatenate([b[low:high] for b in blocks], axis=0) for low, high in zip(edges[:-1], edges[1:])
     ]
+    starts = lax.optimization_barrier(starts)
+    got = [swap(block, near_steps(part)[-1]) for part, block in enumerate(starts)]
     pieces = []
-    for part, block in enumerate(lax.optimization_barrier(starts)):
+    for part, (block, more) in enumerate(zip(starts, lax.optimization_barrier(got))):
+        block = jnp.concatenate([block, more], axis=0)
         steps = near_steps(part)
-        for step in reversed(steps[1:]):
+        for step in reversed(steps[1:-1]):
             block = jnp.concatenate([block, swap(block, step)], axis=0)
         pieces.append((block, swap(block, steps[0])))
     return pieces
@@ -86,11 +100,12 @@
     return [jnp.concatenate(group, axis=0) for group in zip(*parts)]
 
 
-def reduce_far(blocks):
+def reduce_far(blocks, beside):
     for step in far_steps():
         middle = len(blocks) // 2
         send = blocks[middle:]
         got = swap(jnp.concatenate(send, axis=0) if middle > 1 else send[0], step)
+        got = after(got, beside)
         blocks = [b + g for b, g in zip(blocks[:middle], jnp.split(got, middle))]
     return blocks[0]
 
@@ -137,12 +152,12 @@
     )(tiles, *given)
 
 
-def apply_kernel(span, skip, counts, has_base, ends_ref, order_ref, row_ref, col_ref, pairs_ref, *refs):
+def apply_kernel(span, skip, counts, has_base, places_ref, pairs_ref, *refs):
     ends, refs = refs[: len(counts)], refs[len(counts) :]
     base_ref, refs = (refs[0], refs[1:]) if has_base else (None, refs)
     *outs, flux_ref, sum_ref, held_ref, sem, held_sem = refs
-    total = order_ref.shape[0]
-    start, stop = ends_ref[span], ends_ref[span + 1]
+    total = pairs_ref.shape[0]
+    start, stop = places_ref[span], places_ref[span + 1]
     chunks = (stop - start + CHUNK - 1) // CHUNK
 
     def fetch(chunk):
@@ -150,7 +165,7 @@
         for k in range(CHUNK):
             at = jnp.minimum(start + chunk * CHUNK + k, total - 1)
             pltpu.make_async_copy(
-                pairs_ref.at[order_ref[at]], held_ref.at[slot, k], held_sem.at[slot]
+                pairs_ref.at[places_ref[SPANS + at]], held_ref.at[slot, k], held_sem.at[slot]
             ).start()
 
     copies = [
@@ -190,7 +205,7 @@
             at = start + chunk * CHUNK + k
             valid = jnp.where(at < stop, 1.0, 0.0)
             at = jnp.minimum(at, stop - 1)
-            flux = flux_ref[col_ref[at]] * valid
+            flux = flux_ref[places_ref[SPANS + 2 * total + at]] * valid
             high = flux.astype(jnp.bfloat16)
             low = (flux - high.astype(jnp.float32)).astype(jnp.bfloat16)
             left = jnp.concatenate([high, low], axis=0)
@@ -201,7 +216,7 @@
             )
             temps = flux.shape[0]
             products.append(both[:temps] + both[temps:])
-            rows.append(row_ref[at] - skip)
+            rows.append(places_ref[SPANS + total + at] - skip)
         for row, product in zip(rows, products):
             sum_ref[row] += product
 
@@ -226,7 +241,7 @@
         functools.partial(apply_kernel, span, skip, counts, base is not None),
         out_shape=[jax.ShapeDtypeStruct((n, temps, size), jnp.float32) for n in sizes],
         grid_spec=pltpu.PrefetchScalarGridSpec(
-            num_scalar_prefetch=4,
+            num_scalar_prefetch=1,
             grid=(),
             in_specs=[anywhere] * len(given),
             out_specs=[anywhere] * len(sizes),
@@ -244,7 +259,7 @@
             bytes_accessed=int(share * total * size * size * 4) + 8 * sum(sizes) * temps * size,
             transcendentals=0,
         ),
-    )(*places, *given)
+    )(places, *given)
 
 
 def shards(
@@ -259,9 +274,9 @@
     num = chips * chip_tiles
     half = columns // CORES
     core = lax.axis_index("core")
-    cores = ("core", 1)
-
-    edges = [chip_tiles * k // len(NEAR) for k in range(len(NEAR) + 1)]
+
+    thirds = [sum(third for third, _ in PARTS[:k]) for k in range(len(PARTS) + 1)]
+    edges = [chip_tiles * third // thirds[-1] for third in thirds]
 
     def place(tile):
         chip, inside = tile // chip_tiles, tile % chip_tiles
@@ -271,35 +286,39 @@
             away[axis] = ((chip // width) % n) ^ lax.axis_index(axis)
             width *= n
         side, out = jnp.zeros_like(tile), jnp.zeros_like(tile)
-        for part in range(len(NEAR)):
+        for part in range(len(PARTS)):
             low, high = edges[part], edges[part + 1]
-            (first, _), *steps = near_steps(part)
+            bits = [
+                (jnp.where(core == 0, away[axes[0]], away[axes[1]]) // distance) % 2
+                for axes, distance in near_steps(part) + far_steps()
+            ]
             slot = jnp.zeros_like(tile)
-            for axis, distance in steps + far_steps():
-                slot = 2 * slot + (away[axis] // distance) % 2
+            for bit in bits[1:]:
+                slot = 2 * slot + bit
             slot = chips // 2 * low + slot * (high - low) + inside - low
             out = jnp.where(inside >= low, slot, out)
-            side = jnp.where(inside >= low, away[first] % 2, side)
+            side = jnp.where(inside >= low, bits[0], side)
         return side, out
 
     owners = tile_owner[:, 0]
-    row_side, row = place((owners // n_cols) * (n_cols * per) + tile_row)
-    col_side, col = place(((tile_col // per) * n_cols + owners % n_cols) * per + tile_col % per)
+    row = (owners // n_cols) * (n_cols * per) + tile_row
+    col = ((tile_col // per) * n_cols + owners % n_cols) * per + tile_col % per
     used = jnp.arange(length, dtype=jnp.int32) < tile_count[0]
-    kind = jnp.where(used, jnp.where(col_side == 0, 0, 2 - row_side), 3)
+    code = jnp.where(used, row * num + col, num * num)
+    other_code = swap_cores(code)
+    code = jnp.concatenate([code, other_code])
+    row_side, row = place(code // num % num)
+    col_side, col = place(code % num)
+    kind = jnp.where(code < num * num, jnp.where(col_side == 0, 0, 2 - row_side), 3)
     row = jnp.where(row_side == 1, row, row + num // 2)
-    code = (kind * num + row) * num + col
-    other_code = swap(code, cores)
-    code = jnp.concatenate([code, other_code])
-    kind = code // (num * num)
     slots = jnp.arange(CORES * length, dtype=jnp.int32)
     key = kind * (CORES * length) + slots
     rank = jnp.sum((key[None, :] < key[:, None]).astype(jnp.int32), axis=1)
-    ends = jnp.sum((kind[None, :] < jnp.arange(4, dtype=jnp.int32)[:, None]).astype(jnp.int32), axis=1)
+    ends = jnp.sum((kind[None, :] < jnp.arange(SPANS, dtype=jnp.int32)[:, None]).astype(jnp.int32), axis=1)
     sorts = rank[None, :] == slots[:, None]
     order = jnp.sum(jnp.where(sorts, slots[None, :], 0), axis=1)
-    code = jnp.sum(jnp.where(sorts, code[None, :] % (num * num), 0), axis=1)
-    places = (ends, order, code // num, code % num)
+    code = jnp.sum(jnp.where(sorts, (row * num + col)[None, :], 0), axis=1)
+    places = jnp.concatenate([ends, order, code // num, code % num])
 
     def by_core(own, other):
         return jnp.concatenate(
@@ -313,9 +332,9 @@
     mine = jnp.where(core == 0, low, high)
     theirs = jnp.where(core == 0, high, low)
     packed = [theirs, jnp.broadcast_to(relax, (per, 8, size)), jnp.broadcast_to(heat, (per, 8, size))]
-    got = swap(jnp.concatenate(packed, axis=1), cores)
+    got = swap_cores(jnp.concatenate(packed, axis=1))
     tile_values = after(tile_values, got, other_code)
-    other_values = swap(tile_values, cores)
+    other_values = swap_cores(tile_values)
     drive_half = by_core(mine, got[:, :half])
     relax_both = by_core(relax, got[:, half : half + 1])
     heat_both = by_core(heat, got[:, half + 8 : half + 9])
@@ -344,16 +363,15 @@
     )
     totals = jnp.concatenate([weighted, jnp.sum(heat).reshape(1)])
     totals = jnp.pad(totals[None], ((0, 0), (0, size - half - 1)))
-    *blocks, totals = lax.optimization_barrier((*blocks, totals))
     totals = lax.all_to_all(
         jnp.broadcast_to(totals, (chips * CORES, size)), ALL, split_axis=0, concat_axis=0, tiled=True
     )
     totals = jnp.sum(totals.reshape(chips, CORES, size), axis=0)
     conductivity = totals[:, :half].reshape(columns) / jnp.sum(totals[:, half])
-    flux = relax_both * (drive_half + after(reduce_far(blocks), conductivity))
+    flux = relax_both * (drive_half + reduce_far(blocks, conductivity))
     first, second = flux[:per], flux[per:]
     mine = jnp.where(core == 0, first, second)
-    got = swap(jnp.where(core == 0, second, first), cores)
+    got = swap_cores(jnp.where(core == 0, second, first))
     both = jnp.concatenate(
         [jnp.where(core == 0, mine, got), jnp.where(core == 0, got, mine)], axis=1
     )

time: 278 us -> 324 us (1.17)
  waiting for transfers between devices: 76.7 us -> 142 us
  starting transfers between devices: 79.6 us -> 60.9 us
    ppermute x63 -> x45, waiting for transfers between devices: 72.3 us -> 137 us  [the longest x41 135 us: swap(): return lax.ppermute(array, ALL, pairs)]
    ppermute x63 -> x45, starting transfers between devices: 76 us -> 53.2 us  [the longest x41 52.3 us: swap(): return lax.ppermute(array, ALL, pairs)]
    all_to_all x1, starting transfers between devices: 3.6 us -> 7.77 us  [shards(): lax.all_to_all(jnp.broadcast_to(totals, (chips * CORES, size)), ALL, spli...]
    add x18 -> x12, other arithmetic: 8.89 us -> 7.1 us  [reduce_near(): sum([halves(t)[1] for t in terms[1:]], halves(terms[0])[1])]
  transfers between devices with their start and end apart: 64 -> 46, of which waited for: 34 -> 30; matrix products, arithmetic and copies ran while one was open for 6% -> 5% of each run, Pallas kernels for 25% -> 21%
where the time goes in v10:
time: 324 us; the launch traced here: 322 us
  waiting for transfers between devices  142 us (44%)
  Pallas kernels  90.2 us (28%)
  starting transfers between devices  60.9 us (19%)
  other arithmetic  17.2 us (5%)
  local copies, waits for them, and re-layouts  9.83 us (3%)
    ppermute x41, waiting for transfers between devices, swap(): return lax.ppermute(array, ALL, pairs)  135 us
    pallas_call x9, Pallas kernels, apply_tiles(): pl.pallas_call(functools.partial(apply_kernel, span, skip, counts, base i...  69.6 us
    ppermute x41, starting transfers between devices, swap(): return lax.ppermute(array, ALL, pairs)  52.3 us
    pallas_call x2, Pallas kernels, split_tiles(): pl.pallas_call(split_kernel, out_shape=jax.ShapeDtypeStruct((CORES * leng...  20.6 us
    all_to_all x1, starting transfers between devices, shards(): lax.all_to_all(jnp.broadcast_to(totals, (chips * CORES, size)), ALL, spli...  7.77 us
    add x12, other arithmetic, reduce_near(): sum([halves(t)[1] for t in terms[1:]], halves(terms[0])[1])  7.1 us
  transfers between devices with their start and end apart: 46, of which 30 were waited for; matrix products, arithmetic and copies ran while one was open for 5% of the time, Pallas kernels for 21%

profile of v10, /device:TPU:0, one launch (start us, length us, event | category | flops | bytes accessed | tf_op | source)
XLA Modules:
  0.0 322.1 jit_solution(7791506463582835327)
XLA Ops:
  7.7 4.0 %collective-permute-start.3 = (f32[12,2,128]{2,0,1:T(8,128)S(1)}, f32[12,2,128]{2,0,1:T(8,128)S(1)}, u32[]{:S(2)}, u32[]{:S(2)}) collective-permute-start(f32[12,2,128]{2,0,1:T(8,128)S(1)} %pad_maximum_fusion.18), channel_id=1, source_target_pairs={{0,16},{1,17},{2,18},{3,19},{4,20},{5,21},{6,22},{7,23},{8,24},{9,... | collective-permute-start | bytes 36872 | tf_op jit(solution)/shard_map/ppermute | solution.py:46
  12.3 10.3 %shard_map.95.refs_0_ = bf16[256,256,128]{2,1,0:T(8,128)(2,1)} custom-call(f32[128,128,128]{2,1,0:T(8,128)} %tile_ref), custom_call_target="tpu_custom_call" | custom-call | flops 6291456 | bytes 16777216 | tf_op jit(solution)/shard_map/pallas_call | solution.py:140
  33.2 6.5 %collective-permute-done.7 = f32[32,32,128]{2,1,0:T(8,128)S(1)} collective-permute-done((f32[32,32,128]{2,1,0:T(8,128)S(1)}, f32[32,32,128]{2,1,0:T(8,128)S(1)}, u32[]{:S(2)}, u32[]{:S(2)}) %collective-permute-start.7) | collective-permute-done | bytes 524320 | tf_op jit(solution)/shard_map/ppermute | solution.py:46
  43.7 10.3 %shard_map.96.pairs_ref = bf16[256,256,128]{2,1,0:T(8,128)(2,1)} custom-call(f32[128,128,128]{2,1,0:T(8,128)} %collective-permute-done.2.tile_ref, bf16[256,256,128]{2,1,0:T(8,128)(2,1)} %shard_map.95.refs_0_), custom_call_target="tpu_custom_call", output_to_operand_aliasing={{}: (1, {})} | custom-call | flops 6291456 | bytes 16777216 | tf_op jit(solution)/shard_map/pallas_call | solution.py:140
  54.0 8.4 %shard_map.97 = (f32[96,32,128]{2,1,0:T(8,128)}, f32[96,32,128]{2,1,0:T(8,128)}) custom-call(s32[772]{0:T(1024)} %pad_add_fusion.places_ref, bf16[256,256,128]{2,1,0:T(8,128)(2,1)} %shard_map.96.pairs_ref, f32[64,32,128]{2,1,0:T(8,128)} %copy-done.8, f32[32,32,128]{2,1,0:T(8,128)} %copy-done.14), custom_call_target="tpu_custom_call" | custom-call | flops 536870912 | bytes 14680064 | tf_op jit(solution)/shard_map/pallas_call | solution.py:240
  63.5 7.4 %shard_map.99 = (f32[64,32,128]{2,1,0:T(8,128)}, f32[32,32,128]{2,1,0:T(8,128)}) custom-call(s32[772]{0:T(1024)} %pad_add_fusion.places_ref, bf16[256,256,128]{2,1,0:T(8,128)(2,1)} %shard_map.96.pairs_ref, f32[64,32,128]{2,1,0:T(8,128)} %copy-done.2, f32[32,32,128]{2,1,0:T(8,128)} %copy-done.5, f32[96,32,128]{2,1,0:T(8,128)} %get-tuple-element.85.refs_2_), custom_call_target="tpu_custom_call" | custom-call | flops 268435456 | bytes 7340032 | tf_op jit(solution)/shard_map/pallas_call | solution.py:240
  73.0 7.4 %shard_map.98 = (f32[64,32,128]{2,1,0:T(8,128)}, f32[32,32,128]{2,1,0:T(8,128)}) custom-call(s32[772]{0:T(1024)} %pad_add_fusion.places_ref, bf16[256,256,128]{2,1,0:T(8,128)(2,1)} %shard_map.96.pairs_ref, f32[64,32,128]{2,1,0:T(8,128)} %copy-done.2, f32[32,32,128]{2,1,0:T(8,128)} %copy-done.5, f32[96,32,128]{2,1,0:T(8,128)} %get-tuple-element.83.refs_2_), custom_call_target="tpu_custom_call" | custom-call | flops 268435456 | bytes 7340032 | tf_op jit(solution)/shard_map/pallas_call | solution.py:240
  80.4 5.6 %collective-permute-done.11 = f32[64,32,128]{2,1,0:T(8,128)S(1)} collective-permute-done((f32[64,32,128]{2,1,0:T(8,128)}, f32[64,32,128]{2,1,0:T(8,128)S(1)}, u32[]{:S(2)}, u32[]{:S(2)}) %collective-permute-start.11) | collective-permute-done | bytes 1048608 | tf_op jit(solution)/shard_map/ppermute | solution.py:46
  89.9 5.0 %collective-permute-done.15 = f32[16,32,128]{2,1,0:T(8,128)S(1)} collective-permute-done((f32[16,32,128]{2,1,0:T(8,128)S(1)}, f32[16,32,128]{2,1,0:T(8,128)S(1)}, u32[]{:S(2)}, u32[]{:S(2)}) %collective-permute-start.15) | collective-permute-done | bytes 262176 | tf_op jit(solution)/shard_map/ppermute | solution.py:46
  100.1 3.7 %collective-permute-done.13 = f32[16,32,128]{2,1,0:T(8,128)S(1)} collective-permute-done((f32[16,32,128]{2,1,0:T(8,128)S(1)}, f32[16,32,128]{2,1,0:T(8,128)S(1)}, u32[]{:S(2)}, u32[]{:S(2)}) %collective-permute-start.13) | collective-permute-done | bytes 262176 | tf_op jit(solution)/shard_map/ppermute | solution.py:46
  107.2 12.6 %collective-permute-done.17 = f32[24,32,128]{2,1,0:T(8,128)S(1)} collective-permute-done((f32[24,32,128]{2,1,0:T(8,128)S(1)}, f32[24,32,128]{2,1,0:T(8,128)S(1)}, u32[]{:S(2)}, u32[]{:S(2)}) %collective-permute-start.17) | collective-permute-done | bytes 393248 | tf_op jit(solution)/shard_map/ppermute | solution.py:46
  122.1 4.1 %collective-permute-done.19 = f32[8,32,128]{2,1,0:T(8,128)S(1)} collective-permute-done((f32[8,32,128]{2,1,0:T(8,128)S(1)}, f32[8,32,128]{2,1,0:T(8,128)S(1)}, u32[]{:S(2)}, u32[]{:S(2)}) %collective-permute-start.19) | collective-permute-done | bytes 131104 | tf_op jit(solution)/shard_map/ppermute | solution.py:46
  126.7 9.1 %collective-permute-done.20 = f32[32,32,128]{2,1,0:T(8,128)S(1)} collective-permute-done((f32[32,32,128]{2,1,0:T(8,128)S(1)}, f32[32,32,128]{2,1,0:T(8,128)S(1)}, u32[]{:S(2)}, u32[]{:S(2)}) %collective-permute-start.20) | collective-permute-done | bytes 524320 | tf_op jit(solution)/shard_map/ppermute | solution.py:46
  138.0 7.8 %collective-permute-done.22 = f32[16,32,128]{2,1,0:T(8,128)S(1)} collective-permute-done((f32[16,32,128]{2,1,0:T(8,128)S(1)}, f32[16,32,128]{2,1,0:T(8,128)S(1)}, u32[]{:S(2)}, u32[]{:S(2)}) %collective-permute-start.22) | collective-permute-done | bytes 262176 | tf_op jit(solution)/shard_map/ppermute | solution.py:46
  146.6 8.4 %shard_map.100 = (f32[96,32,128]{2,1,0:T(8,128)}, f32[96,32,128]{2,1,0:T(8,128)}) custom-call(s32[772]{0:T(1024)} %pad_add_fusion.places_ref, bf16[256,256,128]{2,1,0:T(8,128)(2,1)} %shard_map.96.pairs_ref, f32[64,32,128]{2,1,0:T(8,128)} %copy-done.9, f32[32,32,128]{2,1,0:T(8,128)} %copy-done.15), custom_call_target="tpu_custom_call" | custom-call | flops 536870912 | bytes 14680064 | tf_op jit(solution)/shard_map/pallas_call | solution.py:240
  156.3 7.4 %shard_map.102 = (f32[64,32,128]{2,1,0:T(8,128)}, f32[32,32,128]{2,1,0:T(8,128)}) custom-call(s32[772]{0:T(1024)} %pad_add_fusion.places_ref, bf16[256,256,128]{2,1,0:T(8,128)(2,1)} %shard_map.96.pairs_ref, f32[64,32,128]{2,1,0:T(8,128)} %copy-done.4, f32[32,32,128]{2,1,0:T(8,128)} %copy-done.7, f32[96,32,128]{2,1,0:T(8,128)} %get-tuple-element.109.refs_2_), custom_call_target="tpu_custom_call" | custom-call | flops 268435456 | bytes 7340032 | tf_op jit(solution)/shard_map/pallas_call | solution.py:240
  167.0 7.4 %shard_map.101 = (f32[64,32,128]{2,1,0:T(8,128)}, f32[32,32,128]{2,1,0:T(8,128)}) custom-call(s32[772]{0:T(1024)} %pad_add_fusion.places_ref, bf16[256,256,128]{2,1,0:T(8,128)(2,1)} %shard_map.96.pairs_ref, f32[64,32,128]{2,1,0:T(8,128)} %copy-done.4, f32[32,32,128]{2,1,0:T(8,128)} %copy-done.7, f32[96,32,128]{2,1,0:T(8,128)} %get-tuple-element.107.refs_2_), custom_call_target="tpu_custom_call" | custom-call | flops 268435456 | bytes 7340032 | tf_op jit(solution)/shard_map/pallas_call | solution.py:240
  174.4 4.3 %collective-permute-done.24 = f32[64,32,128]{2,1,0:T(8,128)S(1)} collective-permute-done((f32[64,32,128]{2,1,0:T(8,128)}, f32[64,32,128]{2,1,0:T(8,128)S(1)}, u32[]{:S(2)}, u32[]{:S(2)}) %collective-permute-start.24) | collective-permute-done | bytes 1048608 | tf_op jit(solution)/shard_map/ppermute | solution.py:46
  183.0 5.0 %collective-permute-done.28 = f32[16,32,128]{2,1,0:T(8,128)S(1)} collective-permute-done((f32[16,32,128]{2,1,0:T(8,128)S(1)}, f32[16,32,128]{2,1,0:T(8,128)S(1)}, u32[]{:S(2)}, u32[]{:S(2)}) %collective-permute-start.28) | collective-permute-done | bytes 262176 | tf_op jit(solution)/shard_map/ppermute | solution.py:46
  197.6 19.0 %collective-permute-done.30 = f32[24,32,128]{2,1,0:T(8,128)S(1)} collective-permute-done((f32[24,32,128]{2,1,0:T(8,128)S(1)}, f32[24,32,128]{2,1,0:T(8,128)S(1)}, u32[]{:S(2)}, u32[]{:S(2)}) %collective-permute-start.30) | collective-permute-done | bytes 393248 | tf_op jit(solution)/shard_map/ppermute | solution.py:46
  218.4 5.0 %collective-permute-done.32 = f32[8,32,128]{2,1,0:T(8,128)S(1)} collective-permute-done((f32[8,32,128]{2,1,0:T(8,128)S(1)}, f32[8,32,128]{2,1,0:T(8,128)S(1)}, u32[]{:S(2)}, u32[]{:S(2)}) %collective-permute-start.32) | collective-permute-done | bytes 131104 | tf_op jit(solution)/shard_map/ppermute | solution.py:46
  223.8 8.9 %collective-permute-done.33 = f32[32,32,128]{2,1,0:T(8,128)S(1)} collective-permute-done((f32[32,32,128]{2,1,0:T(8,128)S(1)}, f32[32,32,128]{2,1,0:T(8,128)S(1)}, u32[]{:S(2)}, u32[]{:S(2)}) %collective-permute-start.33) | collective-permute-done | bytes 524320 | tf_op jit(solution)/shard_map/ppermute | solution.py:46
  234.8 8.1 %collective-permute-done.35 = f32[16,32,128]{2,1,0:T(8,128)S(1)} collective-permute-done((f32[16,32,128]{2,1,0:T(8,128)S(1)}, f32[16,32,128]{2,1,0:T(8,128)S(1)}, u32[]{:S(2)}, u32[]{:S(2)}) %collective-permute-start.35) | collective-permute-done | bytes 262176 | tf_op jit(solution)/shard_map/ppermute | solution.py:46
  243.7 8.4 %shard_map.103 = (f32[96,32,128]{2,1,0:T(8,128)}, f32[96,32,128]{2,1,0:T(8,128)}) custom-call(s32[772]{0:T(1024)} %pad_add_fusion.places_ref, bf16[256,256,128]{2,1,0:T(8,128)(2,1)} %shard_map.96.pairs_ref, f32[64,32,128]{2,1,0:T(8,128)} %copy-done.10, f32[32,32,128]{2,1,0:T(8,128)} %copy-done.16), custom_call_target="tpu_custom_call" | custom-call | flops 536870912 | bytes 14680064 | tf_op jit(solution)/shard_map/pallas_call | solution.py:240
  253.3 7.4 %shard_map.105 = (f32[64,32,128]{2,1,0:T(8,128)}, f32[32,32,128]{2,1,0:T(8,128)}) custom-call(s32[772]{0:T(1024)} %pad_add_fusion.places_ref, bf16[256,256,128]{2,1,0:T(8,128)(2,1)} %shard_map.96.pairs_ref, f32[64,32,128]{2,1,0:T(8,128)} %copy-done.3, f32[32,32,128]{2,1,0:T(8,128)} %copy-done.6, f32[96,32,128]{2,1,0:T(8,128)} %get-tuple-element.133.refs_2_), custom_call_target="tpu_custom_call" | custom-call | flops 268435456 | bytes 7340032 | tf_op jit(solution)/shard_map/pallas_call | solution.py:240
  263.9 7.4 %shard_map.104 = (f32[64,32,128]{2,1,0:T(8,128)}, f32[32,32,128]{2,1,0:T(8,128)}) custom-call(s32[772]{0:T(1024)} %pad_add_fusion.places_ref, bf16[256,256,128]{2,1,0:T(8,128)(2,1)} %shard_map.96.pairs_ref, f32[64,32,128]{2,1,0:T(8,128)} %copy-done.3, f32[32,32,128]{2,1,0:T(8,128)} %copy-done.6, f32[96,32,128]{2,1,0:T(8,128)} %get-tuple-element.131.refs_2_), custom_call_target="tpu_custom_call" | custom-call | flops 268435456 | bytes 7340032 | tf_op jit(solution)/shard_map/pallas_call | solution.py:240
  271.3 4.5 %collective-permute-done.37 = f32[64,32,128]{2,1,0:T(8,128)S(1)} collective-permute-done((f32[64,32,128]{2,1,0:T(8,128)}, f32[64,32,128]{2,1,0:T(8,128)S(1)}, u32[]{:S(2)}, u32[]{:S(2)}) %collective-permute-start.37) | collective-permute-done | bytes 1048608 | tf_op jit(solution)/shard_map/ppermute | solution.py:46
  281.7 5.2 %collective-permute-done.41 = f32[16,32,128]{2,1,0:T(8,128)} collective-permute-done((f32[16,32,128]{2,1,0:T(8,128)}, f32[16,32,128]{2,1,0:T(8,128)}, u32[]{:S(2)}, u32[]{:S(2)}) %collective-permute-start.41) | collective-permute-done | bytes 262176 | tf_op jit(solution)/shard_map/ppermute | solution.py:46
  290.6 3.8 %collective-permute-done.42 = f32[8,32,128]{2,1,0:T(8,128)S(1)} collective-permute-done((f32[8,32,128]{2,1,0:T(8,128)S(1)}, f32[8,32,128]{2,1,0:T(8,128)S(1)}, u32[]{:S(2)}, u32[]{:S(2)}) %collective-permute-start.42) | collective-permute-done | bytes 131104 | tf_op jit(solution)/shard_map/ppermute | solution.py:46
  299.5 7.8 %all-to-all-start = ((f32[32,1,128]{2,1,0:T(1,128)}), f32[32,1,128]{2,1,0:T(1,128)S(1)}, u32[]{:S(2)}, u32[]{:S(2)}) async-start(f32[32,1,128]{2,1,0:T(1,128)} %broadcast_in_dim.65), calls=%async_computation | async-start | bytes 32768 | tf_op jit(solution)/shard_map/all_to_all | solution.py:366
  310.0 4.4 %all-to-all-done = f32[32,1,128]{2,1,0:T(1,128)S(1)} async-done(((f32[32,1,128]{2,1,0:T(1,128)}), f32[32,1,128]{2,1,0:T(1,128)S(1)}, u32[]{:S(2)}, u32[]{:S(2)}) %all-to-all-start) | async-done | bytes 16416 | tf_op jit(solution)/shard_map/all_to_all | solution.py:366
  316.3 3.6 %collective-permute-done.43 = f32[12,32,128]{2,1,0:T(8,128)S(1)} collective-permute-done((f32[12,32,128]{2,1,0:T(8,128)S(1)}, f32[12,32,128]{2,1,0:T(8,128)S(1)}, u32[]{:S(2)}, u32[]{:S(2)}) %collective-permute-start.43) | collective-permute-done | bytes 196640 | tf_op jit(solution)/shard_map/ppermute | solution.py:46
  (237 shorter events, 91.8 us)
Async XLA Ops:
  6.1 37.6 %collective-permute-start.2 = (f32[128,128,128]{2,1,0:T(8,128)}, f32[128,128,128]{2,1,0:T(8,128)}, u32[]{:S(2)}, u32[]{:S(2)}) collective-permute-start(f32[128,128,128]{2,1,0:T(8,128)} %tile_ref), channel_id=1, source_target_pairs={{0,1},{1,0},{2,3},{3,2},{4,5},{5,4},{6,7},{7,6},{8,9},{9,8},{10,11... | collective-permute-start | bytes 25165832 | tf_op jit(solution)/shard_map/ppermute | solution.py:50
  7.7 14.9 %collective-permute-start.3 = (f32[12,2,128]{2,0,1:T(8,128)S(1)}, f32[12,2,128]{2,0,1:T(8,128)S(1)}, u32[]{:S(2)}, u32[]{:S(2)}) collective-permute-start(f32[12,2,128]{2,0,1:T(8,128)S(1)} %pad_maximum_fusion.18), channel_id=1, source_target_pairs={{0,16},{1,17},{2,18},{3,19},{4,20},{5,21},{6,22},{7,23},{8,24},{9,... | collective-permute-start | bytes 36872 | tf_op jit(solution)/shard_map/ppermute | solution.py:46
  11.8 11.9 %collective-permute-start.4 = (f32[12,32,128]{2,1,0:T(8,128)S(1)}, f32[12,32,128]{2,1,0:T(8,128)S(1)}, u32[]{:S(2)}, u32[]{:S(2)}) collective-permute-start(f32[12,32,128]{2,1,0:T(8,128)S(1)} %get-tuple-element.183), channel_id=1, source_target_pairs={{0,16},{1,17},{2,18},{3,19},{4,20},{5,21},{6,22},{7,23},{8,24},{9,... | collective-permute-start | bytes 589832 | tf_op jit(solution)/shard_map/ppermute | solution.py:46
  23.8 6.6 %collective-permute-start.5 = (f32[16,32,128]{2,1,0:T(8,128)S(1)}, f32[16,32,128]{2,1,0:T(8,128)S(1)}, u32[]{:S(2)}, u32[]{:S(2)}) collective-permute-start(f32[16,32,128]{2,1,0:T(8,128)S(1)} %pad_maximum_fusion.5), channel_id=1, source_target_pairs={{0,4},{1,9},{2,6},{3,11},{4,0},{5,13},{6,2},{7,15},{8,12},{9,1},{1... | collective-permute-start | bytes 786440 | tf_op jit(solution)/shard_map/ppermute | solution.py:46
  30.4 9.2 %collective-permute-start.7 = (f32[32,32,128]{2,1,0:T(8,128)S(1)}, f32[32,32,128]{2,1,0:T(8,128)S(1)}, u32[]{:S(2)}, u32[]{:S(2)}) collective-permute-start(f32[32,32,128]{2,1,0:T(8,128)S(1)} %pad_maximum_fusion), channel_id=1, source_target_pairs={{0,8},{1,3},{2,10},{3,1},{4,12},{5,7},{6,14},{7,5},{8,0},{9,11},{1... | collective-permute-start | bytes 1572872 | tf_op jit(solution)/shard_map/ppermute | solution.py:46
  31.7 9.8 %collective-permute-start.9 = (f32[16,32,128]{2,1,0:T(8,128)S(1)}, f32[16,32,128]{2,1,0:T(8,128)S(1)}, u32[]{:S(2)}, u32[]{:S(2)}) collective-permute-start(f32[16,32,128]{2,1,0:T(8,128)S(1)} %pad_maximum_fusion.6), channel_id=1, source_target_pairs={{0,4},{1,5},{2,6},{3,7},{4,0},{5,1},{6,2},{7,3},{8,12},{9,13},{10,... | collective-permute-start | bytes 786440 | tf_op jit(solution)/shard_map/ppermute | solution.py:46
  39.7 22.7 %collective-permute-start.8 = (f32[64,32,128]{2,1,0:T(8,128)S(1)}, f32[64,32,128]{2,1,0:T(8,128)S(1)}, u32[]{:S(2)}, u32[]{:S(2)}) collective-permute-start(f32[64,32,128]{2,1,0:T(8,128)S(1)} %constant_dynamic-update-slice_fusion.refs_0_), channel_id=1, source_target_pairs={{0,2},{1,5},{2,0},{3,7},{4,6},{5,1},{6,4},{7,3},{8,10},{9,13},{10,... | collective-permute-start | bytes 3145736 | tf_op jit(solution)/shard_map/ppermute | solution.py:46
  41.5 20.8 %collective-permute-start.10 = (f32[32,32,128]{2,1,0:T(8,128)S(1)}, f32[32,32,128]{2,1,0:T(8,128)S(1)}, u32[]{:S(2)}, u32[]{:S(2)}) collective-permute-start(f32[32,32,128]{2,1,0:T(8,128)S(1)} %constant_dynamic-update-slice_fusion.3.refs_1_), channel_id=1, source_target_pairs={{0,8},{1,9},{2,10},{3,11},{4,12},{5,13},{6,14},{7,15},{8,0},{9,1},... | collective-permute-start | bytes 1572872 | tf_op jit(solution)/shard_map/ppermute | solution.py:46
  70.9 15.1 %collective-permute-start.11 = (f32[64,32,128]{2,1,0:T(8,128)}, f32[64,32,128]{2,1,0:T(8,128)S(1)}, u32[]{:S(2)}, u32[]{:S(2)}) collective-permute-start(f32[64,32,128]{2,1,0:T(8,128)} %get-tuple-element.86), channel_id=1, source_target_pairs={{0,2},{1,5},{2,0},{3,7},{4,6},{5,1},{6,4},{7,3},{8,10},{9,13},{10,... | collective-permute-start | bytes 3145736 | tf_op jit(solution)/shard_map/ppermute | solution.py:46
  71.2 17.2 %collective-permute-start.14 = (f32[32,32,128]{2,1,0:T(8,128)}, f32[32,32,128]{2,1,0:T(8,128)S(1)}, u32[]{:S(2)}, u32[]{:S(2)}) collective-permute-start(f32[32,32,128]{2,1,0:T(8,128)} %get-tuple-element.95), channel_id=1, source_target_pairs={{0,8},{1,9},{2,10},{3,11},{4,12},{5,13},{6,14},{7,15},{8,0},{9,1},... | collective-permute-start | bytes 1572872 | tf_op jit(solution)/shard_map/ppermute | solution.py:46
  87.1 10.1 %collective-permute-start.12 = (f32[32,32,128]{2,1,0:T(8,128)S(1)}, f32[32,32,128]{2,1,0:T(8,128)S(1)}, u32[]{:S(2)}, u32[]{:S(2)}) collective-permute-start(f32[32,32,128]{2,1,0:T(8,128)S(1)} %slice_add_fusion.2), channel_id=1, source_target_pairs={{0,8},{1,3},{2,10},{3,1},{4,12},{5,7},{6,14},{7,5},{8,0},{9,11},{1... | collective-permute-start | bytes 1572872 | tf_op jit(solution)/shard_map/ppermute | solution.py:46
  103.9 16.0 %collective-permute-start.17 = (f32[24,32,128]{2,1,0:T(8,128)S(1)}, f32[24,32,128]{2,1,0:T(8,128)S(1)}, u32[]{:S(2)}, u32[]{:S(2)}) collective-permute-start(f32[24,32,128]{2,1,0:T(8,128)S(1)} %pad_maximum_fusion.3), channel_id=1, source_target_pairs={{0,16},{1,17},{2,18},{3,19},{4,20},{5,21},{6,22},{7,23},{8,24},{9,... | collective-permute-start | bytes 1179656 | tf_op jit(solution)/shard_map/ppermute | solution.py:46
  126.6 9.2 %collective-permute-start.20 = (f32[32,32,128]{2,1,0:T(8,128)S(1)}, f32[32,32,128]{2,1,0:T(8,128)S(1)}, u32[]{:S(2)}, u32[]{:S(2)}) collective-permute-start(f32[32,32,128]{2,1,0:T(8,128)S(1)} %pad_maximum_fusion.1), channel_id=1, source_target_pairs={{0,8},{1,3},{2,10},{3,1},{4,12},{5,7},{6,14},{7,5},{8,0},{9,11},{1... | collective-permute-start | bytes 1572872 | tf_op jit(solution)/shard_map/ppermute | solution.py:46
  135.9 19.3 %collective-permute-start.21 = (f32[64,32,128]{2,1,0:T(8,128)S(1)}, f32[64,32,128]{2,1,0:T(8,128)S(1)}, u32[]{:S(2)}, u32[]{:S(2)}) collective-permute-start(f32[64,32,128]{2,1,0:T(8,128)S(1)} %constant_dynamic-update-slice_fusion.6.refs_0_), channel_id=1, source_target_pairs={{0,2},{1,5},{2,0},{3,7},{4,6},{5,1},{6,4},{7,3},{8,10},{9,13},{10,... | collective-permute-start | bytes 3145736 | tf_op jit(solution)/shard_map/ppermute | solution.py:46
  136.5 9.3 %collective-permute-start.22 = (f32[16,32,128]{2,1,0:T(8,128)S(1)}, f32[16,32,128]{2,1,0:T(8,128)S(1)}, u32[]{:S(2)}, u32[]{:S(2)}) collective-permute-start(f32[16,32,128]{2,1,0:T(8,128)S(1)} %pad_maximum_fusion.8), channel_id=1, source_target_pairs={{0,4},{1,5},{2,6},{3,7},{4,0},{5,1},{6,2},{7,3},{8,12},{9,13},{10,... | collective-permute-start | bytes 786440 | tf_op jit(solution)/shard_map/ppermute | solution.py:46
  145.8 9.3 %collective-permute-start.23 = (f32[32,32,128]{2,1,0:T(8,128)S(1)}, f32[32,32,128]{2,1,0:T(8,128)S(1)}, u32[]{:S(2)}, u32[]{:S(2)}) collective-permute-start(f32[32,32,128]{2,1,0:T(8,128)S(1)} %constant_dynamic-update-slice_fusion.9.refs_1_), channel_id=1, source_target_pairs={{0,8},{1,9},{2,10},{3,11},{4,12},{5,13},{6,14},{7,15},{8,0},{9,1},... | collective-permute-start | bytes 1572872 | tf_op jit(solution)/shard_map/ppermute | solution.py:46
  163.7 15.1 %collective-permute-start.24 = (f32[64,32,128]{2,1,0:T(8,128)}, f32[64,32,128]{2,1,0:T(8,128)S(1)}, u32[]{:S(2)}, u32[]{:S(2)}) collective-permute-start(f32[64,32,128]{2,1,0:T(8,128)} %get-tuple-element.110), channel_id=1, source_target_pairs={{0,2},{1,5},{2,0},{3,7},{4,6},{5,1},{6,4},{7,3},{8,10},{9,13},{10,... | collective-permute-start | bytes 3145736 | tf_op jit(solution)/shard_map/ppermute | solution.py:46
  165.1 16.3 %collective-permute-start.27 = (f32[32,32,128]{2,1,0:T(8,128)}, f32[32,32,128]{2,1,0:T(8,128)S(1)}, u32[]{:S(2)}, u32[]{:S(2)}) collective-permute-start(f32[32,32,128]{2,1,0:T(8,128)} %get-tuple-element.119), channel_id=1, source_target_pairs={{0,8},{1,9},{2,10},{3,11},{4,12},{5,13},{6,14},{7,15},{8,0},{9,1},... | collective-permute-start | bytes 1572872 | tf_op jit(solution)/shard_map/ppermute | solution.py:46
  179.9 9.9 %collective-permute-start.25 = (f32[32,32,128]{2,1,0:T(8,128)S(1)}, f32[32,32,128]{2,1,0:T(8,128)S(1)}, u32[]{:S(2)}, u32[]{:S(2)}) collective-permute-start(f32[32,32,128]{2,1,0:T(8,128)S(1)} %slice_add_fusion.1), channel_id=1, source_target_pairs={{0,8},{1,3},{2,10},{3,1},{4,12},{5,7},{6,14},{7,5},{8,0},{9,11},{1... | collective-permute-start | bytes 1572872 | tf_op jit(solution)/shard_map/ppermute | solution.py:46
  188.0 6.5 %collective-permute-start.29 = (f32[8,32,128]{2,1,0:T(8,128)S(1)}, f32[8,32,128]{2,1,0:T(8,128)S(1)}, u32[]{:S(2)}, u32[]{:S(2)}) collective-permute-start(f32[8,32,128]{2,1,0:T(8,128)S(1)} %slice_add_fusion.17), channel_id=1, source_target_pairs={{0,2},{1,3},{2,0},{3,1},{4,6},{5,7},{6,4},{7,5},{8,10},{9,11},{10,... | collective-permute-start | bytes 393224 | tf_op jit(solution)/shard_map/ppermute | solution.py:46
  196.4 20.2 %collective-permute-start.30 = (f32[24,32,128]{2,1,0:T(8,128)S(1)}, f32[24,32,128]{2,1,0:T(8,128)S(1)}, u32[]{:S(2)}, u32[]{:S(2)}) collective-permute-start(f32[24,32,128]{2,1,0:T(8,128)S(1)} %pad_maximum_fusion.4), channel_id=1, source_target_pairs={{0,16},{1,17},{2,18},{3,19},{4,20},{5,21},{6,22},{7,23},{8,24},{9,... | collective-permute-start | bytes 1179656 | tf_op jit(solution)/shard_map/ppermute | solution.py:46
  216.8 6.6 %collective-permute-start.31 = (f32[16,32,128]{2,1,0:T(8,128)S(1)}, f32[16,32,128]{2,1,0:T(8,128)S(1)}, u32[]{:S(2)}, u32[]{:S(2)}) collective-permute-start(f32[16,32,128]{2,1,0:T(8,128)S(1)} %pad_maximum_fusion.9), channel_id=1, source_target_pairs={{0,4},{1,9},{2,6},{3,11},{4,0},{5,13},{6,2},{7,15},{8,12},{9,1},{1... | collective-permute-start | bytes 786440 | tf_op jit(solution)/shard_map/ppermute | solution.py:46
  223.5 9.2 %collective-permute-start.33 = (f32[32,32,128]{2,1,0:T(8,128)S(1)}, f32[32,32,128]{2,1,0:T(8,128)S(1)}, u32[]{:S(2)}, u32[]{:S(2)}) collective-permute-start(f32[32,32,128]{2,1,0:T(8,128)S(1)} %pad_maximum_fusion.2), channel_id=1, source_target_pairs={{0,8},{1,3},{2,10},{3,1},{4,12},{5,7},{6,14},{7,5},{8,0},{9,11},{1... | collective-permute-start | bytes 1572872 | tf_op jit(solution)/shard_map/ppermute | solution.py:46
  232.7 19.4 %collective-permute-start.34 = (f32[64,32,128]{2,1,0:T(8,128)S(1)}, f32[64,32,128]{2,1,0:T(8,128)S(1)}, u32[]{:S(2)}, u32[]{:S(2)}) collective-permute-start(f32[64,32,128]{2,1,0:T(8,128)S(1)} %constant_dynamic-update-slice_fusion.12.refs_0_), channel_id=1, source_target_pairs={{0,2},{1,5},{2,0},{3,7},{4,6},{5,1},{6,4},{7,3},{8,10},{9,13},{10,... | collective-permute-start | bytes 3145736 | tf_op jit(solution)/shard_map/ppermute | solution.py:46
  233.6 9.3 %collective-permute-start.35 = (f32[16,32,128]{2,1,0:T(8,128)S(1)}, f32[16,32,128]{2,1,0:T(8,128)S(1)}, u32[]{:S(2)}, u32[]{:S(2)}) collective-permute-start(f32[16,32,128]{2,1,0:T(8,128)S(1)} %pad_maximum_fusion.10), channel_id=1, source_target_pairs={{0,4},{1,5},{2,6},{3,7},{4,0},{5,1},{6,2},{7,3},{8,12},{9,13},{10,... | collective-permute-start | bytes 786440 | tf_op jit(solution)/shard_map/ppermute | solution.py:46
  242.9 9.2 %collective-permute-start.36 = (f32[32,32,128]{2,1,0:T(8,128)S(1)}, f32[32,32,128]{2,1,0:T(8,128)S(1)}, u32[]{:S(2)}, u32[]{:S(2)}) collective-permute-start(f32[32,32,128]{2,1,0:T(8,128)S(1)} %constant_dynamic-update-slice_fusion.15.refs_1_), channel_id=1, source_target_pairs={{0,8},{1,9},{2,10},{3,11},{4,12},{5,13},{6,14},{7,15},{8,0},{9,1},... | collective-permute-start | bytes 1572872 | tf_op jit(solution)/shard_map/ppermute | solution.py:46
  260.8 15.1 %collective-permute-start.37 = (f32[64,32,128]{2,1,0:T(8,128)}, f32[64,32,128]{2,1,0:T(8,128)S(1)}, u32[]{:S(2)}, u32[]{:S(2)}) collective-permute-start(f32[64,32,128]{2,1,0:T(8,128)} %get-tuple-element.134), channel_id=1, source_target_pairs={{0,2},{1,5},{2,0},{3,7},{4,6},{5,1},{6,4},{7,3},{8,10},{9,13},{10,... | collective-permute-start | bytes 3145736 | tf_op jit(solution)/shard_map/ppermute | solution.py:46
  261.7 17.6 %collective-permute-start.40 = (f32[32,32,128]{2,1,0:T(8,128)}, f32[32,32,128]{2,1,0:T(8,128)S(1)}, u32[]{:S(2)}, u32[]{:S(2)}) collective-permute-start(f32[32,32,128]{2,1,0:T(8,128)} %get-tuple-element.143), channel_id=1, source_target_pairs={{0,8},{1,9},{2,10},{3,11},{4,12},{5,13},{6,14},{7,15},{8,0},{9,1},... | collective-permute-start | bytes 1572872 | tf_op jit(solution)/shard_map/ppermute | solution.py:46
  277.8 11.5 %collective-permute-start.38 = (f32[32,32,128]{2,1,0:T(8,128)}, f32[32,32,128]{2,1,0:T(8,128)}, u32[]{:S(2)}, u32[]{:S(2)}) collective-permute-start(f32[32,32,128]{2,1,0:T(8,128)} %slice_add_fusion), channel_id=1, source_target_pairs={{0,8},{1,3},{2,10},{3,1},{4,12},{5,7},{6,14},{7,5},{8,0},{9,11},{1... | collective-permute-start | bytes 1572872 | tf_op jit(solution)/shard_map/ppermute | solution.py:46
  280.0 6.9 %collective-permute-start.41 = (f32[16,32,128]{2,1,0:T(8,128)}, f32[16,32,128]{2,1,0:T(8,128)}, u32[]{:S(2)}, u32[]{:S(2)}) collective-permute-start(f32[16,32,128]{2,1,0:T(8,128)} %slice_add_fusion.3), channel_id=1, source_target_pairs={{0,4},{1,5},{2,6},{3,7},{4,0},{5,1},{6,2},{7,3},{8,12},{9,13},{10,... | collective-permute-start | bytes 786440 | tf_op jit(solution)/shard_map/ppermute | solution.py:46
  299.5 14.9 %all-to-all-start = ((f32[32,1,128]{2,1,0:T(1,128)}), f32[32,1,128]{2,1,0:T(1,128)S(1)}, u32[]{:S(2)}, u32[]{:S(2)}) async-start(f32[32,1,128]{2,1,0:T(1,128)} %broadcast_in_dim.65), calls=%async_computation | async-start | bytes 32768 | tf_op jit(solution)/shard_map/all_to_all | solution.py:366
  307.3 12.7 %collective-permute-start.43 = (f32[12,32,128]{2,1,0:T(8,128)S(1)}, f32[12,32,128]{2,1,0:T(8,128)S(1)}, u32[]{:S(2)}, u32[]{:S(2)}) collective-permute-start(f32[12,32,128]{2,1,0:T(8,128)S(1)} %get-tuple-element.181), channel_id=1, source_target_pairs={{0,16},{1,17},{2,18},{3,19},{4,20},{5,21},{6,22},{7,23},{8,24},{9,... | collective-permute-start | bytes 589832 | tf_op jit(solution)/shard_map/ppermute | solution.py:46
  (40 other events, 271.5 us)

commit v11 on v9

--- a/solution.py
+++ b/solution.py
@@ -14,6 +14,7 @@
 UNROLL = 8
 CHUNK = 8
 SLOTS = 8
+SPANS = 4
 VMEM = 60 * 1024 * 1024
 CHIPS = ("z", "y", "x")
 ALL = ("z", "y", "x", "core")
@@ -33,10 +34,14 @@
     return [(a, 1) for a in NEAR[turn:] + NEAR[:turn]]
 
 
+def label(place):
+    return place ^ (place >> 1)
+
+
 def swap(array, step):
     axis, distance = step
-    pairs = [(i, i ^ distance) for i in range(lax.axis_size(axis))]
-    return lax.ppermute(array, axis, pairs)
+    at = {label(i): i for i in range(lax.axis_size(axis))}
+    return lax.ppermute(array, axis, [(i, at[n ^ distance]) for n, i in at.items()])
 
 
 def after(value, *others):
@@ -137,12 +142,12 @@
     )(tiles, *given)
 
 
-def apply_kernel(span, skip, counts, has_base, ends_ref, order_ref, row_ref, col_ref, pairs_ref, *refs):
+def apply_kernel(span, skip, counts, has_base, places_ref, pairs_ref, *refs):
     ends, refs = refs[: len(counts)], refs[len(counts) :]
     base_ref, refs = (refs[0], refs[1:]) if has_base else (None, refs)
     *outs, flux_ref, sum_ref, held_ref, sem, held_sem = refs
-    total = order_ref.shape[0]
-    start, stop = ends_ref[span], ends_ref[span + 1]
+    total = pairs_ref.shape[0]
+    start, stop = places_ref[span], places_ref[span + 1]
     chunks = (stop - start + CHUNK - 1) // CHUNK
 
     def fetch(chunk):
@@ -150,7 +155,7 @@
         for k in range(CHUNK):
             at = jnp.minimum(start + chunk * CHUNK + k, total - 1)
             pltpu.make_async_copy(
-                pairs_ref.at[order_ref[at]], held_ref.at[slot, k], held_sem.at[slot]
+                pairs_ref.at[places_ref[SPANS + at]], held_ref.at[slot, k], held_sem.at[slot]
             ).start()
 
     copies = [
@@ -190,7 +195,7 @@
             at = start + chunk * CHUNK + k
             valid = jnp.where(at < stop, 1.0, 0.0)
             at = jnp.minimum(at, stop - 1)
-            flux = flux_ref[col_ref[at]] * valid
+            flux = flux_ref[places_ref[SPANS + 2 * total + at]] * valid
             high = flux.astype(jnp.bfloat16)
             low = (flux - high.astype(jnp.float32)).astype(jnp.bfloat16)
             left = jnp.concatenate([high, low], axis=0)
@@ -201,7 +206,7 @@
             )
             temps = flux.shape[0]
             products.append(both[:temps] + both[temps:])
-            rows.append(row_ref[at] - skip)
+            rows.append(places_ref[SPANS + total + at] - skip)
         for row, product in zip(rows, products):
             sum_ref[row] += product
 
@@ -216,7 +221,7 @@
         copy.wait()
 
 
-def apply_tiles(span, skip, places, pairs, flux, sizes, share, base=None):
+def apply_tiles(span, skip, places, pairs, flux, sizes, share, base=None, vmem=VMEM):
     total, _, size = pairs.shape
     counts = [piece.shape[0] for piece in flux]
     temps = flux[0].shape[1]
@@ -226,7 +231,7 @@
         functools.partial(apply_kernel, span, skip, counts, base is not None),
         out_shape=[jax.ShapeDtypeStruct((n, temps, size), jnp.float32) for n in sizes],
         grid_spec=pltpu.PrefetchScalarGridSpec(
-            num_scalar_prefetch=4,
+            num_scalar_prefetch=1,
             grid=(),
             in_specs=[anywhere] * len(given),
             out_specs=[anywhere] * len(sizes),
@@ -238,13 +243,13 @@
                 pltpu.SemaphoreType.DMA((SLOTS,)),
             ],
         ),
-        compiler_params=pltpu.CompilerParams(vmem_limit_bytes=VMEM),
+        compiler_params=pltpu.CompilerParams(vmem_limit_bytes=vmem),
         cost_estimate=pl.CostEstimate(
             flops=int(share * total * size * size * temps * 8),
             bytes_accessed=int(share * total * size * size * 4) + 8 * sum(sizes) * temps * size,
             transcendentals=0,
         ),
-    )(*places, *given)
+    )(places, *given)
 
 
 def shards(
@@ -268,7 +273,7 @@
         away, width = {}, 1
         for axis in reversed(CHIPS):
             n = lax.axis_size(axis)
-            away[axis] = ((chip // width) % n) ^ lax.axis_index(axis)
+            away[axis] = label((chip // width) % n) ^ label(lax.axis_index(axis))
             width *= n
         side, out = jnp.zeros_like(tile), jnp.zeros_like(tile)
         for part in range(len(NEAR)):
@@ -295,11 +300,11 @@
     slots = jnp.arange(CORES * length, dtype=jnp.int32)
     key = kind * (CORES * length) + slots
     rank = jnp.sum((key[None, :] < key[:, None]).astype(jnp.int32), axis=1)
-    ends = jnp.sum((kind[None, :] < jnp.arange(4, dtype=jnp.int32)[:, None]).astype(jnp.int32), axis=1)
+    ends = jnp.sum((kind[None, :] < jnp.arange(SPANS, dtype=jnp.int32)[:, None]).astype(jnp.int32), axis=1)
     sorts = rank[None, :] == slots[:, None]
     order = jnp.sum(jnp.where(sorts, slots[None, :], 0), axis=1)
     code = jnp.sum(jnp.where(sorts, code[None, :] % (num * num), 0), axis=1)
-    places = (ends, order, code // num, code % num)
+    places = jnp.concatenate([ends, order, code // num, code % num])
 
     def by_core(own, other):
         return jnp.concatenate(
@@ -333,7 +338,7 @@
             pairs = split_tiles(other_values, 1, pairs)
         near, far = [p for p, _ in pieces], [p for _, p in pieces]
         base = apply_tiles(0, 0, places, pairs, near, [num // 2, num // 2], 0.5)
-        sends = apply_tiles(1, 0, places, pairs, far, sizes, 0.25, base[0])
+        sends = apply_tiles(1, 0, places, pairs, far, sizes, 0.25, base[0], VMEM // 2)
         keeps = apply_tiles(2, num // 2, places, pairs, far, sizes, 0.25, base[1])
         blocks = reduce_near(keeps, sends)
         if sweep < ITERS - 1:

time: 278 us -> 300 us (1.079)
  local copies, waits for them, and re-layouts: 9.17 us -> 28.6 us
  starting transfers between devices: 79.6 us -> 89.7 us
  waiting for transfers between devices: 76.7 us -> 66.9 us
    unnamed x104 -> x112, local copies, waits for them, and re-layouts: 5.39 us -> 24.4 us
    ppermute x63, starting transfers between devices: 76 us -> 86.8 us  [swap(): lax.ppermute(array, axis, [(i, at[n ^ distance]) for n, i in at.items()])]
    ppermute x63, waiting for transfers between devices: 72.3 us -> 63.4 us  [swap(): lax.ppermute(array, axis, [(i, at[n ^ distance]) for n, i in at.items()])]
  transfers between devices with their start and end apart: 64 -> 64, of which waited for: 34 -> 32; matrix products, arithmetic and copies ran while one was open for 6% -> 6% of each run, Pallas kernels for 25% -> 23%
where the time goes in v11:
time: 300 us; the launch traced here: 299 us
  Pallas kernels  90.9 us (30%)
  starting transfers between devices  89.7 us (30%)
  waiting for transfers between devices  66.9 us (22%)
  local copies, waits for them, and re-layouts  28.6 us (10%)
  other arithmetic  19.8 us (7%)
    ppermute x63, starting transfers between devices, swap(): lax.ppermute(array, axis, [(i, at[n ^ distance]) for n, i in at.items()])  86.8 us
    pallas_call x9, Pallas kernels, apply_tiles(): pl.pallas_call(functools.partial(apply_kernel, span, skip, counts, base i...  70.4 us
    ppermute x63, waiting for transfers between devices, swap(): lax.ppermute(array, axis, [(i, at[n ^ distance]) for n, i in at.items()])  63.4 us
    unnamed x112, local copies, waits for them, and re-layouts  24.4 us
    pallas_call x2, Pallas kernels, split_tiles(): pl.pallas_call(split_kernel, out_shape=jax.ShapeDtypeStruct((CORES * leng...  20.6 us
    add x18, other arithmetic, reduce_near(): sum([halves(t)[1] for t in terms[1:]], halves(terms[0])[1])  10.8 us
  transfers between devices with their start and end apart: 64, of which 32 were waited for; matrix products, arithmetic and copies ran while one was open for 6% of the time, Pallas kernels for 23%

profile of v11, /device:TPU:0, one launch (start us, length us, event | category | flops | bytes accessed | tf_op | source)
XLA Modules:
  0.0 298.5 jit_solution(1266069038971240781)
XLA Ops:
  8.0 5.0 %collective-permute-start.4 = (f32[12,32,128]{2,1,0:T(8,128)S(1)}, f32[12,32,128]{2,1,0:T(8,128)S(1)}, u32[]{:S(2)}, u32[]{:S(2)}) collective-permute-start(f32[12,32,128]{2,1,0:T(8,128)S(1)} %get-tuple-element.272), channel_id=1, source_target_pairs={{0,24},{8,16},{16,8},{24,0},{1,25},{9,17},{17,9},{25,1},{2,26},{10... | collective-permute-start | bytes 589832 | tf_op jit(solution)/shard_map/ppermute | solution.py:44
  13.1 10.2 %shard_map.95.refs_0_ = bf16[256,256,128]{2,1,0:T(8,128)(2,1)} custom-call(f32[128,128,128]{2,1,0:T(8,128)} %tile_ref), custom_call_target="tpu_custom_call" | custom-call | flops 6291456 | bytes 16777216 | tf_op jit(solution)/shard_map/pallas_call | solution.py:130
  32.5 3.7 %collective-permute-done.6 = f32[16,32,128]{2,1,0:T(8,128)S(1)} collective-permute-done((f32[16,32,128]{2,1,0:T(8,128)S(1)}, f32[16,32,128]{2,1,0:T(8,128)S(1)}, u32[]{:S(2)}, u32[]{:S(2)}) %collective-permute-start.6) | collective-permute-done | bytes 262176 | tf_op jit(solution)/shard_map/ppermute | solution.py:44
  41.3 10.3 %shard_map.96.pairs_ref = bf16[256,256,128]{2,1,0:T(8,128)(2,1)} custom-call(f32[128,128,128]{2,1,0:T(8,128)} %collective-permute-done.2.tile_ref, bf16[256,256,128]{2,1,0:T(8,128)(2,1)} %shard_map.95.refs_0_), custom_call_target="tpu_custom_call", output_to_operand_aliasing={{}: (1, {})} | custom-call | flops 6291456 | bytes 16777216 | tf_op jit(solution)/shard_map/pallas_call | solution.py:130
  51.6 9.3 %shard_map.97 = (f32[96,32,128]{2,1,0:T(8,128)}, f32[96,32,128]{2,1,0:T(8,128)}) custom-call(s32[772]{0:T(1024)} %pad_add_fusion.places_ref, bf16[256,256,128]{2,1,0:T(8,128)(2,1)} %shard_map.96.pairs_ref, f32[32,32,128]{2,1,0:T(8,128)} %copy-done.25, f32[32,32,128]{2,1,0:T(8,128)} %copy-done.22, f32[32,32,128]{2,1,0:T(8,128)} %copy-done.26), custom_call_target="tpu_custom_call" | custom-call | flops 536870912 | bytes 14680064 | tf_op jit(solution)/shard_map/pallas_call | solution.py:230
  61.0 6.3 %copy-done.2 = bf16[256,256,128]{2,1,0:T(8,128)(2,1)S(1)} copy-done((bf16[256,256,128]{2,1,0:T(8,128)(2,1)S(1)}, bf16[256,256,128]{2,1,0:T(8,128)(2,1)}, u32[]{:S(2)}) %copy-start.2) | copy-done | bytes 16777240
  68.7 7.7 %shard_map.99 = (f32[32,32,128]{2,1,0:T(8,128)S(1)}, f32[32,32,128]{2,1,0:T(8,128)S(1)}, f32[32,32,128]{2,1,0:T(8,128)S(1)}) custom-call(s32[772]{0:T(1024)S(1)} %copy-done.17, bf16[256,256,128]{2,1,0:T(8,128)(2,1)S(1)} %copy-done.2, f32[32,32,128]{2,1,0:T(8,128)S(1)} %collective-permute-done.7.refs_0_, f32[32,32,128]{2,1,0:T(8,128)S(1)} %collective-permute-done.10.refs_1_, ...), custom_call_target="tpu_custom_call" | custom-call | flops 268435456 | bytes 7340032 | tf_op jit(solution)/shard_map/pallas_call | solution.py:230
  80.4 6.5 %shard_map.98 = (f32[32,32,128]{2,1,0:T(8,128)}, f32[32,32,128]{2,1,0:T(8,128)}, f32[32,32,128]{2,1,0:T(8,128)}) custom-call(s32[772]{0:T(1024)} %pad_add_fusion.places_ref, bf16[256,256,128]{2,1,0:T(8,128)(2,1)} %shard_map.96.pairs_ref, f32[32,32,128]{2,1,0:T(8,128)} %copy-done.5, f32[32,32,128]{2,1,0:T(8,128)} %copy-done.6, f32[32,32,128]{2,1,0:T(8,128)} %copy-done.7, ...), custom_call_target="tpu_custom_call" | custom-call | flops 268435456 | bytes 7340032 | tf_op jit(solution)/shard_map/pallas_call | solution.py:230
  106.2 4.2 %collective-permute-start.23 = (f32[24,32,128]{2,1,0:T(8,128)S(1)}, f32[24,32,128]{2,1,0:T(8,128)S(1)}, u32[]{:S(2)}, u32[]{:S(2)}) collective-permute-start(f32[24,32,128]{2,1,0:T(8,128)S(1)} %get-tuple-element.222), channel_id=1, source_target_pairs={{0,24},{8,16},{16,8},{24,0},{1,25},{9,17},{17,9},{25,1},{2,26},{10... | collective-permute-start | bytes 1179656 | tf_op jit(solution)/shard_map/ppermute | solution.py:44
  110.4 5.9 %collective-permute-done.23 = f32[24,32,128]{2,1,0:T(8,128)S(1)} collective-permute-done((f32[24,32,128]{2,1,0:T(8,128)S(1)}, f32[24,32,128]{2,1,0:T(8,128)S(1)}, u32[]{:S(2)}, u32[]{:S(2)}) %collective-permute-start.23) | collective-permute-done | bytes 393248 | tf_op jit(solution)/shard_map/ppermute | solution.py:44
  116.5 6.1 %collective-permute-start.24 = (f32[8,32,128]{2,1,0:T(8,128)S(1)}, f32[8,32,128]{2,1,0:T(8,128)S(1)}, u32[]{:S(2)}, u32[]{:S(2)}) collective-permute-start(f32[8,32,128]{2,1,0:T(8,128)S(1)} %pad_maximum_fusion.16), channel_id=1, source_target_pairs={{0,8},{8,0},{16,24},{24,16},{1,9},{9,1},{17,25},{25,17},{2,10},{10... | collective-permute-start | bytes 393224 | tf_op jit(solution)/shard_map/ppermute | solution.py:44
  132.9 3.5 %collective-permute-done.28 = f32[16,32,128]{2,1,0:T(8,128)S(1)} collective-permute-done((f32[16,32,128]{2,1,0:T(8,128)S(1)}, f32[16,32,128]{2,1,0:T(8,128)S(1)}, u32[]{:S(2)}, u32[]{:S(2)}) %collective-permute-start.28) | collective-permute-done | bytes 262176 | tf_op jit(solution)/shard_map/ppermute | solution.py:44
  139.9 9.2 %shard_map.100 = (f32[96,32,128]{2,1,0:T(8,128)}, f32[96,32,128]{2,1,0:T(8,128)}) custom-call(s32[772]{0:T(1024)} %pad_add_fusion.places_ref, bf16[256,256,128]{2,1,0:T(8,128)(2,1)} %shard_map.96.pairs_ref, f32[32,32,128]{2,1,0:T(8,128)} %copy-done.20, f32[32,32,128]{2,1,0:T(8,128)} %copy-done.23, f32[32,32,128]{2,1,0:T(8,128)} %copy-done.27), custom_call_target="tpu_custom_call" | custom-call | flops 536870912 | bytes 14680064 | tf_op jit(solution)/shard_map/pallas_call | solution.py:230
  149.1 6.3 %copy-done.3 = bf16[256,256,128]{2,1,0:T(8,128)(2,1)S(1)} copy-done((bf16[256,256,128]{2,1,0:T(8,128)(2,1)S(1)}, bf16[256,256,128]{2,1,0:T(8,128)(2,1)}, u32[]{:S(2)}) %copy-start.3) | copy-done | bytes 16777240
  156.8 7.7 %shard_map.102 = (f32[32,32,128]{2,1,0:T(8,128)S(1)}, f32[32,32,128]{2,1,0:T(8,128)S(1)}, f32[32,32,128]{2,1,0:T(8,128)S(1)}) custom-call(s32[772]{0:T(1024)S(1)} %copy-done.18, bf16[256,256,128]{2,1,0:T(8,128)(2,1)S(1)} %copy-done.3, f32[32,32,128]{2,1,0:T(8,128)S(1)} %collective-permute-done.26.refs_0_, ...), custom_call_target="tpu_custom_call" | custom-call | flops 268435456 | bytes 7340032 | tf_op jit(solution)/shard_map/pallas_call | solution.py:230
  168.2 6.5 %shard_map.101 = (f32[32,32,128]{2,1,0:T(8,128)}, f32[32,32,128]{2,1,0:T(8,128)}, f32[32,32,128]{2,1,0:T(8,128)}) custom-call(s32[772]{0:T(1024)} %pad_add_fusion.places_ref, bf16[256,256,128]{2,1,0:T(8,128)(2,1)} %shard_map.96.pairs_ref, f32[32,32,128]{2,1,0:T(8,128)} %copy-done.9, f32[32,32,128]{2,1,0:T(8,128)} %copy-done.11, f32[32,32,128]{2,1,0:T(8,128)} %copy-done.13, ...), custom_call_target="tpu_custom_call" | custom-call | flops 268435456 | bytes 7340032 | tf_op jit(solution)/shard_map/pallas_call | solution.py:230
  175.9 2.6 collective-permute-start.34
  188.2 2.8 collective-permute-done.38
  192.7 3.1 %collective-permute-start.42 = (f32[24,32,128]{2,1,0:T(8,128)S(1)}, f32[24,32,128]{2,1,0:T(8,128)S(1)}, u32[]{:S(2)}, u32[]{:S(2)}) collective-permute-start(f32[24,32,128]{2,1,0:T(8,128)S(1)} %get-tuple-element.210), channel_id=1, source_target_pairs={{0,24},{8,16},{16,8},{24,0},{1,25},{9,17},{17,9},{25,1},{2,26},{10... | collective-permute-start | bytes 1179656 | tf_op jit(solution)/shard_map/ppermute | solution.py:44
  195.8 8.0 %collective-permute-done.42 = f32[24,32,128]{2,1,0:T(8,128)S(1)} collective-permute-done((f32[24,32,128]{2,1,0:T(8,128)S(1)}, f32[24,32,128]{2,1,0:T(8,128)S(1)}, u32[]{:S(2)}, u32[]{:S(2)}) %collective-permute-start.42) | collective-permute-done | bytes 393248 | tf_op jit(solution)/shard_map/ppermute | solution.py:44
  204.0 2.9 collective-permute-start.43
  214.7 5.4 %collective-permute-done.44 = f32[16,32,128]{2,1,0:T(8,128)S(1)} collective-permute-done((f32[16,32,128]{2,1,0:T(8,128)S(1)}, f32[16,32,128]{2,1,0:T(8,128)S(1)}, u32[]{:S(2)}, u32[]{:S(2)}) %collective-permute-start.44) | collective-permute-done | bytes 262176 | tf_op jit(solution)/shard_map/ppermute | solution.py:44
  224.5 9.2 %shard_map.103 = (f32[96,32,128]{2,1,0:T(8,128)}, f32[96,32,128]{2,1,0:T(8,128)}) custom-call(s32[772]{0:T(1024)} %pad_add_fusion.places_ref, bf16[256,256,128]{2,1,0:T(8,128)(2,1)} %shard_map.96.pairs_ref, f32[32,32,128]{2,1,0:T(8,128)} %copy-done.21, f32[32,32,128]{2,1,0:T(8,128)} %copy-done.24, f32[32,32,128]{2,1,0:T(8,128)} %copy-done.28), custom_call_target="tpu_custom_call" | custom-call | flops 536870912 | bytes 14680064 | tf_op jit(solution)/shard_map/pallas_call | solution.py:230
  233.8 6.3 %copy-done.4 = bf16[256,256,128]{2,1,0:T(8,128)(2,1)S(1)} copy-done((bf16[256,256,128]{2,1,0:T(8,128)(2,1)S(1)}, bf16[256,256,128]{2,1,0:T(8,128)(2,1)}, u32[]{:S(2)}) %copy-start.4) | copy-done | bytes 16777240
  241.5 7.7 %shard_map.105 = (f32[32,32,128]{2,1,0:T(8,128)S(1)}, f32[32,32,128]{2,1,0:T(8,128)S(1)}, f32[32,32,128]{2,1,0:T(8,128)S(1)}) custom-call(s32[772]{0:T(1024)S(1)} %copy-done.19, bf16[256,256,128]{2,1,0:T(8,128)(2,1)S(1)} %copy-done.4, f32[32,32,128]{2,1,0:T(8,128)S(1)} %collective-permute-done.45.refs_0_, ...), custom_call_target="tpu_custom_call" | custom-call | flops 268435456 | bytes 7340032 | tf_op jit(solution)/shard_map/pallas_call | solution.py:230
  249.2 3.1 %collective-permute-start.58 = (f32[32,32,128]{2,1,0:T(8,128)S(1)}, f32[32,32,128]{2,1,0:T(8,128)S(1)}, u32[]{:S(2)}, u32[]{:S(2)}) collective-permute-start(f32[32,32,128]{2,1,0:T(8,128)S(1)} %get-tuple-element.194), channel_id=1, source_target_pairs={{0,8},{8,0},{16,24},{24,16},{1,9},{9,1},{17,25},{25,17},{2,10},{10... | collective-permute-start | bytes 1572872 | tf_op jit(solution)/shard_map/ppermute | solution.py:44
  252.6 6.5 %shard_map.104 = (f32[32,32,128]{2,1,0:T(8,128)}, f32[32,32,128]{2,1,0:T(8,128)}, f32[32,32,128]{2,1,0:T(8,128)}) custom-call(s32[772]{0:T(1024)} %pad_add_fusion.places_ref, bf16[256,256,128]{2,1,0:T(8,128)(2,1)} %shard_map.96.pairs_ref, f32[32,32,128]{2,1,0:T(8,128)} %copy-done.8, f32[32,32,128]{2,1,0:T(8,128)} %copy-done.10, f32[32,32,128]{2,1,0:T(8,128)} %copy-done.12, ...), custom_call_target="tpu_custom_call" | custom-call | flops 268435456 | bytes 7340032 | tf_op jit(solution)/shard_map/pallas_call | solution.py:230
  259.1 3.2 %collective-permute-done.58 = f32[32,32,128]{2,1,0:T(8,128)S(1)} collective-permute-done((f32[32,32,128]{2,1,0:T(8,128)S(1)}, f32[32,32,128]{2,1,0:T(8,128)S(1)}, u32[]{:S(2)}, u32[]{:S(2)}) %collective-permute-start.58) | collective-permute-done | bytes 524320 | tf_op jit(solution)/shard_map/ppermute | solution.py:44
  267.2 2.7 collective-permute-done.59
  284.2 3.0 all-to-all-start
  287.2 3.7 %collective-permute-start.61 = (f32[12,32,128]{2,1,0:T(8,128)S(1)}, f32[12,32,128]{2,1,0:T(8,128)S(1)}, u32[]{:S(2)}, u32[]{:S(2)}) collective-permute-start(f32[12,32,128]{2,1,0:T(8,128)S(1)} %get-tuple-element.203), channel_id=1, source_target_pairs={{0,24},{8,16},{16,8},{24,0},{1,25},{9,17},{17,9},{25,1},{2,26},{10... | collective-permute-start | bytes 589832 | tf_op jit(solution)/shard_map/ppermute | solution.py:44
  290.9 3.5 %all-to-all-done = f32[32,1,128]{2,1,0:T(1,128)S(1)} async-done(((f32[32,1,128]{2,1,0:T(1,128)}), f32[32,1,128]{2,1,0:T(1,128)S(1)}, u32[]{:S(2)}, u32[]{:S(2)}) %all-to-all-start) | async-done | bytes 16416 | tf_op jit(solution)/shard_map/all_to_all | solution.py:353
  (345 shorter events, 113.9 us)
Async XLA Ops:
  6.1 35.2 %collective-permute-start.2 = (f32[128,128,128]{2,1,0:T(8,128)}, f32[128,128,128]{2,1,0:T(8,128)}, u32[]{:S(2)}, u32[]{:S(2)}) collective-permute-start(f32[128,128,128]{2,1,0:T(8,128)} %tile_ref), channel_id=1, source_target_pairs={{0,1},{1,0},{2,3},{3,2},{4,5},{5,4},{6,7},{7,6},{8,9},{9,8},{10,11... | collective-permute-start | bytes 25165832 | tf_op jit(solution)/shard_map/ppermute | solution.py:44
  8.0 15.3 %collective-permute-start.4 = (f32[12,32,128]{2,1,0:T(8,128)S(1)}, f32[12,32,128]{2,1,0:T(8,128)S(1)}, u32[]{:S(2)}, u32[]{:S(2)}) collective-permute-start(f32[12,32,128]{2,1,0:T(8,128)S(1)} %get-tuple-element.272), channel_id=1, source_target_pairs={{0,24},{8,16},{16,8},{24,0},{1,25},{9,17},{17,9},{25,1},{2,26},{10... | collective-permute-start | bytes 589832 | tf_op jit(solution)/shard_map/ppermute | solution.py:44
  13.0 10.4 %collective-permute-start.3 = (f32[12,2,128]{2,0,1:T(8,128)S(1)}, f32[12,2,128]{2,0,1:T(8,128)S(1)}, u32[]{:S(2)}, u32[]{:S(2)}) collective-permute-start(f32[12,2,128]{2,0,1:T(8,128)S(1)} %pad_maximum_fusion.22), channel_id=1, source_target_pairs={{0,24},{8,16},{16,8},{24,0},{1,25},{9,17},{17,9},{25,1},{2,26},{10... | collective-permute-start | bytes 36872 | tf_op jit(solution)/shard_map/ppermute | solution.py:44
  30.9 8.4 %collective-permute-start.12 = (f32[16,32,128]{2,1,0:T(8,128)S(1)}, f32[16,32,128]{2,1,0:T(8,128)S(1)}, u32[]{:S(2)}, u32[]{:S(2)}) collective-permute-start(f32[16,32,128]{2,1,0:T(8,128)S(1)} %pad_maximum_fusion.2), channel_id=1, source_target_pairs={{0,2},{2,0},{1,3},{3,1},{4,6},{6,4},{5,7},{7,5},{8,10},{10,8},{9,1... | collective-permute-start | bytes 786440 | tf_op jit(solution)/shard_map/ppermute | solution.py:44
  36.3 24.7 %collective-permute-start.7 = (f32[32,32,128]{2,1,0:T(8,128)S(1)}, f32[32,32,128]{2,1,0:T(8,128)S(1)}, u32[]{:S(2)}, u32[]{:S(2)}) collective-permute-start(f32[32,32,128]{2,1,0:T(8,128)S(1)} %constant_dynamic-update-slice_fusion.refs_0_), channel_id=1, source_target_pairs={{0,2},{2,0},{1,3},{3,1},{4,6},{6,4},{5,7},{7,5},{8,10},{10,8},{9,1... | collective-permute-start | bytes 1572872 | tf_op jit(solution)/shard_map/ppermute | solution.py:44
  37.7 23.3 %collective-permute-start.10 = (f32[32,32,128]{2,1,0:T(8,128)S(1)}, f32[32,32,128]{2,1,0:T(8,128)S(1)}, u32[]{:S(2)}, u32[]{:S(2)}) collective-permute-start(f32[32,32,128]{2,1,0:T(8,128)S(1)} %constant_dynamic-update-slice_fusion.3.refs_1_), channel_id=1, source_target_pairs={{0,4},{4,0},{1,5},{5,1},{2,6},{6,2},{3,7},{7,3},{8,12},{12,8},{9,1... | collective-permute-start | bytes 1572872 | tf_op jit(solution)/shard_map/ppermute | solution.py:44
  39.3 21.7 %collective-permute-start.13 = (f32[32,32,128]{2,1,0:T(8,128)S(1)}, f32[32,32,128]{2,1,0:T(8,128)S(1)}, u32[]{:S(2)}, u32[]{:S(2)}) collective-permute-start(f32[32,32,128]{2,1,0:T(8,128)S(1)} %constant_dynamic-update-slice_fusion.6.refs_2_), channel_id=1, source_target_pairs={{0,8},{8,0},{16,24},{24,16},{1,9},{9,1},{17,25},{25,17},{2,10},{10... | collective-permute-start | bytes 1572872 | tf_op jit(solution)/shard_map/ppermute | solution.py:44
  76.5 12.1 %collective-permute-start.14 = (f32[32,32,128]{2,1,0:T(8,128)S(1)}, f32[32,32,128]{2,1,0:T(8,128)S(1)}, u32[]{:S(2)}, u32[]{:S(2)}) collective-permute-start(f32[32,32,128]{2,1,0:T(8,128)S(1)} %get-tuple-element.112), channel_id=1, source_target_pairs={{0,2},{2,0},{1,3},{3,1},{4,6},{6,4},{5,7},{7,5},{8,10},{10,8},{9,1... | collective-permute-start | bytes 1572872 | tf_op jit(solution)/shard_map/ppermute | solution.py:44
  78.5 12.8 %collective-permute-start.17 = (f32[32,32,128]{2,1,0:T(8,128)S(1)}, f32[32,32,128]{2,1,0:T(8,128)S(1)}, u32[]{:S(2)}, u32[]{:S(2)}) collective-permute-start(f32[32,32,128]{2,1,0:T(8,128)S(1)} %get-tuple-element.121), channel_id=1, source_target_pairs={{0,4},{4,0},{1,5},{5,1},{2,6},{6,2},{3,7},{7,3},{8,12},{12,8},{9,1... | collective-permute-start | bytes 1572872 | tf_op jit(solution)/shard_map/ppermute | solution.py:44
  80.0 13.2 %collective-permute-start.20 = (f32[32,32,128]{2,1,0:T(8,128)S(1)}, f32[32,32,128]{2,1,0:T(8,128)S(1)}, u32[]{:S(2)}, u32[]{:S(2)}) collective-permute-start(f32[32,32,128]{2,1,0:T(8,128)S(1)} %get-tuple-element.130), channel_id=1, source_target_pairs={{0,8},{8,0},{16,24},{24,16},{1,9},{9,1},{17,25},{25,17},{2,10},{10... | collective-permute-start | bytes 1572872 | tf_op jit(solution)/shard_map/ppermute | solution.py:44
  106.2 10.0 %collective-permute-start.23 = (f32[24,32,128]{2,1,0:T(8,128)S(1)}, f32[24,32,128]{2,1,0:T(8,128)S(1)}, u32[]{:S(2)}, u32[]{:S(2)}) collective-permute-start(f32[24,32,128]{2,1,0:T(8,128)S(1)} %get-tuple-element.222), channel_id=1, source_target_pairs={{0,24},{8,16},{16,8},{24,0},{1,25},{9,17},{17,9},{25,1},{2,26},{10... | collective-permute-start | bytes 1179656 | tf_op jit(solution)/shard_map/ppermute | solution.py:44
  116.5 9.1 %collective-permute-start.24 = (f32[8,32,128]{2,1,0:T(8,128)S(1)}, f32[8,32,128]{2,1,0:T(8,128)S(1)}, u32[]{:S(2)}, u32[]{:S(2)}) collective-permute-start(f32[8,32,128]{2,1,0:T(8,128)S(1)} %pad_maximum_fusion.16), channel_id=1, source_target_pairs={{0,8},{8,0},{16,24},{24,16},{1,9},{9,1},{17,25},{25,17},{2,10},{10... | collective-permute-start | bytes 393224 | tf_op jit(solution)/shard_map/ppermute | solution.py:44
  128.9 9.3 %collective-permute-start.31 = (f32[16,32,128]{2,1,0:T(8,128)S(1)}, f32[16,32,128]{2,1,0:T(8,128)S(1)}, u32[]{:S(2)}, u32[]{:S(2)}) collective-permute-start(f32[16,32,128]{2,1,0:T(8,128)S(1)} %pad_maximum_fusion.5), channel_id=1, source_target_pairs={{0,2},{2,0},{1,3},{3,1},{4,6},{6,4},{5,7},{7,5},{8,10},{10,8},{9,1... | collective-permute-start | bytes 786440 | tf_op jit(solution)/shard_map/ppermute | solution.py:44
  132.3 16.7 %collective-permute-start.26 = (f32[32,32,128]{2,1,0:T(8,128)S(1)}, f32[32,32,128]{2,1,0:T(8,128)S(1)}, u32[]{:S(2)}, u32[]{:S(2)}) collective-permute-start(f32[32,32,128]{2,1,0:T(8,128)S(1)} %constant_dynamic-update-slice_fusion.15.refs_0_), channel_id=1, source_target_pairs={{0,2},{2,0},{1,3},{3,1},{4,6},{6,4},{5,7},{7,5},{8,10},{10,8},{9,1... | collective-permute-start | bytes 1572872 | tf_op jit(solution)/shard_map/ppermute | solution.py:44
  136.4 12.7 %collective-permute-start.29 = (f32[32,32,128]{2,1,0:T(8,128)S(1)}, f32[32,32,128]{2,1,0:T(8,128)S(1)}, u32[]{:S(2)}, u32[]{:S(2)}) collective-permute-start(f32[32,32,128]{2,1,0:T(8,128)S(1)} %constant_dynamic-update-slice_fusion.18.refs_1_), channel_id=1, source_target_pairs={{0,4},{4,0},{1,5},{5,1},{2,6},{6,2},{3,7},{7,3},{8,12},{12,8},{9,1... | collective-permute-start | bytes 1572872 | tf_op jit(solution)/shard_map/ppermute | solution.py:44
  138.3 10.9 %collective-permute-start.32 = (f32[32,32,128]{2,1,0:T(8,128)S(1)}, f32[32,32,128]{2,1,0:T(8,128)S(1)}, u32[]{:S(2)}, u32[]{:S(2)}) collective-permute-start(f32[32,32,128]{2,1,0:T(8,128)S(1)} %constant_dynamic-update-slice_fusion.21.refs_2_), channel_id=1, source_target_pairs={{0,8},{8,0},{16,24},{24,16},{1,9},{9,1},{17,25},{25,17},{2,10},{10... | collective-permute-start | bytes 1572872 | tf_op jit(solution)/shard_map/ppermute | solution.py:44
  164.6 10.2 %collective-permute-start.33 = (f32[32,32,128]{2,1,0:T(8,128)S(1)}, f32[32,32,128]{2,1,0:T(8,128)S(1)}, u32[]{:S(2)}, u32[]{:S(2)}) collective-permute-start(f32[32,32,128]{2,1,0:T(8,128)S(1)} %get-tuple-element.144), channel_id=1, source_target_pairs={{0,2},{2,0},{1,3},{3,1},{4,6},{6,4},{5,7},{7,5},{8,10},{10,8},{9,1... | collective-permute-start | bytes 1572872 | tf_op jit(solution)/shard_map/ppermute | solution.py:44
  165.7 12.8 %collective-permute-start.36 = (f32[32,32,128]{2,1,0:T(8,128)S(1)}, f32[32,32,128]{2,1,0:T(8,128)S(1)}, u32[]{:S(2)}, u32[]{:S(2)}) collective-permute-start(f32[32,32,128]{2,1,0:T(8,128)S(1)} %get-tuple-element.153), channel_id=1, source_target_pairs={{0,4},{4,0},{1,5},{5,1},{2,6},{6,2},{3,7},{7,3},{8,12},{12,8},{9,1... | collective-permute-start | bytes 1572872 | tf_op jit(solution)/shard_map/ppermute | solution.py:44
  167.8 13.1 %collective-permute-start.39 = (f32[32,32,128]{2,1,0:T(8,128)S(1)}, f32[32,32,128]{2,1,0:T(8,128)S(1)}, u32[]{:S(2)}, u32[]{:S(2)}) collective-permute-start(f32[32,32,128]{2,1,0:T(8,128)S(1)} %get-tuple-element.162), channel_id=1, source_target_pairs={{0,8},{8,0},{16,24},{24,16},{1,9},{9,1},{17,25},{25,17},{2,10},{10... | collective-permute-start | bytes 1572872 | tf_op jit(solution)/shard_map/ppermute | solution.py:44
  192.7 11.1 %collective-permute-start.42 = (f32[24,32,128]{2,1,0:T(8,128)S(1)}, f32[24,32,128]{2,1,0:T(8,128)S(1)}, u32[]{:S(2)}, u32[]{:S(2)}) collective-permute-start(f32[24,32,128]{2,1,0:T(8,128)S(1)} %get-tuple-element.210), channel_id=1, source_target_pairs={{0,24},{8,16},{16,8},{24,0},{1,25},{9,17},{17,9},{25,1},{2,26},{10... | collective-permute-start | bytes 1179656 | tf_op jit(solution)/shard_map/ppermute | solution.py:44
  210.9 9.2 %collective-permute-start.44 = (f32[16,32,128]{2,1,0:T(8,128)S(1)}, f32[16,32,128]{2,1,0:T(8,128)S(1)}, u32[]{:S(2)}, u32[]{:S(2)}) collective-permute-start(f32[16,32,128]{2,1,0:T(8,128)S(1)} %pad_maximum_fusion.6), channel_id=1, source_target_pairs={{0,4},{4,0},{1,5},{5,1},{2,6},{6,2},{3,7},{7,3},{8,12},{12,8},{9,1... | collective-permute-start | bytes 786440 | tf_op jit(solution)/shard_map/ppermute | solution.py:44
  212.2 9.2 %collective-permute-start.47 = (f32[16,32,128]{2,1,0:T(8,128)S(1)}, f32[16,32,128]{2,1,0:T(8,128)S(1)}, u32[]{:S(2)}, u32[]{:S(2)}) collective-permute-start(f32[16,32,128]{2,1,0:T(8,128)S(1)} %pad_maximum_fusion.7), channel_id=1, source_target_pairs={{0,8},{8,0},{16,24},{24,16},{1,9},{9,1},{17,25},{25,17},{2,10},{10... | collective-permute-start | bytes 786440 | tf_op jit(solution)/shard_map/ppermute | solution.py:44
  213.5 9.4 %collective-permute-start.50 = (f32[16,32,128]{2,1,0:T(8,128)S(1)}, f32[16,32,128]{2,1,0:T(8,128)S(1)}, u32[]{:S(2)}, u32[]{:S(2)}) collective-permute-start(f32[16,32,128]{2,1,0:T(8,128)S(1)} %pad_maximum_fusion.8), channel_id=1, source_target_pairs={{0,2},{2,0},{1,3},{3,1},{4,6},{6,4},{5,7},{7,5},{8,10},{10,8},{9,1... | collective-permute-start | bytes 786440 | tf_op jit(solution)/shard_map/ppermute | solution.py:44
  220.2 13.5 %collective-permute-start.45 = (f32[32,32,128]{2,1,0:T(8,128)S(1)}, f32[32,32,128]{2,1,0:T(8,128)S(1)}, u32[]{:S(2)}, u32[]{:S(2)}) collective-permute-start(f32[32,32,128]{2,1,0:T(8,128)S(1)} %constant_dynamic-update-slice_fusion.30.refs_0_), channel_id=1, source_target_pairs={{0,2},{2,0},{1,3},{3,1},{4,6},{6,4},{5,7},{7,5},{8,10},{10,8},{9,1... | collective-permute-start | bytes 1572872 | tf_op jit(solution)/shard_map/ppermute | solution.py:44
  221.5 12.3 %collective-permute-start.48 = (f32[32,32,128]{2,1,0:T(8,128)S(1)}, f32[32,32,128]{2,1,0:T(8,128)S(1)}, u32[]{:S(2)}, u32[]{:S(2)}) collective-permute-start(f32[32,32,128]{2,1,0:T(8,128)S(1)} %constant_dynamic-update-slice_fusion.33.refs_1_), channel_id=1, source_target_pairs={{0,4},{4,0},{1,5},{5,1},{2,6},{6,2},{3,7},{7,3},{8,12},{12,8},{9,1... | collective-permute-start | bytes 1572872 | tf_op jit(solution)/shard_map/ppermute | solution.py:44
  223.0 10.7 %collective-permute-start.51 = (f32[32,32,128]{2,1,0:T(8,128)S(1)}, f32[32,32,128]{2,1,0:T(8,128)S(1)}, u32[]{:S(2)}, u32[]{:S(2)}) collective-permute-start(f32[32,32,128]{2,1,0:T(8,128)S(1)} %constant_dynamic-update-slice_fusion.36.refs_2_), channel_id=1, source_target_pairs={{0,8},{8,0},{16,24},{24,16},{1,9},{9,1},{17,25},{25,17},{2,10},{10... | collective-permute-start | bytes 1572872 | tf_op jit(solution)/shard_map/ppermute | solution.py:44
  249.2 13.1 %collective-permute-start.58 = (f32[32,32,128]{2,1,0:T(8,128)S(1)}, f32[32,32,128]{2,1,0:T(8,128)S(1)}, u32[]{:S(2)}, u32[]{:S(2)}) collective-permute-start(f32[32,32,128]{2,1,0:T(8,128)S(1)} %get-tuple-element.194), channel_id=1, source_target_pairs={{0,8},{8,0},{16,24},{24,16},{1,9},{9,1},{17,25},{25,17},{2,10},{10... | collective-permute-start | bytes 1572872 | tf_op jit(solution)/shard_map/ppermute | solution.py:44
  252.4 13.1 %collective-permute-start.55 = (f32[32,32,128]{2,1,0:T(8,128)S(1)}, f32[32,32,128]{2,1,0:T(8,128)S(1)}, u32[]{:S(2)}, u32[]{:S(2)}) collective-permute-start(f32[32,32,128]{2,1,0:T(8,128)S(1)} %get-tuple-element.185), channel_id=1, source_target_pairs={{0,4},{4,0},{1,5},{5,1},{2,6},{6,2},{3,7},{7,3},{8,12},{12,8},{9,1... | collective-permute-start | bytes 1572872 | tf_op jit(solution)/shard_map/ppermute | solution.py:44
  252.4 14.7 %collective-permute-start.52 = (f32[32,32,128]{2,1,0:T(8,128)S(1)}, f32[32,32,128]{2,1,0:T(8,128)S(1)}, u32[]{:S(2)}, u32[]{:S(2)}) collective-permute-start(f32[32,32,128]{2,1,0:T(8,128)S(1)} %get-tuple-element.176), channel_id=1, source_target_pairs={{0,2},{2,0},{1,3},{3,1},{4,6},{6,4},{5,7},{7,5},{8,10},{10,8},{9,1... | collective-permute-start | bytes 1572872 | tf_op jit(solution)/shard_map/ppermute | solution.py:44
  267.1 8.4 %collective-permute-start.53 = (f32[16,32,128]{2,1,0:T(8,128)S(1)}, f32[16,32,128]{2,1,0:T(8,128)S(1)}, u32[]{:S(2)}, u32[]{:S(2)}) collective-permute-start(f32[16,32,128]{2,1,0:T(8,128)S(1)} %slice_add_fusion.2), channel_id=1, source_target_pairs={{0,4},{4,0},{1,5},{5,1},{2,6},{6,2},{3,7},{7,3},{8,12},{12,8},{9,1... | collective-permute-start | bytes 786440 | tf_op jit(solution)/shard_map/ppermute | solution.py:44
  284.2 10.1 %all-to-all-start = ((f32[32,1,128]{2,1,0:T(1,128)}), f32[32,1,128]{2,1,0:T(1,128)S(1)}, u32[]{:S(2)}, u32[]{:S(2)}) async-start(f32[32,1,128]{2,1,0:T(1,128)} %broadcast_in_dim.60), calls=%async_computation | async-start | bytes 32768 | tf_op jit(solution)/shard_map/all_to_all | solution.py:353
  287.2 9.2 %collective-permute-start.61 = (f32[12,32,128]{2,1,0:T(8,128)S(1)}, f32[12,32,128]{2,1,0:T(8,128)S(1)}, u32[]{:S(2)}, u32[]{:S(2)}) collective-permute-start(f32[12,32,128]{2,1,0:T(8,128)S(1)} %get-tuple-element.203), channel_id=1, source_target_pairs={{0,24},{8,16},{16,8},{24,0},{1,25},{9,17},{17,9},{25,1},{2,26},{10... | collective-permute-start | bytes 589832 | tf_op jit(solution)/shard_map/ppermute | solution.py:44
  (81 other events, 609.1 us)

commit v12 on v11

--- a/solution.py
+++ b/solution.py
@@ -15,7 +15,7 @@
 CHUNK = 8
 SLOTS = 8
 SPANS = 4
-VMEM = 60 * 1024 * 1024
+VMEM = 63 * 1024 * 1024
 CHIPS = ("z", "y", "x")
 ALL = ("z", "y", "x", "core")
 NEAR = ("x", "y", "z")
@@ -221,7 +221,7 @@
         copy.wait()
 
 
-def apply_tiles(span, skip, places, pairs, flux, sizes, share, base=None, vmem=VMEM):
+def apply_tiles(span, skip, places, pairs, flux, sizes, share, base=None):
     total, _, size = pairs.shape
     counts = [piece.shape[0] for piece in flux]
     temps = flux[0].shape[1]
@@ -243,7 +243,7 @@
                 pltpu.SemaphoreType.DMA((SLOTS,)),
             ],
         ),
-        compiler_params=pltpu.CompilerParams(vmem_limit_bytes=vmem),
+        compiler_params=pltpu.CompilerParams(vmem_limit_bytes=VMEM),
         cost_estimate=pl.CostEstimate(
             flops=int(share * total * size * size * temps * 8),
             bytes_accessed=int(share * total * size * size * 4) + 8 * sum(sizes) * temps * size,
@@ -338,7 +338,7 @@
             pairs = split_tiles(other_values, 1, pairs)
         near, far = [p for p, _ in pieces], [p for _, p in pieces]
         base = apply_tiles(0, 0, places, pairs, near, [num // 2, num // 2], 0.5)
-        sends = apply_tiles(1, 0, places, pairs, far, sizes, 0.25, base[0], VMEM // 2)
+        sends = apply_tiles(1, 0, places, pairs, far, sizes, 0.25, base[0])
         keeps = apply_tiles(2, num // 2, places, pairs, far, sizes, 0.25, base[1])
         blocks = reduce_near(keeps, sends)
         if sweep < ITERS - 1:

time: 300 us -> 285 us (0.950)
  waiting for transfers between devices: 66.9 us -> 50.1 us
  other arithmetic: 19.8 us -> 26.3 us
  starting transfers between devices: 89.7 us -> 86.1 us
    ppermute x63, waiting for transfers between devices: 63.4 us -> 46.6 us  [swap(): lax.ppermute(array, axis, [(i, at[n ^ distance]) for n, i in at.items()])]
    unnamed x112 -> x62, local copies, waits for them, and re-layouts: 24.4 us -> 13.6 us
    add x18, other arithmetic: 10.8 us -> 17.3 us  [reduce_near(): sum([halves(t)[1] for t in terms[1:]], halves(terms[0])[1])]
    concatenate x9, local copies, waits for them, and re-layouts: 0.17 us -> 6.5 us  [gather_near(): block = jnp.concatenate([block, swap(block, step)], axis=0)]
    ppermute x63, starting transfers between devices: 86.8 us -> 81.8 us  [swap(): lax.ppermute(array, axis, [(i, at[n ^ distance]) for n, i in at.items()])]
    slice x20 -> x19, local copies, waits for them, and re-layouts: 1.3 us -> 6.09 us  [halves(): return (array[:middle], array[middle:])]
  transfers between devices with their start and end apart: 64 -> 64, of which waited for: 32 -> 30; matrix products, arithmetic and copies ran while one was open for 6% -> 16% of each run, Pallas kernels for 23% -> 24%
where the time goes in v12:
time: 285 us; the launch traced here: 283 us
  Pallas kernels  88.9 us (31%)
  starting transfers between devices  86.1 us (30%)
  waiting for transfers between devices  50.1 us (18%)
  local copies, waits for them, and re-layouts  28.9 us (10%)
  other arithmetic  26.3 us (9%)
    ppermute x63, starting transfers between devices, swap(): lax.ppermute(array, axis, [(i, at[n ^ distance]) for n, i in at.items()])  81.8 us
    pallas_call x9, Pallas kernels, apply_tiles(): pl.pallas_call(functools.partial(apply_kernel, span, skip, counts, base i...  68.4 us
    ppermute x63, waiting for transfers between devices, swap(): lax.ppermute(array, axis, [(i, at[n ^ distance]) for n, i in at.items()])  46.6 us
    pallas_call x2, Pallas kernels, split_tiles(): pl.pallas_call(split_kernel, out_shape=jax.ShapeDtypeStruct((CORES * leng...  20.6 us
    add x18, other arithmetic, reduce_near(): sum([halves(t)[1] for t in terms[1:]], halves(terms[0])[1])  17.3 us
    unnamed x62, local copies, waits for them, and re-layouts  13.6 us
    concatenate x9, local copies, waits for them, and re-layouts, gather_near(): block = jnp.concatenate([block, swap(block, step)], axis=0)  6.5 us
    slice x19, local copies, waits for them, and re-layouts, halves(): return (array[:middle], array[middle:])  6.09 us
  transfers between devices with their start and end apart: 64, of which 30 were waited for; matrix products, arithmetic and copies ran while one was open for 16% of the time, Pallas kernels for 24%

profile of v12, /device:TPU:0, one launch (start us, length us, event | category | flops | bytes accessed | tf_op | source)
XLA Modules:
  0.0 282.5 jit_solution(2291262467540154395)
XLA Ops:
  8.0 5.0 %collective-permute-start.4 = (f32[12,32,128]{2,1,0:T(8,128)S(1)}, f32[12,32,128]{2,1,0:T(8,128)S(1)}, u32[]{:S(2)}, u32[]{:S(2)}) collective-permute-start(f32[12,32,128]{2,1,0:T(8,128)S(1)} %get-tuple-element.272), channel_id=1, source_target_pairs={{0,24},{8,16},{16,8},{24,0},{1,25},{9,17},{17,9},{25,1},{2,26},{10... | collective-permute-start | bytes 589832 | tf_op jit(solution)/shard_map/ppermute | solution.py:44
  13.1 10.3 %shard_map.95.refs_0_ = bf16[256,256,128]{2,1,0:T(8,128)(2,1)} custom-call(f32[128,128,128]{2,1,0:T(8,128)} %tile_ref), custom_call_target="tpu_custom_call" | custom-call | flops 6291456 | bytes 16777216 | tf_op jit(solution)/shard_map/pallas_call | solution.py:130
  35.7 2.0 collective-permute-done.6
  44.7 10.3 %shard_map.96.pairs_ref = bf16[256,256,128]{2,1,0:T(8,128)(2,1)} custom-call(f32[128,128,128]{2,1,0:T(8,128)} %collective-permute-done.2.tile_ref, bf16[256,256,128]{2,1,0:T(8,128)(2,1)} %shard_map.95.refs_0_), custom_call_target="tpu_custom_call", output_to_operand_aliasing={{}: (1, {})} | custom-call | flops 6291456 | bytes 16777216 | tf_op jit(solution)/shard_map/pallas_call | solution.py:130
  54.9 8.6 %shard_map.97 = (f32[96,32,128]{2,1,0:T(8,128)}, f32[96,32,128]{2,1,0:T(8,128)}) custom-call(s32[772]{0:T(1024)} %pad_add_fusion.places_ref, bf16[256,256,128]{2,1,0:T(8,128)(2,1)} %shard_map.96.pairs_ref, f32[32,32,128]{2,1,0:T(8,128)} %constant_dynamic-update-slice_fusion.refs_0_, f32[32,32,128]{2,1,0:T(8,128)} %constant_dynamic-update-slice_fusion.3.refs_1_, ...), custom_call_target="tpu_custom_call" | custom-call | flops 536870912 | bytes 14680064 | tf_op jit(solution)/shard_map/pallas_call | solution.py:230
  64.4 7.2 %shard_map.99 = (f32[32,32,128]{2,1,0:T(8,128)}, f32[32,32,128]{2,1,0:T(8,128)}, f32[32,32,128]{2,1,0:T(8,128)}) custom-call(s32[772]{0:T(1024)} %pad_add_fusion.places_ref, bf16[256,256,128]{2,1,0:T(8,128)(2,1)} %shard_map.96.pairs_ref, f32[32,32,128]{2,1,0:T(8,128)} %copy-done.2, f32[32,32,128]{2,1,0:T(8,128)} %collective-permute-done.10.refs_1_, ...), custom_call_target="tpu_custom_call" | custom-call | flops 268435456 | bytes 7340032 | tf_op jit(solution)/shard_map/pallas_call | solution.py:230
  74.5 6.9 %shard_map.98 = (f32[32,32,128]{2,1,0:T(8,128)}, f32[32,32,128]{2,1,0:T(8,128)}, f32[32,32,128]{2,1,0:T(8,128)}) custom-call(s32[772]{0:T(1024)} %pad_add_fusion.places_ref, bf16[256,256,128]{2,1,0:T(8,128)(2,1)} %shard_map.96.pairs_ref, f32[32,32,128]{2,1,0:T(8,128)} %copy-done.2, f32[32,32,128]{2,1,0:T(8,128)} %collective-permute-done.10.refs_1_, ...), custom_call_target="tpu_custom_call" | custom-call | flops 268435456 | bytes 7340032 | tf_op jit(solution)/shard_map/pallas_call | solution.py:230
  81.4 1.7 collective-permute-done.14
  91.2 2.7 collective-permute-done.18
  101.6 3.9 %collective-permute-start.23 = (f32[24,32,128]{2,1,0:T(8,128)S(1)}, f32[24,32,128]{2,1,0:T(8,128)S(1)}, u32[]{:S(2)}, u32[]{:S(2)}) collective-permute-start(f32[24,32,128]{2,1,0:T(8,128)S(1)} %get-tuple-element.222), channel_id=1, source_target_pairs={{0,24},{8,16},{16,8},{24,0},{1,25},{9,17},{17,9},{25,1},{2,26},{10... | collective-permute-start | bytes 1179656 | tf_op jit(solution)/shard_map/ppermute | solution.py:44
  105.5 5.9 %collective-permute-done.23 = f32[24,32,128]{2,1,0:T(8,128)S(1)} collective-permute-done((f32[24,32,128]{2,1,0:T(8,128)S(1)}, f32[24,32,128]{2,1,0:T(8,128)S(1)}, u32[]{:S(2)}, u32[]{:S(2)}) %collective-permute-start.23) | collective-permute-done | bytes 393248 | tf_op jit(solution)/shard_map/ppermute | solution.py:44
  112.3 5.1 %collective-permute-start.24 = (f32[8,32,128]{2,1,0:T(8,128)S(1)}, f32[8,32,128]{2,1,0:T(8,128)S(1)}, u32[]{:S(2)}, u32[]{:S(2)}) collective-permute-start(f32[8,32,128]{2,1,0:T(8,128)S(1)} %pad_maximum_fusion.16), channel_id=1, source_target_pairs={{0,8},{8,0},{16,24},{24,16},{1,9},{9,1},{17,25},{25,17},{2,10},{10... | collective-permute-start | bytes 393224 | tf_op jit(solution)/shard_map/ppermute | solution.py:44
  120.2 1.7 collective-permute-start.30
  123.0 2.5 collective-permute-start.28
  132.4 2.5 collective-permute-done.31
  135.6 8.6 %shard_map.100 = (f32[96,32,128]{2,1,0:T(8,128)}, f32[96,32,128]{2,1,0:T(8,128)}) custom-call(s32[772]{0:T(1024)} %pad_add_fusion.places_ref, bf16[256,256,128]{2,1,0:T(8,128)(2,1)} %shard_map.96.pairs_ref, f32[32,32,128]{2,1,0:T(8,128)} %constant_dynamic-update-slice_fusion.15.refs_0_, f32[32,32,128]{2,1,0:T(8,128)} %constant_dynamic-update-slice_fusion.18.refs_1_, ...), custom_call_target="tpu_custom_call" | custom-call | flops 536870912 | bytes 14680064 | tf_op jit(solution)/shard_map/pallas_call | solution.py:230
  145.1 7.1 %shard_map.102 = (f32[32,32,128]{2,1,0:T(8,128)}, f32[32,32,128]{2,1,0:T(8,128)}, f32[32,32,128]{2,1,0:T(8,128)}) custom-call(s32[772]{0:T(1024)} %pad_add_fusion.places_ref, bf16[256,256,128]{2,1,0:T(8,128)(2,1)} %shard_map.96.pairs_ref, f32[32,32,128]{2,1,0:T(8,128)} %copy-done.4, f32[32,32,128]{2,1,0:T(8,128)} %collective-permute-done.29.refs_1_, ...), custom_call_target="tpu_custom_call" | custom-call | flops 268435456 | bytes 7340032 | tf_op jit(solution)/shard_map/pallas_call | solution.py:230
  153.9 1.8 collective-permute-start.36
  156.8 7.0 %shard_map.101 = (f32[32,32,128]{2,1,0:T(8,128)}, f32[32,32,128]{2,1,0:T(8,128)}, f32[32,32,128]{2,1,0:T(8,128)}) custom-call(s32[772]{0:T(1024)} %pad_add_fusion.places_ref, bf16[256,256,128]{2,1,0:T(8,128)(2,1)} %shard_map.96.pairs_ref, f32[32,32,128]{2,1,0:T(8,128)} %copy-done.4, f32[32,32,128]{2,1,0:T(8,128)} %collective-permute-done.29.refs_1_, ...), custom_call_target="tpu_custom_call" | custom-call | flops 268435456 | bytes 7340032 | tf_op jit(solution)/shard_map/pallas_call | solution.py:230
  182.3 4.2 %collective-permute-start.42 = (f32[24,32,128]{2,1,0:T(8,128)S(1)}, f32[24,32,128]{2,1,0:T(8,128)S(1)}, u32[]{:S(2)}, u32[]{:S(2)}) collective-permute-start(f32[24,32,128]{2,1,0:T(8,128)S(1)} %get-tuple-element.210), channel_id=1, source_target_pairs={{0,24},{8,16},{16,8},{24,0},{1,25},{9,17},{17,9},{25,1},{2,26},{10... | collective-permute-start | bytes 1179656 | tf_op jit(solution)/shard_map/ppermute | solution.py:44
  186.6 7.3 %collective-permute-done.42 = f32[24,32,128]{2,1,0:T(8,128)S(1)} collective-permute-done((f32[24,32,128]{2,1,0:T(8,128)S(1)}, f32[24,32,128]{2,1,0:T(8,128)S(1)}, u32[]{:S(2)}, u32[]{:S(2)}) %collective-permute-start.42) | collective-permute-done | bytes 393248 | tf_op jit(solution)/shard_map/ppermute | solution.py:44
  194.7 1.9 collective-permute-start.43
  201.3 2.0 collective-permute-done.46
  208.2 2.8 collective-permute-done.44
  215.5 8.6 %shard_map.103 = (f32[96,32,128]{2,1,0:T(8,128)}, f32[96,32,128]{2,1,0:T(8,128)}) custom-call(s32[772]{0:T(1024)} %pad_add_fusion.places_ref, bf16[256,256,128]{2,1,0:T(8,128)(2,1)} %shard_map.96.pairs_ref, f32[32,32,128]{2,1,0:T(8,128)} %constant_dynamic-update-slice_fusion.30.refs_0_, f32[32,32,128]{2,1,0:T(8,128)} %constant_dynamic-update-slice_fusion.33.refs_1_, ...), custom_call_target="tpu_custom_call" | custom-call | flops 536870912 | bytes 14680064 | tf_op jit(solution)/shard_map/pallas_call | solution.py:230
  224.2 2.9 %collective-permute-done.51.refs_2_ = f32[32,32,128]{2,1,0:T(8,128)} collective-permute-done((f32[32,32,128]{2,1,0:T(8,128)}, f32[32,32,128]{2,1,0:T(8,128)}, u32[]{:S(2)}, u32[]{:S(2)}) %collective-permute-start.51) | collective-permute-done | bytes 524320 | tf_op jit(solution)/shard_map/ppermute | solution.py:44
  227.0 7.1 %shard_map.105 = (f32[32,32,128]{2,1,0:T(8,128)}, f32[32,32,128]{2,1,0:T(8,128)}, f32[32,32,128]{2,1,0:T(8,128)}) custom-call(s32[772]{0:T(1024)} %pad_add_fusion.places_ref, bf16[256,256,128]{2,1,0:T(8,128)(2,1)} %shard_map.96.pairs_ref, f32[32,32,128]{2,1,0:T(8,128)} %copy-done.3, f32[32,32,128]{2,1,0:T(8,128)} %collective-permute-done.48.refs_1_, ...), custom_call_target="tpu_custom_call" | custom-call | flops 268435456 | bytes 7340032 | tf_op jit(solution)/shard_map/pallas_call | solution.py:230
  236.4 7.0 %shard_map.104 = (f32[32,32,128]{2,1,0:T(8,128)}, f32[32,32,128]{2,1,0:T(8,128)}, f32[32,32,128]{2,1,0:T(8,128)}) custom-call(s32[772]{0:T(1024)} %pad_add_fusion.places_ref, bf16[256,256,128]{2,1,0:T(8,128)(2,1)} %shard_map.96.pairs_ref, f32[32,32,128]{2,1,0:T(8,128)} %copy-done.3, f32[32,32,128]{2,1,0:T(8,128)} %collective-permute-done.48.refs_1_, ...), custom_call_target="tpu_custom_call" | custom-call | flops 268435456 | bytes 7340032 | tf_op jit(solution)/shard_map/pallas_call | solution.py:230
  258.9 1.7 collective-permute-start.54
  266.9 4.3 %all-to-all-start = ((f32[32,1,128]{2,1,0:T(1,128)}), f32[32,1,128]{2,1,0:T(1,128)S(1)}, u32[]{:S(2)}, u32[]{:S(2)}) async-start(f32[32,1,128]{2,1,0:T(1,128)} %broadcast_in_dim.60), calls=%async_computation | async-start | bytes 32768 | tf_op jit(solution)/shard_map/all_to_all | solution.py:353
  271.2 3.7 %collective-permute-start.61 = (f32[12,32,128]{2,1,0:T(8,128)S(1)}, f32[12,32,128]{2,1,0:T(8,128)S(1)}, u32[]{:S(2)}, u32[]{:S(2)}) collective-permute-start(f32[12,32,128]{2,1,0:T(8,128)S(1)} %get-tuple-element.203), channel_id=1, source_target_pairs={{0,24},{8,16},{16,8},{24,0},{1,25},{9,17},{17,9},{25,1},{2,26},{10... | collective-permute-start | bytes 589832 | tf_op jit(solution)/shard_map/ppermute | solution.py:44
  274.9 3.5 %all-to-all-done = f32[32,1,128]{2,1,0:T(1,128)S(1)} async-done(((f32[32,1,128]{2,1,0:T(1,128)}), f32[32,1,128]{2,1,0:T(1,128)S(1)}, u32[]{:S(2)}, u32[]{:S(2)}) %all-to-all-start) | async-done | bytes 16416 | tf_op jit(solution)/shard_map/all_to_all | solution.py:353
  (294 shorter events, 122.4 us)
Async XLA Ops:
  6.1 38.5 %collective-permute-start.2 = (f32[128,128,128]{2,1,0:T(8,128)}, f32[128,128,128]{2,1,0:T(8,128)}, u32[]{:S(2)}, u32[]{:S(2)}) collective-permute-start(f32[128,128,128]{2,1,0:T(8,128)} %tile_ref), channel_id=1, source_target_pairs={{0,1},{1,0},{2,3},{3,2},{4,5},{5,4},{6,7},{7,6},{8,9},{9,8},{10,11... | collective-permute-start | bytes 25165832 | tf_op jit(solution)/shard_map/ppermute | solution.py:44
  8.0 15.4 %collective-permute-start.4 = (f32[12,32,128]{2,1,0:T(8,128)S(1)}, f32[12,32,128]{2,1,0:T(8,128)S(1)}, u32[]{:S(2)}, u32[]{:S(2)}) collective-permute-start(f32[12,32,128]{2,1,0:T(8,128)S(1)} %get-tuple-element.272), channel_id=1, source_target_pairs={{0,24},{8,16},{16,8},{24,0},{1,25},{9,17},{17,9},{25,1},{2,26},{10... | collective-permute-start | bytes 589832 | tf_op jit(solution)/shard_map/ppermute | solution.py:44
  13.0 10.4 %collective-permute-start.3 = (f32[12,2,128]{2,0,1:T(8,128)S(1)}, f32[12,2,128]{2,0,1:T(8,128)S(1)}, u32[]{:S(2)}, u32[]{:S(2)}) collective-permute-start(f32[12,2,128]{2,0,1:T(8,128)S(1)} %pad_maximum_fusion.22), channel_id=1, source_target_pairs={{0,24},{8,16},{16,8},{24,0},{1,25},{9,17},{17,9},{25,1},{2,26},{10... | collective-permute-start | bytes 36872 | tf_op jit(solution)/shard_map/ppermute | solution.py:44
  38.5 25.1 %collective-permute-start.7 = (f32[32,32,128]{2,1,0:T(8,128)}, f32[32,32,128]{2,1,0:T(8,128)S(1)}, u32[]{:S(2)}, u32[]{:S(2)}) collective-permute-start(f32[32,32,128]{2,1,0:T(8,128)} %constant_dynamic-update-slice_fusion.refs_0_), channel_id=1, source_target_pairs={{0,2},{2,0},{1,3},{3,1},{4,6},{6,4},{5,7},{7,5},{8,10},{10,8},{9,1... | collective-permute-start | bytes 1572872 | tf_op jit(solution)/shard_map/ppermute | solution.py:44
  39.7 23.9 %collective-permute-start.10 = (f32[32,32,128]{2,1,0:T(8,128)}, f32[32,32,128]{2,1,0:T(8,128)}, u32[]{:S(2)}, u32[]{:S(2)}) collective-permute-start(f32[32,32,128]{2,1,0:T(8,128)} %constant_dynamic-update-slice_fusion.3.refs_1_), channel_id=1, source_target_pairs={{0,4},{4,0},{1,5},{5,1},{2,6},{6,2},{3,7},{7,3},{8,12},{12,8},{9,1... | collective-permute-start | bytes 1572872 | tf_op jit(solution)/shard_map/ppermute | solution.py:44
  42.0 21.6 %collective-permute-start.13 = (f32[32,32,128]{2,1,0:T(8,128)}, f32[32,32,128]{2,1,0:T(8,128)}, u32[]{:S(2)}, u32[]{:S(2)}) collective-permute-start(f32[32,32,128]{2,1,0:T(8,128)} %constant_dynamic-update-slice_fusion.6.refs_2_), channel_id=1, source_target_pairs={{0,8},{8,0},{16,24},{24,16},{1,9},{9,1},{17,25},{25,17},{2,10},{10... | collective-permute-start | bytes 1572872 | tf_op jit(solution)/shard_map/ppermute | solution.py:44
  71.6 11.6 %collective-permute-start.14 = (f32[32,32,128]{2,1,0:T(8,128)}, f32[32,32,128]{2,1,0:T(8,128)S(1)}, u32[]{:S(2)}, u32[]{:S(2)}) collective-permute-start(f32[32,32,128]{2,1,0:T(8,128)} %get-tuple-element.112), channel_id=1, source_target_pairs={{0,2},{2,0},{1,3},{3,1},{4,6},{6,4},{5,7},{7,5},{8,10},{10,8},{9,1... | collective-permute-start | bytes 1572872 | tf_op jit(solution)/shard_map/ppermute | solution.py:44
  73.2 12.5 %collective-permute-start.17 = (f32[32,32,128]{2,1,0:T(8,128)}, f32[32,32,128]{2,1,0:T(8,128)}, u32[]{:S(2)}, u32[]{:S(2)}) collective-permute-start(f32[32,32,128]{2,1,0:T(8,128)} %get-tuple-element.121), channel_id=1, source_target_pairs={{0,4},{4,0},{1,5},{5,1},{2,6},{6,2},{3,7},{7,3},{8,12},{12,8},{9,1... | collective-permute-start | bytes 1572872 | tf_op jit(solution)/shard_map/ppermute | solution.py:44
  74.0 12.9 %collective-permute-start.20 = (f32[32,32,128]{2,1,0:T(8,128)}, f32[32,32,128]{2,1,0:T(8,128)}, u32[]{:S(2)}, u32[]{:S(2)}) collective-permute-start(f32[32,32,128]{2,1,0:T(8,128)} %get-tuple-element.130), channel_id=1, source_target_pairs={{0,8},{8,0},{16,24},{24,16},{1,9},{9,1},{17,25},{25,17},{2,10},{10... | collective-permute-start | bytes 1572872 | tf_op jit(solution)/shard_map/ppermute | solution.py:44
  90.6 9.3 %collective-permute-start.16 = (f32[8,32,128]{2,1,0:T(8,128)S(1)}, f32[8,32,128]{2,1,0:T(8,128)S(1)}, u32[]{:S(2)}, u32[]{:S(2)}) collective-permute-start(f32[8,32,128]{2,1,0:T(8,128)S(1)} %slice_add_fusion.21), channel_id=1, source_target_pairs={{0,8},{8,0},{16,24},{24,16},{1,9},{9,1},{17,25},{25,17},{2,10},{10... | collective-permute-start | bytes 393224 | tf_op jit(solution)/shard_map/ppermute | solution.py:44
  101.6 9.7 %collective-permute-start.23 = (f32[24,32,128]{2,1,0:T(8,128)S(1)}, f32[24,32,128]{2,1,0:T(8,128)S(1)}, u32[]{:S(2)}, u32[]{:S(2)}) collective-permute-start(f32[24,32,128]{2,1,0:T(8,128)S(1)} %get-tuple-element.222), channel_id=1, source_target_pairs={{0,24},{8,16},{16,8},{24,0},{1,25},{9,17},{17,9},{25,1},{2,26},{10... | collective-permute-start | bytes 1179656 | tf_op jit(solution)/shard_map/ppermute | solution.py:44
  112.3 9.7 %collective-permute-start.24 = (f32[8,32,128]{2,1,0:T(8,128)S(1)}, f32[8,32,128]{2,1,0:T(8,128)S(1)}, u32[]{:S(2)}, u32[]{:S(2)}) collective-permute-start(f32[8,32,128]{2,1,0:T(8,128)S(1)} %pad_maximum_fusion.16), channel_id=1, source_target_pairs={{0,8},{8,0},{16,24},{24,16},{1,9},{9,1},{17,25},{25,17},{2,10},{10... | collective-permute-start | bytes 393224 | tf_op jit(solution)/shard_map/ppermute | solution.py:44
  125.6 9.3 %collective-permute-start.31 = (f32[16,32,128]{2,1,0:T(8,128)S(1)}, f32[16,32,128]{2,1,0:T(8,128)S(1)}, u32[]{:S(2)}, u32[]{:S(2)}) collective-permute-start(f32[16,32,128]{2,1,0:T(8,128)S(1)} %pad_maximum_fusion.5), channel_id=1, source_target_pairs={{0,2},{2,0},{1,3},{3,1},{4,6},{6,4},{5,7},{7,5},{8,10},{10,8},{9,1... | collective-permute-start | bytes 786440 | tf_op jit(solution)/shard_map/ppermute | solution.py:44
  129.2 15.1 %collective-permute-start.26 = (f32[32,32,128]{2,1,0:T(8,128)}, f32[32,32,128]{2,1,0:T(8,128)S(1)}, u32[]{:S(2)}, u32[]{:S(2)}) collective-permute-start(f32[32,32,128]{2,1,0:T(8,128)} %constant_dynamic-update-slice_fusion.15.refs_0_), channel_id=1, source_target_pairs={{0,2},{2,0},{1,3},{3,1},{4,6},{6,4},{5,7},{7,5},{8,10},{10,8},{9,1... | collective-permute-start | bytes 1572872 | tf_op jit(solution)/shard_map/ppermute | solution.py:44
  131.1 13.2 %collective-permute-start.29 = (f32[32,32,128]{2,1,0:T(8,128)}, f32[32,32,128]{2,1,0:T(8,128)}, u32[]{:S(2)}, u32[]{:S(2)}) collective-permute-start(f32[32,32,128]{2,1,0:T(8,128)} %constant_dynamic-update-slice_fusion.18.refs_1_), channel_id=1, source_target_pairs={{0,4},{4,0},{1,5},{5,1},{2,6},{6,2},{3,7},{7,3},{8,12},{12,8},{9,1... | collective-permute-start | bytes 1572872 | tf_op jit(solution)/shard_map/ppermute | solution.py:44
  135.6 9.5 %collective-permute-start.32 = (f32[32,32,128]{2,1,0:T(8,128)}, f32[32,32,128]{2,1,0:T(8,128)}, u32[]{:S(2)}, u32[]{:S(2)}) collective-permute-start(f32[32,32,128]{2,1,0:T(8,128)} %constant_dynamic-update-slice_fusion.21.refs_2_), channel_id=1, source_target_pairs={{0,8},{8,0},{16,24},{24,16},{1,9},{9,1},{17,25},{25,17},{2,10},{10... | collective-permute-start | bytes 1572872 | tf_op jit(solution)/shard_map/ppermute | solution.py:44
  152.3 11.6 %collective-permute-start.33 = (f32[32,32,128]{2,1,0:T(8,128)}, f32[32,32,128]{2,1,0:T(8,128)S(1)}, u32[]{:S(2)}, u32[]{:S(2)}) collective-permute-start(f32[32,32,128]{2,1,0:T(8,128)} %get-tuple-element.144), channel_id=1, source_target_pairs={{0,2},{2,0},{1,3},{3,1},{4,6},{6,4},{5,7},{7,5},{8,10},{10,8},{9,1... | collective-permute-start | bytes 1572872 | tf_op jit(solution)/shard_map/ppermute | solution.py:44
  153.9 12.3 %collective-permute-start.36 = (f32[32,32,128]{2,1,0:T(8,128)}, f32[32,32,128]{2,1,0:T(8,128)}, u32[]{:S(2)}, u32[]{:S(2)}) collective-permute-start(f32[32,32,128]{2,1,0:T(8,128)} %get-tuple-element.153), channel_id=1, source_target_pairs={{0,4},{4,0},{1,5},{5,1},{2,6},{6,2},{3,7},{7,3},{8,12},{12,8},{9,1... | collective-permute-start | bytes 1572872 | tf_op jit(solution)/shard_map/ppermute | solution.py:44
  155.7 13.1 %collective-permute-start.39 = (f32[32,32,128]{2,1,0:T(8,128)}, f32[32,32,128]{2,1,0:T(8,128)}, u32[]{:S(2)}, u32[]{:S(2)}) collective-permute-start(f32[32,32,128]{2,1,0:T(8,128)} %get-tuple-element.162), channel_id=1, source_target_pairs={{0,8},{8,0},{16,24},{24,16},{1,9},{9,1},{17,25},{25,17},{2,10},{10... | collective-permute-start | bytes 1572872 | tf_op jit(solution)/shard_map/ppermute | solution.py:44
  171.5 9.3 %collective-permute-start.35 = (f32[8,32,128]{2,1,0:T(8,128)S(1)}, f32[8,32,128]{2,1,0:T(8,128)S(1)}, u32[]{:S(2)}, u32[]{:S(2)}) collective-permute-start(f32[8,32,128]{2,1,0:T(8,128)S(1)} %slice_add_fusion.18), channel_id=1, source_target_pairs={{0,8},{8,0},{16,24},{24,16},{1,9},{9,1},{17,25},{25,17},{2,10},{10... | collective-permute-start | bytes 393224 | tf_op jit(solution)/shard_map/ppermute | solution.py:44
  182.3 11.5 %collective-permute-start.42 = (f32[24,32,128]{2,1,0:T(8,128)S(1)}, f32[24,32,128]{2,1,0:T(8,128)S(1)}, u32[]{:S(2)}, u32[]{:S(2)}) collective-permute-start(f32[24,32,128]{2,1,0:T(8,128)S(1)} %get-tuple-element.210), channel_id=1, source_target_pairs={{0,24},{8,16},{16,8},{24,0},{1,25},{9,17},{17,9},{25,1},{2,26},{10... | collective-permute-start | bytes 1179656 | tf_op jit(solution)/shard_map/ppermute | solution.py:44
  200.1 10.9 %collective-permute-start.44 = (f32[16,32,128]{2,1,0:T(8,128)S(1)}, f32[16,32,128]{2,1,0:T(8,128)S(1)}, u32[]{:S(2)}, u32[]{:S(2)}) collective-permute-start(f32[16,32,128]{2,1,0:T(8,128)S(1)} %pad_maximum_fusion.6), channel_id=1, source_target_pairs={{0,4},{4,0},{1,5},{5,1},{2,6},{6,2},{3,7},{7,3},{8,12},{12,8},{9,1... | collective-permute-start | bytes 786440 | tf_op jit(solution)/shard_map/ppermute | solution.py:44
  203.3 9.3 %collective-permute-start.47 = (f32[16,32,128]{2,1,0:T(8,128)S(1)}, f32[16,32,128]{2,1,0:T(8,128)S(1)}, u32[]{:S(2)}, u32[]{:S(2)}) collective-permute-start(f32[16,32,128]{2,1,0:T(8,128)S(1)} %pad_maximum_fusion.7), channel_id=1, source_target_pairs={{0,8},{8,0},{16,24},{24,16},{1,9},{9,1},{17,25},{25,17},{2,10},{10... | collective-permute-start | bytes 786440 | tf_op jit(solution)/shard_map/ppermute | solution.py:44
  205.4 9.4 %collective-permute-start.50 = (f32[16,32,128]{2,1,0:T(8,128)S(1)}, f32[16,32,128]{2,1,0:T(8,128)S(1)}, u32[]{:S(2)}, u32[]{:S(2)}) collective-permute-start(f32[16,32,128]{2,1,0:T(8,128)S(1)} %pad_maximum_fusion.8), channel_id=1, source_target_pairs={{0,2},{2,0},{1,3},{3,1},{4,6},{6,4},{5,7},{7,5},{8,10},{10,8},{9,1... | collective-permute-start | bytes 786440 | tf_op jit(solution)/shard_map/ppermute | solution.py:44
  211.7 12.4 %collective-permute-start.45 = (f32[32,32,128]{2,1,0:T(8,128)}, f32[32,32,128]{2,1,0:T(8,128)S(1)}, u32[]{:S(2)}, u32[]{:S(2)}) collective-permute-start(f32[32,32,128]{2,1,0:T(8,128)} %constant_dynamic-update-slice_fusion.30.refs_0_), channel_id=1, source_target_pairs={{0,2},{2,0},{1,3},{3,1},{4,6},{6,4},{5,7},{7,5},{8,10},{10,8},{9,1... | collective-permute-start | bytes 1572872 | tf_op jit(solution)/shard_map/ppermute | solution.py:44
  213.3 10.8 %collective-permute-start.48 = (f32[32,32,128]{2,1,0:T(8,128)}, f32[32,32,128]{2,1,0:T(8,128)}, u32[]{:S(2)}, u32[]{:S(2)}) collective-permute-start(f32[32,32,128]{2,1,0:T(8,128)} %constant_dynamic-update-slice_fusion.33.refs_1_), channel_id=1, source_target_pairs={{0,4},{4,0},{1,5},{5,1},{2,6},{6,2},{3,7},{7,3},{8,12},{12,8},{9,1... | collective-permute-start | bytes 1572872 | tf_op jit(solution)/shard_map/ppermute | solution.py:44
  215.5 11.6 %collective-permute-start.51 = (f32[32,32,128]{2,1,0:T(8,128)}, f32[32,32,128]{2,1,0:T(8,128)}, u32[]{:S(2)}, u32[]{:S(2)}) collective-permute-start(f32[32,32,128]{2,1,0:T(8,128)} %constant_dynamic-update-slice_fusion.36.refs_2_), channel_id=1, source_target_pairs={{0,8},{8,0},{16,24},{24,16},{1,9},{9,1},{17,25},{25,17},{2,10},{10... | collective-permute-start | bytes 1572872 | tf_op jit(solution)/shard_map/ppermute | solution.py:44
  234.2 10.0 %collective-permute-start.58 = (f32[32,32,128]{2,1,0:T(8,128)}, f32[32,32,128]{2,1,0:T(8,128)S(1)}, u32[]{:S(2)}, u32[]{:S(2)}) collective-permute-start(f32[32,32,128]{2,1,0:T(8,128)} %get-tuple-element.194), channel_id=1, source_target_pairs={{0,8},{8,0},{16,24},{24,16},{1,9},{9,1},{17,25},{25,17},{2,10},{10... | collective-permute-start | bytes 1572872 | tf_op jit(solution)/shard_map/ppermute | solution.py:44
  234.3 12.6 %collective-permute-start.55 = (f32[32,32,128]{2,1,0:T(8,128)}, f32[32,32,128]{2,1,0:T(8,128)}, u32[]{:S(2)}, u32[]{:S(2)}) collective-permute-start(f32[32,32,128]{2,1,0:T(8,128)} %get-tuple-element.185), channel_id=1, source_target_pairs={{0,4},{4,0},{1,5},{5,1},{2,6},{6,2},{3,7},{7,3},{8,12},{12,8},{9,1... | collective-permute-start | bytes 1572872 | tf_op jit(solution)/shard_map/ppermute | solution.py:44
  234.9 14.7 %collective-permute-start.52 = (f32[32,32,128]{2,1,0:T(8,128)}, f32[32,32,128]{2,1,0:T(8,128)}, u32[]{:S(2)}, u32[]{:S(2)}) collective-permute-start(f32[32,32,128]{2,1,0:T(8,128)} %get-tuple-element.176), channel_id=1, source_target_pairs={{0,2},{2,0},{1,3},{3,1},{4,6},{6,4},{5,7},{7,5},{8,10},{10,8},{9,1... | collective-permute-start | bytes 1572872 | tf_op jit(solution)/shard_map/ppermute | solution.py:44
  252.5 10.9 %collective-permute-start.60 = (f32[8,32,128]{2,1,0:T(8,128)}, f32[8,32,128]{2,1,0:T(8,128)S(1)}, u32[]{:S(2)}, u32[]{:S(2)}) collective-permute-start(f32[8,32,128]{2,1,0:T(8,128)} %slice_add_fusion.13), channel_id=1, source_target_pairs={{0,4},{4,0},{1,5},{5,1},{2,6},{6,2},{3,7},{7,3},{8,12},{12,8},{9,1... | collective-permute-start | bytes 393224 | tf_op jit(solution)/shard_map/ppermute | solution.py:44
  266.9 11.5 %all-to-all-start = ((f32[32,1,128]{2,1,0:T(1,128)}), f32[32,1,128]{2,1,0:T(1,128)S(1)}, u32[]{:S(2)}, u32[]{:S(2)}) async-start(f32[32,1,128]{2,1,0:T(1,128)} %broadcast_in_dim.60), calls=%async_computation | async-start | bytes 32768 | tf_op jit(solution)/shard_map/all_to_all | solution.py:353
  (55 other events, 345.2 us)

commit v13 on v12

--- a/solution.py
+++ b/solution.py
@@ -15,7 +15,7 @@
 CHUNK = 8
 SLOTS = 8
 SPANS = 4
-VMEM = 63 * 1024 * 1024
+VMEM = 60 * 1024 * 1024
 CHIPS = ("z", "y", "x")
 ALL = ("z", "y", "x", "core")
 NEAR = ("x", "y", "z")
@@ -116,11 +116,11 @@
     @pl.loop(0, STEP // UNROLL)
     def _(group):
         for k in range(UNROLL):
-            tile = jnp.transpose(tile_ref[group * UNROLL + k])
+            tile = tile_ref[group * UNROLL + k]
             high = tile.astype(jnp.bfloat16)
             low = (tile - high.astype(jnp.float32)).astype(jnp.bfloat16)
-            pair_ref[group * UNROLL + k, :size] = high
-            pair_ref[group * UNROLL + k, size:] = low
+            pair_ref[group * UNROLL + k, :, :size] = high
+            pair_ref[group * UNROLL + k, :, size:] = low
 
 
 def split_tiles(tiles, place, pairs=None):
@@ -129,11 +129,11 @@
     given = [] if pairs is None else [pairs]
     return pl.pallas_call(
         split_kernel,
-        out_shape=jax.ShapeDtypeStruct((CORES * length, 2 * size, size), jnp.bfloat16),
+        out_shape=jax.ShapeDtypeStruct((CORES * length, size, 2 * size), jnp.bfloat16),
         grid=(steps,),
         in_specs=[pl.BlockSpec((STEP, size, size), lambda i: (i, 0, 0))]
         + [pl.BlockSpec(memory_space=pltpu.HBM)] * len(given),
-        out_specs=pl.BlockSpec((STEP, 2 * size, size), lambda i: (place * steps + i, 0, 0)),
+        out_specs=pl.BlockSpec((STEP, size, 2 * size), lambda i: (place * steps + i, 0, 0)),
         input_output_aliases={1: 0} if given else {},
         compiler_params=pltpu.CompilerParams(vmem_limit_bytes=VMEM),
         cost_estimate=pl.CostEstimate(
@@ -199,9 +199,10 @@
             high = flux.astype(jnp.bfloat16)
             low = (flux - high.astype(jnp.float32)).astype(jnp.bfloat16)
             left = jnp.concatenate([high, low], axis=0)
-            both = jnp.dot(
+            both = lax.dot_general(
                 jnp.concatenate([left, left], axis=1),
                 held_ref[slot, k],
+                (((1,), (1,)), ((), ())),
                 preferred_element_type=jnp.float32,
             )
             temps = flux.shape[0]
@@ -222,7 +223,7 @@
 
 
 def apply_tiles(span, skip, places, pairs, flux, sizes, share, base=None):
-    total, _, size = pairs.shape
+    total, size, _ = pairs.shape
     counts = [piece.shape[0] for piece in flux]
     temps = flux[0].shape[1]
     anywhere = pl.BlockSpec(memory_space=pltpu.HBM)

time: 285 us -> 280 us (0.982)
  local copies, waits for them, and re-layouts: 28.9 us -> 8.94 us
  waiting for transfers between devices: 50.1 us -> 67.1 us
  other arithmetic: 26.3 us -> 18.8 us
  Pallas kernels: 88.9 us -> 94.5 us
    ppermute x63, waiting for transfers between devices: 46.6 us -> 63.6 us  [swap(): lax.ppermute(array, axis, [(i, at[n ^ distance]) for n, i in at.items()])]
    unnamed x62 -> x104, local copies, waits for them, and re-layouts: 13.6 us -> 5.17 us
    add x18, other arithmetic: 17.3 us -> 8.89 us  [reduce_near(): sum([halves(t)[1] for t in terms[1:]], halves(terms[0])[1])]
    pallas_call x9, Pallas kernels: 68.4 us -> 75.7 us  [apply_tiles(): pl.pallas_call(functools.partial(apply_kernel, span, skip, counts, base i...]
    concatenate x9, local copies, waits for them, and re-layouts: 6.5 us -> 0.17 us  [gather_near(): block = jnp.concatenate([block, swap(block, step)], axis=0)]
    slice x19 -> x20, local copies, waits for them, and re-layouts: 6.09 us -> 0.31 us  [halves(): return (array[:middle], array[middle:])]
    all_to_all x1, starting transfers between devices: 4.28 us -> 7.53 us  [shards(): lax.all_to_all(jnp.broadcast_to(totals, (chips * CORES, size)), ALL, spli...]
  transfers between devices with their start and end apart: 64 -> 64, of which waited for: 30 -> 31; matrix products, arithmetic and copies ran while one was open for 16% -> 6% of each run, Pallas kernels for 24% -> 26%
where the time goes in v13:
time: 280 us; the launch traced here: 279 us
  Pallas kernels  94.5 us (34%)
  starting transfers between devices  86.8 us (31%)
  waiting for transfers between devices  67.1 us (24%)
  other arithmetic  18.8 us (7%)
  local copies, waits for them, and re-layouts  8.94 us (3%)
    ppermute x63, starting transfers between devices, swap(): lax.ppermute(array, axis, [(i, at[n ^ distance]) for n, i in at.items()])  79.3 us
    pallas_call x9, Pallas kernels, apply_tiles(): pl.pallas_call(functools.partial(apply_kernel, span, skip, counts, base i...  75.7 us
    ppermute x63, waiting for transfers between devices, swap(): lax.ppermute(array, axis, [(i, at[n ^ distance]) for n, i in at.items()])  63.6 us
    pallas_call x2, Pallas kernels, split_tiles(): pl.pallas_call(split_kernel, out_shape=jax.ShapeDtypeStruct((CORES * leng...  18.8 us
    add x18, other arithmetic, reduce_near(): sum([halves(t)[1] for t in terms[1:]], halves(terms[0])[1])  8.89 us
    all_to_all x1, starting transfers between devices, shards(): lax.all_to_all(jnp.broadcast_to(totals, (chips * CORES, size)), ALL, spli...  7.53 us
  transfers between devices with their start and end apart: 64, of which 31 were waited for; matrix products, arithmetic and copies ran while one was open for 6% of the time, Pallas kernels for 26%

profile of v13, /device:TPU:0, one launch (start us, length us, event | category | flops | bytes accessed | tf_op | source)
XLA Modules:
  0.0 278.7 jit_solution(8319782751183260617)
XLA Ops:
  8.6 4.9 %collective-permute-start.4 = (f32[12,32,128]{2,1,0:T(8,128)S(1)}, f32[12,32,128]{2,1,0:T(8,128)S(1)}, u32[]{:S(2)}, u32[]{:S(2)}) collective-permute-start(f32[12,32,128]{2,1,0:T(8,128)S(1)} %get-tuple-element.272), channel_id=1, source_target_pairs={{0,24},{8,16},{16,8},{24,0},{1,25},{9,17},{17,9},{25,1},{2,26},{10... | collective-permute-start | bytes 589832 | tf_op jit(solution)/shard_map/ppermute | solution.py:44
  13.6 9.4 %shard_map.95.refs_0_ = bf16[256,128,256]{2,1,0:T(8,128)(2,1)} custom-call(f32[128,128,128]{2,1,0:T(8,128)} %tile_ref), custom_call_target="tpu_custom_call" | custom-call | flops 6291456 | bytes 16777216 | tf_op jit(solution)/shard_map/pallas_call | solution.py:130
  32.7 3.7 %collective-permute-done.6 = f32[16,32,128]{2,1,0:T(8,128)S(1)} collective-permute-done((f32[16,32,128]{2,1,0:T(8,128)S(1)}, f32[16,32,128]{2,1,0:T(8,128)S(1)}, u32[]{:S(2)}, u32[]{:S(2)}) %collective-permute-start.6) | collective-permute-done | bytes 262176 | tf_op jit(solution)/shard_map/ppermute | solution.py:44
  42.6 9.4 %shard_map.96.pairs_ref = bf16[256,128,256]{2,1,0:T(8,128)(2,1)} custom-call(f32[128,128,128]{2,1,0:T(8,128)} %collective-permute-done.2.tile_ref, bf16[256,128,256]{2,1,0:T(8,128)(2,1)} %shard_map.95.refs_0_), custom_call_target="tpu_custom_call", output_to_operand_aliasing={{}: (1, {})} | custom-call | flops 6291456 | bytes 16777216 | tf_op jit(solution)/shard_map/pallas_call | solution.py:130
  52.0 10.0 %shard_map.97 = (f32[96,32,128]{2,1,0:T(8,128)}, f32[96,32,128]{2,1,0:T(8,128)}) custom-call(s32[772]{0:T(1024)} %pad_add_fusion.places_ref, bf16[256,128,256]{2,1,0:T(8,128)(2,1)} %shard_map.96.pairs_ref, f32[32,32,128]{2,1,0:T(8,128)} %copy-done.16, f32[32,32,128]{2,1,0:T(8,128)} %copy-done.13, f32[32,32,128]{2,1,0:T(8,128)} %copy-done.17), custom_call_target="tpu_custom_call" | custom-call | flops 536870912 | bytes 14680064 | tf_op jit(solution)/shard_map/pallas_call | solution.py:231
  63.2 7.7 %shard_map.99 = (f32[32,32,128]{2,1,0:T(8,128)}, f32[32,32,128]{2,1,0:T(8,128)}, f32[32,32,128]{2,1,0:T(8,128)}) custom-call(s32[772]{0:T(1024)} %pad_add_fusion.places_ref, bf16[256,128,256]{2,1,0:T(8,128)(2,1)} %shard_map.96.pairs_ref, f32[32,32,128]{2,1,0:T(8,128)} %copy-done.2, f32[32,32,128]{2,1,0:T(8,128)} %copy-done.3, f32[32,32,128]{2,1,0:T(8,128)} %copy-done.4, ...), custom_call_target="tpu_custom_call" | custom-call | flops 268435456 | bytes 7340032 | tf_op jit(solution)/shard_map/pallas_call | solution.py:231
  72.6 7.4 %shard_map.98 = (f32[32,32,128]{2,1,0:T(8,128)}, f32[32,32,128]{2,1,0:T(8,128)}, f32[32,32,128]{2,1,0:T(8,128)}) custom-call(s32[772]{0:T(1024)} %pad_add_fusion.places_ref, bf16[256,128,256]{2,1,0:T(8,128)(2,1)} %shard_map.96.pairs_ref, f32[32,32,128]{2,1,0:T(8,128)} %copy-done.2, f32[32,32,128]{2,1,0:T(8,128)} %copy-done.3, f32[32,32,128]{2,1,0:T(8,128)} %copy-done.4, ...), custom_call_target="tpu_custom_call" | custom-call | flops 268435456 | bytes 7340032 | tf_op jit(solution)/shard_map/pallas_call | solution.py:231
  83.0 2.2 collective-permute-done.17
  86.5 2.9 %collective-permute-done.15 = f32[16,32,128]{2,1,0:T(8,128)S(1)} collective-permute-done((f32[16,32,128]{2,1,0:T(8,128)S(1)}, f32[16,32,128]{2,1,0:T(8,128)S(1)}, u32[]{:S(2)}, u32[]{:S(2)}) %collective-permute-start.15) | collective-permute-done | bytes 262176 | tf_op jit(solution)/shard_map/ppermute | solution.py:44
  89.5 3.5 %collective-permute-done.18 = f32[16,32,128]{2,1,0:T(8,128)S(1)} collective-permute-done((f32[16,32,128]{2,1,0:T(8,128)S(1)}, f32[16,32,128]{2,1,0:T(8,128)S(1)}, u32[]{:S(2)}, u32[]{:S(2)}) %collective-permute-start.18) | collective-permute-done | bytes 262176 | tf_op jit(solution)/shard_map/ppermute | solution.py:44
  94.7 3.4 %collective-permute-done.19 = f32[8,32,128]{2,1,0:T(8,128)S(1)} collective-permute-done((f32[8,32,128]{2,1,0:T(8,128)S(1)}, f32[8,32,128]{2,1,0:T(8,128)S(1)}, u32[]{:S(2)}, u32[]{:S(2)}) %collective-permute-start.19) | collective-permute-done | bytes 131104 | tf_op jit(solution)/shard_map/ppermute | solution.py:44
  98.7 3.5 %collective-permute-start.23 = (f32[24,32,128]{2,1,0:T(8,128)S(1)}, f32[24,32,128]{2,1,0:T(8,128)S(1)}, u32[]{:S(2)}, u32[]{:S(2)}) collective-permute-start(f32[24,32,128]{2,1,0:T(8,128)S(1)} %get-tuple-element.222), channel_id=1, source_target_pairs={{0,24},{8,16},{16,8},{24,0},{1,25},{9,17},{17,9},{25,1},{2,26},{10... | collective-permute-start | bytes 1179656 | tf_op jit(solution)/shard_map/ppermute | solution.py:44
  102.2 6.3 %collective-permute-done.23 = f32[24,32,128]{2,1,0:T(8,128)S(1)} collective-permute-done((f32[24,32,128]{2,1,0:T(8,128)S(1)}, f32[24,32,128]{2,1,0:T(8,128)S(1)}, u32[]{:S(2)}, u32[]{:S(2)}) %collective-permute-start.23) | collective-permute-done | bytes 393248 | tf_op jit(solution)/shard_map/ppermute | solution.py:44
  108.7 4.4 %collective-permute-start.24 = (f32[8,32,128]{2,1,0:T(8,128)S(1)}, f32[8,32,128]{2,1,0:T(8,128)S(1)}, u32[]{:S(2)}, u32[]{:S(2)}) collective-permute-start(f32[8,32,128]{2,1,0:T(8,128)S(1)} %pad_maximum_fusion.16), channel_id=1, source_target_pairs={{0,8},{8,0},{16,24},{24,16},{1,9},{9,1},{17,25},{25,17},{2,10},{10... | collective-permute-start | bytes 393224 | tf_op jit(solution)/shard_map/ppermute | solution.py:44
  124.7 2.7 collective-permute-done.28
  130.9 10.0 %shard_map.100 = (f32[96,32,128]{2,1,0:T(8,128)}, f32[96,32,128]{2,1,0:T(8,128)}) custom-call(s32[772]{0:T(1024)} %pad_add_fusion.places_ref, bf16[256,128,256]{2,1,0:T(8,128)(2,1)} %shard_map.96.pairs_ref, f32[32,32,128]{2,1,0:T(8,128)} %copy-done.11, f32[32,32,128]{2,1,0:T(8,128)} %copy-done.14, f32[32,32,128]{2,1,0:T(8,128)} %copy-done.18), custom_call_target="tpu_custom_call" | custom-call | flops 536870912 | bytes 14680064 | tf_op jit(solution)/shard_map/pallas_call | solution.py:231
  142.2 7.7 %shard_map.102 = (f32[32,32,128]{2,1,0:T(8,128)}, f32[32,32,128]{2,1,0:T(8,128)}, f32[32,32,128]{2,1,0:T(8,128)}) custom-call(s32[772]{0:T(1024)} %pad_add_fusion.places_ref, bf16[256,128,256]{2,1,0:T(8,128)(2,1)} %shard_map.96.pairs_ref, f32[32,32,128]{2,1,0:T(8,128)} %copy-done.6, f32[32,32,128]{2,1,0:T(8,128)} %copy-done.8, f32[32,32,128]{2,1,0:T(8,128)} %copy-done.10, ...), custom_call_target="tpu_custom_call" | custom-call | flops 268435456 | bytes 7340032 | tf_op jit(solution)/shard_map/pallas_call | solution.py:231
  153.0 7.4 %shard_map.101 = (f32[32,32,128]{2,1,0:T(8,128)}, f32[32,32,128]{2,1,0:T(8,128)}, f32[32,32,128]{2,1,0:T(8,128)}) custom-call(s32[772]{0:T(1024)} %pad_add_fusion.places_ref, bf16[256,128,256]{2,1,0:T(8,128)(2,1)} %shard_map.96.pairs_ref, f32[32,32,128]{2,1,0:T(8,128)} %copy-done.6, f32[32,32,128]{2,1,0:T(8,128)} %copy-done.8, f32[32,32,128]{2,1,0:T(8,128)} %copy-done.10, ...), custom_call_target="tpu_custom_call" | custom-call | flops 268435456 | bytes 7340032 | tf_op jit(solution)/shard_map/pallas_call | solution.py:231
  166.9 2.8 collective-permute-done.34
  171.2 2.1 collective-permute-start.38
  173.6 4.3 %collective-permute-done.35 = f32[8,32,128]{2,1,0:T(8,128)S(1)} collective-permute-done((f32[8,32,128]{2,1,0:T(8,128)S(1)}, f32[8,32,128]{2,1,0:T(8,128)S(1)}, u32[]{:S(2)}, u32[]{:S(2)}) %collective-permute-start.35) | collective-permute-done | bytes 131104 | tf_op jit(solution)/shard_map/ppermute | solution.py:44
  178.5 4.8 %collective-permute-start.42 = (f32[24,32,128]{2,1,0:T(8,128)S(1)}, f32[24,32,128]{2,1,0:T(8,128)S(1)}, u32[]{:S(2)}, u32[]{:S(2)}) collective-permute-start(f32[24,32,128]{2,1,0:T(8,128)S(1)} %get-tuple-element.210), channel_id=1, source_target_pairs={{0,24},{8,16},{16,8},{24,0},{1,25},{9,17},{17,9},{25,1},{2,26},{10... | collective-permute-start | bytes 1179656 | tf_op jit(solution)/shard_map/ppermute | solution.py:44
  183.3 7.8 %collective-permute-done.42 = f32[24,32,128]{2,1,0:T(8,128)S(1)} collective-permute-done((f32[24,32,128]{2,1,0:T(8,128)S(1)}, f32[24,32,128]{2,1,0:T(8,128)S(1)}, u32[]{:S(2)}, u32[]{:S(2)}) %collective-permute-start.42) | collective-permute-done | bytes 393248 | tf_op jit(solution)/shard_map/ppermute | solution.py:44
  196.9 2.2 collective-permute-start.44
  202.1 2.2 collective-permute-done.44
  209.3 10.0 %shard_map.103 = (f32[96,32,128]{2,1,0:T(8,128)}, f32[96,32,128]{2,1,0:T(8,128)}) custom-call(s32[772]{0:T(1024)} %pad_add_fusion.places_ref, bf16[256,128,256]{2,1,0:T(8,128)(2,1)} %shard_map.96.pairs_ref, f32[32,32,128]{2,1,0:T(8,128)} %copy-done.12, f32[32,32,128]{2,1,0:T(8,128)} %copy-done.15, f32[32,32,128]{2,1,0:T(8,128)} %copy-done.19), custom_call_target="tpu_custom_call" | custom-call | flops 536870912 | bytes 14680064 | tf_op jit(solution)/shard_map/pallas_call | solution.py:231
  220.5 7.9 %shard_map.105 = (f32[32,32,128]{2,1,0:T(8,128)}, f32[32,32,128]{2,1,0:T(8,128)}, f32[32,32,128]{2,1,0:T(8,128)}) custom-call(s32[772]{0:T(1024)} %pad_add_fusion.places_ref, bf16[256,128,256]{2,1,0:T(8,128)(2,1)} %shard_map.96.pairs_ref, f32[32,32,128]{2,1,0:T(8,128)} %copy-done.5, f32[32,32,128]{2,1,0:T(8,128)} %copy-done.7, f32[32,32,128]{2,1,0:T(8,128)} %copy-done.9, ...), custom_call_target="tpu_custom_call" | custom-call | flops 268435456 | bytes 7340032 | tf_op jit(solution)/shard_map/pallas_call | solution.py:231
  231.1 7.4 %shard_map.104 = (f32[32,32,128]{2,1,0:T(8,128)}, f32[32,32,128]{2,1,0:T(8,128)}, f32[32,32,128]{2,1,0:T(8,128)}) custom-call(s32[772]{0:T(1024)} %pad_add_fusion.places_ref, bf16[256,128,256]{2,1,0:T(8,128)(2,1)} %shard_map.96.pairs_ref, f32[32,32,128]{2,1,0:T(8,128)} %copy-done.5, f32[32,32,128]{2,1,0:T(8,128)} %copy-done.7, f32[32,32,128]{2,1,0:T(8,128)} %copy-done.9, ...), custom_call_target="tpu_custom_call" | custom-call | flops 268435456 | bytes 7340032 | tf_op jit(solution)/shard_map/pallas_call | solution.py:231
  252.9 2.2 collective-permute-done.57
  259.8 7.5 %all-to-all-start = ((f32[32,1,128]{2,1,0:T(1,128)}), f32[32,1,128]{2,1,0:T(1,128)S(1)}, u32[]{:S(2)}, u32[]{:S(2)}) async-start(f32[32,1,128]{2,1,0:T(1,128)} %broadcast_in_dim.60), calls=%async_computation | async-start | bytes 32768 | tf_op jit(solution)/shard_map/all_to_all | solution.py:354
  267.4 3.7 %collective-permute-start.61 = (f32[12,32,128]{2,1,0:T(8,128)S(1)}, f32[12,32,128]{2,1,0:T(8,128)S(1)}, u32[]{:S(2)}, u32[]{:S(2)}) collective-permute-start(f32[12,32,128]{2,1,0:T(8,128)S(1)} %get-tuple-element.203), channel_id=1, source_target_pairs={{0,24},{8,16},{16,8},{24,0},{1,25},{9,17},{17,9},{25,1},{2,26},{10... | collective-permute-start | bytes 589832 | tf_op jit(solution)/shard_map/ppermute | solution.py:44
  271.1 3.5 %all-to-all-done = f32[32,1,128]{2,1,0:T(1,128)S(1)} async-done(((f32[32,1,128]{2,1,0:T(1,128)}), f32[32,1,128]{2,1,0:T(1,128)S(1)}, u32[]{:S(2)}, u32[]{:S(2)}) %all-to-all-start) | async-done | bytes 16416 | tf_op jit(solution)/shard_map/all_to_all | solution.py:354
  (337 shorter events, 101.3 us)
Async XLA Ops:
  6.1 36.5 %collective-permute-start.2 = (f32[128,128,128]{2,1,0:T(8,128)}, f32[128,128,128]{2,1,0:T(8,128)}, u32[]{:S(2)}, u32[]{:S(2)}) collective-permute-start(f32[128,128,128]{2,1,0:T(8,128)} %tile_ref), channel_id=1, source_target_pairs={{0,1},{1,0},{2,3},{3,2},{4,5},{5,4},{6,7},{7,6},{8,9},{9,8},{10,11... | collective-permute-start | bytes 25165832 | tf_op jit(solution)/shard_map/ppermute | solution.py:44
  8.6 15.0 %collective-permute-start.4 = (f32[12,32,128]{2,1,0:T(8,128)S(1)}, f32[12,32,128]{2,1,0:T(8,128)S(1)}, u32[]{:S(2)}, u32[]{:S(2)}) collective-permute-start(f32[12,32,128]{2,1,0:T(8,128)S(1)} %get-tuple-element.272), channel_id=1, source_target_pairs={{0,24},{8,16},{16,8},{24,0},{1,25},{9,17},{17,9},{25,1},{2,26},{10... | collective-permute-start | bytes 589832 | tf_op jit(solution)/shard_map/ppermute | solution.py:44
  13.5 9.5 %collective-permute-start.3 = (f32[12,2,128]{2,0,1:T(8,128)S(1)}, f32[12,2,128]{2,0,1:T(8,128)S(1)}, u32[]{:S(2)}, u32[]{:S(2)}) collective-permute-start(f32[12,2,128]{2,0,1:T(8,128)S(1)} %pad_maximum_fusion.22), channel_id=1, source_target_pairs={{0,24},{8,16},{16,8},{24,0},{1,25},{9,17},{17,9},{25,1},{2,26},{10... | collective-permute-start | bytes 36872 | tf_op jit(solution)/shard_map/ppermute | solution.py:44
  31.1 8.4 %collective-permute-start.12 = (f32[16,32,128]{2,1,0:T(8,128)S(1)}, f32[16,32,128]{2,1,0:T(8,128)S(1)}, u32[]{:S(2)}, u32[]{:S(2)}) collective-permute-start(f32[16,32,128]{2,1,0:T(8,128)S(1)} %pad_maximum_fusion.2), channel_id=1, source_target_pairs={{0,2},{2,0},{1,3},{3,1},{4,6},{6,4},{5,7},{7,5},{8,10},{10,8},{9,1... | collective-permute-start | bytes 786440 | tf_op jit(solution)/shard_map/ppermute | solution.py:44
  36.5 25.6 %collective-permute-start.7 = (f32[32,32,128]{2,1,0:T(8,128)S(1)}, f32[32,32,128]{2,1,0:T(8,128)S(1)}, u32[]{:S(2)}, u32[]{:S(2)}) collective-permute-start(f32[32,32,128]{2,1,0:T(8,128)S(1)} %constant_dynamic-update-slice_fusion.refs_0_), channel_id=1, source_target_pairs={{0,2},{2,0},{1,3},{3,1},{4,6},{6,4},{5,7},{7,5},{8,10},{10,8},{9,1... | collective-permute-start | bytes 1572872 | tf_op jit(solution)/shard_map/ppermute | solution.py:44
  37.9 24.2 %collective-permute-start.10 = (f32[32,32,128]{2,1,0:T(8,128)S(1)}, f32[32,32,128]{2,1,0:T(8,128)S(1)}, u32[]{:S(2)}, u32[]{:S(2)}) collective-permute-start(f32[32,32,128]{2,1,0:T(8,128)S(1)} %constant_dynamic-update-slice_fusion.3.refs_1_), channel_id=1, source_target_pairs={{0,4},{4,0},{1,5},{5,1},{2,6},{6,2},{3,7},{7,3},{8,12},{12,8},{9,1... | collective-permute-start | bytes 1572872 | tf_op jit(solution)/shard_map/ppermute | solution.py:44
  39.5 22.6 %collective-permute-start.13 = (f32[32,32,128]{2,1,0:T(8,128)S(1)}, f32[32,32,128]{2,1,0:T(8,128)S(1)}, u32[]{:S(2)}, u32[]{:S(2)}) collective-permute-start(f32[32,32,128]{2,1,0:T(8,128)S(1)} %constant_dynamic-update-slice_fusion.6.refs_2_), channel_id=1, source_target_pairs={{0,8},{8,0},{16,24},{24,16},{1,9},{9,1},{17,25},{25,17},{2,10},{10... | collective-permute-start | bytes 1572872 | tf_op jit(solution)/shard_map/ppermute | solution.py:44
  71.0 11.0 %collective-permute-start.14 = (f32[32,32,128]{2,1,0:T(8,128)}, f32[32,32,128]{2,1,0:T(8,128)S(1)}, u32[]{:S(2)}, u32[]{:S(2)}) collective-permute-start(f32[32,32,128]{2,1,0:T(8,128)} %get-tuple-element.112), channel_id=1, source_target_pairs={{0,2},{2,0},{1,3},{3,1},{4,6},{6,4},{5,7},{7,5},{8,10},{10,8},{9,1... | collective-permute-start | bytes 1572872 | tf_op jit(solution)/shard_map/ppermute | solution.py:44
  72.2 13.0 %collective-permute-start.17 = (f32[32,32,128]{2,1,0:T(8,128)}, f32[32,32,128]{2,1,0:T(8,128)S(1)}, u32[]{:S(2)}, u32[]{:S(2)}) collective-permute-start(f32[32,32,128]{2,1,0:T(8,128)} %get-tuple-element.121), channel_id=1, source_target_pairs={{0,4},{4,0},{1,5},{5,1},{2,6},{6,2},{3,7},{7,3},{8,12},{12,8},{9,1... | collective-permute-start | bytes 1572872 | tf_op jit(solution)/shard_map/ppermute | solution.py:44
  72.3 14.0 %collective-permute-start.20 = (f32[32,32,128]{2,1,0:T(8,128)}, f32[32,32,128]{2,1,0:T(8,128)S(1)}, u32[]{:S(2)}, u32[]{:S(2)}) collective-permute-start(f32[32,32,128]{2,1,0:T(8,128)} %get-tuple-element.130), channel_id=1, source_target_pairs={{0,8},{8,0},{16,24},{24,16},{1,9},{9,1},{17,25},{25,17},{2,10},{10... | collective-permute-start | bytes 1572872 | tf_op jit(solution)/shard_map/ppermute | solution.py:44
  98.7 9.7 %collective-permute-start.23 = (f32[24,32,128]{2,1,0:T(8,128)S(1)}, f32[24,32,128]{2,1,0:T(8,128)S(1)}, u32[]{:S(2)}, u32[]{:S(2)}) collective-permute-start(f32[24,32,128]{2,1,0:T(8,128)S(1)} %get-tuple-element.222), channel_id=1, source_target_pairs={{0,24},{8,16},{16,8},{24,0},{1,25},{9,17},{17,9},{25,1},{2,26},{10... | collective-permute-start | bytes 1179656 | tf_op jit(solution)/shard_map/ppermute | solution.py:44
  108.7 7.6 %collective-permute-start.24 = (f32[8,32,128]{2,1,0:T(8,128)S(1)}, f32[8,32,128]{2,1,0:T(8,128)S(1)}, u32[]{:S(2)}, u32[]{:S(2)}) collective-permute-start(f32[8,32,128]{2,1,0:T(8,128)S(1)} %pad_maximum_fusion.16), channel_id=1, source_target_pairs={{0,8},{8,0},{16,24},{24,16},{1,9},{9,1},{17,25},{25,17},{2,10},{10... | collective-permute-start | bytes 393224 | tf_op jit(solution)/shard_map/ppermute | solution.py:44
  116.3 7.5 %collective-permute-start.25 = (f32[16,32,128]{2,1,0:T(8,128)S(1)}, f32[16,32,128]{2,1,0:T(8,128)S(1)}, u32[]{:S(2)}, u32[]{:S(2)}) collective-permute-start(f32[16,32,128]{2,1,0:T(8,128)S(1)} %pad_maximum_fusion.3), channel_id=1, source_target_pairs={{0,4},{4,0},{1,5},{5,1},{2,6},{6,2},{3,7},{7,3},{8,12},{12,8},{9,1... | collective-permute-start | bytes 786440 | tf_op jit(solution)/shard_map/ppermute | solution.py:44
  119.2 8.2 %collective-permute-start.28 = (f32[16,32,128]{2,1,0:T(8,128)S(1)}, f32[16,32,128]{2,1,0:T(8,128)S(1)}, u32[]{:S(2)}, u32[]{:S(2)}) collective-permute-start(f32[16,32,128]{2,1,0:T(8,128)S(1)} %pad_maximum_fusion.4), channel_id=1, source_target_pairs={{0,8},{8,0},{16,24},{24,16},{1,9},{9,1},{17,25},{25,17},{2,10},{10... | collective-permute-start | bytes 786440 | tf_op jit(solution)/shard_map/ppermute | solution.py:44
  120.5 8.9 %collective-permute-start.31 = (f32[16,32,128]{2,1,0:T(8,128)S(1)}, f32[16,32,128]{2,1,0:T(8,128)S(1)}, u32[]{:S(2)}, u32[]{:S(2)}) collective-permute-start(f32[16,32,128]{2,1,0:T(8,128)S(1)} %pad_maximum_fusion.5), channel_id=1, source_target_pairs={{0,2},{2,0},{1,3},{3,1},{4,6},{6,4},{5,7},{7,5},{8,10},{10,8},{9,1... | collective-permute-start | bytes 786440 | tf_op jit(solution)/shard_map/ppermute | solution.py:44
  123.8 17.1 %collective-permute-start.26 = (f32[32,32,128]{2,1,0:T(8,128)S(1)}, f32[32,32,128]{2,1,0:T(8,128)S(1)}, u32[]{:S(2)}, u32[]{:S(2)}) collective-permute-start(f32[32,32,128]{2,1,0:T(8,128)S(1)} %constant_dynamic-update-slice_fusion.15.refs_0_), channel_id=1, source_target_pairs={{0,2},{2,0},{1,3},{3,1},{4,6},{6,4},{5,7},{7,5},{8,10},{10,8},{9,1... | collective-permute-start | bytes 1572872 | tf_op jit(solution)/shard_map/ppermute | solution.py:44
  127.4 13.5 %collective-permute-start.29 = (f32[32,32,128]{2,1,0:T(8,128)S(1)}, f32[32,32,128]{2,1,0:T(8,128)S(1)}, u32[]{:S(2)}, u32[]{:S(2)}) collective-permute-start(f32[32,32,128]{2,1,0:T(8,128)S(1)} %constant_dynamic-update-slice_fusion.18.refs_1_), channel_id=1, source_target_pairs={{0,4},{4,0},{1,5},{5,1},{2,6},{6,2},{3,7},{7,3},{8,12},{12,8},{9,1... | collective-permute-start | bytes 1572872 | tf_op jit(solution)/shard_map/ppermute | solution.py:44
  129.5 11.5 %collective-permute-start.32 = (f32[32,32,128]{2,1,0:T(8,128)S(1)}, f32[32,32,128]{2,1,0:T(8,128)S(1)}, u32[]{:S(2)}, u32[]{:S(2)}) collective-permute-start(f32[32,32,128]{2,1,0:T(8,128)S(1)} %constant_dynamic-update-slice_fusion.21.refs_2_), channel_id=1, source_target_pairs={{0,8},{8,0},{16,24},{24,16},{1,9},{9,1},{17,25},{25,17},{2,10},{10... | collective-permute-start | bytes 1572872 | tf_op jit(solution)/shard_map/ppermute | solution.py:44
  149.9 10.9 %collective-permute-start.33 = (f32[32,32,128]{2,1,0:T(8,128)}, f32[32,32,128]{2,1,0:T(8,128)S(1)}, u32[]{:S(2)}, u32[]{:S(2)}) collective-permute-start(f32[32,32,128]{2,1,0:T(8,128)} %get-tuple-element.144), channel_id=1, source_target_pairs={{0,2},{2,0},{1,3},{3,1},{4,6},{6,4},{5,7},{7,5},{8,10},{10,8},{9,1... | collective-permute-start | bytes 1572872 | tf_op jit(solution)/shard_map/ppermute | solution.py:44
  151.2 12.1 %collective-permute-start.36 = (f32[32,32,128]{2,1,0:T(8,128)}, f32[32,32,128]{2,1,0:T(8,128)S(1)}, u32[]{:S(2)}, u32[]{:S(2)}) collective-permute-start(f32[32,32,128]{2,1,0:T(8,128)} %get-tuple-element.153), channel_id=1, source_target_pairs={{0,4},{4,0},{1,5},{5,1},{2,6},{6,2},{3,7},{7,3},{8,12},{12,8},{9,1... | collective-permute-start | bytes 1572872 | tf_op jit(solution)/shard_map/ppermute | solution.py:44
  152.6 13.5 %collective-permute-start.39 = (f32[32,32,128]{2,1,0:T(8,128)}, f32[32,32,128]{2,1,0:T(8,128)S(1)}, u32[]{:S(2)}, u32[]{:S(2)}) collective-permute-start(f32[32,32,128]{2,1,0:T(8,128)} %get-tuple-element.162), channel_id=1, source_target_pairs={{0,8},{8,0},{16,24},{24,16},{1,9},{9,1},{17,25},{25,17},{2,10},{10... | collective-permute-start | bytes 1572872 | tf_op jit(solution)/shard_map/ppermute | solution.py:44
  161.9 7.8 %collective-permute-start.34 = (f32[16,32,128]{2,1,0:T(8,128)S(1)}, f32[16,32,128]{2,1,0:T(8,128)S(1)}, u32[]{:S(2)}, u32[]{:S(2)}) collective-permute-start(f32[16,32,128]{2,1,0:T(8,128)S(1)} %slice_add_fusion.5), channel_id=1, source_target_pairs={{0,4},{4,0},{1,5},{5,1},{2,6},{6,2},{3,7},{7,3},{8,12},{12,8},{9,1... | collective-permute-start | bytes 786440 | tf_op jit(solution)/shard_map/ppermute | solution.py:44
  169.7 8.1 %collective-permute-start.35 = (f32[8,32,128]{2,1,0:T(8,128)S(1)}, f32[8,32,128]{2,1,0:T(8,128)S(1)}, u32[]{:S(2)}, u32[]{:S(2)}) collective-permute-start(f32[8,32,128]{2,1,0:T(8,128)S(1)} %slice_add_fusion.18), channel_id=1, source_target_pairs={{0,8},{8,0},{16,24},{24,16},{1,9},{9,1},{17,25},{25,17},{2,10},{10... | collective-permute-start | bytes 393224 | tf_op jit(solution)/shard_map/ppermute | solution.py:44
  178.5 12.5 %collective-permute-start.42 = (f32[24,32,128]{2,1,0:T(8,128)S(1)}, f32[24,32,128]{2,1,0:T(8,128)S(1)}, u32[]{:S(2)}, u32[]{:S(2)}) collective-permute-start(f32[24,32,128]{2,1,0:T(8,128)S(1)} %get-tuple-element.210), channel_id=1, source_target_pairs={{0,24},{8,16},{16,8},{24,0},{1,25},{9,17},{17,9},{25,1},{2,26},{10... | collective-permute-start | bytes 1179656 | tf_op jit(solution)/shard_map/ppermute | solution.py:44
  204.3 15.0 %collective-permute-start.45 = (f32[32,32,128]{2,1,0:T(8,128)S(1)}, f32[32,32,128]{2,1,0:T(8,128)S(1)}, u32[]{:S(2)}, u32[]{:S(2)}) collective-permute-start(f32[32,32,128]{2,1,0:T(8,128)S(1)} %constant_dynamic-update-slice_fusion.30.refs_0_), channel_id=1, source_target_pairs={{0,2},{2,0},{1,3},{3,1},{4,6},{6,4},{5,7},{7,5},{8,10},{10,8},{9,1... | collective-permute-start | bytes 1572872 | tf_op jit(solution)/shard_map/ppermute | solution.py:44
  206.4 13.0 %collective-permute-start.48 = (f32[32,32,128]{2,1,0:T(8,128)S(1)}, f32[32,32,128]{2,1,0:T(8,128)S(1)}, u32[]{:S(2)}, u32[]{:S(2)}) collective-permute-start(f32[32,32,128]{2,1,0:T(8,128)S(1)} %constant_dynamic-update-slice_fusion.33.refs_1_), channel_id=1, source_target_pairs={{0,4},{4,0},{1,5},{5,1},{2,6},{6,2},{3,7},{7,3},{8,12},{12,8},{9,1... | collective-permute-start | bytes 1572872 | tf_op jit(solution)/shard_map/ppermute | solution.py:44
  208.1 11.3 %collective-permute-start.51 = (f32[32,32,128]{2,1,0:T(8,128)S(1)}, f32[32,32,128]{2,1,0:T(8,128)S(1)}, u32[]{:S(2)}, u32[]{:S(2)}) collective-permute-start(f32[32,32,128]{2,1,0:T(8,128)S(1)} %constant_dynamic-update-slice_fusion.36.refs_2_), channel_id=1, source_target_pairs={{0,8},{8,0},{16,24},{24,16},{1,9},{9,1},{17,25},{25,17},{2,10},{10... | collective-permute-start | bytes 1572872 | tf_op jit(solution)/shard_map/ppermute | solution.py:44
  228.4 10.1 %collective-permute-start.58 = (f32[32,32,128]{2,1,0:T(8,128)}, f32[32,32,128]{2,1,0:T(8,128)S(1)}, u32[]{:S(2)}, u32[]{:S(2)}) collective-permute-start(f32[32,32,128]{2,1,0:T(8,128)} %get-tuple-element.194), channel_id=1, source_target_pairs={{0,8},{8,0},{16,24},{24,16},{1,9},{9,1},{17,25},{25,17},{2,10},{10... | collective-permute-start | bytes 1572872 | tf_op jit(solution)/shard_map/ppermute | solution.py:44
  228.5 12.9 %collective-permute-start.55 = (f32[32,32,128]{2,1,0:T(8,128)}, f32[32,32,128]{2,1,0:T(8,128)S(1)}, u32[]{:S(2)}, u32[]{:S(2)}) collective-permute-start(f32[32,32,128]{2,1,0:T(8,128)} %get-tuple-element.185), channel_id=1, source_target_pairs={{0,4},{4,0},{1,5},{5,1},{2,6},{6,2},{3,7},{7,3},{8,12},{12,8},{9,1... | collective-permute-start | bytes 1572872 | tf_op jit(solution)/shard_map/ppermute | solution.py:44
  230.2 13.0 %collective-permute-start.52 = (f32[32,32,128]{2,1,0:T(8,128)}, f32[32,32,128]{2,1,0:T(8,128)S(1)}, u32[]{:S(2)}, u32[]{:S(2)}) collective-permute-start(f32[32,32,128]{2,1,0:T(8,128)} %get-tuple-element.176), channel_id=1, source_target_pairs={{0,2},{2,0},{1,3},{3,1},{4,6},{6,4},{5,7},{7,5},{8,10},{10,8},{9,1... | collective-permute-start | bytes 1572872 | tf_op jit(solution)/shard_map/ppermute | solution.py:44
  259.8 14.7 %all-to-all-start = ((f32[32,1,128]{2,1,0:T(1,128)}), f32[32,1,128]{2,1,0:T(1,128)S(1)}, u32[]{:S(2)}, u32[]{:S(2)}) async-start(f32[32,1,128]{2,1,0:T(1,128)} %broadcast_in_dim.60), calls=%async_computation | async-start | bytes 32768 | tf_op jit(solution)/shard_map/all_to_all | solution.py:354
  267.4 9.2 %collective-permute-start.61 = (f32[12,32,128]{2,1,0:T(8,128)S(1)}, f32[12,32,128]{2,1,0:T(8,128)S(1)}, u32[]{:S(2)}, u32[]{:S(2)}) collective-permute-start(f32[12,32,128]{2,1,0:T(8,128)S(1)} %get-tuple-element.203), channel_id=1, source_target_pairs={{0,24},{8,16},{16,8},{24,0},{1,25},{9,17},{17,9},{25,1},{2,26},{10... | collective-permute-start | bytes 589832 | tf_op jit(solution)/shard_map/ppermute | solution.py:44
  (77 other events, 450.2 us)

commit v14 on v12

--- a/solution.py
+++ b/solution.py
@@ -2,6 +2,7 @@
 
 import jax
 import jax.numpy as jnp
+import numpy as np
 from jax import lax
 from jax.experimental import pallas as pl
 from jax.experimental.pallas import tpu as pltpu
@@ -15,7 +16,7 @@
 CHUNK = 8
 SLOTS = 8
 SPANS = 4
-VMEM = 63 * 1024 * 1024
+VMEM = 60 * 1024 * 1024
 CHIPS = ("z", "y", "x")
 ALL = ("z", "y", "x", "core")
 NEAR = ("x", "y", "z")
@@ -34,23 +35,37 @@
     return [(a, 1) for a in NEAR[turn:] + NEAR[:turn]]
 
 
+def later_moves(part):
+    steps = near_steps(part)[1:]
+    count = len(steps)
+    return [
+        [step for place, step in enumerate(steps) if n >> (count - 1 - place) & 1] for n in range(1, 1 << count)
+    ]
+
+
 def label(place):
     return place ^ (place >> 1)
 
 
-def swap(array, step):
-    axis, distance = step
-    at = {label(i): i for i in range(lax.axis_size(axis))}
-    return lax.ppermute(array, axis, [(i, at[n ^ distance]) for n, i in at.items()])
+def swap(array, *steps):
+    sizes = [lax.axis_size(a) for a in CHIPS]
+    pairs = []
+    for at in np.ndindex(*sizes):
+        to = list(at)
+        for axis, distance in steps:
+            k = CHIPS.index(axis)
+            places = {label(i): i for i in range(sizes[k])}
+            to[k] = places[label(to[k]) ^ distance]
+        pairs.append([int(np.ravel_multi_index(i, sizes)) for i in (at, to)])
+    return lax.ppermute(array, CHIPS, pairs)
+
+
+def swap_cores(array):
+    return lax.ppermute(array, "core", [(0, 1), (1, 0)])
 
 
 def after(value, *others):
     return lax.optimization_barrier((value,) + others)[0]
-
-
-def halves(array):
-    middle = array.shape[0] // 2
-    return array[:middle], array[middle:]
 
 
 def gather_far(block):
@@ -67,10 +82,8 @@
     ]
     pieces = []
     for part, block in enumerate(lax.optimization_barrier(starts)):
-        steps = near_steps(part)
-        for step in reversed(steps[1:]):
-            block = jnp.concatenate([block, swap(block, step)], axis=0)
-        pieces.append((block, swap(block, steps[0])))
+        block = jnp.concatenate([block] + [swap(block, *moves) for moves in later_moves(part)], axis=0)
+        pieces.append((block, swap(block, near_steps(part)[0])))
     return pieces
 
 
@@ -78,15 +91,14 @@
     far = 1 << len(far_steps())
     parts = []
     for part, (keep, send) in enumerate(zip(keeps, sends)):
-        steps = near_steps(part)
-        got = swap(send, steps[0])
-        terms = [keep]
-        for step in steps[1:]:
-            terms.append(got)
-            got = swap(sum([halves(t)[1] for t in terms[1:]], halves(terms[0])[1]), step)
-            *terms, got = lax.optimization_barrier((*terms, got))
-            terms = [halves(t)[0] for t in terms]
-        terms = [jnp.split(t, far) for t in (*terms, got)]
+        got = swap(send, near_steps(part)[0])
+        moves = later_moves(part)
+        length = keep.shape[0] // (1 + len(moves))
+        sends = [keep[k * length : (k + 1) * length] + got[k * length : (k + 1) * length] for k in range(1, 1 + len(moves))]
+        terms = [swap(send, *steps) for send, steps in zip(sends, moves)]
+        keep, got, *terms = lax.optimization_barrier((keep, got, *terms))
+        terms = [keep[:length], got[:length]] + terms
+        terms = [jnp.split(t, far) for t in terms]
         parts.append([sum(t[1:], t[0]) for t in zip(*terms)])
     return [jnp.concatenate(group, axis=0) for group in zip(*parts)]
 
@@ -264,7 +276,6 @@
     num = chips * chip_tiles
     half = columns // CORES
     core = lax.axis_index("core")
-    cores = ("core", 1)
 
     edges = [chip_tiles * k // len(NEAR) for k in range(len(NEAR) + 1)]
 
@@ -294,7 +305,7 @@
     kind = jnp.where(used, jnp.where(col_side == 0, 0, 2 - row_side), 3)
     row = jnp.where(row_side == 1, row, row + num // 2)
     code = (kind * num + row) * num + col
-    other_code = swap(code, cores)
+    other_code = swap_cores(code)
     code = jnp.concatenate([code, other_code])
     kind = code // (num * num)
     slots = jnp.arange(CORES * length, dtype=jnp.int32)
@@ -318,9 +329,9 @@
     mine = jnp.where(core == 0, low, high)
     theirs = jnp.where(core == 0, high, low)
     packed = [theirs, jnp.broadcast_to(relax, (per, 8, size)), jnp.broadcast_to(heat, (per, 8, size))]
-    got = swap(jnp.concatenate(packed, axis=1), cores)
+    got = swap_cores(jnp.concatenate(packed, axis=1))
     tile_values = after(tile_values, got, other_code)
-    other_values = swap(tile_values, cores)
+    other_values = swap_cores(tile_values)
     drive_half = by_core(mine, got[:, :half])
     relax_both = by_core(relax, got[:, half : half + 1])
     heat_both = by_core(heat, got[:, half + 8 : half + 9])
@@ -358,7 +369,7 @@
     flux = relax_both * (drive_half + after(reduce_far(blocks), conductivity))
     first, second = flux[:per], flux[per:]
     mine = jnp.where(core == 0, first, second)
-    got = swap(jnp.where(core == 0, second, first), cores)
+    got = swap_cores(jnp.where(core == 0, second, first))
     both = jnp.concatenate(
         [jnp.where(core == 0, mine, got), jnp.where(core == 0, got, mine)], axis=1
     )

time: 285 us -> 300 us (1.053)
  starting transfers between devices: 86.1 us -> 111 us
  local copies, waits for them, and re-layouts: 28.9 us -> 8 us
  waiting for transfers between devices: 50.1 us -> 61.9 us
    ppermute x63 -> x81, starting transfers between devices: 81.8 us -> 109 us  [the longest x77 108 us: swap(): return lax.ppermute(array, CHIPS, pairs)]
    ppermute x63 -> x81, waiting for transfers between devices: 46.6 us -> 58.4 us  [the longest x77 56.1 us: swap(): return lax.ppermute(array, CHIPS, pairs)]
    add x18 -> x9, other arithmetic: 17.3 us -> 6.69 us  [reduce_near(): keep[k * length:(k + 1) * length] + got[k * length:(k + 1) * length]]
    unnamed x62 -> x91, local copies, waits for them, and re-layouts: 13.6 us -> 4.6 us
    unnamed x10, other arithmetic: 0.22 us -> 7.01 us
    concatenate x9, local copies, waits for them, and re-layouts: 6.5 us -> 0.09 us  [gather_near(): jnp.concatenate([block] + [swap(block, *moves) for moves in later_moves(p...]
    slice x19 -> x0, local copies, waits for them, and re-layouts: 6.09 us -> none  [halves(): return (array[:middle], array[middle:])]
  transfers between devices with their start and end apart: 64 -> 82, of which waited for: 30 -> 34; matrix products, arithmetic and copies ran while one was open for 16% -> 5% of each run, Pallas kernels for 24% -> 23%
where the time goes in v14:
time: 300 us; the launch traced here: 298 us
  starting transfers between devices  111 us (37%)
  Pallas kernels  89.2 us (30%)
  waiting for transfers between devices  61.9 us (21%)
  other arithmetic  25 us (8%)
  local copies, waits for them, and re-layouts  8 us (3%)
    ppermute x77, starting transfers between devices, swap(): return lax.ppermute(array, CHIPS, pairs)  108 us
    pallas_call x9, Pallas kernels, apply_tiles(): pl.pallas_call(functools.partial(apply_kernel, span, skip, counts, base i...  68.7 us
    ppermute x77, waiting for transfers between devices, swap(): return lax.ppermute(array, CHIPS, pairs)  56.1 us
    pallas_call x2, Pallas kernels, split_tiles(): pl.pallas_call(split_kernel, out_shape=jax.ShapeDtypeStruct((CORES * leng...  20.6 us
    unnamed x10, other arithmetic  7.01 us
    add x9, other arithmetic, reduce_near(): keep[k * length:(k + 1) * length] + got[k * length:(k + 1) * length]  6.69 us
  transfers between devices with their start and end apart: 82, of which 34 were waited for; matrix products, arithmetic and copies ran while one was open for 5% of the time, Pallas kernels for 23%

profile of v14, /device:TPU:0, one launch (start us, length us, event | category | flops | bytes accessed | tf_op | source)
XLA Modules:
  0.0 297.6 jit_solution(8077112941684481040)
XLA Ops:
  8.6 4.9 %collective-permute-start.4 = (f32[12,32,128]{2,1,0:T(8,128)S(1)}, f32[12,32,128]{2,1,0:T(8,128)S(1)}, u32[]{:S(2)}, u32[]{:S(2)}) collective-permute-start(f32[12,32,128]{2,1,0:T(8,128)S(1)} %get-tuple-element.263), channel_id=1, source_target_pairs={{0,24},{2,26},{4,28},{6,30},{8,16},{10,18},{12,20},{14,22},{16,8},... | collective-permute-start | bytes 589832 | tf_op jit(solution)/shard_map/ppermute | solution.py:60
  13.6 10.2 %shard_map.95.refs_0_ = bf16[256,256,128]{2,1,0:T(8,128)(2,1)} custom-call(f32[128,128,128]{2,1,0:T(8,128)} %tile_ref), custom_call_target="tpu_custom_call" | custom-call | flops 6291456 | bytes 16777216 | tf_op jit(solution)/shard_map/pallas_call | solution.py:142
  31.0 3.7 %collective-permute-start.11 = (f32[8,32,128]{2,1,0:T(8,128)S(1)}, f32[8,32,128]{2,1,0:T(8,128)S(1)}, u32[]{:S(2)}, u32[]{:S(2)}) collective-permute-start(f32[8,32,128]{2,1,0:T(8,128)S(1)} %pad_maximum_fusion.5), channel_id=1, source_target_pairs={{0,10},{2,8},{4,14},{6,12},{8,2},{10,0},{12,6},{14,4},{16,26},{18,... | collective-permute-start | bytes 393224 | tf_op jit(solution)/shard_map/ppermute | solution.py:60
  34.9 2.2 collective-permute-start.13
  42.1 2.5 collective-permute-start.12
  48.0 10.3 %shard_map.96.pairs_ref = bf16[256,256,128]{2,1,0:T(8,128)(2,1)} custom-call(f32[128,128,128]{2,1,0:T(8,128)} %collective-permute-done.2.tile_ref, bf16[256,256,128]{2,1,0:T(8,128)(2,1)} %shard_map.95.refs_0_), custom_call_target="tpu_custom_call", output_to_operand_aliasing={{}: (1, {})} | custom-call | flops 6291456 | bytes 16777216 | tf_op jit(solution)/shard_map/pallas_call | solution.py:142
  58.4 9.2 %shard_map.97 = (f32[96,32,128]{2,1,0:T(8,128)}, f32[96,32,128]{2,1,0:T(8,128)}) custom-call(s32[772]{0:T(1024)} %pad_add_fusion.places_ref, bf16[256,256,128]{2,1,0:T(8,128)(2,1)} %shard_map.96.pairs_ref, f32[32,32,128]{2,1,0:T(8,128)} %copy-done.19, f32[32,32,128]{2,1,0:T(8,128)} %copy-done.16, f32[32,32,128]{2,1,0:T(8,128)} %copy-done.11), custom_call_target="tpu_custom_call" | custom-call | flops 536870912 | bytes 14680064 | tf_op jit(solution)/shard_map/pallas_call | solution.py:242
  68.8 7.2 %shard_map.99 = (f32[32,32,128]{2,1,0:T(8,128)}, f32[32,32,128]{2,1,0:T(8,128)}, f32[32,32,128]{2,1,0:T(8,128)}) custom-call(s32[772]{0:T(1024)} %pad_add_fusion.places_ref, bf16[256,256,128]{2,1,0:T(8,128)(2,1)} %shard_map.96.pairs_ref, f32[32,32,128]{2,1,0:T(8,128)} %copy-done.2, f32[32,32,128]{2,1,0:T(8,128)} %copy-done.3, f32[32,32,128]{2,1,0:T(8,128)} %copy-done.6, ...), custom_call_target="tpu_custom_call" | custom-call | flops 268435456 | bytes 7340032 | tf_op jit(solution)/shard_map/pallas_call | solution.py:242
  78.4 6.5 %shard_map.98 = (f32[32,32,128]{2,1,0:T(8,128)}, f32[32,32,128]{2,1,0:T(8,128)}, f32[32,32,128]{2,1,0:T(8,128)}) custom-call(s32[772]{0:T(1024)} %pad_add_fusion.places_ref, bf16[256,256,128]{2,1,0:T(8,128)(2,1)} %shard_map.96.pairs_ref, f32[32,32,128]{2,1,0:T(8,128)} %copy-done.2, f32[32,32,128]{2,1,0:T(8,128)} %copy-done.3, f32[32,32,128]{2,1,0:T(8,128)} %copy-done.6, ...), custom_call_target="tpu_custom_call" | custom-call | flops 268435456 | bytes 7340032 | tf_op jit(solution)/shard_map/pallas_call | solution.py:242
  97.4 2.3 collective-permute-start.27
  102.6 2.9 collective-permute-done.28
  111.2 7.6 %collective-permute-done.29 = f32[24,32,128]{2,1,0:T(8,128)S(1)} collective-permute-done((f32[24,32,128]{2,1,0:T(8,128)S(1)}, f32[24,32,128]{2,1,0:T(8,128)S(1)}, u32[]{:S(2)}, u32[]{:S(2)}) %collective-permute-start.29) | collective-permute-done | bytes 393248 | tf_op jit(solution)/shard_map/ppermute | solution.py:60
  119.1 4.4 %collective-permute-start.30 = (f32[8,32,128]{2,1,0:T(8,128)S(1)}, f32[8,32,128]{2,1,0:T(8,128)S(1)}, u32[]{:S(2)}, u32[]{:S(2)}) collective-permute-start(f32[8,32,128]{2,1,0:T(8,128)S(1)} %pad_maximum_fusion.7), channel_id=1, source_target_pairs={{0,8},{2,10},{4,12},{6,14},{8,0},{10,2},{12,4},{14,6},{16,24},{18,... | collective-permute-start | bytes 393224 | tf_op jit(solution)/shard_map/ppermute | solution.py:60
  139.4 2.3 collective-permute-done.40
  143.3 9.2 %shard_map.100 = (f32[96,32,128]{2,1,0:T(8,128)}, f32[96,32,128]{2,1,0:T(8,128)}) custom-call(s32[772]{0:T(1024)} %pad_add_fusion.places_ref, bf16[256,256,128]{2,1,0:T(8,128)(2,1)} %shard_map.96.pairs_ref, f32[32,32,128]{2,1,0:T(8,128)} %copy-done.17, f32[32,32,128]{2,1,0:T(8,128)} %copy-done.14, f32[32,32,128]{2,1,0:T(8,128)} %copy-done.12), custom_call_target="tpu_custom_call" | custom-call | flops 536870912 | bytes 14680064 | tf_op jit(solution)/shard_map/pallas_call | solution.py:242
  153.7 7.2 %shard_map.102 = (f32[32,32,128]{2,1,0:T(8,128)}, f32[32,32,128]{2,1,0:T(8,128)}, f32[32,32,128]{2,1,0:T(8,128)}) custom-call(s32[772]{0:T(1024)} %pad_add_fusion.places_ref, bf16[256,256,128]{2,1,0:T(8,128)(2,1)} %shard_map.96.pairs_ref, f32[32,32,128]{2,1,0:T(8,128)} %copy-done.5, f32[32,32,128]{2,1,0:T(8,128)} %copy-done.8, f32[32,32,128]{2,1,0:T(8,128)} %copy-done.10, ...), custom_call_target="tpu_custom_call" | custom-call | flops 268435456 | bytes 7340032 | tf_op jit(solution)/shard_map/pallas_call | solution.py:242
  163.4 6.5 %shard_map.101 = (f32[32,32,128]{2,1,0:T(8,128)}, f32[32,32,128]{2,1,0:T(8,128)}, f32[32,32,128]{2,1,0:T(8,128)}) custom-call(s32[772]{0:T(1024)} %pad_add_fusion.places_ref, bf16[256,256,128]{2,1,0:T(8,128)(2,1)} %shard_map.96.pairs_ref, f32[32,32,128]{2,1,0:T(8,128)} %copy-done.5, f32[32,32,128]{2,1,0:T(8,128)} %copy-done.8, f32[32,32,128]{2,1,0:T(8,128)} %copy-done.10, ...), custom_call_target="tpu_custom_call" | custom-call | flops 268435456 | bytes 7340032 | tf_op jit(solution)/shard_map/pallas_call | solution.py:242
  169.9 2.3 collective-permute-done.42
  187.7 2.9 collective-permute-done.53
  195.2 8.7 %collective-permute-done.54 = f32[24,32,128]{2,1,0:T(8,128)S(1)} collective-permute-done((f32[24,32,128]{2,1,0:T(8,128)S(1)}, f32[24,32,128]{2,1,0:T(8,128)S(1)}, u32[]{:S(2)}, u32[]{:S(2)}) %collective-permute-start.54) | collective-permute-done | bytes 393248 | tf_op jit(solution)/shard_map/ppermute | solution.py:60
  204.2 4.9 %collective-permute-start.55 = (f32[8,32,128]{2,1,0:T(8,128)S(1)}, f32[8,32,128]{2,1,0:T(8,128)S(1)}, u32[]{:S(2)}, u32[]{:S(2)}) collective-permute-start(f32[8,32,128]{2,1,0:T(8,128)S(1)} %pad_maximum_fusion.10), channel_id=1, source_target_pairs={{0,8},{2,10},{4,12},{6,14},{8,0},{10,2},{12,4},{14,6},{16,24},{18,... | collective-permute-start | bytes 393224 | tf_op jit(solution)/shard_map/ppermute | solution.py:60
  209.0 3.0 %collective-permute-start.56 = (f32[8,32,128]{2,1,0:T(8,128)S(1)}, f32[8,32,128]{2,1,0:T(8,128)S(1)}, u32[]{:S(2)}, u32[]{:S(2)}) collective-permute-start(f32[8,32,128]{2,1,0:T(8,128)S(1)} %pad_maximum_fusion.10), channel_id=1, source_target_pairs={{0,4},{2,6},{4,0},{6,2},{8,12},{10,14},{12,8},{14,10},{16,20},{18,... | collective-permute-start | bytes 393224 | tf_op jit(solution)/shard_map/ppermute | solution.py:60
  215.6 2.3 collective-permute-start.61
  226.1 2.7 collective-permute-done.65
  229.7 9.4 %shard_map.103 = (f32[96,32,128]{2,1,0:T(8,128)}, f32[96,32,128]{2,1,0:T(8,128)}) custom-call(s32[772]{0:T(1024)} %pad_add_fusion.places_ref, bf16[256,256,128]{2,1,0:T(8,128)(2,1)} %shard_map.96.pairs_ref, f32[32,32,128]{2,1,0:T(8,128)} %copy-done.18, f32[32,32,128]{2,1,0:T(8,128)} %copy-done.15, f32[32,32,128]{2,1,0:T(8,128)} %copy-done.13), custom_call_target="tpu_custom_call" | custom-call | flops 536870912 | bytes 14680064 | tf_op jit(solution)/shard_map/pallas_call | solution.py:242
  241.5 7.2 %shard_map.105 = (f32[32,32,128]{2,1,0:T(8,128)}, f32[32,32,128]{2,1,0:T(8,128)}, f32[32,32,128]{2,1,0:T(8,128)}) custom-call(s32[772]{0:T(1024)} %pad_add_fusion.places_ref, bf16[256,256,128]{2,1,0:T(8,128)(2,1)} %shard_map.96.pairs_ref, f32[32,32,128]{2,1,0:T(8,128)} %copy-done.4, f32[32,32,128]{2,1,0:T(8,128)} %copy-done.7, f32[32,32,128]{2,1,0:T(8,128)} %copy-done.9, ...), custom_call_target="tpu_custom_call" | custom-call | flops 268435456 | bytes 7340032 | tf_op jit(solution)/shard_map/pallas_call | solution.py:242
  250.7 6.5 %shard_map.104 = (f32[32,32,128]{2,1,0:T(8,128)}, f32[32,32,128]{2,1,0:T(8,128)}, f32[32,32,128]{2,1,0:T(8,128)}) custom-call(s32[772]{0:T(1024)} %pad_add_fusion.places_ref, bf16[256,256,128]{2,1,0:T(8,128)(2,1)} %shard_map.96.pairs_ref, f32[32,32,128]{2,1,0:T(8,128)} %copy-done.4, f32[32,32,128]{2,1,0:T(8,128)} %copy-done.7, f32[32,32,128]{2,1,0:T(8,128)} %copy-done.9, ...), custom_call_target="tpu_custom_call" | custom-call | flops 268435456 | bytes 7340032 | tf_op jit(solution)/shard_map/pallas_call | solution.py:242
  257.3 2.7 collective-permute-done.75
  267.2 2.3 collective-permute-start.74
  283.7 2.5 all-to-all-start
  286.2 3.7 %collective-permute-start.79 = (f32[12,32,128]{2,1,0:T(8,128)S(1)}, f32[12,32,128]{2,1,0:T(8,128)S(1)}, u32[]{:S(2)}, u32[]{:S(2)}) collective-permute-start(f32[12,32,128]{2,1,0:T(8,128)S(1)} %get-tuple-element.167), channel_id=1, source_target_pairs={{0,24},{2,26},{4,28},{6,30},{8,16},{10,18},{12,20},{14,22},{16,8},... | collective-permute-start | bytes 589832 | tf_op jit(solution)/shard_map/ppermute | solution.py:60
  289.9 3.4 %all-to-all-done = f32[32,1,128]{2,1,0:T(1,128)S(1)} async-done(((f32[32,1,128]{2,1,0:T(1,128)}), f32[32,1,128]{2,1,0:T(1,128)S(1)}, u32[]{:S(2)}, u32[]{:S(2)}) %all-to-all-start) | async-done | bytes 16416 | tf_op jit(solution)/shard_map/all_to_all | solution.py:364
  (322 shorter events, 131.8 us)
Async XLA Ops:
  6.1 41.9 %collective-permute-start.2 = (f32[128,128,128]{2,1,0:T(8,128)}, f32[128,128,128]{2,1,0:T(8,128)}, u32[]{:S(2)}, u32[]{:S(2)}) collective-permute-start(f32[128,128,128]{2,1,0:T(8,128)} %tile_ref), channel_id=1, source_target_pairs={{0,1},{1,0},{2,3},{3,2},{4,5},{5,4},{6,7},{7,6},{8,9},{9,8},{10,11... | collective-permute-start | bytes 25165832 | tf_op jit(solution)/shard_map/ppermute | solution.py:64
  8.6 15.9 %collective-permute-start.4 = (f32[12,32,128]{2,1,0:T(8,128)S(1)}, f32[12,32,128]{2,1,0:T(8,128)S(1)}, u32[]{:S(2)}, u32[]{:S(2)}) collective-permute-start(f32[12,32,128]{2,1,0:T(8,128)S(1)} %get-tuple-element.263), channel_id=1, source_target_pairs={{0,24},{2,26},{4,28},{6,30},{8,16},{10,18},{12,20},{14,22},{16,8},... | collective-permute-start | bytes 589832 | tf_op jit(solution)/shard_map/ppermute | solution.py:60
  13.5 10.3 %collective-permute-start.3 = (f32[12,2,128]{2,0,1:T(8,128)S(1)}, f32[12,2,128]{2,0,1:T(8,128)S(1)}, u32[]{:S(2)}, u32[]{:S(2)}) collective-permute-start(f32[12,2,128]{2,0,1:T(8,128)S(1)} %pad_maximum_fusion.13), channel_id=1, source_target_pairs={{0,24},{2,26},{4,28},{6,30},{8,16},{10,18},{12,20},{14,22},{16,8},... | collective-permute-start | bytes 36872 | tf_op jit(solution)/shard_map/ppermute | solution.py:60
  26.3 8.6 %collective-permute-start.7 = (f32[8,32,128]{2,1,0:T(8,128)S(1)}, f32[8,32,128]{2,1,0:T(8,128)S(1)}, u32[]{:S(2)}, u32[]{:S(2)}) collective-permute-start(f32[8,32,128]{2,1,0:T(8,128)S(1)} %pad_maximum_fusion.4), channel_id=1, source_target_pairs={{0,12},{2,14},{4,8},{6,10},{8,4},{10,6},{12,0},{14,2},{16,28},{18,... | collective-permute-start | bytes 393224 | tf_op jit(solution)/shard_map/ppermute | solution.py:60
  28.1 9.1 %collective-permute-start.9 = (f32[8,32,128]{2,1,0:T(8,128)S(1)}, f32[8,32,128]{2,1,0:T(8,128)S(1)}, u32[]{:S(2)}, u32[]{:S(2)}) collective-permute-start(f32[8,32,128]{2,1,0:T(8,128)S(1)} %pad_maximum_fusion.5), channel_id=1, source_target_pairs={{0,2},{2,0},{4,6},{6,4},{8,10},{10,8},{12,14},{14,12},{16,18},{18,... | collective-permute-start | bytes 393224 | tf_op jit(solution)/shard_map/ppermute | solution.py:60
  39.4 28.1 %collective-permute-start.8 = (f32[32,32,128]{2,1,0:T(8,128)S(1)}, f32[32,32,128]{2,1,0:T(8,128)S(1)}, u32[]{:S(2)}, u32[]{:S(2)}) collective-permute-start(f32[32,32,128]{2,1,0:T(8,128)S(1)} %constant_dynamic-update-slice_fusion.refs_0_), channel_id=1, source_target_pairs={{0,2},{2,0},{4,6},{6,4},{8,10},{10,8},{12,14},{14,12},{16,18},{18,... | collective-permute-start | bytes 1572872 | tf_op jit(solution)/shard_map/ppermute | solution.py:60
  42.1 25.4 %collective-permute-start.12 = (f32[32,32,128]{2,1,0:T(8,128)S(1)}, f32[32,32,128]{2,1,0:T(8,128)S(1)}, u32[]{:S(2)}, u32[]{:S(2)}) collective-permute-start(f32[32,32,128]{2,1,0:T(8,128)S(1)} %constant_dynamic-update-slice_fusion.4.refs_1_), channel_id=1, source_target_pairs={{0,4},{2,6},{4,0},{6,2},{8,12},{10,14},{12,8},{14,10},{16,20},{18,... | collective-permute-start | bytes 1572872 | tf_op jit(solution)/shard_map/ppermute | solution.py:60
  46.0 21.6 %collective-permute-start.16 = (f32[32,32,128]{2,1,0:T(8,128)S(1)}, f32[32,32,128]{2,1,0:T(8,128)S(1)}, u32[]{:S(2)}, u32[]{:S(2)}) collective-permute-start(f32[32,32,128]{2,1,0:T(8,128)S(1)} %constant_dynamic-update-slice_fusion.8.refs_2_), channel_id=1, source_target_pairs={{0,8},{2,10},{4,12},{6,14},{8,0},{10,2},{12,4},{14,6},{16,24},{18,... | collective-permute-start | bytes 1572872 | tf_op jit(solution)/shard_map/ppermute | solution.py:60
  75.9 9.8 %collective-permute-start.17 = (f32[32,32,128]{2,1,0:T(8,128)}, f32[32,32,128]{2,1,0:T(8,128)S(1)}, u32[]{:S(2)}, u32[]{:S(2)}) collective-permute-start(f32[32,32,128]{2,1,0:T(8,128)} %get-tuple-element.94), channel_id=1, source_target_pairs={{0,2},{2,0},{4,6},{6,4},{8,10},{10,8},{12,14},{14,12},{16,18},{18,... | collective-permute-start | bytes 1572872 | tf_op jit(solution)/shard_map/ppermute | solution.py:60
  77.2 13.2 %collective-permute-start.21 = (f32[32,32,128]{2,1,0:T(8,128)}, f32[32,32,128]{2,1,0:T(8,128)S(1)}, u32[]{:S(2)}, u32[]{:S(2)}) collective-permute-start(f32[32,32,128]{2,1,0:T(8,128)} %get-tuple-element.101), channel_id=1, source_target_pairs={{0,4},{2,6},{4,0},{6,2},{8,12},{10,14},{12,8},{14,10},{16,20},{18,... | collective-permute-start | bytes 1572872 | tf_op jit(solution)/shard_map/ppermute | solution.py:60
  77.2 15.9 %collective-permute-start.25 = (f32[32,32,128]{2,1,0:T(8,128)}, f32[32,32,128]{2,1,0:T(8,128)S(1)}, u32[]{:S(2)}, u32[]{:S(2)}) collective-permute-start(f32[32,32,128]{2,1,0:T(8,128)} %get-tuple-element.108), channel_id=1, source_target_pairs={{0,8},{2,10},{4,12},{6,14},{8,0},{10,2},{12,4},{14,6},{16,24},{18,... | collective-permute-start | bytes 1572872 | tf_op jit(solution)/shard_map/ppermute | solution.py:60
  109.1 9.7 %collective-permute-start.29 = (f32[24,32,128]{2,1,0:T(8,128)S(1)}, f32[24,32,128]{2,1,0:T(8,128)S(1)}, u32[]{:S(2)}, u32[]{:S(2)}) collective-permute-start(f32[24,32,128]{2,1,0:T(8,128)S(1)} %get-tuple-element.186), channel_id=1, source_target_pairs={{0,24},{2,26},{4,28},{6,30},{8,16},{10,18},{12,20},{14,22},{16,8},... | collective-permute-start | bytes 1179656 | tf_op jit(solution)/shard_map/ppermute | solution.py:60
  119.1 8.9 %collective-permute-start.30 = (f32[8,32,128]{2,1,0:T(8,128)S(1)}, f32[8,32,128]{2,1,0:T(8,128)S(1)}, u32[]{:S(2)}, u32[]{:S(2)}) collective-permute-start(f32[8,32,128]{2,1,0:T(8,128)S(1)} %pad_maximum_fusion.7), channel_id=1, source_target_pairs={{0,8},{2,10},{4,12},{6,14},{8,0},{10,2},{12,4},{14,6},{16,24},{18,... | collective-permute-start | bytes 393224 | tf_op jit(solution)/shard_map/ppermute | solution.py:60
  126.0 8.5 %collective-permute-start.35 = (f32[8,32,128]{2,1,0:T(8,128)S(1)}, f32[8,32,128]{2,1,0:T(8,128)S(1)}, u32[]{:S(2)}, u32[]{:S(2)}) collective-permute-start(f32[8,32,128]{2,1,0:T(8,128)S(1)} %pad_maximum_fusion.8), channel_id=1, source_target_pairs={{0,8},{2,10},{4,12},{6,14},{8,0},{10,2},{12,4},{14,6},{16,24},{18,... | collective-permute-start | bytes 393224 | tf_op jit(solution)/shard_map/ppermute | solution.py:60
  134.6 17.9 %collective-permute-start.33 = (f32[32,32,128]{2,1,0:T(8,128)S(1)}, f32[32,32,128]{2,1,0:T(8,128)S(1)}, u32[]{:S(2)}, u32[]{:S(2)}) collective-permute-start(f32[32,32,128]{2,1,0:T(8,128)S(1)} %constant_dynamic-update-slice_fusion.18.refs_0_), channel_id=1, source_target_pairs={{0,2},{2,0},{4,6},{6,4},{8,10},{10,8},{12,14},{14,12},{16,18},{18,... | collective-permute-start | bytes 1572872 | tf_op jit(solution)/shard_map/ppermute | solution.py:60
  135.4 17.1 %collective-permute-start.37 = (f32[32,32,128]{2,1,0:T(8,128)S(1)}, f32[32,32,128]{2,1,0:T(8,128)S(1)}, u32[]{:S(2)}, u32[]{:S(2)}) collective-permute-start(f32[32,32,128]{2,1,0:T(8,128)S(1)} %constant_dynamic-update-slice_fusion.22.refs_1_), channel_id=1, source_target_pairs={{0,4},{2,6},{4,0},{6,2},{8,12},{10,14},{12,8},{14,10},{16,20},{18,... | collective-permute-start | bytes 1572872 | tf_op jit(solution)/shard_map/ppermute | solution.py:60
  141.8 11.1 %collective-permute-start.41 = (f32[32,32,128]{2,1,0:T(8,128)S(1)}, f32[32,32,128]{2,1,0:T(8,128)S(1)}, u32[]{:S(2)}, u32[]{:S(2)}) collective-permute-start(f32[32,32,128]{2,1,0:T(8,128)S(1)} %constant_dynamic-update-slice_fusion.26.refs_2_), channel_id=1, source_target_pairs={{0,8},{2,10},{4,12},{6,14},{8,0},{10,2},{12,4},{14,6},{16,24},{18,... | collective-permute-start | bytes 1572872 | tf_op jit(solution)/shard_map/ppermute | solution.py:60
  160.9 11.3 %collective-permute-start.42 = (f32[32,32,128]{2,1,0:T(8,128)}, f32[32,32,128]{2,1,0:T(8,128)S(1)}, u32[]{:S(2)}, u32[]{:S(2)}) collective-permute-start(f32[32,32,128]{2,1,0:T(8,128)} %get-tuple-element.120), channel_id=1, source_target_pairs={{0,2},{2,0},{4,6},{6,4},{8,10},{10,8},{12,14},{14,12},{16,18},{18,... | collective-permute-start | bytes 1572872 | tf_op jit(solution)/shard_map/ppermute | solution.py:60
  161.6 15.2 %collective-permute-start.46 = (f32[32,32,128]{2,1,0:T(8,128)}, f32[32,32,128]{2,1,0:T(8,128)S(1)}, u32[]{:S(2)}, u32[]{:S(2)}) collective-permute-start(f32[32,32,128]{2,1,0:T(8,128)} %get-tuple-element.127), channel_id=1, source_target_pairs={{0,4},{2,6},{4,0},{6,2},{8,12},{10,14},{12,8},{14,10},{16,20},{18,... | collective-permute-start | bytes 1572872 | tf_op jit(solution)/shard_map/ppermute | solution.py:60
  163.1 15.3 %collective-permute-start.50 = (f32[32,32,128]{2,1,0:T(8,128)}, f32[32,32,128]{2,1,0:T(8,128)S(1)}, u32[]{:S(2)}, u32[]{:S(2)}) collective-permute-start(f32[32,32,128]{2,1,0:T(8,128)} %get-tuple-element.134), channel_id=1, source_target_pairs={{0,8},{2,10},{4,12},{6,14},{8,0},{10,2},{12,4},{14,6},{16,24},{18,... | collective-permute-start | bytes 1572872 | tf_op jit(solution)/shard_map/ppermute | solution.py:60
  194.2 9.7 %collective-permute-start.54 = (f32[24,32,128]{2,1,0:T(8,128)S(1)}, f32[24,32,128]{2,1,0:T(8,128)S(1)}, u32[]{:S(2)}, u32[]{:S(2)}) collective-permute-start(f32[24,32,128]{2,1,0:T(8,128)S(1)} %get-tuple-element.174), channel_id=1, source_target_pairs={{0,24},{2,26},{4,28},{6,30},{8,16},{10,18},{12,20},{14,22},{16,8},... | collective-permute-start | bytes 1179656 | tf_op jit(solution)/shard_map/ppermute | solution.py:60
  204.2 11.4 %collective-permute-start.55 = (f32[8,32,128]{2,1,0:T(8,128)S(1)}, f32[8,32,128]{2,1,0:T(8,128)S(1)}, u32[]{:S(2)}, u32[]{:S(2)}) collective-permute-start(f32[8,32,128]{2,1,0:T(8,128)S(1)} %pad_maximum_fusion.10), channel_id=1, source_target_pairs={{0,8},{2,10},{4,12},{6,14},{8,0},{10,2},{12,4},{14,6},{16,24},{18,... | collective-permute-start | bytes 393224 | tf_op jit(solution)/shard_map/ppermute | solution.py:60
  209.0 8.8 %collective-permute-start.56 = (f32[8,32,128]{2,1,0:T(8,128)S(1)}, f32[8,32,128]{2,1,0:T(8,128)S(1)}, u32[]{:S(2)}, u32[]{:S(2)}) collective-permute-start(f32[8,32,128]{2,1,0:T(8,128)S(1)} %pad_maximum_fusion.10), channel_id=1, source_target_pairs={{0,4},{2,6},{4,0},{6,2},{8,12},{10,14},{12,8},{14,10},{16,20},{18,... | collective-permute-start | bytes 393224 | tf_op jit(solution)/shard_map/ppermute | solution.py:60
  220.2 8.6 %collective-permute-start.65 = (f32[8,32,128]{2,1,0:T(8,128)S(1)}, f32[8,32,128]{2,1,0:T(8,128)S(1)}, u32[]{:S(2)}, u32[]{:S(2)}) collective-permute-start(f32[8,32,128]{2,1,0:T(8,128)S(1)} %pad_maximum_fusion.12), channel_id=1, source_target_pairs={{0,6},{2,4},{4,2},{6,0},{8,14},{10,12},{12,10},{14,8},{16,22},{18,... | collective-permute-start | bytes 393224 | tf_op jit(solution)/shard_map/ppermute | solution.py:60
  221.7 17.4 %collective-permute-start.58 = (f32[32,32,128]{2,1,0:T(8,128)S(1)}, f32[32,32,128]{2,1,0:T(8,128)S(1)}, u32[]{:S(2)}, u32[]{:S(2)}) collective-permute-start(f32[32,32,128]{2,1,0:T(8,128)S(1)} %constant_dynamic-update-slice_fusion.36.refs_0_), channel_id=1, source_target_pairs={{0,2},{2,0},{4,6},{6,4},{8,10},{10,8},{12,14},{14,12},{16,18},{18,... | collective-permute-start | bytes 1572872 | tf_op jit(solution)/shard_map/ppermute | solution.py:60
  223.1 16.0 %collective-permute-start.62 = (f32[32,32,128]{2,1,0:T(8,128)S(1)}, f32[32,32,128]{2,1,0:T(8,128)S(1)}, u32[]{:S(2)}, u32[]{:S(2)}) collective-permute-start(f32[32,32,128]{2,1,0:T(8,128)S(1)} %constant_dynamic-update-slice_fusion.40.refs_1_), channel_id=1, source_target_pairs={{0,4},{2,6},{4,0},{6,2},{8,12},{10,14},{12,8},{14,10},{16,20},{18,... | collective-permute-start | bytes 1572872 | tf_op jit(solution)/shard_map/ppermute | solution.py:60
  228.8 11.9 %collective-permute-start.66 = (f32[32,32,128]{2,1,0:T(8,128)S(1)}, f32[32,32,128]{2,1,0:T(8,128)S(1)}, u32[]{:S(2)}, u32[]{:S(2)}) collective-permute-start(f32[32,32,128]{2,1,0:T(8,128)S(1)} %constant_dynamic-update-slice_fusion.44.refs_2_), channel_id=1, source_target_pairs={{0,8},{2,10},{4,12},{6,14},{8,0},{10,2},{12,4},{14,6},{16,24},{18,... | collective-permute-start | bytes 1572872 | tf_op jit(solution)/shard_map/ppermute | solution.py:60
  248.6 11.3 %collective-permute-start.75 = (f32[32,32,128]{2,1,0:T(8,128)}, f32[32,32,128]{2,1,0:T(8,128)S(1)}, u32[]{:S(2)}, u32[]{:S(2)}) collective-permute-start(f32[32,32,128]{2,1,0:T(8,128)} %get-tuple-element.160), channel_id=1, source_target_pairs={{0,8},{2,10},{4,12},{6,14},{8,0},{10,2},{12,4},{14,6},{16,24},{18,... | collective-permute-start | bytes 1572872 | tf_op jit(solution)/shard_map/ppermute | solution.py:60
  249.4 15.3 %collective-permute-start.71 = (f32[32,32,128]{2,1,0:T(8,128)}, f32[32,32,128]{2,1,0:T(8,128)S(1)}, u32[]{:S(2)}, u32[]{:S(2)}) collective-permute-start(f32[32,32,128]{2,1,0:T(8,128)} %get-tuple-element.153), channel_id=1, source_target_pairs={{0,4},{2,6},{4,0},{6,2},{8,12},{10,14},{12,8},{14,10},{16,20},{18,... | collective-permute-start | bytes 1572872 | tf_op jit(solution)/shard_map/ppermute | solution.py:60
  249.9 16.7 %collective-permute-start.67 = (f32[32,32,128]{2,1,0:T(8,128)}, f32[32,32,128]{2,1,0:T(8,128)S(1)}, u32[]{:S(2)}, u32[]{:S(2)}) collective-permute-start(f32[32,32,128]{2,1,0:T(8,128)} %get-tuple-element.146), channel_id=1, source_target_pairs={{0,2},{2,0},{4,6},{6,4},{8,10},{10,8},{12,14},{14,12},{16,18},{18,... | collective-permute-start | bytes 1572872 | tf_op jit(solution)/shard_map/ppermute | solution.py:60
  283.7 9.7 %all-to-all-start = ((f32[32,1,128]{2,1,0:T(1,128)}), f32[32,1,128]{2,1,0:T(1,128)S(1)}, u32[]{:S(2)}, u32[]{:S(2)}) async-start(f32[32,1,128]{2,1,0:T(1,128)} %broadcast_in_dim.60), calls=%async_computation | async-start | bytes 32768 | tf_op jit(solution)/shard_map/all_to_all | solution.py:364
  286.2 9.2 %collective-permute-start.79 = (f32[12,32,128]{2,1,0:T(8,128)S(1)}, f32[12,32,128]{2,1,0:T(8,128)S(1)}, u32[]{:S(2)}, u32[]{:S(2)}) collective-permute-start(f32[12,32,128]{2,1,0:T(8,128)S(1)} %get-tuple-element.167), channel_id=1, source_target_pairs={{0,24},{2,26},{4,28},{6,30},{8,16},{10,18},{12,20},{14,22},{16,8},... | collective-permute-start | bytes 589832 | tf_op jit(solution)/shard_map/ppermute | solution.py:60
  (82 other events, 574.1 us)

commit v15 on v12

--- a/solution.py
+++ b/solution.py
@@ -15,7 +15,7 @@
 CHUNK = 8
 SLOTS = 8
 SPANS = 4
-VMEM = 63 * 1024 * 1024
+VMEM = 56 * 1024 * 1024
 CHIPS = ("z", "y", "x")
 ALL = ("z", "y", "x", "core")
 NEAR = ("x", "y", "z")
@@ -34,14 +34,9 @@
     return [(a, 1) for a in NEAR[turn:] + NEAR[:turn]]
 
 
-def label(place):
-    return place ^ (place >> 1)
-
-
 def swap(array, step):
     axis, distance = step
-    at = {label(i): i for i in range(lax.axis_size(axis))}
-    return lax.ppermute(array, axis, [(i, at[n ^ distance]) for n, i in at.items()])
+    return lax.ppermute(array, axis, [(i, i ^ distance) for i in range(lax.axis_size(axis))])
 
 
 def after(value, *others):
@@ -273,7 +268,7 @@
         away, width = {}, 1
         for axis in reversed(CHIPS):
             n = lax.axis_size(axis)
-            away[axis] = label((chip // width) % n) ^ label(lax.axis_index(axis))
+            away[axis] = ((chip // width) % n) ^ lax.axis_index(axis)
             width *= n
         side, out = jnp.zeros_like(tile), jnp.zeros_like(tile)
         for part in range(len(NEAR)):

time: 285 us -> 277 us (0.972)
  waiting for transfers between devices: 50.1 us -> 74.1 us
  local copies, waits for them, and re-layouts: 28.9 us -> 9.94 us
  other arithmetic: 26.3 us -> 18.9 us
  starting transfers between devices: 86.1 us -> 81.2 us
    ppermute x63, waiting for transfers between devices: 46.6 us -> 69.7 us  [swap(): lax.ppermute(array, axis, [(i, i ^ distance) for i in range(lax.axis_size...]
    add x18, other arithmetic: 17.3 us -> 9.03 us  [reduce_near(): sum([halves(t)[1] for t in terms[1:]], halves(terms[0])[1])]
    unnamed x62 -> x104, local copies, waits for them, and re-layouts: 13.6 us -> 6.16 us
    concatenate x9, local copies, waits for them, and re-layouts: 6.5 us -> 0.17 us  [gather_near(): block = jnp.concatenate([block, swap(block, step)], axis=0)]
    slice x19 -> x20, local copies, waits for them, and re-layouts: 6.09 us -> 0.31 us  [halves(): return (array[:middle], array[middle:])]
    ppermute x63, starting transfers between devices: 81.8 us -> 78.1 us  [swap(): lax.ppermute(array, axis, [(i, i ^ distance) for i in range(lax.axis_size...]
  transfers between devices with their start and end apart: 64 -> 64, of which waited for: 30 -> 32; matrix products, arithmetic and copies ran while one was open for 16% -> 6% of each run, Pallas kernels for 24% -> 25%
where the time goes in v15:
time: 277 us; the launch traced here: 275 us
  Pallas kernels  88.6 us (32%)
  starting transfers between devices  81.2 us (29%)
  waiting for transfers between devices  74.1 us (27%)
  other arithmetic  18.9 us (7%)
  local copies, waits for them, and re-layouts  9.94 us (4%)
    ppermute x63, starting transfers between devices, swap(): lax.ppermute(array, axis, [(i, i ^ distance) for i in range(lax.axis_size...  78.1 us
    ppermute x63, waiting for transfers between devices, swap(): lax.ppermute(array, axis, [(i, i ^ distance) for i in range(lax.axis_size...  69.7 us
    pallas_call x9, Pallas kernels, apply_tiles(): pl.pallas_call(functools.partial(apply_kernel, span, skip, counts, base i...  68 us
    pallas_call x2, Pallas kernels, split_tiles(): pl.pallas_call(split_kernel, out_shape=jax.ShapeDtypeStruct((CORES * leng...  20.6 us
    add x18, other arithmetic, reduce_near(): sum([halves(t)[1] for t in terms[1:]], halves(terms[0])[1])  9.03 us
    unnamed x104, local copies, waits for them, and re-layouts  6.16 us
  transfers between devices with their start and end apart: 64, of which 32 were waited for; matrix products, arithmetic and copies ran while one was open for 6% of the time, Pallas kernels for 25%

profile of v15, /device:TPU:0, one launch (start us, length us, event | category | flops | bytes accessed | tf_op | source)
XLA Modules:
  0.0 275.3 jit_solution(5736911461732356560)
XLA Ops:
  8.6 3.9 %collective-permute-start.4 = (f32[12,32,128]{2,1,0:T(8,128)S(1)}, f32[12,32,128]{2,1,0:T(8,128)S(1)}, u32[]{:S(2)}, u32[]{:S(2)}) collective-permute-start(f32[12,32,128]{2,1,0:T(8,128)S(1)} %get-tuple-element.272), channel_id=1, source_target_pairs={{0,16},{8,24},{16,0},{24,8},{1,17},{9,25},{17,1},{25,9},{2,18},{10... | collective-permute-start | bytes 589832 | tf_op jit(solution)/shard_map/ppermute | solution.py:39
  12.5 10.3 %shard_map.95.refs_0_ = bf16[256,256,128]{2,1,0:T(8,128)(2,1)} custom-call(f32[128,128,128]{2,1,0:T(8,128)} %tile_ref), custom_call_target="tpu_custom_call" | custom-call | flops 6291456 | bytes 16777216 | tf_op jit(solution)/shard_map/pallas_call | solution.py:125
  33.9 3.8 %collective-permute-done.6 = f32[16,32,128]{2,1,0:T(8,128)S(1)} collective-permute-done((f32[16,32,128]{2,1,0:T(8,128)S(1)}, f32[16,32,128]{2,1,0:T(8,128)S(1)}, u32[]{:S(2)}, u32[]{:S(2)}) %collective-permute-start.6) | collective-permute-done | bytes 262176 | tf_op jit(solution)/shard_map/ppermute | solution.py:39
  41.9 10.3 %shard_map.96.pairs_ref = bf16[256,256,128]{2,1,0:T(8,128)(2,1)} custom-call(f32[128,128,128]{2,1,0:T(8,128)} %collective-permute-done.2.tile_ref, bf16[256,256,128]{2,1,0:T(8,128)(2,1)} %shard_map.95.refs_0_), custom_call_target="tpu_custom_call", output_to_operand_aliasing={{}: (1, {})} | custom-call | flops 6291456 | bytes 16777216 | tf_op jit(solution)/shard_map/pallas_call | solution.py:125
  52.3 9.2 %shard_map.97 = (f32[96,32,128]{2,1,0:T(8,128)}, f32[96,32,128]{2,1,0:T(8,128)}) custom-call(s32[772]{0:T(1024)} %pad_add_fusion.places_ref, bf16[256,256,128]{2,1,0:T(8,128)(2,1)} %shard_map.96.pairs_ref, f32[32,32,128]{2,1,0:T(8,128)} %copy-done.16, f32[32,32,128]{2,1,0:T(8,128)} %copy-done.13, f32[32,32,128]{2,1,0:T(8,128)} %copy-done.17), custom_call_target="tpu_custom_call" | custom-call | flops 536870912 | bytes 14680064 | tf_op jit(solution)/shard_map/pallas_call | solution.py:225
  62.7 6.5 %shard_map.99 = (f32[32,32,128]{2,1,0:T(8,128)}, f32[32,32,128]{2,1,0:T(8,128)}, f32[32,32,128]{2,1,0:T(8,128)}) custom-call(s32[772]{0:T(1024)} %pad_add_fusion.places_ref, bf16[256,256,128]{2,1,0:T(8,128)(2,1)} %shard_map.96.pairs_ref, f32[32,32,128]{2,1,0:T(8,128)} %copy-done.2, f32[32,32,128]{2,1,0:T(8,128)} %copy-done.3, f32[32,32,128]{2,1,0:T(8,128)} %copy-done.4, ...), custom_call_target="tpu_custom_call" | custom-call | flops 268435456 | bytes 7340032 | tf_op jit(solution)/shard_map/pallas_call | solution.py:225
  72.9 6.9 %shard_map.98 = (f32[32,32,128]{2,1,0:T(8,128)}, f32[32,32,128]{2,1,0:T(8,128)}, f32[32,32,128]{2,1,0:T(8,128)}) custom-call(s32[772]{0:T(1024)} %pad_add_fusion.places_ref, bf16[256,256,128]{2,1,0:T(8,128)(2,1)} %shard_map.96.pairs_ref, f32[32,32,128]{2,1,0:T(8,128)} %copy-done.2, f32[32,32,128]{2,1,0:T(8,128)} %copy-done.3, f32[32,32,128]{2,1,0:T(8,128)} %copy-done.4, ...), custom_call_target="tpu_custom_call" | custom-call | flops 268435456 | bytes 7340032 | tf_op jit(solution)/shard_map/pallas_call | solution.py:225
  83.4 3.0 %collective-permute-start.18 = (f32[16,32,128]{2,1,0:T(8,128)S(1)}, f32[16,32,128]{2,1,0:T(8,128)S(1)}, u32[]{:S(2)}, u32[]{:S(2)}) collective-permute-start(f32[16,32,128]{2,1,0:T(8,128)S(1)} %slice_add_fusion.7), channel_id=1, source_target_pairs={{0,8},{8,0},{16,24},{24,16},{1,9},{9,1},{17,25},{25,17},{2,10},{10... | collective-permute-start | bytes 786440 | tf_op jit(solution)/shard_map/ppermute | solution.py:39
  93.8 2.8 %collective-permute-done.19 = f32[8,32,128]{2,1,0:T(8,128)S(1)} collective-permute-done((f32[8,32,128]{2,1,0:T(8,128)S(1)}, f32[8,32,128]{2,1,0:T(8,128)S(1)}, u32[]{:S(2)}, u32[]{:S(2)}) %collective-permute-start.19) | collective-permute-done | bytes 131104 | tf_op jit(solution)/shard_map/ppermute | solution.py:39
  98.3 2.1 collective-permute-start.23
  100.3 11.1 %collective-permute-done.23 = f32[24,32,128]{2,1,0:T(8,128)S(1)} collective-permute-done((f32[24,32,128]{2,1,0:T(8,128)S(1)}, f32[24,32,128]{2,1,0:T(8,128)S(1)}, u32[]{:S(2)}, u32[]{:S(2)}) %collective-permute-start.23) | collective-permute-done | bytes 393248 | tf_op jit(solution)/shard_map/ppermute | solution.py:39
  116.9 2.5 collective-permute-start.25
  121.5 2.4 collective-permute-done.25
  124.0 3.6 %collective-permute-start.26 = (f32[32,32,128]{2,1,0:T(8,128)S(1)}, f32[32,32,128]{2,1,0:T(8,128)S(1)}, u32[]{:S(2)}, u32[]{:S(2)}) collective-permute-start(f32[32,32,128]{2,1,0:T(8,128)S(1)} %constant_dynamic-update-slice_fusion.15.refs_0_), channel_id=1, source_target_pairs={{0,2},{2,0},{1,3},{3,1},{4,6},{6,4},{5,7},{7,5},{8,10},{10,8},{9,1... | collective-permute-start | bytes 1572872 | tf_op jit(solution)/shard_map/ppermute | solution.py:39
  127.6 2.5 collective-permute-start.29
  131.0 9.2 %shard_map.100 = (f32[96,32,128]{2,1,0:T(8,128)}, f32[96,32,128]{2,1,0:T(8,128)}) custom-call(s32[772]{0:T(1024)} %pad_add_fusion.places_ref, bf16[256,256,128]{2,1,0:T(8,128)(2,1)} %shard_map.96.pairs_ref, f32[32,32,128]{2,1,0:T(8,128)} %copy-done.11, f32[32,32,128]{2,1,0:T(8,128)} %copy-done.14, f32[32,32,128]{2,1,0:T(8,128)} %copy-done.18), custom_call_target="tpu_custom_call" | custom-call | flops 536870912 | bytes 14680064 | tf_op jit(solution)/shard_map/pallas_call | solution.py:225
  141.4 6.5 %shard_map.102 = (f32[32,32,128]{2,1,0:T(8,128)}, f32[32,32,128]{2,1,0:T(8,128)}, f32[32,32,128]{2,1,0:T(8,128)}) custom-call(s32[772]{0:T(1024)} %pad_add_fusion.places_ref, bf16[256,256,128]{2,1,0:T(8,128)(2,1)} %shard_map.96.pairs_ref, f32[32,32,128]{2,1,0:T(8,128)} %copy-done.6, f32[32,32,128]{2,1,0:T(8,128)} %copy-done.8, f32[32,32,128]{2,1,0:T(8,128)} %copy-done.10, ...), custom_call_target="tpu_custom_call" | custom-call | flops 268435456 | bytes 7340032 | tf_op jit(solution)/shard_map/pallas_call | solution.py:225
  148.7 2.2 collective-permute-start.36
  151.7 6.9 %shard_map.101 = (f32[32,32,128]{2,1,0:T(8,128)}, f32[32,32,128]{2,1,0:T(8,128)}, f32[32,32,128]{2,1,0:T(8,128)}) custom-call(s32[772]{0:T(1024)} %pad_add_fusion.places_ref, bf16[256,256,128]{2,1,0:T(8,128)(2,1)} %shard_map.96.pairs_ref, f32[32,32,128]{2,1,0:T(8,128)} %copy-done.6, f32[32,32,128]{2,1,0:T(8,128)} %copy-done.8, f32[32,32,128]{2,1,0:T(8,128)} %copy-done.10, ...), custom_call_target="tpu_custom_call" | custom-call | flops 268435456 | bytes 7340032 | tf_op jit(solution)/shard_map/pallas_call | solution.py:225
  167.6 2.2 collective-permute-start.35
  177.6 12.2 %collective-permute-done.42 = f32[24,32,128]{2,1,0:T(8,128)S(1)} collective-permute-done((f32[24,32,128]{2,1,0:T(8,128)S(1)}, f32[24,32,128]{2,1,0:T(8,128)S(1)}, u32[]{:S(2)}, u32[]{:S(2)}) %collective-permute-start.42) | collective-permute-done | bytes 393248 | tf_op jit(solution)/shard_map/ppermute | solution.py:39
  191.4 3.7 %collective-permute-done.43 = f32[8,32,128]{2,1,0:T(8,128)S(1)} collective-permute-done((f32[8,32,128]{2,1,0:T(8,128)S(1)}, f32[8,32,128]{2,1,0:T(8,128)S(1)}, u32[]{:S(2)}, u32[]{:S(2)}) %collective-permute-start.43) | collective-permute-done | bytes 131104 | tf_op jit(solution)/shard_map/ppermute | solution.py:39
  196.6 2.2 collective-permute-start.47
  199.8 4.6 %collective-permute-done.44 = f32[16,32,128]{2,1,0:T(8,128)S(1)} collective-permute-done((f32[16,32,128]{2,1,0:T(8,128)S(1)}, f32[16,32,128]{2,1,0:T(8,128)S(1)}, u32[]{:S(2)}, u32[]{:S(2)}) %collective-permute-start.44) | collective-permute-done | bytes 262176 | tf_op jit(solution)/shard_map/ppermute | solution.py:39
  206.5 9.2 %shard_map.103 = (f32[96,32,128]{2,1,0:T(8,128)}, f32[96,32,128]{2,1,0:T(8,128)}) custom-call(s32[772]{0:T(1024)} %pad_add_fusion.places_ref, bf16[256,256,128]{2,1,0:T(8,128)(2,1)} %shard_map.96.pairs_ref, f32[32,32,128]{2,1,0:T(8,128)} %copy-done.12, f32[32,32,128]{2,1,0:T(8,128)} %copy-done.15, f32[32,32,128]{2,1,0:T(8,128)} %copy-done.19), custom_call_target="tpu_custom_call" | custom-call | flops 536870912 | bytes 14680064 | tf_op jit(solution)/shard_map/pallas_call | solution.py:225
  216.8 6.7 %shard_map.105 = (f32[32,32,128]{2,1,0:T(8,128)}, f32[32,32,128]{2,1,0:T(8,128)}, f32[32,32,128]{2,1,0:T(8,128)}) custom-call(s32[772]{0:T(1024)} %pad_add_fusion.places_ref, bf16[256,256,128]{2,1,0:T(8,128)(2,1)} %shard_map.96.pairs_ref, f32[32,32,128]{2,1,0:T(8,128)} %copy-done.5, f32[32,32,128]{2,1,0:T(8,128)} %copy-done.7, f32[32,32,128]{2,1,0:T(8,128)} %copy-done.9, ...), custom_call_target="tpu_custom_call" | custom-call | flops 268435456 | bytes 7340032 | tf_op jit(solution)/shard_map/pallas_call | solution.py:225
  227.8 6.9 %shard_map.104 = (f32[32,32,128]{2,1,0:T(8,128)}, f32[32,32,128]{2,1,0:T(8,128)}, f32[32,32,128]{2,1,0:T(8,128)}) custom-call(s32[772]{0:T(1024)} %pad_add_fusion.places_ref, bf16[256,256,128]{2,1,0:T(8,128)(2,1)} %shard_map.96.pairs_ref, f32[32,32,128]{2,1,0:T(8,128)} %copy-done.5, f32[32,32,128]{2,1,0:T(8,128)} %copy-done.7, f32[32,32,128]{2,1,0:T(8,128)} %copy-done.9, ...), custom_call_target="tpu_custom_call" | custom-call | flops 268435456 | bytes 7340032 | tf_op jit(solution)/shard_map/pallas_call | solution.py:225
  251.6 2.3 collective-permute-done.54
  257.5 3.1 %all-to-all-start = ((f32[32,1,128]{2,1,0:T(1,128)}), f32[32,1,128]{2,1,0:T(1,128)S(1)}, u32[]{:S(2)}, u32[]{:S(2)}) async-start(f32[32,1,128]{2,1,0:T(1,128)} %broadcast_in_dim.60), calls=%async_computation | async-start | bytes 32768 | tf_op jit(solution)/shard_map/all_to_all | solution.py:348
  260.6 2.7 collective-permute-start.61
  263.3 4.4 %all-to-all-done = f32[32,1,128]{2,1,0:T(1,128)S(1)} async-done(((f32[32,1,128]{2,1,0:T(1,128)}), f32[32,1,128]{2,1,0:T(1,128)S(1)}, u32[]{:S(2)}, u32[]{:S(2)}) %all-to-all-start) | async-done | bytes 16416 | tf_op jit(solution)/shard_map/all_to_all | solution.py:348
  269.7 3.4 %collective-permute-done.61 = f32[12,32,128]{2,1,0:T(8,128)S(1)} collective-permute-done((f32[12,32,128]{2,1,0:T(8,128)S(1)}, f32[12,32,128]{2,1,0:T(8,128)S(1)}, u32[]{:S(2)}, u32[]{:S(2)}) %collective-permute-start.61) | collective-permute-done | bytes 196640 | tf_op jit(solution)/shard_map/ppermute | solution.py:39
  (337 shorter events, 103.5 us)
Async XLA Ops:
  6.1 35.8 %collective-permute-start.2 = (f32[128,128,128]{2,1,0:T(8,128)}, f32[128,128,128]{2,1,0:T(8,128)}, u32[]{:S(2)}, u32[]{:S(2)}) collective-permute-start(f32[128,128,128]{2,1,0:T(8,128)} %tile_ref), channel_id=1, source_target_pairs={{0,1},{1,0},{2,3},{3,2},{4,5},{5,4},{6,7},{7,6},{8,9},{9,8},{10,11... | collective-permute-start | bytes 25165832 | tf_op jit(solution)/shard_map/ppermute | solution.py:39
  8.6 14.9 %collective-permute-start.4 = (f32[12,32,128]{2,1,0:T(8,128)S(1)}, f32[12,32,128]{2,1,0:T(8,128)S(1)}, u32[]{:S(2)}, u32[]{:S(2)}) collective-permute-start(f32[12,32,128]{2,1,0:T(8,128)S(1)} %get-tuple-element.272), channel_id=1, source_target_pairs={{0,16},{8,24},{16,0},{24,8},{1,17},{9,25},{17,1},{25,9},{2,18},{10... | collective-permute-start | bytes 589832 | tf_op jit(solution)/shard_map/ppermute | solution.py:39
  12.5 10.4 %collective-permute-start.3 = (f32[12,2,128]{2,0,1:T(8,128)S(1)}, f32[12,2,128]{2,0,1:T(8,128)S(1)}, u32[]{:S(2)}, u32[]{:S(2)}) collective-permute-start(f32[12,2,128]{2,0,1:T(8,128)S(1)} %pad_maximum_fusion.22), channel_id=1, source_target_pairs={{0,16},{8,24},{16,0},{24,8},{1,17},{9,25},{17,1},{25,9},{2,18},{10... | collective-permute-start | bytes 36872 | tf_op jit(solution)/shard_map/ppermute | solution.py:39
  28.9 8.7 %collective-permute-start.6 = (f32[16,32,128]{2,1,0:T(8,128)S(1)}, f32[16,32,128]{2,1,0:T(8,128)S(1)}, u32[]{:S(2)}, u32[]{:S(2)}) collective-permute-start(f32[16,32,128]{2,1,0:T(8,128)S(1)} %pad_maximum_fusion), channel_id=1, source_target_pairs={{0,4},{4,0},{1,5},{5,1},{2,6},{6,2},{3,7},{7,3},{8,12},{12,8},{9,1... | collective-permute-start | bytes 786440 | tf_op jit(solution)/shard_map/ppermute | solution.py:39
  37.7 23.7 %collective-permute-start.7 = (f32[32,32,128]{2,1,0:T(8,128)S(1)}, f32[32,32,128]{2,1,0:T(8,128)S(1)}, u32[]{:S(2)}, u32[]{:S(2)}) collective-permute-start(f32[32,32,128]{2,1,0:T(8,128)S(1)} %constant_dynamic-update-slice_fusion.refs_0_), channel_id=1, source_target_pairs={{0,2},{2,0},{1,3},{3,1},{4,6},{6,4},{5,7},{7,5},{8,10},{10,8},{9,1... | collective-permute-start | bytes 1572872 | tf_op jit(solution)/shard_map/ppermute | solution.py:39
  38.3 23.1 %collective-permute-start.10 = (f32[32,32,128]{2,1,0:T(8,128)S(1)}, f32[32,32,128]{2,1,0:T(8,128)S(1)}, u32[]{:S(2)}, u32[]{:S(2)}) collective-permute-start(f32[32,32,128]{2,1,0:T(8,128)S(1)} %constant_dynamic-update-slice_fusion.3.refs_1_), channel_id=1, source_target_pairs={{0,4},{4,0},{1,5},{5,1},{2,6},{6,2},{3,7},{7,3},{8,12},{12,8},{9,1... | collective-permute-start | bytes 1572872 | tf_op jit(solution)/shard_map/ppermute | solution.py:39
  40.7 20.8 %collective-permute-start.13 = (f32[32,32,128]{2,1,0:T(8,128)S(1)}, f32[32,32,128]{2,1,0:T(8,128)S(1)}, u32[]{:S(2)}, u32[]{:S(2)}) collective-permute-start(f32[32,32,128]{2,1,0:T(8,128)S(1)} %constant_dynamic-update-slice_fusion.6.refs_2_), channel_id=1, source_target_pairs={{0,8},{8,0},{16,24},{24,16},{1,9},{9,1},{17,25},{25,17},{2,10},{10... | collective-permute-start | bytes 1572872 | tf_op jit(solution)/shard_map/ppermute | solution.py:39
  69.2 11.2 %collective-permute-start.14 = (f32[32,32,128]{2,1,0:T(8,128)}, f32[32,32,128]{2,1,0:T(8,128)S(1)}, u32[]{:S(2)}, u32[]{:S(2)}) collective-permute-start(f32[32,32,128]{2,1,0:T(8,128)} %get-tuple-element.112), channel_id=1, source_target_pairs={{0,2},{2,0},{1,3},{3,1},{4,6},{6,4},{5,7},{7,5},{8,10},{10,8},{9,1... | collective-permute-start | bytes 1572872 | tf_op jit(solution)/shard_map/ppermute | solution.py:39
  69.9 12.5 %collective-permute-start.17 = (f32[32,32,128]{2,1,0:T(8,128)}, f32[32,32,128]{2,1,0:T(8,128)S(1)}, u32[]{:S(2)}, u32[]{:S(2)}) collective-permute-start(f32[32,32,128]{2,1,0:T(8,128)} %get-tuple-element.121), channel_id=1, source_target_pairs={{0,4},{4,0},{1,5},{5,1},{2,6},{6,2},{3,7},{7,3},{8,12},{12,8},{9,1... | collective-permute-start | bytes 1572872 | tf_op jit(solution)/shard_map/ppermute | solution.py:39
  71.9 14.5 %collective-permute-start.20 = (f32[32,32,128]{2,1,0:T(8,128)}, f32[32,32,128]{2,1,0:T(8,128)S(1)}, u32[]{:S(2)}, u32[]{:S(2)}) collective-permute-start(f32[32,32,128]{2,1,0:T(8,128)} %get-tuple-element.130), channel_id=1, source_target_pairs={{0,8},{8,0},{16,24},{24,16},{1,9},{9,1},{17,25},{25,17},{2,10},{10... | collective-permute-start | bytes 1572872 | tf_op jit(solution)/shard_map/ppermute | solution.py:39
  83.4 8.0 %collective-permute-start.18 = (f32[16,32,128]{2,1,0:T(8,128)S(1)}, f32[16,32,128]{2,1,0:T(8,128)S(1)}, u32[]{:S(2)}, u32[]{:S(2)}) collective-permute-start(f32[16,32,128]{2,1,0:T(8,128)S(1)} %slice_add_fusion.7), channel_id=1, source_target_pairs={{0,8},{8,0},{16,24},{24,16},{1,9},{9,1},{17,25},{25,17},{2,10},{10... | collective-permute-start | bytes 786440 | tf_op jit(solution)/shard_map/ppermute | solution.py:39
  98.3 13.2 %collective-permute-start.23 = (f32[24,32,128]{2,1,0:T(8,128)S(1)}, f32[24,32,128]{2,1,0:T(8,128)S(1)}, u32[]{:S(2)}, u32[]{:S(2)}) collective-permute-start(f32[24,32,128]{2,1,0:T(8,128)S(1)} %get-tuple-element.222), channel_id=1, source_target_pairs={{0,16},{8,24},{16,0},{24,8},{1,17},{9,25},{17,1},{25,9},{2,18},{10... | collective-permute-start | bytes 1179656 | tf_op jit(solution)/shard_map/ppermute | solution.py:39
  119.4 8.2 %collective-permute-start.28 = (f32[16,32,128]{2,1,0:T(8,128)S(1)}, f32[16,32,128]{2,1,0:T(8,128)S(1)}, u32[]{:S(2)}, u32[]{:S(2)}) collective-permute-start(f32[16,32,128]{2,1,0:T(8,128)S(1)} %pad_maximum_fusion.4), channel_id=1, source_target_pairs={{0,8},{8,0},{16,24},{24,16},{1,9},{9,1},{17,25},{25,17},{2,10},{10... | collective-permute-start | bytes 786440 | tf_op jit(solution)/shard_map/ppermute | solution.py:39
  119.5 10.6 %collective-permute-start.31 = (f32[16,32,128]{2,1,0:T(8,128)S(1)}, f32[16,32,128]{2,1,0:T(8,128)S(1)}, u32[]{:S(2)}, u32[]{:S(2)}) collective-permute-start(f32[16,32,128]{2,1,0:T(8,128)S(1)} %pad_maximum_fusion.5), channel_id=1, source_target_pairs={{0,2},{2,0},{1,3},{3,1},{4,6},{6,4},{5,7},{7,5},{8,10},{10,8},{9,1... | collective-permute-start | bytes 786440 | tf_op jit(solution)/shard_map/ppermute | solution.py:39
  124.0 16.2 %collective-permute-start.26 = (f32[32,32,128]{2,1,0:T(8,128)S(1)}, f32[32,32,128]{2,1,0:T(8,128)S(1)}, u32[]{:S(2)}, u32[]{:S(2)}) collective-permute-start(f32[32,32,128]{2,1,0:T(8,128)S(1)} %constant_dynamic-update-slice_fusion.15.refs_0_), channel_id=1, source_target_pairs={{0,2},{2,0},{1,3},{3,1},{4,6},{6,4},{5,7},{7,5},{8,10},{10,8},{9,1... | collective-permute-start | bytes 1572872 | tf_op jit(solution)/shard_map/ppermute | solution.py:39
  127.6 12.6 %collective-permute-start.29 = (f32[32,32,128]{2,1,0:T(8,128)S(1)}, f32[32,32,128]{2,1,0:T(8,128)S(1)}, u32[]{:S(2)}, u32[]{:S(2)}) collective-permute-start(f32[32,32,128]{2,1,0:T(8,128)S(1)} %constant_dynamic-update-slice_fusion.18.refs_1_), channel_id=1, source_target_pairs={{0,4},{4,0},{1,5},{5,1},{2,6},{6,2},{3,7},{7,3},{8,12},{12,8},{9,1... | collective-permute-start | bytes 1572872 | tf_op jit(solution)/shard_map/ppermute | solution.py:39
  130.2 10.0 %collective-permute-start.32 = (f32[32,32,128]{2,1,0:T(8,128)S(1)}, f32[32,32,128]{2,1,0:T(8,128)S(1)}, u32[]{:S(2)}, u32[]{:S(2)}) collective-permute-start(f32[32,32,128]{2,1,0:T(8,128)S(1)} %constant_dynamic-update-slice_fusion.21.refs_2_), channel_id=1, source_target_pairs={{0,8},{8,0},{16,24},{24,16},{1,9},{9,1},{17,25},{25,17},{2,10},{10... | collective-permute-start | bytes 1572872 | tf_op jit(solution)/shard_map/ppermute | solution.py:39
  147.9 10.8 %collective-permute-start.33 = (f32[32,32,128]{2,1,0:T(8,128)}, f32[32,32,128]{2,1,0:T(8,128)S(1)}, u32[]{:S(2)}, u32[]{:S(2)}) collective-permute-start(f32[32,32,128]{2,1,0:T(8,128)} %get-tuple-element.144), channel_id=1, source_target_pairs={{0,2},{2,0},{1,3},{3,1},{4,6},{6,4},{5,7},{7,5},{8,10},{10,8},{9,1... | collective-permute-start | bytes 1572872 | tf_op jit(solution)/shard_map/ppermute | solution.py:39
  148.7 12.9 %collective-permute-start.36 = (f32[32,32,128]{2,1,0:T(8,128)}, f32[32,32,128]{2,1,0:T(8,128)S(1)}, u32[]{:S(2)}, u32[]{:S(2)}) collective-permute-start(f32[32,32,128]{2,1,0:T(8,128)} %get-tuple-element.153), channel_id=1, source_target_pairs={{0,4},{4,0},{1,5},{5,1},{2,6},{6,2},{3,7},{7,3},{8,12},{12,8},{9,1... | collective-permute-start | bytes 1572872 | tf_op jit(solution)/shard_map/ppermute | solution.py:39
  150.9 13.6 %collective-permute-start.39 = (f32[32,32,128]{2,1,0:T(8,128)}, f32[32,32,128]{2,1,0:T(8,128)S(1)}, u32[]{:S(2)}, u32[]{:S(2)}) collective-permute-start(f32[32,32,128]{2,1,0:T(8,128)} %get-tuple-element.162), channel_id=1, source_target_pairs={{0,8},{8,0},{16,24},{24,16},{1,9},{9,1},{17,25},{25,17},{2,10},{10... | collective-permute-start | bytes 1572872 | tf_op jit(solution)/shard_map/ppermute | solution.py:39
  159.7 7.8 %collective-permute-start.34 = (f32[16,32,128]{2,1,0:T(8,128)S(1)}, f32[16,32,128]{2,1,0:T(8,128)S(1)}, u32[]{:S(2)}, u32[]{:S(2)}) collective-permute-start(f32[16,32,128]{2,1,0:T(8,128)S(1)} %slice_add_fusion.5), channel_id=1, source_target_pairs={{0,4},{4,0},{1,5},{5,1},{2,6},{6,2},{3,7},{7,3},{8,12},{12,8},{9,1... | collective-permute-start | bytes 786440 | tf_op jit(solution)/shard_map/ppermute | solution.py:39
  176.7 13.1 %collective-permute-start.42 = (f32[24,32,128]{2,1,0:T(8,128)S(1)}, f32[24,32,128]{2,1,0:T(8,128)S(1)}, u32[]{:S(2)}, u32[]{:S(2)}) collective-permute-start(f32[24,32,128]{2,1,0:T(8,128)S(1)} %get-tuple-element.210), channel_id=1, source_target_pairs={{0,16},{8,24},{16,0},{24,8},{1,17},{9,25},{17,1},{25,9},{2,18},{10... | collective-permute-start | bytes 1179656 | tf_op jit(solution)/shard_map/ppermute | solution.py:39
  195.1 9.3 %collective-permute-start.44 = (f32[16,32,128]{2,1,0:T(8,128)S(1)}, f32[16,32,128]{2,1,0:T(8,128)S(1)}, u32[]{:S(2)}, u32[]{:S(2)}) collective-permute-start(f32[16,32,128]{2,1,0:T(8,128)S(1)} %pad_maximum_fusion.6), channel_id=1, source_target_pairs={{0,4},{4,0},{1,5},{5,1},{2,6},{6,2},{3,7},{7,3},{8,12},{12,8},{9,1... | collective-permute-start | bytes 786440 | tf_op jit(solution)/shard_map/ppermute | solution.py:39
  196.6 8.6 %collective-permute-start.47 = (f32[16,32,128]{2,1,0:T(8,128)S(1)}, f32[16,32,128]{2,1,0:T(8,128)S(1)}, u32[]{:S(2)}, u32[]{:S(2)}) collective-permute-start(f32[16,32,128]{2,1,0:T(8,128)S(1)} %pad_maximum_fusion.7), channel_id=1, source_target_pairs={{0,8},{8,0},{16,24},{24,16},{1,9},{9,1},{17,25},{25,17},{2,10},{10... | collective-permute-start | bytes 786440 | tf_op jit(solution)/shard_map/ppermute | solution.py:39
  204.4 11.2 %collective-permute-start.45 = (f32[32,32,128]{2,1,0:T(8,128)S(1)}, f32[32,32,128]{2,1,0:T(8,128)S(1)}, u32[]{:S(2)}, u32[]{:S(2)}) collective-permute-start(f32[32,32,128]{2,1,0:T(8,128)S(1)} %constant_dynamic-update-slice_fusion.30.refs_0_), channel_id=1, source_target_pairs={{0,2},{2,0},{1,3},{3,1},{4,6},{6,4},{5,7},{7,5},{8,10},{10,8},{9,1... | collective-permute-start | bytes 1572872 | tf_op jit(solution)/shard_map/ppermute | solution.py:39
  205.2 10.5 %collective-permute-start.48 = (f32[32,32,128]{2,1,0:T(8,128)S(1)}, f32[32,32,128]{2,1,0:T(8,128)S(1)}, u32[]{:S(2)}, u32[]{:S(2)}) collective-permute-start(f32[32,32,128]{2,1,0:T(8,128)S(1)} %constant_dynamic-update-slice_fusion.33.refs_1_), channel_id=1, source_target_pairs={{0,4},{4,0},{1,5},{5,1},{2,6},{6,2},{3,7},{7,3},{8,12},{12,8},{9,1... | collective-permute-start | bytes 1572872 | tf_op jit(solution)/shard_map/ppermute | solution.py:39
  205.7 10.0 %collective-permute-start.51 = (f32[32,32,128]{2,1,0:T(8,128)S(1)}, f32[32,32,128]{2,1,0:T(8,128)S(1)}, u32[]{:S(2)}, u32[]{:S(2)}) collective-permute-start(f32[32,32,128]{2,1,0:T(8,128)S(1)} %constant_dynamic-update-slice_fusion.36.refs_2_), channel_id=1, source_target_pairs={{0,8},{8,0},{16,24},{24,16},{1,9},{9,1},{17,25},{25,17},{2,10},{10... | collective-permute-start | bytes 1572872 | tf_op jit(solution)/shard_map/ppermute | solution.py:39
  223.6 11.4 %collective-permute-start.58 = (f32[32,32,128]{2,1,0:T(8,128)}, f32[32,32,128]{2,1,0:T(8,128)S(1)}, u32[]{:S(2)}, u32[]{:S(2)}) collective-permute-start(f32[32,32,128]{2,1,0:T(8,128)} %get-tuple-element.194), channel_id=1, source_target_pairs={{0,8},{8,0},{16,24},{24,16},{1,9},{9,1},{17,25},{25,17},{2,10},{10... | collective-permute-start | bytes 1572872 | tf_op jit(solution)/shard_map/ppermute | solution.py:39
  225.0 12.9 %collective-permute-start.55 = (f32[32,32,128]{2,1,0:T(8,128)}, f32[32,32,128]{2,1,0:T(8,128)S(1)}, u32[]{:S(2)}, u32[]{:S(2)}) collective-permute-start(f32[32,32,128]{2,1,0:T(8,128)} %get-tuple-element.185), channel_id=1, source_target_pairs={{0,4},{4,0},{1,5},{5,1},{2,6},{6,2},{3,7},{7,3},{8,12},{12,8},{9,1... | collective-permute-start | bytes 1572872 | tf_op jit(solution)/shard_map/ppermute | solution.py:39
  226.3 14.5 %collective-permute-start.52 = (f32[32,32,128]{2,1,0:T(8,128)}, f32[32,32,128]{2,1,0:T(8,128)S(1)}, u32[]{:S(2)}, u32[]{:S(2)}) collective-permute-start(f32[32,32,128]{2,1,0:T(8,128)} %get-tuple-element.176), channel_id=1, source_target_pairs={{0,2},{2,0},{1,3},{3,1},{4,6},{6,4},{5,7},{7,5},{8,10},{10,8},{9,1... | collective-permute-start | bytes 1572872 | tf_op jit(solution)/shard_map/ppermute | solution.py:39
  257.5 10.2 %all-to-all-start = ((f32[32,1,128]{2,1,0:T(1,128)}), f32[32,1,128]{2,1,0:T(1,128)S(1)}, u32[]{:S(2)}, u32[]{:S(2)}) async-start(f32[32,1,128]{2,1,0:T(1,128)} %broadcast_in_dim.60), calls=%async_computation | async-start | bytes 32768 | tf_op jit(solution)/shard_map/all_to_all | solution.py:348
  260.6 12.5 %collective-permute-start.61 = (f32[12,32,128]{2,1,0:T(8,128)S(1)}, f32[12,32,128]{2,1,0:T(8,128)S(1)}, u32[]{:S(2)}, u32[]{:S(2)}) collective-permute-start(f32[12,32,128]{2,1,0:T(8,128)S(1)} %get-tuple-element.203), channel_id=1, source_target_pairs={{0,16},{8,24},{16,0},{24,8},{1,17},{9,25},{17,1},{25,9},{2,18},{10... | collective-permute-start | bytes 589832 | tf_op jit(solution)/shard_map/ppermute | solution.py:39
  (77 other events, 445.0 us)

commit v16 on v15

--- a/solution.py
+++ b/solution.py
@@ -137,10 +137,10 @@
     )(tiles, *given)
 
 
-def apply_kernel(span, skip, counts, has_base, places_ref, pairs_ref, *refs):
-    ends, refs = refs[: len(counts)], refs[len(counts) :]
+def apply_kernel(span, skip, pieces, has_base, places_ref, pairs_ref, *refs):
+    flux, refs = refs[:pieces], refs[pieces:]
     base_ref, refs = (refs[0], refs[1:]) if has_base else (None, refs)
-    *outs, flux_ref, sum_ref, held_ref, sem, held_sem = refs
+    *outs, flux_ref, sum_ref, held_ref, held_sem = refs
     total = pairs_ref.shape[0]
     start, stop = places_ref[span], places_ref[span + 1]
     chunks = (stop - start + CHUNK - 1) // CHUNK
@@ -153,26 +153,20 @@
                 pairs_ref.at[places_ref[SPANS + at]], held_ref.at[slot, k], held_sem.at[slot]
             ).start()
 
-    copies = [
-        pltpu.make_async_copy(
-            piece, flux_ref.at[pl.ds(sum(counts[:k]), counts[k])], sem.at[k]
-        )
-        for k, piece in enumerate(ends)
-    ]
-    if has_base:
-        copies.append(pltpu.make_async_copy(base_ref, sum_ref, sem.at[len(counts)]))
-    for copy in copies:
-        copy.start()
     for chunk in range(SLOTS - 1):
 
         @pl.when(chunk < chunks)
         def _():
             fetch(jnp.int32(chunk))
 
-    if not has_base:
+    done = 0
+    for piece in flux:
+        flux_ref[done : done + piece.shape[0]] = piece[...]
+        done += piece.shape[0]
+    if has_base:
+        sum_ref[...] = base_ref[...]
+    else:
         sum_ref[...] = jnp.zeros_like(sum_ref)
-    for copy in copies:
-        copy.wait()
 
     @pl.loop(0, chunks)
     def _(chunk):
@@ -190,61 +184,55 @@
             at = start + chunk * CHUNK + k
             valid = jnp.where(at < stop, 1.0, 0.0)
             at = jnp.minimum(at, stop - 1)
-            flux = flux_ref[places_ref[SPANS + 2 * total + at]] * valid
-            high = flux.astype(jnp.bfloat16)
-            low = (flux - high.astype(jnp.float32)).astype(jnp.bfloat16)
+            values = flux_ref[places_ref[SPANS + 2 * total + at]] * valid
+            high = values.astype(jnp.bfloat16)
+            low = (values - high.astype(jnp.float32)).astype(jnp.bfloat16)
             left = jnp.concatenate([high, low], axis=0)
             both = jnp.dot(
                 jnp.concatenate([left, left], axis=1),
                 held_ref[slot, k],
                 preferred_element_type=jnp.float32,
             )
-            temps = flux.shape[0]
+            temps = values.shape[0]
             products.append(both[:temps] + both[temps:])
             rows.append(places_ref[SPANS + total + at] - skip)
         for row, product in zip(rows, products):
             sum_ref[row] += product
 
-    sizes = [out.shape[0] for out in outs]
-    copies = [
-        pltpu.make_async_copy(sum_ref.at[pl.ds(sum(sizes[:k]), sizes[k])], out, sem.at[k])
-        for k, out in enumerate(outs)
-    ]
-    for copy in copies:
-        copy.start()
-    for copy in copies:
-        copy.wait()
+    done = 0
+    for out in outs:
+        out[...] = sum_ref[done : done + out.shape[0]]
+        done += out.shape[0]
 
 
 def apply_tiles(span, skip, places, pairs, flux, sizes, share, base=None):
     total, _, size = pairs.shape
-    counts = [piece.shape[0] for piece in flux]
     temps = flux[0].shape[1]
-    anywhere = pl.BlockSpec(memory_space=pltpu.HBM)
-    given = [pairs, *flux] + ([] if base is None else [base])
+    rows = sum(sizes)
+    inside = pl.BlockSpec(memory_space=pltpu.VMEM)
+    given = [*flux] + ([] if base is None else [base])
     return pl.pallas_call(
-        functools.partial(apply_kernel, span, skip, counts, base is not None),
+        functools.partial(apply_kernel, span, skip, len(flux), base is not None),
         out_shape=[jax.ShapeDtypeStruct((n, temps, size), jnp.float32) for n in sizes],
         grid_spec=pltpu.PrefetchScalarGridSpec(
             num_scalar_prefetch=1,
             grid=(),
-            in_specs=[anywhere] * len(given),
-            out_specs=[anywhere] * len(sizes),
+            in_specs=[pl.BlockSpec(memory_space=pltpu.HBM)] + [inside] * len(given),
+            out_specs=[inside] * len(sizes),
             scratch_shapes=[
-                pltpu.VMEM((sum(counts), temps, size), jnp.float32),
-                pltpu.VMEM((sum(sizes), temps, size), jnp.float32),
+                pltpu.VMEM((sum(piece.shape[0] for piece in flux), temps, size), jnp.float32),
+                pltpu.VMEM((rows, temps, size), jnp.float32),
                 pltpu.VMEM((SLOTS, CHUNK) + pairs.shape[1:], jnp.bfloat16),
-                pltpu.SemaphoreType.DMA((len(counts) + 1,)),
                 pltpu.SemaphoreType.DMA((SLOTS,)),
             ],
         ),
         compiler_params=pltpu.CompilerParams(vmem_limit_bytes=VMEM),
         cost_estimate=pl.CostEstimate(
             flops=int(share * total * size * size * temps * 8),
-            bytes_accessed=int(share * total * size * size * 4) + 8 * sum(sizes) * temps * size,
+            bytes_accessed=int(share * total * size * size * 4) + 8 * rows * temps * size,
             transcendentals=0,
         ),
-    )(places, *given)
+    )(places, pairs, *given)
 
 
 def shards(

time: 277 us -> 276 us (level)
  transfers between devices with their start and end apart: 64 -> 64, of which waited for: 32 -> 31; matrix products, arithmetic and copies ran while one was open for 6% -> 6% of each run, Pallas kernels for 25% -> 25%
where the time goes in v16:
time: 276 us; the launch traced here: 275 us
  Pallas kernels  89.2 us (32%)
  starting transfers between devices  81.3 us (29%)
  waiting for transfers between devices  73.8 us (27%)
  other arithmetic  18.8 us (7%)
  local copies, waits for them, and re-layouts  9.08 us (3%)
    ppermute x63, starting transfers between devices, swap(): lax.ppermute(array, axis, [(i, i ^ distance) for i in range(lax.axis_size...  77.7 us
    ppermute x63, waiting for transfers between devices, swap(): lax.ppermute(array, axis, [(i, i ^ distance) for i in range(lax.axis_size...  69.4 us
    pallas_call x9, Pallas kernels, apply_tiles(): pl.pallas_call(functools.partial(apply_kernel, span, skip, len(flux), bas...  68.6 us
    pallas_call x2, Pallas kernels, split_tiles(): pl.pallas_call(split_kernel, out_shape=jax.ShapeDtypeStruct((CORES * leng...  20.6 us
    add x18, other arithmetic, reduce_near(): sum([halves(t)[1] for t in terms[1:]], halves(terms[0])[1])  8.98 us
  transfers between devices with their start and end apart: 64, of which 31 were waited for; matrix products, arithmetic and copies ran while one was open for 6% of the time, Pallas kernels for 25%

profile of v16, /device:TPU:0, one launch (start us, length us, event | category | flops | bytes accessed | tf_op | source)
XLA Modules:
  0.0 274.8 jit_solution(12499615022285961066)
XLA Ops:
  8.6 3.9 %collective-permute-start.4 = (f32[12,32,128]{2,1,0:T(8,128)S(1)}, f32[12,32,128]{2,1,0:T(8,128)S(1)}, u32[]{:S(2)}, u32[]{:S(2)}) collective-permute-start(f32[12,32,128]{2,1,0:T(8,128)S(1)} %get-tuple-element.272), channel_id=1, source_target_pairs={{0,16},{8,24},{16,0},{24,8},{1,17},{9,25},{17,1},{25,9},{2,18},{10... | collective-permute-start | bytes 589832 | tf_op jit(solution)/shard_map/ppermute | solution.py:39
  12.5 10.3 %shard_map.95.refs_0_ = bf16[256,256,128]{2,1,0:T(8,128)(2,1)} custom-call(f32[128,128,128]{2,1,0:T(8,128)} %tile_ref), custom_call_target="tpu_custom_call" | custom-call | flops 6291456 | bytes 16777216 | tf_op jit(solution)/shard_map/pallas_call | solution.py:125
  33.9 3.8 %collective-permute-done.6 = f32[16,32,128]{2,1,0:T(8,128)S(1)} collective-permute-done((f32[16,32,128]{2,1,0:T(8,128)S(1)}, f32[16,32,128]{2,1,0:T(8,128)S(1)}, u32[]{:S(2)}, u32[]{:S(2)}) %collective-permute-start.6) | collective-permute-done | bytes 262176 | tf_op jit(solution)/shard_map/ppermute | solution.py:39
  41.9 10.3 %shard_map.96.pairs_ref = bf16[256,256,128]{2,1,0:T(8,128)(2,1)} custom-call(f32[128,128,128]{2,1,0:T(8,128)} %collective-permute-done.2.tile_ref, bf16[256,256,128]{2,1,0:T(8,128)(2,1)} %shard_map.95.refs_0_), custom_call_target="tpu_custom_call", output_to_operand_aliasing={{}: (1, {})} | custom-call | flops 6291456 | bytes 16777216 | tf_op jit(solution)/shard_map/pallas_call | solution.py:125
  52.3 8.6 %shard_map.97 = (f32[96,32,128]{2,1,0:T(8,128)}, f32[96,32,128]{2,1,0:T(8,128)}) custom-call(s32[772]{0:T(1024)} %pad_add_fusion.places_ref, bf16[256,256,128]{2,1,0:T(8,128)(2,1)} %shard_map.96.pairs_ref, f32[32,32,128]{2,1,0:T(8,128)} %copy-done.16, f32[32,32,128]{2,1,0:T(8,128)} %copy-done.13, f32[32,32,128]{2,1,0:T(8,128)} %copy-done.17), custom_call_target="tpu_custom_call" | custom-call | flops 536870912 | bytes 14680064 | tf_op jit(solution)/shard_map/pallas_call | solution.py:214
  62.1 6.7 %shard_map.99 = (f32[32,32,128]{2,1,0:T(8,128)}, f32[32,32,128]{2,1,0:T(8,128)}, f32[32,32,128]{2,1,0:T(8,128)}) custom-call(s32[772]{0:T(1024)} %pad_add_fusion.places_ref, bf16[256,256,128]{2,1,0:T(8,128)(2,1)} %shard_map.96.pairs_ref, f32[32,32,128]{2,1,0:T(8,128)} %copy-done.2, f32[32,32,128]{2,1,0:T(8,128)} %copy-done.3, f32[32,32,128]{2,1,0:T(8,128)} %copy-done.4, ...), custom_call_target="tpu_custom_call" | custom-call | flops 268435456 | bytes 7340032 | tf_op jit(solution)/shard_map/pallas_call | solution.py:214
  71.4 2.7 collective-permute-start.20
  74.1 7.5 %shard_map.98 = (f32[32,32,128]{2,1,0:T(8,128)}, f32[32,32,128]{2,1,0:T(8,128)}, f32[32,32,128]{2,1,0:T(8,128)}) custom-call(s32[772]{0:T(1024)} %pad_add_fusion.places_ref, bf16[256,256,128]{2,1,0:T(8,128)(2,1)} %shard_map.96.pairs_ref, f32[32,32,128]{2,1,0:T(8,128)} %copy-done.2, f32[32,32,128]{2,1,0:T(8,128)} %copy-done.3, f32[32,32,128]{2,1,0:T(8,128)} %copy-done.4, ...), custom_call_target="tpu_custom_call" | custom-call | flops 268435456 | bytes 7340032 | tf_op jit(solution)/shard_map/pallas_call | solution.py:214
  86.6 3.0 %collective-permute-done.15 = f32[16,32,128]{2,1,0:T(8,128)S(1)} collective-permute-done((f32[16,32,128]{2,1,0:T(8,128)S(1)}, f32[16,32,128]{2,1,0:T(8,128)S(1)}, u32[]{:S(2)}, u32[]{:S(2)}) %collective-permute-start.15) | collective-permute-done | bytes 262176 | tf_op jit(solution)/shard_map/ppermute | solution.py:39
  99.7 11.8 %collective-permute-done.23 = f32[24,32,128]{2,1,0:T(8,128)S(1)} collective-permute-done((f32[24,32,128]{2,1,0:T(8,128)S(1)}, f32[24,32,128]{2,1,0:T(8,128)S(1)}, u32[]{:S(2)}, u32[]{:S(2)}) %collective-permute-start.23) | collective-permute-done | bytes 393248 | tf_op jit(solution)/shard_map/ppermute | solution.py:39
  114.7 2.5 collective-permute-done.24
  121.0 3.0 %collective-permute-done.25 = f32[16,32,128]{2,1,0:T(8,128)S(1)} collective-permute-done((f32[16,32,128]{2,1,0:T(8,128)S(1)}, f32[16,32,128]{2,1,0:T(8,128)S(1)}, u32[]{:S(2)}, u32[]{:S(2)}) %collective-permute-start.25) | collective-permute-done | bytes 262176 | tf_op jit(solution)/shard_map/ppermute | solution.py:39
  124.0 2.8 %collective-permute-start.26 = (f32[32,32,128]{2,1,0:T(8,128)S(1)}, f32[32,32,128]{2,1,0:T(8,128)S(1)}, u32[]{:S(2)}, u32[]{:S(2)}) collective-permute-start(f32[32,32,128]{2,1,0:T(8,128)S(1)} %constant_dynamic-update-slice_fusion.15.refs_0_), channel_id=1, source_target_pairs={{0,2},{2,0},{1,3},{3,1},{4,6},{6,4},{5,7},{7,5},{8,10},{10,8},{9,1... | collective-permute-start | bytes 1572872 | tf_op jit(solution)/shard_map/ppermute | solution.py:39
  126.9 2.5 collective-permute-start.29
  130.3 8.6 %shard_map.100 = (f32[96,32,128]{2,1,0:T(8,128)}, f32[96,32,128]{2,1,0:T(8,128)}) custom-call(s32[772]{0:T(1024)} %pad_add_fusion.places_ref, bf16[256,256,128]{2,1,0:T(8,128)(2,1)} %shard_map.96.pairs_ref, f32[32,32,128]{2,1,0:T(8,128)} %copy-done.11, f32[32,32,128]{2,1,0:T(8,128)} %copy-done.14, f32[32,32,128]{2,1,0:T(8,128)} %copy-done.18), custom_call_target="tpu_custom_call" | custom-call | flops 536870912 | bytes 14680064 | tf_op jit(solution)/shard_map/pallas_call | solution.py:214
  140.1 6.7 %shard_map.102 = (f32[32,32,128]{2,1,0:T(8,128)}, f32[32,32,128]{2,1,0:T(8,128)}, f32[32,32,128]{2,1,0:T(8,128)}) custom-call(s32[772]{0:T(1024)} %pad_add_fusion.places_ref, bf16[256,256,128]{2,1,0:T(8,128)(2,1)} %shard_map.96.pairs_ref, f32[32,32,128]{2,1,0:T(8,128)} %copy-done.6, f32[32,32,128]{2,1,0:T(8,128)} %copy-done.8, f32[32,32,128]{2,1,0:T(8,128)} %copy-done.10, ...), custom_call_target="tpu_custom_call" | custom-call | flops 268435456 | bytes 7340032 | tf_op jit(solution)/shard_map/pallas_call | solution.py:214
  146.8 2.3 collective-permute-start.33
  151.6 7.5 %shard_map.101 = (f32[32,32,128]{2,1,0:T(8,128)}, f32[32,32,128]{2,1,0:T(8,128)}, f32[32,32,128]{2,1,0:T(8,128)}) custom-call(s32[772]{0:T(1024)} %pad_add_fusion.places_ref, bf16[256,256,128]{2,1,0:T(8,128)(2,1)} %shard_map.96.pairs_ref, f32[32,32,128]{2,1,0:T(8,128)} %copy-done.6, f32[32,32,128]{2,1,0:T(8,128)} %copy-done.8, f32[32,32,128]{2,1,0:T(8,128)} %copy-done.10, ...), custom_call_target="tpu_custom_call" | custom-call | flops 268435456 | bytes 7340032 | tf_op jit(solution)/shard_map/pallas_call | solution.py:214
  163.1 2.2 collective-permute-start.40
  165.2 2.7 collective-permute-done.34
  175.4 2.5 collective-permute-start.42
  177.9 10.5 %collective-permute-done.42 = f32[24,32,128]{2,1,0:T(8,128)S(1)} collective-permute-done((f32[24,32,128]{2,1,0:T(8,128)S(1)}, f32[24,32,128]{2,1,0:T(8,128)S(1)}, u32[]{:S(2)}, u32[]{:S(2)}) %collective-permute-start.42) | collective-permute-done | bytes 393248 | tf_op jit(solution)/shard_map/ppermute | solution.py:39
  191.2 2.5 collective-permute-done.43
  198.8 4.2 %collective-permute-done.44 = f32[16,32,128]{2,1,0:T(8,128)S(1)} collective-permute-done((f32[16,32,128]{2,1,0:T(8,128)S(1)}, f32[16,32,128]{2,1,0:T(8,128)S(1)}, u32[]{:S(2)}, u32[]{:S(2)}) %collective-permute-start.44) | collective-permute-done | bytes 262176 | tf_op jit(solution)/shard_map/ppermute | solution.py:39
  206.5 8.6 %shard_map.103 = (f32[96,32,128]{2,1,0:T(8,128)}, f32[96,32,128]{2,1,0:T(8,128)}) custom-call(s32[772]{0:T(1024)} %pad_add_fusion.places_ref, bf16[256,256,128]{2,1,0:T(8,128)(2,1)} %shard_map.96.pairs_ref, f32[32,32,128]{2,1,0:T(8,128)} %copy-done.12, f32[32,32,128]{2,1,0:T(8,128)} %copy-done.15, f32[32,32,128]{2,1,0:T(8,128)} %copy-done.19), custom_call_target="tpu_custom_call" | custom-call | flops 536870912 | bytes 14680064 | tf_op jit(solution)/shard_map/pallas_call | solution.py:214
  216.3 6.8 %shard_map.105 = (f32[32,32,128]{2,1,0:T(8,128)}, f32[32,32,128]{2,1,0:T(8,128)}, f32[32,32,128]{2,1,0:T(8,128)}) custom-call(s32[772]{0:T(1024)} %pad_add_fusion.places_ref, bf16[256,256,128]{2,1,0:T(8,128)(2,1)} %shard_map.96.pairs_ref, f32[32,32,128]{2,1,0:T(8,128)} %copy-done.5, f32[32,32,128]{2,1,0:T(8,128)} %copy-done.7, f32[32,32,128]{2,1,0:T(8,128)} %copy-done.9, ...), custom_call_target="tpu_custom_call" | custom-call | flops 268435456 | bytes 7340032 | tf_op jit(solution)/shard_map/pallas_call | solution.py:214
  224.2 2.4 collective-permute-start.55
  226.7 7.5 %shard_map.104 = (f32[32,32,128]{2,1,0:T(8,128)}, f32[32,32,128]{2,1,0:T(8,128)}, f32[32,32,128]{2,1,0:T(8,128)}) custom-call(s32[772]{0:T(1024)} %pad_add_fusion.places_ref, bf16[256,256,128]{2,1,0:T(8,128)(2,1)} %shard_map.96.pairs_ref, f32[32,32,128]{2,1,0:T(8,128)} %copy-done.5, f32[32,32,128]{2,1,0:T(8,128)} %copy-done.7, f32[32,32,128]{2,1,0:T(8,128)} %copy-done.9, ...), custom_call_target="tpu_custom_call" | custom-call | flops 268435456 | bytes 7340032 | tf_op jit(solution)/shard_map/pallas_call | solution.py:214
  256.5 3.5 %all-to-all-start = ((f32[32,1,128]{2,1,0:T(1,128)}), f32[32,1,128]{2,1,0:T(1,128)S(1)}, u32[]{:S(2)}, u32[]{:S(2)}) async-start(f32[32,1,128]{2,1,0:T(1,128)} %broadcast_in_dim.60), calls=%async_computation | async-start | bytes 32768 | tf_op jit(solution)/shard_map/all_to_all | solution.py:336
  260.1 2.7 collective-permute-start.61
  262.8 4.4 %all-to-all-done = f32[32,1,128]{2,1,0:T(1,128)S(1)} async-done(((f32[32,1,128]{2,1,0:T(1,128)}), f32[32,1,128]{2,1,0:T(1,128)S(1)}, u32[]{:S(2)}, u32[]{:S(2)}) %all-to-all-start) | async-done | bytes 16416 | tf_op jit(solution)/shard_map/all_to_all | solution.py:336
  269.2 3.4 %collective-permute-done.61 = f32[12,32,128]{2,1,0:T(8,128)S(1)} collective-permute-done((f32[12,32,128]{2,1,0:T(8,128)S(1)}, f32[12,32,128]{2,1,0:T(8,128)S(1)}, u32[]{:S(2)}, u32[]{:S(2)}) %collective-permute-start.61) | collective-permute-done | bytes 196640 | tf_op jit(solution)/shard_map/ppermute | solution.py:39
  (337 shorter events, 103.7 us)
Async XLA Ops:
  6.1 35.8 %collective-permute-start.2 = (f32[128,128,128]{2,1,0:T(8,128)}, f32[128,128,128]{2,1,0:T(8,128)}, u32[]{:S(2)}, u32[]{:S(2)}) collective-permute-start(f32[128,128,128]{2,1,0:T(8,128)} %tile_ref), channel_id=1, source_target_pairs={{0,1},{1,0},{2,3},{3,2},{4,5},{5,4},{6,7},{7,6},{8,9},{9,8},{10,11... | collective-permute-start | bytes 25165832 | tf_op jit(solution)/shard_map/ppermute | solution.py:39
  8.6 14.9 %collective-permute-start.4 = (f32[12,32,128]{2,1,0:T(8,128)S(1)}, f32[12,32,128]{2,1,0:T(8,128)S(1)}, u32[]{:S(2)}, u32[]{:S(2)}) collective-permute-start(f32[12,32,128]{2,1,0:T(8,128)S(1)} %get-tuple-element.272), channel_id=1, source_target_pairs={{0,16},{8,24},{16,0},{24,8},{1,17},{9,25},{17,1},{25,9},{2,18},{10... | collective-permute-start | bytes 589832 | tf_op jit(solution)/shard_map/ppermute | solution.py:39
  12.5 10.4 %collective-permute-start.3 = (f32[12,2,128]{2,0,1:T(8,128)S(1)}, f32[12,2,128]{2,0,1:T(8,128)S(1)}, u32[]{:S(2)}, u32[]{:S(2)}) collective-permute-start(f32[12,2,128]{2,0,1:T(8,128)S(1)} %pad_maximum_fusion.22), channel_id=1, source_target_pairs={{0,16},{8,24},{16,0},{24,8},{1,17},{9,25},{17,1},{25,9},{2,18},{10... | collective-permute-start | bytes 36872 | tf_op jit(solution)/shard_map/ppermute | solution.py:39
  28.9 8.7 %collective-permute-start.6 = (f32[16,32,128]{2,1,0:T(8,128)S(1)}, f32[16,32,128]{2,1,0:T(8,128)S(1)}, u32[]{:S(2)}, u32[]{:S(2)}) collective-permute-start(f32[16,32,128]{2,1,0:T(8,128)S(1)} %pad_maximum_fusion), channel_id=1, source_target_pairs={{0,4},{4,0},{1,5},{5,1},{2,6},{6,2},{3,7},{7,3},{8,12},{12,8},{9,1... | collective-permute-start | bytes 786440 | tf_op jit(solution)/shard_map/ppermute | solution.py:39
  30.6 7.7 %collective-permute-start.9 = (f32[16,32,128]{2,1,0:T(8,128)S(1)}, f32[16,32,128]{2,1,0:T(8,128)S(1)}, u32[]{:S(2)}, u32[]{:S(2)}) collective-permute-start(f32[16,32,128]{2,1,0:T(8,128)S(1)} %pad_maximum_fusion.1), channel_id=1, source_target_pairs={{0,8},{8,0},{16,24},{24,16},{1,9},{9,1},{17,25},{25,17},{2,10},{10... | collective-permute-start | bytes 786440 | tf_op jit(solution)/shard_map/ppermute | solution.py:39
  37.7 23.1 %collective-permute-start.7 = (f32[32,32,128]{2,1,0:T(8,128)S(1)}, f32[32,32,128]{2,1,0:T(8,128)S(1)}, u32[]{:S(2)}, u32[]{:S(2)}) collective-permute-start(f32[32,32,128]{2,1,0:T(8,128)S(1)} %constant_dynamic-update-slice_fusion.refs_0_), channel_id=1, source_target_pairs={{0,2},{2,0},{1,3},{3,1},{4,6},{6,4},{5,7},{7,5},{8,10},{10,8},{9,1... | collective-permute-start | bytes 1572872 | tf_op jit(solution)/shard_map/ppermute | solution.py:39
  38.3 22.5 %collective-permute-start.10 = (f32[32,32,128]{2,1,0:T(8,128)S(1)}, f32[32,32,128]{2,1,0:T(8,128)S(1)}, u32[]{:S(2)}, u32[]{:S(2)}) collective-permute-start(f32[32,32,128]{2,1,0:T(8,128)S(1)} %constant_dynamic-update-slice_fusion.3.refs_1_), channel_id=1, source_target_pairs={{0,4},{4,0},{1,5},{5,1},{2,6},{6,2},{3,7},{7,3},{8,12},{12,8},{9,1... | collective-permute-start | bytes 1572872 | tf_op jit(solution)/shard_map/ppermute | solution.py:39
  40.7 20.2 %collective-permute-start.13 = (f32[32,32,128]{2,1,0:T(8,128)S(1)}, f32[32,32,128]{2,1,0:T(8,128)S(1)}, u32[]{:S(2)}, u32[]{:S(2)}) collective-permute-start(f32[32,32,128]{2,1,0:T(8,128)S(1)} %constant_dynamic-update-slice_fusion.6.refs_2_), channel_id=1, source_target_pairs={{0,8},{8,0},{16,24},{24,16},{1,9},{9,1},{17,25},{25,17},{2,10},{10... | collective-permute-start | bytes 1572872 | tf_op jit(solution)/shard_map/ppermute | solution.py:39
  68.8 12.9 %collective-permute-start.14 = (f32[32,32,128]{2,1,0:T(8,128)}, f32[32,32,128]{2,1,0:T(8,128)S(1)}, u32[]{:S(2)}, u32[]{:S(2)}) collective-permute-start(f32[32,32,128]{2,1,0:T(8,128)} %get-tuple-element.112), channel_id=1, source_target_pairs={{0,2},{2,0},{1,3},{3,1},{4,6},{6,4},{5,7},{7,5},{8,10},{10,8},{9,1... | collective-permute-start | bytes 1572872 | tf_op jit(solution)/shard_map/ppermute | solution.py:39
  70.4 12.5 %collective-permute-start.17 = (f32[32,32,128]{2,1,0:T(8,128)}, f32[32,32,128]{2,1,0:T(8,128)S(1)}, u32[]{:S(2)}, u32[]{:S(2)}) collective-permute-start(f32[32,32,128]{2,1,0:T(8,128)} %get-tuple-element.121), channel_id=1, source_target_pairs={{0,4},{4,0},{1,5},{5,1},{2,6},{6,2},{3,7},{7,3},{8,12},{12,8},{9,1... | collective-permute-start | bytes 1572872 | tf_op jit(solution)/shard_map/ppermute | solution.py:39
  71.4 14.3 %collective-permute-start.20 = (f32[32,32,128]{2,1,0:T(8,128)}, f32[32,32,128]{2,1,0:T(8,128)S(1)}, u32[]{:S(2)}, u32[]{:S(2)}) collective-permute-start(f32[32,32,128]{2,1,0:T(8,128)} %get-tuple-element.130), channel_id=1, source_target_pairs={{0,8},{8,0},{16,24},{24,16},{1,9},{9,1},{17,25},{25,17},{2,10},{10... | collective-permute-start | bytes 1572872 | tf_op jit(solution)/shard_map/ppermute | solution.py:39
  97.8 13.7 %collective-permute-start.23 = (f32[24,32,128]{2,1,0:T(8,128)S(1)}, f32[24,32,128]{2,1,0:T(8,128)S(1)}, u32[]{:S(2)}, u32[]{:S(2)}) collective-permute-start(f32[24,32,128]{2,1,0:T(8,128)S(1)} %get-tuple-element.222), channel_id=1, source_target_pairs={{0,16},{8,24},{16,0},{24,8},{1,17},{9,25},{17,1},{25,9},{2,18},{10... | collective-permute-start | bytes 1179656 | tf_op jit(solution)/shard_map/ppermute | solution.py:39
  119.0 7.9 %collective-permute-start.28 = (f32[16,32,128]{2,1,0:T(8,128)S(1)}, f32[16,32,128]{2,1,0:T(8,128)S(1)}, u32[]{:S(2)}, u32[]{:S(2)}) collective-permute-start(f32[16,32,128]{2,1,0:T(8,128)S(1)} %pad_maximum_fusion.4), channel_id=1, source_target_pairs={{0,8},{8,0},{16,24},{24,16},{1,9},{9,1},{17,25},{25,17},{2,10},{10... | collective-permute-start | bytes 786440 | tf_op jit(solution)/shard_map/ppermute | solution.py:39
  119.7 9.8 %collective-permute-start.31 = (f32[16,32,128]{2,1,0:T(8,128)S(1)}, f32[16,32,128]{2,1,0:T(8,128)S(1)}, u32[]{:S(2)}, u32[]{:S(2)}) collective-permute-start(f32[16,32,128]{2,1,0:T(8,128)S(1)} %pad_maximum_fusion.5), channel_id=1, source_target_pairs={{0,2},{2,0},{1,3},{3,1},{4,6},{6,4},{5,7},{7,5},{8,10},{10,8},{9,1... | collective-permute-start | bytes 786440 | tf_op jit(solution)/shard_map/ppermute | solution.py:39
  124.0 14.9 %collective-permute-start.26 = (f32[32,32,128]{2,1,0:T(8,128)S(1)}, f32[32,32,128]{2,1,0:T(8,128)S(1)}, u32[]{:S(2)}, u32[]{:S(2)}) collective-permute-start(f32[32,32,128]{2,1,0:T(8,128)S(1)} %constant_dynamic-update-slice_fusion.15.refs_0_), channel_id=1, source_target_pairs={{0,2},{2,0},{1,3},{3,1},{4,6},{6,4},{5,7},{7,5},{8,10},{10,8},{9,1... | collective-permute-start | bytes 1572872 | tf_op jit(solution)/shard_map/ppermute | solution.py:39
  126.9 12.0 %collective-permute-start.29 = (f32[32,32,128]{2,1,0:T(8,128)S(1)}, f32[32,32,128]{2,1,0:T(8,128)S(1)}, u32[]{:S(2)}, u32[]{:S(2)}) collective-permute-start(f32[32,32,128]{2,1,0:T(8,128)S(1)} %constant_dynamic-update-slice_fusion.18.refs_1_), channel_id=1, source_target_pairs={{0,4},{4,0},{1,5},{5,1},{2,6},{6,2},{3,7},{7,3},{8,12},{12,8},{9,1... | collective-permute-start | bytes 1572872 | tf_op jit(solution)/shard_map/ppermute | solution.py:39
  129.5 9.4 %collective-permute-start.32 = (f32[32,32,128]{2,1,0:T(8,128)S(1)}, f32[32,32,128]{2,1,0:T(8,128)S(1)}, u32[]{:S(2)}, u32[]{:S(2)}) collective-permute-start(f32[32,32,128]{2,1,0:T(8,128)S(1)} %constant_dynamic-update-slice_fusion.21.refs_2_), channel_id=1, source_target_pairs={{0,8},{8,0},{16,24},{24,16},{1,9},{9,1},{17,25},{25,17},{2,10},{10... | collective-permute-start | bytes 1572872 | tf_op jit(solution)/shard_map/ppermute | solution.py:39
  146.8 12.4 %collective-permute-start.33 = (f32[32,32,128]{2,1,0:T(8,128)}, f32[32,32,128]{2,1,0:T(8,128)S(1)}, u32[]{:S(2)}, u32[]{:S(2)}) collective-permute-start(f32[32,32,128]{2,1,0:T(8,128)} %get-tuple-element.144), channel_id=1, source_target_pairs={{0,2},{2,0},{1,3},{3,1},{4,6},{6,4},{5,7},{7,5},{8,10},{10,8},{9,1... | collective-permute-start | bytes 1572872 | tf_op jit(solution)/shard_map/ppermute | solution.py:39
  149.1 12.2 %collective-permute-start.36 = (f32[32,32,128]{2,1,0:T(8,128)}, f32[32,32,128]{2,1,0:T(8,128)S(1)}, u32[]{:S(2)}, u32[]{:S(2)}) collective-permute-start(f32[32,32,128]{2,1,0:T(8,128)} %get-tuple-element.153), channel_id=1, source_target_pairs={{0,4},{4,0},{1,5},{5,1},{2,6},{6,2},{3,7},{7,3},{8,12},{12,8},{9,1... | collective-permute-start | bytes 1572872 | tf_op jit(solution)/shard_map/ppermute | solution.py:39
  150.1 12.9 %collective-permute-start.39 = (f32[32,32,128]{2,1,0:T(8,128)}, f32[32,32,128]{2,1,0:T(8,128)S(1)}, u32[]{:S(2)}, u32[]{:S(2)}) collective-permute-start(f32[32,32,128]{2,1,0:T(8,128)} %get-tuple-element.162), channel_id=1, source_target_pairs={{0,8},{8,0},{16,24},{24,16},{1,9},{9,1},{17,25},{25,17},{2,10},{10... | collective-permute-start | bytes 1572872 | tf_op jit(solution)/shard_map/ppermute | solution.py:39
  175.4 13.0 %collective-permute-start.42 = (f32[24,32,128]{2,1,0:T(8,128)S(1)}, f32[24,32,128]{2,1,0:T(8,128)S(1)}, u32[]{:S(2)}, u32[]{:S(2)}) collective-permute-start(f32[24,32,128]{2,1,0:T(8,128)S(1)} %get-tuple-element.210), channel_id=1, source_target_pairs={{0,16},{8,24},{16,0},{24,8},{1,17},{9,25},{17,1},{25,9},{2,18},{10... | collective-permute-start | bytes 1179656 | tf_op jit(solution)/shard_map/ppermute | solution.py:39
  193.7 9.3 %collective-permute-start.44 = (f32[16,32,128]{2,1,0:T(8,128)S(1)}, f32[16,32,128]{2,1,0:T(8,128)S(1)}, u32[]{:S(2)}, u32[]{:S(2)}) collective-permute-start(f32[16,32,128]{2,1,0:T(8,128)S(1)} %pad_maximum_fusion.6), channel_id=1, source_target_pairs={{0,4},{4,0},{1,5},{5,1},{2,6},{6,2},{3,7},{7,3},{8,12},{12,8},{9,1... | collective-permute-start | bytes 786440 | tf_op jit(solution)/shard_map/ppermute | solution.py:39
  195.6 8.9 %collective-permute-start.47 = (f32[16,32,128]{2,1,0:T(8,128)S(1)}, f32[16,32,128]{2,1,0:T(8,128)S(1)}, u32[]{:S(2)}, u32[]{:S(2)}) collective-permute-start(f32[16,32,128]{2,1,0:T(8,128)S(1)} %pad_maximum_fusion.7), channel_id=1, source_target_pairs={{0,8},{8,0},{16,24},{24,16},{1,9},{9,1},{17,25},{25,17},{2,10},{10... | collective-permute-start | bytes 786440 | tf_op jit(solution)/shard_map/ppermute | solution.py:39
  197.4 7.7 %collective-permute-start.50 = (f32[16,32,128]{2,1,0:T(8,128)S(1)}, f32[16,32,128]{2,1,0:T(8,128)S(1)}, u32[]{:S(2)}, u32[]{:S(2)}) collective-permute-start(f32[16,32,128]{2,1,0:T(8,128)S(1)} %pad_maximum_fusion.8), channel_id=1, source_target_pairs={{0,2},{2,0},{1,3},{3,1},{4,6},{6,4},{5,7},{7,5},{8,10},{10,8},{9,1... | collective-permute-start | bytes 786440 | tf_op jit(solution)/shard_map/ppermute | solution.py:39
  203.1 12.0 %collective-permute-start.45 = (f32[32,32,128]{2,1,0:T(8,128)S(1)}, f32[32,32,128]{2,1,0:T(8,128)S(1)}, u32[]{:S(2)}, u32[]{:S(2)}) collective-permute-start(f32[32,32,128]{2,1,0:T(8,128)S(1)} %constant_dynamic-update-slice_fusion.30.refs_0_), channel_id=1, source_target_pairs={{0,2},{2,0},{1,3},{3,1},{4,6},{6,4},{5,7},{7,5},{8,10},{10,8},{9,1... | collective-permute-start | bytes 1572872 | tf_op jit(solution)/shard_map/ppermute | solution.py:39
  204.5 10.7 %collective-permute-start.48 = (f32[32,32,128]{2,1,0:T(8,128)S(1)}, f32[32,32,128]{2,1,0:T(8,128)S(1)}, u32[]{:S(2)}, u32[]{:S(2)}) collective-permute-start(f32[32,32,128]{2,1,0:T(8,128)S(1)} %constant_dynamic-update-slice_fusion.33.refs_1_), channel_id=1, source_target_pairs={{0,4},{4,0},{1,5},{5,1},{2,6},{6,2},{3,7},{7,3},{8,12},{12,8},{9,1... | collective-permute-start | bytes 1572872 | tf_op jit(solution)/shard_map/ppermute | solution.py:39
  205.1 10.0 %collective-permute-start.51 = (f32[32,32,128]{2,1,0:T(8,128)S(1)}, f32[32,32,128]{2,1,0:T(8,128)S(1)}, u32[]{:S(2)}, u32[]{:S(2)}) collective-permute-start(f32[32,32,128]{2,1,0:T(8,128)S(1)} %constant_dynamic-update-slice_fusion.36.refs_2_), channel_id=1, source_target_pairs={{0,8},{8,0},{16,24},{24,16},{1,9},{9,1},{17,25},{25,17},{2,10},{10... | collective-permute-start | bytes 1572872 | tf_op jit(solution)/shard_map/ppermute | solution.py:39
  223.0 12.3 %collective-permute-start.58 = (f32[32,32,128]{2,1,0:T(8,128)}, f32[32,32,128]{2,1,0:T(8,128)S(1)}, u32[]{:S(2)}, u32[]{:S(2)}) collective-permute-start(f32[32,32,128]{2,1,0:T(8,128)} %get-tuple-element.194), channel_id=1, source_target_pairs={{0,8},{8,0},{16,24},{24,16},{1,9},{9,1},{17,25},{25,17},{2,10},{10... | collective-permute-start | bytes 1572872 | tf_op jit(solution)/shard_map/ppermute | solution.py:39
  224.2 13.5 %collective-permute-start.55 = (f32[32,32,128]{2,1,0:T(8,128)}, f32[32,32,128]{2,1,0:T(8,128)S(1)}, u32[]{:S(2)}, u32[]{:S(2)}) collective-permute-start(f32[32,32,128]{2,1,0:T(8,128)} %get-tuple-element.185), channel_id=1, source_target_pairs={{0,4},{4,0},{1,5},{5,1},{2,6},{6,2},{3,7},{7,3},{8,12},{12,8},{9,1... | collective-permute-start | bytes 1572872 | tf_op jit(solution)/shard_map/ppermute | solution.py:39
  226.6 13.3 %collective-permute-start.52 = (f32[32,32,128]{2,1,0:T(8,128)}, f32[32,32,128]{2,1,0:T(8,128)S(1)}, u32[]{:S(2)}, u32[]{:S(2)}) collective-permute-start(f32[32,32,128]{2,1,0:T(8,128)} %get-tuple-element.176), channel_id=1, source_target_pairs={{0,2},{2,0},{1,3},{3,1},{4,6},{6,4},{5,7},{7,5},{8,10},{10,8},{9,1... | collective-permute-start | bytes 1572872 | tf_op jit(solution)/shard_map/ppermute | solution.py:39
  256.5 10.7 %all-to-all-start = ((f32[32,1,128]{2,1,0:T(1,128)}), f32[32,1,128]{2,1,0:T(1,128)S(1)}, u32[]{:S(2)}, u32[]{:S(2)}) async-start(f32[32,1,128]{2,1,0:T(1,128)} %broadcast_in_dim.60), calls=%async_computation | async-start | bytes 32768 | tf_op jit(solution)/shard_map/all_to_all | solution.py:336
  260.1 12.5 %collective-permute-start.61 = (f32[12,32,128]{2,1,0:T(8,128)S(1)}, f32[12,32,128]{2,1,0:T(8,128)S(1)}, u32[]{:S(2)}, u32[]{:S(2)}) collective-permute-start(f32[12,32,128]{2,1,0:T(8,128)S(1)} %get-tuple-element.203), channel_id=1, source_target_pairs={{0,16},{8,24},{16,0},{24,8},{1,17},{9,25},{17,1},{25,9},{2,18},{10... | collective-permute-start | bytes 589832 | tf_op jit(solution)/shard_map/ppermute | solution.py:39
  (77 other events, 433.0 us)

commit v17 on v16

--- a/solution.py
+++ b/solution.py
@@ -15,7 +15,8 @@
 CHUNK = 8
 SLOTS = 8
 SPANS = 4
-VMEM = 56 * 1024 * 1024
+VMEM = 48 * 1024 * 1024
+SPLIT_VMEM = 62 * 1024 * 1024
 CHIPS = ("z", "y", "x")
 ALL = ("z", "y", "x", "core")
 NEAR = ("x", "y", "z")
@@ -130,7 +131,7 @@
         + [pl.BlockSpec(memory_space=pltpu.HBM)] * len(given),
         out_specs=pl.BlockSpec((STEP, 2 * size, size), lambda i: (place * steps + i, 0, 0)),
         input_output_aliases={1: 0} if given else {},
-        compiler_params=pltpu.CompilerParams(vmem_limit_bytes=VMEM),
+        compiler_params=pltpu.CompilerParams(vmem_limit_bytes=SPLIT_VMEM),
         cost_estimate=pl.CostEstimate(
             flops=3 * length * size * size, bytes_accessed=8 * length * size * size, transcendentals=0
         ),

time: 276 us -> 261 us (0.946)
  waiting for transfers between devices: 73.8 us -> 105 us
  Pallas kernels: 89.2 us -> 62.8 us
  starting transfers between devices: 81.3 us -> 67.6 us
  other arithmetic: 18.8 us -> 12 us
    ppermute x63, waiting for transfers between devices: 69.4 us -> 101 us  [swap(): lax.ppermute(array, axis, [(i, i ^ distance) for i in range(lax.axis_size...]
    pallas_call x9, Pallas kernels: 68.6 us -> 42.3 us  [apply_tiles(): pl.pallas_call(functools.partial(apply_kernel, span, skip, len(flux), bas...]
    ppermute x63, starting transfers between devices: 77.7 us -> 64.6 us  [swap(): lax.ppermute(array, axis, [(i, i ^ distance) for i in range(lax.axis_size...]
    add x18, other arithmetic: 8.98 us -> 2.72 us  [reduce_near(): sum([halves(t)[1] for t in terms[1:]], halves(terms[0])[1])]
    unnamed x104 -> x48, local copies, waits for them, and re-layouts: 5.31 us -> 5.72 us
  transfers between devices with their start and end apart: 64 -> 64, of which waited for: 31 -> 41; matrix products, arithmetic and copies ran while one was open for 6% -> 6% of each run, Pallas kernels for 25% -> 20%
where the time goes in v17:
time: 261 us
  waiting for transfers between devices  105 us (40%)
  starting transfers between devices  67.6 us (26%)
  Pallas kernels  62.8 us (24%)
  other arithmetic  12 us (5%)
  local copies, waits for them, and re-layouts  11 us (4%)
    ppermute x63, waiting for transfers between devices, swap(): lax.ppermute(array, axis, [(i, i ^ distance) for i in range(lax.axis_size...  101 us
    ppermute x63, starting transfers between devices, swap(): lax.ppermute(array, axis, [(i, i ^ distance) for i in range(lax.axis_size...  64.6 us
    pallas_call x9, Pallas kernels, apply_tiles(): pl.pallas_call(functools.partial(apply_kernel, span, skip, len(flux), bas...  42.3 us
    pallas_call x2, Pallas kernels, split_tiles(): pl.pallas_call(split_kernel, out_shape=jax.ShapeDtypeStruct((CORES * leng...  20.6 us
    unnamed x48, local copies, waits for them, and re-layouts  5.72 us
  transfers between devices with their start and end apart: 64, of which 41 were waited for; matrix products, arithmetic and copies ran while one was open for 6% of the time, Pallas kernels for 20%

profile of v17, /device:TPU:0, one launch (start us, length us, event | category | flops | bytes accessed | tf_op | source)
XLA Modules:
  0.0 260.8 jit_solution(17033402338825966412)
XLA Ops:
  8.0 4.0 %collective-permute-start.4 = (f32[12,32,128]{2,1,0:T(8,128)S(1)}, f32[12,32,128]{2,1,0:T(8,128)S(1)}, u32[]{:S(2)}, u32[]{:S(2)}) collective-permute-start(f32[12,32,128]{2,1,0:T(8,128)S(1)} %get-tuple-element.272), channel_id=1, source_target_pairs={{0,16},{8,24},{16,0},{24,8},{1,17},{9,25},{17,1},{25,9},{2,18},{10... | collective-permute-start | bytes 589832 | tf_op jit(solution)/shard_map/ppermute | solution.py:40
  12.1 10.3 %shard_map.95.refs_0_ = bf16[256,256,128]{2,1,0:T(8,128)(2,1)} custom-call(f32[128,128,128]{2,1,0:T(8,128)} %tile_ref), custom_call_target="tpu_custom_call" | custom-call | flops 6291456 | bytes 16777216 | tf_op jit(solution)/shard_map/pallas_call | solution.py:126
  31.2 3.1 %collective-permute-done.11 = f32[8,32,128]{2,1,0:T(8,128)S(1)} collective-permute-done((f32[8,32,128]{2,1,0:T(8,128)S(1)}, f32[8,32,128]{2,1,0:T(8,128)S(1)}, u32[]{:S(2)}, u32[]{:S(2)}) %collective-permute-start.11) | collective-permute-done | bytes 131104 | tf_op jit(solution)/shard_map/ppermute | solution.py:40
  43.5 10.3 %shard_map.96.pairs_ref = bf16[256,256,128]{2,1,0:T(8,128)(2,1)} custom-call(f32[128,128,128]{2,1,0:T(8,128)} %collective-permute-done.2.tile_ref, bf16[256,256,128]{2,1,0:T(8,128)(2,1)} %shard_map.95.refs_0_), custom_call_target="tpu_custom_call", output_to_operand_aliasing={{}: (1, {})} | custom-call | flops 6291456 | bytes 16777216 | tf_op jit(solution)/shard_map/pallas_call | solution.py:126
  53.8 6.9 %shard_map.97 = (f32[96,32,128]{2,1,0:T(8,128)S(1)}, f32[96,32,128]{2,1,0:T(8,128)S(1)}) custom-call(s32[772]{0:T(1024)S(1)} %pad_add_fusion.places_ref, bf16[256,256,128]{2,1,0:T(8,128)(2,1)} %shard_map.96.pairs_ref, f32[32,32,128]{2,1,0:T(8,128)} %constant_dynamic-update-slice_fusion.refs_0_, f32[32,32,128]{2,1,0:T(8,128)} %constant_dynamic-update-slice_fusion.3.refs_1_, ...), custom_call_target="tpu_custom_call" | custom-call | flops 536870912 | bytes 14680064 | tf_op jit(solution)/shard_map/pallas_call | solution.py:215
  60.8 3.9 %shard_map.99 = (f32[32,32,128]{2,1,0:T(8,128)S(1)}, f32[32,32,128]{2,1,0:T(8,128)S(1)}, f32[32,32,128]{2,1,0:T(8,128)S(1)}) custom-call(s32[772]{0:T(1024)S(1)} %pad_add_fusion.places_ref, bf16[256,256,128]{2,1,0:T(8,128)(2,1)} %shard_map.96.pairs_ref, f32[32,32,128]{2,1,0:T(8,128)S(1)} %collective-permute-done.7.refs_0_, ...), custom_call_target="tpu_custom_call" | custom-call | flops 268435456 | bytes 7340032 | tf_op jit(solution)/shard_map/pallas_call | solution.py:215
  68.1 4.1 %shard_map.98 = (f32[32,32,128]{2,1,0:T(8,128)S(1)}, f32[32,32,128]{2,1,0:T(8,128)S(1)}, f32[32,32,128]{2,1,0:T(8,128)S(1)}) custom-call(s32[772]{0:T(1024)S(1)} %pad_add_fusion.places_ref, bf16[256,256,128]{2,1,0:T(8,128)(2,1)} %shard_map.96.pairs_ref, f32[32,32,128]{2,1,0:T(8,128)S(1)} %collective-permute-done.7.refs_0_, ...), custom_call_target="tpu_custom_call" | custom-call | flops 268435456 | bytes 7340032 | tf_op jit(solution)/shard_map/pallas_call | solution.py:215
  72.2 4.2 %collective-permute-done.14 = f32[32,32,128]{2,1,0:T(8,128)S(1)} collective-permute-done((f32[32,32,128]{2,1,0:T(8,128)S(1)}, f32[32,32,128]{2,1,0:T(8,128)S(1)}, u32[]{:S(2)}, u32[]{:S(2)}) %collective-permute-start.14) | collective-permute-done | bytes 524320 | tf_op jit(solution)/shard_map/ppermute | solution.py:40
  93.2 3.0 %collective-permute-start.23 = (f32[24,32,128]{2,1,0:T(8,128)S(1)}, f32[24,32,128]{2,1,0:T(8,128)S(1)}, u32[]{:S(2)}, u32[]{:S(2)}) collective-permute-start(f32[24,32,128]{2,1,0:T(8,128)S(1)} %get-tuple-element.222), channel_id=1, source_target_pairs={{0,16},{8,24},{16,0},{24,8},{1,17},{9,25},{17,1},{25,9},{2,18},{10... | collective-permute-start | bytes 1179656 | tf_op jit(solution)/shard_map/ppermute | solution.py:40
  96.2 11.2 %collective-permute-done.23 = f32[24,32,128]{2,1,0:T(8,128)S(1)} collective-permute-done((f32[24,32,128]{2,1,0:T(8,128)S(1)}, f32[24,32,128]{2,1,0:T(8,128)S(1)}, u32[]{:S(2)}, u32[]{:S(2)}) %collective-permute-start.23) | collective-permute-done | bytes 393248 | tf_op jit(solution)/shard_map/ppermute | solution.py:40
  109.6 4.2 %collective-permute-done.24 = f32[8,32,128]{2,1,0:T(8,128)S(1)} collective-permute-done((f32[8,32,128]{2,1,0:T(8,128)S(1)}, f32[8,32,128]{2,1,0:T(8,128)S(1)}, u32[]{:S(2)}, u32[]{:S(2)}) %collective-permute-start.24) | collective-permute-done | bytes 131104 | tf_op jit(solution)/shard_map/ppermute | solution.py:40
  117.4 4.1 %collective-permute-done.25 = f32[16,32,128]{2,1,0:T(8,128)S(1)} collective-permute-done((f32[16,32,128]{2,1,0:T(8,128)S(1)}, f32[16,32,128]{2,1,0:T(8,128)S(1)}, u32[]{:S(2)}, u32[]{:S(2)}) %collective-permute-start.25) | collective-permute-done | bytes 262176 | tf_op jit(solution)/shard_map/ppermute | solution.py:40
  125.5 5.5 %shard_map.100 = (f32[96,32,128]{2,1,0:T(8,128)S(1)}, f32[96,32,128]{2,1,0:T(8,128)S(1)}) custom-call(s32[772]{0:T(1024)S(1)} %pad_add_fusion.places_ref, bf16[256,256,128]{2,1,0:T(8,128)(2,1)} %shard_map.96.pairs_ref, f32[32,32,128]{2,1,0:T(8,128)S(1)} %constant_dynamic-update-slice_fusion.15.refs_0_, ...), custom_call_target="tpu_custom_call" | custom-call | flops 536870912 | bytes 14680064 | tf_op jit(solution)/shard_map/pallas_call | solution.py:215
  134.0 3.9 %shard_map.102 = (f32[32,32,128]{2,1,0:T(8,128)S(1)}, f32[32,32,128]{2,1,0:T(8,128)S(1)}, f32[32,32,128]{2,1,0:T(8,128)S(1)}) custom-call(s32[772]{0:T(1024)S(1)} %pad_add_fusion.places_ref, bf16[256,256,128]{2,1,0:T(8,128)(2,1)} %shard_map.96.pairs_ref, f32[32,32,128]{2,1,0:T(8,128)S(1)} %collective-permute-done.26.refs_0_, ...), custom_call_target="tpu_custom_call" | custom-call | flops 268435456 | bytes 7340032 | tf_op jit(solution)/shard_map/pallas_call | solution.py:215
  140.8 4.1 %shard_map.101 = (f32[32,32,128]{2,1,0:T(8,128)S(1)}, f32[32,32,128]{2,1,0:T(8,128)S(1)}, f32[32,32,128]{2,1,0:T(8,128)S(1)}) custom-call(s32[772]{0:T(1024)S(1)} %pad_add_fusion.places_ref, bf16[256,256,128]{2,1,0:T(8,128)(2,1)} %shard_map.96.pairs_ref, f32[32,32,128]{2,1,0:T(8,128)S(1)} %collective-permute-done.26.refs_0_, ...), custom_call_target="tpu_custom_call" | custom-call | flops 268435456 | bytes 7340032 | tf_op jit(solution)/shard_map/pallas_call | solution.py:215
  145.0 5.0 %collective-permute-done.33 = f32[32,32,128]{2,1,0:T(8,128)S(1)} collective-permute-done((f32[32,32,128]{2,1,0:T(8,128)S(1)}, f32[32,32,128]{2,1,0:T(8,128)S(1)}, u32[]{:S(2)}, u32[]{:S(2)}) %collective-permute-start.33) | collective-permute-done | bytes 524320 | tf_op jit(solution)/shard_map/ppermute | solution.py:40
  153.0 4.0 %collective-permute-done.34 = f32[16,32,128]{2,1,0:T(8,128)S(1)} collective-permute-done((f32[16,32,128]{2,1,0:T(8,128)S(1)}, f32[16,32,128]{2,1,0:T(8,128)S(1)}, u32[]{:S(2)}, u32[]{:S(2)}) %collective-permute-start.34) | collective-permute-done | bytes 262176 | tf_op jit(solution)/shard_map/ppermute | solution.py:40
  158.9 3.1 %collective-permute-start.41 = (f32[8,32,128]{2,1,0:T(8,128)S(1)}, f32[8,32,128]{2,1,0:T(8,128)S(1)}, u32[]{:S(2)}, u32[]{:S(2)}) collective-permute-start(f32[8,32,128]{2,1,0:T(8,128)S(1)} %slice_add_fusion.16), channel_id=1, source_target_pairs={{0,4},{4,0},{1,5},{5,1},{2,6},{6,2},{3,7},{7,3},{8,12},{12,8},{9,1... | collective-permute-start | bytes 393224 | tf_op jit(solution)/shard_map/ppermute | solution.py:40
  167.0 11.2 %collective-permute-done.42 = f32[24,32,128]{2,1,0:T(8,128)S(1)} collective-permute-done((f32[24,32,128]{2,1,0:T(8,128)S(1)}, f32[24,32,128]{2,1,0:T(8,128)S(1)}, u32[]{:S(2)}, u32[]{:S(2)}) %collective-permute-start.42) | collective-permute-done | bytes 393248 | tf_op jit(solution)/shard_map/ppermute | solution.py:40
  180.7 2.8 %collective-permute-done.43 = f32[8,32,128]{2,1,0:T(8,128)S(1)} collective-permute-done((f32[8,32,128]{2,1,0:T(8,128)S(1)}, f32[8,32,128]{2,1,0:T(8,128)S(1)}, u32[]{:S(2)}, u32[]{:S(2)}) %collective-permute-start.43) | collective-permute-done | bytes 131104 | tf_op jit(solution)/shard_map/ppermute | solution.py:40
  187.4 5.2 %collective-permute-done.44 = f32[16,32,128]{2,1,0:T(8,128)S(1)} collective-permute-done((f32[16,32,128]{2,1,0:T(8,128)S(1)}, f32[16,32,128]{2,1,0:T(8,128)S(1)}, u32[]{:S(2)}, u32[]{:S(2)}) %collective-permute-start.44) | collective-permute-done | bytes 262176 | tf_op jit(solution)/shard_map/ppermute | solution.py:40
  195.3 5.7 %shard_map.103 = (f32[96,32,128]{2,1,0:T(8,128)S(1)}, f32[96,32,128]{2,1,0:T(8,128)S(1)}) custom-call(s32[772]{0:T(1024)S(1)} %pad_add_fusion.places_ref, bf16[256,256,128]{2,1,0:T(8,128)(2,1)} %shard_map.96.pairs_ref, f32[32,32,128]{2,1,0:T(8,128)S(1)} %constant_dynamic-update-slice_fusion.30.refs_0_, ...), custom_call_target="tpu_custom_call" | custom-call | flops 536870912 | bytes 14680064 | tf_op jit(solution)/shard_map/pallas_call | solution.py:215
  202.8 2.7 %collective-permute-done.48.refs_1_ = f32[32,32,128]{2,1,0:T(8,128)S(1)} collective-permute-done((f32[32,32,128]{2,1,0:T(8,128)S(1)}, f32[32,32,128]{2,1,0:T(8,128)S(1)}, u32[]{:S(2)}, u32[]{:S(2)}) %collective-permute-start.48) | collective-permute-done | bytes 524320 | tf_op jit(solution)/shard_map/ppermute | solution.py:40
  205.6 4.0 %collective-permute-done.51.refs_2_ = f32[32,32,128]{2,1,0:T(8,128)S(1)} collective-permute-done((f32[32,32,128]{2,1,0:T(8,128)S(1)}, f32[32,32,128]{2,1,0:T(8,128)S(1)}, u32[]{:S(2)}, u32[]{:S(2)}) %collective-permute-start.51) | collective-permute-done | bytes 524320 | tf_op jit(solution)/shard_map/ppermute | solution.py:40
  209.5 3.9 %shard_map.105 = (f32[32,32,128]{2,1,0:T(8,128)S(1)}, f32[32,32,128]{2,1,0:T(8,128)S(1)}, f32[32,32,128]{2,1,0:T(8,128)S(1)}) custom-call(s32[772]{0:T(1024)S(1)} %pad_add_fusion.places_ref, bf16[256,256,128]{2,1,0:T(8,128)(2,1)} %shard_map.96.pairs_ref, f32[32,32,128]{2,1,0:T(8,128)S(1)} %collective-permute-done.45.refs_0_, ...), custom_call_target="tpu_custom_call" | custom-call | flops 268435456 | bytes 7340032 | tf_op jit(solution)/shard_map/pallas_call | solution.py:215
  215.1 4.1 %shard_map.104 = (f32[32,32,128]{2,1,0:T(8,128)S(1)}, f32[32,32,128]{2,1,0:T(8,128)S(1)}, f32[32,32,128]{2,1,0:T(8,128)S(1)}) custom-call(s32[772]{0:T(1024)S(1)} %pad_add_fusion.places_ref, bf16[256,256,128]{2,1,0:T(8,128)(2,1)} %shard_map.96.pairs_ref, f32[32,32,128]{2,1,0:T(8,128)S(1)} %collective-permute-done.45.refs_0_, ...), custom_call_target="tpu_custom_call" | custom-call | flops 268435456 | bytes 7340032 | tf_op jit(solution)/shard_map/pallas_call | solution.py:215
  219.2 4.7 %collective-permute-done.58 = f32[32,32,128]{2,1,0:T(8,128)S(1)} collective-permute-done((f32[32,32,128]{2,1,0:T(8,128)S(1)}, f32[32,32,128]{2,1,0:T(8,128)S(1)}, u32[]{:S(2)}, u32[]{:S(2)}) %collective-permute-start.58) | collective-permute-done | bytes 524320 | tf_op jit(solution)/shard_map/ppermute | solution.py:40
  226.3 4.1 %collective-permute-done.59 = f32[16,32,128]{2,1,0:T(8,128)S(1)} collective-permute-done((f32[16,32,128]{2,1,0:T(8,128)S(1)}, f32[16,32,128]{2,1,0:T(8,128)S(1)}, u32[]{:S(2)}, u32[]{:S(2)}) %collective-permute-start.59) | collective-permute-done | bytes 262176 | tf_op jit(solution)/shard_map/ppermute | solution.py:40
  243.2 2.9 %all-to-all-start = ((f32[32,1,128]{2,1,0:T(1,128)}), f32[32,1,128]{2,1,0:T(1,128)S(1)}, u32[]{:S(2)}, u32[]{:S(2)}) async-start(f32[32,1,128]{2,1,0:T(1,128)} %broadcast_in_dim.60), calls=%async_computation | async-start | bytes 32768 | tf_op jit(solution)/shard_map/all_to_all | solution.py:337
  246.1 2.7 %collective-permute-start.61 = (f32[12,32,128]{2,1,0:T(8,128)S(1)}, f32[12,32,128]{2,1,0:T(8,128)S(1)}, u32[]{:S(2)}, u32[]{:S(2)}) collective-permute-start(f32[12,32,128]{2,1,0:T(8,128)S(1)} %get-tuple-element.203), channel_id=1, source_target_pairs={{0,16},{8,24},{16,0},{24,8},{1,17},{9,25},{17,1},{25,9},{2,18},{10... | collective-permute-start | bytes 589832 | tf_op jit(solution)/shard_map/ppermute | solution.py:40
  248.9 4.4 %all-to-all-done = f32[32,1,128]{2,1,0:T(1,128)S(1)} async-done(((f32[32,1,128]{2,1,0:T(1,128)}), f32[32,1,128]{2,1,0:T(1,128)S(1)}, u32[]{:S(2)}, u32[]{:S(2)}) %all-to-all-start) | async-done | bytes 16416 | tf_op jit(solution)/shard_map/all_to_all | solution.py:337
  255.2 3.4 %collective-permute-done.61 = f32[12,32,128]{2,1,0:T(8,128)S(1)} collective-permute-done((f32[12,32,128]{2,1,0:T(8,128)S(1)}, f32[12,32,128]{2,1,0:T(8,128)S(1)}, u32[]{:S(2)}, u32[]{:S(2)}) %collective-permute-start.61) | collective-permute-done | bytes 196640 | tf_op jit(solution)/shard_map/ppermute | solution.py:40
  (282 shorter events, 101.8 us)
Async XLA Ops:
  6.1 37.4 %collective-permute-start.2 = (f32[128,128,128]{2,1,0:T(8,128)}, f32[128,128,128]{2,1,0:T(8,128)}, u32[]{:S(2)}, u32[]{:S(2)}) collective-permute-start(f32[128,128,128]{2,1,0:T(8,128)} %tile_ref), channel_id=1, source_target_pairs={{0,1},{1,0},{2,3},{3,2},{4,5},{5,4},{6,7},{7,6},{8,9},{9,8},{10,11... | collective-permute-start | bytes 25165832 | tf_op jit(solution)/shard_map/ppermute | solution.py:40
  8.0 14.4 %collective-permute-start.4 = (f32[12,32,128]{2,1,0:T(8,128)S(1)}, f32[12,32,128]{2,1,0:T(8,128)S(1)}, u32[]{:S(2)}, u32[]{:S(2)}) collective-permute-start(f32[12,32,128]{2,1,0:T(8,128)S(1)} %get-tuple-element.272), channel_id=1, source_target_pairs={{0,16},{8,24},{16,0},{24,8},{1,17},{9,25},{17,1},{25,9},{2,18},{10... | collective-permute-start | bytes 589832 | tf_op jit(solution)/shard_map/ppermute | solution.py:40
  12.0 10.4 %collective-permute-start.3 = (f32[12,2,128]{2,0,1:T(8,128)S(1)}, f32[12,2,128]{2,0,1:T(8,128)S(1)}, u32[]{:S(2)}, u32[]{:S(2)}) collective-permute-start(f32[12,2,128]{2,0,1:T(8,128)S(1)} %pad_maximum_fusion.22), channel_id=1, source_target_pairs={{0,16},{8,24},{16,0},{24,8},{1,17},{9,25},{17,1},{25,9},{2,18},{10... | collective-permute-start | bytes 36872 | tf_op jit(solution)/shard_map/ppermute | solution.py:40
  29.5 8.6 %collective-permute-start.6 = (f32[16,32,128]{2,1,0:T(8,128)S(1)}, f32[16,32,128]{2,1,0:T(8,128)S(1)}, u32[]{:S(2)}, u32[]{:S(2)}) collective-permute-start(f32[16,32,128]{2,1,0:T(8,128)S(1)} %pad_maximum_fusion), channel_id=1, source_target_pairs={{0,4},{4,0},{1,5},{5,1},{2,6},{6,2},{3,7},{7,3},{8,12},{12,8},{9,1... | collective-permute-start | bytes 786440 | tf_op jit(solution)/shard_map/ppermute | solution.py:40
  30.8 8.6 %collective-permute-start.9 = (f32[16,32,128]{2,1,0:T(8,128)S(1)}, f32[16,32,128]{2,1,0:T(8,128)S(1)}, u32[]{:S(2)}, u32[]{:S(2)}) collective-permute-start(f32[16,32,128]{2,1,0:T(8,128)S(1)} %pad_maximum_fusion.1), channel_id=1, source_target_pairs={{0,8},{8,0},{16,24},{24,16},{1,9},{9,1},{17,25},{25,17},{2,10},{10... | collective-permute-start | bytes 786440 | tf_op jit(solution)/shard_map/ppermute | solution.py:40
  38.8 21.9 %collective-permute-start.7 = (f32[32,32,128]{2,1,0:T(8,128)}, f32[32,32,128]{2,1,0:T(8,128)S(1)}, u32[]{:S(2)}, u32[]{:S(2)}) collective-permute-start(f32[32,32,128]{2,1,0:T(8,128)} %constant_dynamic-update-slice_fusion.refs_0_), channel_id=1, source_target_pairs={{0,2},{2,0},{1,3},{3,1},{4,6},{6,4},{5,7},{7,5},{8,10},{10,8},{9,1... | collective-permute-start | bytes 1572872 | tf_op jit(solution)/shard_map/ppermute | solution.py:40
  40.0 20.7 %collective-permute-start.10 = (f32[32,32,128]{2,1,0:T(8,128)}, f32[32,32,128]{2,1,0:T(8,128)S(1)}, u32[]{:S(2)}, u32[]{:S(2)}) collective-permute-start(f32[32,32,128]{2,1,0:T(8,128)} %constant_dynamic-update-slice_fusion.3.refs_1_), channel_id=1, source_target_pairs={{0,4},{4,0},{1,5},{5,1},{2,6},{6,2},{3,7},{7,3},{8,12},{12,8},{9,1... | collective-permute-start | bytes 1572872 | tf_op jit(solution)/shard_map/ppermute | solution.py:40
  42.5 18.3 %collective-permute-start.13 = (f32[32,32,128]{2,1,0:T(8,128)}, f32[32,32,128]{2,1,0:T(8,128)S(1)}, u32[]{:S(2)}, u32[]{:S(2)}) collective-permute-start(f32[32,32,128]{2,1,0:T(8,128)} %constant_dynamic-update-slice_fusion.6.refs_2_), channel_id=1, source_target_pairs={{0,8},{8,0},{16,24},{24,16},{1,9},{9,1},{17,25},{25,17},{2,10},{10... | collective-permute-start | bytes 1572872 | tf_op jit(solution)/shard_map/ppermute | solution.py:40
  64.7 11.8 %collective-permute-start.14 = (f32[32,32,128]{2,1,0:T(8,128)S(1)}, f32[32,32,128]{2,1,0:T(8,128)S(1)}, u32[]{:S(2)}, u32[]{:S(2)}) collective-permute-start(f32[32,32,128]{2,1,0:T(8,128)S(1)} %get-tuple-element.112), channel_id=1, source_target_pairs={{0,2},{2,0},{1,3},{3,1},{4,6},{6,4},{5,7},{7,5},{8,10},{10,8},{9,1... | collective-permute-start | bytes 1572872 | tf_op jit(solution)/shard_map/ppermute | solution.py:40
  66.1 11.6 %collective-permute-start.17 = (f32[32,32,128]{2,1,0:T(8,128)S(1)}, f32[32,32,128]{2,1,0:T(8,128)S(1)}, u32[]{:S(2)}, u32[]{:S(2)}) collective-permute-start(f32[32,32,128]{2,1,0:T(8,128)S(1)} %get-tuple-element.121), channel_id=1, source_target_pairs={{0,4},{4,0},{1,5},{5,1},{2,6},{6,2},{3,7},{7,3},{8,12},{12,8},{9,1... | collective-permute-start | bytes 1572872 | tf_op jit(solution)/shard_map/ppermute | solution.py:40
  66.1 12.9 %collective-permute-start.20 = (f32[32,32,128]{2,1,0:T(8,128)S(1)}, f32[32,32,128]{2,1,0:T(8,128)S(1)}, u32[]{:S(2)}, u32[]{:S(2)}) collective-permute-start(f32[32,32,128]{2,1,0:T(8,128)S(1)} %get-tuple-element.130), channel_id=1, source_target_pairs={{0,8},{8,0},{16,24},{24,16},{1,9},{9,1},{17,25},{25,17},{2,10},{10... | collective-permute-start | bytes 1572872 | tf_op jit(solution)/shard_map/ppermute | solution.py:40
  79.0 8.9 %collective-permute-start.21 = (f32[16,32,128]{2,1,0:T(8,128)S(1)}, f32[16,32,128]{2,1,0:T(8,128)S(1)}, u32[]{:S(2)}, u32[]{:S(2)}) collective-permute-start(f32[16,32,128]{2,1,0:T(8,128)S(1)} %slice_add_fusion.6), channel_id=1, source_target_pairs={{0,2},{2,0},{1,3},{3,1},{4,6},{6,4},{5,7},{7,5},{8,10},{10,8},{9,1... | collective-permute-start | bytes 786440 | tf_op jit(solution)/shard_map/ppermute | solution.py:40
  93.2 14.2 %collective-permute-start.23 = (f32[24,32,128]{2,1,0:T(8,128)S(1)}, f32[24,32,128]{2,1,0:T(8,128)S(1)}, u32[]{:S(2)}, u32[]{:S(2)}) collective-permute-start(f32[24,32,128]{2,1,0:T(8,128)S(1)} %get-tuple-element.222), channel_id=1, source_target_pairs={{0,16},{8,24},{16,0},{24,8},{1,17},{9,25},{17,1},{25,9},{2,18},{10... | collective-permute-start | bytes 1179656 | tf_op jit(solution)/shard_map/ppermute | solution.py:40
  114.0 8.9 %collective-permute-start.28 = (f32[16,32,128]{2,1,0:T(8,128)S(1)}, f32[16,32,128]{2,1,0:T(8,128)S(1)}, u32[]{:S(2)}, u32[]{:S(2)}) collective-permute-start(f32[16,32,128]{2,1,0:T(8,128)S(1)} %pad_maximum_fusion.4), channel_id=1, source_target_pairs={{0,8},{8,0},{16,24},{24,16},{1,9},{9,1},{17,25},{25,17},{2,10},{10... | collective-permute-start | bytes 786440 | tf_op jit(solution)/shard_map/ppermute | solution.py:40
  115.5 9.2 %collective-permute-start.31 = (f32[16,32,128]{2,1,0:T(8,128)S(1)}, f32[16,32,128]{2,1,0:T(8,128)S(1)}, u32[]{:S(2)}, u32[]{:S(2)}) collective-permute-start(f32[16,32,128]{2,1,0:T(8,128)S(1)} %pad_maximum_fusion.5), channel_id=1, source_target_pairs={{0,2},{2,0},{1,3},{3,1},{4,6},{6,4},{5,7},{7,5},{8,10},{10,8},{9,1... | collective-permute-start | bytes 786440 | tf_op jit(solution)/shard_map/ppermute | solution.py:40
  121.5 10.7 %collective-permute-start.26 = (f32[32,32,128]{2,1,0:T(8,128)S(1)}, f32[32,32,128]{2,1,0:T(8,128)S(1)}, u32[]{:S(2)}, u32[]{:S(2)}) collective-permute-start(f32[32,32,128]{2,1,0:T(8,128)S(1)} %constant_dynamic-update-slice_fusion.15.refs_0_), channel_id=1, source_target_pairs={{0,2},{2,0},{1,3},{3,1},{4,6},{6,4},{5,7},{7,5},{8,10},{10,8},{9,1... | collective-permute-start | bytes 1572872 | tf_op jit(solution)/shard_map/ppermute | solution.py:40
  122.9 9.4 %collective-permute-start.29 = (f32[32,32,128]{2,1,0:T(8,128)S(1)}, f32[32,32,128]{2,1,0:T(8,128)S(1)}, u32[]{:S(2)}, u32[]{:S(2)}) collective-permute-start(f32[32,32,128]{2,1,0:T(8,128)S(1)} %constant_dynamic-update-slice_fusion.18.refs_1_), channel_id=1, source_target_pairs={{0,4},{4,0},{1,5},{5,1},{2,6},{6,2},{3,7},{7,3},{8,12},{12,8},{9,1... | collective-permute-start | bytes 1572872 | tf_op jit(solution)/shard_map/ppermute | solution.py:40
  124.7 9.2 %collective-permute-start.32 = (f32[32,32,128]{2,1,0:T(8,128)S(1)}, f32[32,32,128]{2,1,0:T(8,128)S(1)}, u32[]{:S(2)}, u32[]{:S(2)}) collective-permute-start(f32[32,32,128]{2,1,0:T(8,128)S(1)} %constant_dynamic-update-slice_fusion.21.refs_2_), channel_id=1, source_target_pairs={{0,8},{8,0},{16,24},{24,16},{1,9},{9,1},{17,25},{25,17},{2,10},{10... | collective-permute-start | bytes 1572872 | tf_op jit(solution)/shard_map/ppermute | solution.py:40
  137.9 12.1 %collective-permute-start.33 = (f32[32,32,128]{2,1,0:T(8,128)S(1)}, f32[32,32,128]{2,1,0:T(8,128)S(1)}, u32[]{:S(2)}, u32[]{:S(2)}) collective-permute-start(f32[32,32,128]{2,1,0:T(8,128)S(1)} %get-tuple-element.144), channel_id=1, source_target_pairs={{0,2},{2,0},{1,3},{3,1},{4,6},{6,4},{5,7},{7,5},{8,10},{10,8},{9,1... | collective-permute-start | bytes 1572872 | tf_op jit(solution)/shard_map/ppermute | solution.py:40
  139.8 11.4 %collective-permute-start.36 = (f32[32,32,128]{2,1,0:T(8,128)S(1)}, f32[32,32,128]{2,1,0:T(8,128)S(1)}, u32[]{:S(2)}, u32[]{:S(2)}) collective-permute-start(f32[32,32,128]{2,1,0:T(8,128)S(1)} %get-tuple-element.153), channel_id=1, source_target_pairs={{0,4},{4,0},{1,5},{5,1},{2,6},{6,2},{3,7},{7,3},{8,12},{12,8},{9,1... | collective-permute-start | bytes 1572872 | tf_op jit(solution)/shard_map/ppermute | solution.py:40
  139.8 12.6 %collective-permute-start.39 = (f32[32,32,128]{2,1,0:T(8,128)S(1)}, f32[32,32,128]{2,1,0:T(8,128)S(1)}, u32[]{:S(2)}, u32[]{:S(2)}) collective-permute-start(f32[32,32,128]{2,1,0:T(8,128)S(1)} %get-tuple-element.162), channel_id=1, source_target_pairs={{0,8},{8,0},{16,24},{24,16},{1,9},{9,1},{17,25},{25,17},{2,10},{10... | collective-permute-start | bytes 1572872 | tf_op jit(solution)/shard_map/ppermute | solution.py:40
  165.1 13.1 %collective-permute-start.42 = (f32[24,32,128]{2,1,0:T(8,128)S(1)}, f32[24,32,128]{2,1,0:T(8,128)S(1)}, u32[]{:S(2)}, u32[]{:S(2)}) collective-permute-start(f32[24,32,128]{2,1,0:T(8,128)S(1)} %get-tuple-element.210), channel_id=1, source_target_pairs={{0,16},{8,24},{16,0},{24,8},{1,17},{9,25},{17,1},{25,9},{2,18},{10... | collective-permute-start | bytes 1179656 | tf_op jit(solution)/shard_map/ppermute | solution.py:40
  183.5 9.1 %collective-permute-start.44 = (f32[16,32,128]{2,1,0:T(8,128)S(1)}, f32[16,32,128]{2,1,0:T(8,128)S(1)}, u32[]{:S(2)}, u32[]{:S(2)}) collective-permute-start(f32[16,32,128]{2,1,0:T(8,128)S(1)} %pad_maximum_fusion.6), channel_id=1, source_target_pairs={{0,4},{4,0},{1,5},{5,1},{2,6},{6,2},{3,7},{7,3},{8,12},{12,8},{9,1... | collective-permute-start | bytes 786440 | tf_op jit(solution)/shard_map/ppermute | solution.py:40
  185.2 8.0 %collective-permute-start.47 = (f32[16,32,128]{2,1,0:T(8,128)S(1)}, f32[16,32,128]{2,1,0:T(8,128)S(1)}, u32[]{:S(2)}, u32[]{:S(2)}) collective-permute-start(f32[16,32,128]{2,1,0:T(8,128)S(1)} %pad_maximum_fusion.7), channel_id=1, source_target_pairs={{0,8},{8,0},{16,24},{24,16},{1,9},{9,1},{17,25},{25,17},{2,10},{10... | collective-permute-start | bytes 786440 | tf_op jit(solution)/shard_map/ppermute | solution.py:40
  192.6 10.3 %collective-permute-start.45 = (f32[32,32,128]{2,1,0:T(8,128)S(1)}, f32[32,32,128]{2,1,0:T(8,128)S(1)}, u32[]{:S(2)}, u32[]{:S(2)}) collective-permute-start(f32[32,32,128]{2,1,0:T(8,128)S(1)} %constant_dynamic-update-slice_fusion.30.refs_0_), channel_id=1, source_target_pairs={{0,2},{2,0},{1,3},{3,1},{4,6},{6,4},{5,7},{7,5},{8,10},{10,8},{9,1... | collective-permute-start | bytes 1572872 | tf_op jit(solution)/shard_map/ppermute | solution.py:40
  193.3 12.3 %collective-permute-start.48 = (f32[32,32,128]{2,1,0:T(8,128)S(1)}, f32[32,32,128]{2,1,0:T(8,128)S(1)}, u32[]{:S(2)}, u32[]{:S(2)}) collective-permute-start(f32[32,32,128]{2,1,0:T(8,128)S(1)} %constant_dynamic-update-slice_fusion.33.refs_1_), channel_id=1, source_target_pairs={{0,4},{4,0},{1,5},{5,1},{2,6},{6,2},{3,7},{7,3},{8,12},{12,8},{9,1... | collective-permute-start | bytes 1572872 | tf_op jit(solution)/shard_map/ppermute | solution.py:40
  195.0 14.5 %collective-permute-start.51 = (f32[32,32,128]{2,1,0:T(8,128)S(1)}, f32[32,32,128]{2,1,0:T(8,128)S(1)}, u32[]{:S(2)}, u32[]{:S(2)}) collective-permute-start(f32[32,32,128]{2,1,0:T(8,128)S(1)} %constant_dynamic-update-slice_fusion.36.refs_2_), channel_id=1, source_target_pairs={{0,8},{8,0},{16,24},{24,16},{1,9},{9,1},{17,25},{25,17},{2,10},{10... | collective-permute-start | bytes 1572872 | tf_op jit(solution)/shard_map/ppermute | solution.py:40
  213.4 10.5 %collective-permute-start.58 = (f32[32,32,128]{2,1,0:T(8,128)S(1)}, f32[32,32,128]{2,1,0:T(8,128)S(1)}, u32[]{:S(2)}, u32[]{:S(2)}) collective-permute-start(f32[32,32,128]{2,1,0:T(8,128)S(1)} %get-tuple-element.194), channel_id=1, source_target_pairs={{0,8},{8,0},{16,24},{24,16},{1,9},{9,1},{17,25},{25,17},{2,10},{10... | collective-permute-start | bytes 1572872 | tf_op jit(solution)/shard_map/ppermute | solution.py:40
  213.5 12.1 %collective-permute-start.55 = (f32[32,32,128]{2,1,0:T(8,128)S(1)}, f32[32,32,128]{2,1,0:T(8,128)S(1)}, u32[]{:S(2)}, u32[]{:S(2)}) collective-permute-start(f32[32,32,128]{2,1,0:T(8,128)S(1)} %get-tuple-element.185), channel_id=1, source_target_pairs={{0,4},{4,0},{1,5},{5,1},{2,6},{6,2},{3,7},{7,3},{8,12},{12,8},{9,1... | collective-permute-start | bytes 1572872 | tf_op jit(solution)/shard_map/ppermute | solution.py:40
  213.6 12.4 %collective-permute-start.52 = (f32[32,32,128]{2,1,0:T(8,128)S(1)}, f32[32,32,128]{2,1,0:T(8,128)S(1)}, u32[]{:S(2)}, u32[]{:S(2)}) collective-permute-start(f32[32,32,128]{2,1,0:T(8,128)S(1)} %get-tuple-element.176), channel_id=1, source_target_pairs={{0,2},{2,0},{1,3},{3,1},{4,6},{6,4},{5,7},{7,5},{8,10},{10,8},{9,1... | collective-permute-start | bytes 1572872 | tf_op jit(solution)/shard_map/ppermute | solution.py:40
  243.2 10.1 %all-to-all-start = ((f32[32,1,128]{2,1,0:T(1,128)}), f32[32,1,128]{2,1,0:T(1,128)S(1)}, u32[]{:S(2)}, u32[]{:S(2)}) async-start(f32[32,1,128]{2,1,0:T(1,128)} %broadcast_in_dim.60), calls=%async_computation | async-start | bytes 32768 | tf_op jit(solution)/shard_map/all_to_all | solution.py:337
  246.1 12.5 %collective-permute-start.61 = (f32[12,32,128]{2,1,0:T(8,128)S(1)}, f32[12,32,128]{2,1,0:T(8,128)S(1)}, u32[]{:S(2)}, u32[]{:S(2)}) collective-permute-start(f32[12,32,128]{2,1,0:T(8,128)S(1)} %get-tuple-element.203), channel_id=1, source_target_pairs={{0,16},{8,24},{16,0},{24,8},{1,17},{9,25},{17,1},{25,9},{2,18},{10... | collective-permute-start | bytes 589832 | tf_op jit(solution)/shard_map/ppermute | solution.py:40
  (50 other events, 305.1 us)

commit v18 on v17

--- a/solution.py
+++ b/solution.py
@@ -10,13 +10,10 @@
 
 ITERS = 3
 CORES = 2
-STEP = 16
-UNROLL = 8
 CHUNK = 8
 SLOTS = 8
 SPANS = 4
 VMEM = 48 * 1024 * 1024
-SPLIT_VMEM = 62 * 1024 * 1024
 CHIPS = ("z", "y", "x")
 ALL = ("z", "y", "x", "core")
 NEAR = ("x", "y", "z")
@@ -105,54 +102,26 @@
     return blocks
 
 
-def split_kernel(tile_ref, *refs):
-    pair_ref = refs[-1]
-    size = tile_ref.shape[1]
-
-    @pl.loop(0, STEP // UNROLL)
-    def _(group):
-        for k in range(UNROLL):
-            tile = jnp.transpose(tile_ref[group * UNROLL + k])
-            high = tile.astype(jnp.bfloat16)
-            low = (tile - high.astype(jnp.float32)).astype(jnp.bfloat16)
-            pair_ref[group * UNROLL + k, :size] = high
-            pair_ref[group * UNROLL + k, size:] = low
-
-
-def split_tiles(tiles, place, pairs=None):
-    length, size, _ = tiles.shape
-    steps = length // STEP
-    given = [] if pairs is None else [pairs]
-    return pl.pallas_call(
-        split_kernel,
-        out_shape=jax.ShapeDtypeStruct((CORES * length, 2 * size, size), jnp.bfloat16),
-        grid=(steps,),
-        in_specs=[pl.BlockSpec((STEP, size, size), lambda i: (i, 0, 0))]
-        + [pl.BlockSpec(memory_space=pltpu.HBM)] * len(given),
-        out_specs=pl.BlockSpec((STEP, 2 * size, size), lambda i: (place * steps + i, 0, 0)),
-        input_output_aliases={1: 0} if given else {},
-        compiler_params=pltpu.CompilerParams(vmem_limit_bytes=SPLIT_VMEM),
-        cost_estimate=pl.CostEstimate(
-            flops=3 * length * size * size, bytes_accessed=8 * length * size * size, transcendentals=0
-        ),
-    )(tiles, *given)
-
-
-def apply_kernel(span, skip, pieces, has_base, places_ref, pairs_ref, *refs):
+def apply_kernel(span, skip, pieces, has_base, places_ref, own_ref, other_ref, *refs):
     flux, refs = refs[:pieces], refs[pieces:]
     base_ref, refs = (refs[0], refs[1:]) if has_base else (None, refs)
     *outs, flux_ref, sum_ref, held_ref, held_sem = refs
-    total = pairs_ref.shape[0]
+    length = own_ref.shape[0]
+    total = 2 * length
     start, stop = places_ref[span], places_ref[span + 1]
     chunks = (stop - start + CHUNK - 1) // CHUNK
 
     def fetch(chunk):
         slot = lax.rem(chunk, SLOTS)
         for k in range(CHUNK):
-            at = jnp.minimum(start + chunk * CHUNK + k, total - 1)
-            pltpu.make_async_copy(
-                pairs_ref.at[places_ref[SPANS + at]], held_ref.at[slot, k], held_sem.at[slot]
-            ).start()
+            at = places_ref[SPANS + jnp.minimum(start + chunk * CHUNK + k, total - 1)]
+            for tiles_ref, low in ((own_ref, 0), (other_ref, length)):
+
+                @pl.when((at >= low) & (at < low + length))
+                def _():
+                    pltpu.make_async_copy(
+                        tiles_ref.at[at - low], held_ref.at[slot, k], held_sem.at[slot]
+                    ).start()
 
     for chunk in range(SLOTS - 1):
 
@@ -173,7 +142,7 @@
     def _(chunk):
         slot = lax.rem(chunk, SLOTS)
         pltpu.make_async_copy(
-            pairs_ref.at[pl.ds(0, CHUNK)], held_ref.at[slot], held_sem.at[slot]
+            own_ref.at[pl.ds(0, CHUNK)], held_ref.at[slot], held_sem.at[slot]
         ).wait()
 
         @pl.when(chunk + SLOTS - 1 < chunks)
@@ -189,9 +158,13 @@
             high = values.astype(jnp.bfloat16)
             low = (values - high.astype(jnp.float32)).astype(jnp.bfloat16)
             left = jnp.concatenate([high, low], axis=0)
-            both = jnp.dot(
+            tile = held_ref[slot, k]
+            high = tile.astype(jnp.bfloat16)
+            low = (tile - high.astype(jnp.float32)).astype(jnp.bfloat16)
+            both = lax.dot_general(
                 jnp.concatenate([left, left], axis=1),
-                held_ref[slot, k],
+                jnp.concatenate([high, low], axis=1),
+                (((1,), (1,)), ((), ())),
                 preferred_element_type=jnp.float32,
             )
             temps = values.shape[0]
@@ -206,8 +179,8 @@
         done += out.shape[0]
 
 
-def apply_tiles(span, skip, places, pairs, flux, sizes, share, base=None):
-    total, _, size = pairs.shape
+def apply_tiles(span, skip, places, tiles, flux, sizes, share, base=None):
+    length, size, _ = tiles[0].shape
     temps = flux[0].shape[1]
     rows = sum(sizes)
     inside = pl.BlockSpec(memory_space=pltpu.VMEM)
@@ -218,22 +191,22 @@
         grid_spec=pltpu.PrefetchScalarGridSpec(
             num_scalar_prefetch=1,
             grid=(),
-            in_specs=[pl.BlockSpec(memory_space=pltpu.HBM)] + [inside] * len(given),
+            in_specs=[pl.BlockSpec(memory_space=pltpu.HBM)] * 2 + [inside] * len(given),
             out_specs=[inside] * len(sizes),
             scratch_shapes=[
                 pltpu.VMEM((sum(piece.shape[0] for piece in flux), temps, size), jnp.float32),
                 pltpu.VMEM((rows, temps, size), jnp.float32),
-                pltpu.VMEM((SLOTS, CHUNK) + pairs.shape[1:], jnp.bfloat16),
+                pltpu.VMEM((SLOTS, CHUNK, size, size), jnp.float32),
                 pltpu.SemaphoreType.DMA((SLOTS,)),
             ],
         ),
         compiler_params=pltpu.CompilerParams(vmem_limit_bytes=VMEM),
         cost_estimate=pl.CostEstimate(
-            flops=int(share * total * size * size * temps * 8),
-            bytes_accessed=int(share * total * size * size * 4) + 8 * rows * temps * size,
+            flops=int(share * 2 * length * size * size * temps * 8),
+            bytes_accessed=int(share * 2 * length * size * size * 4) + 8 * rows * temps * size,
             transcendentals=0,
         ),
-    )(places, pairs, *given)
+    )(places, *tiles, *given)
 
 
 def shards(
@@ -312,18 +285,16 @@
     drives = gather_far(drive_half)
     small = gather_far(jnp.concatenate([relax_both, heat_both * relax_both], axis=1))
     relaxes, heats = [s[:, :1] for s in small], [s[:, 1:] for s in small]
-    pairs = split_tiles(tile_values, 0)
-    drives[-1] = after(drives[-1], pairs)
+    drives[-1], other_values = lax.optimization_barrier((drives[-1], other_values))
     fluxes = [r * d for r, d in zip(relaxes, drives)]
+    tiles = (tile_values, other_values)
     sizes = [chips // 2 * (high - low) for low, high in zip(edges[:-1], edges[1:])]
     for sweep in range(ITERS):
         pieces = gather_near(fluxes, edges)
-        if sweep == 0:
-            pairs = split_tiles(other_values, 1, pairs)
         near, far = [p for p, _ in pieces], [p for _, p in pieces]
-        base = apply_tiles(0, 0, places, pairs, near, [num // 2, num // 2], 0.5)
-        sends = apply_tiles(1, 0, places, pairs, far, sizes, 0.25, base[0])
-        keeps = apply_tiles(2, num // 2, places, pairs, far, sizes, 0.25, base[1])
+        base = apply_tiles(0, 0, places, tiles, near, [num // 2, num // 2], 0.5)
+        sends = apply_tiles(1, 0, places, tiles, far, sizes, 0.25, base[0])
+        keeps = apply_tiles(2, num // 2, places, tiles, far, sizes, 0.25, base[1])
         blocks = reduce_near(keeps, sends)
         if sweep < ITERS - 1:
             fluxes = [r * (d + s) for r, d, s in zip(relaxes, drives, sum_far(blocks))]

time: 261 us -> 253 us (0.969)
  Pallas kernels: 62.8 us -> 43.9 us
  starting transfers between devices: 67.6 us -> 75.6 us
  waiting for transfers between devices: 105 us -> 113 us
  local copies, waits for them, and re-layouts: 11 us -> 5.47 us
    pallas_call x2 -> x0, Pallas kernels: 20.6 us -> none  [split_tiles(): pl.pallas_call(split_kernel, out_shape=jax.ShapeDtypeStruct((CORES * leng...]
    ppermute x63, waiting for transfers between devices: 101 us -> 109 us  [swap(): lax.ppermute(array, axis, [(i, i ^ distance) for i in range(lax.axis_size...]
    ppermute x63, starting transfers between devices: 64.6 us -> 71.9 us  [swap(): lax.ppermute(array, axis, [(i, i ^ distance) for i in range(lax.axis_size...]
    unnamed x48 -> x56, local copies, waits for them, and re-layouts: 5.72 us -> 1.69 us
  transfers between devices with their start and end apart: 64 -> 64, of which waited for: 41 -> 43; matrix products, arithmetic and copies ran while one was open for 6% -> 4% of each run, Pallas kernels for 20% -> 12%
where the time goes in v18:
time: 253 us
  waiting for transfers between devices  113 us (45%)
  starting transfers between devices  75.6 us (30%)
  Pallas kernels  43.9 us (17%)
  other arithmetic  12 us (5%)
  local copies, waits for them, and re-layouts  5.47 us (2%)
    ppermute x63, waiting for transfers between devices, swap(): lax.ppermute(array, axis, [(i, i ^ distance) for i in range(lax.axis_size...  109 us
    ppermute x63, starting transfers between devices, swap(): lax.ppermute(array, axis, [(i, i ^ distance) for i in range(lax.axis_size...  71.9 us
    pallas_call x9, Pallas kernels, apply_tiles(): pl.pallas_call(functools.partial(apply_kernel, span, skip, len(flux), bas...  43.9 us
  transfers between devices with their start and end apart: 64, of which 43 were waited for; matrix products, arithmetic and copies ran while one was open for 4% of the time, Pallas kernels for 12%

profile of v18, /device:TPU:0, one launch (start us, length us, event | category | flops | bytes accessed | tf_op | source)
XLA Modules:
  0.0 252.7 jit_solution(852162681162070261)
XLA Ops:
  8.6 3.9 %collective-permute-start.2 = (f32[12,32,128]{2,1,0:T(8,128)S(1)}, f32[12,32,128]{2,1,0:T(8,128)S(1)}, u32[]{:S(2)}, u32[]{:S(2)}) collective-permute-start(f32[12,32,128]{2,1,0:T(8,128)S(1)} %get-tuple-element.274), channel_id=1, source_target_pairs={{0,16},{8,24},{16,0},{24,8},{1,17},{9,25},{17,1},{25,9},{2,18},{10... | collective-permute-start | bytes 589832 | tf_op jit(solution)/shard_map/ppermute | solution.py:37
  12.5 10.1 %collective-permute-done.4 = f32[12,2,128]{2,0,1:T(8,128)S(1)} collective-permute-done((f32[12,2,128]{2,0,1:T(8,128)S(1)}, f32[12,2,128]{2,0,1:T(8,128)S(1)}, u32[]{:S(2)}, u32[]{:S(2)}) %collective-permute-start.4) | collective-permute-done | bytes 12320 | tf_op jit(solution)/shard_map/ppermute | solution.py:37
  33.0 3.4 %collective-permute-done.6 = f32[16,32,128]{2,1,0:T(8,128)S(1)} collective-permute-done((f32[16,32,128]{2,1,0:T(8,128)S(1)}, f32[16,32,128]{2,1,0:T(8,128)S(1)}, u32[]{:S(2)}, u32[]{:S(2)}) %collective-permute-start.6) | collective-permute-done | bytes 262176 | tf_op jit(solution)/shard_map/ppermute | solution.py:37
  40.8 6.2 %shard_map.95 = (f32[96,32,128]{2,1,0:T(8,128)S(1)}, f32[96,32,128]{2,1,0:T(8,128)S(1)}) custom-call(s32[772]{0:T(1024)S(1)} %pad_add_fusion.places_ref, f32[128,128,128]{2,1,0:T(8,128)} %own_ref.8, f32[128,128,128]{2,1,0:T(8,128)} %copy-done.2, f32[32,32,128]{2,1,0:T(8,128)S(1)} %constant_dynamic-update-slice_fusion.refs_0_, ...), custom_call_target="tpu_custom_call" | custom-call | flops 536870912 | bytes 14680064 | tf_op jit(solution)/shard_map/pallas_call | solution.py:188
  47.0 2.5 collective-permute-done.7.refs_0_
  50.5 4.3 %shard_map.97 = (f32[32,32,128]{2,1,0:T(8,128)S(1)}, f32[32,32,128]{2,1,0:T(8,128)S(1)}, f32[32,32,128]{2,1,0:T(8,128)S(1)}) custom-call(s32[772]{0:T(1024)S(1)} %pad_add_fusion.places_ref, f32[128,128,128]{2,1,0:T(8,128)} %own_ref.8, f32[128,128,128]{2,1,0:T(8,128)} %copy-done.2, f32[32,32,128]{2,1,0:T(8,128)S(1)} %collective-permute-done.7.refs_0_, ...), custom_call_target="tpu_custom_call" | custom-call | flops 268435456 | bytes 7340032 | tf_op jit(solution)/shard_map/pallas_call | solution.py:188
  58.7 4.0 %shard_map.96 = (f32[32,32,128]{2,1,0:T(8,128)S(1)}, f32[32,32,128]{2,1,0:T(8,128)S(1)}, f32[32,32,128]{2,1,0:T(8,128)S(1)}) custom-call(s32[772]{0:T(1024)S(1)} %pad_add_fusion.places_ref, f32[128,128,128]{2,1,0:T(8,128)} %own_ref.8, f32[128,128,128]{2,1,0:T(8,128)} %copy-done.2, f32[32,32,128]{2,1,0:T(8,128)S(1)} %collective-permute-done.7.refs_0_, ...), custom_call_target="tpu_custom_call" | custom-call | flops 268435456 | bytes 7340032 | tf_op jit(solution)/shard_map/pallas_call | solution.py:188
  62.7 3.3 %collective-permute-done.14 = f32[32,32,128]{2,1,0:T(8,128)S(1)} collective-permute-done((f32[32,32,128]{2,1,0:T(8,128)S(1)}, f32[32,32,128]{2,1,0:T(8,128)S(1)}, u32[]{:S(2)}, u32[]{:S(2)}) %collective-permute-start.14) | collective-permute-done | bytes 524320 | tf_op jit(solution)/shard_map/ppermute | solution.py:37
  83.6 3.4 %collective-permute-start.23 = (f32[24,32,128]{2,1,0:T(8,128)S(1)}, f32[24,32,128]{2,1,0:T(8,128)S(1)}, u32[]{:S(2)}, u32[]{:S(2)}) collective-permute-start(f32[24,32,128]{2,1,0:T(8,128)S(1)} %get-tuple-element.224), channel_id=1, source_target_pairs={{0,16},{8,24},{16,0},{24,8},{1,17},{9,25},{17,1},{25,9},{2,18},{10... | collective-permute-start | bytes 1179656 | tf_op jit(solution)/shard_map/ppermute | solution.py:37
  87.0 11.7 %collective-permute-done.23 = f32[24,32,128]{2,1,0:T(8,128)S(1)} collective-permute-done((f32[24,32,128]{2,1,0:T(8,128)S(1)}, f32[24,32,128]{2,1,0:T(8,128)S(1)}, u32[]{:S(2)}, u32[]{:S(2)}) %collective-permute-start.23) | collective-permute-done | bytes 393248 | tf_op jit(solution)/shard_map/ppermute | solution.py:37
  101.3 2.6 %collective-permute-done.24 = f32[8,32,128]{2,1,0:T(8,128)S(1)} collective-permute-done((f32[8,32,128]{2,1,0:T(8,128)S(1)}, f32[8,32,128]{2,1,0:T(8,128)S(1)}, u32[]{:S(2)}, u32[]{:S(2)}) %collective-permute-start.24) | collective-permute-done | bytes 131104 | tf_op jit(solution)/shard_map/ppermute | solution.py:37
  107.5 3.5 %collective-permute-done.25 = f32[16,32,128]{2,1,0:T(8,128)S(1)} collective-permute-done((f32[16,32,128]{2,1,0:T(8,128)S(1)}, f32[16,32,128]{2,1,0:T(8,128)S(1)}, u32[]{:S(2)}, u32[]{:S(2)}) %collective-permute-start.25) | collective-permute-done | bytes 262176 | tf_op jit(solution)/shard_map/ppermute | solution.py:37
  116.9 6.2 %shard_map.98 = (f32[96,32,128]{2,1,0:T(8,128)S(1)}, f32[96,32,128]{2,1,0:T(8,128)S(1)}) custom-call(s32[772]{0:T(1024)S(1)} %pad_add_fusion.places_ref, f32[128,128,128]{2,1,0:T(8,128)} %own_ref.8, f32[128,128,128]{2,1,0:T(8,128)} %copy-done.2, f32[32,32,128]{2,1,0:T(8,128)S(1)} %constant_dynamic-update-slice_fusion.15.refs_0_, ...), custom_call_target="tpu_custom_call" | custom-call | flops 536870912 | bytes 14680064 | tf_op jit(solution)/shard_map/pallas_call | solution.py:188
  124.9 4.3 %shard_map.100 = (f32[32,32,128]{2,1,0:T(8,128)S(1)}, f32[32,32,128]{2,1,0:T(8,128)S(1)}, f32[32,32,128]{2,1,0:T(8,128)S(1)}) custom-call(s32[772]{0:T(1024)S(1)} %pad_add_fusion.places_ref, f32[128,128,128]{2,1,0:T(8,128)} %own_ref.8, f32[128,128,128]{2,1,0:T(8,128)} %copy-done.2, f32[32,32,128]{2,1,0:T(8,128)S(1)} %collective-permute-done.26.refs_0_, ...), custom_call_target="tpu_custom_call" | custom-call | flops 268435456 | bytes 7340032 | tf_op jit(solution)/shard_map/pallas_call | solution.py:188
  132.4 4.2 %shard_map.99 = (f32[32,32,128]{2,1,0:T(8,128)S(1)}, f32[32,32,128]{2,1,0:T(8,128)S(1)}, f32[32,32,128]{2,1,0:T(8,128)S(1)}) custom-call(s32[772]{0:T(1024)S(1)} %pad_add_fusion.places_ref, f32[128,128,128]{2,1,0:T(8,128)} %own_ref.8, f32[128,128,128]{2,1,0:T(8,128)} %copy-done.2, f32[32,32,128]{2,1,0:T(8,128)S(1)} %collective-permute-done.26.refs_0_, ...), custom_call_target="tpu_custom_call" | custom-call | flops 268435456 | bytes 7340032 | tf_op jit(solution)/shard_map/pallas_call | solution.py:188
  136.6 4.1 %collective-permute-done.33 = f32[32,32,128]{2,1,0:T(8,128)S(1)} collective-permute-done((f32[32,32,128]{2,1,0:T(8,128)S(1)}, f32[32,32,128]{2,1,0:T(8,128)S(1)}, u32[]{:S(2)}, u32[]{:S(2)}) %collective-permute-start.33) | collective-permute-done | bytes 524320 | tf_op jit(solution)/shard_map/ppermute | solution.py:37
  144.9 3.1 %collective-permute-done.34 = f32[16,32,128]{2,1,0:T(8,128)S(1)} collective-permute-done((f32[16,32,128]{2,1,0:T(8,128)S(1)}, f32[16,32,128]{2,1,0:T(8,128)S(1)}, u32[]{:S(2)}, u32[]{:S(2)}) %collective-permute-start.34) | collective-permute-done | bytes 262176 | tf_op jit(solution)/shard_map/ppermute | solution.py:37
  155.4 3.3 %collective-permute-start.42 = (f32[24,32,128]{2,1,0:T(8,128)S(1)}, f32[24,32,128]{2,1,0:T(8,128)S(1)}, u32[]{:S(2)}, u32[]{:S(2)}) collective-permute-start(f32[24,32,128]{2,1,0:T(8,128)S(1)} %get-tuple-element.212), channel_id=1, source_target_pairs={{0,16},{8,24},{16,0},{24,8},{1,17},{9,25},{17,1},{25,9},{2,18},{10... | collective-permute-start | bytes 1179656 | tf_op jit(solution)/shard_map/ppermute | solution.py:37
  158.7 10.7 %collective-permute-done.42 = f32[24,32,128]{2,1,0:T(8,128)S(1)} collective-permute-done((f32[24,32,128]{2,1,0:T(8,128)S(1)}, f32[24,32,128]{2,1,0:T(8,128)S(1)}, u32[]{:S(2)}, u32[]{:S(2)}) %collective-permute-start.42) | collective-permute-done | bytes 393248 | tf_op jit(solution)/shard_map/ppermute | solution.py:37
  171.9 4.0 %collective-permute-done.43 = f32[8,32,128]{2,1,0:T(8,128)S(1)} collective-permute-done((f32[8,32,128]{2,1,0:T(8,128)S(1)}, f32[8,32,128]{2,1,0:T(8,128)S(1)}, u32[]{:S(2)}, u32[]{:S(2)}) %collective-permute-start.43) | collective-permute-done | bytes 131104 | tf_op jit(solution)/shard_map/ppermute | solution.py:37
  178.7 6.0 %collective-permute-done.44 = f32[16,32,128]{2,1,0:T(8,128)S(1)} collective-permute-done((f32[16,32,128]{2,1,0:T(8,128)S(1)}, f32[16,32,128]{2,1,0:T(8,128)S(1)}, u32[]{:S(2)}, u32[]{:S(2)}) %collective-permute-start.44) | collective-permute-done | bytes 262176 | tf_op jit(solution)/shard_map/ppermute | solution.py:37
  187.7 6.2 %shard_map.101 = (f32[96,32,128]{2,1,0:T(8,128)S(1)}, f32[96,32,128]{2,1,0:T(8,128)S(1)}) custom-call(s32[772]{0:T(1024)S(1)} %pad_add_fusion.places_ref, f32[128,128,128]{2,1,0:T(8,128)} %own_ref.8, f32[128,128,128]{2,1,0:T(8,128)} %copy-done.2, f32[32,32,128]{2,1,0:T(8,128)S(1)} %constant_dynamic-update-slice_fusion.30.refs_0_, ...), custom_call_target="tpu_custom_call" | custom-call | flops 536870912 | bytes 14680064 | tf_op jit(solution)/shard_map/pallas_call | solution.py:188
  194.3 3.4 %collective-permute-done.51.refs_2_ = f32[32,32,128]{2,1,0:T(8,128)S(1)} collective-permute-done((f32[32,32,128]{2,1,0:T(8,128)S(1)}, f32[32,32,128]{2,1,0:T(8,128)S(1)}, u32[]{:S(2)}, u32[]{:S(2)}) %collective-permute-start.51) | collective-permute-done | bytes 524320 | tf_op jit(solution)/shard_map/ppermute | solution.py:37
  197.7 4.3 %shard_map.103 = (f32[32,32,128]{2,1,0:T(8,128)S(1)}, f32[32,32,128]{2,1,0:T(8,128)S(1)}, f32[32,32,128]{2,1,0:T(8,128)S(1)}) custom-call(s32[772]{0:T(1024)S(1)} %pad_add_fusion.places_ref, f32[128,128,128]{2,1,0:T(8,128)} %own_ref.8, f32[128,128,128]{2,1,0:T(8,128)} %copy-done.2, f32[32,32,128]{2,1,0:T(8,128)S(1)} %collective-permute-done.45.refs_0_, ...), custom_call_target="tpu_custom_call" | custom-call | flops 268435456 | bytes 7340032 | tf_op jit(solution)/shard_map/pallas_call | solution.py:188
  204.4 4.0 %shard_map.102 = (f32[32,32,128]{2,1,0:T(8,128)S(1)}, f32[32,32,128]{2,1,0:T(8,128)S(1)}, f32[32,32,128]{2,1,0:T(8,128)S(1)}) custom-call(s32[772]{0:T(1024)S(1)} %pad_add_fusion.places_ref, f32[128,128,128]{2,1,0:T(8,128)} %own_ref.8, f32[128,128,128]{2,1,0:T(8,128)} %copy-done.2, f32[32,32,128]{2,1,0:T(8,128)S(1)} %collective-permute-done.45.refs_0_, ...), custom_call_target="tpu_custom_call" | custom-call | flops 268435456 | bytes 7340032 | tf_op jit(solution)/shard_map/pallas_call | solution.py:188
  208.5 5.6 %collective-permute-done.58 = f32[32,32,128]{2,1,0:T(8,128)S(1)} collective-permute-done((f32[32,32,128]{2,1,0:T(8,128)S(1)}, f32[32,32,128]{2,1,0:T(8,128)S(1)}, u32[]{:S(2)}, u32[]{:S(2)}) %collective-permute-start.58) | collective-permute-done | bytes 524320 | tf_op jit(solution)/shard_map/ppermute | solution.py:37
  217.8 2.7 %collective-permute-done.59 = f32[16,32,128]{2,1,0:T(8,128)S(1)} collective-permute-done((f32[16,32,128]{2,1,0:T(8,128)S(1)}, f32[16,32,128]{2,1,0:T(8,128)S(1)}, u32[]{:S(2)}, u32[]{:S(2)}) %collective-permute-start.59) | collective-permute-done | bytes 262176 | tf_op jit(solution)/shard_map/ppermute | solution.py:37
  228.1 2.6 %collective-permute-done.54 = f32[8,32,128]{2,1,0:T(8,128)} collective-permute-done((f32[8,32,128]{2,1,0:T(8,128)}, f32[8,32,128]{2,1,0:T(8,128)}, u32[]{:S(2)}, u32[]{:S(2)}) %collective-permute-start.54) | collective-permute-done | bytes 131104 | tf_op jit(solution)/shard_map/ppermute | solution.py:37
  234.3 3.7 %all-to-all-start = ((f32[32,1,128]{2,1,0:T(1,128)}), f32[32,1,128]{2,1,0:T(1,128)S(1)}, u32[]{:S(2)}, u32[]{:S(2)}) async-start(f32[32,1,128]{2,1,0:T(1,128)} %broadcast_in_dim.60), calls=%async_computation | async-start | bytes 32768 | tf_op jit(solution)/shard_map/all_to_all | solution.py:308
  238.0 2.7 %collective-permute-start.61 = (f32[12,32,128]{2,1,0:T(8,128)S(1)}, f32[12,32,128]{2,1,0:T(8,128)S(1)}, u32[]{:S(2)}, u32[]{:S(2)}) collective-permute-start(f32[12,32,128]{2,1,0:T(8,128)S(1)} %get-tuple-element.205), channel_id=1, source_target_pairs={{0,16},{8,24},{16,0},{24,8},{1,17},{9,25},{17,1},{25,9},{2,18},{10... | collective-permute-start | bytes 589832 | tf_op jit(solution)/shard_map/ppermute | solution.py:37
  240.7 4.4 %all-to-all-done = f32[32,1,128]{2,1,0:T(1,128)S(1)} async-done(((f32[32,1,128]{2,1,0:T(1,128)}), f32[32,1,128]{2,1,0:T(1,128)S(1)}, u32[]{:S(2)}, u32[]{:S(2)}) %all-to-all-start) | async-done | bytes 16416 | tf_op jit(solution)/shard_map/all_to_all | solution.py:308
  247.1 3.4 %collective-permute-done.61 = f32[12,32,128]{2,1,0:T(8,128)S(1)} collective-permute-done((f32[12,32,128]{2,1,0:T(8,128)S(1)}, f32[12,32,128]{2,1,0:T(8,128)S(1)}, u32[]{:S(2)}, u32[]{:S(2)}) %collective-permute-start.61) | collective-permute-done | bytes 196640 | tf_op jit(solution)/shard_map/ppermute | solution.py:37
  (287 shorter events, 102.2 us)
Async XLA Ops:
  6.1 17.1 %collective-permute-start.3 = (f32[128,128,128]{2,1,0:T(8,128)}, f32[128,128,128]{2,1,0:T(8,128)S(1)}, u32[]{:S(2)}, u32[]{:S(2)}) collective-permute-start(f32[128,128,128]{2,1,0:T(8,128)} %own_ref.8), channel_id=1, source_target_pairs={{0,1},{1,0},{2,3},{3,2},{4,5},{5,4},{6,7},{7,6},{8,9},{9,8},{10,11... | collective-permute-start | bytes 25165832 | tf_op jit(solution)/shard_map/ppermute | solution.py:37
  8.6 14.7 %collective-permute-start.2 = (f32[12,32,128]{2,1,0:T(8,128)S(1)}, f32[12,32,128]{2,1,0:T(8,128)S(1)}, u32[]{:S(2)}, u32[]{:S(2)}) collective-permute-start(f32[12,32,128]{2,1,0:T(8,128)S(1)} %get-tuple-element.274), channel_id=1, source_target_pairs={{0,16},{8,24},{16,0},{24,8},{1,17},{9,25},{17,1},{25,9},{2,18},{10... | collective-permute-start | bytes 589832 | tf_op jit(solution)/shard_map/ppermute | solution.py:37
  12.5 10.2 %collective-permute-start.4 = (f32[12,2,128]{2,0,1:T(8,128)S(1)}, f32[12,2,128]{2,0,1:T(8,128)S(1)}, u32[]{:S(2)}, u32[]{:S(2)}) collective-permute-start(f32[12,2,128]{2,0,1:T(8,128)S(1)} %pad_maximum_fusion.22), channel_id=1, source_target_pairs={{0,16},{8,24},{16,0},{24,8},{1,17},{9,25},{17,1},{25,9},{2,18},{10... | collective-permute-start | bytes 36872 | tf_op jit(solution)/shard_map/ppermute | solution.py:37
  28.6 7.8 %collective-permute-start.6 = (f32[16,32,128]{2,1,0:T(8,128)S(1)}, f32[16,32,128]{2,1,0:T(8,128)S(1)}, u32[]{:S(2)}, u32[]{:S(2)}) collective-permute-start(f32[16,32,128]{2,1,0:T(8,128)S(1)} %pad_maximum_fusion), channel_id=1, source_target_pairs={{0,4},{4,0},{1,5},{5,1},{2,6},{6,2},{3,7},{7,3},{8,12},{12,8},{9,1... | collective-permute-start | bytes 786440 | tf_op jit(solution)/shard_map/ppermute | solution.py:37
  36.4 13.1 %collective-permute-start.7 = (f32[32,32,128]{2,1,0:T(8,128)S(1)}, f32[32,32,128]{2,1,0:T(8,128)S(1)}, u32[]{:S(2)}, u32[]{:S(2)}) collective-permute-start(f32[32,32,128]{2,1,0:T(8,128)S(1)} %constant_dynamic-update-slice_fusion.refs_0_), channel_id=1, source_target_pairs={{0,2},{2,0},{1,3},{3,1},{4,6},{6,4},{5,7},{7,5},{8,10},{10,8},{9,1... | collective-permute-start | bytes 1572872 | tf_op jit(solution)/shard_map/ppermute | solution.py:37
  37.0 12.5 %collective-permute-start.10 = (f32[32,32,128]{2,1,0:T(8,128)S(1)}, f32[32,32,128]{2,1,0:T(8,128)S(1)}, u32[]{:S(2)}, u32[]{:S(2)}) collective-permute-start(f32[32,32,128]{2,1,0:T(8,128)S(1)} %constant_dynamic-update-slice_fusion.3.refs_1_), channel_id=1, source_target_pairs={{0,4},{4,0},{1,5},{5,1},{2,6},{6,2},{3,7},{7,3},{8,12},{12,8},{9,1... | collective-permute-start | bytes 1572872 | tf_op jit(solution)/shard_map/ppermute | solution.py:37
  39.0 11.5 %collective-permute-start.13 = (f32[32,32,128]{2,1,0:T(8,128)S(1)}, f32[32,32,128]{2,1,0:T(8,128)S(1)}, u32[]{:S(2)}, u32[]{:S(2)}) collective-permute-start(f32[32,32,128]{2,1,0:T(8,128)S(1)} %constant_dynamic-update-slice_fusion.6.refs_2_), channel_id=1, source_target_pairs={{0,8},{8,0},{16,24},{24,16},{1,9},{9,1},{17,25},{25,17},{2,10},{10... | collective-permute-start | bytes 1572872 | tf_op jit(solution)/shard_map/ppermute | solution.py:37
  54.8 11.2 %collective-permute-start.14 = (f32[32,32,128]{2,1,0:T(8,128)S(1)}, f32[32,32,128]{2,1,0:T(8,128)S(1)}, u32[]{:S(2)}, u32[]{:S(2)}) collective-permute-start(f32[32,32,128]{2,1,0:T(8,128)S(1)} %get-tuple-element.114), channel_id=1, source_target_pairs={{0,2},{2,0},{1,3},{3,1},{4,6},{6,4},{5,7},{7,5},{8,10},{10,8},{9,1... | collective-permute-start | bytes 1572872 | tf_op jit(solution)/shard_map/ppermute | solution.py:37
  56.3 12.1 %collective-permute-start.17 = (f32[32,32,128]{2,1,0:T(8,128)S(1)}, f32[32,32,128]{2,1,0:T(8,128)S(1)}, u32[]{:S(2)}, u32[]{:S(2)}) collective-permute-start(f32[32,32,128]{2,1,0:T(8,128)S(1)} %get-tuple-element.123), channel_id=1, source_target_pairs={{0,4},{4,0},{1,5},{5,1},{2,6},{6,2},{3,7},{7,3},{8,12},{12,8},{9,1... | collective-permute-start | bytes 1572872 | tf_op jit(solution)/shard_map/ppermute | solution.py:37
  56.7 14.1 %collective-permute-start.20 = (f32[32,32,128]{2,1,0:T(8,128)S(1)}, f32[32,32,128]{2,1,0:T(8,128)S(1)}, u32[]{:S(2)}, u32[]{:S(2)}) collective-permute-start(f32[32,32,128]{2,1,0:T(8,128)S(1)} %get-tuple-element.132), channel_id=1, source_target_pairs={{0,8},{8,0},{16,24},{24,16},{1,9},{9,1},{17,25},{25,17},{2,10},{10... | collective-permute-start | bytes 1572872 | tf_op jit(solution)/shard_map/ppermute | solution.py:37
  68.4 8.1 %collective-permute-start.18 = (f32[16,32,128]{2,1,0:T(8,128)S(1)}, f32[16,32,128]{2,1,0:T(8,128)S(1)}, u32[]{:S(2)}, u32[]{:S(2)}) collective-permute-start(f32[16,32,128]{2,1,0:T(8,128)S(1)} %slice_add_fusion.7), channel_id=1, source_target_pairs={{0,8},{8,0},{16,24},{24,16},{1,9},{9,1},{17,25},{25,17},{2,10},{10... | collective-permute-start | bytes 786440 | tf_op jit(solution)/shard_map/ppermute | solution.py:37
  70.8 7.5 %collective-permute-start.21 = (f32[16,32,128]{2,1,0:T(8,128)S(1)}, f32[16,32,128]{2,1,0:T(8,128)S(1)}, u32[]{:S(2)}, u32[]{:S(2)}) collective-permute-start(f32[16,32,128]{2,1,0:T(8,128)S(1)} %slice_add_fusion.6), channel_id=1, source_target_pairs={{0,2},{2,0},{1,3},{3,1},{4,6},{6,4},{5,7},{7,5},{8,10},{10,8},{9,1... | collective-permute-start | bytes 786440 | tf_op jit(solution)/shard_map/ppermute | solution.py:37
  83.6 15.1 %collective-permute-start.23 = (f32[24,32,128]{2,1,0:T(8,128)S(1)}, f32[24,32,128]{2,1,0:T(8,128)S(1)}, u32[]{:S(2)}, u32[]{:S(2)}) collective-permute-start(f32[24,32,128]{2,1,0:T(8,128)S(1)} %get-tuple-element.224), channel_id=1, source_target_pairs={{0,16},{8,24},{16,0},{24,8},{1,17},{9,25},{17,1},{25,9},{2,18},{10... | collective-permute-start | bytes 1179656 | tf_op jit(solution)/shard_map/ppermute | solution.py:37
  106.5 9.2 %collective-permute-start.31 = (f32[16,32,128]{2,1,0:T(8,128)S(1)}, f32[16,32,128]{2,1,0:T(8,128)S(1)}, u32[]{:S(2)}, u32[]{:S(2)}) collective-permute-start(f32[16,32,128]{2,1,0:T(8,128)S(1)} %pad_maximum_fusion.5), channel_id=1, source_target_pairs={{0,2},{2,0},{1,3},{3,1},{4,6},{6,4},{5,7},{7,5},{8,10},{10,8},{9,1... | collective-permute-start | bytes 786440 | tf_op jit(solution)/shard_map/ppermute | solution.py:37
  111.0 12.8 %collective-permute-start.26 = (f32[32,32,128]{2,1,0:T(8,128)S(1)}, f32[32,32,128]{2,1,0:T(8,128)S(1)}, u32[]{:S(2)}, u32[]{:S(2)}) collective-permute-start(f32[32,32,128]{2,1,0:T(8,128)S(1)} %constant_dynamic-update-slice_fusion.15.refs_0_), channel_id=1, source_target_pairs={{0,2},{2,0},{1,3},{3,1},{4,6},{6,4},{5,7},{7,5},{8,10},{10,8},{9,1... | collective-permute-start | bytes 1572872 | tf_op jit(solution)/shard_map/ppermute | solution.py:37
  112.5 11.3 %collective-permute-start.29 = (f32[32,32,128]{2,1,0:T(8,128)S(1)}, f32[32,32,128]{2,1,0:T(8,128)S(1)}, u32[]{:S(2)}, u32[]{:S(2)}) collective-permute-start(f32[32,32,128]{2,1,0:T(8,128)S(1)} %constant_dynamic-update-slice_fusion.18.refs_1_), channel_id=1, source_target_pairs={{0,4},{4,0},{1,5},{5,1},{2,6},{6,2},{3,7},{7,3},{8,12},{12,8},{9,1... | collective-permute-start | bytes 1572872 | tf_op jit(solution)/shard_map/ppermute | solution.py:37
  115.7 9.2 %collective-permute-start.32 = (f32[32,32,128]{2,1,0:T(8,128)S(1)}, f32[32,32,128]{2,1,0:T(8,128)S(1)}, u32[]{:S(2)}, u32[]{:S(2)}) collective-permute-start(f32[32,32,128]{2,1,0:T(8,128)S(1)} %constant_dynamic-update-slice_fusion.21.refs_2_), channel_id=1, source_target_pairs={{0,8},{8,0},{16,24},{24,16},{1,9},{9,1},{17,25},{25,17},{2,10},{10... | collective-permute-start | bytes 1572872 | tf_op jit(solution)/shard_map/ppermute | solution.py:37
  129.3 11.5 %collective-permute-start.33 = (f32[32,32,128]{2,1,0:T(8,128)S(1)}, f32[32,32,128]{2,1,0:T(8,128)S(1)}, u32[]{:S(2)}, u32[]{:S(2)}) collective-permute-start(f32[32,32,128]{2,1,0:T(8,128)S(1)} %get-tuple-element.146), channel_id=1, source_target_pairs={{0,2},{2,0},{1,3},{3,1},{4,6},{6,4},{5,7},{7,5},{8,10},{10,8},{9,1... | collective-permute-start | bytes 1572872 | tf_op jit(solution)/shard_map/ppermute | solution.py:37
  129.9 11.6 %collective-permute-start.36 = (f32[32,32,128]{2,1,0:T(8,128)S(1)}, f32[32,32,128]{2,1,0:T(8,128)S(1)}, u32[]{:S(2)}, u32[]{:S(2)}) collective-permute-start(f32[32,32,128]{2,1,0:T(8,128)S(1)} %get-tuple-element.155), channel_id=1, source_target_pairs={{0,4},{4,0},{1,5},{5,1},{2,6},{6,2},{3,7},{7,3},{8,12},{12,8},{9,1... | collective-permute-start | bytes 1572872 | tf_op jit(solution)/shard_map/ppermute | solution.py:37
  130.9 12.2 %collective-permute-start.39 = (f32[32,32,128]{2,1,0:T(8,128)S(1)}, f32[32,32,128]{2,1,0:T(8,128)S(1)}, u32[]{:S(2)}, u32[]{:S(2)}) collective-permute-start(f32[32,32,128]{2,1,0:T(8,128)S(1)} %get-tuple-element.164), channel_id=1, source_target_pairs={{0,8},{8,0},{16,24},{24,16},{1,9},{9,1},{17,25},{25,17},{2,10},{10... | collective-permute-start | bytes 1572872 | tf_op jit(solution)/shard_map/ppermute | solution.py:37
  155.4 14.0 %collective-permute-start.42 = (f32[24,32,128]{2,1,0:T(8,128)S(1)}, f32[24,32,128]{2,1,0:T(8,128)S(1)}, u32[]{:S(2)}, u32[]{:S(2)}) collective-permute-start(f32[24,32,128]{2,1,0:T(8,128)S(1)} %get-tuple-element.212), channel_id=1, source_target_pairs={{0,16},{8,24},{16,0},{24,8},{1,17},{9,25},{17,1},{25,9},{2,18},{10... | collective-permute-start | bytes 1179656 | tf_op jit(solution)/shard_map/ppermute | solution.py:37
  176.0 8.7 %collective-permute-start.44 = (f32[16,32,128]{2,1,0:T(8,128)S(1)}, f32[16,32,128]{2,1,0:T(8,128)S(1)}, u32[]{:S(2)}, u32[]{:S(2)}) collective-permute-start(f32[16,32,128]{2,1,0:T(8,128)S(1)} %pad_maximum_fusion.6), channel_id=1, source_target_pairs={{0,4},{4,0},{1,5},{5,1},{2,6},{6,2},{3,7},{7,3},{8,12},{12,8},{9,1... | collective-permute-start | bytes 786440 | tf_op jit(solution)/shard_map/ppermute | solution.py:37
  176.1 8.7 %collective-permute-start.47 = (f32[16,32,128]{2,1,0:T(8,128)S(1)}, f32[16,32,128]{2,1,0:T(8,128)S(1)}, u32[]{:S(2)}, u32[]{:S(2)}) collective-permute-start(f32[16,32,128]{2,1,0:T(8,128)S(1)} %pad_maximum_fusion.7), channel_id=1, source_target_pairs={{0,8},{8,0},{16,24},{24,16},{1,9},{9,1},{17,25},{25,17},{2,10},{10... | collective-permute-start | bytes 786440 | tf_op jit(solution)/shard_map/ppermute | solution.py:37
  178.3 9.3 %collective-permute-start.50 = (f32[16,32,128]{2,1,0:T(8,128)S(1)}, f32[16,32,128]{2,1,0:T(8,128)S(1)}, u32[]{:S(2)}, u32[]{:S(2)}) collective-permute-start(f32[16,32,128]{2,1,0:T(8,128)S(1)} %pad_maximum_fusion.8), channel_id=1, source_target_pairs={{0,2},{2,0},{1,3},{3,1},{4,6},{6,4},{5,7},{7,5},{8,10},{10,8},{9,1... | collective-permute-start | bytes 786440 | tf_op jit(solution)/shard_map/ppermute | solution.py:37
  184.7 9.2 %collective-permute-start.45 = (f32[32,32,128]{2,1,0:T(8,128)S(1)}, f32[32,32,128]{2,1,0:T(8,128)S(1)}, u32[]{:S(2)}, u32[]{:S(2)}) collective-permute-start(f32[32,32,128]{2,1,0:T(8,128)S(1)} %constant_dynamic-update-slice_fusion.30.refs_0_), channel_id=1, source_target_pairs={{0,2},{2,0},{1,3},{3,1},{4,6},{6,4},{5,7},{7,5},{8,10},{10,8},{9,1... | collective-permute-start | bytes 1572872 | tf_op jit(solution)/shard_map/ppermute | solution.py:37
  184.8 9.5 %collective-permute-start.48 = (f32[32,32,128]{2,1,0:T(8,128)S(1)}, f32[32,32,128]{2,1,0:T(8,128)S(1)}, u32[]{:S(2)}, u32[]{:S(2)}) collective-permute-start(f32[32,32,128]{2,1,0:T(8,128)S(1)} %constant_dynamic-update-slice_fusion.33.refs_1_), channel_id=1, source_target_pairs={{0,4},{4,0},{1,5},{5,1},{2,6},{6,2},{3,7},{7,3},{8,12},{12,8},{9,1... | collective-permute-start | bytes 1572872 | tf_op jit(solution)/shard_map/ppermute | solution.py:37
  187.6 10.1 %collective-permute-start.51 = (f32[32,32,128]{2,1,0:T(8,128)S(1)}, f32[32,32,128]{2,1,0:T(8,128)S(1)}, u32[]{:S(2)}, u32[]{:S(2)}) collective-permute-start(f32[32,32,128]{2,1,0:T(8,128)S(1)} %constant_dynamic-update-slice_fusion.36.refs_2_), channel_id=1, source_target_pairs={{0,8},{8,0},{16,24},{24,16},{1,9},{9,1},{17,25},{25,17},{2,10},{10... | collective-permute-start | bytes 1572872 | tf_op jit(solution)/shard_map/ppermute | solution.py:37
  202.0 12.0 %collective-permute-start.58 = (f32[32,32,128]{2,1,0:T(8,128)S(1)}, f32[32,32,128]{2,1,0:T(8,128)S(1)}, u32[]{:S(2)}, u32[]{:S(2)}) collective-permute-start(f32[32,32,128]{2,1,0:T(8,128)S(1)} %get-tuple-element.196), channel_id=1, source_target_pairs={{0,8},{8,0},{16,24},{24,16},{1,9},{9,1},{17,25},{25,17},{2,10},{10... | collective-permute-start | bytes 1572872 | tf_op jit(solution)/shard_map/ppermute | solution.py:37
  202.1 13.5 %collective-permute-start.55 = (f32[32,32,128]{2,1,0:T(8,128)S(1)}, f32[32,32,128]{2,1,0:T(8,128)S(1)}, u32[]{:S(2)}, u32[]{:S(2)}) collective-permute-start(f32[32,32,128]{2,1,0:T(8,128)S(1)} %get-tuple-element.187), channel_id=1, source_target_pairs={{0,4},{4,0},{1,5},{5,1},{2,6},{6,2},{3,7},{7,3},{8,12},{12,8},{9,1... | collective-permute-start | bytes 1572872 | tf_op jit(solution)/shard_map/ppermute | solution.py:37
  204.1 13.3 %collective-permute-start.52 = (f32[32,32,128]{2,1,0:T(8,128)S(1)}, f32[32,32,128]{2,1,0:T(8,128)S(1)}, u32[]{:S(2)}, u32[]{:S(2)}) collective-permute-start(f32[32,32,128]{2,1,0:T(8,128)S(1)} %get-tuple-element.178), channel_id=1, source_target_pairs={{0,2},{2,0},{1,3},{3,1},{4,6},{6,4},{5,7},{7,5},{8,10},{10,8},{9,1... | collective-permute-start | bytes 1572872 | tf_op jit(solution)/shard_map/ppermute | solution.py:37
  234.3 10.9 %all-to-all-start = ((f32[32,1,128]{2,1,0:T(1,128)}), f32[32,1,128]{2,1,0:T(1,128)S(1)}, u32[]{:S(2)}, u32[]{:S(2)}) async-start(f32[32,1,128]{2,1,0:T(1,128)} %broadcast_in_dim.60), calls=%async_computation | async-start | bytes 32768 | tf_op jit(solution)/shard_map/all_to_all | solution.py:308
  238.0 12.5 %collective-permute-start.61 = (f32[12,32,128]{2,1,0:T(8,128)S(1)}, f32[12,32,128]{2,1,0:T(8,128)S(1)}, u32[]{:S(2)}, u32[]{:S(2)}) collective-permute-start(f32[12,32,128]{2,1,0:T(8,128)S(1)} %get-tuple-element.205), channel_id=1, source_target_pairs={{0,16},{8,24},{16,0},{24,8},{1,17},{9,25},{17,1},{25,9},{2,18},{10... | collective-permute-start | bytes 589832 | tf_op jit(solution)/shard_map/ppermute | solution.py:37
  (53 other events, 342.5 us)

commit v19 on v18

--- a/solution.py
+++ b/solution.py
@@ -271,20 +271,23 @@
     drive = jnp.transpose(driving.reshape(per, size, columns), (0, 2, 1))
     relax = relaxation.reshape(per, 1, size)
     heat = heat_weight.reshape(per, 1, size)
+    drive = jnp.concatenate(gather_far(drive), axis=0)
+    small = jnp.concatenate(gather_far(jnp.concatenate([relax, relax * heat], axis=1)), axis=0)
     low, high = drive[:, :half], drive[:, half:]
     mine = jnp.where(core == 0, low, high)
     theirs = jnp.where(core == 0, high, low)
-    packed = [theirs, jnp.broadcast_to(relax, (per, 8, size)), jnp.broadcast_to(heat, (per, 8, size))]
+    packed = [theirs] + [jnp.broadcast_to(small[:, k : k + 1], (len(small), 8, size)) for k in range(2)]
     got = swap(jnp.concatenate(packed, axis=1), cores)
-    tile_values = after(tile_values, got, other_code)
+    far = 1 << len(far_steps())
+    drives, relaxes, heats = [
+        [by_core(o, t) for o, t in zip(jnp.split(own, far), jnp.split(other, far))]
+        for own, other in (
+            (mine, got[:, :half]),
+            (small[:, :1], got[:, half : half + 1]),
+            (small[:, 1:], got[:, half + 8 : half + 9]),
+        )
+    ]
     other_values = swap(tile_values, cores)
-    drive_half = by_core(mine, got[:, :half])
-    relax_both = by_core(relax, got[:, half : half + 1])
-    heat_both = by_core(heat, got[:, half + 8 : half + 9])
-
-    drives = gather_far(drive_half)
-    small = gather_far(jnp.concatenate([relax_both, heat_both * relax_both], axis=1))
-    relaxes, heats = [s[:, :1] for s in small], [s[:, 1:] for s in small]
     drives[-1], other_values = lax.optimization_barrier((drives[-1], other_values))
     fluxes = [r * d for r, d in zip(relaxes, drives)]
     tiles = (tile_values, other_values)
@@ -300,17 +303,15 @@
             fluxes = [r * (d + s) for r, d, s in zip(relaxes, drives, sum_far(blocks))]
     weighted = sum(
         [jnp.sum(w * b, axis=(0, 2)) for w, b in zip(heats, blocks)],
-        jnp.sum(heats[0] * drive_half, axis=(0, 2)),
+        jnp.sum(heats[0] * drives[0], axis=(0, 2)),
     )
-    totals = jnp.concatenate([weighted, jnp.sum(heat).reshape(1)])
-    totals = jnp.pad(totals[None], ((0, 0), (0, size - half - 1)))
-    *blocks, totals = lax.optimization_barrier((*blocks, totals))
-    totals = lax.all_to_all(
-        jnp.broadcast_to(totals, (chips * CORES, size)), ALL, split_axis=0, concat_axis=0, tiled=True
-    )
-    totals = jnp.sum(totals.reshape(chips, CORES, size), axis=0)
-    conductivity = totals[:, :half].reshape(columns) / jnp.sum(totals[:, half])
-    flux = relax_both * (drive_half + after(reduce_far(blocks), conductivity))
+    totals = jnp.pad(jnp.stack([weighted, jnp.full((half,), jnp.sum(heat))]), ((0, 0), (0, size - half)))
+    both = by_core(totals[None], swap(totals[None], cores))
+    both = jnp.broadcast_to(both.reshape(1, 2 * CORES, size), (chips, 2 * CORES, size))
+    both = lax.all_to_all(both, CHIPS, split_axis=0, concat_axis=0, tiled=True)
+    both = jnp.sum(both, axis=0).reshape(CORES, 2, size)[:, :, :half]
+    conductivity = both[:, 0].reshape(columns) / jnp.sum(both[:, 1, 0])
+    flux = relaxes[0] * (drives[0] + after(reduce_far(blocks), conductivity))
     first, second = flux[:per], flux[per:]
     mine = jnp.where(core == 0, first, second)
     got = swap(jnp.where(core == 0, second, first), cores)

time: 253 us -> 256 us (1.012)
  starting transfers between devices: 75.6 us -> 60.2 us
  waiting for transfers between devices: 113 us -> 127 us
  blocking collectives: 0 us -> 10.9 us
  other arithmetic: 12 us -> 6.62 us
  local copies, waits for them, and re-layouts: 5.47 us -> 2.84 us
    ppermute x63 -> x64, waiting for transfers between devices: 109 us -> 127 us  [swap(): lax.ppermute(array, axis, [(i, i ^ distance) for i in range(lax.axis_size...]
    ppermute x63 -> x64, starting transfers between devices: 71.9 us -> 60.2 us  [swap(): lax.ppermute(array, axis, [(i, i ^ distance) for i in range(lax.axis_size...]
    all_to_all x0 -> x1, blocking collectives: none -> 10.9 us  [shards(): both = lax.all_to_all(both, CHIPS, split_axis=0, concat_axis=0, tiled=True)]
    all_to_all x1 -> x0, waiting for transfers between devices: 4.41 us -> none  [shards(): lax.all_to_all(jnp.broadcast_to(totals, (chips * CORES, size)), ALL, spli...]
    all_to_all x1 -> x0, starting transfers between devices: 3.72 us -> none  [shards(): lax.all_to_all(jnp.broadcast_to(totals, (chips * CORES, size)), ALL, spli...]
  transfers between devices with their start and end apart: 64 -> 64, of which waited for: 43 -> 50; matrix products, arithmetic and copies ran while one was open for 4% -> 2% of each run, Pallas kernels for 12% -> 12%
where the time goes in v19:
time: 256 us; the launch traced here: 255 us
  waiting for transfers between devices  127 us (50%)
  starting transfers between devices  60.2 us (24%)
  Pallas kernels  44.8 us (18%)
  blocking collectives  10.9 us (4%)
  other arithmetic  6.62 us (3%)
  local copies, waits for them, and re-layouts  2.84 us (1%)
    ppermute x64, waiting for transfers between devices, swap(): lax.ppermute(array, axis, [(i, i ^ distance) for i in range(lax.axis_size...  127 us
    ppermute x64, starting transfers between devices, swap(): lax.ppermute(array, axis, [(i, i ^ distance) for i in range(lax.axis_size...  60.2 us
    pallas_call x9, Pallas kernels, apply_tiles(): pl.pallas_call(functools.partial(apply_kernel, span, skip, len(flux), bas...  44.8 us
    all_to_all x1, blocking collectives, shards(): both = lax.all_to_all(both, CHIPS, split_axis=0, concat_axis=0, tiled=True)  10.9 us
  transfers between devices with their start and end apart: 64, of which 50 were waited for; matrix products, arithmetic and copies ran while one was open for 2% of the time, Pallas kernels for 12%

profile of v19, /device:TPU:0, one launch (start us, length us, event | category | flops | bytes accessed | tf_op | source)
XLA Modules:
  0.0 254.9 jit_solution(13350712413414462914)
XLA Ops:
  2.6 3.7 %collective-permute-start.1 = (f32[6,2,128]{2,1,0:T(2,128)S(1)}, f32[6,2,128]{2,1,0:T(2,128)S(1)}, u32[]{:S(2)}, u32[]{:S(2)}) collective-permute-start(f32[6,2,128]{2,1,0:T(2,128)S(1)} %pad_maximum_fusion.25), channel_id=1, source_target_pairs={{0,16},{8,24},{16,0},{24,8},{1,17},{9,25},{17,1},{25,9},{2,18},{10... | collective-permute-start | bytes 18440 | tf_op jit(solution)/shard_map/ppermute | solution.py:37
  7.9 10.5 %collective-permute-done = f32[6,64,128]{2,1,0:T(8,128)S(1)} collective-permute-done((f32[6,64,128]{2,1,0:T(8,128)S(1)}, f32[6,64,128]{2,1,0:T(8,128)S(1)}, u32[]{:S(2)}, u32[]{:S(2)}) %collective-permute-start) | collective-permute-done | bytes 196640 | tf_op jit(solution)/shard_map/ppermute | solution.py:37
  24.0 2.4 collective-permute-done.11
  29.8 4.3 %collective-permute-done.12 = f32[16,32,128]{2,1,0:T(8,128)S(1)} collective-permute-done((f32[16,32,128]{2,1,0:T(8,128)S(1)}, f32[16,32,128]{2,1,0:T(8,128)S(1)}, u32[]{:S(2)}, u32[]{:S(2)}) %collective-permute-start.12) | collective-permute-done | bytes 262176 | tf_op jit(solution)/shard_map/ppermute | solution.py:37
  38.0 5.5 %shard_map.95 = (f32[96,32,128]{2,1,0:T(8,128)S(1)}, f32[96,32,128]{2,1,0:T(8,128)S(1)}) custom-call(s32[772]{0:T(1024)S(1)} %pad_add_fusion.places_ref, f32[128,128,128]{2,1,0:T(8,128)} %own_ref.17, f32[128,128,128]{2,1,0:T(8,128)} %collective-permute-done.4.other_ref, f32[32,32,128]{2,1,0:T(8,128)S(1)} %constant_dynamic-update-slice_fusion.refs_0_, ...), custom_call_target="tpu_custom_call" | custom-call | flops 536870912 | bytes 14680064 | tf_op jit(solution)/shard_map/pallas_call | solution.py:188
  43.5 3.1 %collective-permute-done.13.refs_2_ = f32[32,32,128]{2,1,0:T(8,128)S(1)} collective-permute-done((f32[32,32,128]{2,1,0:T(8,128)S(1)}, f32[32,32,128]{2,1,0:T(8,128)S(1)}, u32[]{:S(2)}, u32[]{:S(2)}) %collective-permute-start.13) | collective-permute-done | bytes 524320 | tf_op jit(solution)/shard_map/ppermute | solution.py:37
  48.8 4.3 %shard_map.97 = (f32[32,32,128]{2,1,0:T(8,128)S(1)}, f32[32,32,128]{2,1,0:T(8,128)S(1)}, f32[32,32,128]{2,1,0:T(8,128)S(1)}) custom-call(s32[772]{0:T(1024)S(1)} %pad_add_fusion.places_ref, f32[128,128,128]{2,1,0:T(8,128)} %own_ref.17, f32[128,128,128]{2,1,0:T(8,128)} %collective-permute-done.4.other_ref, f32[32,32,128]{2,1,0:T(8,128)S(1)} %collective-permute-done.7.refs_0_, ...), custom_call_target="tpu_custom_call" | custom-call | flops 268435456 | bytes 7340032 | tf_op jit(solution)/shard_map/pallas_call | solution.py:188
  55.7 5.0 %shard_map.96 = (f32[32,32,128]{2,1,0:T(8,128)S(1)}, f32[32,32,128]{2,1,0:T(8,128)S(1)}, f32[32,32,128]{2,1,0:T(8,128)S(1)}) custom-call(s32[772]{0:T(1024)S(1)} %pad_add_fusion.places_ref, f32[128,128,128]{2,1,0:T(8,128)} %own_ref.17, f32[128,128,128]{2,1,0:T(8,128)} %collective-permute-done.4.other_ref, f32[32,32,128]{2,1,0:T(8,128)S(1)} %collective-permute-done.7.refs_0_, ...), custom_call_target="tpu_custom_call" | custom-call | flops 268435456 | bytes 7340032 | tf_op jit(solution)/shard_map/pallas_call | solution.py:188
  60.8 3.6 %collective-permute-done.20 = f32[32,32,128]{2,1,0:T(8,128)S(1)} collective-permute-done((f32[32,32,128]{2,1,0:T(8,128)S(1)}, f32[32,32,128]{2,1,0:T(8,128)S(1)}, u32[]{:S(2)}, u32[]{:S(2)}) %collective-permute-start.20) | collective-permute-done | bytes 524320 | tf_op jit(solution)/shard_map/ppermute | solution.py:37
  67.2 2.4 collective-permute-start.15
  80.0 2.7 %collective-permute-start.23 = (f32[24,32,128]{2,1,0:T(8,128)S(1)}, f32[24,32,128]{2,1,0:T(8,128)S(1)}, u32[]{:S(2)}, u32[]{:S(2)}) collective-permute-start(f32[24,32,128]{2,1,0:T(8,128)S(1)} %get-tuple-element.216), channel_id=1, source_target_pairs={{0,16},{8,24},{16,0},{24,8},{1,17},{9,25},{17,1},{25,9},{2,18},{10... | collective-permute-start | bytes 1179656 | tf_op jit(solution)/shard_map/ppermute | solution.py:37
  82.7 11.5 %collective-permute-done.23 = f32[24,32,128]{2,1,0:T(8,128)S(1)} collective-permute-done((f32[24,32,128]{2,1,0:T(8,128)S(1)}, f32[24,32,128]{2,1,0:T(8,128)S(1)}, u32[]{:S(2)}, u32[]{:S(2)}) %collective-permute-start.23) | collective-permute-done | bytes 393248 | tf_op jit(solution)/shard_map/ppermute | solution.py:37
  96.9 3.0 %collective-permute-done.30 = f32[8,32,128]{2,1,0:T(8,128)S(1)} collective-permute-done((f32[8,32,128]{2,1,0:T(8,128)S(1)}, f32[8,32,128]{2,1,0:T(8,128)S(1)}, u32[]{:S(2)}, u32[]{:S(2)}) %collective-permute-start.30) | collective-permute-done | bytes 131104 | tf_op jit(solution)/shard_map/ppermute | solution.py:37
  104.3 3.0 %collective-permute-done.31 = f32[16,32,128]{2,1,0:T(8,128)S(1)} collective-permute-done((f32[16,32,128]{2,1,0:T(8,128)S(1)}, f32[16,32,128]{2,1,0:T(8,128)S(1)}, u32[]{:S(2)}, u32[]{:S(2)}) %collective-permute-start.31) | collective-permute-done | bytes 262176 | tf_op jit(solution)/shard_map/ppermute | solution.py:37
  107.4 4.0 %collective-permute-done.28 = f32[16,32,128]{2,1,0:T(8,128)S(1)} collective-permute-done((f32[16,32,128]{2,1,0:T(8,128)S(1)}, f32[16,32,128]{2,1,0:T(8,128)S(1)}, u32[]{:S(2)}, u32[]{:S(2)}) %collective-permute-start.28) | collective-permute-done | bytes 262176 | tf_op jit(solution)/shard_map/ppermute | solution.py:37
  113.4 5.5 %shard_map.98 = (f32[96,32,128]{2,1,0:T(8,128)S(1)}, f32[96,32,128]{2,1,0:T(8,128)S(1)}) custom-call(s32[772]{0:T(1024)S(1)} %pad_add_fusion.places_ref, f32[128,128,128]{2,1,0:T(8,128)} %own_ref.17, f32[128,128,128]{2,1,0:T(8,128)} %collective-permute-done.4.other_ref, f32[32,32,128]{2,1,0:T(8,128)S(1)} %constant_dynamic-update-slice_fusion.15.refs_0_, ...), custom_call_target="tpu_custom_call" | custom-call | flops 536870912 | bytes 14680064 | tf_op jit(solution)/shard_map/pallas_call | solution.py:188
  121.4 4.3 %shard_map.100 = (f32[32,32,128]{2,1,0:T(8,128)S(1)}, f32[32,32,128]{2,1,0:T(8,128)S(1)}, f32[32,32,128]{2,1,0:T(8,128)S(1)}) custom-call(s32[772]{0:T(1024)S(1)} %pad_add_fusion.places_ref, f32[128,128,128]{2,1,0:T(8,128)} %own_ref.17, f32[128,128,128]{2,1,0:T(8,128)} %collective-permute-done.4.other_ref, ...), custom_call_target="tpu_custom_call" | custom-call | flops 268435456 | bytes 7340032 | tf_op jit(solution)/shard_map/pallas_call | solution.py:188
  128.5 5.2 %shard_map.99 = (f32[32,32,128]{2,1,0:T(8,128)S(1)}, f32[32,32,128]{2,1,0:T(8,128)S(1)}, f32[32,32,128]{2,1,0:T(8,128)S(1)}) custom-call(s32[772]{0:T(1024)S(1)} %pad_add_fusion.places_ref, f32[128,128,128]{2,1,0:T(8,128)} %own_ref.17, f32[128,128,128]{2,1,0:T(8,128)} %collective-permute-done.4.other_ref, ...), custom_call_target="tpu_custom_call" | custom-call | flops 268435456 | bytes 7340032 | tf_op jit(solution)/shard_map/pallas_call | solution.py:188
  133.8 4.1 %collective-permute-done.39 = f32[32,32,128]{2,1,0:T(8,128)S(1)} collective-permute-done((f32[32,32,128]{2,1,0:T(8,128)S(1)}, f32[32,32,128]{2,1,0:T(8,128)S(1)}, u32[]{:S(2)}, u32[]{:S(2)}) %collective-permute-start.39) | collective-permute-done | bytes 524320 | tf_op jit(solution)/shard_map/ppermute | solution.py:37
  151.2 4.5 %collective-permute-done.35 = f32[8,32,128]{2,1,0:T(8,128)S(1)} collective-permute-done((f32[8,32,128]{2,1,0:T(8,128)S(1)}, f32[8,32,128]{2,1,0:T(8,128)S(1)}, u32[]{:S(2)}, u32[]{:S(2)}) %collective-permute-start.35) | collective-permute-done | bytes 131104 | tf_op jit(solution)/shard_map/ppermute | solution.py:37
  155.9 12.0 %collective-permute-done.42 = f32[24,32,128]{2,1,0:T(8,128)S(1)} collective-permute-done((f32[24,32,128]{2,1,0:T(8,128)S(1)}, f32[24,32,128]{2,1,0:T(8,128)S(1)}, u32[]{:S(2)}, u32[]{:S(2)}) %collective-permute-start.42) | collective-permute-done | bytes 393248 | tf_op jit(solution)/shard_map/ppermute | solution.py:37
  168.2 2.5 collective-permute-start.49
  170.8 4.1 %collective-permute-done.49 = f32[8,32,128]{2,1,0:T(8,128)S(1)} collective-permute-done((f32[8,32,128]{2,1,0:T(8,128)S(1)}, f32[8,32,128]{2,1,0:T(8,128)S(1)}, u32[]{:S(2)}, u32[]{:S(2)}) %collective-permute-start.49) | collective-permute-done | bytes 131104 | tf_op jit(solution)/shard_map/ppermute | solution.py:37
  177.5 5.2 %collective-permute-done.50 = f32[16,32,128]{2,1,0:T(8,128)S(1)} collective-permute-done((f32[16,32,128]{2,1,0:T(8,128)S(1)}, f32[16,32,128]{2,1,0:T(8,128)S(1)}, u32[]{:S(2)}, u32[]{:S(2)}) %collective-permute-start.50) | collective-permute-done | bytes 262176 | tf_op jit(solution)/shard_map/ppermute | solution.py:37
  185.8 5.5 %shard_map.101 = (f32[96,32,128]{2,1,0:T(8,128)S(1)}, f32[96,32,128]{2,1,0:T(8,128)S(1)}) custom-call(s32[772]{0:T(1024)S(1)} %pad_add_fusion.places_ref, f32[128,128,128]{2,1,0:T(8,128)} %own_ref.17, f32[128,128,128]{2,1,0:T(8,128)} %collective-permute-done.4.other_ref, f32[32,32,128]{2,1,0:T(8,128)S(1)} %constant_dynamic-update-slice_fusion.30.refs_0_, ...), custom_call_target="tpu_custom_call" | custom-call | flops 536870912 | bytes 14680064 | tf_op jit(solution)/shard_map/pallas_call | solution.py:188
  191.3 4.1 %collective-permute-done.51.refs_2_ = f32[32,32,128]{2,1,0:T(8,128)S(1)} collective-permute-done((f32[32,32,128]{2,1,0:T(8,128)S(1)}, f32[32,32,128]{2,1,0:T(8,128)S(1)}, u32[]{:S(2)}, u32[]{:S(2)}) %collective-permute-start.51) | collective-permute-done | bytes 524320 | tf_op jit(solution)/shard_map/ppermute | solution.py:37
  198.1 4.3 %shard_map.103 = (f32[32,32,128]{2,1,0:T(8,128)S(1)}, f32[32,32,128]{2,1,0:T(8,128)S(1)}, f32[32,32,128]{2,1,0:T(8,128)S(1)}) custom-call(s32[772]{0:T(1024)S(1)} %pad_add_fusion.places_ref, f32[128,128,128]{2,1,0:T(8,128)} %own_ref.17, f32[128,128,128]{2,1,0:T(8,128)} %collective-permute-done.4.other_ref, ...), custom_call_target="tpu_custom_call" | custom-call | flops 268435456 | bytes 7340032 | tf_op jit(solution)/shard_map/pallas_call | solution.py:188
  205.4 5.0 %shard_map.102 = (f32[32,32,128]{2,1,0:T(8,128)S(1)}, f32[32,32,128]{2,1,0:T(8,128)S(1)}, f32[32,32,128]{2,1,0:T(8,128)S(1)}) custom-call(s32[772]{0:T(1024)S(1)} %pad_add_fusion.places_ref, f32[128,128,128]{2,1,0:T(8,128)} %own_ref.17, f32[128,128,128]{2,1,0:T(8,128)} %collective-permute-done.4.other_ref, ...), custom_call_target="tpu_custom_call" | custom-call | flops 268435456 | bytes 7340032 | tf_op jit(solution)/shard_map/pallas_call | solution.py:188
  210.4 2.7 %collective-permute-done.52 = f32[32,32,128]{2,1,0:T(8,128)S(1)} collective-permute-done((f32[32,32,128]{2,1,0:T(8,128)S(1)}, f32[32,32,128]{2,1,0:T(8,128)S(1)}, u32[]{:S(2)}, u32[]{:S(2)}) %collective-permute-start.52) | collective-permute-done | bytes 524320 | tf_op jit(solution)/shard_map/ppermute | solution.py:37
  219.6 2.4 collective-permute-start.54
  229.3 8.0 %collective-permute-done.61 = f32[12,32,128]{2,1,0:T(8,128)S(1)} collective-permute-done((f32[12,32,128]{2,1,0:T(8,128)S(1)}, f32[12,32,128]{2,1,0:T(8,128)S(1)}, u32[]{:S(2)}, u32[]{:S(2)}) %collective-permute-start.61) | collective-permute-done | bytes 196640 | tf_op jit(solution)/shard_map/ppermute | solution.py:37
  240.0 10.9 %all_to_all.5 = f32[16,4,128]{2,1,0:T(4,128)S(1)} all-to-all(f32[16,4,128]{2,1,0:T(4,128)S(1)} %broadcast_in_dim.64), channel_id=1, replica_groups=mesh['z'=4,'y'=2,'x'=2,'core'=2] {'z','y','x'}, dimensions={0} | all-to-all | bytes 65536 | tf_op jit(solution)/shard_map/all_to_all | solution.py:311
  (276 shorter events, 93.1 us)
Async XLA Ops:
  0.7 20.0 %collective-permute-start.4 = (f32[128,128,128]{2,1,0:T(8,128)}, f32[128,128,128]{2,1,0:T(8,128)}, u32[]{:S(2)}, u32[]{:S(2)}) collective-permute-start(f32[128,128,128]{2,1,0:T(8,128)} %own_ref.17), channel_id=1, source_target_pairs={{0,1},{1,0},{2,3},{3,2},{4,5},{5,4},{6,7},{7,6},{8,9},{9,8},{10,11... | collective-permute-start | bytes 25165832 | tf_op jit(solution)/shard_map/ppermute | solution.py:37
  6.3 12.2 %collective-permute-start = (f32[6,64,128]{2,1,0:T(8,128)S(1)}, f32[6,64,128]{2,1,0:T(8,128)S(1)}, u32[]{:S(2)}, u32[]{:S(2)}) collective-permute-start(f32[6,64,128]{2,1,0:T(8,128)S(1)} %bitcast_bitcast_fusion), channel_id=1, source_target_pairs={{0,16},{8,24},{16,0},{24,8},{1,17},{9,25},{17,1},{25,9},{2,18},{10... | collective-permute-start | bytes 589832 | tf_op jit(solution)/shard_map/ppermute | solution.py:37
  26.5 7.7 %collective-permute-start.12 = (f32[16,32,128]{2,1,0:T(8,128)S(1)}, f32[16,32,128]{2,1,0:T(8,128)S(1)}, u32[]{:S(2)}, u32[]{:S(2)}) collective-permute-start(f32[16,32,128]{2,1,0:T(8,128)S(1)} %pad_maximum_fusion.3), channel_id=1, source_target_pairs={{0,2},{2,0},{1,3},{3,1},{4,6},{6,4},{5,7},{7,5},{8,10},{10,8},{9,1... | collective-permute-start | bytes 786440 | tf_op jit(solution)/shard_map/ppermute | solution.py:37
  28.0 7.5 %collective-permute-start.9 = (f32[16,32,128]{2,1,0:T(8,128)S(1)}, f32[16,32,128]{2,1,0:T(8,128)S(1)}, u32[]{:S(2)}, u32[]{:S(2)}) collective-permute-start(f32[16,32,128]{2,1,0:T(8,128)S(1)} %pad_maximum_fusion.2), channel_id=1, source_target_pairs={{0,8},{8,0},{16,24},{24,16},{1,9},{9,1},{17,25},{25,17},{2,10},{10... | collective-permute-start | bytes 786440 | tf_op jit(solution)/shard_map/ppermute | solution.py:37
  29.1 8.1 %collective-permute-start.6 = (f32[16,32,128]{2,1,0:T(8,128)S(1)}, f32[16,32,128]{2,1,0:T(8,128)S(1)}, u32[]{:S(2)}, u32[]{:S(2)}) collective-permute-start(f32[16,32,128]{2,1,0:T(8,128)S(1)} %pad_maximum_fusion.1), channel_id=1, source_target_pairs={{0,4},{4,0},{1,5},{5,1},{2,6},{6,2},{3,7},{7,3},{8,12},{12,8},{9,1... | collective-permute-start | bytes 786440 | tf_op jit(solution)/shard_map/ppermute | solution.py:37
  34.1 12.5 %collective-permute-start.13 = (f32[32,32,128]{2,1,0:T(8,128)S(1)}, f32[32,32,128]{2,1,0:T(8,128)S(1)}, u32[]{:S(2)}, u32[]{:S(2)}) collective-permute-start(f32[32,32,128]{2,1,0:T(8,128)S(1)} %constant_dynamic-update-slice_fusion.6.refs_2_), channel_id=1, source_target_pairs={{0,8},{8,0},{16,24},{24,16},{1,9},{9,1},{17,25},{25,17},{2,10},{10... | collective-permute-start | bytes 1572872 | tf_op jit(solution)/shard_map/ppermute | solution.py:37
  35.5 12.0 %collective-permute-start.10 = (f32[32,32,128]{2,1,0:T(8,128)S(1)}, f32[32,32,128]{2,1,0:T(8,128)S(1)}, u32[]{:S(2)}, u32[]{:S(2)}) collective-permute-start(f32[32,32,128]{2,1,0:T(8,128)S(1)} %constant_dynamic-update-slice_fusion.3.refs_1_), channel_id=1, source_target_pairs={{0,4},{4,0},{1,5},{5,1},{2,6},{6,2},{3,7},{7,3},{8,12},{12,8},{9,1... | collective-permute-start | bytes 1572872 | tf_op jit(solution)/shard_map/ppermute | solution.py:37
  37.1 11.7 %collective-permute-start.7 = (f32[32,32,128]{2,1,0:T(8,128)S(1)}, f32[32,32,128]{2,1,0:T(8,128)S(1)}, u32[]{:S(2)}, u32[]{:S(2)}) collective-permute-start(f32[32,32,128]{2,1,0:T(8,128)S(1)} %constant_dynamic-update-slice_fusion.refs_0_), channel_id=1, source_target_pairs={{0,2},{2,0},{1,3},{3,1},{4,6},{6,4},{5,7},{7,5},{8,10},{10,8},{9,1... | collective-permute-start | bytes 1572872 | tf_op jit(solution)/shard_map/ppermute | solution.py:37
  53.2 11.3 %collective-permute-start.20 = (f32[32,32,128]{2,1,0:T(8,128)S(1)}, f32[32,32,128]{2,1,0:T(8,128)S(1)}, u32[]{:S(2)}, u32[]{:S(2)}) collective-permute-start(f32[32,32,128]{2,1,0:T(8,128)S(1)} %get-tuple-element.127), channel_id=1, source_target_pairs={{0,8},{8,0},{16,24},{24,16},{1,9},{9,1},{17,25},{25,17},{2,10},{10... | collective-permute-start | bytes 1572872 | tf_op jit(solution)/shard_map/ppermute | solution.py:37
  54.4 11.3 %collective-permute-start.17 = (f32[32,32,128]{2,1,0:T(8,128)S(1)}, f32[32,32,128]{2,1,0:T(8,128)S(1)}, u32[]{:S(2)}, u32[]{:S(2)}) collective-permute-start(f32[32,32,128]{2,1,0:T(8,128)S(1)} %get-tuple-element.118), channel_id=1, source_target_pairs={{0,4},{4,0},{1,5},{5,1},{2,6},{6,2},{3,7},{7,3},{8,12},{12,8},{9,1... | collective-permute-start | bytes 1572872 | tf_op jit(solution)/shard_map/ppermute | solution.py:37
  54.7 12.5 %collective-permute-start.14 = (f32[32,32,128]{2,1,0:T(8,128)S(1)}, f32[32,32,128]{2,1,0:T(8,128)S(1)}, u32[]{:S(2)}, u32[]{:S(2)}) collective-permute-start(f32[32,32,128]{2,1,0:T(8,128)S(1)} %get-tuple-element.109), channel_id=1, source_target_pairs={{0,2},{2,0},{1,3},{3,1},{4,6},{6,4},{5,7},{7,5},{8,10},{10,8},{9,1... | collective-permute-start | bytes 1572872 | tf_op jit(solution)/shard_map/ppermute | solution.py:37
  80.0 14.2 %collective-permute-start.23 = (f32[24,32,128]{2,1,0:T(8,128)S(1)}, f32[24,32,128]{2,1,0:T(8,128)S(1)}, u32[]{:S(2)}, u32[]{:S(2)}) collective-permute-start(f32[24,32,128]{2,1,0:T(8,128)S(1)} %get-tuple-element.216), channel_id=1, source_target_pairs={{0,16},{8,24},{16,0},{24,8},{1,17},{9,25},{17,1},{25,9},{2,18},{10... | collective-permute-start | bytes 1179656 | tf_op jit(solution)/shard_map/ppermute | solution.py:37
  99.9 7.3 %collective-permute-start.31 = (f32[16,32,128]{2,1,0:T(8,128)S(1)}, f32[16,32,128]{2,1,0:T(8,128)S(1)}, u32[]{:S(2)}, u32[]{:S(2)}) collective-permute-start(f32[16,32,128]{2,1,0:T(8,128)S(1)} %pad_maximum_fusion.6), channel_id=1, source_target_pairs={{0,2},{2,0},{1,3},{3,1},{4,6},{6,4},{5,7},{7,5},{8,10},{10,8},{9,1... | collective-permute-start | bytes 786440 | tf_op jit(solution)/shard_map/ppermute | solution.py:37
  102.1 9.2 %collective-permute-start.28 = (f32[16,32,128]{2,1,0:T(8,128)S(1)}, f32[16,32,128]{2,1,0:T(8,128)S(1)}, u32[]{:S(2)}, u32[]{:S(2)}) collective-permute-start(f32[16,32,128]{2,1,0:T(8,128)S(1)} %pad_maximum_fusion.5), channel_id=1, source_target_pairs={{0,8},{8,0},{16,24},{24,16},{1,9},{9,1},{17,25},{25,17},{2,10},{10... | collective-permute-start | bytes 786440 | tf_op jit(solution)/shard_map/ppermute | solution.py:37
  102.9 9.3 %collective-permute-start.25 = (f32[16,32,128]{2,1,0:T(8,128)S(1)}, f32[16,32,128]{2,1,0:T(8,128)S(1)}, u32[]{:S(2)}, u32[]{:S(2)}) collective-permute-start(f32[16,32,128]{2,1,0:T(8,128)S(1)} %pad_maximum_fusion.4), channel_id=1, source_target_pairs={{0,4},{4,0},{1,5},{5,1},{2,6},{6,2},{3,7},{7,3},{8,12},{12,8},{9,1... | collective-permute-start | bytes 786440 | tf_op jit(solution)/shard_map/ppermute | solution.py:37
  107.3 11.9 %collective-permute-start.32 = (f32[32,32,128]{2,1,0:T(8,128)S(1)}, f32[32,32,128]{2,1,0:T(8,128)S(1)}, u32[]{:S(2)}, u32[]{:S(2)}) collective-permute-start(f32[32,32,128]{2,1,0:T(8,128)S(1)} %constant_dynamic-update-slice_fusion.21.refs_2_), channel_id=1, source_target_pairs={{0,8},{8,0},{16,24},{24,16},{1,9},{9,1},{17,25},{25,17},{2,10},{10... | collective-permute-start | bytes 1572872 | tf_op jit(solution)/shard_map/ppermute | solution.py:37
  111.4 9.2 %collective-permute-start.29 = (f32[32,32,128]{2,1,0:T(8,128)S(1)}, f32[32,32,128]{2,1,0:T(8,128)S(1)}, u32[]{:S(2)}, u32[]{:S(2)}) collective-permute-start(f32[32,32,128]{2,1,0:T(8,128)S(1)} %constant_dynamic-update-slice_fusion.18.refs_1_), channel_id=1, source_target_pairs={{0,4},{4,0},{1,5},{5,1},{2,6},{6,2},{3,7},{7,3},{8,12},{12,8},{9,1... | collective-permute-start | bytes 1572872 | tf_op jit(solution)/shard_map/ppermute | solution.py:37
  112.2 9.2 %collective-permute-start.26 = (f32[32,32,128]{2,1,0:T(8,128)S(1)}, f32[32,32,128]{2,1,0:T(8,128)S(1)}, u32[]{:S(2)}, u32[]{:S(2)}) collective-permute-start(f32[32,32,128]{2,1,0:T(8,128)S(1)} %constant_dynamic-update-slice_fusion.15.refs_0_), channel_id=1, source_target_pairs={{0,2},{2,0},{1,3},{3,1},{4,6},{6,4},{5,7},{7,5},{8,10},{10,8},{9,1... | collective-permute-start | bytes 1572872 | tf_op jit(solution)/shard_map/ppermute | solution.py:37
  125.8 12.1 %collective-permute-start.39 = (f32[32,32,128]{2,1,0:T(8,128)S(1)}, f32[32,32,128]{2,1,0:T(8,128)S(1)}, u32[]{:S(2)}, u32[]{:S(2)}) collective-permute-start(f32[32,32,128]{2,1,0:T(8,128)S(1)} %get-tuple-element.159), channel_id=1, source_target_pairs={{0,8},{8,0},{16,24},{24,16},{1,9},{9,1},{17,25},{25,17},{2,10},{10... | collective-permute-start | bytes 1572872 | tf_op jit(solution)/shard_map/ppermute | solution.py:37
  127.5 12.1 %collective-permute-start.36 = (f32[32,32,128]{2,1,0:T(8,128)S(1)}, f32[32,32,128]{2,1,0:T(8,128)S(1)}, u32[]{:S(2)}, u32[]{:S(2)}) collective-permute-start(f32[32,32,128]{2,1,0:T(8,128)S(1)} %get-tuple-element.150), channel_id=1, source_target_pairs={{0,4},{4,0},{1,5},{5,1},{2,6},{6,2},{3,7},{7,3},{8,12},{12,8},{9,1... | collective-permute-start | bytes 1572872 | tf_op jit(solution)/shard_map/ppermute | solution.py:37
  127.6 12.9 %collective-permute-start.33 = (f32[32,32,128]{2,1,0:T(8,128)S(1)}, f32[32,32,128]{2,1,0:T(8,128)S(1)}, u32[]{:S(2)}, u32[]{:S(2)}) collective-permute-start(f32[32,32,128]{2,1,0:T(8,128)S(1)} %get-tuple-element.141), channel_id=1, source_target_pairs={{0,2},{2,0},{1,3},{3,1},{4,6},{6,4},{5,7},{7,5},{8,10},{10,8},{9,1... | collective-permute-start | bytes 1572872 | tf_op jit(solution)/shard_map/ppermute | solution.py:37
  147.1 8.5 %collective-permute-start.35 = (f32[8,32,128]{2,1,0:T(8,128)S(1)}, f32[8,32,128]{2,1,0:T(8,128)S(1)}, u32[]{:S(2)}, u32[]{:S(2)}) collective-permute-start(f32[8,32,128]{2,1,0:T(8,128)S(1)} %slice_add_fusion.18), channel_id=1, source_target_pairs={{0,8},{8,0},{16,24},{24,16},{1,9},{9,1},{17,25},{25,17},{2,10},{10... | collective-permute-start | bytes 393224 | tf_op jit(solution)/shard_map/ppermute | solution.py:37
  155.8 12.1 %collective-permute-start.42 = (f32[24,32,128]{2,1,0:T(8,128)S(1)}, f32[24,32,128]{2,1,0:T(8,128)S(1)}, u32[]{:S(2)}, u32[]{:S(2)}) collective-permute-start(f32[24,32,128]{2,1,0:T(8,128)S(1)} %get-tuple-element.204), channel_id=1, source_target_pairs={{0,16},{8,24},{16,0},{24,8},{1,17},{9,25},{17,1},{25,9},{2,18},{10... | collective-permute-start | bytes 1179656 | tf_op jit(solution)/shard_map/ppermute | solution.py:37
  175.0 7.7 %collective-permute-start.50 = (f32[16,32,128]{2,1,0:T(8,128)S(1)}, f32[16,32,128]{2,1,0:T(8,128)S(1)}, u32[]{:S(2)}, u32[]{:S(2)}) collective-permute-start(f32[16,32,128]{2,1,0:T(8,128)S(1)} %pad_maximum_fusion.9), channel_id=1, source_target_pairs={{0,2},{2,0},{1,3},{3,1},{4,6},{6,4},{5,7},{7,5},{8,10},{10,8},{9,1... | collective-permute-start | bytes 786440 | tf_op jit(solution)/shard_map/ppermute | solution.py:37
  182.7 12.6 %collective-permute-start.51 = (f32[32,32,128]{2,1,0:T(8,128)S(1)}, f32[32,32,128]{2,1,0:T(8,128)S(1)}, u32[]{:S(2)}, u32[]{:S(2)}) collective-permute-start(f32[32,32,128]{2,1,0:T(8,128)S(1)} %constant_dynamic-update-slice_fusion.36.refs_2_), channel_id=1, source_target_pairs={{0,8},{8,0},{16,24},{24,16},{1,9},{9,1},{17,25},{25,17},{2,10},{10... | collective-permute-start | bytes 1572872 | tf_op jit(solution)/shard_map/ppermute | solution.py:37
  183.6 13.8 %collective-permute-start.48 = (f32[32,32,128]{2,1,0:T(8,128)S(1)}, f32[32,32,128]{2,1,0:T(8,128)S(1)}, u32[]{:S(2)}, u32[]{:S(2)}) collective-permute-start(f32[32,32,128]{2,1,0:T(8,128)S(1)} %constant_dynamic-update-slice_fusion.33.refs_1_), channel_id=1, source_target_pairs={{0,4},{4,0},{1,5},{5,1},{2,6},{6,2},{3,7},{7,3},{8,12},{12,8},{9,1... | collective-permute-start | bytes 1572872 | tf_op jit(solution)/shard_map/ppermute | solution.py:37
  183.9 14.2 %collective-permute-start.45 = (f32[32,32,128]{2,1,0:T(8,128)S(1)}, f32[32,32,128]{2,1,0:T(8,128)S(1)}, u32[]{:S(2)}, u32[]{:S(2)}) collective-permute-start(f32[32,32,128]{2,1,0:T(8,128)S(1)} %constant_dynamic-update-slice_fusion.30.refs_0_), channel_id=1, source_target_pairs={{0,2},{2,0},{1,3},{3,1},{4,6},{6,4},{5,7},{7,5},{8,10},{10,8},{9,1... | collective-permute-start | bytes 1572872 | tf_op jit(solution)/shard_map/ppermute | solution.py:37
  202.5 10.7 %collective-permute-start.52 = (f32[32,32,128]{2,1,0:T(8,128)S(1)}, f32[32,32,128]{2,1,0:T(8,128)S(1)}, u32[]{:S(2)}, u32[]{:S(2)}) collective-permute-start(f32[32,32,128]{2,1,0:T(8,128)S(1)} %get-tuple-element.173), channel_id=1, source_target_pairs={{0,2},{2,0},{1,3},{3,1},{4,6},{6,4},{5,7},{7,5},{8,10},{10,8},{9,1... | collective-permute-start | bytes 1572872 | tf_op jit(solution)/shard_map/ppermute | solution.py:37
  203.5 11.7 %collective-permute-start.55 = (f32[32,32,128]{2,1,0:T(8,128)S(1)}, f32[32,32,128]{2,1,0:T(8,128)S(1)}, u32[]{:S(2)}, u32[]{:S(2)}) collective-permute-start(f32[32,32,128]{2,1,0:T(8,128)S(1)} %get-tuple-element.182), channel_id=1, source_target_pairs={{0,4},{4,0},{1,5},{5,1},{2,6},{6,2},{3,7},{7,3},{8,12},{12,8},{9,1... | collective-permute-start | bytes 1572872 | tf_op jit(solution)/shard_map/ppermute | solution.py:37
  204.5 11.3 %collective-permute-start.58 = (f32[32,32,128]{2,1,0:T(8,128)S(1)}, f32[32,32,128]{2,1,0:T(8,128)S(1)}, u32[]{:S(2)}, u32[]{:S(2)}) collective-permute-start(f32[32,32,128]{2,1,0:T(8,128)S(1)} %get-tuple-element.191), channel_id=1, source_target_pairs={{0,8},{8,0},{16,24},{24,16},{1,9},{9,1},{17,25},{25,17},{2,10},{10... | collective-permute-start | bytes 1572872 | tf_op jit(solution)/shard_map/ppermute | solution.py:37
  215.9 7.3 %collective-permute-start.59 = (f32[16,32,128]{2,1,0:T(8,128)S(1)}, f32[16,32,128]{2,1,0:T(8,128)S(1)}, u32[]{:S(2)}, u32[]{:S(2)}) collective-permute-start(f32[16,32,128]{2,1,0:T(8,128)S(1)} %slice_add_fusion), channel_id=1, source_target_pairs={{0,2},{2,0},{1,3},{3,1},{4,6},{6,4},{5,7},{7,5},{8,10},{10,8},{9,1... | collective-permute-start | bytes 786440 | tf_op jit(solution)/shard_map/ppermute | solution.py:37
  228.6 8.7 %collective-permute-start.61 = (f32[12,32,128]{2,1,0:T(8,128)S(1)}, f32[12,32,128]{2,1,0:T(8,128)S(1)}, u32[]{:S(2)}, u32[]{:S(2)}) collective-permute-start(f32[12,32,128]{2,1,0:T(8,128)S(1)} %get-tuple-element.264), channel_id=1, source_target_pairs={{0,16},{8,24},{16,0},{24,8},{1,17},{9,25},{17,1},{25,9},{2,18},{10... | collective-permute-start | bytes 589832 | tf_op jit(solution)/shard_map/ppermute | solution.py:37
  (42 other events, 291.6 us)

commit v20 on v19

--- a/solution.py
+++ b/solution.py
@@ -302,7 +302,7 @@
         if sweep < ITERS - 1:
             fluxes = [r * (d + s) for r, d, s in zip(relaxes, drives, sum_far(blocks))]
     weighted = sum(
-        [jnp.sum(w * b, axis=(0, 2)) for w, b in zip(heats, blocks)],
+        [jnp.sum(w * b, axis=(0, 2)) for w, b in zip(heats, lax.optimization_barrier(blocks))],
         jnp.sum(heats[0] * drives[0], axis=(0, 2)),
     )
     totals = jnp.pad(jnp.stack([weighted, jnp.full((half,), jnp.sum(heat))]), ((0, 0), (0, size - half)))

time: 256 us -> 260 us (1.016)
  waiting for transfers between devices: 127 us -> 122 us
  other arithmetic: 6.62 us -> 10.6 us
  starting transfers between devices: 60.2 us -> 63.3 us
    ppermute x64, waiting for transfers between devices: 127 us -> 122 us  [swap(): lax.ppermute(array, axis, [(i, i ^ distance) for i in range(lax.axis_size...]
    ppermute x64, starting transfers between devices: 60.2 us -> 63.3 us  [swap(): lax.ppermute(array, axis, [(i, i ^ distance) for i in range(lax.axis_size...]
  transfers between devices with their start and end apart: 64 -> 64, of which waited for: 50 -> 45; matrix products, arithmetic and copies ran while one was open for 2% -> 2% of each run, Pallas kernels for 12% -> 13%
where the time goes in v20:
time: 260 us; the launch traced here: 258 us
  waiting for transfers between devices  122 us (47%)
  starting transfers between devices  63.3 us (24%)
  Pallas kernels  44.9 us (17%)
  blocking collectives  12.7 us (5%)
  other arithmetic  10.6 us (4%)
  local copies, waits for them, and re-layouts  2.86 us (1%)
    ppermute x64, waiting for transfers between devices, swap(): lax.ppermute(array, axis, [(i, i ^ distance) for i in range(lax.axis_size...  122 us
    ppermute x64, starting transfers between devices, swap(): lax.ppermute(array, axis, [(i, i ^ distance) for i in range(lax.axis_size...  63.3 us
    pallas_call x9, Pallas kernels, apply_tiles(): pl.pallas_call(functools.partial(apply_kernel, span, skip, len(flux), bas...  44.9 us
    all_to_all x1, blocking collectives, shards(): both = lax.all_to_all(both, CHIPS, split_axis=0, concat_axis=0, tiled=True)  12.7 us
  transfers between devices with their start and end apart: 64, of which 45 were waited for; matrix products, arithmetic and copies ran while one was open for 2% of the time, Pallas kernels for 13%

profile of v20, /device:TPU:0, one launch (start us, length us, event | category | flops | bytes accessed | tf_op | source)
XLA Modules:
  0.0 258.4 jit_solution(7343016758699856496)
XLA Ops:
  2.6 3.7 %collective-permute-start.1 = (f32[6,2,128]{2,1,0:T(2,128)S(1)}, f32[6,2,128]{2,1,0:T(2,128)S(1)}, u32[]{:S(2)}, u32[]{:S(2)}) collective-permute-start(f32[6,2,128]{2,1,0:T(2,128)S(1)} %pad_maximum_fusion.25), channel_id=1, source_target_pairs={{0,16},{8,24},{16,0},{24,8},{1,17},{9,25},{17,1},{25,9},{2,18},{10... | collective-permute-start | bytes 18440 | tf_op jit(solution)/shard_map/ppermute | solution.py:37
  7.9 10.5 %collective-permute-done = f32[6,64,128]{2,1,0:T(8,128)S(1)} collective-permute-done((f32[6,64,128]{2,1,0:T(8,128)S(1)}, f32[6,64,128]{2,1,0:T(8,128)S(1)}, u32[]{:S(2)}, u32[]{:S(2)}) %collective-permute-start) | collective-permute-done | bytes 196640 | tf_op jit(solution)/shard_map/ppermute | solution.py:37
  24.0 2.4 collective-permute-done.11
  29.8 4.3 %collective-permute-done.12 = f32[16,32,128]{2,1,0:T(8,128)S(1)} collective-permute-done((f32[16,32,128]{2,1,0:T(8,128)S(1)}, f32[16,32,128]{2,1,0:T(8,128)S(1)}, u32[]{:S(2)}, u32[]{:S(2)}) %collective-permute-start.12) | collective-permute-done | bytes 262176 | tf_op jit(solution)/shard_map/ppermute | solution.py:37
  38.0 6.6 %shard_map.95 = (f32[96,32,128]{2,1,0:T(8,128)S(1)}, f32[96,32,128]{2,1,0:T(8,128)S(1)}) custom-call(s32[772]{0:T(1024)S(1)} %pad_add_fusion.places_ref, f32[128,128,128]{2,1,0:T(8,128)} %own_ref.17, f32[128,128,128]{2,1,0:T(8,128)} %collective-permute-done.4.other_ref, f32[32,32,128]{2,1,0:T(8,128)S(1)} %constant_dynamic-update-slice_fusion.refs_0_, ...), custom_call_target="tpu_custom_call" | custom-call | flops 536870912 | bytes 14680064 | tf_op jit(solution)/shard_map/pallas_call | solution.py:188
  48.8 4.0 %shard_map.97 = (f32[32,32,128]{2,1,0:T(8,128)S(1)}, f32[32,32,128]{2,1,0:T(8,128)S(1)}, f32[32,32,128]{2,1,0:T(8,128)S(1)}) custom-call(s32[772]{0:T(1024)S(1)} %pad_add_fusion.places_ref, f32[128,128,128]{2,1,0:T(8,128)} %own_ref.17, f32[128,128,128]{2,1,0:T(8,128)} %collective-permute-done.4.other_ref, f32[32,32,128]{2,1,0:T(8,128)S(1)} %collective-permute-done.7.refs_0_, ...), custom_call_target="tpu_custom_call" | custom-call | flops 268435456 | bytes 7340032 | tf_op jit(solution)/shard_map/pallas_call | solution.py:188
  56.1 4.3 %shard_map.96 = (f32[32,32,128]{2,1,0:T(8,128)S(1)}, f32[32,32,128]{2,1,0:T(8,128)S(1)}, f32[32,32,128]{2,1,0:T(8,128)S(1)}) custom-call(s32[772]{0:T(1024)S(1)} %pad_add_fusion.places_ref, f32[128,128,128]{2,1,0:T(8,128)} %own_ref.17, f32[128,128,128]{2,1,0:T(8,128)} %collective-permute-done.4.other_ref, f32[32,32,128]{2,1,0:T(8,128)S(1)} %collective-permute-done.7.refs_0_, ...), custom_call_target="tpu_custom_call" | custom-call | flops 268435456 | bytes 7340032 | tf_op jit(solution)/shard_map/pallas_call | solution.py:188
  60.4 3.4 %collective-permute-done.20 = f32[32,32,128]{2,1,0:T(8,128)S(1)} collective-permute-done((f32[32,32,128]{2,1,0:T(8,128)S(1)}, f32[32,32,128]{2,1,0:T(8,128)S(1)}, u32[]{:S(2)}, u32[]{:S(2)}) %collective-permute-start.20) | collective-permute-done | bytes 524320 | tf_op jit(solution)/shard_map/ppermute | solution.py:37
  64.8 2.5 collective-permute-start.18
  77.1 4.3 %collective-permute-done.16 = f32[8,32,128]{2,1,0:T(8,128)S(1)} collective-permute-done((f32[8,32,128]{2,1,0:T(8,128)S(1)}, f32[8,32,128]{2,1,0:T(8,128)S(1)}, u32[]{:S(2)}, u32[]{:S(2)}) %collective-permute-start.16) | collective-permute-done | bytes 131104 | tf_op jit(solution)/shard_map/ppermute | solution.py:37
  82.1 12.5 %collective-permute-done.23 = f32[24,32,128]{2,1,0:T(8,128)S(1)} collective-permute-done((f32[24,32,128]{2,1,0:T(8,128)S(1)}, f32[24,32,128]{2,1,0:T(8,128)S(1)}, u32[]{:S(2)}, u32[]{:S(2)}) %collective-permute-start.23) | collective-permute-done | bytes 393248 | tf_op jit(solution)/shard_map/ppermute | solution.py:37
  97.2 4.1 %collective-permute-done.30 = f32[8,32,128]{2,1,0:T(8,128)S(1)} collective-permute-done((f32[8,32,128]{2,1,0:T(8,128)S(1)}, f32[8,32,128]{2,1,0:T(8,128)S(1)}, u32[]{:S(2)}, u32[]{:S(2)}) %collective-permute-start.30) | collective-permute-done | bytes 131104 | tf_op jit(solution)/shard_map/ppermute | solution.py:37
  104.5 5.8 %collective-permute-done.31 = f32[16,32,128]{2,1,0:T(8,128)S(1)} collective-permute-done((f32[16,32,128]{2,1,0:T(8,128)S(1)}, f32[16,32,128]{2,1,0:T(8,128)S(1)}, u32[]{:S(2)}, u32[]{:S(2)}) %collective-permute-start.31) | collective-permute-done | bytes 262176 | tf_op jit(solution)/shard_map/ppermute | solution.py:37
  112.9 6.6 %shard_map.98 = (f32[96,32,128]{2,1,0:T(8,128)S(1)}, f32[96,32,128]{2,1,0:T(8,128)S(1)}) custom-call(s32[772]{0:T(1024)S(1)} %pad_add_fusion.places_ref, f32[128,128,128]{2,1,0:T(8,128)} %own_ref.17, f32[128,128,128]{2,1,0:T(8,128)} %collective-permute-done.4.other_ref, f32[32,32,128]{2,1,0:T(8,128)S(1)} %constant_dynamic-update-slice_fusion.15.refs_0_, ...), custom_call_target="tpu_custom_call" | custom-call | flops 536870912 | bytes 14680064 | tf_op jit(solution)/shard_map/pallas_call | solution.py:188
  121.7 4.0 %shard_map.100 = (f32[32,32,128]{2,1,0:T(8,128)S(1)}, f32[32,32,128]{2,1,0:T(8,128)S(1)}, f32[32,32,128]{2,1,0:T(8,128)S(1)}) custom-call(s32[772]{0:T(1024)S(1)} %pad_add_fusion.places_ref, f32[128,128,128]{2,1,0:T(8,128)} %own_ref.17, f32[128,128,128]{2,1,0:T(8,128)} %collective-permute-done.4.other_ref, ...), custom_call_target="tpu_custom_call" | custom-call | flops 268435456 | bytes 7340032 | tf_op jit(solution)/shard_map/pallas_call | solution.py:188
  129.7 4.5 %shard_map.99 = (f32[32,32,128]{2,1,0:T(8,128)S(1)}, f32[32,32,128]{2,1,0:T(8,128)S(1)}, f32[32,32,128]{2,1,0:T(8,128)S(1)}) custom-call(s32[772]{0:T(1024)S(1)} %pad_add_fusion.places_ref, f32[128,128,128]{2,1,0:T(8,128)} %own_ref.17, f32[128,128,128]{2,1,0:T(8,128)} %collective-permute-done.4.other_ref, ...), custom_call_target="tpu_custom_call" | custom-call | flops 268435456 | bytes 7340032 | tf_op jit(solution)/shard_map/pallas_call | solution.py:188
  134.2 3.0 %collective-permute-done.39 = f32[32,32,128]{2,1,0:T(8,128)S(1)} collective-permute-done((f32[32,32,128]{2,1,0:T(8,128)S(1)}, f32[32,32,128]{2,1,0:T(8,128)S(1)}, u32[]{:S(2)}, u32[]{:S(2)}) %collective-permute-start.39) | collective-permute-done | bytes 524320 | tf_op jit(solution)/shard_map/ppermute | solution.py:37
  148.8 2.8 %collective-permute-done.38 = f32[8,32,128]{2,1,0:T(8,128)S(1)} collective-permute-done((f32[8,32,128]{2,1,0:T(8,128)S(1)}, f32[8,32,128]{2,1,0:T(8,128)S(1)}, u32[]{:S(2)}, u32[]{:S(2)}) %collective-permute-start.38) | collective-permute-done | bytes 131104 | tf_op jit(solution)/shard_map/ppermute | solution.py:37
  151.6 3.6 %collective-permute-done.35 = f32[8,32,128]{2,1,0:T(8,128)S(1)} collective-permute-done((f32[8,32,128]{2,1,0:T(8,128)S(1)}, f32[8,32,128]{2,1,0:T(8,128)S(1)}, u32[]{:S(2)}, u32[]{:S(2)}) %collective-permute-start.35) | collective-permute-done | bytes 131104 | tf_op jit(solution)/shard_map/ppermute | solution.py:37
  155.5 12.3 %collective-permute-done.42 = f32[24,32,128]{2,1,0:T(8,128)S(1)} collective-permute-done((f32[24,32,128]{2,1,0:T(8,128)S(1)}, f32[24,32,128]{2,1,0:T(8,128)S(1)}, u32[]{:S(2)}, u32[]{:S(2)}) %collective-permute-start.42) | collective-permute-done | bytes 393248 | tf_op jit(solution)/shard_map/ppermute | solution.py:37
  170.4 4.1 %collective-permute-done.49 = f32[8,32,128]{2,1,0:T(8,128)S(1)} collective-permute-done((f32[8,32,128]{2,1,0:T(8,128)S(1)}, f32[8,32,128]{2,1,0:T(8,128)S(1)}, u32[]{:S(2)}, u32[]{:S(2)}) %collective-permute-start.49) | collective-permute-done | bytes 131104 | tf_op jit(solution)/shard_map/ppermute | solution.py:37
  177.0 4.0 %collective-permute-done.50 = f32[16,32,128]{2,1,0:T(8,128)S(1)} collective-permute-done((f32[16,32,128]{2,1,0:T(8,128)S(1)}, f32[16,32,128]{2,1,0:T(8,128)S(1)}, u32[]{:S(2)}, u32[]{:S(2)}) %collective-permute-start.50) | collective-permute-done | bytes 262176 | tf_op jit(solution)/shard_map/ppermute | solution.py:37
  184.3 6.6 %shard_map.101 = (f32[96,32,128]{2,1,0:T(8,128)S(1)}, f32[96,32,128]{2,1,0:T(8,128)S(1)}) custom-call(s32[772]{0:T(1024)S(1)} %pad_add_fusion.places_ref, f32[128,128,128]{2,1,0:T(8,128)} %own_ref.17, f32[128,128,128]{2,1,0:T(8,128)} %collective-permute-done.4.other_ref, f32[32,32,128]{2,1,0:T(8,128)S(1)} %constant_dynamic-update-slice_fusion.30.refs_0_, ...), custom_call_target="tpu_custom_call" | custom-call | flops 536870912 | bytes 14680064 | tf_op jit(solution)/shard_map/pallas_call | solution.py:188
  190.9 4.4 %collective-permute-done.51.refs_2_ = f32[32,32,128]{2,1,0:T(8,128)S(1)} collective-permute-done((f32[32,32,128]{2,1,0:T(8,128)S(1)}, f32[32,32,128]{2,1,0:T(8,128)S(1)}, u32[]{:S(2)}, u32[]{:S(2)}) %collective-permute-start.51) | collective-permute-done | bytes 524320 | tf_op jit(solution)/shard_map/ppermute | solution.py:37
  195.9 4.0 %shard_map.103 = (f32[32,32,128]{2,1,0:T(8,128)S(1)}, f32[32,32,128]{2,1,0:T(8,128)S(1)}, f32[32,32,128]{2,1,0:T(8,128)S(1)}) custom-call(s32[772]{0:T(1024)S(1)} %pad_add_fusion.places_ref, f32[128,128,128]{2,1,0:T(8,128)} %own_ref.17, f32[128,128,128]{2,1,0:T(8,128)} %collective-permute-done.4.other_ref, ...), custom_call_target="tpu_custom_call" | custom-call | flops 268435456 | bytes 7340032 | tf_op jit(solution)/shard_map/pallas_call | solution.py:188
  200.0 2.1 collective-permute-start.52
  204.6 4.3 %shard_map.102 = (f32[32,32,128]{2,1,0:T(8,128)S(1)}, f32[32,32,128]{2,1,0:T(8,128)S(1)}, f32[32,32,128]{2,1,0:T(8,128)S(1)}) custom-call(s32[772]{0:T(1024)S(1)} %pad_add_fusion.places_ref, f32[128,128,128]{2,1,0:T(8,128)} %own_ref.17, f32[128,128,128]{2,1,0:T(8,128)} %collective-permute-done.4.other_ref, ...), custom_call_target="tpu_custom_call" | custom-call | flops 268435456 | bytes 7340032 | tf_op jit(solution)/shard_map/pallas_call | solution.py:188
  214.4 2.8 %collective-permute-done.53 = f32[16,32,128]{2,1,0:T(8,128)S(1)} collective-permute-done((f32[16,32,128]{2,1,0:T(8,128)S(1)}, f32[16,32,128]{2,1,0:T(8,128)S(1)}, u32[]{:S(2)}, u32[]{:S(2)}) %collective-permute-start.53) | collective-permute-done | bytes 262176 | tf_op jit(solution)/shard_map/ppermute | solution.py:37
  222.7 2.2 collective-permute-start.60
  225.7 2.5 collective-permute-done.60
  232.2 6.6 %collective-permute-done.61 = f32[12,32,128]{2,1,0:T(8,128)S(1)} collective-permute-done((f32[12,32,128]{2,1,0:T(8,128)S(1)}, f32[12,32,128]{2,1,0:T(8,128)S(1)}, u32[]{:S(2)}, u32[]{:S(2)}) %collective-permute-start.61) | collective-permute-done | bytes 196640 | tf_op jit(solution)/shard_map/ppermute | solution.py:37
  241.7 12.7 %all_to_all.5 = f32[16,4,128]{2,1,0:T(4,128)S(1)} all-to-all(f32[16,4,128]{2,1,0:T(4,128)S(1)} %broadcast_in_dim.64), channel_id=1, replica_groups=mesh['z'=4,'y'=2,'x'=2,'core'=2] {'z','y','x'}, dimensions={0} | all-to-all | bytes 65536 | tf_op jit(solution)/shard_map/all_to_all | solution.py:311
  (290 shorter events, 94.5 us)
Async XLA Ops:
  0.7 20.0 %collective-permute-start.4 = (f32[128,128,128]{2,1,0:T(8,128)}, f32[128,128,128]{2,1,0:T(8,128)}, u32[]{:S(2)}, u32[]{:S(2)}) collective-permute-start(f32[128,128,128]{2,1,0:T(8,128)} %own_ref.17), channel_id=1, source_target_pairs={{0,1},{1,0},{2,3},{3,2},{4,5},{5,4},{6,7},{7,6},{8,9},{9,8},{10,11... | collective-permute-start | bytes 25165832 | tf_op jit(solution)/shard_map/ppermute | solution.py:37
  6.3 12.2 %collective-permute-start = (f32[6,64,128]{2,1,0:T(8,128)S(1)}, f32[6,64,128]{2,1,0:T(8,128)S(1)}, u32[]{:S(2)}, u32[]{:S(2)}) collective-permute-start(f32[6,64,128]{2,1,0:T(8,128)S(1)} %bitcast_bitcast_fusion), channel_id=1, source_target_pairs={{0,16},{8,24},{16,0},{24,8},{1,17},{9,25},{17,1},{25,9},{2,18},{10... | collective-permute-start | bytes 589832 | tf_op jit(solution)/shard_map/ppermute | solution.py:37
  26.5 7.7 %collective-permute-start.12 = (f32[16,32,128]{2,1,0:T(8,128)S(1)}, f32[16,32,128]{2,1,0:T(8,128)S(1)}, u32[]{:S(2)}, u32[]{:S(2)}) collective-permute-start(f32[16,32,128]{2,1,0:T(8,128)S(1)} %pad_maximum_fusion.3), channel_id=1, source_target_pairs={{0,2},{2,0},{1,3},{3,1},{4,6},{6,4},{5,7},{7,5},{8,10},{10,8},{9,1... | collective-permute-start | bytes 786440 | tf_op jit(solution)/shard_map/ppermute | solution.py:37
  28.0 7.5 %collective-permute-start.9 = (f32[16,32,128]{2,1,0:T(8,128)S(1)}, f32[16,32,128]{2,1,0:T(8,128)S(1)}, u32[]{:S(2)}, u32[]{:S(2)}) collective-permute-start(f32[16,32,128]{2,1,0:T(8,128)S(1)} %pad_maximum_fusion.2), channel_id=1, source_target_pairs={{0,8},{8,0},{16,24},{24,16},{1,9},{9,1},{17,25},{25,17},{2,10},{10... | collective-permute-start | bytes 786440 | tf_op jit(solution)/shard_map/ppermute | solution.py:37
  29.1 8.1 %collective-permute-start.6 = (f32[16,32,128]{2,1,0:T(8,128)S(1)}, f32[16,32,128]{2,1,0:T(8,128)S(1)}, u32[]{:S(2)}, u32[]{:S(2)}) collective-permute-start(f32[16,32,128]{2,1,0:T(8,128)S(1)} %pad_maximum_fusion.1), channel_id=1, source_target_pairs={{0,4},{4,0},{1,5},{5,1},{2,6},{6,2},{3,7},{7,3},{8,12},{12,8},{9,1... | collective-permute-start | bytes 786440 | tf_op jit(solution)/shard_map/ppermute | solution.py:37
  34.1 12.5 %collective-permute-start.13 = (f32[32,32,128]{2,1,0:T(8,128)S(1)}, f32[32,32,128]{2,1,0:T(8,128)S(1)}, u32[]{:S(2)}, u32[]{:S(2)}) collective-permute-start(f32[32,32,128]{2,1,0:T(8,128)S(1)} %constant_dynamic-update-slice_fusion.6.refs_2_), channel_id=1, source_target_pairs={{0,8},{8,0},{16,24},{24,16},{1,9},{9,1},{17,25},{25,17},{2,10},{10... | collective-permute-start | bytes 1572872 | tf_op jit(solution)/shard_map/ppermute | solution.py:37
  35.5 12.0 %collective-permute-start.10 = (f32[32,32,128]{2,1,0:T(8,128)S(1)}, f32[32,32,128]{2,1,0:T(8,128)S(1)}, u32[]{:S(2)}, u32[]{:S(2)}) collective-permute-start(f32[32,32,128]{2,1,0:T(8,128)S(1)} %constant_dynamic-update-slice_fusion.3.refs_1_), channel_id=1, source_target_pairs={{0,4},{4,0},{1,5},{5,1},{2,6},{6,2},{3,7},{7,3},{8,12},{12,8},{9,1... | collective-permute-start | bytes 1572872 | tf_op jit(solution)/shard_map/ppermute | solution.py:37
  37.1 11.7 %collective-permute-start.7 = (f32[32,32,128]{2,1,0:T(8,128)S(1)}, f32[32,32,128]{2,1,0:T(8,128)S(1)}, u32[]{:S(2)}, u32[]{:S(2)}) collective-permute-start(f32[32,32,128]{2,1,0:T(8,128)S(1)} %constant_dynamic-update-slice_fusion.refs_0_), channel_id=1, source_target_pairs={{0,2},{2,0},{1,3},{3,1},{4,6},{6,4},{5,7},{7,5},{8,10},{10,8},{9,1... | collective-permute-start | bytes 1572872 | tf_op jit(solution)/shard_map/ppermute | solution.py:37
  52.9 10.9 %collective-permute-start.20 = (f32[32,32,128]{2,1,0:T(8,128)S(1)}, f32[32,32,128]{2,1,0:T(8,128)S(1)}, u32[]{:S(2)}, u32[]{:S(2)}) collective-permute-start(f32[32,32,128]{2,1,0:T(8,128)S(1)} %get-tuple-element.129), channel_id=1, source_target_pairs={{0,8},{8,0},{16,24},{24,16},{1,9},{9,1},{17,25},{25,17},{2,10},{10... | collective-permute-start | bytes 1572872 | tf_op jit(solution)/shard_map/ppermute | solution.py:37
  54.1 10.7 %collective-permute-start.17 = (f32[32,32,128]{2,1,0:T(8,128)S(1)}, f32[32,32,128]{2,1,0:T(8,128)S(1)}, u32[]{:S(2)}, u32[]{:S(2)}) collective-permute-start(f32[32,32,128]{2,1,0:T(8,128)S(1)} %get-tuple-element.120), channel_id=1, source_target_pairs={{0,4},{4,0},{1,5},{5,1},{2,6},{6,2},{3,7},{7,3},{8,12},{12,8},{9,1... | collective-permute-start | bytes 1572872 | tf_op jit(solution)/shard_map/ppermute | solution.py:37
  55.3 13.0 %collective-permute-start.14 = (f32[32,32,128]{2,1,0:T(8,128)S(1)}, f32[32,32,128]{2,1,0:T(8,128)S(1)}, u32[]{:S(2)}, u32[]{:S(2)}) collective-permute-start(f32[32,32,128]{2,1,0:T(8,128)S(1)} %get-tuple-element.111), channel_id=1, source_target_pairs={{0,2},{2,0},{1,3},{3,1},{4,6},{6,4},{5,7},{7,5},{8,10},{10,8},{9,1... | collective-permute-start | bytes 1572872 | tf_op jit(solution)/shard_map/ppermute | solution.py:37
  81.5 13.0 %collective-permute-start.23 = (f32[24,32,128]{2,1,0:T(8,128)S(1)}, f32[24,32,128]{2,1,0:T(8,128)S(1)}, u32[]{:S(2)}, u32[]{:S(2)}) collective-permute-start(f32[24,32,128]{2,1,0:T(8,128)S(1)} %get-tuple-element.220), channel_id=1, source_target_pairs={{0,16},{8,24},{16,0},{24,8},{1,17},{9,25},{17,1},{25,9},{2,18},{10... | collective-permute-start | bytes 1179656 | tf_op jit(solution)/shard_map/ppermute | solution.py:37
  101.3 9.1 %collective-permute-start.31 = (f32[16,32,128]{2,1,0:T(8,128)S(1)}, f32[16,32,128]{2,1,0:T(8,128)S(1)}, u32[]{:S(2)}, u32[]{:S(2)}) collective-permute-start(f32[16,32,128]{2,1,0:T(8,128)S(1)} %pad_maximum_fusion.6), channel_id=1, source_target_pairs={{0,2},{2,0},{1,3},{3,1},{4,6},{6,4},{5,7},{7,5},{8,10},{10,8},{9,1... | collective-permute-start | bytes 786440 | tf_op jit(solution)/shard_map/ppermute | solution.py:37
  102.4 8.1 %collective-permute-start.28 = (f32[16,32,128]{2,1,0:T(8,128)S(1)}, f32[16,32,128]{2,1,0:T(8,128)S(1)}, u32[]{:S(2)}, u32[]{:S(2)}) collective-permute-start(f32[16,32,128]{2,1,0:T(8,128)S(1)} %pad_maximum_fusion.5), channel_id=1, source_target_pairs={{0,8},{8,0},{16,24},{24,16},{1,9},{9,1},{17,25},{25,17},{2,10},{10... | collective-permute-start | bytes 786440 | tf_op jit(solution)/shard_map/ppermute | solution.py:37
  102.5 9.3 %collective-permute-start.25 = (f32[16,32,128]{2,1,0:T(8,128)S(1)}, f32[16,32,128]{2,1,0:T(8,128)S(1)}, u32[]{:S(2)}, u32[]{:S(2)}) collective-permute-start(f32[16,32,128]{2,1,0:T(8,128)S(1)} %pad_maximum_fusion.4), channel_id=1, source_target_pairs={{0,4},{4,0},{1,5},{5,1},{2,6},{6,2},{3,7},{7,3},{8,12},{12,8},{9,1... | collective-permute-start | bytes 786440 | tf_op jit(solution)/shard_map/ppermute | solution.py:37
  110.3 9.2 %collective-permute-start.32 = (f32[32,32,128]{2,1,0:T(8,128)S(1)}, f32[32,32,128]{2,1,0:T(8,128)S(1)}, u32[]{:S(2)}, u32[]{:S(2)}) collective-permute-start(f32[32,32,128]{2,1,0:T(8,128)S(1)} %constant_dynamic-update-slice_fusion.21.refs_2_), channel_id=1, source_target_pairs={{0,8},{8,0},{16,24},{24,16},{1,9},{9,1},{17,25},{25,17},{2,10},{10... | collective-permute-start | bytes 1572872 | tf_op jit(solution)/shard_map/ppermute | solution.py:37
  110.6 9.2 %collective-permute-start.29 = (f32[32,32,128]{2,1,0:T(8,128)S(1)}, f32[32,32,128]{2,1,0:T(8,128)S(1)}, u32[]{:S(2)}, u32[]{:S(2)}) collective-permute-start(f32[32,32,128]{2,1,0:T(8,128)S(1)} %constant_dynamic-update-slice_fusion.18.refs_1_), channel_id=1, source_target_pairs={{0,4},{4,0},{1,5},{5,1},{2,6},{6,2},{3,7},{7,3},{8,12},{12,8},{9,1... | collective-permute-start | bytes 1572872 | tf_op jit(solution)/shard_map/ppermute | solution.py:37
  111.9 9.8 %collective-permute-start.26 = (f32[32,32,128]{2,1,0:T(8,128)S(1)}, f32[32,32,128]{2,1,0:T(8,128)S(1)}, u32[]{:S(2)}, u32[]{:S(2)}) collective-permute-start(f32[32,32,128]{2,1,0:T(8,128)S(1)} %constant_dynamic-update-slice_fusion.15.refs_0_), channel_id=1, source_target_pairs={{0,2},{2,0},{1,3},{3,1},{4,6},{6,4},{5,7},{7,5},{8,10},{10,8},{9,1... | collective-permute-start | bytes 1572872 | tf_op jit(solution)/shard_map/ppermute | solution.py:37
  125.7 11.6 %collective-permute-start.39 = (f32[32,32,128]{2,1,0:T(8,128)S(1)}, f32[32,32,128]{2,1,0:T(8,128)S(1)}, u32[]{:S(2)}, u32[]{:S(2)}) collective-permute-start(f32[32,32,128]{2,1,0:T(8,128)S(1)} %get-tuple-element.161), channel_id=1, source_target_pairs={{0,8},{8,0},{16,24},{24,16},{1,9},{9,1},{17,25},{25,17},{2,10},{10... | collective-permute-start | bytes 1572872 | tf_op jit(solution)/shard_map/ppermute | solution.py:37
  127.7 11.8 %collective-permute-start.36 = (f32[32,32,128]{2,1,0:T(8,128)S(1)}, f32[32,32,128]{2,1,0:T(8,128)S(1)}, u32[]{:S(2)}, u32[]{:S(2)}) collective-permute-start(f32[32,32,128]{2,1,0:T(8,128)S(1)} %get-tuple-element.152), channel_id=1, source_target_pairs={{0,4},{4,0},{1,5},{5,1},{2,6},{6,2},{3,7},{7,3},{8,12},{12,8},{9,1... | collective-permute-start | bytes 1572872 | tf_op jit(solution)/shard_map/ppermute | solution.py:37
  129.0 11.8 %collective-permute-start.33 = (f32[32,32,128]{2,1,0:T(8,128)S(1)}, f32[32,32,128]{2,1,0:T(8,128)S(1)}, u32[]{:S(2)}, u32[]{:S(2)}) collective-permute-start(f32[32,32,128]{2,1,0:T(8,128)S(1)} %get-tuple-element.143), channel_id=1, source_target_pairs={{0,2},{2,0},{1,3},{3,1},{4,6},{6,4},{5,7},{7,5},{8,10},{10,8},{9,1... | collective-permute-start | bytes 1572872 | tf_op jit(solution)/shard_map/ppermute | solution.py:37
  140.9 7.6 %collective-permute-start.34 = (f32[16,32,128]{2,1,0:T(8,128)S(1)}, f32[16,32,128]{2,1,0:T(8,128)S(1)}, u32[]{:S(2)}, u32[]{:S(2)}) collective-permute-start(f32[16,32,128]{2,1,0:T(8,128)S(1)} %slice_add_fusion.5), channel_id=1, source_target_pairs={{0,4},{4,0},{1,5},{5,1},{2,6},{6,2},{3,7},{7,3},{8,12},{12,8},{9,1... | collective-permute-start | bytes 786440 | tf_op jit(solution)/shard_map/ppermute | solution.py:37
  155.4 12.4 %collective-permute-start.42 = (f32[24,32,128]{2,1,0:T(8,128)S(1)}, f32[24,32,128]{2,1,0:T(8,128)S(1)}, u32[]{:S(2)}, u32[]{:S(2)}) collective-permute-start(f32[24,32,128]{2,1,0:T(8,128)S(1)} %get-tuple-element.208), channel_id=1, source_target_pairs={{0,16},{8,24},{16,0},{24,8},{1,17},{9,25},{17,1},{25,9},{2,18},{10... | collective-permute-start | bytes 1179656 | tf_op jit(solution)/shard_map/ppermute | solution.py:37
  181.0 14.3 %collective-permute-start.51 = (f32[32,32,128]{2,1,0:T(8,128)S(1)}, f32[32,32,128]{2,1,0:T(8,128)S(1)}, u32[]{:S(2)}, u32[]{:S(2)}) collective-permute-start(f32[32,32,128]{2,1,0:T(8,128)S(1)} %constant_dynamic-update-slice_fusion.36.refs_2_), channel_id=1, source_target_pairs={{0,8},{8,0},{16,24},{24,16},{1,9},{9,1},{17,25},{25,17},{2,10},{10... | collective-permute-start | bytes 1572872 | tf_op jit(solution)/shard_map/ppermute | solution.py:37
  182.2 13.8 %collective-permute-start.48 = (f32[32,32,128]{2,1,0:T(8,128)S(1)}, f32[32,32,128]{2,1,0:T(8,128)S(1)}, u32[]{:S(2)}, u32[]{:S(2)}) collective-permute-start(f32[32,32,128]{2,1,0:T(8,128)S(1)} %constant_dynamic-update-slice_fusion.33.refs_1_), channel_id=1, source_target_pairs={{0,4},{4,0},{1,5},{5,1},{2,6},{6,2},{3,7},{7,3},{8,12},{12,8},{9,1... | collective-permute-start | bytes 1572872 | tf_op jit(solution)/shard_map/ppermute | solution.py:37
  183.3 12.6 %collective-permute-start.45 = (f32[32,32,128]{2,1,0:T(8,128)S(1)}, f32[32,32,128]{2,1,0:T(8,128)S(1)}, u32[]{:S(2)}, u32[]{:S(2)}) collective-permute-start(f32[32,32,128]{2,1,0:T(8,128)S(1)} %constant_dynamic-update-slice_fusion.30.refs_0_), channel_id=1, source_target_pairs={{0,2},{2,0},{1,3},{3,1},{4,6},{6,4},{5,7},{7,5},{8,10},{10,8},{9,1... | collective-permute-start | bytes 1572872 | tf_op jit(solution)/shard_map/ppermute | solution.py:37
  200.0 10.7 %collective-permute-start.52 = (f32[32,32,128]{2,1,0:T(8,128)S(1)}, f32[32,32,128]{2,1,0:T(8,128)S(1)}, u32[]{:S(2)}, u32[]{:S(2)}) collective-permute-start(f32[32,32,128]{2,1,0:T(8,128)S(1)} %get-tuple-element.175), channel_id=1, source_target_pairs={{0,2},{2,0},{1,3},{3,1},{4,6},{6,4},{5,7},{7,5},{8,10},{10,8},{9,1... | collective-permute-start | bytes 1572872 | tf_op jit(solution)/shard_map/ppermute | solution.py:37
  202.1 10.6 %collective-permute-start.55 = (f32[32,32,128]{2,1,0:T(8,128)S(1)}, f32[32,32,128]{2,1,0:T(8,128)S(1)}, u32[]{:S(2)}, u32[]{:S(2)}) collective-permute-start(f32[32,32,128]{2,1,0:T(8,128)S(1)} %get-tuple-element.184), channel_id=1, source_target_pairs={{0,4},{4,0},{1,5},{5,1},{2,6},{6,2},{3,7},{7,3},{8,12},{12,8},{9,1... | collective-permute-start | bytes 1572872 | tf_op jit(solution)/shard_map/ppermute | solution.py:37
  203.1 11.0 %collective-permute-start.58 = (f32[32,32,128]{2,1,0:T(8,128)S(1)}, f32[32,32,128]{2,1,0:T(8,128)S(1)}, u32[]{:S(2)}, u32[]{:S(2)}) collective-permute-start(f32[32,32,128]{2,1,0:T(8,128)S(1)} %get-tuple-element.193), channel_id=1, source_target_pairs={{0,8},{8,0},{16,24},{24,16},{1,9},{9,1},{17,25},{25,17},{2,10},{10... | collective-permute-start | bytes 1572872 | tf_op jit(solution)/shard_map/ppermute | solution.py:37
  214.1 7.8 %collective-permute-start.59 = (f32[16,32,128]{2,1,0:T(8,128)S(1)}, f32[16,32,128]{2,1,0:T(8,128)S(1)}, u32[]{:S(2)}, u32[]{:S(2)}) collective-permute-start(f32[16,32,128]{2,1,0:T(8,128)S(1)} %slice_add_fusion), channel_id=1, source_target_pairs={{0,2},{2,0},{1,3},{3,1},{4,6},{6,4},{5,7},{7,5},{8,10},{10,8},{9,1... | collective-permute-start | bytes 786440 | tf_op jit(solution)/shard_map/ppermute | solution.py:37
  217.9 7.8 %collective-permute-start.54 = (f32[8,32,128]{2,1,0:T(8,128)}, f32[8,32,128]{2,1,0:T(8,128)S(1)}, u32[]{:S(2)}, u32[]{:S(2)}) collective-permute-start(f32[8,32,128]{2,1,0:T(8,128)} %slice_add_fusion.15), channel_id=1, source_target_pairs={{0,8},{8,0},{16,24},{24,16},{1,9},{9,1},{17,25},{25,17},{2,10},{10... | collective-permute-start | bytes 393224 | tf_op jit(solution)/shard_map/ppermute | solution.py:37
  230.1 8.7 %collective-permute-start.61 = (f32[12,32,128]{2,1,0:T(8,128)S(1)}, f32[12,32,128]{2,1,0:T(8,128)S(1)}, u32[]{:S(2)}, u32[]{:S(2)}) collective-permute-start(f32[12,32,128]{2,1,0:T(8,128)S(1)} %pad_maximum_fusion.14), channel_id=1, source_target_pairs={{0,16},{8,24},{16,0},{24,8},{1,17},{9,25},{17,1},{25,9},{2,18},{10... | collective-permute-start | bytes 589832 | tf_op jit(solution)/shard_map/ppermute | solution.py:37
  (48 other events, 319.3 us)

commit v21 on v19

--- a/solution.py
+++ b/solution.py
@@ -305,12 +305,15 @@
         [jnp.sum(w * b, axis=(0, 2)) for w, b in zip(heats, blocks)],
         jnp.sum(heats[0] * drives[0], axis=(0, 2)),
     )
-    totals = jnp.pad(jnp.stack([weighted, jnp.full((half,), jnp.sum(heat))]), ((0, 0), (0, size - half)))
-    both = by_core(totals[None], swap(totals[None], cores))
-    both = jnp.broadcast_to(both.reshape(1, 2 * CORES, size), (chips, 2 * CORES, size))
-    both = lax.all_to_all(both, CHIPS, split_axis=0, concat_axis=0, tiled=True)
-    both = jnp.sum(both, axis=0).reshape(CORES, 2, size)[:, :, :half]
-    conductivity = both[:, 0].reshape(columns) / jnp.sum(both[:, 1, 0])
+    totals = jnp.concatenate([weighted, jnp.sum(heat).reshape(1)])
+    totals = jnp.pad(totals[None], ((0, 0), (0, size - half - 1)))
+    *blocks, totals = lax.optimization_barrier((*blocks, totals))
+    totals = lax.all_to_all(
+        jnp.broadcast_to(totals, (chips, size)), CHIPS, split_axis=0, concat_axis=0, tiled=True
+    )
+    totals = jnp.sum(totals, axis=0, keepdims=True)
+    totals = by_core(totals, swap(totals, cores))
+    conductivity = totals[:, :half].reshape(columns) / jnp.sum(totals[:, half])
     flux = relaxes[0] * (drives[0] + after(reduce_far(blocks), conductivity))
     first, second = flux[:per], flux[per:]
     mine = jnp.where(core == 0, first, second)

time: 256 us -> 261 us (1.020)
  waiting for transfers between devices: 127 us -> 115 us
  starting transfers between devices: 60.2 us -> 65.3 us
  other arithmetic: 6.62 us -> 11.7 us
  local copies, waits for them, and re-layouts: 2.84 us -> 5.72 us
    ppermute x64, waiting for transfers between devices: 127 us -> 115 us  [swap(): lax.ppermute(array, axis, [(i, i ^ distance) for i in range(lax.axis_size...]
    add x18, other arithmetic: 0.57 us -> 6.15 us  [reduce_near(): sum([halves(t)[1] for t in terms[1:]], halves(terms[0])[1])]
    ppermute x64, starting transfers between devices: 60.2 us -> 65.3 us  [swap(): lax.ppermute(array, axis, [(i, i ^ distance) for i in range(lax.axis_size...]
    slice x20 -> x18, local copies, waits for them, and re-layouts: 0.31 us -> 3.19 us  [halves(): return (array[:middle], array[middle:])]
  transfers between devices with their start and end apart: 64 -> 64, of which waited for: 50 -> 45; matrix products, arithmetic and copies ran while one was open for 2% -> 6% of each run, Pallas kernels for 12% -> 13%
where the time goes in v21:
time: 261 us; the launch traced here: 259 us
  waiting for transfers between devices  115 us (44%)
  starting transfers between devices  65.3 us (25%)
  Pallas kernels  47.2 us (18%)
  other arithmetic  11.7 us (4%)
  blocking collectives  11.7 us (4%)
  local copies, waits for them, and re-layouts  5.72 us (2%)
    ppermute x64, waiting for transfers between devices, swap(): lax.ppermute(array, axis, [(i, i ^ distance) for i in range(lax.axis_size...  115 us
    ppermute x64, starting transfers between devices, swap(): lax.ppermute(array, axis, [(i, i ^ distance) for i in range(lax.axis_size...  65.3 us
    pallas_call x9, Pallas kernels, apply_tiles(): pl.pallas_call(functools.partial(apply_kernel, span, skip, len(flux), bas...  47.2 us
    all_to_all x1, blocking collectives, shards(): lax.all_to_all(jnp.broadcast_to(totals, (chips, size)), CHIPS, split_axis...  11.7 us
    add x18, other arithmetic, reduce_near(): sum([halves(t)[1] for t in terms[1:]], halves(terms[0])[1])  6.15 us
  transfers between devices with their start and end apart: 64, of which 45 were waited for; matrix products, arithmetic and copies ran while one was open for 6% of the time, Pallas kernels for 13%

profile of v21, /device:TPU:0, one launch (start us, length us, event | category | flops | bytes accessed | tf_op | source)
XLA Modules:
  0.0 259.2 jit_solution(13859019951515086469)
XLA Ops:
  2.6 3.7 %collective-permute-start.1 = (f32[6,2,128]{2,1,0:T(2,128)S(1)}, f32[6,2,128]{2,1,0:T(2,128)S(1)}, u32[]{:S(2)}, u32[]{:S(2)}) collective-permute-start(f32[6,2,128]{2,1,0:T(2,128)S(1)} %pad_maximum_fusion.25), channel_id=1, source_target_pairs={{0,16},{8,24},{16,0},{24,8},{1,17},{9,25},{17,1},{25,9},{2,18},{10... | collective-permute-start | bytes 18440 | tf_op jit(solution)/shard_map/ppermute | solution.py:37
  7.9 10.5 %collective-permute-done = f32[6,64,128]{2,1,0:T(8,128)S(1)} collective-permute-done((f32[6,64,128]{2,1,0:T(8,128)S(1)}, f32[6,64,128]{2,1,0:T(8,128)S(1)}, u32[]{:S(2)}, u32[]{:S(2)}) %collective-permute-start) | collective-permute-done | bytes 196640 | tf_op jit(solution)/shard_map/ppermute | solution.py:37
  24.0 2.4 collective-permute-done.11
  29.8 4.3 %collective-permute-done.12 = f32[16,32,128]{2,1,0:T(8,128)S(1)} collective-permute-done((f32[16,32,128]{2,1,0:T(8,128)S(1)}, f32[16,32,128]{2,1,0:T(8,128)S(1)}, u32[]{:S(2)}, u32[]{:S(2)}) %collective-permute-start.12) | collective-permute-done | bytes 262176 | tf_op jit(solution)/shard_map/ppermute | solution.py:37
  38.0 7.3 %shard_map.95 = (f32[96,32,128]{2,1,0:T(8,128)S(1)}, f32[96,32,128]{2,1,0:T(8,128)S(1)}) custom-call(s32[772]{0:T(1024)S(1)} %pad_add_fusion.places_ref, f32[128,128,128]{2,1,0:T(8,128)} %own_ref.17, f32[128,128,128]{2,1,0:T(8,128)} %collective-permute-done.4.other_ref, f32[32,32,128]{2,1,0:T(8,128)S(1)} %constant_dynamic-update-slice_fusion.refs_0_, ...), custom_call_target="tpu_custom_call" | custom-call | flops 536870912 | bytes 14680064 | tf_op jit(solution)/shard_map/pallas_call | solution.py:188
  48.8 4.0 %shard_map.97 = (f32[32,32,128]{2,1,0:T(8,128)S(1)}, f32[32,32,128]{2,1,0:T(8,128)S(1)}, f32[32,32,128]{2,1,0:T(8,128)S(1)}) custom-call(s32[772]{0:T(1024)S(1)} %pad_add_fusion.places_ref, f32[128,128,128]{2,1,0:T(8,128)} %own_ref.17, f32[128,128,128]{2,1,0:T(8,128)} %collective-permute-done.4.other_ref, f32[32,32,128]{2,1,0:T(8,128)S(1)} %collective-permute-done.7.refs_0_, ...), custom_call_target="tpu_custom_call" | custom-call | flops 268435456 | bytes 7340032 | tf_op jit(solution)/shard_map/pallas_call | solution.py:188
  56.0 4.0 %shard_map.96 = (f32[32,32,128]{2,1,0:T(8,128)S(1)}, f32[32,32,128]{2,1,0:T(8,128)S(1)}, f32[32,32,128]{2,1,0:T(8,128)S(1)}) custom-call(s32[772]{0:T(1024)S(1)} %pad_add_fusion.places_ref, f32[128,128,128]{2,1,0:T(8,128)} %own_ref.17, f32[128,128,128]{2,1,0:T(8,128)} %collective-permute-done.4.other_ref, f32[32,32,128]{2,1,0:T(8,128)S(1)} %collective-permute-done.7.refs_0_, ...), custom_call_target="tpu_custom_call" | custom-call | flops 268435456 | bytes 7340032 | tf_op jit(solution)/shard_map/pallas_call | solution.py:188
  60.1 3.6 %collective-permute-done.20 = f32[32,32,128]{2,1,0:T(8,128)S(1)} collective-permute-done((f32[32,32,128]{2,1,0:T(8,128)S(1)}, f32[32,32,128]{2,1,0:T(8,128)S(1)}, u32[]{:S(2)}, u32[]{:S(2)}) %collective-permute-start.20) | collective-permute-done | bytes 524320 | tf_op jit(solution)/shard_map/ppermute | solution.py:37
  72.1 2.1 collective-permute-start.19
  77.1 4.0 %collective-permute-done.16 = f32[8,32,128]{2,1,0:T(8,128)S(1)} collective-permute-done((f32[8,32,128]{2,1,0:T(8,128)S(1)}, f32[8,32,128]{2,1,0:T(8,128)S(1)}, u32[]{:S(2)}, u32[]{:S(2)}) %collective-permute-start.16) | collective-permute-done | bytes 131104 | tf_op jit(solution)/shard_map/ppermute | solution.py:37
  81.4 12.8 %collective-permute-done.23 = f32[24,32,128]{2,1,0:T(8,128)S(1)} collective-permute-done((f32[24,32,128]{2,1,0:T(8,128)S(1)}, f32[24,32,128]{2,1,0:T(8,128)S(1)}, u32[]{:S(2)}, u32[]{:S(2)}) %collective-permute-start.23) | collective-permute-done | bytes 393248 | tf_op jit(solution)/shard_map/ppermute | solution.py:37
  96.8 3.7 %collective-permute-done.30 = f32[8,32,128]{2,1,0:T(8,128)S(1)} collective-permute-done((f32[8,32,128]{2,1,0:T(8,128)S(1)}, f32[8,32,128]{2,1,0:T(8,128)S(1)}, u32[]{:S(2)}, u32[]{:S(2)}) %collective-permute-start.30) | collective-permute-done | bytes 131104 | tf_op jit(solution)/shard_map/ppermute | solution.py:37
  103.3 5.2 %collective-permute-done.31 = f32[16,32,128]{2,1,0:T(8,128)S(1)} collective-permute-done((f32[16,32,128]{2,1,0:T(8,128)S(1)}, f32[16,32,128]{2,1,0:T(8,128)S(1)}, u32[]{:S(2)}, u32[]{:S(2)}) %collective-permute-start.31) | collective-permute-done | bytes 262176 | tf_op jit(solution)/shard_map/ppermute | solution.py:37
  112.9 7.3 %shard_map.98 = (f32[96,32,128]{2,1,0:T(8,128)S(1)}, f32[96,32,128]{2,1,0:T(8,128)S(1)}) custom-call(s32[772]{0:T(1024)S(1)} %pad_add_fusion.places_ref, f32[128,128,128]{2,1,0:T(8,128)} %own_ref.17, f32[128,128,128]{2,1,0:T(8,128)} %collective-permute-done.4.other_ref, f32[32,32,128]{2,1,0:T(8,128)S(1)} %constant_dynamic-update-slice_fusion.15.refs_0_, ...), custom_call_target="tpu_custom_call" | custom-call | flops 536870912 | bytes 14680064 | tf_op jit(solution)/shard_map/pallas_call | solution.py:188
  121.6 4.0 %shard_map.100 = (f32[32,32,128]{2,1,0:T(8,128)S(1)}, f32[32,32,128]{2,1,0:T(8,128)S(1)}, f32[32,32,128]{2,1,0:T(8,128)S(1)}) custom-call(s32[772]{0:T(1024)S(1)} %pad_add_fusion.places_ref, f32[128,128,128]{2,1,0:T(8,128)} %own_ref.17, f32[128,128,128]{2,1,0:T(8,128)} %collective-permute-done.4.other_ref, ...), custom_call_target="tpu_custom_call" | custom-call | flops 268435456 | bytes 7340032 | tf_op jit(solution)/shard_map/pallas_call | solution.py:188
  128.5 4.2 %shard_map.99 = (f32[32,32,128]{2,1,0:T(8,128)S(1)}, f32[32,32,128]{2,1,0:T(8,128)S(1)}, f32[32,32,128]{2,1,0:T(8,128)S(1)}) custom-call(s32[772]{0:T(1024)S(1)} %pad_add_fusion.places_ref, f32[128,128,128]{2,1,0:T(8,128)} %own_ref.17, f32[128,128,128]{2,1,0:T(8,128)} %collective-permute-done.4.other_ref, ...), custom_call_target="tpu_custom_call" | custom-call | flops 268435456 | bytes 7340032 | tf_op jit(solution)/shard_map/pallas_call | solution.py:188
  132.6 5.0 %collective-permute-done.39 = f32[32,32,128]{2,1,0:T(8,128)S(1)} collective-permute-done((f32[32,32,128]{2,1,0:T(8,128)S(1)}, f32[32,32,128]{2,1,0:T(8,128)S(1)}, u32[]{:S(2)}, u32[]{:S(2)}) %collective-permute-start.39) | collective-permute-done | bytes 524320 | tf_op jit(solution)/shard_map/ppermute | solution.py:37
  141.4 2.8 %collective-permute-done.40 = f32[16,32,128]{2,1,0:T(8,128)S(1)} collective-permute-done((f32[16,32,128]{2,1,0:T(8,128)S(1)}, f32[16,32,128]{2,1,0:T(8,128)S(1)}, u32[]{:S(2)}, u32[]{:S(2)}) %collective-permute-start.40) | collective-permute-done | bytes 262176 | tf_op jit(solution)/shard_map/ppermute | solution.py:37
  144.4 3.6 %collective-permute-done.37 = f32[16,32,128]{2,1,0:T(8,128)S(1)} collective-permute-done((f32[16,32,128]{2,1,0:T(8,128)S(1)}, f32[16,32,128]{2,1,0:T(8,128)S(1)}, u32[]{:S(2)}, u32[]{:S(2)}) %collective-permute-start.37) | collective-permute-done | bytes 262176 | tf_op jit(solution)/shard_map/ppermute | solution.py:37
  149.4 2.1 collective-permute-start.35
  154.6 2.9 %collective-permute-start.42 = (f32[24,32,128]{2,1,0:T(8,128)S(1)}, f32[24,32,128]{2,1,0:T(8,128)S(1)}, u32[]{:S(2)}, u32[]{:S(2)}) collective-permute-start(f32[24,32,128]{2,1,0:T(8,128)S(1)} %get-tuple-element.210), channel_id=1, source_target_pairs={{0,16},{8,24},{16,0},{24,8},{1,17},{9,25},{17,1},{25,9},{2,18},{10... | collective-permute-start | bytes 1179656 | tf_op jit(solution)/shard_map/ppermute | solution.py:37
  157.6 9.3 %collective-permute-done.42 = f32[24,32,128]{2,1,0:T(8,128)S(1)} collective-permute-done((f32[24,32,128]{2,1,0:T(8,128)S(1)}, f32[24,32,128]{2,1,0:T(8,128)S(1)}, u32[]{:S(2)}, u32[]{:S(2)}) %collective-permute-start.42) | collective-permute-done | bytes 393248 | tf_op jit(solution)/shard_map/ppermute | solution.py:37
  167.1 2.5 collective-permute-start.49
  170.2 3.8 %collective-permute-done.49 = f32[8,32,128]{2,1,0:T(8,128)S(1)} collective-permute-done((f32[8,32,128]{2,1,0:T(8,128)S(1)}, f32[8,32,128]{2,1,0:T(8,128)S(1)}, u32[]{:S(2)}, u32[]{:S(2)}) %collective-permute-start.49) | collective-permute-done | bytes 131104 | tf_op jit(solution)/shard_map/ppermute | solution.py:37
  184.8 7.3 %shard_map.101 = (f32[96,32,128]{2,1,0:T(8,128)S(1)}, f32[96,32,128]{2,1,0:T(8,128)S(1)}) custom-call(s32[772]{0:T(1024)S(1)} %pad_add_fusion.places_ref, f32[128,128,128]{2,1,0:T(8,128)} %own_ref.17, f32[128,128,128]{2,1,0:T(8,128)} %collective-permute-done.4.other_ref, f32[32,32,128]{2,1,0:T(8,128)S(1)} %constant_dynamic-update-slice_fusion.30.refs_0_, ...), custom_call_target="tpu_custom_call" | custom-call | flops 536870912 | bytes 14680064 | tf_op jit(solution)/shard_map/pallas_call | solution.py:188
  193.2 3.0 %collective-permute-done.48.refs_1_ = f32[32,32,128]{2,1,0:T(8,128)S(1)} collective-permute-done((f32[32,32,128]{2,1,0:T(8,128)S(1)}, f32[32,32,128]{2,1,0:T(8,128)S(1)}, u32[]{:S(2)}, u32[]{:S(2)}) %collective-permute-start.48) | collective-permute-done | bytes 524320 | tf_op jit(solution)/shard_map/ppermute | solution.py:37
  197.2 5.1 %shard_map.103 = (f32[32,32,128]{2,1,0:T(8,128)}, f32[32,32,128]{2,1,0:T(8,128)}, f32[32,32,128]{2,1,0:T(8,128)}) custom-call(s32[772]{0:T(1024)S(1)} %pad_add_fusion.places_ref, f32[128,128,128]{2,1,0:T(8,128)} %own_ref.17, f32[128,128,128]{2,1,0:T(8,128)} %collective-permute-done.4.other_ref, f32[32,32,128]{2,1,0:T(8,128)S(1)} %collective-permute-done.45.refs_0_, ...), custom_call_target="tpu_custom_call" | custom-call | flops 268435456 | bytes 7340032 | tf_op jit(solution)/shard_map/pallas_call | solution.py:188
  202.3 2.5 collective-permute-start.52
  205.5 4.0 %shard_map.102 = (f32[32,32,128]{2,1,0:T(8,128)S(1)}, f32[32,32,128]{2,1,0:T(8,128)S(1)}, f32[32,32,128]{2,1,0:T(8,128)S(1)}) custom-call(s32[772]{0:T(1024)S(1)} %pad_add_fusion.places_ref, f32[128,128,128]{2,1,0:T(8,128)} %own_ref.17, f32[128,128,128]{2,1,0:T(8,128)} %collective-permute-done.4.other_ref, ...), custom_call_target="tpu_custom_call" | custom-call | flops 268435456 | bytes 7340032 | tf_op jit(solution)/shard_map/pallas_call | solution.py:188
  209.5 4.2 %collective-permute-done.52 = f32[32,32,128]{2,1,0:T(8,128)} collective-permute-done((f32[32,32,128]{2,1,0:T(8,128)}, f32[32,32,128]{2,1,0:T(8,128)}, u32[]{:S(2)}, u32[]{:S(2)}) %collective-permute-start.52) | collective-permute-done | bytes 524320 | tf_op jit(solution)/shard_map/ppermute | solution.py:37
  232.7 11.7 %all_to_all.6 = f32[16,1,128]{2,1,0:T(1,128)S(1)} all-to-all(f32[16,1,128]{2,1,0:T(1,128)S(1)} %broadcast_in_dim.63), channel_id=1, replica_groups=mesh['z'=4,'y'=2,'x'=2,'core'=2] {'z','y','x'}, dimensions={0} | all-to-all | bytes 16384 | tf_op jit(solution)/shard_map/all_to_all | solution.py:311
  247.6 9.4 %collective-permute-done.61 = f32[12,32,128]{2,1,0:T(8,128)S(1)} collective-permute-done((f32[12,32,128]{2,1,0:T(8,128)S(1)}, f32[12,32,128]{2,1,0:T(8,128)S(1)}, u32[]{:S(2)}, u32[]{:S(2)}) %collective-permute-start.61) | collective-permute-done | bytes 196640 | tf_op jit(solution)/shard_map/ppermute | solution.py:37
  (272 shorter events, 94.4 us)
Async XLA Ops:
  0.7 20.0 %collective-permute-start.4 = (f32[128,128,128]{2,1,0:T(8,128)}, f32[128,128,128]{2,1,0:T(8,128)}, u32[]{:S(2)}, u32[]{:S(2)}) collective-permute-start(f32[128,128,128]{2,1,0:T(8,128)} %own_ref.17), channel_id=1, source_target_pairs={{0,1},{1,0},{2,3},{3,2},{4,5},{5,4},{6,7},{7,6},{8,9},{9,8},{10,11... | collective-permute-start | bytes 25165832 | tf_op jit(solution)/shard_map/ppermute | solution.py:37
  6.3 12.2 %collective-permute-start = (f32[6,64,128]{2,1,0:T(8,128)S(1)}, f32[6,64,128]{2,1,0:T(8,128)S(1)}, u32[]{:S(2)}, u32[]{:S(2)}) collective-permute-start(f32[6,64,128]{2,1,0:T(8,128)S(1)} %bitcast_bitcast_fusion), channel_id=1, source_target_pairs={{0,16},{8,24},{16,0},{24,8},{1,17},{9,25},{17,1},{25,9},{2,18},{10... | collective-permute-start | bytes 589832 | tf_op jit(solution)/shard_map/ppermute | solution.py:37
  26.4 7.7 %collective-permute-start.12 = (f32[16,32,128]{2,1,0:T(8,128)S(1)}, f32[16,32,128]{2,1,0:T(8,128)S(1)}, u32[]{:S(2)}, u32[]{:S(2)}) collective-permute-start(f32[16,32,128]{2,1,0:T(8,128)S(1)} %pad_maximum_fusion.3), channel_id=1, source_target_pairs={{0,2},{2,0},{1,3},{3,1},{4,6},{6,4},{5,7},{7,5},{8,10},{10,8},{9,1... | collective-permute-start | bytes 786440 | tf_op jit(solution)/shard_map/ppermute | solution.py:37
  29.1 8.1 %collective-permute-start.6 = (f32[16,32,128]{2,1,0:T(8,128)S(1)}, f32[16,32,128]{2,1,0:T(8,128)S(1)}, u32[]{:S(2)}, u32[]{:S(2)}) collective-permute-start(f32[16,32,128]{2,1,0:T(8,128)S(1)} %pad_maximum_fusion.1), channel_id=1, source_target_pairs={{0,4},{4,0},{1,5},{5,1},{2,6},{6,2},{3,7},{7,3},{8,12},{12,8},{9,1... | collective-permute-start | bytes 786440 | tf_op jit(solution)/shard_map/ppermute | solution.py:37
  34.1 12.5 %collective-permute-start.13 = (f32[32,32,128]{2,1,0:T(8,128)S(1)}, f32[32,32,128]{2,1,0:T(8,128)S(1)}, u32[]{:S(2)}, u32[]{:S(2)}) collective-permute-start(f32[32,32,128]{2,1,0:T(8,128)S(1)} %constant_dynamic-update-slice_fusion.6.refs_2_), channel_id=1, source_target_pairs={{0,8},{8,0},{16,24},{24,16},{1,9},{9,1},{17,25},{25,17},{2,10},{10... | collective-permute-start | bytes 1572872 | tf_op jit(solution)/shard_map/ppermute | solution.py:37
  35.5 12.0 %collective-permute-start.10 = (f32[32,32,128]{2,1,0:T(8,128)S(1)}, f32[32,32,128]{2,1,0:T(8,128)S(1)}, u32[]{:S(2)}, u32[]{:S(2)}) collective-permute-start(f32[32,32,128]{2,1,0:T(8,128)S(1)} %constant_dynamic-update-slice_fusion.3.refs_1_), channel_id=1, source_target_pairs={{0,4},{4,0},{1,5},{5,1},{2,6},{6,2},{3,7},{7,3},{8,12},{12,8},{9,1... | collective-permute-start | bytes 1572872 | tf_op jit(solution)/shard_map/ppermute | solution.py:37
  37.1 11.7 %collective-permute-start.7 = (f32[32,32,128]{2,1,0:T(8,128)S(1)}, f32[32,32,128]{2,1,0:T(8,128)S(1)}, u32[]{:S(2)}, u32[]{:S(2)}) collective-permute-start(f32[32,32,128]{2,1,0:T(8,128)S(1)} %constant_dynamic-update-slice_fusion.refs_0_), channel_id=1, source_target_pairs={{0,2},{2,0},{1,3},{3,1},{4,6},{6,4},{5,7},{7,5},{8,10},{10,8},{9,1... | collective-permute-start | bytes 1572872 | tf_op jit(solution)/shard_map/ppermute | solution.py:37
  52.9 10.8 %collective-permute-start.20 = (f32[32,32,128]{2,1,0:T(8,128)S(1)}, f32[32,32,128]{2,1,0:T(8,128)S(1)}, u32[]{:S(2)}, u32[]{:S(2)}) collective-permute-start(f32[32,32,128]{2,1,0:T(8,128)S(1)} %get-tuple-element.130), channel_id=1, source_target_pairs={{0,8},{8,0},{16,24},{24,16},{1,9},{9,1},{17,25},{25,17},{2,10},{10... | collective-permute-start | bytes 1572872 | tf_op jit(solution)/shard_map/ppermute | solution.py:37
  53.7 11.8 %collective-permute-start.17 = (f32[32,32,128]{2,1,0:T(8,128)S(1)}, f32[32,32,128]{2,1,0:T(8,128)S(1)}, u32[]{:S(2)}, u32[]{:S(2)}) collective-permute-start(f32[32,32,128]{2,1,0:T(8,128)S(1)} %get-tuple-element.121), channel_id=1, source_target_pairs={{0,4},{4,0},{1,5},{5,1},{2,6},{6,2},{3,7},{7,3},{8,12},{12,8},{9,1... | collective-permute-start | bytes 1572872 | tf_op jit(solution)/shard_map/ppermute | solution.py:37
  54.7 12.9 %collective-permute-start.14 = (f32[32,32,128]{2,1,0:T(8,128)S(1)}, f32[32,32,128]{2,1,0:T(8,128)S(1)}, u32[]{:S(2)}, u32[]{:S(2)}) collective-permute-start(f32[32,32,128]{2,1,0:T(8,128)S(1)} %get-tuple-element.112), channel_id=1, source_target_pairs={{0,2},{2,0},{1,3},{3,1},{4,6},{6,4},{5,7},{7,5},{8,10},{10,8},{9,1... | collective-permute-start | bytes 1572872 | tf_op jit(solution)/shard_map/ppermute | solution.py:37
  81.3 13.0 %collective-permute-start.23 = (f32[24,32,128]{2,1,0:T(8,128)S(1)}, f32[24,32,128]{2,1,0:T(8,128)S(1)}, u32[]{:S(2)}, u32[]{:S(2)}) collective-permute-start(f32[24,32,128]{2,1,0:T(8,128)S(1)} %get-tuple-element.222), channel_id=1, source_target_pairs={{0,16},{8,24},{16,0},{24,8},{1,17},{9,25},{17,1},{25,9},{2,18},{10... | collective-permute-start | bytes 1179656 | tf_op jit(solution)/shard_map/ppermute | solution.py:37
  100.5 7.9 %collective-permute-start.31 = (f32[16,32,128]{2,1,0:T(8,128)S(1)}, f32[16,32,128]{2,1,0:T(8,128)S(1)}, u32[]{:S(2)}, u32[]{:S(2)}) collective-permute-start(f32[16,32,128]{2,1,0:T(8,128)S(1)} %pad_maximum_fusion.6), channel_id=1, source_target_pairs={{0,2},{2,0},{1,3},{3,1},{4,6},{6,4},{5,7},{7,5},{8,10},{10,8},{9,1... | collective-permute-start | bytes 786440 | tf_op jit(solution)/shard_map/ppermute | solution.py:37
  101.3 9.3 %collective-permute-start.28 = (f32[16,32,128]{2,1,0:T(8,128)S(1)}, f32[16,32,128]{2,1,0:T(8,128)S(1)}, u32[]{:S(2)}, u32[]{:S(2)}) collective-permute-start(f32[16,32,128]{2,1,0:T(8,128)S(1)} %pad_maximum_fusion.5), channel_id=1, source_target_pairs={{0,8},{8,0},{16,24},{24,16},{1,9},{9,1},{17,25},{25,17},{2,10},{10... | collective-permute-start | bytes 786440 | tf_op jit(solution)/shard_map/ppermute | solution.py:37
  102.8 9.5 %collective-permute-start.25 = (f32[16,32,128]{2,1,0:T(8,128)S(1)}, f32[16,32,128]{2,1,0:T(8,128)S(1)}, u32[]{:S(2)}, u32[]{:S(2)}) collective-permute-start(f32[16,32,128]{2,1,0:T(8,128)S(1)} %pad_maximum_fusion.4), channel_id=1, source_target_pairs={{0,4},{4,0},{1,5},{5,1},{2,6},{6,2},{3,7},{7,3},{8,12},{12,8},{9,1... | collective-permute-start | bytes 786440 | tf_op jit(solution)/shard_map/ppermute | solution.py:37
  108.5 11.7 %collective-permute-start.32 = (f32[32,32,128]{2,1,0:T(8,128)S(1)}, f32[32,32,128]{2,1,0:T(8,128)S(1)}, u32[]{:S(2)}, u32[]{:S(2)}) collective-permute-start(f32[32,32,128]{2,1,0:T(8,128)S(1)} %constant_dynamic-update-slice_fusion.21.refs_2_), channel_id=1, source_target_pairs={{0,8},{8,0},{16,24},{24,16},{1,9},{9,1},{17,25},{25,17},{2,10},{10... | collective-permute-start | bytes 1572872 | tf_op jit(solution)/shard_map/ppermute | solution.py:37
  110.7 9.5 %collective-permute-start.29 = (f32[32,32,128]{2,1,0:T(8,128)S(1)}, f32[32,32,128]{2,1,0:T(8,128)S(1)}, u32[]{:S(2)}, u32[]{:S(2)}) collective-permute-start(f32[32,32,128]{2,1,0:T(8,128)S(1)} %constant_dynamic-update-slice_fusion.18.refs_1_), channel_id=1, source_target_pairs={{0,4},{4,0},{1,5},{5,1},{2,6},{6,2},{3,7},{7,3},{8,12},{12,8},{9,1... | collective-permute-start | bytes 1572872 | tf_op jit(solution)/shard_map/ppermute | solution.py:37
  112.3 9.2 %collective-permute-start.26 = (f32[32,32,128]{2,1,0:T(8,128)S(1)}, f32[32,32,128]{2,1,0:T(8,128)S(1)}, u32[]{:S(2)}, u32[]{:S(2)}) collective-permute-start(f32[32,32,128]{2,1,0:T(8,128)S(1)} %constant_dynamic-update-slice_fusion.15.refs_0_), channel_id=1, source_target_pairs={{0,2},{2,0},{1,3},{3,1},{4,6},{6,4},{5,7},{7,5},{8,10},{10,8},{9,1... | collective-permute-start | bytes 1572872 | tf_op jit(solution)/shard_map/ppermute | solution.py:37
  125.6 12.1 %collective-permute-start.39 = (f32[32,32,128]{2,1,0:T(8,128)S(1)}, f32[32,32,128]{2,1,0:T(8,128)S(1)}, u32[]{:S(2)}, u32[]{:S(2)}) collective-permute-start(f32[32,32,128]{2,1,0:T(8,128)S(1)} %get-tuple-element.162), channel_id=1, source_target_pairs={{0,8},{8,0},{16,24},{24,16},{1,9},{9,1},{17,25},{25,17},{2,10},{10... | collective-permute-start | bytes 1572872 | tf_op jit(solution)/shard_map/ppermute | solution.py:37
  126.1 13.4 %collective-permute-start.36 = (f32[32,32,128]{2,1,0:T(8,128)S(1)}, f32[32,32,128]{2,1,0:T(8,128)S(1)}, u32[]{:S(2)}, u32[]{:S(2)}) collective-permute-start(f32[32,32,128]{2,1,0:T(8,128)S(1)} %get-tuple-element.153), channel_id=1, source_target_pairs={{0,4},{4,0},{1,5},{5,1},{2,6},{6,2},{3,7},{7,3},{8,12},{12,8},{9,1... | collective-permute-start | bytes 1572872 | tf_op jit(solution)/shard_map/ppermute | solution.py:37
  127.7 13.4 %collective-permute-start.33 = (f32[32,32,128]{2,1,0:T(8,128)S(1)}, f32[32,32,128]{2,1,0:T(8,128)S(1)}, u32[]{:S(2)}, u32[]{:S(2)}) collective-permute-start(f32[32,32,128]{2,1,0:T(8,128)S(1)} %get-tuple-element.144), channel_id=1, source_target_pairs={{0,2},{2,0},{1,3},{3,1},{4,6},{6,4},{5,7},{7,5},{8,10},{10,8},{9,1... | collective-permute-start | bytes 1572872 | tf_op jit(solution)/shard_map/ppermute | solution.py:37
  139.5 8.5 %collective-permute-start.37 = (f32[16,32,128]{2,1,0:T(8,128)S(1)}, f32[16,32,128]{2,1,0:T(8,128)S(1)}, u32[]{:S(2)}, u32[]{:S(2)}) collective-permute-start(f32[16,32,128]{2,1,0:T(8,128)S(1)} %slice_add_fusion.4), channel_id=1, source_target_pairs={{0,8},{8,0},{16,24},{24,16},{1,9},{9,1},{17,25},{25,17},{2,10},{10... | collective-permute-start | bytes 786440 | tf_op jit(solution)/shard_map/ppermute | solution.py:37
  141.1 8.2 %collective-permute-start.34 = (f32[16,32,128]{2,1,0:T(8,128)S(1)}, f32[16,32,128]{2,1,0:T(8,128)S(1)}, u32[]{:S(2)}, u32[]{:S(2)}) collective-permute-start(f32[16,32,128]{2,1,0:T(8,128)S(1)} %slice_add_fusion.5), channel_id=1, source_target_pairs={{0,4},{4,0},{1,5},{5,1},{2,6},{6,2},{3,7},{7,3},{8,12},{12,8},{9,1... | collective-permute-start | bytes 786440 | tf_op jit(solution)/shard_map/ppermute | solution.py:37
  144.2 7.5 %collective-permute-start.41 = (f32[8,32,128]{2,1,0:T(8,128)S(1)}, f32[8,32,128]{2,1,0:T(8,128)S(1)}, u32[]{:S(2)}, u32[]{:S(2)}) collective-permute-start(f32[8,32,128]{2,1,0:T(8,128)S(1)} %slice_add_fusion.16), channel_id=1, source_target_pairs={{0,4},{4,0},{1,5},{5,1},{2,6},{6,2},{3,7},{7,3},{8,12},{12,8},{9,1... | collective-permute-start | bytes 393224 | tf_op jit(solution)/shard_map/ppermute | solution.py:37
  154.6 12.3 %collective-permute-start.42 = (f32[24,32,128]{2,1,0:T(8,128)S(1)}, f32[24,32,128]{2,1,0:T(8,128)S(1)}, u32[]{:S(2)}, u32[]{:S(2)}) collective-permute-start(f32[24,32,128]{2,1,0:T(8,128)S(1)} %get-tuple-element.210), channel_id=1, source_target_pairs={{0,16},{8,24},{16,0},{24,8},{1,17},{9,25},{17,1},{25,9},{2,18},{10... | collective-permute-start | bytes 1179656 | tf_op jit(solution)/shard_map/ppermute | solution.py:37
  180.5 12.7 %collective-permute-start.51 = (f32[32,32,128]{2,1,0:T(8,128)S(1)}, f32[32,32,128]{2,1,0:T(8,128)S(1)}, u32[]{:S(2)}, u32[]{:S(2)}) collective-permute-start(f32[32,32,128]{2,1,0:T(8,128)S(1)} %constant_dynamic-update-slice_fusion.36.refs_2_), channel_id=1, source_target_pairs={{0,8},{8,0},{16,24},{24,16},{1,9},{9,1},{17,25},{25,17},{2,10},{10... | collective-permute-start | bytes 1572872 | tf_op jit(solution)/shard_map/ppermute | solution.py:37
  182.6 13.6 %collective-permute-start.48 = (f32[32,32,128]{2,1,0:T(8,128)S(1)}, f32[32,32,128]{2,1,0:T(8,128)S(1)}, u32[]{:S(2)}, u32[]{:S(2)}) collective-permute-start(f32[32,32,128]{2,1,0:T(8,128)S(1)} %constant_dynamic-update-slice_fusion.33.refs_1_), channel_id=1, source_target_pairs={{0,4},{4,0},{1,5},{5,1},{2,6},{6,2},{3,7},{7,3},{8,12},{12,8},{9,1... | collective-permute-start | bytes 1572872 | tf_op jit(solution)/shard_map/ppermute | solution.py:37
  183.0 14.2 %collective-permute-start.45 = (f32[32,32,128]{2,1,0:T(8,128)S(1)}, f32[32,32,128]{2,1,0:T(8,128)S(1)}, u32[]{:S(2)}, u32[]{:S(2)}) collective-permute-start(f32[32,32,128]{2,1,0:T(8,128)S(1)} %constant_dynamic-update-slice_fusion.30.refs_0_), channel_id=1, source_target_pairs={{0,2},{2,0},{1,3},{3,1},{4,6},{6,4},{5,7},{7,5},{8,10},{10,8},{9,1... | collective-permute-start | bytes 1572872 | tf_op jit(solution)/shard_map/ppermute | solution.py:37
  202.3 11.4 %collective-permute-start.52 = (f32[32,32,128]{2,1,0:T(8,128)}, f32[32,32,128]{2,1,0:T(8,128)}, u32[]{:S(2)}, u32[]{:S(2)}) collective-permute-start(f32[32,32,128]{2,1,0:T(8,128)} %get-tuple-element.176), channel_id=1, source_target_pairs={{0,2},{2,0},{1,3},{3,1},{4,6},{6,4},{5,7},{7,5},{8,10},{10,8},{9,1... | collective-permute-start | bytes 1572872 | tf_op jit(solution)/shard_map/ppermute | solution.py:37
  204.8 10.9 %collective-permute-start.55 = (f32[32,32,128]{2,1,0:T(8,128)}, f32[32,32,128]{2,1,0:T(8,128)}, u32[]{:S(2)}, u32[]{:S(2)}) collective-permute-start(f32[32,32,128]{2,1,0:T(8,128)} %get-tuple-element.185), channel_id=1, source_target_pairs={{0,4},{4,0},{1,5},{5,1},{2,6},{6,2},{3,7},{7,3},{8,12},{12,8},{9,1... | collective-permute-start | bytes 1572872 | tf_op jit(solution)/shard_map/ppermute | solution.py:37
  204.8 13.3 %collective-permute-start.58 = (f32[32,32,128]{2,1,0:T(8,128)}, f32[32,32,128]{2,1,0:T(8,128)}, u32[]{:S(2)}, u32[]{:S(2)}) collective-permute-start(f32[32,32,128]{2,1,0:T(8,128)} %get-tuple-element.194), channel_id=1, source_target_pairs={{0,8},{8,0},{16,24},{24,16},{1,9},{9,1},{17,25},{25,17},{2,10},{10... | collective-permute-start | bytes 1572872 | tf_op jit(solution)/shard_map/ppermute | solution.py:37
  222.1 9.3 %collective-permute-start.54 = (f32[8,32,128]{2,1,0:T(8,128)S(1)}, f32[8,32,128]{2,1,0:T(8,128)S(1)}, u32[]{:S(2)}, u32[]{:S(2)}) collective-permute-start(f32[8,32,128]{2,1,0:T(8,128)S(1)} %slice_add_fusion.15), channel_id=1, source_target_pairs={{0,8},{8,0},{16,24},{24,16},{1,9},{9,1},{17,25},{25,17},{2,10},{10... | collective-permute-start | bytes 393224 | tf_op jit(solution)/shard_map/ppermute | solution.py:37
  244.6 12.4 %collective-permute-start.61 = (f32[12,32,128]{2,1,0:T(8,128)S(1)}, f32[12,32,128]{2,1,0:T(8,128)S(1)}, u32[]{:S(2)}, u32[]{:S(2)}) collective-permute-start(f32[12,32,128]{2,1,0:T(8,128)S(1)} %get-tuple-element.203), channel_id=1, source_target_pairs={{0,16},{8,24},{16,0},{24,8},{1,17},{9,25},{17,1},{25,9},{2,18},{10... | collective-permute-start | bytes 589832 | tf_op jit(solution)/shard_map/ppermute | solution.py:37
  (38 other events, 272.5 us)

commit v22 on v18

--- a/solution.py
+++ b/solution.py
@@ -310,7 +310,7 @@
     )
     totals = jnp.sum(totals.reshape(chips, CORES, size), axis=0)
     conductivity = totals[:, :half].reshape(columns) / jnp.sum(totals[:, half])
-    flux = relax_both * (drive_half + after(reduce_far(blocks), conductivity))
+    flux = relax_both * (drive_half + reduce_far(blocks))
     first, second = flux[:per], flux[per:]
     mine = jnp.where(core == 0, first, second)
     got = swap(jnp.where(core == 0, second, first), cores)

time: 253 us -> 250 us (0.988)
  blocking collectives: 0 us -> 8.84 us
  starting transfers between devices: 75.6 us -> 68.3 us
  waiting for transfers between devices: 113 us -> 106 us
  Pallas kernels: 43.9 us -> 48 us
    all_to_all x0 -> x1, blocking collectives: none -> 8.84 us  [shards(): lax.all_to_all(jnp.broadcast_to(totals, (chips * CORES, size)), ALL, spli...]
    all_to_all x1 -> x0, waiting for transfers between devices: 4.41 us -> none  [shards(): lax.all_to_all(jnp.broadcast_to(totals, (chips * CORES, size)), ALL, spli...]
    pallas_call x9, Pallas kernels: 43.9 us -> 48 us  [apply_tiles(): pl.pallas_call(functools.partial(apply_kernel, span, skip, len(flux), bas...]
    all_to_all x1 -> x0, starting transfers between devices: 3.72 us -> none  [shards(): lax.all_to_all(jnp.broadcast_to(totals, (chips * CORES, size)), ALL, spli...]
    ppermute x63, starting transfers between devices: 71.9 us -> 68.3 us  [swap(): lax.ppermute(array, axis, [(i, i ^ distance) for i in range(lax.axis_size...]
    ppermute x63, waiting for transfers between devices: 109 us -> 106 us  [swap(): lax.ppermute(array, axis, [(i, i ^ distance) for i in range(lax.axis_size...]
  transfers between devices with their start and end apart: 64 -> 63, of which waited for: 43 -> 37; matrix products, arithmetic and copies ran while one was open for 4% -> 4% of each run, Pallas kernels for 12% -> 14%
where the time goes in v22:
time: 250 us; the launch traced here: 251 us
  waiting for transfers between devices  106 us (42%)
  starting transfers between devices  68.3 us (27%)
  Pallas kernels  48 us (19%)
  other arithmetic  12 us (5%)
  blocking collectives  8.84 us (4%)
  local copies, waits for them, and re-layouts  4.86 us (2%)
    ppermute x63, waiting for transfers between devices, swap(): lax.ppermute(array, axis, [(i, i ^ distance) for i in range(lax.axis_size...  106 us
    ppermute x63, starting transfers between devices, swap(): lax.ppermute(array, axis, [(i, i ^ distance) for i in range(lax.axis_size...  68.3 us
    pallas_call x9, Pallas kernels, apply_tiles(): pl.pallas_call(functools.partial(apply_kernel, span, skip, len(flux), bas...  48 us
    all_to_all x1, blocking collectives, shards(): lax.all_to_all(jnp.broadcast_to(totals, (chips * CORES, size)), ALL, spli...  8.84 us
  transfers between devices with their start and end apart: 63, of which 37 were waited for; matrix products, arithmetic and copies ran while one was open for 4% of the time, Pallas kernels for 14%

profile of v22, /device:TPU:0, one launch (start us, length us, event | category | flops | bytes accessed | tf_op | source)
XLA Modules:
  0.0 250.8 jit_solution(3634048577175513427)
XLA Ops:
  8.6 3.9 %collective-permute-start.2 = (f32[12,32,128]{2,1,0:T(8,128)S(1)}, f32[12,32,128]{2,1,0:T(8,128)S(1)}, u32[]{:S(2)}, u32[]{:S(2)}) collective-permute-start(f32[12,32,128]{2,1,0:T(8,128)S(1)} %get-tuple-element.272), channel_id=1, source_target_pairs={{0,16},{8,24},{16,0},{24,8},{1,17},{9,25},{17,1},{25,9},{2,18},{10... | collective-permute-start | bytes 589832 | tf_op jit(solution)/shard_map/ppermute | solution.py:37
  12.5 10.1 %collective-permute-done.4 = f32[12,2,128]{2,0,1:T(8,128)S(1)} collective-permute-done((f32[12,2,128]{2,0,1:T(8,128)S(1)}, f32[12,2,128]{2,0,1:T(8,128)S(1)}, u32[]{:S(2)}, u32[]{:S(2)}) %collective-permute-start.4) | collective-permute-done | bytes 12320 | tf_op jit(solution)/shard_map/ppermute | solution.py:37
  33.0 3.4 %collective-permute-done.6 = f32[16,32,128]{2,1,0:T(8,128)S(1)} collective-permute-done((f32[16,32,128]{2,1,0:T(8,128)S(1)}, f32[16,32,128]{2,1,0:T(8,128)S(1)}, u32[]{:S(2)}, u32[]{:S(2)}) %collective-permute-start.6) | collective-permute-done | bytes 262176 | tf_op jit(solution)/shard_map/ppermute | solution.py:37
  40.8 6.9 %shard_map.95 = (f32[96,32,128]{2,1,0:T(8,128)S(1)}, f32[96,32,128]{2,1,0:T(8,128)S(1)}) custom-call(s32[772]{0:T(1024)S(1)} %pad_add_fusion.places_ref, f32[128,128,128]{2,1,0:T(8,128)} %own_ref.8, f32[128,128,128]{2,1,0:T(8,128)} %copy-done.2, f32[32,32,128]{2,1,0:T(8,128)S(1)} %constant_dynamic-update-slice_fusion.refs_0_, ...), custom_call_target="tpu_custom_call" | custom-call | flops 536870912 | bytes 14680064 | tf_op jit(solution)/shard_map/pallas_call | solution.py:188
  50.5 4.7 %shard_map.97 = (f32[32,32,128]{2,1,0:T(8,128)S(1)}, f32[32,32,128]{2,1,0:T(8,128)S(1)}, f32[32,32,128]{2,1,0:T(8,128)S(1)}) custom-call(s32[772]{0:T(1024)S(1)} %pad_add_fusion.places_ref, f32[128,128,128]{2,1,0:T(8,128)} %own_ref.8, f32[128,128,128]{2,1,0:T(8,128)} %copy-done.2, f32[32,32,128]{2,1,0:T(8,128)S(1)} %collective-permute-done.7.refs_0_, ...), custom_call_target="tpu_custom_call" | custom-call | flops 268435456 | bytes 7340032 | tf_op jit(solution)/shard_map/pallas_call | solution.py:188
  58.4 4.3 %shard_map.96 = (f32[32,32,128]{2,1,0:T(8,128)S(1)}, f32[32,32,128]{2,1,0:T(8,128)S(1)}, f32[32,32,128]{2,1,0:T(8,128)S(1)}) custom-call(s32[772]{0:T(1024)S(1)} %pad_add_fusion.places_ref, f32[128,128,128]{2,1,0:T(8,128)} %own_ref.8, f32[128,128,128]{2,1,0:T(8,128)} %copy-done.2, f32[32,32,128]{2,1,0:T(8,128)S(1)} %collective-permute-done.7.refs_0_, ...), custom_call_target="tpu_custom_call" | custom-call | flops 268435456 | bytes 7340032 | tf_op jit(solution)/shard_map/pallas_call | solution.py:188
  62.7 3.7 %collective-permute-done.14 = f32[32,32,128]{2,1,0:T(8,128)S(1)} collective-permute-done((f32[32,32,128]{2,1,0:T(8,128)S(1)}, f32[32,32,128]{2,1,0:T(8,128)S(1)}, u32[]{:S(2)}, u32[]{:S(2)}) %collective-permute-start.14) | collective-permute-done | bytes 524320 | tf_op jit(solution)/shard_map/ppermute | solution.py:37
  74.2 2.6 %collective-permute-done.18 = f32[16,32,128]{2,1,0:T(8,128)S(1)} collective-permute-done((f32[16,32,128]{2,1,0:T(8,128)S(1)}, f32[16,32,128]{2,1,0:T(8,128)S(1)}, u32[]{:S(2)}, u32[]{:S(2)}) %collective-permute-start.18) | collective-permute-done | bytes 262176 | tf_op jit(solution)/shard_map/ppermute | solution.py:37
  83.9 3.9 %collective-permute-start.23 = (f32[24,32,128]{2,1,0:T(8,128)S(1)}, f32[24,32,128]{2,1,0:T(8,128)S(1)}, u32[]{:S(2)}, u32[]{:S(2)}) collective-permute-start(f32[24,32,128]{2,1,0:T(8,128)S(1)} %get-tuple-element.222), channel_id=1, source_target_pairs={{0,16},{8,24},{16,0},{24,8},{1,17},{9,25},{17,1},{25,9},{2,18},{10... | collective-permute-start | bytes 1179656 | tf_op jit(solution)/shard_map/ppermute | solution.py:37
  87.8 11.4 %collective-permute-done.23 = f32[24,32,128]{2,1,0:T(8,128)S(1)} collective-permute-done((f32[24,32,128]{2,1,0:T(8,128)S(1)}, f32[24,32,128]{2,1,0:T(8,128)S(1)}, u32[]{:S(2)}, u32[]{:S(2)}) %collective-permute-start.23) | collective-permute-done | bytes 393248 | tf_op jit(solution)/shard_map/ppermute | solution.py:37
  101.1 4.1 %collective-permute-done.24 = f32[8,32,128]{2,1,0:T(8,128)S(1)} collective-permute-done((f32[8,32,128]{2,1,0:T(8,128)S(1)}, f32[8,32,128]{2,1,0:T(8,128)S(1)}, u32[]{:S(2)}, u32[]{:S(2)}) %collective-permute-start.24) | collective-permute-done | bytes 131104 | tf_op jit(solution)/shard_map/ppermute | solution.py:37
  107.9 5.3 %collective-permute-done.25 = f32[16,32,128]{2,1,0:T(8,128)S(1)} collective-permute-done((f32[16,32,128]{2,1,0:T(8,128)S(1)}, f32[16,32,128]{2,1,0:T(8,128)S(1)}, u32[]{:S(2)}, u32[]{:S(2)}) %collective-permute-start.25) | collective-permute-done | bytes 262176 | tf_op jit(solution)/shard_map/ppermute | solution.py:37
  117.3 6.9 %shard_map.98 = (f32[96,32,128]{2,1,0:T(8,128)S(1)}, f32[96,32,128]{2,1,0:T(8,128)S(1)}) custom-call(s32[772]{0:T(1024)S(1)} %pad_add_fusion.places_ref, f32[128,128,128]{2,1,0:T(8,128)} %own_ref.8, f32[128,128,128]{2,1,0:T(8,128)} %copy-done.2, f32[32,32,128]{2,1,0:T(8,128)S(1)} %constant_dynamic-update-slice_fusion.15.refs_0_, ...), custom_call_target="tpu_custom_call" | custom-call | flops 536870912 | bytes 14680064 | tf_op jit(solution)/shard_map/pallas_call | solution.py:188
  126.3 4.7 %shard_map.100 = (f32[32,32,128]{2,1,0:T(8,128)S(1)}, f32[32,32,128]{2,1,0:T(8,128)S(1)}, f32[32,32,128]{2,1,0:T(8,128)S(1)}) custom-call(s32[772]{0:T(1024)S(1)} %pad_add_fusion.places_ref, f32[128,128,128]{2,1,0:T(8,128)} %own_ref.8, f32[128,128,128]{2,1,0:T(8,128)} %copy-done.2, f32[32,32,128]{2,1,0:T(8,128)S(1)} %collective-permute-done.26.refs_0_, ...), custom_call_target="tpu_custom_call" | custom-call | flops 268435456 | bytes 7340032 | tf_op jit(solution)/shard_map/pallas_call | solution.py:188
  132.6 4.5 %shard_map.99 = (f32[32,32,128]{2,1,0:T(8,128)S(1)}, f32[32,32,128]{2,1,0:T(8,128)S(1)}, f32[32,32,128]{2,1,0:T(8,128)S(1)}) custom-call(s32[772]{0:T(1024)S(1)} %pad_add_fusion.places_ref, f32[128,128,128]{2,1,0:T(8,128)} %own_ref.8, f32[128,128,128]{2,1,0:T(8,128)} %copy-done.2, f32[32,32,128]{2,1,0:T(8,128)S(1)} %collective-permute-done.26.refs_0_, ...), custom_call_target="tpu_custom_call" | custom-call | flops 268435456 | bytes 7340032 | tf_op jit(solution)/shard_map/pallas_call | solution.py:188
  137.1 5.7 %collective-permute-done.33 = f32[32,32,128]{2,1,0:T(8,128)S(1)} collective-permute-done((f32[32,32,128]{2,1,0:T(8,128)S(1)}, f32[32,32,128]{2,1,0:T(8,128)S(1)}, u32[]{:S(2)}, u32[]{:S(2)}) %collective-permute-start.33) | collective-permute-done | bytes 524320 | tf_op jit(solution)/shard_map/ppermute | solution.py:37
  146.3 4.0 %collective-permute-done.34 = f32[16,32,128]{2,1,0:T(8,128)S(1)} collective-permute-done((f32[16,32,128]{2,1,0:T(8,128)S(1)}, f32[16,32,128]{2,1,0:T(8,128)S(1)}, u32[]{:S(2)}, u32[]{:S(2)}) %collective-permute-start.34) | collective-permute-done | bytes 262176 | tf_op jit(solution)/shard_map/ppermute | solution.py:37
  152.7 3.3 %collective-permute-done.35 = f32[8,32,128]{2,1,0:T(8,128)S(1)} collective-permute-done((f32[8,32,128]{2,1,0:T(8,128)S(1)}, f32[8,32,128]{2,1,0:T(8,128)S(1)}, u32[]{:S(2)}, u32[]{:S(2)}) %collective-permute-start.35) | collective-permute-done | bytes 131104 | tf_op jit(solution)/shard_map/ppermute | solution.py:37
  156.3 2.9 %collective-permute-start.42 = (f32[24,32,128]{2,1,0:T(8,128)S(1)}, f32[24,32,128]{2,1,0:T(8,128)S(1)}, u32[]{:S(2)}, u32[]{:S(2)}) collective-permute-start(f32[24,32,128]{2,1,0:T(8,128)S(1)} %get-tuple-element.210), channel_id=1, source_target_pairs={{0,16},{8,24},{16,0},{24,8},{1,17},{9,25},{17,1},{25,9},{2,18},{10... | collective-permute-start | bytes 1179656 | tf_op jit(solution)/shard_map/ppermute | solution.py:37
  159.2 10.1 %collective-permute-done.42 = f32[24,32,128]{2,1,0:T(8,128)S(1)} collective-permute-done((f32[24,32,128]{2,1,0:T(8,128)S(1)}, f32[24,32,128]{2,1,0:T(8,128)S(1)}, u32[]{:S(2)}, u32[]{:S(2)}) %collective-permute-start.42) | collective-permute-done | bytes 393248 | tf_op jit(solution)/shard_map/ppermute | solution.py:37
  180.1 4.0 %collective-permute-done.44 = f32[16,32,128]{2,1,0:T(8,128)S(1)} collective-permute-done((f32[16,32,128]{2,1,0:T(8,128)S(1)}, f32[16,32,128]{2,1,0:T(8,128)S(1)}, u32[]{:S(2)}, u32[]{:S(2)}) %collective-permute-start.44) | collective-permute-done | bytes 262176 | tf_op jit(solution)/shard_map/ppermute | solution.py:37
  187.7 6.9 %shard_map.101 = (f32[96,32,128]{2,1,0:T(8,128)S(1)}, f32[96,32,128]{2,1,0:T(8,128)S(1)}) custom-call(s32[772]{0:T(1024)S(1)} %pad_add_fusion.places_ref, f32[128,128,128]{2,1,0:T(8,128)} %own_ref.8, f32[128,128,128]{2,1,0:T(8,128)} %copy-done.2, f32[32,32,128]{2,1,0:T(8,128)S(1)} %constant_dynamic-update-slice_fusion.30.refs_0_, ...), custom_call_target="tpu_custom_call" | custom-call | flops 536870912 | bytes 14680064 | tf_op jit(solution)/shard_map/pallas_call | solution.py:188
  194.6 2.7 %collective-permute-done.48.refs_1_ = f32[32,32,128]{2,1,0:T(8,128)S(1)} collective-permute-done((f32[32,32,128]{2,1,0:T(8,128)S(1)}, f32[32,32,128]{2,1,0:T(8,128)S(1)}, u32[]{:S(2)}, u32[]{:S(2)}) %collective-permute-start.48) | collective-permute-done | bytes 524320 | tf_op jit(solution)/shard_map/ppermute | solution.py:37
  197.3 4.0 %collective-permute-done.51.refs_2_ = f32[32,32,128]{2,1,0:T(8,128)S(1)} collective-permute-done((f32[32,32,128]{2,1,0:T(8,128)S(1)}, f32[32,32,128]{2,1,0:T(8,128)S(1)}, u32[]{:S(2)}, u32[]{:S(2)}) %collective-permute-start.51) | collective-permute-done | bytes 524320 | tf_op jit(solution)/shard_map/ppermute | solution.py:37
  201.3 4.7 %shard_map.103 = (f32[32,32,128]{2,1,0:T(8,128)S(1)}, f32[32,32,128]{2,1,0:T(8,128)S(1)}, f32[32,32,128]{2,1,0:T(8,128)S(1)}) custom-call(s32[772]{0:T(1024)S(1)} %pad_add_fusion.places_ref, f32[128,128,128]{2,1,0:T(8,128)} %own_ref.8, f32[128,128,128]{2,1,0:T(8,128)} %copy-done.2, f32[32,32,128]{2,1,0:T(8,128)S(1)} %collective-permute-done.45.refs_0_, ...), custom_call_target="tpu_custom_call" | custom-call | flops 268435456 | bytes 7340032 | tf_op jit(solution)/shard_map/pallas_call | solution.py:188
  207.1 4.3 %shard_map.102 = (f32[32,32,128]{2,1,0:T(8,128)S(1)}, f32[32,32,128]{2,1,0:T(8,128)S(1)}, f32[32,32,128]{2,1,0:T(8,128)S(1)}) custom-call(s32[772]{0:T(1024)S(1)} %pad_add_fusion.places_ref, f32[128,128,128]{2,1,0:T(8,128)} %own_ref.8, f32[128,128,128]{2,1,0:T(8,128)} %copy-done.2, f32[32,32,128]{2,1,0:T(8,128)S(1)} %collective-permute-done.45.refs_0_, ...), custom_call_target="tpu_custom_call" | custom-call | flops 268435456 | bytes 7340032 | tf_op jit(solution)/shard_map/pallas_call | solution.py:188
  211.4 4.5 %collective-permute-done.58 = f32[32,32,128]{2,1,0:T(8,128)S(1)} collective-permute-done((f32[32,32,128]{2,1,0:T(8,128)S(1)}, f32[32,32,128]{2,1,0:T(8,128)S(1)}, u32[]{:S(2)}, u32[]{:S(2)}) %collective-permute-start.58) | collective-permute-done | bytes 524320 | tf_op jit(solution)/shard_map/ppermute | solution.py:37
  218.9 3.5 %collective-permute-done.59 = f32[16,32,128]{2,1,0:T(8,128)S(1)} collective-permute-done((f32[16,32,128]{2,1,0:T(8,128)S(1)}, f32[16,32,128]{2,1,0:T(8,128)S(1)}, u32[]{:S(2)}, u32[]{:S(2)}) %collective-permute-start.59) | collective-permute-done | bytes 262176 | tf_op jit(solution)/shard_map/ppermute | solution.py:37
  224.2 2.8 %collective-permute-start.57 = (f32[8,32,128]{2,1,0:T(8,128)}, f32[8,32,128]{2,1,0:T(8,128)}, u32[]{:S(2)}, u32[]{:S(2)}) collective-permute-start(f32[8,32,128]{2,1,0:T(8,128)} %slice_add_fusion.14), channel_id=1, source_target_pairs={{0,2},{2,0},{1,3},{3,1},{4,6},{6,4},{5,7},{7,5},{8,10},{10,8},{9,1... | collective-permute-start | bytes 393224 | tf_op jit(solution)/shard_map/ppermute | solution.py:37
  230.3 2.8 %collective-permute-done.54 = f32[8,32,128]{2,1,0:T(8,128)} collective-permute-done((f32[8,32,128]{2,1,0:T(8,128)}, f32[8,32,128]{2,1,0:T(8,128)}, u32[]{:S(2)}, u32[]{:S(2)}) %collective-permute-start.54) | collective-permute-done | bytes 131104 | tf_op jit(solution)/shard_map/ppermute | solution.py:37
  236.0 3.0 %collective-permute-start.61 = (f32[12,32,128]{2,1,0:T(8,128)S(1)}, f32[12,32,128]{2,1,0:T(8,128)S(1)}, u32[]{:S(2)}, u32[]{:S(2)}) collective-permute-start(f32[12,32,128]{2,1,0:T(8,128)S(1)} %get-tuple-element.204), channel_id=1, source_target_pairs={{0,16},{8,24},{16,0},{24,8},{1,17},{9,25},{17,1},{25,9},{2,18},{10... | collective-permute-start | bytes 589832 | tf_op jit(solution)/shard_map/ppermute | solution.py:37
  239.1 8.8 %all_to_all.6 = f32[32,1,128]{2,1,0:T(1,128)S(1)} all-to-all(f32[32,1,128]{2,1,0:T(1,128)S(1)} %broadcast_in_dim.60), channel_id=1, replica_groups=mesh['z'=4,'y'=2,'x'=2,'core'=2] {'z','y','x','core'}, dimensions={0} | all-to-all | bytes 32768 | tf_op jit(solution)/shard_map/all_to_all | solution.py:308
  (285 shorter events, 89.8 us)
Async XLA Ops:
  6.1 17.1 %collective-permute-start.3 = (f32[128,128,128]{2,1,0:T(8,128)}, f32[128,128,128]{2,1,0:T(8,128)S(1)}, u32[]{:S(2)}, u32[]{:S(2)}) collective-permute-start(f32[128,128,128]{2,1,0:T(8,128)} %own_ref.8), channel_id=1, source_target_pairs={{0,1},{1,0},{2,3},{3,2},{4,5},{5,4},{6,7},{7,6},{8,9},{9,8},{10,11... | collective-permute-start | bytes 25165832 | tf_op jit(solution)/shard_map/ppermute | solution.py:37
  8.6 14.7 %collective-permute-start.2 = (f32[12,32,128]{2,1,0:T(8,128)S(1)}, f32[12,32,128]{2,1,0:T(8,128)S(1)}, u32[]{:S(2)}, u32[]{:S(2)}) collective-permute-start(f32[12,32,128]{2,1,0:T(8,128)S(1)} %get-tuple-element.272), channel_id=1, source_target_pairs={{0,16},{8,24},{16,0},{24,8},{1,17},{9,25},{17,1},{25,9},{2,18},{10... | collective-permute-start | bytes 589832 | tf_op jit(solution)/shard_map/ppermute | solution.py:37
  12.5 10.2 %collective-permute-start.4 = (f32[12,2,128]{2,0,1:T(8,128)S(1)}, f32[12,2,128]{2,0,1:T(8,128)S(1)}, u32[]{:S(2)}, u32[]{:S(2)}) collective-permute-start(f32[12,2,128]{2,0,1:T(8,128)S(1)} %pad_maximum_fusion.22), channel_id=1, source_target_pairs={{0,16},{8,24},{16,0},{24,8},{1,17},{9,25},{17,1},{25,9},{2,18},{10... | collective-permute-start | bytes 36872 | tf_op jit(solution)/shard_map/ppermute | solution.py:37
  36.4 13.1 %collective-permute-start.7 = (f32[32,32,128]{2,1,0:T(8,128)S(1)}, f32[32,32,128]{2,1,0:T(8,128)S(1)}, u32[]{:S(2)}, u32[]{:S(2)}) collective-permute-start(f32[32,32,128]{2,1,0:T(8,128)S(1)} %constant_dynamic-update-slice_fusion.refs_0_), channel_id=1, source_target_pairs={{0,2},{2,0},{1,3},{3,1},{4,6},{6,4},{5,7},{7,5},{8,10},{10,8},{9,1... | collective-permute-start | bytes 1572872 | tf_op jit(solution)/shard_map/ppermute | solution.py:37
  37.1 12.5 %collective-permute-start.10 = (f32[32,32,128]{2,1,0:T(8,128)S(1)}, f32[32,32,128]{2,1,0:T(8,128)S(1)}, u32[]{:S(2)}, u32[]{:S(2)}) collective-permute-start(f32[32,32,128]{2,1,0:T(8,128)S(1)} %constant_dynamic-update-slice_fusion.3.refs_1_), channel_id=1, source_target_pairs={{0,4},{4,0},{1,5},{5,1},{2,6},{6,2},{3,7},{7,3},{8,12},{12,8},{9,1... | collective-permute-start | bytes 1572872 | tf_op jit(solution)/shard_map/ppermute | solution.py:37
  39.0 11.5 %collective-permute-start.13 = (f32[32,32,128]{2,1,0:T(8,128)S(1)}, f32[32,32,128]{2,1,0:T(8,128)S(1)}, u32[]{:S(2)}, u32[]{:S(2)}) collective-permute-start(f32[32,32,128]{2,1,0:T(8,128)S(1)} %constant_dynamic-update-slice_fusion.6.refs_2_), channel_id=1, source_target_pairs={{0,8},{8,0},{16,24},{24,16},{1,9},{9,1},{17,25},{25,17},{2,10},{10... | collective-permute-start | bytes 1572872 | tf_op jit(solution)/shard_map/ppermute | solution.py:37
  55.2 11.2 %collective-permute-start.14 = (f32[32,32,128]{2,1,0:T(8,128)S(1)}, f32[32,32,128]{2,1,0:T(8,128)S(1)}, u32[]{:S(2)}, u32[]{:S(2)}) collective-permute-start(f32[32,32,128]{2,1,0:T(8,128)S(1)} %get-tuple-element.113), channel_id=1, source_target_pairs={{0,2},{2,0},{1,3},{3,1},{4,6},{6,4},{5,7},{7,5},{8,10},{10,8},{9,1... | collective-permute-start | bytes 1572872 | tf_op jit(solution)/shard_map/ppermute | solution.py:37
  56.0 12.8 %collective-permute-start.17 = (f32[32,32,128]{2,1,0:T(8,128)S(1)}, f32[32,32,128]{2,1,0:T(8,128)S(1)}, u32[]{:S(2)}, u32[]{:S(2)}) collective-permute-start(f32[32,32,128]{2,1,0:T(8,128)S(1)} %get-tuple-element.122), channel_id=1, source_target_pairs={{0,4},{4,0},{1,5},{5,1},{2,6},{6,2},{3,7},{7,3},{8,12},{12,8},{9,1... | collective-permute-start | bytes 1572872 | tf_op jit(solution)/shard_map/ppermute | solution.py:37
  56.7 14.4 %collective-permute-start.20 = (f32[32,32,128]{2,1,0:T(8,128)S(1)}, f32[32,32,128]{2,1,0:T(8,128)S(1)}, u32[]{:S(2)}, u32[]{:S(2)}) collective-permute-start(f32[32,32,128]{2,1,0:T(8,128)S(1)} %get-tuple-element.131), channel_id=1, source_target_pairs={{0,8},{8,0},{16,24},{24,16},{1,9},{9,1},{17,25},{25,17},{2,10},{10... | collective-permute-start | bytes 1572872 | tf_op jit(solution)/shard_map/ppermute | solution.py:37
  68.8 8.1 %collective-permute-start.18 = (f32[16,32,128]{2,1,0:T(8,128)S(1)}, f32[16,32,128]{2,1,0:T(8,128)S(1)}, u32[]{:S(2)}, u32[]{:S(2)}) collective-permute-start(f32[16,32,128]{2,1,0:T(8,128)S(1)} %slice_add_fusion.7), channel_id=1, source_target_pairs={{0,8},{8,0},{16,24},{24,16},{1,9},{9,1},{17,25},{25,17},{2,10},{10... | collective-permute-start | bytes 786440 | tf_op jit(solution)/shard_map/ppermute | solution.py:37
  83.9 15.3 %collective-permute-start.23 = (f32[24,32,128]{2,1,0:T(8,128)S(1)}, f32[24,32,128]{2,1,0:T(8,128)S(1)}, u32[]{:S(2)}, u32[]{:S(2)}) collective-permute-start(f32[24,32,128]{2,1,0:T(8,128)S(1)} %get-tuple-element.222), channel_id=1, source_target_pairs={{0,16},{8,24},{16,0},{24,8},{1,17},{9,25},{17,1},{25,9},{2,18},{10... | collective-permute-start | bytes 1179656 | tf_op jit(solution)/shard_map/ppermute | solution.py:37
  105.3 8.0 %collective-permute-start.25 = (f32[16,32,128]{2,1,0:T(8,128)S(1)}, f32[16,32,128]{2,1,0:T(8,128)S(1)}, u32[]{:S(2)}, u32[]{:S(2)}) collective-permute-start(f32[16,32,128]{2,1,0:T(8,128)S(1)} %pad_maximum_fusion.3), channel_id=1, source_target_pairs={{0,4},{4,0},{1,5},{5,1},{2,6},{6,2},{3,7},{7,3},{8,12},{12,8},{9,1... | collective-permute-start | bytes 786440 | tf_op jit(solution)/shard_map/ppermute | solution.py:37
  105.4 8.2 %collective-permute-start.28 = (f32[16,32,128]{2,1,0:T(8,128)S(1)}, f32[16,32,128]{2,1,0:T(8,128)S(1)}, u32[]{:S(2)}, u32[]{:S(2)}) collective-permute-start(f32[16,32,128]{2,1,0:T(8,128)S(1)} %pad_maximum_fusion.4), channel_id=1, source_target_pairs={{0,8},{8,0},{16,24},{24,16},{1,9},{9,1},{17,25},{25,17},{2,10},{10... | collective-permute-start | bytes 786440 | tf_op jit(solution)/shard_map/ppermute | solution.py:37
  107.8 9.3 %collective-permute-start.31 = (f32[16,32,128]{2,1,0:T(8,128)S(1)}, f32[16,32,128]{2,1,0:T(8,128)S(1)}, u32[]{:S(2)}, u32[]{:S(2)}) collective-permute-start(f32[16,32,128]{2,1,0:T(8,128)S(1)} %pad_maximum_fusion.5), channel_id=1, source_target_pairs={{0,2},{2,0},{1,3},{3,1},{4,6},{6,4},{5,7},{7,5},{8,10},{10,8},{9,1... | collective-permute-start | bytes 786440 | tf_op jit(solution)/shard_map/ppermute | solution.py:37
  113.3 11.0 %collective-permute-start.26 = (f32[32,32,128]{2,1,0:T(8,128)S(1)}, f32[32,32,128]{2,1,0:T(8,128)S(1)}, u32[]{:S(2)}, u32[]{:S(2)}) collective-permute-start(f32[32,32,128]{2,1,0:T(8,128)S(1)} %constant_dynamic-update-slice_fusion.15.refs_0_), channel_id=1, source_target_pairs={{0,2},{2,0},{1,3},{3,1},{4,6},{6,4},{5,7},{7,5},{8,10},{10,8},{9,1... | collective-permute-start | bytes 1572872 | tf_op jit(solution)/shard_map/ppermute | solution.py:37
  113.6 10.6 %collective-permute-start.29 = (f32[32,32,128]{2,1,0:T(8,128)S(1)}, f32[32,32,128]{2,1,0:T(8,128)S(1)}, u32[]{:S(2)}, u32[]{:S(2)}) collective-permute-start(f32[32,32,128]{2,1,0:T(8,128)S(1)} %constant_dynamic-update-slice_fusion.18.refs_1_), channel_id=1, source_target_pairs={{0,4},{4,0},{1,5},{5,1},{2,6},{6,2},{3,7},{7,3},{8,12},{12,8},{9,1... | collective-permute-start | bytes 1572872 | tf_op jit(solution)/shard_map/ppermute | solution.py:37
  117.1 9.2 %collective-permute-start.32 = (f32[32,32,128]{2,1,0:T(8,128)S(1)}, f32[32,32,128]{2,1,0:T(8,128)S(1)}, u32[]{:S(2)}, u32[]{:S(2)}) collective-permute-start(f32[32,32,128]{2,1,0:T(8,128)S(1)} %constant_dynamic-update-slice_fusion.21.refs_2_), channel_id=1, source_target_pairs={{0,8},{8,0},{16,24},{24,16},{1,9},{9,1},{17,25},{25,17},{2,10},{10... | collective-permute-start | bytes 1572872 | tf_op jit(solution)/shard_map/ppermute | solution.py:37
  131.0 11.8 %collective-permute-start.33 = (f32[32,32,128]{2,1,0:T(8,128)S(1)}, f32[32,32,128]{2,1,0:T(8,128)S(1)}, u32[]{:S(2)}, u32[]{:S(2)}) collective-permute-start(f32[32,32,128]{2,1,0:T(8,128)S(1)} %get-tuple-element.145), channel_id=1, source_target_pairs={{0,2},{2,0},{1,3},{3,1},{4,6},{6,4},{5,7},{7,5},{8,10},{10,8},{9,1... | collective-permute-start | bytes 1572872 | tf_op jit(solution)/shard_map/ppermute | solution.py:37
  131.1 12.1 %collective-permute-start.36 = (f32[32,32,128]{2,1,0:T(8,128)S(1)}, f32[32,32,128]{2,1,0:T(8,128)S(1)}, u32[]{:S(2)}, u32[]{:S(2)}) collective-permute-start(f32[32,32,128]{2,1,0:T(8,128)S(1)} %get-tuple-element.154), channel_id=1, source_target_pairs={{0,4},{4,0},{1,5},{5,1},{2,6},{6,2},{3,7},{7,3},{8,12},{12,8},{9,1... | collective-permute-start | bytes 1572872 | tf_op jit(solution)/shard_map/ppermute | solution.py:37
  131.3 12.5 %collective-permute-start.39 = (f32[32,32,128]{2,1,0:T(8,128)S(1)}, f32[32,32,128]{2,1,0:T(8,128)S(1)}, u32[]{:S(2)}, u32[]{:S(2)}) collective-permute-start(f32[32,32,128]{2,1,0:T(8,128)S(1)} %get-tuple-element.163), channel_id=1, source_target_pairs={{0,8},{8,0},{16,24},{24,16},{1,9},{9,1},{17,25},{25,17},{2,10},{10... | collective-permute-start | bytes 1572872 | tf_op jit(solution)/shard_map/ppermute | solution.py:37
  156.3 13.0 %collective-permute-start.42 = (f32[24,32,128]{2,1,0:T(8,128)S(1)}, f32[24,32,128]{2,1,0:T(8,128)S(1)}, u32[]{:S(2)}, u32[]{:S(2)}) collective-permute-start(f32[24,32,128]{2,1,0:T(8,128)S(1)} %get-tuple-element.210), channel_id=1, source_target_pairs={{0,16},{8,24},{16,0},{24,8},{1,17},{9,25},{17,1},{25,9},{2,18},{10... | collective-permute-start | bytes 1179656 | tf_op jit(solution)/shard_map/ppermute | solution.py:37
  174.7 9.3 %collective-permute-start.44 = (f32[16,32,128]{2,1,0:T(8,128)S(1)}, f32[16,32,128]{2,1,0:T(8,128)S(1)}, u32[]{:S(2)}, u32[]{:S(2)}) collective-permute-start(f32[16,32,128]{2,1,0:T(8,128)S(1)} %pad_maximum_fusion.6), channel_id=1, source_target_pairs={{0,4},{4,0},{1,5},{5,1},{2,6},{6,2},{3,7},{7,3},{8,12},{12,8},{9,1... | collective-permute-start | bytes 786440 | tf_op jit(solution)/shard_map/ppermute | solution.py:37
  176.8 8.9 %collective-permute-start.47 = (f32[16,32,128]{2,1,0:T(8,128)S(1)}, f32[16,32,128]{2,1,0:T(8,128)S(1)}, u32[]{:S(2)}, u32[]{:S(2)}) collective-permute-start(f32[16,32,128]{2,1,0:T(8,128)S(1)} %pad_maximum_fusion.7), channel_id=1, source_target_pairs={{0,8},{8,0},{16,24},{24,16},{1,9},{9,1},{17,25},{25,17},{2,10},{10... | collective-permute-start | bytes 786440 | tf_op jit(solution)/shard_map/ppermute | solution.py:37
  178.3 9.2 %collective-permute-start.50 = (f32[16,32,128]{2,1,0:T(8,128)S(1)}, f32[16,32,128]{2,1,0:T(8,128)S(1)}, u32[]{:S(2)}, u32[]{:S(2)}) collective-permute-start(f32[16,32,128]{2,1,0:T(8,128)S(1)} %pad_maximum_fusion.8), channel_id=1, source_target_pairs={{0,2},{2,0},{1,3},{3,1},{4,6},{6,4},{5,7},{7,5},{8,10},{10,8},{9,1... | collective-permute-start | bytes 786440 | tf_op jit(solution)/shard_map/ppermute | solution.py:37
  184.1 10.5 %collective-permute-start.45 = (f32[32,32,128]{2,1,0:T(8,128)S(1)}, f32[32,32,128]{2,1,0:T(8,128)S(1)}, u32[]{:S(2)}, u32[]{:S(2)}) collective-permute-start(f32[32,32,128]{2,1,0:T(8,128)S(1)} %constant_dynamic-update-slice_fusion.30.refs_0_), channel_id=1, source_target_pairs={{0,2},{2,0},{1,3},{3,1},{4,6},{6,4},{5,7},{7,5},{8,10},{10,8},{9,1... | collective-permute-start | bytes 1572872 | tf_op jit(solution)/shard_map/ppermute | solution.py:37
  185.7 11.6 %collective-permute-start.48 = (f32[32,32,128]{2,1,0:T(8,128)S(1)}, f32[32,32,128]{2,1,0:T(8,128)S(1)}, u32[]{:S(2)}, u32[]{:S(2)}) collective-permute-start(f32[32,32,128]{2,1,0:T(8,128)S(1)} %constant_dynamic-update-slice_fusion.33.refs_1_), channel_id=1, source_target_pairs={{0,4},{4,0},{1,5},{5,1},{2,6},{6,2},{3,7},{7,3},{8,12},{12,8},{9,1... | collective-permute-start | bytes 1572872 | tf_op jit(solution)/shard_map/ppermute | solution.py:37
  187.5 13.8 %collective-permute-start.51 = (f32[32,32,128]{2,1,0:T(8,128)S(1)}, f32[32,32,128]{2,1,0:T(8,128)S(1)}, u32[]{:S(2)}, u32[]{:S(2)}) collective-permute-start(f32[32,32,128]{2,1,0:T(8,128)S(1)} %constant_dynamic-update-slice_fusion.36.refs_2_), channel_id=1, source_target_pairs={{0,8},{8,0},{16,24},{24,16},{1,9},{9,1},{17,25},{25,17},{2,10},{10... | collective-permute-start | bytes 1572872 | tf_op jit(solution)/shard_map/ppermute | solution.py:37
  206.0 10.0 %collective-permute-start.58 = (f32[32,32,128]{2,1,0:T(8,128)S(1)}, f32[32,32,128]{2,1,0:T(8,128)S(1)}, u32[]{:S(2)}, u32[]{:S(2)}) collective-permute-start(f32[32,32,128]{2,1,0:T(8,128)S(1)} %get-tuple-element.195), channel_id=1, source_target_pairs={{0,8},{8,0},{16,24},{24,16},{1,9},{9,1},{17,25},{25,17},{2,10},{10... | collective-permute-start | bytes 1572872 | tf_op jit(solution)/shard_map/ppermute | solution.py:37
  206.1 10.7 %collective-permute-start.55 = (f32[32,32,128]{2,1,0:T(8,128)S(1)}, f32[32,32,128]{2,1,0:T(8,128)S(1)}, u32[]{:S(2)}, u32[]{:S(2)}) collective-permute-start(f32[32,32,128]{2,1,0:T(8,128)S(1)} %get-tuple-element.186), channel_id=1, source_target_pairs={{0,4},{4,0},{1,5},{5,1},{2,6},{6,2},{3,7},{7,3},{8,12},{12,8},{9,1... | collective-permute-start | bytes 1572872 | tf_op jit(solution)/shard_map/ppermute | solution.py:37
  206.1 12.2 %collective-permute-start.52 = (f32[32,32,128]{2,1,0:T(8,128)S(1)}, f32[32,32,128]{2,1,0:T(8,128)S(1)}, u32[]{:S(2)}, u32[]{:S(2)}) collective-permute-start(f32[32,32,128]{2,1,0:T(8,128)S(1)} %get-tuple-element.177), channel_id=1, source_target_pairs={{0,2},{2,0},{1,3},{3,1},{4,6},{6,4},{5,7},{7,5},{8,10},{10,8},{9,1... | collective-permute-start | bytes 1572872 | tf_op jit(solution)/shard_map/ppermute | solution.py:37
  218.4 8.6 %collective-permute-start.53 = (f32[16,32,128]{2,1,0:T(8,128)S(1)}, f32[16,32,128]{2,1,0:T(8,128)S(1)}, u32[]{:S(2)}, u32[]{:S(2)}) collective-permute-start(f32[16,32,128]{2,1,0:T(8,128)S(1)} %slice_add_fusion.2), channel_id=1, source_target_pairs={{0,4},{4,0},{1,5},{5,1},{2,6},{6,2},{3,7},{7,3},{8,12},{12,8},{9,1... | collective-permute-start | bytes 786440 | tf_op jit(solution)/shard_map/ppermute | solution.py:37
  236.0 12.6 %collective-permute-start.61 = (f32[12,32,128]{2,1,0:T(8,128)S(1)}, f32[12,32,128]{2,1,0:T(8,128)S(1)}, u32[]{:S(2)}, u32[]{:S(2)}) collective-permute-start(f32[12,32,128]{2,1,0:T(8,128)S(1)} %get-tuple-element.204), channel_id=1, source_target_pairs={{0,16},{8,24},{16,0},{24,8},{1,17},{9,25},{17,1},{25,9},{2,18},{10... | collective-permute-start | bytes 589832 | tf_op jit(solution)/shard_map/ppermute | solution.py:37
  (52 other events, 342.5 us)

commit v23 on v22

--- a/solution.py
+++ b/solution.py
@@ -16,7 +16,7 @@
 VMEM = 48 * 1024 * 1024
 CHIPS = ("z", "y", "x")
 ALL = ("z", "y", "x", "core")
-NEAR = ("x", "y", "z")
+NEAR = ("z", "x", "y")
 
 
 def depth_of(n_rows):

time: 250 us -> 251 us (level)
  Pallas kernels: 48 us -> 44.9 us
  starting transfers between devices: 68.3 us -> 71.1 us
    pallas_call x9, Pallas kernels: 48 us -> 44.9 us  [apply_tiles(): pl.pallas_call(functools.partial(apply_kernel, span, skip, len(flux), bas...]
    ppermute x63, starting transfers between devices: 68.3 us -> 71.1 us  [swap(): lax.ppermute(array, axis, [(i, i ^ distance) for i in range(lax.axis_size...]
  transfers between devices with their start and end apart: 63 -> 63, of which waited for: 37 -> 41; matrix products, arithmetic and copies ran while one was open for 4% -> 4% of each run, Pallas kernels for 14% -> 13%
where the time goes in v23:
time: 251 us
  waiting for transfers between devices  106 us (42%)
  starting transfers between devices  71.1 us (28%)
  Pallas kernels  44.9 us (18%)
  other arithmetic  12 us (5%)
  blocking collectives  9.62 us (4%)
  local copies, waits for them, and re-layouts  4.86 us (2%)
    ppermute x63, waiting for transfers between devices, swap(): lax.ppermute(array, axis, [(i, i ^ distance) for i in range(lax.axis_size...  106 us
    ppermute x63, starting transfers between devices, swap(): lax.ppermute(array, axis, [(i, i ^ distance) for i in range(lax.axis_size...  71.1 us
    pallas_call x9, Pallas kernels, apply_tiles(): pl.pallas_call(functools.partial(apply_kernel, span, skip, len(flux), bas...  44.9 us
    all_to_all x1, blocking collectives, shards(): lax.all_to_all(jnp.broadcast_to(totals, (chips * CORES, size)), ALL, spli...  9.62 us
  transfers between devices with their start and end apart: 63, of which 41 were waited for; matrix products, arithmetic and copies ran while one was open for 4% of the time, Pallas kernels for 13%

profile of v23, /device:TPU:0, one launch (start us, length us, event | category | flops | bytes accessed | tf_op | source)
XLA Modules:
  0.0 251.1 jit_solution(15105576749855552592)
XLA Ops:
  8.6 3.9 %collective-permute-start.2 = (f32[12,32,128]{2,1,0:T(8,128)S(1)}, f32[12,32,128]{2,1,0:T(8,128)S(1)}, u32[]{:S(2)}, u32[]{:S(2)}) collective-permute-start(f32[12,32,128]{2,1,0:T(8,128)S(1)} %get-tuple-element.272), channel_id=1, source_target_pairs={{0,16},{8,24},{16,0},{24,8},{1,17},{9,25},{17,1},{25,9},{2,18},{10... | collective-permute-start | bytes 589832 | tf_op jit(solution)/shard_map/ppermute | solution.py:37
  12.5 10.1 %collective-permute-done.4 = f32[12,2,128]{2,0,1:T(8,128)S(1)} collective-permute-done((f32[12,2,128]{2,0,1:T(8,128)S(1)}, f32[12,2,128]{2,0,1:T(8,128)S(1)}, u32[]{:S(2)}, u32[]{:S(2)}) %collective-permute-start.4) | collective-permute-done | bytes 12320 | tf_op jit(solution)/shard_map/ppermute | solution.py:37
  33.0 3.4 %collective-permute-done.6 = f32[16,32,128]{2,1,0:T(8,128)S(1)} collective-permute-done((f32[16,32,128]{2,1,0:T(8,128)S(1)}, f32[16,32,128]{2,1,0:T(8,128)S(1)}, u32[]{:S(2)}, u32[]{:S(2)}) %collective-permute-start.6) | collective-permute-done | bytes 262176 | tf_op jit(solution)/shard_map/ppermute | solution.py:37
  40.8 6.6 %shard_map.95 = (f32[96,32,128]{2,1,0:T(8,128)S(1)}, f32[96,32,128]{2,1,0:T(8,128)S(1)}) custom-call(s32[772]{0:T(1024)S(1)} %pad_add_fusion.places_ref, f32[128,128,128]{2,1,0:T(8,128)} %own_ref.8, f32[128,128,128]{2,1,0:T(8,128)} %copy-done.2, f32[32,32,128]{2,1,0:T(8,128)S(1)} %constant_dynamic-update-slice_fusion.refs_0_, ...), custom_call_target="tpu_custom_call" | custom-call | flops 536870912 | bytes 14680064 | tf_op jit(solution)/shard_map/pallas_call | solution.py:188
  51.8 4.3 %shard_map.97 = (f32[32,32,128]{2,1,0:T(8,128)S(1)}, f32[32,32,128]{2,1,0:T(8,128)S(1)}, f32[32,32,128]{2,1,0:T(8,128)S(1)}) custom-call(s32[772]{0:T(1024)S(1)} %pad_add_fusion.places_ref, f32[128,128,128]{2,1,0:T(8,128)} %own_ref.8, f32[128,128,128]{2,1,0:T(8,128)} %copy-done.2, f32[32,32,128]{2,1,0:T(8,128)S(1)} %collective-permute-done.7.refs_0_, ...), custom_call_target="tpu_custom_call" | custom-call | flops 268435456 | bytes 7340032 | tf_op jit(solution)/shard_map/pallas_call | solution.py:188
  58.1 4.0 %shard_map.96 = (f32[32,32,128]{2,1,0:T(8,128)S(1)}, f32[32,32,128]{2,1,0:T(8,128)S(1)}, f32[32,32,128]{2,1,0:T(8,128)S(1)}) custom-call(s32[772]{0:T(1024)S(1)} %pad_add_fusion.places_ref, f32[128,128,128]{2,1,0:T(8,128)} %own_ref.8, f32[128,128,128]{2,1,0:T(8,128)} %copy-done.2, f32[32,32,128]{2,1,0:T(8,128)S(1)} %collective-permute-done.7.refs_0_, ...), custom_call_target="tpu_custom_call" | custom-call | flops 268435456 | bytes 7340032 | tf_op jit(solution)/shard_map/pallas_call | solution.py:188
  62.1 5.3 %collective-permute-done.14 = f32[32,32,128]{2,1,0:T(8,128)S(1)} collective-permute-done((f32[32,32,128]{2,1,0:T(8,128)S(1)}, f32[32,32,128]{2,1,0:T(8,128)S(1)}, u32[]{:S(2)}, u32[]{:S(2)}) %collective-permute-start.14) | collective-permute-done | bytes 524320 | tf_op jit(solution)/shard_map/ppermute | solution.py:37
  71.4 2.6 %collective-permute-done.15 = f32[16,32,128]{2,1,0:T(8,128)S(1)} collective-permute-done((f32[16,32,128]{2,1,0:T(8,128)S(1)}, f32[16,32,128]{2,1,0:T(8,128)S(1)}, u32[]{:S(2)}, u32[]{:S(2)}) %collective-permute-start.15) | collective-permute-done | bytes 262176 | tf_op jit(solution)/shard_map/ppermute | solution.py:37
  76.2 2.9 %collective-permute-start.19 = (f32[8,32,128]{2,1,0:T(8,128)S(1)}, f32[8,32,128]{2,1,0:T(8,128)S(1)}, u32[]{:S(2)}, u32[]{:S(2)}) collective-permute-start(f32[8,32,128]{2,1,0:T(8,128)S(1)} %slice_add_fusion.20), channel_id=1, source_target_pairs={{0,8},{8,0},{16,24},{24,16},{1,9},{9,1},{17,25},{25,17},{2,10},{10... | collective-permute-start | bytes 393224 | tf_op jit(solution)/shard_map/ppermute | solution.py:37
  79.6 3.1 %collective-permute-done.19 = f32[8,32,128]{2,1,0:T(8,128)S(1)} collective-permute-done((f32[8,32,128]{2,1,0:T(8,128)S(1)}, f32[8,32,128]{2,1,0:T(8,128)S(1)}, u32[]{:S(2)}, u32[]{:S(2)}) %collective-permute-start.19) | collective-permute-done | bytes 131104 | tf_op jit(solution)/shard_map/ppermute | solution.py:37
  86.5 12.2 %collective-permute-done.23 = f32[24,32,128]{2,1,0:T(8,128)S(1)} collective-permute-done((f32[24,32,128]{2,1,0:T(8,128)S(1)}, f32[24,32,128]{2,1,0:T(8,128)S(1)}, u32[]{:S(2)}, u32[]{:S(2)}) %collective-permute-start.23) | collective-permute-done | bytes 393248 | tf_op jit(solution)/shard_map/ppermute | solution.py:37
  102.1 2.6 %collective-permute-done.24 = f32[8,32,128]{2,1,0:T(8,128)S(1)} collective-permute-done((f32[8,32,128]{2,1,0:T(8,128)S(1)}, f32[8,32,128]{2,1,0:T(8,128)S(1)}, u32[]{:S(2)}, u32[]{:S(2)}) %collective-permute-start.24) | collective-permute-done | bytes 131104 | tf_op jit(solution)/shard_map/ppermute | solution.py:37
  108.2 4.4 %collective-permute-done.25 = f32[16,32,128]{2,1,0:T(8,128)S(1)} collective-permute-done((f32[16,32,128]{2,1,0:T(8,128)S(1)}, f32[16,32,128]{2,1,0:T(8,128)S(1)}, u32[]{:S(2)}, u32[]{:S(2)}) %collective-permute-start.25) | collective-permute-done | bytes 262176 | tf_op jit(solution)/shard_map/ppermute | solution.py:37
  112.7 2.6 %collective-permute-start.29 = (f32[32,32,128]{2,1,0:T(8,128)S(1)}, f32[32,32,128]{2,1,0:T(8,128)S(1)}, u32[]{:S(2)}, u32[]{:S(2)}) collective-permute-start(f32[32,32,128]{2,1,0:T(8,128)S(1)} %constant_dynamic-update-slice_fusion.18.refs_1_), channel_id=1, source_target_pairs={{0,2},{2,0},{1,3},{3,1},{4,6},{6,4},{5,7},{7,5},{8,10},{10,8},{9,1... | collective-permute-start | bytes 1572872 | tf_op jit(solution)/shard_map/ppermute | solution.py:37
  117.2 6.6 %shard_map.98 = (f32[96,32,128]{2,1,0:T(8,128)S(1)}, f32[96,32,128]{2,1,0:T(8,128)S(1)}) custom-call(s32[772]{0:T(1024)S(1)} %pad_add_fusion.places_ref, f32[128,128,128]{2,1,0:T(8,128)} %own_ref.8, f32[128,128,128]{2,1,0:T(8,128)} %copy-done.2, f32[32,32,128]{2,1,0:T(8,128)S(1)} %constant_dynamic-update-slice_fusion.15.refs_0_, ...), custom_call_target="tpu_custom_call" | custom-call | flops 536870912 | bytes 14680064 | tf_op jit(solution)/shard_map/pallas_call | solution.py:188
  125.7 4.3 %shard_map.100 = (f32[32,32,128]{2,1,0:T(8,128)S(1)}, f32[32,32,128]{2,1,0:T(8,128)S(1)}, f32[32,32,128]{2,1,0:T(8,128)S(1)}) custom-call(s32[772]{0:T(1024)S(1)} %pad_add_fusion.places_ref, f32[128,128,128]{2,1,0:T(8,128)} %own_ref.8, f32[128,128,128]{2,1,0:T(8,128)} %copy-done.2, f32[32,32,128]{2,1,0:T(8,128)S(1)} %collective-permute-done.26.refs_0_, ...), custom_call_target="tpu_custom_call" | custom-call | flops 268435456 | bytes 7340032 | tf_op jit(solution)/shard_map/pallas_call | solution.py:188
  133.0 4.2 %shard_map.99 = (f32[32,32,128]{2,1,0:T(8,128)S(1)}, f32[32,32,128]{2,1,0:T(8,128)S(1)}, f32[32,32,128]{2,1,0:T(8,128)S(1)}) custom-call(s32[772]{0:T(1024)S(1)} %pad_add_fusion.places_ref, f32[128,128,128]{2,1,0:T(8,128)} %own_ref.8, f32[128,128,128]{2,1,0:T(8,128)} %copy-done.2, f32[32,32,128]{2,1,0:T(8,128)S(1)} %collective-permute-done.26.refs_0_, ...), custom_call_target="tpu_custom_call" | custom-call | flops 268435456 | bytes 7340032 | tf_op jit(solution)/shard_map/pallas_call | solution.py:188
  137.2 3.6 %collective-permute-done.33 = f32[32,32,128]{2,1,0:T(8,128)S(1)} collective-permute-done((f32[32,32,128]{2,1,0:T(8,128)S(1)}, f32[32,32,128]{2,1,0:T(8,128)S(1)}, u32[]{:S(2)}, u32[]{:S(2)}) %collective-permute-start.33) | collective-permute-done | bytes 524320 | tf_op jit(solution)/shard_map/ppermute | solution.py:37
  145.6 3.2 %collective-permute-done.34 = f32[16,32,128]{2,1,0:T(8,128)S(1)} collective-permute-done((f32[16,32,128]{2,1,0:T(8,128)S(1)}, f32[16,32,128]{2,1,0:T(8,128)S(1)}, u32[]{:S(2)}, u32[]{:S(2)}) %collective-permute-start.34) | collective-permute-done | bytes 262176 | tf_op jit(solution)/shard_map/ppermute | solution.py:37
  153.8 2.8 %collective-permute-done.38 = f32[8,32,128]{2,1,0:T(8,128)S(1)} collective-permute-done((f32[8,32,128]{2,1,0:T(8,128)S(1)}, f32[8,32,128]{2,1,0:T(8,128)S(1)}, u32[]{:S(2)}, u32[]{:S(2)}) %collective-permute-start.38) | collective-permute-done | bytes 131104 | tf_op jit(solution)/shard_map/ppermute | solution.py:37
  156.8 4.1 %collective-permute-start.42 = (f32[24,32,128]{2,1,0:T(8,128)S(1)}, f32[24,32,128]{2,1,0:T(8,128)S(1)}, u32[]{:S(2)}, u32[]{:S(2)}) collective-permute-start(f32[24,32,128]{2,1,0:T(8,128)S(1)} %get-tuple-element.210), channel_id=1, source_target_pairs={{0,16},{8,24},{16,0},{24,8},{1,17},{9,25},{17,1},{25,9},{2,18},{10... | collective-permute-start | bytes 1179656 | tf_op jit(solution)/shard_map/ppermute | solution.py:37
  160.9 10.1 %collective-permute-done.42 = f32[24,32,128]{2,1,0:T(8,128)S(1)} collective-permute-done((f32[24,32,128]{2,1,0:T(8,128)S(1)}, f32[24,32,128]{2,1,0:T(8,128)S(1)}, u32[]{:S(2)}, u32[]{:S(2)}) %collective-permute-start.42) | collective-permute-done | bytes 393248 | tf_op jit(solution)/shard_map/ppermute | solution.py:37
  173.7 2.5 %collective-permute-done.43 = f32[8,32,128]{2,1,0:T(8,128)S(1)} collective-permute-done((f32[8,32,128]{2,1,0:T(8,128)S(1)}, f32[8,32,128]{2,1,0:T(8,128)S(1)}, u32[]{:S(2)}, u32[]{:S(2)}) %collective-permute-start.43) | collective-permute-done | bytes 131104 | tf_op jit(solution)/shard_map/ppermute | solution.py:37
  182.1 2.7 %collective-permute-done.44 = f32[16,32,128]{2,1,0:T(8,128)S(1)} collective-permute-done((f32[16,32,128]{2,1,0:T(8,128)S(1)}, f32[16,32,128]{2,1,0:T(8,128)S(1)}, u32[]{:S(2)}, u32[]{:S(2)}) %collective-permute-start.44) | collective-permute-done | bytes 262176 | tf_op jit(solution)/shard_map/ppermute | solution.py:37
  188.5 6.6 %shard_map.101 = (f32[96,32,128]{2,1,0:T(8,128)S(1)}, f32[96,32,128]{2,1,0:T(8,128)S(1)}) custom-call(s32[772]{0:T(1024)S(1)} %pad_add_fusion.places_ref, f32[128,128,128]{2,1,0:T(8,128)} %own_ref.8, f32[128,128,128]{2,1,0:T(8,128)} %copy-done.2, f32[32,32,128]{2,1,0:T(8,128)S(1)} %constant_dynamic-update-slice_fusion.30.refs_0_, ...), custom_call_target="tpu_custom_call" | custom-call | flops 536870912 | bytes 14680064 | tf_op jit(solution)/shard_map/pallas_call | solution.py:188
  195.3 4.5 %collective-permute-done.48.refs_1_ = f32[32,32,128]{2,1,0:T(8,128)S(1)} collective-permute-done((f32[32,32,128]{2,1,0:T(8,128)S(1)}, f32[32,32,128]{2,1,0:T(8,128)S(1)}, u32[]{:S(2)}, u32[]{:S(2)}) %collective-permute-start.48) | collective-permute-done | bytes 524320 | tf_op jit(solution)/shard_map/ppermute | solution.py:37
  201.6 4.3 %shard_map.103 = (f32[32,32,128]{2,1,0:T(8,128)S(1)}, f32[32,32,128]{2,1,0:T(8,128)S(1)}, f32[32,32,128]{2,1,0:T(8,128)S(1)}) custom-call(s32[772]{0:T(1024)S(1)} %pad_add_fusion.places_ref, f32[128,128,128]{2,1,0:T(8,128)} %own_ref.8, f32[128,128,128]{2,1,0:T(8,128)} %copy-done.2, f32[32,32,128]{2,1,0:T(8,128)S(1)} %collective-permute-done.45.refs_0_, ...), custom_call_target="tpu_custom_call" | custom-call | flops 268435456 | bytes 7340032 | tf_op jit(solution)/shard_map/pallas_call | solution.py:188
  208.8 4.0 %shard_map.102 = (f32[32,32,128]{2,1,0:T(8,128)S(1)}, f32[32,32,128]{2,1,0:T(8,128)S(1)}, f32[32,32,128]{2,1,0:T(8,128)S(1)}) custom-call(s32[772]{0:T(1024)S(1)} %pad_add_fusion.places_ref, f32[128,128,128]{2,1,0:T(8,128)} %own_ref.8, f32[128,128,128]{2,1,0:T(8,128)} %copy-done.2, f32[32,32,128]{2,1,0:T(8,128)S(1)} %collective-permute-done.45.refs_0_, ...), custom_call_target="tpu_custom_call" | custom-call | flops 268435456 | bytes 7340032 | tf_op jit(solution)/shard_map/pallas_call | solution.py:188
  212.8 3.8 %collective-permute-done.58 = f32[32,32,128]{2,1,0:T(8,128)S(1)} collective-permute-done((f32[32,32,128]{2,1,0:T(8,128)S(1)}, f32[32,32,128]{2,1,0:T(8,128)S(1)}, u32[]{:S(2)}, u32[]{:S(2)}) %collective-permute-start.58) | collective-permute-done | bytes 524320 | tf_op jit(solution)/shard_map/ppermute | solution.py:37
  219.7 3.4 %collective-permute-done.59 = f32[16,32,128]{2,1,0:T(8,128)S(1)} collective-permute-done((f32[16,32,128]{2,1,0:T(8,128)S(1)}, f32[16,32,128]{2,1,0:T(8,128)S(1)}, u32[]{:S(2)}, u32[]{:S(2)}) %collective-permute-start.59) | collective-permute-done | bytes 262176 | tf_op jit(solution)/shard_map/ppermute | solution.py:37
  235.3 3.3 %collective-permute-start.61 = (f32[12,32,128]{2,1,0:T(8,128)S(1)}, f32[12,32,128]{2,1,0:T(8,128)S(1)}, u32[]{:S(2)}, u32[]{:S(2)}) collective-permute-start(f32[12,32,128]{2,1,0:T(8,128)S(1)} %get-tuple-element.204), channel_id=1, source_target_pairs={{0,16},{8,24},{16,0},{24,8},{1,17},{9,25},{17,1},{25,9},{2,18},{10... | collective-permute-start | bytes 589832 | tf_op jit(solution)/shard_map/ppermute | solution.py:37
  238.6 9.6 %all_to_all.6 = f32[32,1,128]{2,1,0:T(1,128)S(1)} all-to-all(f32[32,1,128]{2,1,0:T(1,128)S(1)} %broadcast_in_dim.60), channel_id=1, replica_groups=mesh['z'=4,'y'=2,'x'=2,'core'=2] {'z','y','x','core'}, dimensions={0} | all-to-all | bytes 32768 | tf_op jit(solution)/shard_map/all_to_all | solution.py:308
  (285 shorter events, 97.2 us)
Async XLA Ops:
  6.1 17.1 %collective-permute-start.3 = (f32[128,128,128]{2,1,0:T(8,128)}, f32[128,128,128]{2,1,0:T(8,128)S(1)}, u32[]{:S(2)}, u32[]{:S(2)}) collective-permute-start(f32[128,128,128]{2,1,0:T(8,128)} %own_ref.8), channel_id=1, source_target_pairs={{0,1},{1,0},{2,3},{3,2},{4,5},{5,4},{6,7},{7,6},{8,9},{9,8},{10,11... | collective-permute-start | bytes 25165832 | tf_op jit(solution)/shard_map/ppermute | solution.py:37
  8.6 14.7 %collective-permute-start.2 = (f32[12,32,128]{2,1,0:T(8,128)S(1)}, f32[12,32,128]{2,1,0:T(8,128)S(1)}, u32[]{:S(2)}, u32[]{:S(2)}) collective-permute-start(f32[12,32,128]{2,1,0:T(8,128)S(1)} %get-tuple-element.272), channel_id=1, source_target_pairs={{0,16},{8,24},{16,0},{24,8},{1,17},{9,25},{17,1},{25,9},{2,18},{10... | collective-permute-start | bytes 589832 | tf_op jit(solution)/shard_map/ppermute | solution.py:37
  12.5 10.2 %collective-permute-start.4 = (f32[12,2,128]{2,0,1:T(8,128)S(1)}, f32[12,2,128]{2,0,1:T(8,128)S(1)}, u32[]{:S(2)}, u32[]{:S(2)}) collective-permute-start(f32[12,2,128]{2,0,1:T(8,128)S(1)} %pad_maximum_fusion.22), channel_id=1, source_target_pairs={{0,16},{8,24},{16,0},{24,8},{1,17},{9,25},{17,1},{25,9},{2,18},{10... | collective-permute-start | bytes 36872 | tf_op jit(solution)/shard_map/ppermute | solution.py:37
  28.6 7.9 %collective-permute-start.6 = (f32[16,32,128]{2,1,0:T(8,128)S(1)}, f32[16,32,128]{2,1,0:T(8,128)S(1)}, u32[]{:S(2)}, u32[]{:S(2)}) collective-permute-start(f32[16,32,128]{2,1,0:T(8,128)S(1)} %pad_maximum_fusion), channel_id=1, source_target_pairs={{0,2},{2,0},{1,3},{3,1},{4,6},{6,4},{5,7},{7,5},{8,10},{10,8},{9,1... | collective-permute-start | bytes 786440 | tf_op jit(solution)/shard_map/ppermute | solution.py:37
  36.5 12.9 %collective-permute-start.7 = (f32[32,32,128]{2,1,0:T(8,128)S(1)}, f32[32,32,128]{2,1,0:T(8,128)S(1)}, u32[]{:S(2)}, u32[]{:S(2)}) collective-permute-start(f32[32,32,128]{2,1,0:T(8,128)S(1)} %constant_dynamic-update-slice_fusion.refs_0_), channel_id=1, source_target_pairs={{0,8},{8,0},{16,24},{24,16},{1,9},{9,1},{17,25},{25,17},{2,10},{10... | collective-permute-start | bytes 1572872 | tf_op jit(solution)/shard_map/ppermute | solution.py:37
  37.9 12.6 %collective-permute-start.10 = (f32[32,32,128]{2,1,0:T(8,128)S(1)}, f32[32,32,128]{2,1,0:T(8,128)S(1)}, u32[]{:S(2)}, u32[]{:S(2)}) collective-permute-start(f32[32,32,128]{2,1,0:T(8,128)S(1)} %constant_dynamic-update-slice_fusion.3.refs_1_), channel_id=1, source_target_pairs={{0,2},{2,0},{1,3},{3,1},{4,6},{6,4},{5,7},{7,5},{8,10},{10,8},{9,1... | collective-permute-start | bytes 1572872 | tf_op jit(solution)/shard_map/ppermute | solution.py:37
  39.5 12.3 %collective-permute-start.13 = (f32[32,32,128]{2,1,0:T(8,128)S(1)}, f32[32,32,128]{2,1,0:T(8,128)S(1)}, u32[]{:S(2)}, u32[]{:S(2)}) collective-permute-start(f32[32,32,128]{2,1,0:T(8,128)S(1)} %constant_dynamic-update-slice_fusion.6.refs_2_), channel_id=1, source_target_pairs={{0,4},{4,0},{1,5},{5,1},{2,6},{6,2},{3,7},{7,3},{8,12},{12,8},{9,1... | collective-permute-start | bytes 1572872 | tf_op jit(solution)/shard_map/ppermute | solution.py:37
  56.1 11.4 %collective-permute-start.14 = (f32[32,32,128]{2,1,0:T(8,128)S(1)}, f32[32,32,128]{2,1,0:T(8,128)S(1)}, u32[]{:S(2)}, u32[]{:S(2)}) collective-permute-start(f32[32,32,128]{2,1,0:T(8,128)S(1)} %get-tuple-element.113), channel_id=1, source_target_pairs={{0,8},{8,0},{16,24},{24,16},{1,9},{9,1},{17,25},{25,17},{2,10},{10... | collective-permute-start | bytes 1572872 | tf_op jit(solution)/shard_map/ppermute | solution.py:37
  56.2 12.1 %collective-permute-start.17 = (f32[32,32,128]{2,1,0:T(8,128)S(1)}, f32[32,32,128]{2,1,0:T(8,128)S(1)}, u32[]{:S(2)}, u32[]{:S(2)}) collective-permute-start(f32[32,32,128]{2,1,0:T(8,128)S(1)} %get-tuple-element.122), channel_id=1, source_target_pairs={{0,2},{2,0},{1,3},{3,1},{4,6},{6,4},{5,7},{7,5},{8,10},{10,8},{9,1... | collective-permute-start | bytes 1572872 | tf_op jit(solution)/shard_map/ppermute | solution.py:37
  57.4 11.5 %collective-permute-start.20 = (f32[32,32,128]{2,1,0:T(8,128)S(1)}, f32[32,32,128]{2,1,0:T(8,128)S(1)}, u32[]{:S(2)}, u32[]{:S(2)}) collective-permute-start(f32[32,32,128]{2,1,0:T(8,128)S(1)} %get-tuple-element.131), channel_id=1, source_target_pairs={{0,4},{4,0},{1,5},{5,1},{2,6},{6,2},{3,7},{7,3},{8,12},{12,8},{9,1... | collective-permute-start | bytes 1572872 | tf_op jit(solution)/shard_map/ppermute | solution.py:37
  68.4 7.8 %collective-permute-start.18 = (f32[16,32,128]{2,1,0:T(8,128)S(1)}, f32[16,32,128]{2,1,0:T(8,128)S(1)}, u32[]{:S(2)}, u32[]{:S(2)}) collective-permute-start(f32[16,32,128]{2,1,0:T(8,128)S(1)} %slice_add_fusion.7), channel_id=1, source_target_pairs={{0,4},{4,0},{1,5},{5,1},{2,6},{6,2},{3,7},{7,3},{8,12},{12,8},{9,1... | collective-permute-start | bytes 786440 | tf_op jit(solution)/shard_map/ppermute | solution.py:37
  69.0 10.1 %collective-permute-start.21 = (f32[16,32,128]{2,1,0:T(8,128)S(1)}, f32[16,32,128]{2,1,0:T(8,128)S(1)}, u32[]{:S(2)}, u32[]{:S(2)}) collective-permute-start(f32[16,32,128]{2,1,0:T(8,128)S(1)} %slice_add_fusion.6), channel_id=1, source_target_pairs={{0,8},{8,0},{16,24},{24,16},{1,9},{9,1},{17,25},{25,17},{2,10},{10... | collective-permute-start | bytes 786440 | tf_op jit(solution)/shard_map/ppermute | solution.py:37
  84.4 14.4 %collective-permute-start.23 = (f32[24,32,128]{2,1,0:T(8,128)S(1)}, f32[24,32,128]{2,1,0:T(8,128)S(1)}, u32[]{:S(2)}, u32[]{:S(2)}) collective-permute-start(f32[24,32,128]{2,1,0:T(8,128)S(1)} %get-tuple-element.222), channel_id=1, source_target_pairs={{0,16},{8,24},{16,0},{24,8},{1,17},{9,25},{17,1},{25,9},{2,18},{10... | collective-permute-start | bytes 1179656 | tf_op jit(solution)/shard_map/ppermute | solution.py:37
  104.7 7.9 %collective-permute-start.25 = (f32[16,32,128]{2,1,0:T(8,128)S(1)}, f32[16,32,128]{2,1,0:T(8,128)S(1)}, u32[]{:S(2)}, u32[]{:S(2)}) collective-permute-start(f32[16,32,128]{2,1,0:T(8,128)S(1)} %pad_maximum_fusion.3), channel_id=1, source_target_pairs={{0,2},{2,0},{1,3},{3,1},{4,6},{6,4},{5,7},{7,5},{8,10},{10,8},{9,1... | collective-permute-start | bytes 786440 | tf_op jit(solution)/shard_map/ppermute | solution.py:37
  104.8 7.9 %collective-permute-start.28 = (f32[16,32,128]{2,1,0:T(8,128)S(1)}, f32[16,32,128]{2,1,0:T(8,128)S(1)}, u32[]{:S(2)}, u32[]{:S(2)}) collective-permute-start(f32[16,32,128]{2,1,0:T(8,128)S(1)} %pad_maximum_fusion.4), channel_id=1, source_target_pairs={{0,4},{4,0},{1,5},{5,1},{2,6},{6,2},{3,7},{7,3},{8,12},{12,8},{9,1... | collective-permute-start | bytes 786440 | tf_op jit(solution)/shard_map/ppermute | solution.py:37
  107.2 9.3 %collective-permute-start.31 = (f32[16,32,128]{2,1,0:T(8,128)S(1)}, f32[16,32,128]{2,1,0:T(8,128)S(1)}, u32[]{:S(2)}, u32[]{:S(2)}) collective-permute-start(f32[16,32,128]{2,1,0:T(8,128)S(1)} %pad_maximum_fusion.5), channel_id=1, source_target_pairs={{0,8},{8,0},{16,24},{24,16},{1,9},{9,1},{17,25},{25,17},{2,10},{10... | collective-permute-start | bytes 786440 | tf_op jit(solution)/shard_map/ppermute | solution.py:37
  112.6 11.1 %collective-permute-start.26 = (f32[32,32,128]{2,1,0:T(8,128)S(1)}, f32[32,32,128]{2,1,0:T(8,128)S(1)}, u32[]{:S(2)}, u32[]{:S(2)}) collective-permute-start(f32[32,32,128]{2,1,0:T(8,128)S(1)} %constant_dynamic-update-slice_fusion.15.refs_0_), channel_id=1, source_target_pairs={{0,8},{8,0},{16,24},{24,16},{1,9},{9,1},{17,25},{25,17},{2,10},{10... | collective-permute-start | bytes 1572872 | tf_op jit(solution)/shard_map/ppermute | solution.py:37
  112.7 11.0 %collective-permute-start.29 = (f32[32,32,128]{2,1,0:T(8,128)S(1)}, f32[32,32,128]{2,1,0:T(8,128)S(1)}, u32[]{:S(2)}, u32[]{:S(2)}) collective-permute-start(f32[32,32,128]{2,1,0:T(8,128)S(1)} %constant_dynamic-update-slice_fusion.18.refs_1_), channel_id=1, source_target_pairs={{0,2},{2,0},{1,3},{3,1},{4,6},{6,4},{5,7},{7,5},{8,10},{10,8},{9,1... | collective-permute-start | bytes 1572872 | tf_op jit(solution)/shard_map/ppermute | solution.py:37
  116.5 9.2 %collective-permute-start.32 = (f32[32,32,128]{2,1,0:T(8,128)S(1)}, f32[32,32,128]{2,1,0:T(8,128)S(1)}, u32[]{:S(2)}, u32[]{:S(2)}) collective-permute-start(f32[32,32,128]{2,1,0:T(8,128)S(1)} %constant_dynamic-update-slice_fusion.21.refs_2_), channel_id=1, source_target_pairs={{0,4},{4,0},{1,5},{5,1},{2,6},{6,2},{3,7},{7,3},{8,12},{12,8},{9,1... | collective-permute-start | bytes 1572872 | tf_op jit(solution)/shard_map/ppermute | solution.py:37
  130.1 10.8 %collective-permute-start.33 = (f32[32,32,128]{2,1,0:T(8,128)S(1)}, f32[32,32,128]{2,1,0:T(8,128)S(1)}, u32[]{:S(2)}, u32[]{:S(2)}) collective-permute-start(f32[32,32,128]{2,1,0:T(8,128)S(1)} %get-tuple-element.145), channel_id=1, source_target_pairs={{0,8},{8,0},{16,24},{24,16},{1,9},{9,1},{17,25},{25,17},{2,10},{10... | collective-permute-start | bytes 1572872 | tf_op jit(solution)/shard_map/ppermute | solution.py:37
  130.8 12.0 %collective-permute-start.36 = (f32[32,32,128]{2,1,0:T(8,128)S(1)}, f32[32,32,128]{2,1,0:T(8,128)S(1)}, u32[]{:S(2)}, u32[]{:S(2)}) collective-permute-start(f32[32,32,128]{2,1,0:T(8,128)S(1)} %get-tuple-element.154), channel_id=1, source_target_pairs={{0,2},{2,0},{1,3},{3,1},{4,6},{6,4},{5,7},{7,5},{8,10},{10,8},{9,1... | collective-permute-start | bytes 1572872 | tf_op jit(solution)/shard_map/ppermute | solution.py:37
  132.0 12.8 %collective-permute-start.39 = (f32[32,32,128]{2,1,0:T(8,128)S(1)}, f32[32,32,128]{2,1,0:T(8,128)S(1)}, u32[]{:S(2)}, u32[]{:S(2)}) collective-permute-start(f32[32,32,128]{2,1,0:T(8,128)S(1)} %get-tuple-element.163), channel_id=1, source_target_pairs={{0,4},{4,0},{1,5},{5,1},{2,6},{6,2},{3,7},{7,3},{8,12},{12,8},{9,1... | collective-permute-start | bytes 1572872 | tf_op jit(solution)/shard_map/ppermute | solution.py:37
  156.8 14.2 %collective-permute-start.42 = (f32[24,32,128]{2,1,0:T(8,128)S(1)}, f32[24,32,128]{2,1,0:T(8,128)S(1)}, u32[]{:S(2)}, u32[]{:S(2)}) collective-permute-start(f32[24,32,128]{2,1,0:T(8,128)S(1)} %get-tuple-element.210), channel_id=1, source_target_pairs={{0,16},{8,24},{16,0},{24,8},{1,17},{9,25},{17,1},{25,9},{2,18},{10... | collective-permute-start | bytes 1179656 | tf_op jit(solution)/shard_map/ppermute | solution.py:37
  176.3 8.5 %collective-permute-start.44 = (f32[16,32,128]{2,1,0:T(8,128)S(1)}, f32[16,32,128]{2,1,0:T(8,128)S(1)}, u32[]{:S(2)}, u32[]{:S(2)}) collective-permute-start(f32[16,32,128]{2,1,0:T(8,128)S(1)} %pad_maximum_fusion.6), channel_id=1, source_target_pairs={{0,2},{2,0},{1,3},{3,1},{4,6},{6,4},{5,7},{7,5},{8,10},{10,8},{9,1... | collective-permute-start | bytes 786440 | tf_op jit(solution)/shard_map/ppermute | solution.py:37
  184.8 10.5 %collective-permute-start.45 = (f32[32,32,128]{2,1,0:T(8,128)S(1)}, f32[32,32,128]{2,1,0:T(8,128)S(1)}, u32[]{:S(2)}, u32[]{:S(2)}) collective-permute-start(f32[32,32,128]{2,1,0:T(8,128)S(1)} %constant_dynamic-update-slice_fusion.30.refs_0_), channel_id=1, source_target_pairs={{0,8},{8,0},{16,24},{24,16},{1,9},{9,1},{17,25},{25,17},{2,10},{10... | collective-permute-start | bytes 1572872 | tf_op jit(solution)/shard_map/ppermute | solution.py:37
  186.3 13.5 %collective-permute-start.48 = (f32[32,32,128]{2,1,0:T(8,128)S(1)}, f32[32,32,128]{2,1,0:T(8,128)S(1)}, u32[]{:S(2)}, u32[]{:S(2)}) collective-permute-start(f32[32,32,128]{2,1,0:T(8,128)S(1)} %constant_dynamic-update-slice_fusion.33.refs_1_), channel_id=1, source_target_pairs={{0,2},{2,0},{1,3},{3,1},{4,6},{6,4},{5,7},{7,5},{8,10},{10,8},{9,1... | collective-permute-start | bytes 1572872 | tf_op jit(solution)/shard_map/ppermute | solution.py:37
  187.1 14.5 %collective-permute-start.51 = (f32[32,32,128]{2,1,0:T(8,128)S(1)}, f32[32,32,128]{2,1,0:T(8,128)S(1)}, u32[]{:S(2)}, u32[]{:S(2)}) collective-permute-start(f32[32,32,128]{2,1,0:T(8,128)S(1)} %constant_dynamic-update-slice_fusion.36.refs_2_), channel_id=1, source_target_pairs={{0,4},{4,0},{1,5},{5,1},{2,6},{6,2},{3,7},{7,3},{8,12},{12,8},{9,1... | collective-permute-start | bytes 1572872 | tf_op jit(solution)/shard_map/ppermute | solution.py:37
  206.0 10.7 %collective-permute-start.58 = (f32[32,32,128]{2,1,0:T(8,128)S(1)}, f32[32,32,128]{2,1,0:T(8,128)S(1)}, u32[]{:S(2)}, u32[]{:S(2)}) collective-permute-start(f32[32,32,128]{2,1,0:T(8,128)S(1)} %get-tuple-element.195), channel_id=1, source_target_pairs={{0,4},{4,0},{1,5},{5,1},{2,6},{6,2},{3,7},{7,3},{8,12},{12,8},{9,1... | collective-permute-start | bytes 1572872 | tf_op jit(solution)/shard_map/ppermute | solution.py:37
  206.7 10.6 %collective-permute-start.55 = (f32[32,32,128]{2,1,0:T(8,128)S(1)}, f32[32,32,128]{2,1,0:T(8,128)S(1)}, u32[]{:S(2)}, u32[]{:S(2)}) collective-permute-start(f32[32,32,128]{2,1,0:T(8,128)S(1)} %get-tuple-element.186), channel_id=1, source_target_pairs={{0,2},{2,0},{1,3},{3,1},{4,6},{6,4},{5,7},{7,5},{8,10},{10,8},{9,1... | collective-permute-start | bytes 1572872 | tf_op jit(solution)/shard_map/ppermute | solution.py:37
  207.7 10.6 %collective-permute-start.52 = (f32[32,32,128]{2,1,0:T(8,128)S(1)}, f32[32,32,128]{2,1,0:T(8,128)S(1)}, u32[]{:S(2)}, u32[]{:S(2)}) collective-permute-start(f32[32,32,128]{2,1,0:T(8,128)S(1)} %get-tuple-element.177), channel_id=1, source_target_pairs={{0,8},{8,0},{16,24},{24,16},{1,9},{9,1},{17,25},{25,17},{2,10},{10... | collective-permute-start | bytes 1572872 | tf_op jit(solution)/shard_map/ppermute | solution.py:37
  218.3 7.9 %collective-permute-start.53 = (f32[16,32,128]{2,1,0:T(8,128)S(1)}, f32[16,32,128]{2,1,0:T(8,128)S(1)}, u32[]{:S(2)}, u32[]{:S(2)}) collective-permute-start(f32[16,32,128]{2,1,0:T(8,128)S(1)} %slice_add_fusion.2), channel_id=1, source_target_pairs={{0,2},{2,0},{1,3},{3,1},{4,6},{6,4},{5,7},{7,5},{8,10},{10,8},{9,1... | collective-permute-start | bytes 786440 | tf_op jit(solution)/shard_map/ppermute | solution.py:37
  235.3 13.7 %collective-permute-start.61 = (f32[12,32,128]{2,1,0:T(8,128)S(1)}, f32[12,32,128]{2,1,0:T(8,128)S(1)}, u32[]{:S(2)}, u32[]{:S(2)}) collective-permute-start(f32[12,32,128]{2,1,0:T(8,128)S(1)} %get-tuple-element.204), channel_id=1, source_target_pairs={{0,16},{8,24},{16,0},{24,8},{1,17},{9,25},{17,1},{25,9},{2,18},{10... | collective-permute-start | bytes 589832 | tf_op jit(solution)/shard_map/ppermute | solution.py:37
  (52 other events, 329.8 us)
